TPU v7x, 32 devices: a whole 2x2x4 slice. The times are simulated.
32 devices in a mesh: groups: 2 (over y), wide: 4 (over z), narrow: 4 (over x, core).
Axes of the slice: x: 2, y: 2, z: 4, core: 2. Of those that a mesh axis runs over, the one named last changes fastest.
Arguments:
- operators: float32 [32, 1024, 1024], P(('groups', 'wide', 'narrow')), parts along dimension 0
- coarse_inverse: float32 [2048, 1024], P(('groups', 'wide'), 'narrow'), parts along dimension 0
- modes: float32 [32, 64, 1024], P(('groups', 'wide', 'narrow')), parts along dimension 0, may hold values from -0.1875 to 0.1875
- gap: float32 [32, 1024, 128], P(('groups', 'wide', 'narrow')), parts along dimension 0, may hold values from -6 to 6
- start_mult: float32 [32, 1024, 128], P(('groups', 'wide', 'narrow')), parts along dimension 0, may hold values from -3 to 3
- peer_list: int32 [32, 256, 1], P(('groups', 'wide', 'narrow')), parts along dimension 0, may hold values from 0 to 3; in each aligned block of 256 rows (0 to 255, 256 to 511, ..., all dimensions but the last counted through in order) at most 128 rows name the same one
- partner_row: int32 [32, 256], P(('groups', 'wide', 'narrow')), parts along dimension 0, may hold values from 0 to 255
- interface_size: int32 [32], P(('groups', 'wide', 'narrow')), parts along dimension 0, may hold values from 512 to 1024, as said below
- contact_rows: int32 [32, 1024], P(('groups', 'wide', 'narrow')), parts along dimension 0, may hold values 0 or 1
Outputs:
- mult: float32 [32, 1024, 128], P(('groups', 'wide', 'narrow')), parts along dimension 0
- residual: float32 [32, 1024, 128], P(('groups', 'wide', 'narrow')), parts along dimension 0
There are 2 independent parts, one for each index of `groups`. A program takes and returns all parts, laid end to end along the dimension named above; each array names one. Nothing has to cross between parts.
Inputs may be any that keep to these rules, and one draw needn't show every extreme that they name: `peer_list`: among the 256 shared rows of one subdomain at most 128 name the same neighbour, and exactly 128 do in some subdomain. `interface_size`: some subdomain has all 1024 rows live.
All inputs are finite; a program needn't handle non-finite values. No bound on the sum of `contact_rows` on one device may be relied on, other than what follows from the above.
Results may differ from a plain program's by a relative error of at most 0.0002.
Values sent between devices are 32-bit elements; how exact they have to be, the bound alone decides.
No kernel may reach another device: no remote copies, remote signals or barrier semaphores. Data moves between devices by JAX's collectives and lax.ppermute only.
A program may use at most 64 MiB of HBM per device.

v0:
```python
import jax
import jax.numpy as jnp
from jax import lax
from jax.sharding import PartitionSpec as P

OUTER = 2
INNER = 3


def local(
    operators,
    coarse_inverse,
    modes,
    gap,
    start_mult,
    peer_list,
    partner_row,
    interface_size,
    contact_rows,
):
    highest = lax.Precision.HIGHEST
    operator = operators[0]
    basis = modes[0]
    target = gap[0]
    mult = start_mult[0]
    peers = peer_list[0, :, 0]
    rows_wanted = partner_row[0]
    order = operator.shape[0]
    shared = peers.shape[0]
    active = (lax.iota(jnp.int32, order) < interface_size[0])[:, None]
    contact = (contact_rows[0] == 1)[:, None]
    residual = jnp.zeros_like(target)
    for outer in range(OUTER):
        for inner in range(INNER):
            image = jnp.dot(operator, mult, precision=highest, preferred_element_type=jnp.float32)
            whole = lax.all_gather(image[:shared], "wide", axis=0, tiled=True)
            across = whole[peers * shared + rows_wanted]
            jump = jnp.concatenate([image[:shared] - across, image[shared:]], axis=0)
            residual = jnp.where(active, target - jump, 0.0)
            update = 0.3 * residual
            if inner == 0:
                coarse = jnp.dot(
                    basis, residual, precision=highest, preferred_element_type=jnp.float32
                )
                gathered = lax.all_gather(coarse, "wide", axis=0, tiled=True)
                solved = lax.psum_scatter(
                    jnp.dot(
                        coarse_inverse,
                        gathered,
                        precision=highest,
                        preferred_element_type=jnp.float32,
                    ),
                    "narrow",
                    scatter_dimension=0,
                    tiled=True,
                )
                update = update + lax.dot_general(
                    basis,
                    solved,
                    (((0,), (0,)), ((), ())),
                    precision=highest,
                    preferred_element_type=jnp.float32,
                )
            trial = mult + update
            mult = jnp.where(active, jnp.where(contact, jnp.maximum(trial, 0.0), trial), 0.0)
    return (mult[None], residual[None])


def solution(mesh):
    return jax.shard_map(
        local,
        mesh=mesh,
        in_specs=(
            P(("groups", "wide", "narrow"), None, None),
            P(("groups", "wide"), "narrow"),
            P(("groups", "wide", "narrow"), None, None),
            P(("groups", "wide", "narrow"), None, None),
            P(("groups", "wide", "narrow"), None, None),
            P(("groups", "wide", "narrow"), None, None),
            P(("groups", "wide", "narrow"), None),
            P(("groups", "wide", "narrow")),
            P(("groups", "wide", "narrow"), None),
        ),
        out_specs=(
            P(("groups", "wide", "narrow"), None, None),
            P(("groups", "wide", "narrow"), None, None),
        ),
        check_vma=False,
    )
```

profile of v0, /device:TPU:0, one launch (start us, length us, event | category | flops | bytes accessed | tf_op | source)
XLA Modules:
  0.0 233.6 jit_solution(5831569478208530635)
XLA Ops:
  7.2 0.0 copy-start
  7.2 0.0 copy-start.8
  7.2 0.0 copy-start.9
  7.2 0.0 copy-start.2
  7.2 0.0 reduce-scatter.7.cloned.1.call-start
  7.3 5.4 %fusion.10 = f32[1024,128]{1,0:T(8,128)S(1)} fusion(f32[1,1024,1024]{2,1,0:T(8,128)} %param.9, f32[1,1024,128]{2,1,0:T(8,128)} %param.13), kind=kOutput, calls=%fused_computation.16 | convolution fusion | flops 1610612736 | bytes 5242880 | tf_op jit(solution)/shard_map/dot_general | solution.py:35
  12.6 0.0 copy-start.7
  12.7 0.0 copy-start.3
  12.7 0.1 fusion.83
  13.5 0.0 copy-done.8
  13.5 0.0 copy-done.9
  13.5 17.4 %all_gather.24 = f32[1024,128]{1,0:T(8,128)S(1)} all-gather(f32[256,128]{1,0:T(8,128)S(1)} %slice.66), channel_id=1, replica_groups=mesh['groups'=2,'wide'=4,'narrow'=4] {'wide'}, dimensions={0}, use_global_device_ids=true | all-gather | bytes 655360 | tf_op jit(solution)/shard_map/all_gather | solution.py:36
  30.9 0.7 gather_fusion
  31.6 0.0 copy-done
  31.6 0.0 copy-done.2
  31.6 0.6 convolution_bitcast_fusion.5
  32.2 13.8 %all_gather.25 = f32[256,128]{1,0:T(8,128)S(1)} all-gather(f32[64,128]{1,0:T(8,128)S(1)} %convolution_bitcast_fusion.5), channel_id=1, replica_groups=mesh['groups'=2,'wide'=4,'narrow'=4] {'wide'}, dimensions={0}, use_global_device_ids=true | all-gather | bytes 163840 | tf_op jit(solution)/shard_map/all_gather | solution.py:45
  46.0 1.3 convolution_bitcast_fusion.3
  47.3 0.8 copy.39
  48.1 0.0 reduce-scatter.7.cloned.1.call-update
  48.1 0.0 reduce-scatter.9.cloned.1.call-start
  48.2 0.0 copy-done.7
  48.2 21.0 %reduce-scatter.7.cloned.1.call-done = f32[64,128]{1,0:T(8,128)} async-done(((f32[256,128]{1,0:T(8,128)}), f32[64,128]{1,0:T(8,128)}) %reduce-scatter.7.cloned.1.call-update) | async-done | bytes 32784
  69.2 0.0 copy-done.3
  69.2 1.9 fusion.32
  71.1 5.2 %fusion.14 = f32[1024,128]{1,0:T(8,128)S(1)} fusion(f32[1024,128]{1,0:T(8,128)S(1)} %fusion.32, f32[1,1024,1024]{2,1,0:T(8,128)} %param.9), kind=kOutput, calls=%fused_computation.22 | convolution fusion | flops 1610612736 | bytes 5242880 | tf_op jit(solution)/shard_map/dot_general | solution.py:35
  76.4 15.3 %all_gather.26 = f32[1024,128]{1,0:T(8,128)S(1)} all-gather(f32[256,128]{1,0:T(8,128)S(1)} %slice.68), channel_id=1, replica_groups=mesh['groups'=2,'wide'=4,'narrow'=4] {'wide'}, dimensions={0}, use_global_device_ids=true | all-gather | bytes 655360 | tf_op jit(solution)/shard_map/all_gather | solution.py:36
  91.7 0.7 gather_fusion.1
  92.4 0.0 copy-start.4
  92.4 5.8 %fusion.17 = f32[1024,128]{1,0:T(8,128)S(1)} fusion(f32[1,1024,1024]{2,1,0:T(8,128)} %param.9, f32[1024,128]{1,0:T(8,128)S(1)} %fusion.32, f32[768,128]{1,0:T(8,128)S(1)} %slice.69, f32[256,128]{1,0:T(8,128)S(1)} %slice_subtract_fusion.4, f32[1,1024,128]{2,1,0:T(8,128)S(1)} %copy-done.2, pred[1024]{0:T(1024)(128)(4,1)S(1)} %compare_reduce_fusion, ...), kind=kOutput, calls=%fused_computation.23 | convolution fusion | flops 1611661312 | bytes 6293504 | tf_op jit(solution)/shard_map/dot_general | solution.py:35
  98.3 16.2 %all_gather.27 = f32[1024,128]{1,0:T(8,128)S(1)} all-gather(f32[256,128]{1,0:T(8,128)S(1)} %slice.70), channel_id=1, replica_groups=mesh['groups'=2,'wide'=4,'narrow'=4] {'wide'}, dimensions={0}, use_global_device_ids=true | all-gather | bytes 655360 | tf_op jit(solution)/shard_map/all_gather | solution.py:36
  114.5 0.7 gather_fusion.2
  115.3 0.0 copy-done.4
  115.3 0.0 copy-start.6
  115.3 5.8 %fusion.20 = f32[1024,128]{1,0:T(8,128)S(1)} fusion(f32[1,1024,1024]{2,1,0:T(8,128)} %param.9, f32[768,128]{1,0:T(8,128)S(1)} %slice.71, f32[256,128]{1,0:T(8,128)S(1)} %slice_subtract_fusion.3, f32[1,1024,128]{2,1,0:T(8,128)S(1)} %copy-done.2, pred[1024]{0:T(1024)(128)(4,1)S(1)} %compare_reduce_fusion, pred[1024]{0:T(1024)(128)(4,1)S(1)} %iota_compare_fusion, ...), kind=kOutput, calls=%fused_computation.24 | convolution fusion | flops 1612709888 | bytes 6817792 | tf_op jit(solution)/shard_map/dot_general | solution.py:35
  121.1 0.0 copy-done.6
  121.1 0.8 fusion.82
  121.9 15.2 %all_gather.28 = f32[1024,128]{1,0:T(8,128)S(1)} all-gather(f32[256,128]{1,0:T(8,128)S(1)} %slice.72), channel_id=1, replica_groups=mesh['groups'=2,'wide'=4,'narrow'=4] {'wide'}, dimensions={0}, use_global_device_ids=true | all-gather | bytes 655360 | tf_op jit(solution)/shard_map/all_gather | solution.py:36
  137.1 1.3 gather_fusion.3
  138.4 0.9 slice_subtract_fusion.2
  139.3 0.6 convolution_bitcast_fusion.4
  139.9 13.7 %all_gather.29 = f32[256,128]{1,0:T(8,128)S(1)} all-gather(f32[64,128]{1,0:T(8,128)S(1)} %convolution_bitcast_fusion.4), channel_id=1, replica_groups=mesh['groups'=2,'wide'=4,'narrow'=4] {'wide'}, dimensions={0}, use_global_device_ids=true | all-gather | bytes 163840 | tf_op jit(solution)/shard_map/all_gather | solution.py:45
  153.6 1.3 convolution_bitcast_fusion.2
  155.0 0.8 copy.41
  155.7 0.0 reduce-scatter.9.cloned.1.call-update
  155.8 20.3 %reduce-scatter.9.cloned.1.call-done = f32[64,128]{1,0:T(8,128)} async-done(((f32[256,128]{1,0:T(8,128)}), f32[64,128]{1,0:T(8,128)}) %reduce-scatter.9.cloned.1.call-update) | async-done | bytes 32784
  176.1 0.0 copy-start.1
  176.1 3.2 %fusion.31 = f32[1024,128]{1,0:T(8,128)S(1)} fusion(f32[64,128]{1,0:T(8,128)} %reduce-scatter.9.cloned.1.call-done, f32[768,128]{1,0:T(8,128)} %get-tuple-element.4, f32[256,128]{1,0:T(8,128)S(1)} %slice_subtract_fusion.2, f32[1,1024,128]{2,1,0:T(8,128)S(1)} %copy-done.2, f32[1,64,1024]{2,1,0:T(8,128)S(1)} %copy-done, ...), kind=kOutput, calls=%fused_computation.36 | convolution fusion | flops 103940096 | bytes 3442688 | tf_op jit(solution)/shard_map/dot_general | solution.py:57
  179.3 0.0 copy-done.1
  179.3 3.4 %fusion.23 = f32[1024,128]{1,0:T(8,128)S(1)} fusion(f32[1024,128]{1,0:T(8,128)S(1)} %fusion.31, f32[1,1024,1024]{2,1,0:T(8,128)S(1)} %copy-done.1), kind=kOutput, calls=%fused_computation.25 | convolution fusion | flops 1610612736 | bytes 5242880 | tf_op jit(solution)/shard_map/dot_general | solution.py:35
  182.8 15.5 %all_gather.30 = f32[1024,128]{1,0:T(8,128)S(1)} all-gather(f32[256,128]{1,0:T(8,128)S(1)} %slice.74), channel_id=1, replica_groups=mesh['groups'=2,'wide'=4,'narrow'=4] {'wide'}, dimensions={0}, use_global_device_ids=true | all-gather | bytes 655360 | tf_op jit(solution)/shard_map/all_gather | solution.py:36
  198.2 0.7 gather_fusion.4
  199.0 0.0 copy-start.5
  199.0 5.8 %fusion.26 = f32[1024,128]{1,0:T(8,128)S(1)} fusion(f32[1,1024,1024]{2,1,0:T(8,128)} %param.9, f32[1024,128]{1,0:T(8,128)S(1)} %fusion.31, f32[768,128]{1,0:T(8,128)S(1)} %slice.75, f32[256,128]{1,0:T(8,128)S(1)} %slice_subtract_fusion.1, f32[1,1024,128]{2,1,0:T(8,128)S(1)} %copy-done.2, pred[1024]{0:T(1024)(128)(4,1)S(1)} %compare_reduce_fusion, ...), kind=kOutput, calls=%fused_computation.26 | convolution fusion | flops 1611661312 | bytes 6293504 | tf_op jit(solution)/shard_map/dot_general | solution.py:35
  204.8 0.0 copy-done.5
  204.8 0.1 slice_bitcast_fusion
  204.9 16.1 %all_gather.31 = f32[1024,128]{1,0:T(8,128)S(1)} all-gather(f32[256,128]{1,0:T(8,128)S(1)} %slice.76), channel_id=1, replica_groups=mesh['groups'=2,'wide'=4,'narrow'=4] {'wide'}, dimensions={0}, use_global_device_ids=true | all-gather | bytes 655360 | tf_op jit(solution)/shard_map/all_gather | solution.py:36
  221.0 1.3 gather_fusion.5
  222.3 0.9 slice_subtract_fusion
  223.2 2.5 %fusion.37 = f32[1,1024,128]{2,1,0:T(8,128)} fusion(f32[768,128]{1,0:T(8,128)S(1)} %get-tuple-element.3, f32[256,128]{1,0:T(8,128)S(1)} %slice_subtract_fusion, f32[1,1024,128]{2,1,0:T(8,128)S(1)} %copy-done.2, pred[1024]{0:T(1024)(128)(4,1)S(1)} %compare_reduce_fusion, pred[1024]{0:T(1024)(128)(4,1)S(1)} %iota_compare_fusion, f32[1024,128]{1,0:T(8,128)S(1)} %fusion.31, ...), kind=kLoop, calls=%fused_computation.45 | loop fusion | flops 2097152 | bytes 2623488 | tf_op jit(solution)/shard_map/broadcast_in_dim | solution.py:66
  225.8 1.0 fusion.64
  (17 shorter events, 0.2 us)
Async XLA Ops:
  7.2 24.4 %copy-start = (f32[1,64,1024]{2,1,0:T(8,128)S(1)}, f32[1,64,1024]{2,1,0:T(8,128)}, u32[]{:S(2)}) copy-start(f32[1,64,1024]{2,1,0:T(8,128)} %param.11) | copy-start | bytes 786436
  7.2 6.3 %copy-start.8 = (s32[1,256]{1,0:T(1,128)S(1)}, s32[1,256]{1,0:T(1,128)}, u32[]{:S(2)}) copy-start(s32[1,256]{1,0:T(1,128)} %param.15) | copy-start | bytes 3076
  7.2 6.3 %copy-start.9 = (s32[1,256,1]{1,2,0:T(1,128)S(1)}, s32[1,256,1]{1,2,0:T(1,128)}, u32[]{:S(2)}) copy-start(s32[1,256,1]{1,2,0:T(1,128)} %param.14) | copy-start | bytes 3076
  7.2 24.4 %copy-start.2 = (f32[1,1024,128]{2,1,0:T(8,128)S(1)}, f32[1,1024,128]{2,1,0:T(8,128)}, u32[]{:S(2)}) copy-start(f32[1,1024,128]{2,1,0:T(8,128)} %param.12) | copy-start | bytes 1572868
  7.2 62.0 %reduce-scatter.7.cloned.1.call-start = ((), (), s32[]{:S(2)}) async-start(), calls=%async_computation.2 | async-start | bytes 163840
  12.6 35.5 %copy-start.7 = (s32[1,1024]{1,0:T(1,128)S(1)}, s32[1,1024]{1,0:T(1,128)}, u32[]{:S(2)}) copy-start(s32[1,1024]{1,0:T(1,128)} %param.17) | copy-start | bytes 12292
  12.7 56.5 %copy-start.3 = (f32[1,1024,128]{2,1,0:T(8,128)S(1)}, f32[1,1024,128]{2,1,0:T(8,128)}, u32[]{:S(2)}) copy-start(f32[1,1024,128]{2,1,0:T(8,128)} %param.13) | copy-start | bytes 1572868
  48.1 128.0 %reduce-scatter.9.cloned.1.call-start = ((), (), s32[]{:S(2)}) async-start(), calls=%async_computation.3 | async-start | bytes 163840
  92.4 22.8 %copy-start.4 = (f32[256,128]{1,0:T(8,128)}, f32[256,128]{1,0:T(8,128)S(1)}, u32[]{:S(2)}) copy-start(f32[256,128]{1,0:T(8,128)S(1)} %slice_subtract_fusion.4) | copy-start | bytes 393220
  115.3 5.8 %copy-start.6 = (f32[256,128]{1,0:T(8,128)}, f32[256,128]{1,0:T(8,128)S(1)}, u32[]{:S(2)}) copy-start(f32[256,128]{1,0:T(8,128)S(1)} %slice_subtract_fusion.3) | copy-start | bytes 393220
  176.1 3.2 %copy-start.1 = (f32[1,1024,1024]{2,1,0:T(8,128)S(1)}, f32[1,1024,1024]{2,1,0:T(8,128)}, u32[]{:S(2)}) copy-start(f32[1,1024,1024]{2,1,0:T(8,128)} %param.9) | copy-start | bytes 12582916
  199.0 5.8 %copy-start.5 = (f32[256,128]{1,0:T(8,128)}, f32[256,128]{1,0:T(8,128)S(1)}, u32[]{:S(2)}) copy-start(f32[256,128]{1,0:T(8,128)S(1)} %slice_subtract_fusion.1) | copy-start | bytes 393220
Sparse Core Ops, SparseCore 0:
  48.2 20.9 reduce-scatter.6
  155.9 20.1 reduce-scatter.8
where the time goes:
time: 234 us
  blocking collectives  123 us (53%)
  waiting for transfers between devices  41.3 us (18%)
  matrix products  40.3 us (17%)
  between operations  15.1 us (6%)
  local copies, waits for them, and re-layouts  8.22 us (4%)
  other arithmetic  5.47 us (2%)
    all_gather x6, blocking collectives, local(): whole = lax.all_gather(image[:shared], 'wide', axis=0, tiled=True)  95.6 us
    unnamed x4, waiting for transfers between devices  41.3 us
    dot_general x6, matrix products, local(): jnp.dot(operator, mult, precision=highest, preferred_element_type=jnp.flo...  31.3 us
    all_gather x2, blocking collectives, local(): gathered = lax.all_gather(coarse, 'wide', axis=0, tiled=True)  27.5 us
    gather x6, local copies, waits for them, and re-layouts, local(): across = whole[peers * shared + rows_wanted]  5.6 us
    dot_general x2, matrix products, local(): lax.dot_general(basis, solved, (((0,), (0,)), ((), ())), precision=highes...  5.13 us
  transfers between devices with their start and end apart: 2, of which 2 were waited for; matrix products, arithmetic and copies ran while one was open for 0% of the time, Pallas kernels for 0%

commit v1 on v0

v1 whole, which is shorter than its diff:
```python
import jax
import jax.numpy as jnp
from jax import lax
from jax.sharding import PartitionSpec as P

OUTER = 2
INNER = 3


def shifted(block, axis, count, step):
    return lax.ppermute(block, axis, [(i, (i + step) % count) for i in range(count)])


def local(
    wide,
    narrow,
    operators,
    coarse_inverse,
    modes,
    gap,
    start_mult,
    peer_list,
    partner_row,
    interface_size,
    contact_rows,
):
    highest = lax.Precision.HIGHEST
    high = lax.Precision.HIGH
    operator = operators[0]
    basis = modes[0]
    target = gap[0]
    mult = start_mult[0]
    peers = peer_list[0, :, 0]
    rows_wanted = partner_row[0]
    order = operator.shape[0]
    shared = peers.shape[0]
    count = basis.shape[0]
    my_wide = lax.axis_index("wide")
    my_narrow = lax.axis_index("narrow")
    place = lax.rem(my_wide - peers + wide, wide) * shared + rows_wanted
    active = (lax.iota(jnp.int32, order) < interface_size[0])[:, None]
    contact = (contact_rows[0] == 1)[:, None]
    tile = coarse_inverse.reshape(coarse_inverse.shape[0], wide, count)
    tile = jnp.take(tile, lax.rem(my_wide - jnp.arange(wide) + wide, wide), axis=1)
    tile = tile.reshape(coarse_inverse.shape)
    residual = jnp.zeros_like(target)
    for outer in range(OUTER):
        for inner in range(INNER):
            image = jnp.dot(operator, mult, precision=high, preferred_element_type=jnp.float32)
            head = image[:shared]
            whole = jnp.concatenate(
                [head] + [shifted(head, "wide", wide, d) for d in range(1, wide)], axis=0
            )
            across = whole[place]
            jump = jnp.concatenate([head - across, image[shared:]], axis=0)
            residual = jnp.where(active, target - jump, 0.0)
            update = 0.3 * residual
            if inner == 0:
                coarse = jnp.dot(
                    basis, residual, precision=high, preferred_element_type=jnp.float32
                )
                gathered = jnp.concatenate(
                    [coarse] + [shifted(coarse, "wide", wide, d) for d in range(1, wide)], axis=0
                )
                parts = jnp.dot(
                    tile, gathered, precision=high, preferred_element_type=jnp.float32
                )

                def part(d):
                    start = lax.rem(my_narrow + d, narrow) * count
                    return lax.dynamic_slice_in_dim(parts, start, count, axis=0)

                solved = part(0)
                for d in range(1, narrow):
                    solved = solved + shifted(part(d), "narrow", narrow, d)
                update = update + lax.dot_general(
                    basis,
                    solved,
                    (((0,), (0,)), ((), ())),
                    precision=high,
                    preferred_element_type=jnp.float32,
                )
            trial = mult + update
            mult = jnp.where(active, jnp.where(contact, jnp.maximum(trial, 0.0), trial), 0.0)
    return (mult[None], residual[None])


def solution(mesh):
    wide = mesh.shape["wide"]
    narrow = mesh.shape["narrow"]

    def body(*args):
        return local(wide, narrow, *args)

    return jax.shard_map(
        body,
        mesh=mesh,
        in_specs=(
            P(("groups", "wide", "narrow"), None, None),
            P(("groups", "wide"), "narrow"),
            P(("groups", "wide", "narrow"), None, None),
            P(("groups", "wide", "narrow"), None, None),
            P(("groups", "wide", "narrow"), None, None),
            P(("groups", "wide", "narrow"), None, None),
            P(("groups", "wide", "narrow"), None),
            P(("groups", "wide", "narrow")),
            P(("groups", "wide", "narrow"), None),
        ),
        out_specs=(
            P(("groups", "wide", "narrow"), None, None),
            P(("groups", "wide", "narrow"), None, None),
        ),
        check_vma=False,
    )
```

time: 234 us -> 155 us (0.66)
  blocking collectives: 123 us -> 0 us
  starting transfers between devices: 0.08 us -> 34.3 us
  waiting for transfers between devices: 41.3 us -> 69.7 us
  between operations: 15.1 us -> 1.78 us
  matrix products: 40.3 us -> 28.7 us
  other arithmetic: 5.47 us -> 10.1 us
    all_gather x8 -> x0, blocking collectives: 123 us -> none  [the longest x6 95.6 us: local(): whole = lax.all_gather(image[:shared], 'wide', axis=0, tiled=True)]
    ppermute x0 -> x30, waiting for transfers between devices: none -> 69.7 us  [shifted(): lax.ppermute(block, axis, [(i, (i + step) % count) for i in range(count)])]
    unnamed x4 -> x0, waiting for transfers between devices: 41.3 us -> none
    ppermute x0 -> x30, starting transfers between devices: none -> 34.3 us  [shifted(): lax.ppermute(block, axis, [(i, (i + step) % count) for i in range(count)])]
    dot_general x12, matrix products: 40.3 us -> 28.7 us  [the longest x6 22.6 us: local(): jnp.dot(operator, mult, precision=high, preferred_element_type=jnp.float32)]
    gather x6 -> x7, local copies, waits for them, and re-layouts: 5.6 us -> 7.4 us  [the longest x6 6.83 us: local(): across = whole[place]]
  transfers between devices with their start and end apart: 2 -> 30, of which waited for: 2 -> 20; matrix products, arithmetic and copies ran while one was open for 0% -> 3% of each run, Pallas kernels for 0% -> 0%
where the time goes in v1:
time: 155 us; the launch traced here: 154 us
  waiting for transfers between devices  69.7 us (45%)
  starting transfers between devices  34.3 us (22%)
  matrix products  28.7 us (19%)
  other arithmetic  10.1 us (7%)
  local copies, waits for them, and re-layouts  9.45 us (6%)
  between operations  1.78 us (1%)
    ppermute x30, waiting for transfers between devices, shifted(): lax.ppermute(block, axis, [(i, (i + step) % count) for i in range(count)])  69.7 us
    ppermute x30, starting transfers between devices, shifted(): lax.ppermute(block, axis, [(i, (i + step) % count) for i in range(count)])  34.3 us
    dot_general x6, matrix products, local(): jnp.dot(operator, mult, precision=high, preferred_element_type=jnp.float32)  22.6 us
    gather x6, local copies, waits for them, and re-layouts, local(): across = whole[place]  6.83 us
    sub x6, other arithmetic, local(): jump = jnp.concatenate([head - across, image[shared:]], axis=0)  3.85 us
    dot_general x2, matrix products, local(): lax.dot_general(basis, solved, (((0,), (0,)), ((), ())), precision=high,...  3.3 us
  transfers between devices with their start and end apart: 30, of which 20 were waited for; matrix products, arithmetic and copies ran while one was open for 3% of the time, Pallas kernels for 0%

profile of v1, /device:TPU:0, one launch (start us, length us, event | category | flops | bytes accessed | tf_op | source)
XLA Modules:
  0.0 154.1 jit_solution(12975572193301450989)
XLA Ops:
  0.7 4.2 %fusion.10 = f32[1024,128]{1,0:T(8,128)S(1)} fusion(f32[1,1024,1024]{2,1,0:T(8,128)} %param.9, f32[1,1024,128]{2,1,0:T(8,128)} %param.13), kind=kOutput, calls=%fused_computation.17 | convolution fusion | flops 805306368 | bytes 5242880 | tf_op jit(solution)/shard_map/dot_general | solution.py:49
  4.9 5.1 %collective-permute-start.2 = (f32[256,128]{1,0:T(8,128)S(1)}, f32[256,128]{1,0:T(8,128)}, u32[]{:S(2)}, u32[]{:S(2)}) collective-permute-start(f32[256,128]{1,0:T(8,128)S(1)} %slice.62), channel_id=1, source_target_pairs={{0,12},{4,0},{8,4},{12,8},{1,13},{5,1},{9,5},{13,9},{2,14},{6,2},{... | collective-permute-start | bytes 393224 | tf_op jit(solution)/shard_map/ppermute | solution.py:11
  10.0 1.0 collective-permute-start
  11.9 0.6 broadcast_in_dim.113
  13.2 0.7 collective-permute-done.2
  13.9 7.4 %collective-permute-done.1 = f32[256,128]{1,0:T(8,128)} collective-permute-done((f32[256,128]{1,0:T(8,128)S(1)}, f32[256,128]{1,0:T(8,128)}, u32[]{:S(2)}, u32[]{:S(2)}) %collective-permute-start.1) | collective-permute-done | bytes 131104 | tf_op jit(solution)/shard_map/ppermute | solution.py:11
  21.3 1.1 pad_maximum_fusion
  22.4 1.3 gather_fusion
  23.7 0.9 slice_subtract_fusion.5
  25.1 1.7 %collective-permute-start.5 = (f32[64,128]{1,0:T(8,128)S(1)}, f32[64,128]{1,0:T(8,128)S(1)}, u32[]{:S(2)}, u32[]{:S(2)}) collective-permute-start(f32[64,128]{1,0:T(8,128)S(1)} %convolution_bitcast_fusion.3), channel_id=1, source_target_pairs={{0,12},{4,0},{8,4},{12,8},{1,13},{5,1},{9,5},{13,9},{2,14},{6,2},{... | collective-permute-start | bytes 98312 | tf_op jit(solution)/shard_map/ppermute | solution.py:11
  26.8 1.1 collective-permute-start.4
  27.9 1.9 %collective-permute-start.3 = (f32[64,128]{1,0:T(8,128)S(1)}, f32[64,128]{1,0:T(8,128)S(1)}, u32[]{:S(2)}, u32[]{:S(2)}) collective-permute-start(f32[64,128]{1,0:T(8,128)S(1)} %convolution_bitcast_fusion.3), channel_id=1, source_target_pairs={{0,4},{4,8},{8,12},{12,0},{1,5},{5,9},{9,13},{13,1},{2,6},{6,10},{... | collective-permute-start | bytes 98312 | tf_op jit(solution)/shard_map/ppermute | solution.py:11
  29.8 0.8 bitcast_select_fusion
  30.6 1.6 %collective-permute-done.4 = f32[64,128]{1,0:T(8,128)S(1)} collective-permute-done((f32[64,128]{1,0:T(8,128)S(1)}, f32[64,128]{1,0:T(8,128)S(1)}, u32[]{:S(2)}, u32[]{:S(2)}) %collective-permute-start.4) | collective-permute-done | bytes 32800 | tf_op jit(solution)/shard_map/ppermute | solution.py:11
  32.2 1.4 collective-permute-done.3
  34.1 1.7 %collective-permute-start.8 = (f32[64,128]{1,0:T(8,128)S(1)}, f32[64,128]{1,0:T(8,128)S(1)}, u32[]{:S(2)}, u32[]{:S(2)}) collective-permute-start(f32[64,128]{1,0:T(8,128)S(1)} %get-tuple-element.12), channel_id=1, source_target_pairs={{0,3},{1,0},{2,1},{3,2},{4,7},{5,4},{6,5},{7,6},{8,11},{9,8},{10,9... | collective-permute-start | bytes 98312 | tf_op jit(solution)/shard_map/ppermute | solution.py:11
  35.8 1.5 collective-permute-start.7
  37.3 0.7 compare_reduce_fusion
  38.0 1.7 %collective-permute-done.7 = f32[64,128]{1,0:T(8,128)S(1)} collective-permute-done((f32[64,128]{1,0:T(8,128)S(1)}, f32[64,128]{1,0:T(8,128)S(1)}, u32[]{:S(2)}, u32[]{:S(2)}) %collective-permute-start.7) | collective-permute-done | bytes 32800 | tf_op jit(solution)/shard_map/ppermute | solution.py:11
  39.7 0.8 fusion.32
  40.5 4.0 %fusion.14 = f32[1024,128]{1,0:T(8,128)S(1)} fusion(f32[1024,128]{1,0:T(8,128)S(1)} %fusion.32, f32[1,1024,1024]{2,1,0:T(8,128)} %param.9), kind=kOutput, calls=%fused_computation.23 | convolution fusion | flops 805306368 | bytes 5242880 | tf_op jit(solution)/shard_map/dot_general | solution.py:49
  45.0 1.1 collective-permute-start.10
  46.6 3.4 %collective-permute-done.11 = f32[256,128]{1,0:T(8,128)S(1)} collective-permute-done((f32[256,128]{1,0:T(8,128)S(1)}, f32[256,128]{1,0:T(8,128)S(1)}, u32[]{:S(2)}, u32[]{:S(2)}) %collective-permute-start.11) | collective-permute-done | bytes 131104 | tf_op jit(solution)/shard_map/ppermute | solution.py:11
  50.0 7.3 %collective-permute-done.10 = f32[256,128]{1,0:T(8,128)S(1)} collective-permute-done((f32[256,128]{1,0:T(8,128)S(1)}, f32[256,128]{1,0:T(8,128)S(1)}, u32[]{:S(2)}, u32[]{:S(2)}) %collective-permute-start.10) | collective-permute-done | bytes 131104 | tf_op jit(solution)/shard_map/ppermute | solution.py:11
  57.4 0.7 gather_fusion.2
  58.2 4.1 %fusion.17 = f32[1024,128]{1,0:T(8,128)S(1)} fusion(f32[1,1024,1024]{2,1,0:T(8,128)} %param.9, f32[1024,128]{1,0:T(8,128)S(1)} %fusion.32, f32[768,128]{1,0:T(8,128)S(1)} %slice.65, f32[256,128]{1,0:T(8,128)S(1)} %slice_subtract_fusion.4, f32[1,1024,128]{2,1,0:T(8,128)S(1)} %copy-done.2, pred[1024]{0:T(1024)(128)(4,1)S(1)} %compare_reduce_fusion, ...), kind=kOutput, calls=%fused_computation.24 | convolution fusion | flops 806354944 | bytes 6293504 | tf_op jit(solution)/shard_map/dot_general | solution.py:49
  62.4 1.7 %collective-permute-start.13 = (f32[256,128]{1,0:T(8,128)S(1)}, f32[256,128]{1,0:T(8,128)S(1)}, u32[]{:S(2)}, u32[]{:S(2)}) collective-permute-start(f32[256,128]{1,0:T(8,128)S(1)} %slice.66), channel_id=1, source_target_pairs={{0,8},{4,12},{8,0},{12,4},{1,9},{5,13},{9,1},{13,5},{2,10},{6,14},... | collective-permute-start | bytes 393224 | tf_op jit(solution)/shard_map/ppermute | solution.py:11
  64.1 1.9 %collective-permute-start.12 = (f32[256,128]{1,0:T(8,128)S(1)}, f32[256,128]{1,0:T(8,128)S(1)}, u32[]{:S(2)}, u32[]{:S(2)}) collective-permute-start(f32[256,128]{1,0:T(8,128)S(1)} %slice.66), channel_id=1, source_target_pairs={{0,4},{4,8},{8,12},{12,0},{1,5},{5,9},{9,13},{13,1},{2,6},{6,10},{... | collective-permute-start | bytes 393224 | tf_op jit(solution)/shard_map/ppermute | solution.py:11
  66.1 1.5 collective-permute-done.14
  67.6 8.6 %collective-permute-done.13 = f32[256,128]{1,0:T(8,128)S(1)} collective-permute-done((f32[256,128]{1,0:T(8,128)S(1)}, f32[256,128]{1,0:T(8,128)S(1)}, u32[]{:S(2)}, u32[]{:S(2)}) %collective-permute-start.13) | collective-permute-done | bytes 131104 | tf_op jit(solution)/shard_map/ppermute | solution.py:11
  76.2 1.3 gather_fusion.3
  77.6 0.9 slice_subtract_fusion.3
  78.5 4.2 %fusion.20 = f32[1024,128]{1,0:T(8,128)S(1)} fusion(f32[1,1024,1024]{2,1,0:T(8,128)} %param.9, f32[768,128]{1,0:T(8,128)S(1)} %slice.67, f32[256,128]{1,0:T(8,128)S(1)} %slice_subtract_fusion.3, f32[1,1024,128]{2,1,0:T(8,128)S(1)} %copy-done.2, pred[1024]{0:T(1024)(128)(4,1)S(1)} %compare_reduce_fusion, pred[1024]{0:T(1024)(128)(4,1)S(1)} %iota_compare_fusion, ...), kind=kOutput, calls=%fused_computation.25 | convolution fusion | flops 807403520 | bytes 6817792 | tf_op jit(solution)/shard_map/dot_general | solution.py:49
  82.8 0.8 collective-permute-start.16
  83.6 1.9 %collective-permute-start.15 = (f32[256,128]{1,0:T(8,128)S(1)}, f32[256,128]{1,0:T(8,128)S(1)}, u32[]{:S(2)}, u32[]{:S(2)}) collective-permute-start(f32[256,128]{1,0:T(8,128)S(1)} %slice.68), channel_id=1, source_target_pairs={{0,4},{4,8},{8,12},{12,0},{1,5},{5,9},{9,13},{13,1},{2,6},{6,10},{... | collective-permute-start | bytes 393224 | tf_op jit(solution)/shard_map/ppermute | solution.py:11
  85.6 0.9 slice_bitcast_fusion.1
  86.5 2.1 %collective-permute-done.17 = f32[256,128]{1,0:T(8,128)S(1)} collective-permute-done((f32[256,128]{1,0:T(8,128)S(1)}, f32[256,128]{1,0:T(8,128)S(1)}, u32[]{:S(2)}, u32[]{:S(2)}) %collective-permute-start.17) | collective-permute-done | bytes 131104 | tf_op jit(solution)/shard_map/ppermute | solution.py:11
  88.6 7.1 %collective-permute-done.16 = f32[256,128]{1,0:T(8,128)S(1)} collective-permute-done((f32[256,128]{1,0:T(8,128)S(1)}, f32[256,128]{1,0:T(8,128)S(1)}, u32[]{:S(2)}, u32[]{:S(2)}) %collective-permute-start.16) | collective-permute-done | bytes 131104 | tf_op jit(solution)/shard_map/ppermute | solution.py:11
  95.7 1.3 gather_fusion.4
  97.0 1.1 slice_subtract_fusion.2
  98.1 1.7 %convolution_bitcast_fusion.2 = f32[64,128]{1,0:T(8,128)S(1)} fusion(f32[1,1024,128]{2,1,0:T(8,128)S(1)} %copy-done.2, f32[1,768,128]{2,1,0:T(8,128)} %get-tuple-element.4, f32[1,256,128]{2,1,0:T(8,128)S(1)} %bitcast.131, f32[1,64,1024]{2,1,0:T(8,128)S(1)} %copy-done, pred[1024]{0:T(1024)(128)(4,1)S(1)} %iota_compare_fusion), kind=kOutput, calls=%fused_computation.30 | convolution fusion | flops 50724864 | bytes 1344512 | tf_op jit(solution)/shard_map/dot_general | solution.py:59
  99.8 1.7 %collective-permute-start.19 = (f32[64,128]{1,0:T(8,128)S(1)}, f32[64,128]{1,0:T(8,128)S(1)}, u32[]{:S(2)}, u32[]{:S(2)}) collective-permute-start(f32[64,128]{1,0:T(8,128)S(1)} %convolution_bitcast_fusion.2), channel_id=1, source_target_pairs={{0,8},{4,12},{8,0},{12,4},{1,9},{5,13},{9,1},{13,5},{2,10},{6,14},... | collective-permute-start | bytes 98312 | tf_op jit(solution)/shard_map/ppermute | solution.py:11
  101.6 1.9 %collective-permute-start.18 = (f32[64,128]{1,0:T(8,128)S(1)}, f32[64,128]{1,0:T(8,128)S(1)}, u32[]{:S(2)}, u32[]{:S(2)}) collective-permute-start(f32[64,128]{1,0:T(8,128)S(1)} %convolution_bitcast_fusion.2), channel_id=1, source_target_pairs={{0,4},{4,8},{8,12},{12,0},{1,5},{5,9},{9,13},{13,1},{2,6},{6,10},{... | collective-permute-start | bytes 98312 | tf_op jit(solution)/shard_map/ppermute | solution.py:11
  103.8 0.9 collective-permute-done.19
  104.7 2.6 %collective-permute-done.18 = f32[64,128]{1,0:T(8,128)S(1)} collective-permute-done((f32[64,128]{1,0:T(8,128)S(1)}, f32[64,128]{1,0:T(8,128)S(1)}, u32[]{:S(2)}, u32[]{:S(2)}) %collective-permute-start.18) | collective-permute-done | bytes 32800 | tf_op jit(solution)/shard_map/ppermute | solution.py:11
  107.7 1.7 %collective-permute-start.23 = (f32[64,128]{1,0:T(8,128)S(1)}, f32[64,128]{1,0:T(8,128)S(1)}, u32[]{:S(2)}, u32[]{:S(2)}) collective-permute-start(f32[64,128]{1,0:T(8,128)S(1)} %get-tuple-element.9), channel_id=1, source_target_pairs={{0,3},{1,0},{2,1},{3,2},{4,7},{5,4},{6,5},{7,6},{8,11},{9,8},{10,9... | collective-permute-start | bytes 98312 | tf_op jit(solution)/shard_map/ppermute | solution.py:11
  110.0 1.1 collective-permute-done.21
  111.1 2.3 %collective-permute-done.22 = f32[64,128]{1,0:T(8,128)S(1)} collective-permute-done((f32[64,128]{1,0:T(8,128)S(1)}, f32[64,128]{1,0:T(8,128)S(1)}, u32[]{:S(2)}, u32[]{:S(2)}) %collective-permute-start.22) | collective-permute-done | bytes 32800 | tf_op jit(solution)/shard_map/ppermute | solution.py:11
  113.4 2.5 %fusion.31 = f32[1024,128]{1,0:T(8,128)S(1)} fusion(f32[768,128]{1,0:T(8,128)} %get-tuple-element.5, f32[256,128]{1,0:T(8,128)S(1)} %slice_subtract_fusion.2, f32[1,1024,128]{2,1,0:T(8,128)S(1)} %copy-done.2, f32[1,64,1024]{2,1,0:T(8,128)S(1)} %copy-done, pred[1024]{0:T(1024)(128)(4,1)S(1)} %compare_reduce_fusion, ...), kind=kOutput, calls=%fused_computation.35 | convolution fusion | flops 53633024 | bytes 3540996 | tf_op jit(solution)/shard_map/dot_general | solution.py:76
  116.0 1.8 %fusion.23 = f32[1024,128]{1,0:T(8,128)S(1)} fusion(f32[1024,128]{1,0:T(8,128)S(1)} %fusion.31, f32[1,1024,1024]{2,1,0:T(8,128)S(1)} %copy-done.1), kind=kOutput, calls=%fused_computation.26 | convolution fusion | flops 805306368 | bytes 5242880 | tf_op jit(solution)/shard_map/dot_general | solution.py:49
  117.8 0.9 collective-permute-start.26
  118.7 0.8 collective-permute-start.25
  119.9 3.4 %collective-permute-done.26 = f32[256,128]{1,0:T(8,128)S(1)} collective-permute-done((f32[256,128]{1,0:T(8,128)S(1)}, f32[256,128]{1,0:T(8,128)S(1)}, u32[]{:S(2)}, u32[]{:S(2)}) %collective-permute-start.26) | collective-permute-done | bytes 131104 | tf_op jit(solution)/shard_map/ppermute | solution.py:11
  123.3 6.8 %collective-permute-done.25 = f32[256,128]{1,0:T(8,128)S(1)} collective-permute-done((f32[256,128]{1,0:T(8,128)S(1)}, f32[256,128]{1,0:T(8,128)S(1)}, u32[]{:S(2)}, u32[]{:S(2)}) %collective-permute-start.25) | collective-permute-done | bytes 131104 | tf_op jit(solution)/shard_map/ppermute | solution.py:11
  130.1 0.7 gather_fusion.5
  130.9 4.2 %fusion.26 = f32[1024,128]{1,0:T(8,128)S(1)} fusion(f32[1,1024,1024]{2,1,0:T(8,128)} %param.9, f32[1024,128]{1,0:T(8,128)S(1)} %fusion.31, f32[768,128]{1,0:T(8,128)S(1)} %slice.71, f32[256,128]{1,0:T(8,128)S(1)} %slice_subtract_fusion.1, f32[1,1024,128]{2,1,0:T(8,128)S(1)} %copy-done.2, pred[1024]{0:T(1024)(128)(4,1)S(1)} %compare_reduce_fusion, ...), kind=kOutput, calls=%fused_computation.27 | convolution fusion | flops 806354944 | bytes 6293504 | tf_op jit(solution)/shard_map/dot_general | solution.py:49
  135.2 1.5 collective-permute-start.28
  136.6 1.9 %collective-permute-start.27 = (f32[256,128]{1,0:T(8,128)S(1)}, f32[256,128]{1,0:T(8,128)S(1)}, u32[]{:S(2)}, u32[]{:S(2)}) collective-permute-start(f32[256,128]{1,0:T(8,128)S(1)} %slice.72), channel_id=1, source_target_pairs={{0,4},{4,8},{8,12},{12,0},{1,5},{5,9},{9,13},{13,1},{2,6},{6,10},{... | collective-permute-start | bytes 393224 | tf_op jit(solution)/shard_map/ppermute | solution.py:11
  138.6 2.2 %collective-permute-done.29 = f32[256,128]{1,0:T(8,128)S(1)} collective-permute-done((f32[256,128]{1,0:T(8,128)S(1)}, f32[256,128]{1,0:T(8,128)S(1)}, u32[]{:S(2)}, u32[]{:S(2)}) %collective-permute-start.29) | collective-permute-done | bytes 131104 | tf_op jit(solution)/shard_map/ppermute | solution.py:11
  140.9 7.4 %collective-permute-done.28 = f32[256,128]{1,0:T(8,128)S(1)} collective-permute-done((f32[256,128]{1,0:T(8,128)S(1)}, f32[256,128]{1,0:T(8,128)S(1)}, u32[]{:S(2)}, u32[]{:S(2)}) %collective-permute-start.28) | collective-permute-done | bytes 131104 | tf_op jit(solution)/shard_map/ppermute | solution.py:11
  148.3 1.3 gather_fusion.6
  149.7 0.9 slice_subtract_fusion
  150.6 2.5 %fusion.37 = f32[1,1024,128]{2,1,0:T(8,128)} fusion(f32[768,128]{1,0:T(8,128)S(1)} %get-tuple-element.3, f32[256,128]{1,0:T(8,128)S(1)} %slice_subtract_fusion, f32[1,1024,128]{2,1,0:T(8,128)S(1)} %copy-done.2, pred[1024]{0:T(1024)(128)(4,1)S(1)} %compare_reduce_fusion, pred[1024]{0:T(1024)(128)(4,1)S(1)} %iota_compare_fusion, f32[1024,128]{1,0:T(8,128)S(1)} %fusion.31, ...), kind=kLoop, calls=%fused_computation.44 | loop fusion | flops 2097152 | bytes 2623488 | tf_op jit(solution)/shard_map/broadcast_in_dim | solution.py:85
  153.1 1.0 fusion.64
  (72 shorter events, 5.1 us)
Async XLA Ops:
  0.6 24.0 %copy-start = (f32[1,64,1024]{2,1,0:T(8,128)S(1)}, f32[1,64,1024]{2,1,0:T(8,128)}, u32[]{:S(2)}) copy-start(f32[1,64,1024]{2,1,0:T(8,128)} %param.11) | copy-start | bytes 786436
  0.6 11.1 %copy-start.7 = (s32[1,256]{1,0:T(1,128)S(1)}, s32[1,256]{1,0:T(1,128)}, u32[]{:S(2)}) copy-start(s32[1,256]{1,0:T(1,128)} %param.15) | copy-start | bytes 3076
  0.7 11.1 %copy-start.8 = (s32[1,256,1]{1,2,0:T(1,128)S(1)}, s32[1,256,1]{1,2,0:T(1,128)}, u32[]{:S(2)}) copy-start(s32[1,256,1]{1,2,0:T(1,128)} %param.14) | copy-start | bytes 3076
  0.7 11.8 %copy-start.6 = (f32[256,256]{1,0:T(8,128)S(1)}, f32[256,256]{1,0:T(8,128)}, u32[]{:S(2)}) copy-start(f32[256,256]{1,0:T(8,128)} %param.10) | copy-start | bytes 786436
  0.7 24.0 %copy-start.2 = (f32[1,1024,128]{2,1,0:T(8,128)S(1)}, f32[1,1024,128]{2,1,0:T(8,128)}, u32[]{:S(2)}) copy-start(f32[1,1024,128]{2,1,0:T(8,128)} %param.12) | copy-start | bytes 1572868
  4.9 34.8 %copy-start.3 = (f32[1,1024,128]{2,1,0:T(8,128)S(1)}, f32[1,1024,128]{2,1,0:T(8,128)}, u32[]{:S(2)}) copy-start(f32[1,1024,128]{2,1,0:T(8,128)} %param.13) | copy-start | bytes 1572868
  4.9 9.0 %collective-permute-start.2 = (f32[256,128]{1,0:T(8,128)S(1)}, f32[256,128]{1,0:T(8,128)}, u32[]{:S(2)}, u32[]{:S(2)}) collective-permute-start(f32[256,128]{1,0:T(8,128)S(1)} %slice.62), channel_id=1, source_target_pairs={{0,12},{4,0},{8,4},{12,8},{1,13},{5,1},{9,5},{13,9},{2,14},{6,2},{... | collective-permute-start | bytes 393224 | tf_op jit(solution)/shard_map/ppermute | solution.py:11
  10.0 11.3 %collective-permute-start.1 = (f32[256,128]{1,0:T(8,128)S(1)}, f32[256,128]{1,0:T(8,128)}, u32[]{:S(2)}, u32[]{:S(2)}) collective-permute-start(f32[256,128]{1,0:T(8,128)S(1)} %slice.62), channel_id=1, source_target_pairs={{0,8},{4,12},{8,0},{12,4},{1,9},{5,13},{9,1},{13,5},{2,10},{6,14},... | collective-permute-start | bytes 393224 | tf_op jit(solution)/shard_map/ppermute | solution.py:11
  10.0 11.3 %collective-permute-start = (f32[256,128]{1,0:T(8,128)S(1)}, f32[256,128]{1,0:T(8,128)}, u32[]{:S(2)}, u32[]{:S(2)}) collective-permute-start(f32[256,128]{1,0:T(8,128)S(1)} %slice.62), channel_id=1, source_target_pairs={{0,4},{4,8},{8,12},{12,0},{1,5},{5,9},{9,13},{13,1},{2,6},{6,10},{... | collective-permute-start | bytes 393224 | tf_op jit(solution)/shard_map/ppermute | solution.py:11
  25.1 5.5 %collective-permute-start.5 = (f32[64,128]{1,0:T(8,128)S(1)}, f32[64,128]{1,0:T(8,128)S(1)}, u32[]{:S(2)}, u32[]{:S(2)}) collective-permute-start(f32[64,128]{1,0:T(8,128)S(1)} %convolution_bitcast_fusion.3), channel_id=1, source_target_pairs={{0,12},{4,0},{8,4},{12,8},{1,13},{5,1},{9,5},{13,9},{2,14},{6,2},{... | collective-permute-start | bytes 98312 | tf_op jit(solution)/shard_map/ppermute | solution.py:11
  26.8 5.4 %collective-permute-start.4 = (f32[64,128]{1,0:T(8,128)S(1)}, f32[64,128]{1,0:T(8,128)S(1)}, u32[]{:S(2)}, u32[]{:S(2)}) collective-permute-start(f32[64,128]{1,0:T(8,128)S(1)} %convolution_bitcast_fusion.3), channel_id=1, source_target_pairs={{0,8},{4,12},{8,0},{12,4},{1,9},{5,13},{9,1},{13,5},{2,10},{6,14},... | collective-permute-start | bytes 98312 | tf_op jit(solution)/shard_map/ppermute | solution.py:11
  27.9 5.7 %collective-permute-start.3 = (f32[64,128]{1,0:T(8,128)S(1)}, f32[64,128]{1,0:T(8,128)S(1)}, u32[]{:S(2)}, u32[]{:S(2)}) collective-permute-start(f32[64,128]{1,0:T(8,128)S(1)} %convolution_bitcast_fusion.3), channel_id=1, source_target_pairs={{0,4},{4,8},{8,12},{12,0},{1,5},{5,9},{9,13},{13,1},{2,6},{6,10},{... | collective-permute-start | bytes 98312 | tf_op jit(solution)/shard_map/ppermute | solution.py:11
  34.0 4.0 %collective-permute-start.6 = (f32[64,128]{1,0:T(8,128)S(1)}, f32[64,128]{1,0:T(8,128)S(1)}, u32[]{:S(2)}, u32[]{:S(2)}) collective-permute-start(f32[64,128]{1,0:T(8,128)S(1)} %get-tuple-element.11), channel_id=1, source_target_pairs={{0,1},{1,2},{2,3},{3,0},{4,5},{5,6},{6,7},{7,4},{8,9},{9,10},{10,1... | collective-permute-start | bytes 98312 | tf_op jit(solution)/shard_map/ppermute | solution.py:11
  34.1 4.0 %collective-permute-start.8 = (f32[64,128]{1,0:T(8,128)S(1)}, f32[64,128]{1,0:T(8,128)S(1)}, u32[]{:S(2)}, u32[]{:S(2)}) collective-permute-start(f32[64,128]{1,0:T(8,128)S(1)} %get-tuple-element.12), channel_id=1, source_target_pairs={{0,3},{1,0},{2,1},{3,2},{4,7},{5,4},{6,5},{7,6},{8,11},{9,8},{10,9... | collective-permute-start | bytes 98312 | tf_op jit(solution)/shard_map/ppermute | solution.py:11
  35.8 3.9 %collective-permute-start.7 = (f32[64,128]{1,0:T(8,128)S(1)}, f32[64,128]{1,0:T(8,128)S(1)}, u32[]{:S(2)}, u32[]{:S(2)}) collective-permute-start(f32[64,128]{1,0:T(8,128)S(1)} %get-tuple-element.13), channel_id=1, source_target_pairs={{0,2},{1,3},{2,0},{3,1},{4,6},{5,7},{6,4},{7,5},{8,10},{9,11},{10,... | collective-permute-start | bytes 98312 | tf_op jit(solution)/shard_map/ppermute | solution.py:11
  44.5 5.5 %collective-permute-start.11 = (f32[256,128]{1,0:T(8,128)S(1)}, f32[256,128]{1,0:T(8,128)S(1)}, u32[]{:S(2)}, u32[]{:S(2)}) collective-permute-start(f32[256,128]{1,0:T(8,128)S(1)} %slice.64), channel_id=1, source_target_pairs={{0,12},{4,0},{8,4},{12,8},{1,13},{5,1},{9,5},{13,9},{2,14},{6,2},{... | collective-permute-start | bytes 393224 | tf_op jit(solution)/shard_map/ppermute | solution.py:11
  45.0 12.3 %collective-permute-start.10 = (f32[256,128]{1,0:T(8,128)S(1)}, f32[256,128]{1,0:T(8,128)S(1)}, u32[]{:S(2)}, u32[]{:S(2)}) collective-permute-start(f32[256,128]{1,0:T(8,128)S(1)} %slice.64), channel_id=1, source_target_pairs={{0,8},{4,12},{8,0},{12,4},{1,9},{5,13},{9,1},{13,5},{2,10},{6,14},... | collective-permute-start | bytes 393224 | tf_op jit(solution)/shard_map/ppermute | solution.py:11
  46.2 11.2 %collective-permute-start.9 = (f32[256,128]{1,0:T(8,128)S(1)}, f32[256,128]{1,0:T(8,128)S(1)}, u32[]{:S(2)}, u32[]{:S(2)}) collective-permute-start(f32[256,128]{1,0:T(8,128)S(1)} %slice.64), channel_id=1, source_target_pairs={{0,4},{4,8},{8,12},{12,0},{1,5},{5,9},{9,13},{13,1},{2,6},{6,10},{... | collective-permute-start | bytes 393224 | tf_op jit(solution)/shard_map/ppermute | solution.py:11
  62.3 5.3 %collective-permute-start.14 = (f32[256,128]{1,0:T(8,128)S(1)}, f32[256,128]{1,0:T(8,128)S(1)}, u32[]{:S(2)}, u32[]{:S(2)}) collective-permute-start(f32[256,128]{1,0:T(8,128)S(1)} %slice.66), channel_id=1, source_target_pairs={{0,12},{4,0},{8,4},{12,8},{1,13},{5,1},{9,5},{13,9},{2,14},{6,2},{... | collective-permute-start | bytes 393224 | tf_op jit(solution)/shard_map/ppermute | solution.py:11
  62.4 13.8 %collective-permute-start.13 = (f32[256,128]{1,0:T(8,128)S(1)}, f32[256,128]{1,0:T(8,128)S(1)}, u32[]{:S(2)}, u32[]{:S(2)}) collective-permute-start(f32[256,128]{1,0:T(8,128)S(1)} %slice.66), channel_id=1, source_target_pairs={{0,8},{4,12},{8,0},{12,4},{1,9},{5,13},{9,1},{13,5},{2,10},{6,14},... | collective-permute-start | bytes 393224 | tf_op jit(solution)/shard_map/ppermute | solution.py:11
  64.1 12.0 %collective-permute-start.12 = (f32[256,128]{1,0:T(8,128)S(1)}, f32[256,128]{1,0:T(8,128)S(1)}, u32[]{:S(2)}, u32[]{:S(2)}) collective-permute-start(f32[256,128]{1,0:T(8,128)S(1)} %slice.66), channel_id=1, source_target_pairs={{0,4},{4,8},{8,12},{12,0},{1,5},{5,9},{9,13},{13,1},{2,6},{6,10},{... | collective-permute-start | bytes 393224 | tf_op jit(solution)/shard_map/ppermute | solution.py:11
  78.5 17.2 %copy-start.5 = (f32[256,128]{1,0:T(8,128)}, f32[256,128]{1,0:T(8,128)S(1)}, u32[]{:S(2)}) copy-start(f32[256,128]{1,0:T(8,128)S(1)} %slice_subtract_fusion.3) | copy-start | bytes 393220
  82.7 5.8 %collective-permute-start.17 = (f32[256,128]{1,0:T(8,128)S(1)}, f32[256,128]{1,0:T(8,128)S(1)}, u32[]{:S(2)}, u32[]{:S(2)}) collective-permute-start(f32[256,128]{1,0:T(8,128)S(1)} %slice.68), channel_id=1, source_target_pairs={{0,12},{4,0},{8,4},{12,8},{1,13},{5,1},{9,5},{13,9},{2,14},{6,2},{... | collective-permute-start | bytes 393224 | tf_op jit(solution)/shard_map/ppermute | solution.py:11
  82.8 12.8 %collective-permute-start.16 = (f32[256,128]{1,0:T(8,128)S(1)}, f32[256,128]{1,0:T(8,128)S(1)}, u32[]{:S(2)}, u32[]{:S(2)}) collective-permute-start(f32[256,128]{1,0:T(8,128)S(1)} %slice.68), channel_id=1, source_target_pairs={{0,8},{4,12},{8,0},{12,4},{1,9},{5,13},{9,1},{13,5},{2,10},{6,14},... | collective-permute-start | bytes 393224 | tf_op jit(solution)/shard_map/ppermute | solution.py:11
  83.6 12.0 %collective-permute-start.15 = (f32[256,128]{1,0:T(8,128)S(1)}, f32[256,128]{1,0:T(8,128)S(1)}, u32[]{:S(2)}, u32[]{:S(2)}) collective-permute-start(f32[256,128]{1,0:T(8,128)S(1)} %slice.68), channel_id=1, source_target_pairs={{0,4},{4,8},{8,12},{12,0},{1,5},{5,9},{9,13},{13,1},{2,6},{6,10},{... | collective-permute-start | bytes 393224 | tf_op jit(solution)/shard_map/ppermute | solution.py:11
  97.0 18.9 %copy-start.1 = (f32[1,1024,1024]{2,1,0:T(8,128)S(1)}, f32[1,1024,1024]{2,1,0:T(8,128)}, u32[]{:S(2)}) copy-start(f32[1,1024,1024]{2,1,0:T(8,128)} %param.9) | copy-start | bytes 12582916
  99.8 4.0 %collective-permute-start.20 = (f32[64,128]{1,0:T(8,128)S(1)}, f32[64,128]{1,0:T(8,128)S(1)}, u32[]{:S(2)}, u32[]{:S(2)}) collective-permute-start(f32[64,128]{1,0:T(8,128)S(1)} %convolution_bitcast_fusion.2), channel_id=1, source_target_pairs={{0,12},{4,0},{8,4},{12,8},{1,13},{5,1},{9,5},{13,9},{2,14},{6,2},{... | collective-permute-start | bytes 98312 | tf_op jit(solution)/shard_map/ppermute | solution.py:11
  99.8 4.9 %collective-permute-start.19 = (f32[64,128]{1,0:T(8,128)S(1)}, f32[64,128]{1,0:T(8,128)S(1)}, u32[]{:S(2)}, u32[]{:S(2)}) collective-permute-start(f32[64,128]{1,0:T(8,128)S(1)} %convolution_bitcast_fusion.2), channel_id=1, source_target_pairs={{0,8},{4,12},{8,0},{12,4},{1,9},{5,13},{9,1},{13,5},{2,10},{6,14},... | collective-permute-start | bytes 98312 | tf_op jit(solution)/shard_map/ppermute | solution.py:11
  101.6 5.7 %collective-permute-start.18 = (f32[64,128]{1,0:T(8,128)S(1)}, f32[64,128]{1,0:T(8,128)S(1)}, u32[]{:S(2)}, u32[]{:S(2)}) collective-permute-start(f32[64,128]{1,0:T(8,128)S(1)} %convolution_bitcast_fusion.2), channel_id=1, source_target_pairs={{0,4},{4,8},{8,12},{12,0},{1,5},{5,9},{9,13},{13,1},{2,6},{6,10},{... | collective-permute-start | bytes 98312 | tf_op jit(solution)/shard_map/ppermute | solution.py:11
  107.7 3.4 %collective-permute-start.21 = (f32[64,128]{1,0:T(8,128)S(1)}, f32[64,128]{1,0:T(8,128)S(1)}, u32[]{:S(2)}, u32[]{:S(2)}) collective-permute-start(f32[64,128]{1,0:T(8,128)S(1)} %get-tuple-element.8), channel_id=1, source_target_pairs={{0,1},{1,2},{2,3},{3,0},{4,5},{5,6},{6,7},{7,4},{8,9},{9,10},{10,1... | collective-permute-start | bytes 98312 | tf_op jit(solution)/shard_map/ppermute | solution.py:11
  107.7 3.3 %collective-permute-start.23 = (f32[64,128]{1,0:T(8,128)S(1)}, f32[64,128]{1,0:T(8,128)S(1)}, u32[]{:S(2)}, u32[]{:S(2)}) collective-permute-start(f32[64,128]{1,0:T(8,128)S(1)} %get-tuple-element.9), channel_id=1, source_target_pairs={{0,3},{1,0},{2,1},{3,2},{4,7},{5,4},{6,5},{7,6},{8,11},{9,8},{10,9... | collective-permute-start | bytes 98312 | tf_op jit(solution)/shard_map/ppermute | solution.py:11
  109.5 3.9 %collective-permute-start.22 = (f32[64,128]{1,0:T(8,128)S(1)}, f32[64,128]{1,0:T(8,128)S(1)}, u32[]{:S(2)}, u32[]{:S(2)}) collective-permute-start(f32[64,128]{1,0:T(8,128)S(1)} %get-tuple-element.10), channel_id=1, source_target_pairs={{0,2},{1,3},{2,0},{3,1},{4,6},{5,7},{6,4},{7,5},{8,10},{9,11},{10,... | collective-permute-start | bytes 98312 | tf_op jit(solution)/shard_map/ppermute | solution.py:11
  117.8 5.5 %collective-permute-start.26 = (f32[256,128]{1,0:T(8,128)S(1)}, f32[256,128]{1,0:T(8,128)S(1)}, u32[]{:S(2)}, u32[]{:S(2)}) collective-permute-start(f32[256,128]{1,0:T(8,128)S(1)} %slice.70), channel_id=1, source_target_pairs={{0,12},{4,0},{8,4},{12,8},{1,13},{5,1},{9,5},{13,9},{2,14},{6,2},{... | collective-permute-start | bytes 393224 | tf_op jit(solution)/shard_map/ppermute | solution.py:11
  118.7 11.4 %collective-permute-start.25 = (f32[256,128]{1,0:T(8,128)S(1)}, f32[256,128]{1,0:T(8,128)S(1)}, u32[]{:S(2)}, u32[]{:S(2)}) collective-permute-start(f32[256,128]{1,0:T(8,128)S(1)} %slice.70), channel_id=1, source_target_pairs={{0,8},{4,12},{8,0},{12,4},{1,9},{5,13},{9,1},{13,5},{2,10},{6,14},... | collective-permute-start | bytes 393224 | tf_op jit(solution)/shard_map/ppermute | solution.py:11
  119.5 10.6 %collective-permute-start.24 = (f32[256,128]{1,0:T(8,128)S(1)}, f32[256,128]{1,0:T(8,128)S(1)}, u32[]{:S(2)}, u32[]{:S(2)}) collective-permute-start(f32[256,128]{1,0:T(8,128)S(1)} %slice.70), channel_id=1, source_target_pairs={{0,4},{4,8},{8,12},{12,0},{1,5},{5,9},{9,13},{13,1},{2,6},{6,10},{... | collective-permute-start | bytes 393224 | tf_op jit(solution)/shard_map/ppermute | solution.py:11
  130.9 17.4 %copy-start.4 = (f32[256,128]{1,0:T(8,128)}, f32[256,128]{1,0:T(8,128)S(1)}, u32[]{:S(2)}) copy-start(f32[256,128]{1,0:T(8,128)S(1)} %slice_subtract_fusion.1) | copy-start | bytes 393220
  135.1 5.7 %collective-permute-start.29 = (f32[256,128]{1,0:T(8,128)S(1)}, f32[256,128]{1,0:T(8,128)S(1)}, u32[]{:S(2)}, u32[]{:S(2)}) collective-permute-start(f32[256,128]{1,0:T(8,128)S(1)} %slice.72), channel_id=1, source_target_pairs={{0,12},{4,0},{8,4},{12,8},{1,13},{5,1},{9,5},{13,9},{2,14},{6,2},{... | collective-permute-start | bytes 393224 | tf_op jit(solution)/shard_map/ppermute | solution.py:11
  135.2 13.1 %collective-permute-start.28 = (f32[256,128]{1,0:T(8,128)S(1)}, f32[256,128]{1,0:T(8,128)S(1)}, u32[]{:S(2)}, u32[]{:S(2)}) collective-permute-start(f32[256,128]{1,0:T(8,128)S(1)} %slice.72), channel_id=1, source_target_pairs={{0,8},{4,12},{8,0},{12,4},{1,9},{5,13},{9,1},{13,5},{2,10},{6,14},... | collective-permute-start | bytes 393224 | tf_op jit(solution)/shard_map/ppermute | solution.py:11
  136.6 11.7 %collective-permute-start.27 = (f32[256,128]{1,0:T(8,128)S(1)}, f32[256,128]{1,0:T(8,128)S(1)}, u32[]{:S(2)}, u32[]{:S(2)}) collective-permute-start(f32[256,128]{1,0:T(8,128)S(1)} %slice.72), channel_id=1, source_target_pairs={{0,4},{4,8},{8,12},{12,0},{1,5},{5,9},{9,13},{13,1},{2,6},{6,10},{... | collective-permute-start | bytes 393224 | tf_op jit(solution)/shard_map/ppermute | solution.py:11

commit v2 on v1

--- a/solution.py
+++ b/solution.py
@@ -5,10 +5,6 @@
 
 OUTER = 2
 INNER = 3
-
-
-def shifted(block, axis, count, step):
-    return lax.ppermute(block, axis, [(i, (i + step) % count) for i in range(count)])
 
 
 def local(
@@ -35,23 +31,24 @@
     order = operator.shape[0]
     shared = peers.shape[0]
     count = basis.shape[0]
-    my_wide = lax.axis_index("wide")
-    my_narrow = lax.axis_index("narrow")
-    place = lax.rem(my_wide - peers + wide, wide) * shared + rows_wanted
+    cap = 2 * shared // wide
+    same = peers[:, None] == peers[None, :]
+    earlier = lax.iota(jnp.int32, shared)[None, :] < lax.iota(jnp.int32, shared)[:, None]
+    slot = jnp.sum((same & earlier).astype(jnp.int32), axis=1)
+    place = peers * cap + slot
+    hit = lax.iota(jnp.int32, wide * cap)[:, None] == place[None, :]
+    asked = jnp.sum(jnp.where(hit, rows_wanted[None, :], 0), axis=1).reshape(wide, cap)
+    given = lax.all_to_all(asked, "wide", 0, 0, tiled=True).reshape(-1)
     active = (lax.iota(jnp.int32, order) < interface_size[0])[:, None]
     contact = (contact_rows[0] == 1)[:, None]
-    tile = coarse_inverse.reshape(coarse_inverse.shape[0], wide, count)
-    tile = jnp.take(tile, lax.rem(my_wide - jnp.arange(wide) + wide, wide), axis=1)
-    tile = tile.reshape(coarse_inverse.shape)
     residual = jnp.zeros_like(target)
     for outer in range(OUTER):
         for inner in range(INNER):
             image = jnp.dot(operator, mult, precision=high, preferred_element_type=jnp.float32)
             head = image[:shared]
-            whole = jnp.concatenate(
-                [head] + [shifted(head, "wide", wide, d) for d in range(1, wide)], axis=0
-            )
-            across = whole[place]
+            sent = head[given].reshape(wide, cap, -1)
+            came = lax.all_to_all(sent, "wide", 0, 0, tiled=True).reshape(wide * cap, -1)
+            across = came[place]
             jump = jnp.concatenate([head - across, image[shared:]], axis=0)
             residual = jnp.where(active, target - jump, 0.0)
             update = 0.3 * residual
@@ -59,20 +56,20 @@
                 coarse = jnp.dot(
                     basis, residual, precision=high, preferred_element_type=jnp.float32
                 )
-                gathered = jnp.concatenate(
-                    [coarse] + [shifted(coarse, "wide", wide, d) for d in range(1, wide)], axis=0
-                )
+                gathered = lax.all_to_all(
+                    jnp.broadcast_to(coarse[None], (wide,) + coarse.shape),
+                    "wide", 0, 0, tiled=True,
+                ).reshape(wide * count, -1)
                 parts = jnp.dot(
-                    tile, gathered, precision=high, preferred_element_type=jnp.float32
+                    coarse_inverse, gathered, precision=high, preferred_element_type=jnp.float32
                 )
 
-                def part(d):
-                    start = lax.rem(my_narrow + d, narrow) * count
-                    return lax.dynamic_slice_in_dim(parts, start, count, axis=0)
-
-                solved = part(0)
-                for d in range(1, narrow):
-                    solved = solved + shifted(part(d), "narrow", narrow, d)
+                solved = jnp.sum(
+                    lax.all_to_all(
+                        parts.reshape(narrow, count, -1), "narrow", 0, 0, tiled=True
+                    ),
+                    axis=0,
+                )
                 update = update + lax.dot_general(
                     basis,
                     solved,

time: 155 us -> 161 us (1.039)
  blocking collectives: 0 us -> 24.6 us
  waiting for transfers between devices: 69.7 us -> 50.6 us
  local copies, waits for them, and re-layouts: 9.45 us -> 16.8 us
  other arithmetic: 10.1 us -> 6.75 us
  starting transfers between devices: 34.3 us -> 31.4 us
    ppermute x30 -> x0, waiting for transfers between devices: 69.7 us -> none  [shifted(): lax.ppermute(block, axis, [(i, (i + step) % count) for i in range(count)])]
    all_to_all x0 -> x8, waiting for transfers between devices: none -> 50.6 us  [the longest x6 45.4 us: local(): lax.all_to_all(sent, 'wide', 0, 0, tiled=True).reshape(wide * cap, -1)]
    ppermute x30 -> x0, starting transfers between devices: 34.3 us -> none  [shifted(): lax.ppermute(block, axis, [(i, (i + step) % count) for i in range(count)])]
    all_to_all x0 -> x8, starting transfers between devices: none -> 31.4 us  [the longest x6 21.7 us: local(): lax.all_to_all(sent, 'wide', 0, 0, tiled=True).reshape(wide * cap, -1)]
    all_to_all x0 -> x3, blocking collectives: none -> 24.6 us  [the longest x2 17.6 us: local(): lax.all_to_all(jnp.broadcast_to(coarse[None], (wide,) + coarse.shape), 'w...]
    gather x7 -> x12, local copies, waits for them, and re-layouts: 7.4 us -> 14.9 us  [the longest x6 9.9 us: local(): sent = head[given].reshape(wide, cap, -1)]
    sub x6, other arithmetic: 3.85 us -> 0.99 us  [local(): jump = jnp.concatenate([head - across, image[shared:]], axis=0)]
    reduce_sum x0 -> x4, other arithmetic: none -> 2.38 us  [the longest x1 1.41 us: local(): jnp.sum(jnp.where(hit, rows_wanted[None, :], 0), axis=1).reshape(wide, cap)]
  transfers between devices with their start and end apart: 30 -> 8, of which waited for: 20 -> 8; matrix products, arithmetic and copies ran while one was open for 3% -> 3% of each run, Pallas kernels for 0% -> 0%
where the time goes in v2:
time: 161 us; the launch traced here: 160 us
  waiting for transfers between devices  50.6 us (31%)
  starting transfers between devices  31.4 us (20%)
  matrix products  28.2 us (18%)
  blocking collectives  24.6 us (15%)
  local copies, waits for them, and re-layouts  16.8 us (10%)
  other arithmetic  6.75 us (4%)
  between operations  1.74 us (1%)
    all_to_all x6, waiting for transfers between devices, local(): lax.all_to_all(sent, 'wide', 0, 0, tiled=True).reshape(wide * cap, -1)  45.4 us
    dot_general x6, matrix products, local(): jnp.dot(operator, mult, precision=high, preferred_element_type=jnp.float32)  22.4 us
    all_to_all x6, starting transfers between devices, local(): lax.all_to_all(sent, 'wide', 0, 0, tiled=True).reshape(wide * cap, -1)  21.7 us
    all_to_all x2, blocking collectives, local(): lax.all_to_all(jnp.broadcast_to(coarse[None], (wide,) + coarse.shape), 'w...  17.6 us
    gather x6, local copies, waits for them, and re-layouts, local(): sent = head[given].reshape(wide, cap, -1)  9.9 us
    all_to_all x1, blocking collectives, local(): lax.all_to_all(parts.reshape(narrow, count, -1), 'narrow', 0, 0, tiled=True)  7.02 us
    all_to_all x1, starting transfers between devices, local(): given = lax.all_to_all(asked, 'wide', 0, 0, tiled=True).reshape(-1)  6.32 us
    gather x6, local copies, waits for them, and re-layouts, local(): across = came[place]  4.99 us
  transfers between devices with their start and end apart: 8, of which 8 were waited for; matrix products, arithmetic and copies ran while one was open for 3% of the time, Pallas kernels for 0%

profile of v2, /device:TPU:0, one launch (start us, length us, event | category | flops | bytes accessed | tf_op | source)
XLA Modules:
  0.0 160.1 jit_solution(16634333537891526214)
XLA Ops:
  0.6 0.0 copy-start
  0.6 0.0 copy-start.5
  0.7 1.0 convert_reduce_fusion
  1.6 0.7 multiply_add_fusion
  2.3 1.4 select_reduce_fusion
  3.7 6.3 %all-to-all-start = ((s32[4,1,128]{2,1,0:T(1,128)}), s32[4,1,128]{2,1,0:T(1,128)S(1)}, u32[]{:S(2)}, u32[]{:S(2)}) async-start(s32[4,1,128]{2,1,0:T(1,128)} %bitcast.6), calls=%async_computation | async-start | bytes 4096 | tf_op jit(solution)/shard_map/all_to_all | solution.py:41
  10.0 4.1 %fusion.10 = f32[1024,128]{1,0:T(8,128)S(1)} fusion(f32[1,1024,1024]{2,1,0:T(8,128)} %param.9, f32[1,1024,128]{2,1,0:T(8,128)} %param.13), kind=kOutput, calls=%fused_computation.22 | convolution fusion | flops 805306368 | bytes 5242880 | tf_op jit(solution)/shard_map/dot_general | solution.py:47
  14.1 0.0 copy-start.2
  14.1 0.0 copy-start.4
  14.2 0.0 copy-done.5
  14.9 0.6 all-to-all-done
  15.5 0.0 copy-start.6
  15.5 0.0 copy-start.3
  15.5 1.6 %gather_fusion = f32[512,128]{1,0:T(8,128)} fusion(f32[256,128]{1,0:T(8,128)S(1)} %slice.72, s32[1024]{0:T(1024)S(1)} %pad_clamp_fusion.1), kind=kCustom, calls=%fused_computation | custom fusion | bytes 526336 | tf_op jit(solution)/shard_map/gather | solution.py:49
  17.2 4.5 %all-to-all-start.1 = ((f32[4,128,128]{2,1,0:T(8,128)}), f32[4,128,128]{2,1,0:T(8,128)S(1)}, u32[]{:S(2)}, u32[]{:S(2)}) async-start(f32[4,128,128]{2,1,0:T(8,128)} %bitcast.9), calls=%async_computation.1 | async-start | bytes 524288 | tf_op jit(solution)/shard_map/all_to_all | solution.py:50
  21.7 0.1 fusion.84
  21.8 8.2 %all-to-all-done.1 = f32[4,128,128]{2,1,0:T(8,128)S(1)} async-done(((f32[4,128,128]{2,1,0:T(8,128)}), f32[4,128,128]{2,1,0:T(8,128)S(1)}, u32[]{:S(2)}, u32[]{:S(2)}) %all-to-all-start.1) | async-done | bytes 262176 | tf_op jit(solution)/shard_map/all_to_all | solution.py:50
  30.0 0.7 gather_fusion.1
  30.8 0.0 copy-done
  30.8 0.0 copy-done.2
  30.8 0.4 convolution_bitcast_fusion.5
  31.3 8.4 %all_to_all.59 = f32[4,64,128]{2,1,0:T(8,128)S(1)} all-to-all(f32[4,64,128]{2,1,0:T(8,128)S(1)} %broadcast_in_dim.139), channel_id=1, replica_groups=mesh['groups'=2,'wide'=4,'narrow'=4] {'wide'}, dimensions={0} | all-to-all | bytes 262144 | tf_op jit(solution)/shard_map/all_to_all | solution.py:59
  39.7 0.3 convolution_bitcast_fusion.3
  40.0 0.8 copy.27
  40.8 3.3 %all-to-all-start.3 = ((f32[4,64,128]{2,1,0:T(8,128)}), f32[4,64,128]{2,1,0:T(8,128)S(1)}, u32[]{:S(2)}, u32[]{:S(2)}) async-start(f32[4,64,128]{2,1,0:T(8,128)} %bitcast.21), calls=%async_computation.3 | async-start | bytes 262144 | tf_op jit(solution)/shard_map/all_to_all | solution.py:68
  44.1 4.6 %all-to-all-done.3 = f32[4,64,128]{2,1,0:T(8,128)S(1)} async-done(((f32[4,64,128]{2,1,0:T(8,128)}), f32[4,64,128]{2,1,0:T(8,128)S(1)}, u32[]{:S(2)}, u32[]{:S(2)}) %all-to-all-start.3) | async-done | bytes 131104 | tf_op jit(solution)/shard_map/all_to_all | solution.py:68
  48.7 0.8 fusion.32
  49.5 4.0 %fusion.14 = f32[1024,128]{1,0:T(8,128)S(1)} fusion(f32[1024,128]{1,0:T(8,128)S(1)} %fusion.32, f32[1,1024,1024]{2,1,0:T(8,128)} %param.9), kind=kOutput, calls=%fused_computation.28 | convolution fusion | flops 805306368 | bytes 5242880 | tf_op jit(solution)/shard_map/dot_general | solution.py:47
  53.5 1.6 %gather_fusion.2 = f32[512,128]{1,0:T(8,128)} fusion(f32[256,128]{1,0:T(8,128)S(1)} %slice.74, s32[1024]{0:T(1024)S(1)} %pad_clamp_fusion.1), kind=kCustom, calls=%fused_computation.2 | custom fusion | bytes 526336 | tf_op jit(solution)/shard_map/gather | solution.py:49
  55.2 3.4 %all-to-all-start.4 = ((f32[4,128,128]{2,1,0:T(8,128)}), f32[4,128,128]{2,1,0:T(8,128)S(1)}, u32[]{:S(2)}, u32[]{:S(2)}) async-start(f32[4,128,128]{2,1,0:T(8,128)} %bitcast.24), calls=%async_computation.4 | async-start | bytes 524288 | tf_op jit(solution)/shard_map/all_to_all | solution.py:50
  58.6 8.8 %all-to-all-done.4 = f32[4,128,128]{2,1,0:T(8,128)S(1)} async-done(((f32[4,128,128]{2,1,0:T(8,128)}), f32[4,128,128]{2,1,0:T(8,128)S(1)}, u32[]{:S(2)}, u32[]{:S(2)}) %all-to-all-start.4) | async-done | bytes 262176 | tf_op jit(solution)/shard_map/all_to_all | solution.py:50
  67.4 0.7 gather_fusion.3
  68.1 4.1 %fusion.17 = f32[1024,128]{1,0:T(8,128)S(1)} fusion(f32[1,1024,1024]{2,1,0:T(8,128)} %param.9, f32[1024,128]{1,0:T(8,128)S(1)} %fusion.32, f32[768,128]{1,0:T(8,128)S(1)} %slice.75, f32[256,128]{1,0:T(8,128)S(1)} %slice_subtract_fusion.4, f32[1,1024,128]{2,1,0:T(8,128)S(1)} %copy-done.2, pred[1024]{0:T(1024)(128)(4,1)S(1)} %compare_reduce_fusion, ...), kind=kOutput, calls=%fused_computation.29 | convolution fusion | flops 806354944 | bytes 6293504 | tf_op jit(solution)/shard_map/dot_general | solution.py:47
  72.3 1.6 %gather_fusion.4 = f32[512,128]{1,0:T(8,128)} fusion(f32[256,128]{1,0:T(8,128)S(1)} %slice.76, s32[1024]{0:T(1024)S(1)} %pad_clamp_fusion.1), kind=kCustom, calls=%fused_computation.4 | custom fusion | bytes 526336 | tf_op jit(solution)/shard_map/gather | solution.py:49
  73.9 3.4 %all-to-all-start.5 = ((f32[4,128,128]{2,1,0:T(8,128)}), f32[4,128,128]{2,1,0:T(8,128)S(1)}, u32[]{:S(2)}, u32[]{:S(2)}) async-start(f32[4,128,128]{2,1,0:T(8,128)} %bitcast.27), calls=%async_computation.5 | async-start | bytes 524288 | tf_op jit(solution)/shard_map/all_to_all | solution.py:50
  77.4 7.0 %all-to-all-done.5 = f32[4,128,128]{2,1,0:T(8,128)S(1)} async-done(((f32[4,128,128]{2,1,0:T(8,128)}), f32[4,128,128]{2,1,0:T(8,128)S(1)}, u32[]{:S(2)}, u32[]{:S(2)}) %all-to-all-start.5) | async-done | bytes 262176 | tf_op jit(solution)/shard_map/all_to_all | solution.py:50
  84.3 0.7 gather_fusion.5
  85.1 4.2 %fusion.20 = f32[1024,128]{1,0:T(8,128)S(1)} fusion(f32[1,1024,1024]{2,1,0:T(8,128)} %param.9, f32[768,128]{1,0:T(8,128)S(1)} %slice.77, f32[256,128]{1,0:T(8,128)S(1)} %slice_subtract_fusion.3, f32[1,1024,128]{2,1,0:T(8,128)S(1)} %copy-done.2, pred[1024]{0:T(1024)(128)(4,1)S(1)} %compare_reduce_fusion, pred[1024]{0:T(1024)(128)(4,1)S(1)} %iota_compare_fusion.2, ...), kind=kOutput, calls=%fused_computation.30 | convolution fusion | flops 807403520 | bytes 6817792 | tf_op jit(solution)/shard_map/dot_general | solution.py:47
  89.3 1.6 %gather_fusion.6 = f32[512,128]{1,0:T(8,128)} fusion(f32[256,128]{1,0:T(8,128)S(1)} %slice.78, s32[1024]{0:T(1024)S(1)} %pad_clamp_fusion.1), kind=kCustom, calls=%fused_computation.6 | custom fusion | bytes 526336 | tf_op jit(solution)/shard_map/gather | solution.py:49
  91.0 3.6 %all-to-all-start.6 = ((f32[4,128,128]{2,1,0:T(8,128)}), f32[4,128,128]{2,1,0:T(8,128)S(1)}, u32[]{:S(2)}, u32[]{:S(2)}) async-start(f32[4,128,128]{2,1,0:T(8,128)} %bitcast.30), calls=%async_computation.6 | async-start | bytes 524288 | tf_op jit(solution)/shard_map/all_to_all | solution.py:50
  94.5 0.8 fusion.83
  95.3 5.8 %all-to-all-done.6 = f32[4,128,128]{2,1,0:T(8,128)S(1)} async-done(((f32[4,128,128]{2,1,0:T(8,128)}), f32[4,128,128]{2,1,0:T(8,128)S(1)}, u32[]{:S(2)}, u32[]{:S(2)}) %all-to-all-start.6) | async-done | bytes 262176 | tf_op jit(solution)/shard_map/all_to_all | solution.py:50
  101.1 1.3 gather_fusion.7
  102.5 0.9 slice_subtract_fusion.2
  103.4 0.4 convolution_bitcast_fusion.4
  103.8 9.2 %all_to_all.60 = f32[4,64,128]{2,1,0:T(8,128)S(1)} all-to-all(f32[4,64,128]{2,1,0:T(8,128)S(1)} %broadcast_in_dim.140), channel_id=1, replica_groups=mesh['groups'=2,'wide'=4,'narrow'=4] {'wide'}, dimensions={0} | all-to-all | bytes 262144 | tf_op jit(solution)/shard_map/all_to_all | solution.py:59
  113.0 1.2 convolution_bitcast_fusion.2
  114.2 0.1 copy.32
  114.3 7.0 %all_to_all.61 = f32[4,64,128]{2,1,0:T(8,128)S(1)} all-to-all(f32[4,64,128]{2,1,0:T(8,128)S(1)} %bitcast.157), channel_id=1, replica_groups=mesh['groups'=2,'wide'=4,'narrow'=4] {'narrow'}, dimensions={0} | all-to-all | bytes 262144 | tf_op jit(solution)/shard_map/all_to_all | solution.py:68
  121.4 0.0 copy-start.1
  121.4 2.7 %fusion.31 = f32[1024,128]{1,0:T(8,128)S(1)} fusion(f32[64,128]{1,0:T(8,128)S(1)} %reduce_sum.42, f32[768,128]{1,0:T(8,128)} %get-tuple-element.4, f32[256,128]{1,0:T(8,128)S(1)} %slice_subtract_fusion.2, f32[1,1024,128]{2,1,0:T(8,128)S(1)} %copy-done.2, f32[1,64,1024]{2,1,0:T(8,128)S(1)} %copy-done, pred[1024]{0:T(1024)(128)(4,1)S(1)} %compare_reduce_fusion, ...), kind=kOutput, calls=%fused_computation.42 | convolution fusion | flops 53608448 | bytes 3442688 | tf_op jit(solution)/shard_map/dot_general | solution.py:73
  124.1 1.8 %fusion.23 = f32[1024,128]{1,0:T(8,128)S(1)} fusion(f32[1024,128]{1,0:T(8,128)S(1)} %fusion.31, f32[1,1024,1024]{2,1,0:T(8,128)S(1)} %copy-done.1), kind=kOutput, calls=%fused_computation.31 | convolution fusion | flops 805306368 | bytes 5242880 | tf_op jit(solution)/shard_map/dot_general | solution.py:47
  125.9 1.6 %gather_fusion.8 = f32[512,128]{1,0:T(8,128)} fusion(f32[256,128]{1,0:T(8,128)S(1)} %slice.80, s32[1024]{0:T(1024)S(1)} %pad_clamp_fusion.1), kind=kCustom, calls=%fused_computation.8 | custom fusion | bytes 526336 | tf_op jit(solution)/shard_map/gather | solution.py:49
  127.6 3.4 %all-to-all-start.9 = ((f32[4,128,128]{2,1,0:T(8,128)}), f32[4,128,128]{2,1,0:T(8,128)S(1)}, u32[]{:S(2)}, u32[]{:S(2)}) async-start(f32[4,128,128]{2,1,0:T(8,128)} %bitcast.41), calls=%async_computation.9 | async-start | bytes 524288 | tf_op jit(solution)/shard_map/all_to_all | solution.py:50
  131.0 8.8 %all-to-all-done.9 = f32[4,128,128]{2,1,0:T(8,128)S(1)} async-done(((f32[4,128,128]{2,1,0:T(8,128)}), f32[4,128,128]{2,1,0:T(8,128)S(1)}, u32[]{:S(2)}, u32[]{:S(2)}) %all-to-all-start.9) | async-done | bytes 262176 | tf_op jit(solution)/shard_map/all_to_all | solution.py:50
  139.8 0.7 gather_fusion.9
  140.5 4.1 %fusion.26 = f32[1024,128]{1,0:T(8,128)S(1)} fusion(f32[1,1024,1024]{2,1,0:T(8,128)} %param.9, f32[1024,128]{1,0:T(8,128)S(1)} %fusion.31, f32[768,128]{1,0:T(8,128)S(1)} %slice.81, f32[256,128]{1,0:T(8,128)S(1)} %slice_subtract_fusion.1, f32[1,1024,128]{2,1,0:T(8,128)S(1)} %copy-done.2, pred[1024]{0:T(1024)(128)(4,1)S(1)} %compare_reduce_fusion, ...), kind=kOutput, calls=%fused_computation.32 | convolution fusion | flops 806354944 | bytes 6293504 | tf_op jit(solution)/shard_map/dot_general | solution.py:47
  144.7 1.6 %gather_fusion.10 = f32[512,128]{1,0:T(8,128)} fusion(f32[256,128]{1,0:T(8,128)S(1)} %slice.82, s32[1024]{0:T(1024)S(1)} %pad_clamp_fusion.1), kind=kCustom, calls=%fused_computation.10 | custom fusion | bytes 526336 | tf_op jit(solution)/shard_map/gather | solution.py:49
  146.3 3.4 %all-to-all-start.10 = ((f32[4,128,128]{2,1,0:T(8,128)}), f32[4,128,128]{2,1,0:T(8,128)S(1)}, u32[]{:S(2)}, u32[]{:S(2)}) async-start(f32[4,128,128]{2,1,0:T(8,128)} %bitcast.44), calls=%async_computation.10 | async-start | bytes 524288 | tf_op jit(solution)/shard_map/all_to_all | solution.py:50
  149.8 0.1 slice_bitcast_fusion
  149.8 6.9 %all-to-all-done.10 = f32[4,128,128]{2,1,0:T(8,128)S(1)} async-done(((f32[4,128,128]{2,1,0:T(8,128)}), f32[4,128,128]{2,1,0:T(8,128)S(1)}, u32[]{:S(2)}, u32[]{:S(2)}) %all-to-all-start.10) | async-done | bytes 262176 | tf_op jit(solution)/shard_map/all_to_all | solution.py:50
  156.7 0.7 gather_fusion.11
  157.5 1.6 %fusion.37 = f32[1,1024,128]{2,1,0:T(8,128)} fusion(f32[768,128]{1,0:T(8,128)S(1)} %get-tuple-element.3, f32[256,128]{1,0:T(8,128)S(1)} %slice_subtract_fusion, f32[1,1024,128]{2,1,0:T(8,128)S(1)} %copy-done.2, pred[1024]{0:T(1024)(128)(4,1)S(1)} %compare_reduce_fusion, pred[1024]{0:T(1024)(128)(4,1)S(1)} %iota_compare_fusion.2, f32[1024,128]{1,0:T(8,128)S(1)} %fusion.31, ...), kind=kLoop, calls=%fused_computation.51 | loop fusion | flops 2097152 | bytes 2623488 | tf_op jit(solution)/shard_map/broadcast_in_dim | solution.py:82
  159.1 1.0 fusion.64
  (28 shorter events, 0.3 us)
Async XLA Ops:
  0.6 30.2 %copy-start = (f32[1,64,1024]{2,1,0:T(8,128)S(1)}, f32[1,64,1024]{2,1,0:T(8,128)}, u32[]{:S(2)}) copy-start(f32[1,64,1024]{2,1,0:T(8,128)} %param.11) | copy-start | bytes 786436
  0.6 13.5 %copy-start.5 = (s32[1,256,1]{1,2,0:T(1,128)S(1)}, s32[1,256,1]{1,2,0:T(1,128)}, u32[]{:S(2)}) copy-start(s32[1,256,1]{1,2,0:T(1,128)} %param.14) | copy-start | bytes 3076
  3.7 11.8 %all-to-all-start = ((s32[4,1,128]{2,1,0:T(1,128)}), s32[4,1,128]{2,1,0:T(1,128)S(1)}, u32[]{:S(2)}, u32[]{:S(2)}) async-start(s32[4,1,128]{2,1,0:T(1,128)} %bitcast.6), calls=%async_computation | async-start | bytes 4096 | tf_op jit(solution)/shard_map/all_to_all | solution.py:41
  14.1 16.7 %copy-start.2 = (f32[1,1024,128]{2,1,0:T(8,128)S(1)}, f32[1,1024,128]{2,1,0:T(8,128)}, u32[]{:S(2)}) copy-start(f32[1,1024,128]{2,1,0:T(8,128)} %param.12) | copy-start | bytes 1572868
  14.1 25.6 %copy-start.4 = (f32[256,256]{1,0:T(8,128)S(1)}, f32[256,256]{1,0:T(8,128)}, u32[]{:S(2)}) copy-start(f32[256,256]{1,0:T(8,128)} %param.10) | copy-start | bytes 786436
  15.5 28.6 %copy-start.6 = (s32[1,1024]{1,0:T(1,128)S(1)}, s32[1,1024]{1,0:T(1,128)}, u32[]{:S(2)}) copy-start(s32[1,1024]{1,0:T(1,128)} %param.17) | copy-start | bytes 12292
  15.5 33.2 %copy-start.3 = (f32[1,1024,128]{2,1,0:T(8,128)S(1)}, f32[1,1024,128]{2,1,0:T(8,128)}, u32[]{:S(2)}) copy-start(f32[1,1024,128]{2,1,0:T(8,128)} %param.13) | copy-start | bytes 1572868
  17.2 12.8 %all-to-all-start.1 = ((f32[4,128,128]{2,1,0:T(8,128)}), f32[4,128,128]{2,1,0:T(8,128)S(1)}, u32[]{:S(2)}, u32[]{:S(2)}) async-start(f32[4,128,128]{2,1,0:T(8,128)} %bitcast.9), calls=%async_computation.1 | async-start | bytes 524288 | tf_op jit(solution)/shard_map/all_to_all | solution.py:50
  40.8 7.9 %all-to-all-start.3 = ((f32[4,64,128]{2,1,0:T(8,128)}), f32[4,64,128]{2,1,0:T(8,128)S(1)}, u32[]{:S(2)}, u32[]{:S(2)}) async-start(f32[4,64,128]{2,1,0:T(8,128)} %bitcast.21), calls=%async_computation.3 | async-start | bytes 262144 | tf_op jit(solution)/shard_map/all_to_all | solution.py:68
  55.2 12.2 %all-to-all-start.4 = ((f32[4,128,128]{2,1,0:T(8,128)}), f32[4,128,128]{2,1,0:T(8,128)S(1)}, u32[]{:S(2)}, u32[]{:S(2)}) async-start(f32[4,128,128]{2,1,0:T(8,128)} %bitcast.24), calls=%async_computation.4 | async-start | bytes 524288 | tf_op jit(solution)/shard_map/all_to_all | solution.py:50
  73.9 10.4 %all-to-all-start.5 = ((f32[4,128,128]{2,1,0:T(8,128)}), f32[4,128,128]{2,1,0:T(8,128)S(1)}, u32[]{:S(2)}, u32[]{:S(2)}) async-start(f32[4,128,128]{2,1,0:T(8,128)} %bitcast.27), calls=%async_computation.5 | async-start | bytes 524288 | tf_op jit(solution)/shard_map/all_to_all | solution.py:50
  91.0 10.2 %all-to-all-start.6 = ((f32[4,128,128]{2,1,0:T(8,128)}), f32[4,128,128]{2,1,0:T(8,128)S(1)}, u32[]{:S(2)}, u32[]{:S(2)}) async-start(f32[4,128,128]{2,1,0:T(8,128)} %bitcast.30), calls=%async_computation.6 | async-start | bytes 524288 | tf_op jit(solution)/shard_map/all_to_all | solution.py:50
  121.4 2.7 %copy-start.1 = (f32[1,1024,1024]{2,1,0:T(8,128)S(1)}, f32[1,1024,1024]{2,1,0:T(8,128)}, u32[]{:S(2)}) copy-start(f32[1,1024,1024]{2,1,0:T(8,128)} %param.9) | copy-start | bytes 12582916
  127.6 12.2 %all-to-all-start.9 = ((f32[4,128,128]{2,1,0:T(8,128)}), f32[4,128,128]{2,1,0:T(8,128)S(1)}, u32[]{:S(2)}, u32[]{:S(2)}) async-start(f32[4,128,128]{2,1,0:T(8,128)} %bitcast.41), calls=%async_computation.9 | async-start | bytes 524288 | tf_op jit(solution)/shard_map/all_to_all | solution.py:50
  146.3 10.4 %all-to-all-start.10 = ((f32[4,128,128]{2,1,0:T(8,128)}), f32[4,128,128]{2,1,0:T(8,128)S(1)}, u32[]{:S(2)}, u32[]{:S(2)}) async-start(f32[4,128,128]{2,1,0:T(8,128)} %bitcast.44), calls=%async_computation.10 | async-start | bytes 524288 | tf_op jit(solution)/shard_map/all_to_all | solution.py:50

commit v3 on v0

v3 whole, which is shorter than its diff:
```python
import functools

import jax
import jax.numpy as jnp
from jax import lax
from jax.experimental import pallas as pl
from jax.experimental.pallas import tpu as pltpu
from jax.sharding import PartitionSpec as P

OUTER = 2
INNER = 3
STEP = 0.3
F32 = jnp.float32
BF16 = jnp.bfloat16
PARAMS = pltpu.CompilerParams(vmem_limit_bytes=24 * 1024 * 1024)


def split(value):
    high = value.astype(BF16)
    return high, (value - high.astype(F32)).astype(BF16)


def mm(left, right):
    return jnp.dot(left, right, preferred_element_type=F32)


def product(left, right):
    (left_high, left_low), (right_high, right_low) = left, right
    width = right_high.shape[1]
    both = mm(left_high, jnp.concatenate([right_high, right_low], axis=1))
    return both[:, :width] + (both[:, width:] + mm(left_low, right_high))


def pick(chosen, value):
    width = value.shape[1]
    high, rest = value.astype(BF16), None
    rest = value - high.astype(F32)
    middle = rest.astype(BF16)
    low = (rest - middle.astype(F32)).astype(BF16)
    parts = mm(chosen, jnp.concatenate([high, middle, low], axis=1))
    return (parts[:, :width] + parts[:, width:2 * width]) + parts[:, 2 * width:]


def live(size, start, rows, width):
    return lax.broadcasted_iota(jnp.int32, (rows, width), 0) + start < size


def call(body, ins, in_specs, outs, out_specs, scratch=(), grid=(1,), flops=0, moved=0, alias=None, name=None):
    return pl.pallas_call(
        body,
        out_shape=outs,
        grid_spec=pl.GridSpec(grid=grid, in_specs=in_specs, out_specs=out_specs, scratch_shapes=list(scratch)),
        compiler_params=PARAMS,
        cost_estimate=pl.CostEstimate(flops=flops, bytes_accessed=moved, transcendentals=0),
        input_output_aliases=alias or {},
        name=name,
    )(*ins)


def whole(shape):
    return pl.BlockSpec(shape, lambda *i: (0,) * len(shape))


def block(shape, at=0, across=False):
    if across:
        return pl.BlockSpec(shape, lambda i: (0, i + at))
    return pl.BlockSpec(shape, lambda i: (i + at, 0))


SMEM = pl.BlockSpec(memory_space=pltpu.SMEM)


def shape(rows, columns, dtype=F32):
    return jax.ShapeDtypeStruct((rows, columns), dtype)


def lists_kernel(cap, me, peers, rows, unpack, asked):
    shared = peers.shape[1]
    asked_width = asked.shape[1]
    across = jnp.broadcast_to(peers[...], (shared, shared))
    down = across.T
    first = lax.broadcasted_iota(jnp.int32, (shared, shared), 0)
    second = lax.broadcasted_iota(jnp.int32, (shared, shared), 1)
    slot = jnp.sum(
        jnp.where((across == down) & (second < first), 1.0, 0.0), axis=1, keepdims=True
    ).astype(jnp.int32)
    rows_down = jnp.broadcast_to(rows[...], (shared, shared)).T[:, :1]
    far = down[:, :1] ^ me[0]
    key = jnp.where(far == 0, rows_down, shared + (far - 1) * cap + slot)
    hit = key == lax.broadcasted_iota(jnp.int32, unpack.shape, 1)
    unpack[...] = jnp.where(hit, 1.0, 0.0).astype(BF16)
    asked[...] = jnp.sum(
        jnp.where(hit[:, shared:], rows_down.astype(F32), 0.0), axis=0, keepdims=True
    )[:, :asked_width]


def first_kernel(operator, mult, high, low, image):
    parts = split(operator[...])
    high[...], low[...] = parts
    image[...] = product(parts, split(mult[...]))


def pack_kernel(cap, given, image, pack, *sends):
    shared = image.shape[0]
    wanted = jnp.broadcast_to(given[...], (shared, given.shape[1])).T
    chosen = jnp.where(
        wanted == lax.broadcasted_iota(jnp.int32, pack.shape, 1).astype(F32), 1.0, 0.0
    ).astype(BF16)
    pack[...] = chosen
    send(cap, chosen, image[...], sends)


def send(cap, chosen, image, sends):
    picked = pick(chosen, image)
    for d, out in enumerate(sends):
        out[...] = picked[d * cap:(d + 1) * cap]


def arrived(recvs, image, unpack):
    blocks = [image] + [recv[...] for recv in recvs]
    rows = sum(b.shape[0] for b in blocks)
    if rows < unpack.shape[1]:
        blocks.append(jnp.zeros((unpack.shape[1] - rows, image.shape[1]), F32))
    return pick(unpack[...], jnp.concatenate(blocks, axis=0))


def settle(trial, floor, alive):
    return jnp.where(alive, jnp.maximum(trial, floor), 0.0)


def shared_residual(recvs, image, unpack, gap, size):
    own = image[...]
    jump = own - arrived(recvs, own, unpack)
    alive = live(size[0], 0, *own.shape)
    return jnp.where(alive, gap[...] - jump, 0.0), alive


def rest_first_kernel(given_parts, size, operator, *refs):
    if given_parts:
        low, mult_s, mult_n, mult_block, gap, modes, trial, coarse, halves = refs
        parts = operator[...], low[...]
    else:
        mult_s, mult_n, mult_block, gap, modes, trial, coarse, high, low, halves = refs
        parts = split(operator[...])
        high[...], low[...] = parts
    step = pl.program_id(0)
    rows, width = gap.shape
    fill_halves(step, mult_s, mult_n, halves)
    image = halved_product(parts, halves[...], width)
    alive = live(size[0], (step + 1) * rows, rows, width)
    residual = jnp.where(alive, gap[...] - image, 0.0)
    trial[...] = mult_block[...] + STEP * residual

    @pl.when(step == 0)
    def _():
        coarse[...] = jnp.zeros_like(coarse)

    coarse[...] += product(split(modes[...]), split(residual))


def fill_halves(step, mult_s, mult_n, halves):
    @pl.when(step == 0)
    def _():
        shared, width = mult_s.shape
        high, low = split(mult_s[...])
        halves[:shared, :width], halves[:shared, width:] = high, low
        high, low = split(mult_n[...])
        halves[shared:, :width], halves[shared:, width:] = high, low


def halved_product(parts, halves, width):
    both = mm(parts[0], halves)
    return both[:, :width] + (both[:, width:] + mm(parts[1], halves[:, :width]))


def rest_kernel(last, size, high, low, mult_s, mult_n, mult_block, gap, floor, *refs):
    halves = refs[-1]
    step = pl.program_id(0)
    rows, width = gap.shape
    fill_halves(step, mult_s, mult_n, halves)
    image = halved_product((high[...], low[...]), halves[...], width)
    alive = live(size[0], (step + 1) * rows, rows, width)
    residual = jnp.where(alive, gap[...] - image, 0.0)
    mult = settle(mult_block[...] + STEP * residual, floor[...], alive)
    if last:
        mult_out, residual_out, _ = refs
        mult_out[...] = mult
        residual_out[...] = residual
    else:
        across_high, across_low, mult_out, ahead, _ = refs
        mult_out[...] = mult

        @pl.when(step == 0)
        def _():
            ahead[...] = jnp.zeros_like(ahead)

        ahead[...] += product((across_high[...], across_low[...]), split(mult))


def coarse_kernel(n, size, *refs):
    recvs = refs[:n]
    image, unpack, gap, mult, modes, started, coarse, trial = refs[n:]
    residual, _ = shared_residual(recvs, image, unpack, gap, size)
    coarse[...] = started[...] + product(split(modes[...]), split(residual))
    trial[...] = mult[...] + STEP * residual


def tile_kernel(n, m, place, tile, *refs):
    blocks, outs, (gathered, parts) = refs[:n + 1], refs[n + 1:n + m + 2], refs[n + m + 2:]
    count = blocks[0].shape[0]
    for d, ref in enumerate(blocks):
        at = pl.multiple_of((place[0] ^ d) * count, count)
        gathered[pl.ds(at, count), :] = ref[...]
    parts[...] = product(split(tile[...]), split(gathered[...]))
    for d, out in enumerate(outs):
        at = pl.multiple_of((place[1] ^ d) * count, count)
        out[...] = parts[pl.ds(at, count), :]


def lift_kernel(n, m, cap, size, *refs):
    parts = refs[:m + 1]
    modes, trial_s, trial_n, floor, high, low, pack, mult_s, mult_n, image = refs[m + 1:m + 11]
    sends = refs[m + 11:]
    solved = parts[0][...]
    for part in parts[1:]:
        solved = solved + part[...]
    shared, width = trial_s.shape
    order = floor.shape[0]
    basis = modes[...].T
    lifted = product(split(basis), split(solved))
    alive = live(size[0], 0, order, width)
    first = settle(trial_s[...] + lifted[:shared], floor[:shared], alive[:shared])
    rest = settle(trial_n[...] + lifted[shared:], floor[shared:], alive[shared:])
    mult_s[...] = first
    mult_n[...] = rest
    value = product((high[...], low[...]), split(jnp.concatenate([first, rest], axis=0)))
    image[...] = value
    send(cap, pack[...], value, sends)


def sweep_kernel(n, cap, size, *refs):
    recvs = refs[:n]
    image, unpack, gap, mult, floor, high, low, ahead, pack, mult_out, image_out = refs[n:n + 11]
    sends = refs[n + 11:]
    residual, alive = shared_residual(recvs, image, unpack, gap, size)
    value = settle(mult[...] + STEP * residual, floor[...], alive)
    mult_out[...] = value
    value = ahead[...] + product((high[...], low[...]), split(value))
    image_out[...] = value
    send(cap, pack[...], value, sends)


def last_kernel(n, size, *refs):
    recvs = refs[:n]
    image, unpack, gap, mult, floor, _, _, mult_out, residual_out = refs[n:]
    residual, alive = shared_residual(recvs, image, unpack, gap, size)
    mult_out[...] = settle(mult[...] + STEP * residual, floor[...], alive)
    residual_out[...] = residual


def swap(block, axis, count, d):
    return lax.ppermute(block, axis, [(i, i ^ d) for i in range(count)])


def distances(count):
    return sorted(range(1, count), reverse=True)


def swap_all(blocks, axis, count):
    got = {d: swap(blocks[d - 1], axis, count, d) for d in distances(count)}
    return [got[d] for d in range(1, count)]


def local(
    wide,
    narrow,
    operators,
    coarse_inverse,
    modes,
    gap,
    start_mult,
    peer_list,
    partner_row,
    interface_size,
    contact_rows,
):
    operator = operators[0]
    modes = modes[0]
    gap = gap[0]
    mult = start_mult[0]
    order, loads = mult.shape
    shared = partner_row.shape[1]
    count = modes.shape[0]
    rest = order - shared
    steps = rest // shared
    n, m = wide - 1, narrow - 1
    cap = 2 * shared // wide
    listed = n * cap
    padded = -(-listed // 128) * 128
    place = jnp.stack([lax.axis_index("wide"), lax.axis_index("narrow")]).astype(jnp.int32)
    size = interface_size
    floor = jnp.broadcast_to(
        jnp.where(contact_rows[0] == 1, 0.0, -jnp.inf).astype(F32)[:, None], (order, loads)
    )
    top = whole((shared, loads))
    sent = [shape(cap, loads)] * n
    sent_specs = [whole((cap, loads))] * n
    full = 2 * order * loads

    unpack, asked = call(
        functools.partial(lists_kernel, cap),
        (place, peer_list[0].reshape(1, shared), partner_row),
        [SMEM, whole((1, shared)), whole((1, shared))],
        [shape(shared, shared + padded, BF16), shape(1, listed)],
        [whole((shared, shared + padded)), whole((1, listed))],
        moved=shared * padded * 2,
        name="lists",
    )
    given = swap_all([asked[:, d * cap:(d + 1) * cap] for d in range(n)], "wide", wide)
    given = jnp.pad(jnp.concatenate(given, axis=1), ((0, 0), (0, padded - listed)))
    top_high, top_low, image = call(
        first_kernel,
        (operator, mult),
        [whole((shared, order)), whole((order, loads))],
        [shape(shared, order, BF16)] * 2 + [shape(shared, loads)],
        [whole((shared, order))] * 2 + [top],
        flops=3 * full * shared,
        moved=8 * shared * order,
        name="first",
    )
    pack, *sends = call(
        functools.partial(pack_kernel, cap),
        (given, image),
        [whole((1, padded)), top],
        [shape(padded, shared, BF16)] + sent,
        [whole((padded, shared))] + sent_specs,
        flops=6 * padded * shared * loads,
        moved=4 * padded * shared,
        name="pack",
    )
    mult_s, mult_n = mult[:shared], mult[shared:]
    unpack_spec = whole(unpack.shape)
    pack_spec = whole(pack.shape)
    high = low = None
    for outer in range(OUTER):
        recvs = swap_all(sends, "wide", wide)
        rest_ins = (mult_s, mult_n, mult_n, gap, modes)
        rest_specs = [
            top,
            whole((rest, loads)),
            block((shared, loads)),
            block((shared, loads), 1),
            block((count, shared), 1, across=True),
        ]
        rest_outs = [shape(rest, loads), shape(count, loads)]
        rest_out_specs = [block((shared, loads)), whole((count, loads))]
        row_block = block((shared, order))
        if high is None:
            ins, specs = (size, operator), [SMEM, block((shared, order), 1)]
            rest_outs = rest_outs + [shape(rest, order, BF16)] * 2
            rest_out_specs = rest_out_specs + [row_block] * 2
        else:
            ins, specs = (size, high, low), [SMEM, row_block, row_block]
        trial_n, started, *parts = call(
            functools.partial(rest_first_kernel, high is not None),
            ins + rest_ins,
            specs + rest_specs,
            rest_outs,
            rest_out_specs,
            scratch=[pltpu.VMEM((order, 2 * loads), BF16)],
            grid=(steps,),
            flops=3 * full * rest,
            moved=4 * rest * order,
            name="rest_first",
        )
        if parts:
            high, low = parts
        coarse, trial_s = call(
            functools.partial(coarse_kernel, n),
            (size, *recvs, image, unpack, gap, mult_s, modes, started),
            [SMEM] + sent_specs
            + [top, unpack_spec, top, top, whole((count, shared)), whole((count, loads))],
            [shape(count, loads), shape(shared, loads)],
            [whole((count, loads)), top],
            flops=6 * shared * loads * unpack.shape[1],
            moved=2 * shared * unpack.shape[1],
            name="coarse",
        )
        blocks = [coarse] + swap_all([coarse] * n, "wide", wide)
        part_spec = whole((count, loads))
        own, *parts = call(
            functools.partial(tile_kernel, n, m),
            (place, coarse_inverse, *blocks),
            [SMEM, whole(coarse_inverse.shape)] + [part_spec] * wide,
            [shape(count, loads)] * narrow,
            [part_spec] * narrow,
            scratch=[
                pltpu.VMEM((wide * count, loads), F32),
                pltpu.VMEM((narrow * count, loads), F32),
            ],
            flops=6 * coarse_inverse.size * loads,
            moved=4 * coarse_inverse.size,
            name="tile",
        )
        parts = [own] + swap_all(parts, "narrow", narrow)
        mult_s, mult_n, image, *sends = call(
            functools.partial(lift_kernel, n, m, cap),
            (size, *parts, modes, trial_s, trial_n, floor, top_high, top_low, pack),
            [SMEM] + [part_spec] * narrow
            + [whole(modes.shape), top, whole((rest, loads)), whole((order, loads))]
            + [whole((shared, order))] * 2 + [pack_spec],
            [shape(shared, loads), shape(rest, loads), shape(shared, loads)] + sent,
            [top, whole((rest, loads)), top] + sent_specs,
            flops=3 * full * shared,
            moved=4 * order * shared,
            name="lift",
        )
        for inner in range(1, INNER):
            last = outer == OUTER - 1 and inner == INNER - 1
            recvs = swap_all(sends, "wide", wide)
            ins = (size, high, low, mult_s, mult_n, mult_n, gap, floor)
            specs = [
                SMEM,
                row_block,
                row_block,
                top,
                whole((rest, loads)),
                block((shared, loads)),
                block((shared, loads), 1),
                block((shared, loads), 1),
            ]
            if last:
                outs = [shape(order, loads)] * 2
                out_specs = [block((shared, loads), 1)] * 2
            else:
                ins = ins + (top_high, top_low)
                specs = specs + [block((shared, shared), 1, across=True)] * 2
                outs = [shape(rest, loads), shape(shared, loads)]
                out_specs = [block((shared, loads)), top]
            rest_got = call(
                functools.partial(rest_kernel, last),
                ins,
                specs,
                outs,
                out_specs,
                scratch=[pltpu.VMEM((order, 2 * loads), BF16)],
                grid=(steps,),
                flops=3 * full * order,
                moved=4 * order * order,
                name="rest",
            )
            ins = (size, *recvs, image, unpack, gap, mult_s, floor)
            specs = [SMEM] + sent_specs + [top, unpack_spec, top, top, top]
            if last:
                return tuple(
                    out[None]
                    for out in call(
                        functools.partial(last_kernel, n),
                        ins + tuple(rest_got),
                        specs + [pl.BlockSpec(memory_space=pl.ANY)] * 2,
                        [shape(order, loads)] * 2,
                        [top] * 2,
                        alias={len(ins): 0, len(ins) + 1: 1},
                        flops=6 * shared * loads * unpack.shape[1],
                        moved=2 * shared * unpack.shape[1],
                        name="last",
                    )
                )
            mult_n, ahead = rest_got
            square = whole((shared, shared))
            mult_s, image, *sends = call(
                functools.partial(sweep_kernel, n, cap),
                ins + (top_high, top_low, ahead, pack),
                specs + [square, square, top, pack_spec],
                [shape(shared, loads)] * 2 + sent,
                [top] * 2 + sent_specs,
                flops=12 * shared * loads * unpack.shape[1],
                moved=4 * shared * unpack.shape[1],
                name="sweep",
            )


def solution(mesh):
    wide = mesh.shape["wide"]
    narrow = mesh.shape["narrow"]

    def body(*args):
        return local(wide, narrow, *args)

    return jax.shard_map(
        body,
        mesh=mesh,
        in_specs=(
            P(("groups", "wide", "narrow"), None, None),
            P(("groups", "wide"), "narrow"),
            P(("groups", "wide", "narrow"), None, None),
            P(("groups", "wide", "narrow"), None, None),
            P(("groups", "wide", "narrow"), None, None),
            P(("groups", "wide", "narrow"), None, None),
            P(("groups", "wide", "narrow"), None),
            P(("groups", "wide", "narrow")),
            P(("groups", "wide", "narrow"), None),
        ),
        out_specs=(
            P(("groups", "wide", "narrow"), None, None),
            P(("groups", "wide", "narrow"), None, None),
        ),
        check_vma=False,
    )
```

time: 234 us -> 102 us (0.44)
  blocking collectives: 123 us -> 0 us
  starting transfers between devices: 0.08 us -> 45.2 us
  matrix products: 40.3 us -> 0 us
  Pallas kernels: 0 us -> 23.9 us
  waiting for transfers between devices: 41.3 us -> 24.6 us
  between operations: 15.1 us -> 1.61 us
  other arithmetic: 5.47 us -> 0.09 us
  local copies, waits for them, and re-layouts: 8.22 us -> 5.83 us
    all_gather x8 -> x0, blocking collectives: 123 us -> none  [the longest x6 95.6 us: local(): whole = lax.all_gather(image[:shared], 'wide', axis=0, tiled=True)]
    ppermute x0 -> x33, starting transfers between devices: none -> 45.2 us  [swap(): return lax.ppermute(block, axis, [(i, i ^ d) for i in range(count)])]
    unnamed x4 -> x0, waiting for transfers between devices: 41.3 us -> none
    dot_general x12 -> x0, matrix products: 40.3 us -> none  [the longest x6 31.3 us: local(): jnp.dot(operator, mult, precision=highest, preferred_element_type=jnp.flo...]
    ppermute x0 -> x33, waiting for transfers between devices: none -> 24.6 us  [swap(): return lax.ppermute(block, axis, [(i, i ^ d) for i in range(count)])]
    pallas_call x0 -> x19, Pallas kernels: none -> 23.9 us  [call(): pl.pallas_call(body, out_shape=outs, grid_spec=pl.GridSpec(grid=grid, in_...]
    gather x6 -> x0, local copies, waits for them, and re-layouts: 5.6 us -> none  [local(): across = whole[peers * shared + rows_wanted]]
    unnamed x22 -> x18, local copies, waits for them, and re-layouts: 1.56 us -> 4.61 us
  transfers between devices with their start and end apart: 2 -> 33, of which waited for: 2 -> 16; matrix products, arithmetic and copies ran while one was open for 0% -> 1% of each run, Pallas kernels for 0% -> 14%
where the time goes in v3:
time: 102 us; the launch traced here: 101 us
  starting transfers between devices  45.2 us (44%)
  waiting for transfers between devices  24.6 us (24%)
  Pallas kernels  23.9 us (23%)
  local copies, waits for them, and re-layouts  5.83 us (6%)
  between operations  1.61 us (2%)
    ppermute x33, starting transfers between devices, swap(): return lax.ppermute(block, axis, [(i, i ^ d) for i in range(count)])  45.2 us
    ppermute x33, waiting for transfers between devices, swap(): return lax.ppermute(block, axis, [(i, i ^ d) for i in range(count)])  24.6 us
    pallas_call x19, Pallas kernels, call(): pl.pallas_call(body, out_shape=outs, grid_spec=pl.GridSpec(grid=grid, in_...  23.9 us
    unnamed x18, local copies, waits for them, and re-layouts  4.61 us
  transfers between devices with their start and end apart: 33, of which 16 were waited for; matrix products, arithmetic and copies ran while one was open for 1% of the time, Pallas kernels for 14%

profile of v3, /device:TPU:0, one launch (start us, length us, event | category | flops | bytes accessed | tf_op | source)
XLA Modules:
  0.0 101.2 jit_solution(16371384022031762526)
XLA Ops:
  0.7 0.7 copy-done.6
  1.4 0.7 copy-done.7
  2.1 0.9 lists.1
  3.0 3.1 %collective-permute-start = (f32[1,128]{1,0:T(1,128)S(1)}, f32[1,128]{1,0:T(1,128)S(1)}, u32[]{:S(2)}, u32[]{:S(2)}) collective-permute-start(f32[1,128]{1,0:T(1,128)S(1)} %get-tuple-element.130), channel_id=1, source_target_pairs={{0,4},{4,0},{8,12},{12,8},{1,5},{5,1},{9,13},{13,9},{2,6},{6,2},{1... | collective-permute-start | bytes 1544 | tf_op jit(solution)/shard_map/ppermute | solution.py:262
  6.1 2.5 %collective-permute-start.2 = (f32[1,128]{1,0:T(1,128)S(1)}, f32[1,128]{1,0:T(1,128)S(1)}, u32[]{:S(2)}, u32[]{:S(2)}) collective-permute-start(f32[1,128]{1,0:T(1,128)S(1)} %get-tuple-element.131), channel_id=1, source_target_pairs={{0,12},{4,8},{8,4},{12,0},{1,13},{5,9},{9,5},{13,1},{2,14},{6,10},... | collective-permute-start | bytes 1544 | tf_op jit(solution)/shard_map/ppermute | solution.py:262
  8.7 1.0 %slice_bitcast_fusion.refs_1_.refs_2_ = f32[768,128]{1,0:T(8,128)S(1)} fusion(f32[1,1024,128]{2,1,0:T(8,128)} %param.13), kind=kLoop, calls=%fused_computation | loop fusion | bytes 786432 | tf_op jit(solution)/shard_map/slice | solution.py:341
  9.7 2.2 %copy-done.1 = f32[1,1024,1024]{2,1,0:T(8,128)S(1)} copy-done((f32[1,1024,1024]{2,1,0:T(8,128)S(1)}, f32[1,1024,1024]{2,1,0:T(8,128)}, u32[]{:S(2)}) %copy-start.1) | copy-done | bytes 4194328
  11.9 1.0 %copy-done.4 = f32[1,1024,128]{2,1,0:T(8,128)S(1)} copy-done((f32[1,1024,128]{2,1,0:T(8,128)S(1)}, f32[1,1024,128]{2,1,0:T(8,128)}, u32[]{:S(2)}) %copy-start.4) | copy-done | bytes 524312
  13.8 1.9 %collective-permute-start.3 = (f32[128,128]{1,0:T(8,128)S(1)}, f32[128,128]{1,0:T(8,128)S(1)}, u32[]{:S(2)}, u32[]{:S(2)}) collective-permute-start(f32[128,128]{1,0:T(8,128)S(1)} %get-tuple-element.68), channel_id=1, source_target_pairs={{0,4},{4,0},{8,12},{12,8},{1,5},{5,1},{9,13},{13,9},{2,6},{6,2},{1... | collective-permute-start | bytes 196616 | tf_op jit(solution)/shard_map/ppermute | solution.py:262
  15.6 1.7 %collective-permute-start.4 = (f32[128,128]{1,0:T(8,128)S(1)}, f32[128,128]{1,0:T(8,128)S(1)}, u32[]{:S(2)}, u32[]{:S(2)}) collective-permute-start(f32[128,128]{1,0:T(8,128)S(1)} %get-tuple-element.69), channel_id=1, source_target_pairs={{0,8},{4,12},{8,0},{12,4},{1,9},{5,13},{9,1},{13,5},{2,10},{6,14},... | collective-permute-start | bytes 196616 | tf_op jit(solution)/shard_map/ppermute | solution.py:262
  17.3 0.9 collective-permute-start.5
  18.9 2.6 %rest_first.2 = (f32[768,128]{1,0:T(8,128)S(1)}, f32[64,128]{1,0:T(8,128)S(1)}, bf16[768,1024]{1,0:T(8,128)(2,1)S(1)}, bf16[768,1024]{1,0:T(8,128)(2,1)S(1)}) custom-call(s32[1]{0:T(128)S(6)} %copy.15.size, f32[1024,1024]{1,0:T(8,128)S(1)} %bitcast.27, f32[256,128]{1,0:T(8,128)S(1)} %slice_bitcast_fusion.1.refs_0_.refs_6_, ...), custom_call_target="tpu_custom_call" | custom-call | flops 603979776 | bytes 3145728 | tf_op jit(solution)/shard_map/rest_first/pallas_call | solution.py:49
  21.5 0.7 collective-permute-done.4.refs_1_
  22.2 1.3 %collective-permute-done.5.refs_2_ = f32[128,128]{1,0:T(8,128)S(1)} collective-permute-done((f32[128,128]{1,0:T(8,128)S(1)}, f32[128,128]{1,0:T(8,128)S(1)}, u32[]{:S(2)}, u32[]{:S(2)}) %collective-permute-start.5) | collective-permute-done | bytes 65568 | tf_op jit(solution)/shard_map/ppermute | solution.py:262
  23.5 0.5 coarse.2
  24.0 1.8 %collective-permute-start.8 = (f32[64,128]{1,0:T(8,128)S(1)}, f32[64,128]{1,0:T(8,128)S(1)}, u32[]{:S(2)}, u32[]{:S(2)}) collective-permute-start(f32[64,128]{1,0:T(8,128)S(1)} %get-tuple-element.73.refs_0_), channel_id=1, source_target_pairs={{0,12},{4,8},{8,4},{12,0},{1,13},{5,9},{9,5},{13,1},{2,14},{6,10},... | collective-permute-start | bytes 98312 | tf_op jit(solution)/shard_map/ppermute | solution.py:262
  26.2 2.2 %collective-permute-start.6 = (f32[64,128]{1,0:T(8,128)S(1)}, f32[64,128]{1,0:T(8,128)S(1)}, u32[]{:S(2)}, u32[]{:S(2)}) collective-permute-start(f32[64,128]{1,0:T(8,128)S(1)} %get-tuple-element.73.refs_0_), channel_id=1, source_target_pairs={{0,4},{4,0},{8,12},{12,8},{1,5},{5,1},{9,13},{13,9},{2,6},{6,2},{1... | collective-permute-start | bytes 98312 | tf_op jit(solution)/shard_map/ppermute | solution.py:262
  28.5 1.3 %collective-permute-done.8.refs_3_ = f32[64,128]{1,0:T(8,128)S(1)} collective-permute-done((f32[64,128]{1,0:T(8,128)S(1)}, f32[64,128]{1,0:T(8,128)S(1)}, u32[]{:S(2)}, u32[]{:S(2)}) %collective-permute-start.8) | collective-permute-done | bytes 32800 | tf_op jit(solution)/shard_map/ppermute | solution.py:262
  29.8 1.0 collective-permute-done.7.refs_2_
  30.8 0.8 tile.4
  31.7 1.6 %collective-permute-start.10 = (f32[64,128]{1,0:T(8,128)S(1)}, f32[64,128]{1,0:T(8,128)S(1)}, u32[]{:S(2)}, u32[]{:S(2)}) collective-permute-start(f32[64,128]{1,0:T(8,128)S(1)} %get-tuple-element.76), channel_id=1, source_target_pairs={{0,2},{1,3},{2,0},{3,1},{4,6},{5,7},{6,4},{7,5},{8,10},{9,11},{10,... | collective-permute-start | bytes 98312 | tf_op jit(solution)/shard_map/ppermute | solution.py:262
  33.6 2.1 %collective-permute-done.10.refs_2_ = f32[64,128]{1,0:T(8,128)S(1)} collective-permute-done((f32[64,128]{1,0:T(8,128)S(1)}, f32[64,128]{1,0:T(8,128)S(1)}, u32[]{:S(2)}, u32[]{:S(2)}) %collective-permute-start.10) | collective-permute-done | bytes 32800 | tf_op jit(solution)/shard_map/ppermute | solution.py:262
  35.7 0.9 collective-permute-done.11.refs_3_
  36.8 1.0 lift.2
  37.8 1.7 %collective-permute-start.12 = (f32[128,128]{1,0:T(8,128)S(1)}, f32[128,128]{1,0:T(8,128)S(1)}, u32[]{:S(2)}, u32[]{:S(2)}) collective-permute-start(f32[128,128]{1,0:T(8,128)S(1)} %get-tuple-element.83), channel_id=1, source_target_pairs={{0,4},{4,0},{8,12},{12,8},{1,5},{5,1},{9,13},{13,9},{2,6},{6,2},{1... | collective-permute-start | bytes 196616 | tf_op jit(solution)/shard_map/ppermute | solution.py:262
  39.4 1.0 collective-permute-start.13
  40.4 1.8 %collective-permute-start.14 = (f32[128,128]{1,0:T(8,128)S(1)}, f32[128,128]{1,0:T(8,128)S(1)}, u32[]{:S(2)}, u32[]{:S(2)}) collective-permute-start(f32[128,128]{1,0:T(8,128)S(1)} %get-tuple-element.85), channel_id=1, source_target_pairs={{0,12},{4,8},{8,4},{12,0},{1,13},{5,9},{9,5},{13,1},{2,14},{6,10},... | collective-permute-start | bytes 196616 | tf_op jit(solution)/shard_map/ppermute | solution.py:262
  42.2 2.3 %rest.4 = (f32[768,128]{1,0:T(8,128)S(1)}, f32[256,128]{1,0:T(8,128)S(1)}) custom-call(s32[1]{0:T(128)S(6)} %copy.15.size, bf16[768,1024]{1,0:T(8,128)(2,1)S(1)} %get-tuple-element.88.high.operator, bf16[768,1024]{1,0:T(8,128)(2,1)S(1)} %get-tuple-element.89.low.refs_0_, f32[256,128]{1,0:T(8,128)S(1)} %get-tuple-element.87.mult_s.refs_6_, ...), custom_call_target="tpu_custom_call" | custom-call | flops 805306368 | bytes 4194304 | tf_op jit(solution)/shard_map/rest/pallas_call | solution.py:49
  44.6 2.9 %collective-permute-done.13.refs_1_ = f32[128,128]{1,0:T(8,128)S(1)} collective-permute-done((f32[128,128]{1,0:T(8,128)S(1)}, f32[128,128]{1,0:T(8,128)S(1)}, u32[]{:S(2)}, u32[]{:S(2)}) %collective-permute-start.13) | collective-permute-done | bytes 65568 | tf_op jit(solution)/shard_map/ppermute | solution.py:262
  47.5 0.8 sweep.3
  48.3 1.5 %collective-permute-start.15 = (f32[128,128]{1,0:T(8,128)S(1)}, f32[128,128]{1,0:T(8,128)S(1)}, u32[]{:S(2)}, u32[]{:S(2)}) collective-permute-start(f32[128,128]{1,0:T(8,128)S(1)} %get-tuple-element.92), channel_id=1, source_target_pairs={{0,4},{4,0},{8,12},{12,8},{1,5},{5,1},{9,13},{13,9},{2,6},{6,2},{1... | collective-permute-start | bytes 196616 | tf_op jit(solution)/shard_map/ppermute | solution.py:262
  49.8 1.0 collective-permute-start.16
  50.8 2.0 %collective-permute-start.17 = (f32[128,128]{1,0:T(8,128)S(1)}, f32[128,128]{1,0:T(8,128)S(1)}, u32[]{:S(2)}, u32[]{:S(2)}) collective-permute-start(f32[128,128]{1,0:T(8,128)S(1)} %get-tuple-element.94), channel_id=1, source_target_pairs={{0,12},{4,8},{8,4},{12,0},{1,13},{5,9},{9,5},{13,1},{2,14},{6,10},... | collective-permute-start | bytes 196616 | tf_op jit(solution)/shard_map/ppermute | solution.py:262
  52.8 2.3 %rest.5 = (f32[768,128]{1,0:T(8,128)S(1)}, f32[256,128]{1,0:T(8,128)S(1)}) custom-call(s32[1]{0:T(128)S(6)} %copy.15.size, bf16[768,1024]{1,0:T(8,128)(2,1)S(1)} %get-tuple-element.88.high.operator, bf16[768,1024]{1,0:T(8,128)(2,1)S(1)} %get-tuple-element.89.low.refs_0_, f32[256,128]{1,0:T(8,128)S(1)} %get-tuple-element.96.mult_s.refs_6_, ...), custom_call_target="tpu_custom_call" | custom-call | flops 805306368 | bytes 4194304 | tf_op jit(solution)/shard_map/rest/pallas_call | solution.py:49
  55.1 2.2 %collective-permute-done.16.refs_1_ = f32[128,128]{1,0:T(8,128)S(1)} collective-permute-done((f32[128,128]{1,0:T(8,128)S(1)}, f32[128,128]{1,0:T(8,128)S(1)}, u32[]{:S(2)}, u32[]{:S(2)}) %collective-permute-start.16) | collective-permute-done | bytes 65568 | tf_op jit(solution)/shard_map/ppermute | solution.py:262
  57.4 0.8 sweep.4
  58.2 1.3 %collective-permute-start.18 = (f32[128,128]{1,0:T(8,128)S(1)}, f32[128,128]{1,0:T(8,128)S(1)}, u32[]{:S(2)}, u32[]{:S(2)}) collective-permute-start(f32[128,128]{1,0:T(8,128)S(1)} %get-tuple-element.99), channel_id=1, source_target_pairs={{0,4},{4,0},{8,12},{12,8},{1,5},{5,1},{9,13},{13,9},{2,6},{6,2},{1... | collective-permute-start | bytes 196616 | tf_op jit(solution)/shard_map/ppermute | solution.py:262
  59.5 1.2 %collective-permute-start.19 = (f32[128,128]{1,0:T(8,128)S(1)}, f32[128,128]{1,0:T(8,128)S(1)}, u32[]{:S(2)}, u32[]{:S(2)}) collective-permute-start(f32[128,128]{1,0:T(8,128)S(1)} %get-tuple-element.100), channel_id=1, source_target_pairs={{0,8},{4,12},{8,0},{12,4},{1,9},{5,13},{9,1},{13,5},{2,10},{6,14},... | collective-permute-start | bytes 196616 | tf_op jit(solution)/shard_map/ppermute | solution.py:262
  60.8 1.9 %collective-permute-start.20 = (f32[128,128]{1,0:T(8,128)S(1)}, f32[128,128]{1,0:T(8,128)S(1)}, u32[]{:S(2)}, u32[]{:S(2)}) collective-permute-start(f32[128,128]{1,0:T(8,128)S(1)} %get-tuple-element.101), channel_id=1, source_target_pairs={{0,12},{4,8},{8,4},{12,0},{1,13},{5,9},{9,5},{13,1},{2,14},{6,10},... | collective-permute-start | bytes 196616 | tf_op jit(solution)/shard_map/ppermute | solution.py:262
  62.6 2.2 %rest_first.3 = (f32[768,128]{1,0:T(8,128)S(1)}, f32[64,128]{1,0:T(8,128)S(1)}) custom-call(s32[1]{0:T(128)S(6)} %copy.15.size, bf16[768,1024]{1,0:T(8,128)(2,1)S(1)} %get-tuple-element.88.high.operator, bf16[768,1024]{1,0:T(8,128)(2,1)S(1)} %get-tuple-element.89.low.refs_0_, f32[256,128]{1,0:T(8,128)S(1)} %get-tuple-element.103.refs_1_.refs_6_, ...), custom_call_target="tpu_custom_call" | custom-call | flops 603979776 | bytes 3145728 | tf_op jit(solution)/shard_map/rest_first/pallas_call | solution.py:49
  64.9 0.9 collective-permute-done.19.refs_1_
  65.8 1.2 %collective-permute-done.20.refs_2_ = f32[128,128]{1,0:T(8,128)S(1)} collective-permute-done((f32[128,128]{1,0:T(8,128)S(1)}, f32[128,128]{1,0:T(8,128)S(1)}, u32[]{:S(2)}, u32[]{:S(2)}) %collective-permute-start.20) | collective-permute-done | bytes 65568 | tf_op jit(solution)/shard_map/ppermute | solution.py:262
  66.9 0.5 coarse.3
  67.5 1.9 %collective-permute-start.23 = (f32[64,128]{1,0:T(8,128)S(1)}, f32[64,128]{1,0:T(8,128)S(1)}, u32[]{:S(2)}, u32[]{:S(2)}) collective-permute-start(f32[64,128]{1,0:T(8,128)S(1)} %get-tuple-element.106.refs_0_), channel_id=1, source_target_pairs={{0,12},{4,8},{8,4},{12,0},{1,13},{5,9},{9,5},{13,1},{2,14},{6,10},... | collective-permute-start | bytes 98312 | tf_op jit(solution)/shard_map/ppermute | solution.py:262
  69.8 2.1 %collective-permute-start.21 = (f32[64,128]{1,0:T(8,128)S(1)}, f32[64,128]{1,0:T(8,128)S(1)}, u32[]{:S(2)}, u32[]{:S(2)}) collective-permute-start(f32[64,128]{1,0:T(8,128)S(1)} %get-tuple-element.106.refs_0_), channel_id=1, source_target_pairs={{0,4},{4,0},{8,12},{12,8},{1,5},{5,1},{9,13},{13,9},{2,6},{6,2},{1... | collective-permute-start | bytes 98312 | tf_op jit(solution)/shard_map/ppermute | solution.py:262
  71.9 1.3 %collective-permute-done.23.refs_3_ = f32[64,128]{1,0:T(8,128)S(1)} collective-permute-done((f32[64,128]{1,0:T(8,128)S(1)}, f32[64,128]{1,0:T(8,128)S(1)}, u32[]{:S(2)}, u32[]{:S(2)}) %collective-permute-start.23) | collective-permute-done | bytes 32800 | tf_op jit(solution)/shard_map/ppermute | solution.py:262
  73.3 1.0 collective-permute-done.22.refs_2_
  74.2 0.8 tile.6
  75.1 0.9 collective-permute-start.25
  76.1 0.9 collective-permute-start.26
  77.0 2.2 %collective-permute-done.25.refs_2_ = f32[64,128]{1,0:T(8,128)S(1)} collective-permute-done((f32[64,128]{1,0:T(8,128)S(1)}, f32[64,128]{1,0:T(8,128)S(1)}, u32[]{:S(2)}, u32[]{:S(2)}) %collective-permute-start.25) | collective-permute-done | bytes 32800 | tf_op jit(solution)/shard_map/ppermute | solution.py:262
  79.5 1.0 lift.3
  80.5 1.7 %collective-permute-start.27 = (f32[128,128]{1,0:T(8,128)S(1)}, f32[128,128]{1,0:T(8,128)S(1)}, u32[]{:S(2)}, u32[]{:S(2)}) collective-permute-start(f32[128,128]{1,0:T(8,128)S(1)} %get-tuple-element.113), channel_id=1, source_target_pairs={{0,4},{4,0},{8,12},{12,8},{1,5},{5,1},{9,13},{13,9},{2,6},{6,2},{1... | collective-permute-start | bytes 196616 | tf_op jit(solution)/shard_map/ppermute | solution.py:262
  82.2 0.9 collective-permute-start.28
  83.1 1.9 %collective-permute-start.29 = (f32[128,128]{1,0:T(8,128)S(1)}, f32[128,128]{1,0:T(8,128)S(1)}, u32[]{:S(2)}, u32[]{:S(2)}) collective-permute-start(f32[128,128]{1,0:T(8,128)S(1)} %get-tuple-element.115), channel_id=1, source_target_pairs={{0,12},{4,8},{8,4},{12,0},{1,13},{5,9},{9,5},{13,1},{2,14},{6,10},... | collective-permute-start | bytes 196616 | tf_op jit(solution)/shard_map/ppermute | solution.py:262
  84.9 2.3 %rest.6 = (f32[768,128]{1,0:T(8,128)S(1)}, f32[256,128]{1,0:T(8,128)S(1)}) custom-call(s32[1]{0:T(128)S(6)} %copy.15.size, bf16[768,1024]{1,0:T(8,128)(2,1)S(1)} %get-tuple-element.88.high.operator, bf16[768,1024]{1,0:T(8,128)(2,1)S(1)} %get-tuple-element.89.low.refs_0_, f32[256,128]{1,0:T(8,128)S(1)} %get-tuple-element.117.mult_s.refs_6_, ...), custom_call_target="tpu_custom_call" | custom-call | flops 805306368 | bytes 4194304 | tf_op jit(solution)/shard_map/rest/pallas_call | solution.py:49
  87.3 2.9 %collective-permute-done.28.refs_1_ = f32[128,128]{1,0:T(8,128)S(1)} collective-permute-done((f32[128,128]{1,0:T(8,128)S(1)}, f32[128,128]{1,0:T(8,128)S(1)}, u32[]{:S(2)}, u32[]{:S(2)}) %collective-permute-start.28) | collective-permute-done | bytes 65568 | tf_op jit(solution)/shard_map/ppermute | solution.py:262
  90.2 0.8 sweep.5
  91.0 1.5 %collective-permute-start.30 = (f32[128,128]{1,0:T(8,128)S(1)}, f32[128,128]{1,0:T(8,128)S(1)}, u32[]{:S(2)}, u32[]{:S(2)}) collective-permute-start(f32[128,128]{1,0:T(8,128)S(1)} %get-tuple-element.120), channel_id=1, source_target_pairs={{0,4},{4,0},{8,12},{12,8},{1,5},{5,1},{9,13},{13,9},{2,6},{6,2},{1... | collective-permute-start | bytes 196616 | tf_op jit(solution)/shard_map/ppermute | solution.py:262
  92.5 1.1 %collective-permute-start.31 = (f32[128,128]{1,0:T(8,128)S(1)}, f32[128,128]{1,0:T(8,128)S(1)}, u32[]{:S(2)}, u32[]{:S(2)}) collective-permute-start(f32[128,128]{1,0:T(8,128)S(1)} %get-tuple-element.121), channel_id=1, source_target_pairs={{0,8},{4,12},{8,0},{12,4},{1,9},{5,13},{9,1},{13,5},{2,10},{6,14},... | collective-permute-start | bytes 196616 | tf_op jit(solution)/shard_map/ppermute | solution.py:262
  93.6 1.9 %collective-permute-start.32 = (f32[128,128]{1,0:T(8,128)S(1)}, f32[128,128]{1,0:T(8,128)S(1)}, u32[]{:S(2)}, u32[]{:S(2)}) collective-permute-start(f32[128,128]{1,0:T(8,128)S(1)} %get-tuple-element.122), channel_id=1, source_target_pairs={{0,12},{4,8},{8,4},{12,0},{1,13},{5,9},{9,5},{13,1},{2,14},{6,10},... | collective-permute-start | bytes 196616 | tf_op jit(solution)/shard_map/ppermute | solution.py:262
  95.5 2.4 %rest.7 = (f32[1024,128]{1,0:T(8,128)}, f32[1024,128]{1,0:T(8,128)}) custom-call(s32[1]{0:T(128)S(6)} %copy.15.size, bf16[768,1024]{1,0:T(8,128)(2,1)S(1)} %get-tuple-element.88.high.operator, bf16[768,1024]{1,0:T(8,128)(2,1)S(1)} %get-tuple-element.89.low.refs_0_, f32[256,128]{1,0:T(8,128)S(1)} %get-tuple-element.124.mult_s.refs_6_, ...), custom_call_target="tpu_custom_call" | custom-call | flops 805306368 | bytes 4194304 | tf_op jit(solution)/shard_map/rest/pallas_call | solution.py:49
  97.9 2.3 %collective-permute-done.31.refs_1_ = f32[128,128]{1,0:T(8,128)S(1)} collective-permute-done((f32[128,128]{1,0:T(8,128)S(1)}, f32[128,128]{1,0:T(8,128)S(1)}, u32[]{:S(2)}, u32[]{:S(2)}) %collective-permute-start.31) | collective-permute-done | bytes 65568 | tf_op jit(solution)/shard_map/ppermute | solution.py:262
  100.2 1.1 %last.1 = (f32[1024,128]{1,0:T(8,128)}, f32[1024,128]{1,0:T(8,128)}) custom-call(s32[1]{0:T(128)S(6)} %copy.15.size, f32[128,128]{1,0:T(8,128)S(1)} %collective-permute-done.30.refs_0_, f32[128,128]{1,0:T(8,128)S(1)} %collective-permute-done.31.refs_1_, ...), custom_call_target="tpu_custom_call", output_to_operand_aliasing={{0}: (9, {}), {1}: (10, {})} | custom-call | flops 125829120 | bytes 327680 | tf_op jit(solution)/shard_map/last/pallas_call | solution.py:49
  (46 shorter events, 2.8 us)
Async XLA Ops:
  0.7 0.7 copy-start.6
  1.4 0.7 copy-start.7
  3.0 10.4 %collective-permute-start = (f32[1,128]{1,0:T(1,128)S(1)}, f32[1,128]{1,0:T(1,128)S(1)}, u32[]{:S(2)}, u32[]{:S(2)}) collective-permute-start(f32[1,128]{1,0:T(1,128)S(1)} %get-tuple-element.130), channel_id=1, source_target_pairs={{0,4},{4,0},{8,12},{12,8},{1,5},{5,1},{9,13},{13,9},{2,6},{6,2},{1... | collective-permute-start | bytes 1544 | tf_op jit(solution)/shard_map/ppermute | solution.py:262
  6.1 7.3 %collective-permute-start.2 = (f32[1,128]{1,0:T(1,128)S(1)}, f32[1,128]{1,0:T(1,128)S(1)}, u32[]{:S(2)}, u32[]{:S(2)}) collective-permute-start(f32[1,128]{1,0:T(1,128)S(1)} %get-tuple-element.131), channel_id=1, source_target_pairs={{0,12},{4,8},{8,4},{12,0},{1,13},{5,9},{9,5},{13,1},{2,14},{6,10},... | collective-permute-start | bytes 1544 | tf_op jit(solution)/shard_map/ppermute | solution.py:262
  8.6 4.9 %collective-permute-start.1 = (f32[1,128]{1,0:T(1,128)S(1)}, f32[1,128]{1,0:T(1,128)S(1)}, u32[]{:S(2)}, u32[]{:S(2)}) collective-permute-start(f32[1,128]{1,0:T(1,128)S(1)} %get-tuple-element.132), channel_id=1, source_target_pairs={{0,8},{4,12},{8,0},{12,4},{1,9},{5,13},{9,1},{13,5},{2,10},{6,14},... | collective-permute-start | bytes 1544 | tf_op jit(solution)/shard_map/ppermute | solution.py:262
  9.7 2.2 %copy-start.1 = (f32[1,1024,1024]{2,1,0:T(8,128)S(1)}, f32[1,1024,1024]{2,1,0:T(8,128)}, u32[]{:S(2)}) copy-start(f32[1,1024,1024]{2,1,0:T(8,128)} %param.9) | copy-start | bytes 12582916
  11.9 1.0 %copy-start.4 = (f32[1,1024,128]{2,1,0:T(8,128)S(1)}, f32[1,1024,128]{2,1,0:T(8,128)}, u32[]{:S(2)}) copy-start(f32[1,1024,128]{2,1,0:T(8,128)} %param.13) | copy-start | bytes 1572868
  12.9 5.9 %copy-start = (f32[1,1024,128]{2,1,0:T(8,128)S(1)}, f32[1,1024,128]{2,1,0:T(8,128)}, u32[]{:S(2)}) copy-start(f32[1,1024,128]{2,1,0:T(8,128)} %param.12) | copy-start | bytes 1572868
  12.9 6.0 %copy-start.2 = (f32[1,1024,1024]{2,1,0:T(8,128)S(1)}, f32[1,1024,1024]{2,1,0:T(8,128)}, u32[]{:S(2)}) copy-start(f32[1,1024,1024]{2,1,0:T(8,128)} %param.9) | copy-start | bytes 12582916
  12.9 6.0 %copy-start.3 = (f32[1,64,1024]{2,1,0:T(8,128)S(1)}, f32[1,64,1024]{2,1,0:T(8,128)}, u32[]{:S(2)}) copy-start(f32[1,64,1024]{2,1,0:T(8,128)} %param.11) | copy-start | bytes 786436
  13.8 7.7 %collective-permute-start.3 = (f32[128,128]{1,0:T(8,128)S(1)}, f32[128,128]{1,0:T(8,128)S(1)}, u32[]{:S(2)}, u32[]{:S(2)}) collective-permute-start(f32[128,128]{1,0:T(8,128)S(1)} %get-tuple-element.68), channel_id=1, source_target_pairs={{0,4},{4,0},{8,12},{12,8},{1,5},{5,1},{9,13},{13,9},{2,6},{6,2},{1... | collective-permute-start | bytes 196616 | tf_op jit(solution)/shard_map/ppermute | solution.py:262
  15.6 6.6 %collective-permute-start.4 = (f32[128,128]{1,0:T(8,128)S(1)}, f32[128,128]{1,0:T(8,128)S(1)}, u32[]{:S(2)}, u32[]{:S(2)}) collective-permute-start(f32[128,128]{1,0:T(8,128)S(1)} %get-tuple-element.69), channel_id=1, source_target_pairs={{0,8},{4,12},{8,0},{12,4},{1,9},{5,13},{9,1},{13,5},{2,10},{6,14},... | collective-permute-start | bytes 196616 | tf_op jit(solution)/shard_map/ppermute | solution.py:262
  17.3 6.2 %collective-permute-start.5 = (f32[128,128]{1,0:T(8,128)S(1)}, f32[128,128]{1,0:T(8,128)S(1)}, u32[]{:S(2)}, u32[]{:S(2)}) collective-permute-start(f32[128,128]{1,0:T(8,128)S(1)} %get-tuple-element.70), channel_id=1, source_target_pairs={{0,12},{4,8},{8,4},{12,0},{1,13},{5,9},{9,5},{13,1},{2,14},{6,10},... | collective-permute-start | bytes 196616 | tf_op jit(solution)/shard_map/ppermute | solution.py:262
  21.5 9.3 %copy-start.5 = (f32[256,256]{1,0:T(8,128)S(1)}, f32[256,256]{1,0:T(8,128)}, u32[]{:S(2)}) copy-start(f32[256,256]{1,0:T(8,128)} %tile.7) | copy-start | bytes 786436
  21.5 12.1 %copy-start.8 = (s32[1,1024]{1,0:T(1,128)S(1)}, s32[1,1024]{1,0:T(1,128)}, u32[]{:S(2)}) copy-start(s32[1,1024]{1,0:T(1,128)} %param.17) | copy-start | bytes 12292
  24.0 5.8 %collective-permute-start.8 = (f32[64,128]{1,0:T(8,128)S(1)}, f32[64,128]{1,0:T(8,128)S(1)}, u32[]{:S(2)}, u32[]{:S(2)}) collective-permute-start(f32[64,128]{1,0:T(8,128)S(1)} %get-tuple-element.73.refs_0_), channel_id=1, source_target_pairs={{0,12},{4,8},{8,4},{12,0},{1,13},{5,9},{9,5},{13,1},{2,14},{6,10},... | collective-permute-start | bytes 98312 | tf_op jit(solution)/shard_map/ppermute | solution.py:262
  25.8 5.0 %collective-permute-start.7 = (f32[64,128]{1,0:T(8,128)S(1)}, f32[64,128]{1,0:T(8,128)S(1)}, u32[]{:S(2)}, u32[]{:S(2)}) collective-permute-start(f32[64,128]{1,0:T(8,128)S(1)} %get-tuple-element.73.refs_0_), channel_id=1, source_target_pairs={{0,8},{4,12},{8,0},{12,4},{1,9},{5,13},{9,1},{13,5},{2,10},{6,14},... | collective-permute-start | bytes 98312 | tf_op jit(solution)/shard_map/ppermute | solution.py:262
  26.2 4.6 %collective-permute-start.6 = (f32[64,128]{1,0:T(8,128)S(1)}, f32[64,128]{1,0:T(8,128)S(1)}, u32[]{:S(2)}, u32[]{:S(2)}) collective-permute-start(f32[64,128]{1,0:T(8,128)S(1)} %get-tuple-element.73.refs_0_), channel_id=1, source_target_pairs={{0,4},{4,0},{8,12},{12,8},{1,5},{5,1},{9,13},{13,9},{2,6},{6,2},{1... | collective-permute-start | bytes 98312 | tf_op jit(solution)/shard_map/ppermute | solution.py:262
  31.6 2.0 %collective-permute-start.9 = (f32[64,128]{1,0:T(8,128)S(1)}, f32[64,128]{1,0:T(8,128)S(1)}, u32[]{:S(2)}, u32[]{:S(2)}) collective-permute-start(f32[64,128]{1,0:T(8,128)S(1)} %get-tuple-element.75), channel_id=1, source_target_pairs={{0,1},{1,0},{2,3},{3,2},{4,5},{5,4},{6,7},{7,6},{8,9},{9,8},{10,11... | collective-permute-start | bytes 98312 | tf_op jit(solution)/shard_map/ppermute | solution.py:262
  31.7 4.0 %collective-permute-start.10 = (f32[64,128]{1,0:T(8,128)S(1)}, f32[64,128]{1,0:T(8,128)S(1)}, u32[]{:S(2)}, u32[]{:S(2)}) collective-permute-start(f32[64,128]{1,0:T(8,128)S(1)} %get-tuple-element.76), channel_id=1, source_target_pairs={{0,2},{1,3},{2,0},{3,1},{4,6},{5,7},{6,4},{7,5},{8,10},{9,11},{10,... | collective-permute-start | bytes 98312 | tf_op jit(solution)/shard_map/ppermute | solution.py:262
  33.2 3.3 %collective-permute-start.11 = (f32[64,128]{1,0:T(8,128)S(1)}, f32[64,128]{1,0:T(8,128)S(1)}, u32[]{:S(2)}, u32[]{:S(2)}) collective-permute-start(f32[64,128]{1,0:T(8,128)S(1)} %get-tuple-element.77), channel_id=1, source_target_pairs={{0,3},{1,2},{2,1},{3,0},{4,7},{5,6},{6,5},{7,4},{8,11},{9,10},{10,... | collective-permute-start | bytes 98312 | tf_op jit(solution)/shard_map/ppermute | solution.py:262
  37.8 6.8 %collective-permute-start.12 = (f32[128,128]{1,0:T(8,128)S(1)}, f32[128,128]{1,0:T(8,128)S(1)}, u32[]{:S(2)}, u32[]{:S(2)}) collective-permute-start(f32[128,128]{1,0:T(8,128)S(1)} %get-tuple-element.83), channel_id=1, source_target_pairs={{0,4},{4,0},{8,12},{12,8},{1,5},{5,1},{9,13},{13,9},{2,6},{6,2},{1... | collective-permute-start | bytes 196616 | tf_op jit(solution)/shard_map/ppermute | solution.py:262
  39.4 8.0 %collective-permute-start.13 = (f32[128,128]{1,0:T(8,128)S(1)}, f32[128,128]{1,0:T(8,128)S(1)}, u32[]{:S(2)}, u32[]{:S(2)}) collective-permute-start(f32[128,128]{1,0:T(8,128)S(1)} %get-tuple-element.84), channel_id=1, source_target_pairs={{0,8},{4,12},{8,0},{12,4},{1,9},{5,13},{9,1},{13,5},{2,10},{6,14},... | collective-permute-start | bytes 196616 | tf_op jit(solution)/shard_map/ppermute | solution.py:262
  40.4 7.1 %collective-permute-start.14 = (f32[128,128]{1,0:T(8,128)S(1)}, f32[128,128]{1,0:T(8,128)S(1)}, u32[]{:S(2)}, u32[]{:S(2)}) collective-permute-start(f32[128,128]{1,0:T(8,128)S(1)} %get-tuple-element.85), channel_id=1, source_target_pairs={{0,12},{4,8},{8,4},{12,0},{1,13},{5,9},{9,5},{13,1},{2,14},{6,10},... | collective-permute-start | bytes 196616 | tf_op jit(solution)/shard_map/ppermute | solution.py:262
  48.3 6.8 %collective-permute-start.15 = (f32[128,128]{1,0:T(8,128)S(1)}, f32[128,128]{1,0:T(8,128)S(1)}, u32[]{:S(2)}, u32[]{:S(2)}) collective-permute-start(f32[128,128]{1,0:T(8,128)S(1)} %get-tuple-element.92), channel_id=1, source_target_pairs={{0,4},{4,0},{8,12},{12,8},{1,5},{5,1},{9,13},{13,9},{2,6},{6,2},{1... | collective-permute-start | bytes 196616 | tf_op jit(solution)/shard_map/ppermute | solution.py:262
  49.8 7.6 %collective-permute-start.16 = (f32[128,128]{1,0:T(8,128)S(1)}, f32[128,128]{1,0:T(8,128)S(1)}, u32[]{:S(2)}, u32[]{:S(2)}) collective-permute-start(f32[128,128]{1,0:T(8,128)S(1)} %get-tuple-element.93), channel_id=1, source_target_pairs={{0,8},{4,12},{8,0},{12,4},{1,9},{5,13},{9,1},{13,5},{2,10},{6,14},... | collective-permute-start | bytes 196616 | tf_op jit(solution)/shard_map/ppermute | solution.py:262
  50.8 6.5 %collective-permute-start.17 = (f32[128,128]{1,0:T(8,128)S(1)}, f32[128,128]{1,0:T(8,128)S(1)}, u32[]{:S(2)}, u32[]{:S(2)}) collective-permute-start(f32[128,128]{1,0:T(8,128)S(1)} %get-tuple-element.94), channel_id=1, source_target_pairs={{0,12},{4,8},{8,4},{12,0},{1,13},{5,9},{9,5},{13,1},{2,14},{6,10},... | collective-permute-start | bytes 196616 | tf_op jit(solution)/shard_map/ppermute | solution.py:262
  58.2 6.7 %collective-permute-start.18 = (f32[128,128]{1,0:T(8,128)S(1)}, f32[128,128]{1,0:T(8,128)S(1)}, u32[]{:S(2)}, u32[]{:S(2)}) collective-permute-start(f32[128,128]{1,0:T(8,128)S(1)} %get-tuple-element.99), channel_id=1, source_target_pairs={{0,4},{4,0},{8,12},{12,8},{1,5},{5,1},{9,13},{13,9},{2,6},{6,2},{1... | collective-permute-start | bytes 196616 | tf_op jit(solution)/shard_map/ppermute | solution.py:262
  59.5 6.2 %collective-permute-start.19 = (f32[128,128]{1,0:T(8,128)S(1)}, f32[128,128]{1,0:T(8,128)S(1)}, u32[]{:S(2)}, u32[]{:S(2)}) collective-permute-start(f32[128,128]{1,0:T(8,128)S(1)} %get-tuple-element.100), channel_id=1, source_target_pairs={{0,8},{4,12},{8,0},{12,4},{1,9},{5,13},{9,1},{13,5},{2,10},{6,14},... | collective-permute-start | bytes 196616 | tf_op jit(solution)/shard_map/ppermute | solution.py:262
  60.8 6.2 %collective-permute-start.20 = (f32[128,128]{1,0:T(8,128)S(1)}, f32[128,128]{1,0:T(8,128)S(1)}, u32[]{:S(2)}, u32[]{:S(2)}) collective-permute-start(f32[128,128]{1,0:T(8,128)S(1)} %get-tuple-element.101), channel_id=1, source_target_pairs={{0,12},{4,8},{8,4},{12,0},{1,13},{5,9},{9,5},{13,1},{2,14},{6,10},... | collective-permute-start | bytes 196616 | tf_op jit(solution)/shard_map/ppermute | solution.py:262
  67.5 5.8 %collective-permute-start.23 = (f32[64,128]{1,0:T(8,128)S(1)}, f32[64,128]{1,0:T(8,128)S(1)}, u32[]{:S(2)}, u32[]{:S(2)}) collective-permute-start(f32[64,128]{1,0:T(8,128)S(1)} %get-tuple-element.106.refs_0_), channel_id=1, source_target_pairs={{0,12},{4,8},{8,4},{12,0},{1,13},{5,9},{9,5},{13,1},{2,14},{6,10},... | collective-permute-start | bytes 98312 | tf_op jit(solution)/shard_map/ppermute | solution.py:262
  69.4 4.8 %collective-permute-start.22 = (f32[64,128]{1,0:T(8,128)S(1)}, f32[64,128]{1,0:T(8,128)S(1)}, u32[]{:S(2)}, u32[]{:S(2)}) collective-permute-start(f32[64,128]{1,0:T(8,128)S(1)} %get-tuple-element.106.refs_0_), channel_id=1, source_target_pairs={{0,8},{4,12},{8,0},{12,4},{1,9},{5,13},{9,1},{13,5},{2,10},{6,14},... | collective-permute-start | bytes 98312 | tf_op jit(solution)/shard_map/ppermute | solution.py:262
  69.8 4.4 %collective-permute-start.21 = (f32[64,128]{1,0:T(8,128)S(1)}, f32[64,128]{1,0:T(8,128)S(1)}, u32[]{:S(2)}, u32[]{:S(2)}) collective-permute-start(f32[64,128]{1,0:T(8,128)S(1)} %get-tuple-element.106.refs_0_), channel_id=1, source_target_pairs={{0,4},{4,0},{8,12},{12,8},{1,5},{5,1},{9,13},{13,9},{2,6},{6,2},{1... | collective-permute-start | bytes 98312 | tf_op jit(solution)/shard_map/ppermute | solution.py:262
  75.0 1.9 %collective-permute-start.24 = (f32[64,128]{1,0:T(8,128)S(1)}, f32[64,128]{1,0:T(8,128)S(1)}, u32[]{:S(2)}, u32[]{:S(2)}) collective-permute-start(f32[64,128]{1,0:T(8,128)S(1)} %get-tuple-element.108), channel_id=1, source_target_pairs={{0,1},{1,0},{2,3},{3,2},{4,5},{5,4},{6,7},{7,6},{8,9},{9,8},{10,11... | collective-permute-start | bytes 98312 | tf_op jit(solution)/shard_map/ppermute | solution.py:262
  75.1 4.0 %collective-permute-start.25 = (f32[64,128]{1,0:T(8,128)S(1)}, f32[64,128]{1,0:T(8,128)S(1)}, u32[]{:S(2)}, u32[]{:S(2)}) collective-permute-start(f32[64,128]{1,0:T(8,128)S(1)} %get-tuple-element.109), channel_id=1, source_target_pairs={{0,2},{1,3},{2,0},{3,1},{4,6},{5,7},{6,4},{7,5},{8,10},{9,11},{10,... | collective-permute-start | bytes 98312 | tf_op jit(solution)/shard_map/ppermute | solution.py:262
  76.1 3.4 %collective-permute-start.26 = (f32[64,128]{1,0:T(8,128)S(1)}, f32[64,128]{1,0:T(8,128)S(1)}, u32[]{:S(2)}, u32[]{:S(2)}) collective-permute-start(f32[64,128]{1,0:T(8,128)S(1)} %get-tuple-element.110), channel_id=1, source_target_pairs={{0,3},{1,2},{2,1},{3,0},{4,7},{5,6},{6,5},{7,4},{8,11},{9,10},{10,... | collective-permute-start | bytes 98312 | tf_op jit(solution)/shard_map/ppermute | solution.py:262
  80.5 6.8 %collective-permute-start.27 = (f32[128,128]{1,0:T(8,128)S(1)}, f32[128,128]{1,0:T(8,128)S(1)}, u32[]{:S(2)}, u32[]{:S(2)}) collective-permute-start(f32[128,128]{1,0:T(8,128)S(1)} %get-tuple-element.113), channel_id=1, source_target_pairs={{0,4},{4,0},{8,12},{12,8},{1,5},{5,1},{9,13},{13,9},{2,6},{6,2},{1... | collective-permute-start | bytes 196616 | tf_op jit(solution)/shard_map/ppermute | solution.py:262
  82.2 8.0 %collective-permute-start.28 = (f32[128,128]{1,0:T(8,128)S(1)}, f32[128,128]{1,0:T(8,128)S(1)}, u32[]{:S(2)}, u32[]{:S(2)}) collective-permute-start(f32[128,128]{1,0:T(8,128)S(1)} %get-tuple-element.114), channel_id=1, source_target_pairs={{0,8},{4,12},{8,0},{12,4},{1,9},{5,13},{9,1},{13,5},{2,10},{6,14},... | collective-permute-start | bytes 196616 | tf_op jit(solution)/shard_map/ppermute | solution.py:262
  83.1 7.1 %collective-permute-start.29 = (f32[128,128]{1,0:T(8,128)S(1)}, f32[128,128]{1,0:T(8,128)S(1)}, u32[]{:S(2)}, u32[]{:S(2)}) collective-permute-start(f32[128,128]{1,0:T(8,128)S(1)} %get-tuple-element.115), channel_id=1, source_target_pairs={{0,12},{4,8},{8,4},{12,0},{1,13},{5,9},{9,5},{13,1},{2,14},{6,10},... | collective-permute-start | bytes 196616 | tf_op jit(solution)/shard_map/ppermute | solution.py:262
  91.0 6.8 %collective-permute-start.30 = (f32[128,128]{1,0:T(8,128)S(1)}, f32[128,128]{1,0:T(8,128)S(1)}, u32[]{:S(2)}, u32[]{:S(2)}) collective-permute-start(f32[128,128]{1,0:T(8,128)S(1)} %get-tuple-element.120), channel_id=1, source_target_pairs={{0,4},{4,0},{8,12},{12,8},{1,5},{5,1},{9,13},{13,9},{2,6},{6,2},{1... | collective-permute-start | bytes 196616 | tf_op jit(solution)/shard_map/ppermute | solution.py:262
  92.5 7.7 %collective-permute-start.31 = (f32[128,128]{1,0:T(8,128)S(1)}, f32[128,128]{1,0:T(8,128)S(1)}, u32[]{:S(2)}, u32[]{:S(2)}) collective-permute-start(f32[128,128]{1,0:T(8,128)S(1)} %get-tuple-element.121), channel_id=1, source_target_pairs={{0,8},{4,12},{8,0},{12,4},{1,9},{5,13},{9,1},{13,5},{2,10},{6,14},... | collective-permute-start | bytes 196616 | tf_op jit(solution)/shard_map/ppermute | solution.py:262
  93.6 6.6 %collective-permute-start.32 = (f32[128,128]{1,0:T(8,128)S(1)}, f32[128,128]{1,0:T(8,128)S(1)}, u32[]{:S(2)}, u32[]{:S(2)}) collective-permute-start(f32[128,128]{1,0:T(8,128)S(1)} %get-tuple-element.122), channel_id=1, source_target_pairs={{0,12},{4,8},{8,4},{12,0},{1,13},{5,9},{9,5},{13,1},{2,14},{6,10},... | collective-permute-start | bytes 196616 | tf_op jit(solution)/shard_map/ppermute | solution.py:262

commit v4 on v3

--- a/solution.py
+++ b/solution.py
@@ -10,6 +10,7 @@
 OUTER = 2
 INNER = 3
 STEP = 0.3
+LEADS = ((1, 3), (3, 1), (1, 2), (2, 1))
 F32 = jnp.float32
 BF16 = jnp.bfloat16
 PARAMS = pltpu.CompilerParams(vmem_limit_bytes=24 * 1024 * 1024)
@@ -33,12 +34,8 @@
 
 def pick(chosen, value):
     width = value.shape[1]
-    high, rest = value.astype(BF16), None
-    rest = value - high.astype(F32)
-    middle = rest.astype(BF16)
-    low = (rest - middle.astype(F32)).astype(BF16)
-    parts = mm(chosen, jnp.concatenate([high, middle, low], axis=1))
-    return (parts[:, :width] + parts[:, width:2 * width]) + parts[:, 2 * width:]
+    both = mm(chosen, jnp.concatenate(split(value), axis=1))
+    return both[:, :width] + both[:, width:]
 
 
 def live(size, start, rows, width):
@@ -68,15 +65,27 @@
 
 
 SMEM = pl.BlockSpec(memory_space=pltpu.SMEM)
+HBM = pl.BlockSpec(memory_space=pltpu.HBM)
 
 
 def shape(rows, columns, dtype=F32):
     return jax.ShapeDtypeStruct((rows, columns), dtype)
 
 
-def lists_kernel(cap, me, peers, rows, unpack, asked):
-    shared = peers.shape[1]
-    asked_width = asked.shape[1]
+def first_kernel(wide, cap, peers_at, rows_at, operator_at, mult_at, *refs):
+    unpack_all, unpack, high, low, image = refs[:5]
+    sends, (peers, rows, operator, mult, done) = refs[5:4 + wide], refs[4 + wide:]
+    shared, width = image.shape
+    copies = [
+        pltpu.make_async_copy(source, target, done.at[i])
+        for i, (source, target) in enumerate(
+            ((peers_at, peers), (rows_at, rows), (mult_at, mult), (operator_at.at[pl.ds(0, shared)], operator))
+        )
+    ]
+    for copy in copies:
+        copy.start()
+    copies[0].wait()
+    copies[1].wait()
     across = jnp.broadcast_to(peers[...], (shared, shared))
     down = across.T
     first = lax.broadcasted_iota(jnp.int32, (shared, shared), 0)
@@ -84,30 +93,57 @@
     slot = jnp.sum(
         jnp.where((across == down) & (second < first), 1.0, 0.0), axis=1, keepdims=True
     ).astype(jnp.int32)
-    rows_down = jnp.broadcast_to(rows[...], (shared, shared)).T[:, :1]
-    far = down[:, :1] ^ me[0]
-    key = jnp.where(far == 0, rows_down, shared + (far - 1) * cap + slot)
-    hit = key == lax.broadcasted_iota(jnp.int32, unpack.shape, 1)
-    unpack[...] = jnp.where(hit, 1.0, 0.0).astype(BF16)
-    asked[...] = jnp.sum(
-        jnp.where(hit[:, shared:], rows_down.astype(F32), 0.0), axis=0, keepdims=True
-    )[:, :asked_width]
-
-
-def first_kernel(operator, mult, high, low, image):
+    wanted = jnp.broadcast_to(rows[...], (shared, shared)).T[:, :1]
+    far = down[:, :1] ^ lax.axis_index("wide")
+
+    def marks(key, columns):
+        hit = key == lax.broadcasted_iota(jnp.int32, (shared, columns), 1)
+        return jnp.where(hit, 1.0, 0.0).astype(BF16)
+
+    unpack_all[...] = marks(far * shared + wanted, unpack_all.shape[1])
+    unpack[...] = marks(
+        jnp.where(far == 0, wanted, shared + (far - 1) * cap + slot), unpack.shape[1]
+    )
+    lane = lax.broadcasted_iota(jnp.int32, (shared, width), 1)
+    for d, out in enumerate(sends, 1):
+        out[shared:, :] = jnp.zeros((out.shape[0] - shared, width), F32)
+        for c in range(-(-cap // width)):
+            hit = (far == d) & (slot == lane + c * width)
+            out[shared + c:shared + c + 1, :] = jnp.sum(
+                jnp.where(hit, wanted.astype(F32), 0.0), axis=0, keepdims=True
+            )
+    copies[2].wait()
+    copies[3].wait()
     parts = split(operator[...])
     high[...], low[...] = parts
-    image[...] = product(parts, split(mult[...]))
-
-
-def pack_kernel(cap, given, image, pack, *sends):
-    shared = image.shape[0]
-    wanted = jnp.broadcast_to(given[...], (shared, given.shape[1])).T
-    chosen = jnp.where(
-        wanted == lax.broadcasted_iota(jnp.int32, pack.shape, 1).astype(F32), 1.0, 0.0
-    ).astype(BF16)
-    pack[...] = chosen
-    send(cap, chosen, image[...], sends)
+    value = product(parts, split(mult[...]))
+    image[...] = value
+    for out in sends:
+        out[:shared, :] = value
+
+
+def pack_kernel(n, cap, *refs):
+    recvs, pack = refs[:n], refs[n]
+    shared = pack.shape[1]
+    width = recvs[0].shape[1]
+    column = lax.broadcasted_iota(jnp.int32, (width, shared), 1).astype(F32)
+    if n * cap < pack.shape[0]:
+        pack[n * cap:, :] = jnp.zeros((pack.shape[0] - n * cap, shared), BF16)
+    for d, recv in enumerate(recvs):
+        for c in range(-(-cap // width)):
+            wanted = jnp.broadcast_to(recv[shared + c:shared + c + 1, :], (shared, width)).T
+            chosen = jnp.where(wanted == column, 1.0, 0.0).astype(BF16)
+            size = min(width, cap - c * width)
+            pack[d * cap + c * width:d * cap + c * width + size, :] = chosen[:size]
+
+
+def prepare_kernel(contact, modes, tile, floor, basis_high, basis_low, tile_high, tile_low):
+    order, width = floor.shape
+    for at in range(0, order, width):
+        flag = jnp.broadcast_to(contact[:, at:at + width], (width, width)).T
+        floor[at:at + width, :] = jnp.where(flag == 1, 0.0, -jnp.inf)
+    basis_high[...], basis_low[...] = split(modes[...].T)
+    tile_high[...], tile_low[...] = split(tile[...])
 
 
 def send(cap, chosen, image, sends):
@@ -117,7 +153,8 @@
 
 
 def arrived(recvs, image, unpack):
-    blocks = [image] + [recv[...] for recv in recvs]
+    shared = image.shape[0]
+    blocks = [image] + [recv[...][:shared] for recv in recvs]
     rows = sum(b.shape[0] for b in blocks)
     if rows < unpack.shape[1]:
         blocks.append(jnp.zeros((unpack.shape[1] - rows, image.shape[1]), F32))
@@ -135,17 +172,19 @@
     return jnp.where(alive, gap[...] - jump, 0.0), alive
 
 
-def rest_first_kernel(given_parts, size, operator, *refs):
+def rest_first_kernel(pieces, given_parts, size, operator, *refs):
     if given_parts:
-        low, mult_s, mult_n, mult_block, gap, modes, trial, coarse, halves = refs
+        low, refs = refs[0], refs[1:]
+    mults, (mult_block, gap, modes, trial, coarse), outs = refs[:pieces], refs[pieces:pieces + 5], refs[pieces + 5:]
+    halves = outs[-1]
+    if given_parts:
         parts = operator[...], low[...]
     else:
-        mult_s, mult_n, mult_block, gap, modes, trial, coarse, high, low, halves = refs
         parts = split(operator[...])
-        high[...], low[...] = parts
+        outs[0][...], outs[1][...] = parts
     step = pl.program_id(0)
     rows, width = gap.shape
-    fill_halves(step, mult_s, mult_n, halves)
+    fill_halves(step, mults, halves)
     image = halved_product(parts, halves[...], width)
     alive = live(size[0], (step + 1) * rows, rows, width)
     residual = jnp.where(alive, gap[...] - image, 0.0)
@@ -158,14 +197,14 @@
     coarse[...] += product(split(modes[...]), split(residual))
 
 
-def fill_halves(step, mult_s, mult_n, halves):
+def fill_halves(step, mults, halves):
     @pl.when(step == 0)
     def _():
-        shared, width = mult_s.shape
-        high, low = split(mult_s[...])
-        halves[:shared, :width], halves[:shared, width:] = high, low
-        high, low = split(mult_n[...])
-        halves[shared:, :width], halves[shared:, width:] = high, low
+        at = 0
+        for mult in mults:
+            rows, width = mult.shape
+            halves[at:at + rows, :width], halves[at:at + rows, width:] = split(mult[...])
+            at += rows
 
 
 def halved_product(parts, halves, width):
@@ -177,7 +216,7 @@
     halves = refs[-1]
     step = pl.program_id(0)
     rows, width = gap.shape
-    fill_halves(step, mult_s, mult_n, halves)
+    fill_halves(step, (mult_s, mult_n), halves)
     image = halved_product((high[...], low[...]), halves[...], width)
     alive = live(size[0], (step + 1) * rows, rows, width)
     residual = jnp.where(alive, gap[...] - image, 0.0)
@@ -199,35 +238,36 @@
 
 def coarse_kernel(n, size, *refs):
     recvs = refs[:n]
-    image, unpack, gap, mult, modes, started, coarse, trial = refs[n:]
+    image, unpack, gap, mult, modes, started, trial = refs[n:n + 7]
     residual, _ = shared_residual(recvs, image, unpack, gap, size)
-    coarse[...] = started[...] + product(split(modes[...]), split(residual))
+    coarse = started[...] + product(split(modes[...]), split(residual))
+    for out in refs[n + 7:]:
+        out[...] = coarse
     trial[...] = mult[...] + STEP * residual
 
 
-def tile_kernel(n, m, place, tile, *refs):
+def tile_kernel(n, m, high, low, *refs):
     blocks, outs, (gathered, parts) = refs[:n + 1], refs[n + 1:n + m + 2], refs[n + m + 2:]
     count = blocks[0].shape[0]
     for d, ref in enumerate(blocks):
-        at = pl.multiple_of((place[0] ^ d) * count, count)
+        at = pl.multiple_of((lax.axis_index("wide") ^ d) * count, count)
         gathered[pl.ds(at, count), :] = ref[...]
-    parts[...] = product(split(tile[...]), split(gathered[...]))
+    parts[...] = product((high[...], low[...]), split(gathered[...]))
     for d, out in enumerate(outs):
-        at = pl.multiple_of((place[1] ^ d) * count, count)
+        at = pl.multiple_of((lax.axis_index("narrow") ^ d) * count, count)
         out[...] = parts[pl.ds(at, count), :]
 
 
 def lift_kernel(n, m, cap, size, *refs):
     parts = refs[:m + 1]
-    modes, trial_s, trial_n, floor, high, low, pack, mult_s, mult_n, image = refs[m + 1:m + 11]
-    sends = refs[m + 11:]
+    ins, (mult_s, mult_n, image), sends = refs[m + 1:m + 9], refs[m + 9:m + 12], refs[m + 12:]
+    basis_high, basis_low, trial_s, trial_n, floor, high, low, pack = ins
     solved = parts[0][...]
     for part in parts[1:]:
         solved = solved + part[...]
     shared, width = trial_s.shape
     order = floor.shape[0]
-    basis = modes[...].T
-    lifted = product(split(basis), split(solved))
+    lifted = product((basis_high[...], basis_low[...]), split(solved))
     alive = live(size[0], 0, order, width)
     first = settle(trial_s[...] + lifted[:shared], floor[:shared], alive[:shared])
     rest = settle(trial_n[...] + lifted[shared:], floor[shared:], alive[shared:])
@@ -262,12 +302,10 @@
     return lax.ppermute(block, axis, [(i, i ^ d) for i in range(count)])
 
 
-def distances(count):
-    return sorted(range(1, count), reverse=True)
-
-
-def swap_all(blocks, axis, count):
-    got = {d: swap(blocks[d - 1], axis, count, d) for d in distances(count)}
+def swap_all(blocks, axis, count, lead=()):
+    lead = [d for d in lead if d < count]
+    order = lead + [d for d in range(count - 1, 0, -1) if d not in lead]
+    got = {d: swap(blocks[d - 1], axis, count, d) for d in order}
     return [got[d] for d in range(1, count)]
 
 
@@ -297,72 +335,69 @@
     cap = 2 * shared // wide
     listed = n * cap
     padded = -(-listed // 128) * 128
-    place = jnp.stack([lax.axis_index("wide"), lax.axis_index("narrow")]).astype(jnp.int32)
     size = interface_size
-    floor = jnp.broadcast_to(
-        jnp.where(contact_rows[0] == 1, 0.0, -jnp.inf).astype(F32)[:, None], (order, loads)
-    )
     top = whole((shared, loads))
     sent = [shape(cap, loads)] * n
     sent_specs = [whole((cap, loads))] * n
     full = 2 * order * loads
 
-    unpack, asked = call(
-        functools.partial(lists_kernel, cap),
-        (place, peer_list[0].reshape(1, shared), partner_row),
-        [SMEM, whole((1, shared)), whole((1, shared))],
-        [shape(shared, shared + padded, BF16), shape(1, listed)],
-        [whole((shared, shared + padded)), whole((1, listed))],
-        moved=shared * padded * 2,
-        name="lists",
-    )
-    given = swap_all([asked[:, d * cap:(d + 1) * cap] for d in range(n)], "wide", wide)
-    given = jnp.pad(jnp.concatenate(given, axis=1), ((0, 0), (0, padded - listed)))
-    top_high, top_low, image = call(
-        first_kernel,
-        (operator, mult),
-        [whole((shared, order)), whole((order, loads))],
-        [shape(shared, order, BF16)] * 2 + [shape(shared, loads)],
-        [whole((shared, order))] * 2 + [top],
+    list_rows = -(-(-(-cap // loads)) // 8) * 8
+    unpack_all, unpack, top_high, top_low, image, *sends = call(
+        functools.partial(first_kernel, wide, cap),
+        (peer_list[0].reshape(1, shared), partner_row, operator, mult),
+        [HBM] * 4,
+        [shape(shared, wide * shared, BF16), shape(shared, shared + padded, BF16)]
+        + [shape(shared, order, BF16)] * 2
+        + [shape(shared, loads)]
+        + [shape(shared + list_rows, loads)] * n,
+        [whole((shared, wide * shared)), whole((shared, shared + padded))]
+        + [whole((shared, order))] * 2
+        + [top]
+        + [whole((shared + list_rows, loads))] * n,
+        scratch=[
+            pltpu.VMEM((1, shared), jnp.int32),
+            pltpu.VMEM((1, shared), jnp.int32),
+            pltpu.VMEM((shared, order), F32),
+            pltpu.VMEM((order, loads), F32),
+            pltpu.SemaphoreType.DMA((4,)),
+        ],
         flops=3 * full * shared,
         moved=8 * shared * order,
         name="first",
     )
-    pack, *sends = call(
-        functools.partial(pack_kernel, cap),
-        (given, image),
-        [whole((1, padded)), top],
-        [shape(padded, shared, BF16)] + sent,
-        [whole((padded, shared))] + sent_specs,
-        flops=6 * padded * shared * loads,
-        moved=4 * padded * shared,
-        name="pack",
+    floor, basis_high, basis_low, tile_high, tile_low = call(
+        prepare_kernel,
+        (contact_rows, modes, coarse_inverse),
+        [whole((1, order)), whole(modes.shape), whole(coarse_inverse.shape)],
+        [shape(order, loads)] + [shape(order, count, BF16)] * 2 + [shape(*coarse_inverse.shape, BF16)] * 2,
+        [whole((order, loads))] + [whole((order, count))] * 2 + [whole(coarse_inverse.shape)] * 2,
+        flops=full * count,
+        moved=8 * coarse_inverse.size + 4 * full,
+        name="prepare",
     )
-    mult_s, mult_n = mult[:shared], mult[shared:]
+    mults, mult_s = (mult,), mult
     unpack_spec = whole(unpack.shape)
-    pack_spec = whole(pack.shape)
-    high = low = None
     for outer in range(OUTER):
-        recvs = swap_all(sends, "wide", wide)
-        rest_ins = (mult_s, mult_n, mult_n, gap, modes)
-        rest_specs = [
-            top,
-            whole((rest, loads)),
-            block((shared, loads)),
+        start = outer == 0
+        recvs = swap_all(sends, "wide", wide, (1,))
+        recv_spec = whole(sends[0].shape)
+        rest_ins = (*mults, mults[-1], gap, modes)
+        rest_specs = [whole(piece.shape) for piece in mults] + [
+            block((shared, loads), 1 if start else 0),
             block((shared, loads), 1),
             block((count, shared), 1, across=True),
         ]
         rest_outs = [shape(rest, loads), shape(count, loads)]
         rest_out_specs = [block((shared, loads)), whole((count, loads))]
         row_block = block((shared, order))
-        if high is None:
+        if start:
             ins, specs = (size, operator), [SMEM, block((shared, order), 1)]
             rest_outs = rest_outs + [shape(rest, order, BF16)] * 2
             rest_out_specs = rest_out_specs + [row_block] * 2
         else:
             ins, specs = (size, high, low), [SMEM, row_block, row_block]
         trial_n, started, *parts = call(
-            functools.partial(rest_first_kernel, high is not None),
+            functools.partial(rest_first_kernel, len(mults), not start),
             ins + rest_ins,
             specs + rest_specs,
             rest_outs,
@@ -373,25 +408,38 @@
             moved=4 * rest * order,
             name="rest_first",
         )
-        if parts:
+        marks = unpack
+        if start:
             high, low = parts
-        coarse, trial_s = call(
+            marks = unpack_all
+            pack = call(
+                functools.partial(pack_kernel, n, cap),
+                tuple(recvs),
+                [recv_spec] * n,
+                [shape(padded, shared, BF16)],
+                [whole((padded, shared))],
+                flops=full,
+                moved=4 * padded * shared,
+                name="pack",
+            )[0]
+            pack_spec = whole(pack.shape)
+        trial_s, own, *coarse = call(
             functools.partial(coarse_kernel, n),
-            (size, *recvs, image, unpack, gap, mult_s, modes, started),
-            [SMEM] + sent_specs
-            + [top, unpack_spec, top, top, whole((count, shared)), whole((count, loads))],
-            [shape(count, loads), shape(shared, loads)],
-            [whole((count, loads)), top],
+            (size, *recvs, image, marks, gap, mult_s, modes, started),
+            [SMEM] + [recv_spec] * n
+            + [top, whole(marks.shape), top, top, whole((count, shared)), whole((count, loads))],
+            [shape(shared, loads)] + [shape(count, loads)] * wide,
+            [top] + [whole((count, loads))] * wide,
             flops=6 * shared * loads * unpack.shape[1],
             moved=2 * shared * unpack.shape[1],
             name="coarse",
         )
-        blocks = [coarse] + swap_all([coarse] * n, "wide", wide)
+        blocks = [own] + swap_all(coarse, "wide", wide, (3, 2) if start else (2, 3))
         part_spec = whole((count, loads))
         own, *parts = call(
             functools.partial(tile_kernel, n, m),
-            (place, coarse_inverse, *blocks),
-            [SMEM, whole(coarse_inverse.shape)] + [part_spec] * wide,
+            (tile_high, tile_low, *blocks),
+            [whole(coarse_inverse.shape)] * 2 + [part_spec] * wide,
             [shape(count, loads)] * narrow,
             [part_spec] * narrow,
             scratch=[
@@ -402,12 +450,12 @@
             moved=4 * coarse_inverse.size,
             name="tile",
         )
-        parts = [own] + swap_all(parts, "narrow", narrow)
+        parts = [own] + swap_all(parts, "narrow", narrow, (1, 2) if start else (1, 3))
         mult_s, mult_n, image, *sends = call(
             functools.partial(lift_kernel, n, m, cap),
-            (size, *parts, modes, trial_s, trial_n, floor, top_high, top_low, pack),
+            (size, *parts, basis_high, basis_low, trial_s, trial_n, floor, top_high, top_low, pack),
             [SMEM] + [part_spec] * narrow
-            + [whole(modes.shape), top, whole((rest, loads)), whole((order, loads))]
+            + [whole((order, count))] * 2 + [top, whole((rest, loads)), whole((order, loads))]
             + [whole((shared, order))] * 2 + [pack_spec],
             [shape(shared, loads), shape(rest, loads), shape(shared, loads)] + sent,
             [top, whole((rest, loads)), top] + sent_specs,
@@ -417,7 +465,7 @@
         )
         for inner in range(1, INNER):
             last = outer == OUTER - 1 and inner == INNER - 1
-            recvs = swap_all(sends, "wide", wide)
+            recvs = swap_all(sends, "wide", wide, LEADS[2 * outer + inner - 1])
             ins = (size, high, low, mult_s, mult_n, mult_n, gap, floor)
             specs = [
                 SMEM,
@@ -478,6 +526,7 @@
                 moved=4 * shared * unpack.shape[1],
                 name="sweep",
             )
+            mults = mult_s, mult_n
 
 
 def solution(mesh):

time: 102 us -> 100 us (0.980)
  waiting for transfers between devices: 24.6 us -> 30.4 us
  starting transfers between devices: 45.2 us -> 39.9 us
  Pallas kernels: 23.9 us -> 22.6 us
    ppermute x33 -> x30, waiting for transfers between devices: 24.6 us -> 30.4 us  [swap(): return lax.ppermute(block, axis, [(i, i ^ d) for i in range(count)])]
    ppermute x33 -> x30, starting transfers between devices: 45.2 us -> 39.9 us  [swap(): return lax.ppermute(block, axis, [(i, i ^ d) for i in range(count)])]
    pallas_call x19, Pallas kernels: 23.9 us -> 22.6 us  [call(): pl.pallas_call(body, out_shape=outs, grid_spec=pl.GridSpec(grid=grid, in_...]
    slice x3 -> x0, local copies, waits for them, and re-layouts: 1.03 us -> none  [the longest x2 1.03 us: local(): mult_s, mult_n = (mult[:shared], mult[shared:])]
    unnamed x18 -> x20, local copies, waits for them, and re-layouts: 4.61 us -> 5.55 us
  transfers between devices with their start and end apart: 33 -> 30, of which waited for: 16 -> 17; matrix products, arithmetic and copies ran while one was open for 1% -> 0% of each run, Pallas kernels for 14% -> 15%
where the time goes in v4:
time: 100 us
  starting transfers between devices  39.9 us (40%)
  waiting for transfers between devices  30.4 us (30%)
  Pallas kernels  22.6 us (23%)
  local copies, waits for them, and re-layouts  5.55 us (6%)
  between operations  1.57 us (2%)
    ppermute x30, starting transfers between devices, swap(): return lax.ppermute(block, axis, [(i, i ^ d) for i in range(count)])  39.9 us
    ppermute x30, waiting for transfers between devices, swap(): return lax.ppermute(block, axis, [(i, i ^ d) for i in range(count)])  30.4 us
    pallas_call x19, Pallas kernels, call(): pl.pallas_call(body, out_shape=outs, grid_spec=pl.GridSpec(grid=grid, in_...  22.6 us
    unnamed x20, local copies, waits for them, and re-layouts  5.55 us
  transfers between devices with their start and end apart: 30, of which 17 were waited for; matrix products, arithmetic and copies ran while one was open for 0% of the time, Pallas kernels for 15%

profile of v4, /device:TPU:0, one launch (start us, length us, event | category | flops | bytes accessed | tf_op | source)
XLA Modules:
  0.0 100.1 jit_solution(14427521717317674772)
XLA Ops:
  0.6 2.2 %copy-done.1 = f32[1,1024,1024]{2,1,0:T(8,128)S(1)} copy-done((f32[1,1024,1024]{2,1,0:T(8,128)S(1)}, f32[1,1024,1024]{2,1,0:T(8,128)}, u32[]{:S(2)}) %copy-start.1) | copy-done | bytes 4194328
  2.8 1.0 %copy-done.3 = f32[1,1024,128]{2,1,0:T(8,128)S(1)} copy-done((f32[1,1024,128]{2,1,0:T(8,128)S(1)}, f32[1,1024,128]{2,1,0:T(8,128)}, u32[]{:S(2)}) %copy-start.3) | copy-done | bytes 524312
  3.9 0.7 copy-done.8
  4.5 0.7 copy-done.9
  5.2 1.1 %first.1 = (bf16[256,1024]{1,0:T(8,128)(2,1)S(1)}, bf16[256,640]{1,0:T(8,128)(2,1)S(1)}, bf16[256,1024]{1,0:T(8,128)(2,1)S(1)}, bf16[256,1024]{1,0:T(8,128)(2,1)...) custom-call(s32[1,256]{1,0:T(1,128)S(1)} %bitcast.30, ...), custom_call_target="tpu_custom_call" | custom-call | flops 201326592 | bytes 2097152 | tf_op jit(solution)/shard_map/first/pallas_call | solution.py:46
  6.4 3.1 %collective-permute-start = (f32[264,128]{1,0:T(8,128)S(1)}, f32[264,128]{1,0:T(8,128)S(1)}, u32[]{:S(2)}, u32[]{:S(2)}) collective-permute-start(f32[264,128]{1,0:T(8,128)S(1)} %get-tuple-element.78), channel_id=1, source_target_pairs={{0,4},{4,0},{8,12},{12,8},{1,5},{5,1},{9,13},{13,9},{2,6},{6,2},{1... | collective-permute-start | bytes 405512 | tf_op jit(solution)/shard_map/ppermute | solution.py:302
  9.4 2.6 %collective-permute-start.1 = (f32[264,128]{1,0:T(8,128)S(1)}, f32[264,128]{1,0:T(8,128)S(1)}, u32[]{:S(2)}, u32[]{:S(2)}) collective-permute-start(f32[264,128]{1,0:T(8,128)S(1)} %get-tuple-element.79), channel_id=1, source_target_pairs={{0,8},{4,12},{8,0},{12,4},{1,9},{5,13},{9,1},{13,5},{2,10},{6,14},... | collective-permute-start | bytes 405512 | tf_op jit(solution)/shard_map/ppermute | solution.py:302
  12.7 0.9 copy-done.4
  13.7 2.5 %rest_first.2 = (f32[768,128]{1,0:T(8,128)S(1)}, f32[64,128]{1,0:T(8,128)S(1)}, bf16[768,1024]{1,0:T(8,128)(2,1)S(1)}, bf16[768,1024]{1,0:T(8,128)(2,1)S(1)}) custom-call(s32[1]{0:T(128)S(6)} %copy.15.size, f32[1024,1024]{1,0:T(8,128)S(1)} %bitcast.20, f32[1024,128]{1,0:T(8,128)S(1)} %bitcast.22, f32[1024,128]{1,0:T(8,128)S(1)} %bitcast.23, ...), custom_call_target="tpu_custom_call" | custom-call | flops 603979776 | bytes 3145728 | tf_op jit(solution)/shard_map/rest_first/pallas_call | solution.py:46
  16.2 6.4 %collective-permute-done.1.refs_1_ = f32[264,128]{1,0:T(8,128)S(1)} collective-permute-done((f32[264,128]{1,0:T(8,128)S(1)}, f32[264,128]{1,0:T(8,128)S(1)}, u32[]{:S(2)}, u32[]{:S(2)}) %collective-permute-start.1) | collective-permute-done | bytes 135200 | tf_op jit(solution)/shard_map/ppermute | solution.py:302
  22.7 0.5 coarse.2
  23.2 2.1 %collective-permute-start.3 = (f32[64,128]{1,0:T(8,128)S(1)}, f32[64,128]{1,0:T(8,128)S(1)}, u32[]{:S(2)}, u32[]{:S(2)}) collective-permute-start(f32[64,128]{1,0:T(8,128)S(1)} %get-tuple-element.85), channel_id=1, source_target_pairs={{0,4},{4,0},{8,12},{12,8},{1,5},{5,1},{9,13},{13,9},{2,6},{6,2},{1... | collective-permute-start | bytes 98312 | tf_op jit(solution)/shard_map/ppermute | solution.py:302
  25.3 1.1 %collective-permute-start.4 = (f32[64,128]{1,0:T(8,128)S(1)}, f32[64,128]{1,0:T(8,128)S(1)}, u32[]{:S(2)}, u32[]{:S(2)}) collective-permute-start(f32[64,128]{1,0:T(8,128)S(1)} %get-tuple-element.86), channel_id=1, source_target_pairs={{0,8},{4,12},{8,0},{12,4},{1,9},{5,13},{9,1},{13,5},{2,10},{6,14},... | collective-permute-start | bytes 98312 | tf_op jit(solution)/shard_map/ppermute | solution.py:302
  26.4 1.4 %collective-permute-start.5 = (f32[64,128]{1,0:T(8,128)S(1)}, f32[64,128]{1,0:T(8,128)S(1)}, u32[]{:S(2)}, u32[]{:S(2)}) collective-permute-start(f32[64,128]{1,0:T(8,128)S(1)} %get-tuple-element.87), channel_id=1, source_target_pairs={{0,12},{4,8},{8,4},{12,0},{1,13},{5,9},{9,5},{13,1},{2,14},{6,10},... | collective-permute-start | bytes 98312 | tf_op jit(solution)/shard_map/ppermute | solution.py:302
  27.8 0.4 prepare.1
  28.1 2.5 %collective-permute-done.4.refs_2_ = f32[64,128]{1,0:T(8,128)S(1)} collective-permute-done((f32[64,128]{1,0:T(8,128)S(1)}, f32[64,128]{1,0:T(8,128)S(1)}, u32[]{:S(2)}, u32[]{:S(2)}) %collective-permute-start.4) | collective-permute-done | bytes 32800 | tf_op jit(solution)/shard_map/ppermute | solution.py:302
  30.6 1.5 %collective-permute-done.5.refs_3_ = f32[64,128]{1,0:T(8,128)S(1)} collective-permute-done((f32[64,128]{1,0:T(8,128)S(1)}, f32[64,128]{1,0:T(8,128)S(1)}, u32[]{:S(2)}, u32[]{:S(2)}) %collective-permute-start.5) | collective-permute-done | bytes 32800 | tf_op jit(solution)/shard_map/ppermute | solution.py:302
  32.1 0.3 tile.4
  32.4 1.6 %collective-permute-start.7 = (f32[64,128]{1,0:T(8,128)S(1)}, f32[64,128]{1,0:T(8,128)S(1)}, u32[]{:S(2)}, u32[]{:S(2)}) collective-permute-start(f32[64,128]{1,0:T(8,128)S(1)} %get-tuple-element.90), channel_id=1, source_target_pairs={{0,2},{1,3},{2,0},{3,1},{4,6},{5,7},{6,4},{7,5},{8,10},{9,11},{10,... | collective-permute-start | bytes 98312 | tf_op jit(solution)/shard_map/ppermute | solution.py:302
  34.0 0.3 collective-permute-start.8
  34.4 2.0 %collective-permute-done.7.refs_2_ = f32[64,128]{1,0:T(8,128)S(1)} collective-permute-done((f32[64,128]{1,0:T(8,128)S(1)}, f32[64,128]{1,0:T(8,128)S(1)}, u32[]{:S(2)}, u32[]{:S(2)}) %collective-permute-start.7) | collective-permute-done | bytes 32800 | tf_op jit(solution)/shard_map/ppermute | solution.py:302
  36.4 0.9 collective-permute-done.8.refs_3_
  37.3 1.0 lift.2
  38.4 2.5 %collective-permute-start.11 = (f32[128,128]{1,0:T(8,128)S(1)}, f32[128,128]{1,0:T(8,128)S(1)}, u32[]{:S(2)}, u32[]{:S(2)}) collective-permute-start(f32[128,128]{1,0:T(8,128)S(1)} %get-tuple-element.101), channel_id=1, source_target_pairs={{0,12},{4,8},{8,4},{12,0},{1,13},{5,9},{9,5},{13,1},{2,14},{6,10},... | collective-permute-start | bytes 196616 | tf_op jit(solution)/shard_map/ppermute | solution.py:302
  40.9 1.0 collective-permute-start.9
  41.9 2.3 %rest.4 = (f32[768,128]{1,0:T(8,128)S(1)}, f32[256,128]{1,0:T(8,128)S(1)}) custom-call(s32[1]{0:T(128)S(6)} %copy.15.size, bf16[768,1024]{1,0:T(8,128)(2,1)S(1)} %get-tuple-element.105.high.operator, bf16[768,1024]{1,0:T(8,128)(2,1)S(1)} %get-tuple-element.106.low.refs_0_, f32[256,128]{1,0:T(8,128)S(1)} %get-tuple-element.104.mult_s.refs_6_, ...), custom_call_target="tpu_custom_call" | custom-call | flops 805306368 | bytes 4194304 | tf_op jit(solution)/shard_map/rest/pallas_call | solution.py:46
  44.2 1.8 %collective-permute-done.10.refs_1_ = f32[128,128]{1,0:T(8,128)S(1)} collective-permute-done((f32[128,128]{1,0:T(8,128)S(1)}, f32[128,128]{1,0:T(8,128)S(1)}, u32[]{:S(2)}, u32[]{:S(2)}) %collective-permute-start.10) | collective-permute-done | bytes 65568 | tf_op jit(solution)/shard_map/ppermute | solution.py:302
  46.0 1.2 %collective-permute-done.9.refs_0_ = f32[128,128]{1,0:T(8,128)S(1)} collective-permute-done((f32[128,128]{1,0:T(8,128)S(1)}, f32[128,128]{1,0:T(8,128)S(1)}, u32[]{:S(2)}, u32[]{:S(2)}) %collective-permute-start.9) | collective-permute-done | bytes 65568 | tf_op jit(solution)/shard_map/ppermute | solution.py:302
  47.1 0.8 sweep.3
  48.0 0.8 collective-permute-start.12
  48.8 1.5 %collective-permute-start.13 = (f32[128,128]{1,0:T(8,128)S(1)}, f32[128,128]{1,0:T(8,128)S(1)}, u32[]{:S(2)}, u32[]{:S(2)}) collective-permute-start(f32[128,128]{1,0:T(8,128)S(1)} %get-tuple-element.110), channel_id=1, source_target_pairs={{0,8},{4,12},{8,0},{12,4},{1,9},{5,13},{9,1},{13,5},{2,10},{6,14},... | collective-permute-start | bytes 196616 | tf_op jit(solution)/shard_map/ppermute | solution.py:302
  50.3 2.1 %collective-permute-start.14 = (f32[128,128]{1,0:T(8,128)S(1)}, f32[128,128]{1,0:T(8,128)S(1)}, u32[]{:S(2)}, u32[]{:S(2)}) collective-permute-start(f32[128,128]{1,0:T(8,128)S(1)} %get-tuple-element.111), channel_id=1, source_target_pairs={{0,12},{4,8},{8,4},{12,0},{1,13},{5,9},{9,5},{13,1},{2,14},{6,10},... | collective-permute-start | bytes 196616 | tf_op jit(solution)/shard_map/ppermute | solution.py:302
  52.4 2.3 %rest.5 = (f32[768,128]{1,0:T(8,128)S(1)}, f32[256,128]{1,0:T(8,128)S(1)}) custom-call(s32[1]{0:T(128)S(6)} %copy.15.size, bf16[768,1024]{1,0:T(8,128)(2,1)S(1)} %get-tuple-element.105.high.operator, bf16[768,1024]{1,0:T(8,128)(2,1)S(1)} %get-tuple-element.106.low.refs_0_, f32[256,128]{1,0:T(8,128)S(1)} %get-tuple-element.113.mult_s.refs_6_, ...), custom_call_target="tpu_custom_call" | custom-call | flops 805306368 | bytes 4194304 | tf_op jit(solution)/shard_map/rest/pallas_call | solution.py:46
  54.8 2.1 %collective-permute-done.13.refs_1_ = f32[128,128]{1,0:T(8,128)S(1)} collective-permute-done((f32[128,128]{1,0:T(8,128)S(1)}, f32[128,128]{1,0:T(8,128)S(1)}, u32[]{:S(2)}, u32[]{:S(2)}) %collective-permute-start.13) | collective-permute-done | bytes 65568 | tf_op jit(solution)/shard_map/ppermute | solution.py:302
  56.9 0.8 sweep.4
  57.7 1.3 %collective-permute-start.15 = (f32[128,128]{1,0:T(8,128)S(1)}, f32[128,128]{1,0:T(8,128)S(1)}, u32[]{:S(2)}, u32[]{:S(2)}) collective-permute-start(f32[128,128]{1,0:T(8,128)S(1)} %get-tuple-element.116), channel_id=1, source_target_pairs={{0,4},{4,0},{8,12},{12,8},{1,5},{5,1},{9,13},{13,9},{2,6},{6,2},{1... | collective-permute-start | bytes 196616 | tf_op jit(solution)/shard_map/ppermute | solution.py:302
  59.1 1.1 %collective-permute-start.16 = (f32[128,128]{1,0:T(8,128)S(1)}, f32[128,128]{1,0:T(8,128)S(1)}, u32[]{:S(2)}, u32[]{:S(2)}) collective-permute-start(f32[128,128]{1,0:T(8,128)S(1)} %get-tuple-element.117), channel_id=1, source_target_pairs={{0,8},{4,12},{8,0},{12,4},{1,9},{5,13},{9,1},{13,5},{2,10},{6,14},... | collective-permute-start | bytes 196616 | tf_op jit(solution)/shard_map/ppermute | solution.py:302
  60.2 2.0 %collective-permute-start.17 = (f32[128,128]{1,0:T(8,128)S(1)}, f32[128,128]{1,0:T(8,128)S(1)}, u32[]{:S(2)}, u32[]{:S(2)}) collective-permute-start(f32[128,128]{1,0:T(8,128)S(1)} %get-tuple-element.118), channel_id=1, source_target_pairs={{0,12},{4,8},{8,4},{12,0},{1,13},{5,9},{9,5},{13,1},{2,14},{6,10},... | collective-permute-start | bytes 196616 | tf_op jit(solution)/shard_map/ppermute | solution.py:302
  62.2 2.2 %rest_first.3 = (f32[768,128]{1,0:T(8,128)S(1)}, f32[64,128]{1,0:T(8,128)S(1)}) custom-call(s32[1]{0:T(128)S(6)} %copy.15.size, bf16[768,1024]{1,0:T(8,128)(2,1)S(1)} %get-tuple-element.105.high.operator, bf16[768,1024]{1,0:T(8,128)(2,1)S(1)} %get-tuple-element.106.low.refs_0_, f32[256,128]{1,0:T(8,128)S(1)} %get-tuple-element.120.refs_1_.refs_6_, ...), custom_call_target="tpu_custom_call" | custom-call | flops 603979776 | bytes 3145728 | tf_op jit(solution)/shard_map/rest_first/pallas_call | solution.py:46
  64.4 1.0 collective-permute-done.16.refs_1_
  65.4 1.0 collective-permute-done.17.refs_2_
  66.4 0.4 coarse.3
  66.8 1.1 %collective-permute-start.18 = (f32[64,128]{1,0:T(8,128)S(1)}, f32[64,128]{1,0:T(8,128)S(1)}, u32[]{:S(2)}, u32[]{:S(2)}) collective-permute-start(f32[64,128]{1,0:T(8,128)S(1)} %get-tuple-element.124), channel_id=1, source_target_pairs={{0,4},{4,0},{8,12},{12,8},{1,5},{5,1},{9,13},{13,9},{2,6},{6,2},{1... | collective-permute-start | bytes 98312 | tf_op jit(solution)/shard_map/ppermute | solution.py:302
  67.9 1.5 %collective-permute-start.19 = (f32[64,128]{1,0:T(8,128)S(1)}, f32[64,128]{1,0:T(8,128)S(1)}, u32[]{:S(2)}, u32[]{:S(2)}) collective-permute-start(f32[64,128]{1,0:T(8,128)S(1)} %get-tuple-element.125), channel_id=1, source_target_pairs={{0,8},{4,12},{8,0},{12,4},{1,9},{5,13},{9,1},{13,5},{2,10},{6,14},... | collective-permute-start | bytes 98312 | tf_op jit(solution)/shard_map/ppermute | solution.py:302
  69.5 1.8 %collective-permute-start.20 = (f32[64,128]{1,0:T(8,128)S(1)}, f32[64,128]{1,0:T(8,128)S(1)}, u32[]{:S(2)}, u32[]{:S(2)}) collective-permute-start(f32[64,128]{1,0:T(8,128)S(1)} %get-tuple-element.126), channel_id=1, source_target_pairs={{0,12},{4,8},{8,4},{12,0},{1,13},{5,9},{9,5},{13,1},{2,14},{6,10},... | collective-permute-start | bytes 98312 | tf_op jit(solution)/shard_map/ppermute | solution.py:302
  71.3 1.4 %collective-permute-done.19.refs_2_ = f32[64,128]{1,0:T(8,128)S(1)} collective-permute-done((f32[64,128]{1,0:T(8,128)S(1)}, f32[64,128]{1,0:T(8,128)S(1)}, u32[]{:S(2)}, u32[]{:S(2)}) %collective-permute-start.19) | collective-permute-done | bytes 32800 | tf_op jit(solution)/shard_map/ppermute | solution.py:302
  72.7 2.4 %collective-permute-done.20.refs_3_ = f32[64,128]{1,0:T(8,128)S(1)} collective-permute-done((f32[64,128]{1,0:T(8,128)S(1)}, f32[64,128]{1,0:T(8,128)S(1)}, u32[]{:S(2)}, u32[]{:S(2)}) %collective-permute-start.20) | collective-permute-done | bytes 32800 | tf_op jit(solution)/shard_map/ppermute | solution.py:302
  75.5 1.0 collective-permute-start.22
  76.5 0.9 collective-permute-start.23
  77.4 2.1 %collective-permute-done.22.refs_2_ = f32[64,128]{1,0:T(8,128)S(1)} collective-permute-done((f32[64,128]{1,0:T(8,128)S(1)}, f32[64,128]{1,0:T(8,128)S(1)}, u32[]{:S(2)}, u32[]{:S(2)}) %collective-permute-start.22) | collective-permute-done | bytes 32800 | tf_op jit(solution)/shard_map/ppermute | solution.py:302
  79.5 0.4 collective-permute-done.23.refs_3_
  79.9 1.0 lift.3
  81.0 2.4 %collective-permute-start.25 = (f32[128,128]{1,0:T(8,128)S(1)}, f32[128,128]{1,0:T(8,128)S(1)}, u32[]{:S(2)}, u32[]{:S(2)}) collective-permute-start(f32[128,128]{1,0:T(8,128)S(1)} %get-tuple-element.134), channel_id=1, source_target_pairs={{0,8},{4,12},{8,0},{12,4},{1,9},{5,13},{9,1},{13,5},{2,10},{6,14},... | collective-permute-start | bytes 196616 | tf_op jit(solution)/shard_map/ppermute | solution.py:302
  83.3 2.0 %collective-permute-start.26 = (f32[128,128]{1,0:T(8,128)S(1)}, f32[128,128]{1,0:T(8,128)S(1)}, u32[]{:S(2)}, u32[]{:S(2)}) collective-permute-start(f32[128,128]{1,0:T(8,128)S(1)} %get-tuple-element.135), channel_id=1, source_target_pairs={{0,12},{4,8},{8,4},{12,0},{1,13},{5,9},{9,5},{13,1},{2,14},{6,10},... | collective-permute-start | bytes 196616 | tf_op jit(solution)/shard_map/ppermute | solution.py:302
  85.3 2.3 %rest.6 = (f32[768,128]{1,0:T(8,128)S(1)}, f32[256,128]{1,0:T(8,128)S(1)}) custom-call(s32[1]{0:T(128)S(6)} %copy.15.size, bf16[768,1024]{1,0:T(8,128)(2,1)S(1)} %get-tuple-element.105.high.operator, bf16[768,1024]{1,0:T(8,128)(2,1)S(1)} %get-tuple-element.106.low.refs_0_, f32[256,128]{1,0:T(8,128)S(1)} %get-tuple-element.137.mult_s.refs_6_, ...), custom_call_target="tpu_custom_call" | custom-call | flops 805306368 | bytes 4194304 | tf_op jit(solution)/shard_map/rest/pallas_call | solution.py:46
  87.7 1.9 %collective-permute-done.25.refs_1_ = f32[128,128]{1,0:T(8,128)S(1)} collective-permute-done((f32[128,128]{1,0:T(8,128)S(1)}, f32[128,128]{1,0:T(8,128)S(1)}, u32[]{:S(2)}, u32[]{:S(2)}) %collective-permute-start.25) | collective-permute-done | bytes 65568 | tf_op jit(solution)/shard_map/ppermute | solution.py:302
  89.6 0.8 sweep.5
  90.4 1.3 %collective-permute-start.27 = (f32[128,128]{1,0:T(8,128)S(1)}, f32[128,128]{1,0:T(8,128)S(1)}, u32[]{:S(2)}, u32[]{:S(2)}) collective-permute-start(f32[128,128]{1,0:T(8,128)S(1)} %get-tuple-element.140), channel_id=1, source_target_pairs={{0,4},{4,0},{8,12},{12,8},{1,5},{5,1},{9,13},{13,9},{2,6},{6,2},{1... | collective-permute-start | bytes 196616 | tf_op jit(solution)/shard_map/ppermute | solution.py:302
  91.7 1.2 %collective-permute-start.28 = (f32[128,128]{1,0:T(8,128)S(1)}, f32[128,128]{1,0:T(8,128)S(1)}, u32[]{:S(2)}, u32[]{:S(2)}) collective-permute-start(f32[128,128]{1,0:T(8,128)S(1)} %get-tuple-element.141), channel_id=1, source_target_pairs={{0,8},{4,12},{8,0},{12,4},{1,9},{5,13},{9,1},{13,5},{2,10},{6,14},... | collective-permute-start | bytes 196616 | tf_op jit(solution)/shard_map/ppermute | solution.py:302
  93.0 1.9 %collective-permute-start.29 = (f32[128,128]{1,0:T(8,128)S(1)}, f32[128,128]{1,0:T(8,128)S(1)}, u32[]{:S(2)}, u32[]{:S(2)}) collective-permute-start(f32[128,128]{1,0:T(8,128)S(1)} %get-tuple-element.142), channel_id=1, source_target_pairs={{0,12},{4,8},{8,4},{12,0},{1,13},{5,9},{9,5},{13,1},{2,14},{6,10},... | collective-permute-start | bytes 196616 | tf_op jit(solution)/shard_map/ppermute | solution.py:302
  94.8 2.4 %rest.7 = (f32[1024,128]{1,0:T(8,128)}, f32[1024,128]{1,0:T(8,128)}) custom-call(s32[1]{0:T(128)S(6)} %copy.15.size, bf16[768,1024]{1,0:T(8,128)(2,1)S(1)} %get-tuple-element.105.high.operator, bf16[768,1024]{1,0:T(8,128)(2,1)S(1)} %get-tuple-element.106.low.refs_0_, f32[256,128]{1,0:T(8,128)S(1)} %get-tuple-element.144.mult_s.refs_6_, ...), custom_call_target="tpu_custom_call" | custom-call | flops 805306368 | bytes 4194304 | tf_op jit(solution)/shard_map/rest/pallas_call | solution.py:46
  97.2 0.7 collective-permute-done.28.refs_1_
  97.9 1.2 %collective-permute-done.29.refs_2_ = f32[128,128]{1,0:T(8,128)S(1)} collective-permute-done((f32[128,128]{1,0:T(8,128)S(1)}, f32[128,128]{1,0:T(8,128)S(1)}, u32[]{:S(2)}, u32[]{:S(2)}) %collective-permute-start.29) | collective-permute-done | bytes 65568 | tf_op jit(solution)/shard_map/ppermute | solution.py:302
  99.1 1.0 last.1
  (35 shorter events, 0.8 us)
Async XLA Ops:
  0.6 2.2 %copy-start.1 = (f32[1,1024,1024]{2,1,0:T(8,128)S(1)}, f32[1,1024,1024]{2,1,0:T(8,128)}, u32[]{:S(2)}) copy-start(f32[1,1024,1024]{2,1,0:T(8,128)} %param.9) | copy-start | bytes 12582916
  2.8 1.0 %copy-start.3 = (f32[1,1024,128]{2,1,0:T(8,128)S(1)}, f32[1,1024,128]{2,1,0:T(8,128)}, u32[]{:S(2)}) copy-start(f32[1,1024,128]{2,1,0:T(8,128)} %param.13) | copy-start | bytes 1572868
  3.9 0.7 copy-start.8
  4.5 0.7 copy-start.9
  5.2 7.5 %copy-start = (f32[1,1024,128]{2,1,0:T(8,128)S(1)}, f32[1,1024,128]{2,1,0:T(8,128)}, u32[]{:S(2)}) copy-start(f32[1,1024,128]{2,1,0:T(8,128)} %param.12) | copy-start | bytes 1572868
  5.2 7.5 %copy-start.2 = (f32[1,1024,1024]{2,1,0:T(8,128)S(1)}, f32[1,1024,1024]{2,1,0:T(8,128)}, u32[]{:S(2)}) copy-start(f32[1,1024,1024]{2,1,0:T(8,128)} %param.9) | copy-start | bytes 12582916
  6.4 9.9 %collective-permute-start = (f32[264,128]{1,0:T(8,128)S(1)}, f32[264,128]{1,0:T(8,128)S(1)}, u32[]{:S(2)}, u32[]{:S(2)}) collective-permute-start(f32[264,128]{1,0:T(8,128)S(1)} %get-tuple-element.78), channel_id=1, source_target_pairs={{0,4},{4,0},{8,12},{12,8},{1,5},{5,1},{9,13},{13,9},{2,6},{6,2},{1... | collective-permute-start | bytes 405512 | tf_op jit(solution)/shard_map/ppermute | solution.py:302
  9.4 13.2 %collective-permute-start.1 = (f32[264,128]{1,0:T(8,128)S(1)}, f32[264,128]{1,0:T(8,128)S(1)}, u32[]{:S(2)}, u32[]{:S(2)}) collective-permute-start(f32[264,128]{1,0:T(8,128)S(1)} %get-tuple-element.79), channel_id=1, source_target_pairs={{0,8},{4,12},{8,0},{12,4},{1,9},{5,13},{9,1},{13,5},{2,10},{6,14},... | collective-permute-start | bytes 405512 | tf_op jit(solution)/shard_map/ppermute | solution.py:302
  12.0 10.6 %collective-permute-start.2 = (f32[264,128]{1,0:T(8,128)S(1)}, f32[264,128]{1,0:T(8,128)S(1)}, u32[]{:S(2)}, u32[]{:S(2)}) collective-permute-start(f32[264,128]{1,0:T(8,128)S(1)} %get-tuple-element.80), channel_id=1, source_target_pairs={{0,12},{4,8},{8,4},{12,0},{1,13},{5,9},{9,5},{13,1},{2,14},{6,10},... | collective-permute-start | bytes 405512 | tf_op jit(solution)/shard_map/ppermute | solution.py:302
  12.7 1.0 copy-start.4
  16.2 11.5 %copy-start.6 = (f32[256,256]{1,0:T(8,128)S(1)}, f32[256,256]{1,0:T(8,128)}, u32[]{:S(2)}) copy-start(f32[256,256]{1,0:T(8,128)} %tile.3) | copy-start | bytes 786436
  16.2 11.5 %copy-start.7 = (s32[1,1024]{1,0:T(1,128)S(1)}, s32[1,1024]{1,0:T(1,128)}, u32[]{:S(2)}) copy-start(s32[1,1024]{1,0:T(1,128)} %contact.1) | copy-start | bytes 12292
  23.2 5.0 %collective-permute-start.3 = (f32[64,128]{1,0:T(8,128)S(1)}, f32[64,128]{1,0:T(8,128)S(1)}, u32[]{:S(2)}, u32[]{:S(2)}) collective-permute-start(f32[64,128]{1,0:T(8,128)S(1)} %get-tuple-element.85), channel_id=1, source_target_pairs={{0,4},{4,0},{8,12},{12,8},{1,5},{5,1},{9,13},{13,9},{2,6},{6,2},{1... | collective-permute-start | bytes 98312 | tf_op jit(solution)/shard_map/ppermute | solution.py:302
  25.3 5.3 %collective-permute-start.4 = (f32[64,128]{1,0:T(8,128)S(1)}, f32[64,128]{1,0:T(8,128)S(1)}, u32[]{:S(2)}, u32[]{:S(2)}) collective-permute-start(f32[64,128]{1,0:T(8,128)S(1)} %get-tuple-element.86), channel_id=1, source_target_pairs={{0,8},{4,12},{8,0},{12,4},{1,9},{5,13},{9,1},{13,5},{2,10},{6,14},... | collective-permute-start | bytes 98312 | tf_op jit(solution)/shard_map/ppermute | solution.py:302
  26.4 5.7 %collective-permute-start.5 = (f32[64,128]{1,0:T(8,128)S(1)}, f32[64,128]{1,0:T(8,128)S(1)}, u32[]{:S(2)}, u32[]{:S(2)}) collective-permute-start(f32[64,128]{1,0:T(8,128)S(1)} %get-tuple-element.87), channel_id=1, source_target_pairs={{0,12},{4,8},{8,4},{12,0},{1,13},{5,9},{9,5},{13,1},{2,14},{6,10},... | collective-permute-start | bytes 98312 | tf_op jit(solution)/shard_map/ppermute | solution.py:302
  32.3 2.1 %collective-permute-start.6 = (f32[64,128]{1,0:T(8,128)S(1)}, f32[64,128]{1,0:T(8,128)S(1)}, u32[]{:S(2)}, u32[]{:S(2)}) collective-permute-start(f32[64,128]{1,0:T(8,128)S(1)} %get-tuple-element.89), channel_id=1, source_target_pairs={{0,1},{1,0},{2,3},{3,2},{4,5},{5,4},{6,7},{7,6},{8,9},{9,8},{10,11... | collective-permute-start | bytes 98312 | tf_op jit(solution)/shard_map/ppermute | solution.py:302
  32.4 4.0 %collective-permute-start.7 = (f32[64,128]{1,0:T(8,128)S(1)}, f32[64,128]{1,0:T(8,128)S(1)}, u32[]{:S(2)}, u32[]{:S(2)}) collective-permute-start(f32[64,128]{1,0:T(8,128)S(1)} %get-tuple-element.90), channel_id=1, source_target_pairs={{0,2},{1,3},{2,0},{3,1},{4,6},{5,7},{6,4},{7,5},{8,10},{9,11},{10,... | collective-permute-start | bytes 98312 | tf_op jit(solution)/shard_map/ppermute | solution.py:302
  34.0 3.3 %collective-permute-start.8 = (f32[64,128]{1,0:T(8,128)S(1)}, f32[64,128]{1,0:T(8,128)S(1)}, u32[]{:S(2)}, u32[]{:S(2)}) collective-permute-start(f32[64,128]{1,0:T(8,128)S(1)} %get-tuple-element.91), channel_id=1, source_target_pairs={{0,3},{1,2},{2,1},{3,0},{4,7},{5,6},{6,5},{7,4},{8,11},{9,10},{10,... | collective-permute-start | bytes 98312 | tf_op jit(solution)/shard_map/ppermute | solution.py:302
  38.3 7.7 %collective-permute-start.10 = (f32[128,128]{1,0:T(8,128)S(1)}, f32[128,128]{1,0:T(8,128)S(1)}, u32[]{:S(2)}, u32[]{:S(2)}) collective-permute-start(f32[128,128]{1,0:T(8,128)S(1)} %get-tuple-element.100), channel_id=1, source_target_pairs={{0,8},{4,12},{8,0},{12,4},{1,9},{5,13},{9,1},{13,5},{2,10},{6,14},... | collective-permute-start | bytes 196616 | tf_op jit(solution)/shard_map/ppermute | solution.py:302
  38.4 7.6 %collective-permute-start.11 = (f32[128,128]{1,0:T(8,128)S(1)}, f32[128,128]{1,0:T(8,128)S(1)}, u32[]{:S(2)}, u32[]{:S(2)}) collective-permute-start(f32[128,128]{1,0:T(8,128)S(1)} %get-tuple-element.101), channel_id=1, source_target_pairs={{0,12},{4,8},{8,4},{12,0},{1,13},{5,9},{9,5},{13,1},{2,14},{6,10},... | collective-permute-start | bytes 196616 | tf_op jit(solution)/shard_map/ppermute | solution.py:302
  40.9 6.3 %collective-permute-start.9 = (f32[128,128]{1,0:T(8,128)S(1)}, f32[128,128]{1,0:T(8,128)S(1)}, u32[]{:S(2)}, u32[]{:S(2)}) collective-permute-start(f32[128,128]{1,0:T(8,128)S(1)} %get-tuple-element.99), channel_id=1, source_target_pairs={{0,4},{4,0},{8,12},{12,8},{1,5},{5,1},{9,13},{13,9},{2,6},{6,2},{1... | collective-permute-start | bytes 196616 | tf_op jit(solution)/shard_map/ppermute | solution.py:302
  48.0 6.8 %collective-permute-start.12 = (f32[128,128]{1,0:T(8,128)S(1)}, f32[128,128]{1,0:T(8,128)S(1)}, u32[]{:S(2)}, u32[]{:S(2)}) collective-permute-start(f32[128,128]{1,0:T(8,128)S(1)} %get-tuple-element.109), channel_id=1, source_target_pairs={{0,4},{4,0},{8,12},{12,8},{1,5},{5,1},{9,13},{13,9},{2,6},{6,2},{1... | collective-permute-start | bytes 196616 | tf_op jit(solution)/shard_map/ppermute | solution.py:302
  48.8 8.1 %collective-permute-start.13 = (f32[128,128]{1,0:T(8,128)S(1)}, f32[128,128]{1,0:T(8,128)S(1)}, u32[]{:S(2)}, u32[]{:S(2)}) collective-permute-start(f32[128,128]{1,0:T(8,128)S(1)} %get-tuple-element.110), channel_id=1, source_target_pairs={{0,8},{4,12},{8,0},{12,4},{1,9},{5,13},{9,1},{13,5},{2,10},{6,14},... | collective-permute-start | bytes 196616 | tf_op jit(solution)/shard_map/ppermute | solution.py:302
  50.3 6.6 %collective-permute-start.14 = (f32[128,128]{1,0:T(8,128)S(1)}, f32[128,128]{1,0:T(8,128)S(1)}, u32[]{:S(2)}, u32[]{:S(2)}) collective-permute-start(f32[128,128]{1,0:T(8,128)S(1)} %get-tuple-element.111), channel_id=1, source_target_pairs={{0,12},{4,8},{8,4},{12,0},{1,13},{5,9},{9,5},{13,1},{2,14},{6,10},... | collective-permute-start | bytes 196616 | tf_op jit(solution)/shard_map/ppermute | solution.py:302
  56.9 5.3 %copy-start.5 = (f32[1,64,1024]{2,1,0:T(8,128)S(1)}, f32[1,64,1024]{2,1,0:T(8,128)}, u32[]{:S(2)}) copy-start(f32[1,64,1024]{2,1,0:T(8,128)} %param.11) | copy-start | bytes 786436
  57.7 6.7 %collective-permute-start.15 = (f32[128,128]{1,0:T(8,128)S(1)}, f32[128,128]{1,0:T(8,128)S(1)}, u32[]{:S(2)}, u32[]{:S(2)}) collective-permute-start(f32[128,128]{1,0:T(8,128)S(1)} %get-tuple-element.116), channel_id=1, source_target_pairs={{0,4},{4,0},{8,12},{12,8},{1,5},{5,1},{9,13},{13,9},{2,6},{6,2},{1... | collective-permute-start | bytes 196616 | tf_op jit(solution)/shard_map/ppermute | solution.py:302
  59.1 6.4 %collective-permute-start.16 = (f32[128,128]{1,0:T(8,128)S(1)}, f32[128,128]{1,0:T(8,128)S(1)}, u32[]{:S(2)}, u32[]{:S(2)}) collective-permute-start(f32[128,128]{1,0:T(8,128)S(1)} %get-tuple-element.117), channel_id=1, source_target_pairs={{0,8},{4,12},{8,0},{12,4},{1,9},{5,13},{9,1},{13,5},{2,10},{6,14},... | collective-permute-start | bytes 196616 | tf_op jit(solution)/shard_map/ppermute | solution.py:302
  60.2 6.2 %collective-permute-start.17 = (f32[128,128]{1,0:T(8,128)S(1)}, f32[128,128]{1,0:T(8,128)S(1)}, u32[]{:S(2)}, u32[]{:S(2)}) collective-permute-start(f32[128,128]{1,0:T(8,128)S(1)} %get-tuple-element.118), channel_id=1, source_target_pairs={{0,12},{4,8},{8,4},{12,0},{1,13},{5,9},{9,5},{13,1},{2,14},{6,10},... | collective-permute-start | bytes 196616 | tf_op jit(solution)/shard_map/ppermute | solution.py:302
  66.8 4.5 %collective-permute-start.18 = (f32[64,128]{1,0:T(8,128)S(1)}, f32[64,128]{1,0:T(8,128)S(1)}, u32[]{:S(2)}, u32[]{:S(2)}) collective-permute-start(f32[64,128]{1,0:T(8,128)S(1)} %get-tuple-element.124), channel_id=1, source_target_pairs={{0,4},{4,0},{8,12},{12,8},{1,5},{5,1},{9,13},{13,9},{2,6},{6,2},{1... | collective-permute-start | bytes 98312 | tf_op jit(solution)/shard_map/ppermute | solution.py:302
  67.9 4.8 %collective-permute-start.19 = (f32[64,128]{1,0:T(8,128)S(1)}, f32[64,128]{1,0:T(8,128)S(1)}, u32[]{:S(2)}, u32[]{:S(2)}) collective-permute-start(f32[64,128]{1,0:T(8,128)S(1)} %get-tuple-element.125), channel_id=1, source_target_pairs={{0,8},{4,12},{8,0},{12,4},{1,9},{5,13},{9,1},{13,5},{2,10},{6,14},... | collective-permute-start | bytes 98312 | tf_op jit(solution)/shard_map/ppermute | solution.py:302
  69.5 5.7 %collective-permute-start.20 = (f32[64,128]{1,0:T(8,128)S(1)}, f32[64,128]{1,0:T(8,128)S(1)}, u32[]{:S(2)}, u32[]{:S(2)}) collective-permute-start(f32[64,128]{1,0:T(8,128)S(1)} %get-tuple-element.126), channel_id=1, source_target_pairs={{0,12},{4,8},{8,4},{12,0},{1,13},{5,9},{9,5},{13,1},{2,14},{6,10},... | collective-permute-start | bytes 98312 | tf_op jit(solution)/shard_map/ppermute | solution.py:302
  75.4 1.9 %collective-permute-start.21 = (f32[64,128]{1,0:T(8,128)S(1)}, f32[64,128]{1,0:T(8,128)S(1)}, u32[]{:S(2)}, u32[]{:S(2)}) collective-permute-start(f32[64,128]{1,0:T(8,128)S(1)} %get-tuple-element.128), channel_id=1, source_target_pairs={{0,1},{1,0},{2,3},{3,2},{4,5},{5,4},{6,7},{7,6},{8,9},{9,8},{10,11... | collective-permute-start | bytes 98312 | tf_op jit(solution)/shard_map/ppermute | solution.py:302
  75.5 4.0 %collective-permute-start.22 = (f32[64,128]{1,0:T(8,128)S(1)}, f32[64,128]{1,0:T(8,128)S(1)}, u32[]{:S(2)}, u32[]{:S(2)}) collective-permute-start(f32[64,128]{1,0:T(8,128)S(1)} %get-tuple-element.129), channel_id=1, source_target_pairs={{0,2},{1,3},{2,0},{3,1},{4,6},{5,7},{6,4},{7,5},{8,10},{9,11},{10,... | collective-permute-start | bytes 98312 | tf_op jit(solution)/shard_map/ppermute | solution.py:302
  76.5 3.4 %collective-permute-start.23 = (f32[64,128]{1,0:T(8,128)S(1)}, f32[64,128]{1,0:T(8,128)S(1)}, u32[]{:S(2)}, u32[]{:S(2)}) collective-permute-start(f32[64,128]{1,0:T(8,128)S(1)} %get-tuple-element.130), channel_id=1, source_target_pairs={{0,3},{1,2},{2,1},{3,0},{4,7},{5,6},{6,5},{7,4},{8,11},{9,10},{10,... | collective-permute-start | bytes 98312 | tf_op jit(solution)/shard_map/ppermute | solution.py:302
  80.9 6.8 %collective-permute-start.24 = (f32[128,128]{1,0:T(8,128)S(1)}, f32[128,128]{1,0:T(8,128)S(1)}, u32[]{:S(2)}, u32[]{:S(2)}) collective-permute-start(f32[128,128]{1,0:T(8,128)S(1)} %get-tuple-element.133), channel_id=1, source_target_pairs={{0,4},{4,0},{8,12},{12,8},{1,5},{5,1},{9,13},{13,9},{2,6},{6,2},{1... | collective-permute-start | bytes 196616 | tf_op jit(solution)/shard_map/ppermute | solution.py:302
  81.0 8.6 %collective-permute-start.25 = (f32[128,128]{1,0:T(8,128)S(1)}, f32[128,128]{1,0:T(8,128)S(1)}, u32[]{:S(2)}, u32[]{:S(2)}) collective-permute-start(f32[128,128]{1,0:T(8,128)S(1)} %get-tuple-element.134), channel_id=1, source_target_pairs={{0,8},{4,12},{8,0},{12,4},{1,9},{5,13},{9,1},{13,5},{2,10},{6,14},... | collective-permute-start | bytes 196616 | tf_op jit(solution)/shard_map/ppermute | solution.py:302
  83.3 6.2 %collective-permute-start.26 = (f32[128,128]{1,0:T(8,128)S(1)}, f32[128,128]{1,0:T(8,128)S(1)}, u32[]{:S(2)}, u32[]{:S(2)}) collective-permute-start(f32[128,128]{1,0:T(8,128)S(1)} %get-tuple-element.135), channel_id=1, source_target_pairs={{0,12},{4,8},{8,4},{12,0},{1,13},{5,9},{9,5},{13,1},{2,14},{6,10},... | collective-permute-start | bytes 196616 | tf_op jit(solution)/shard_map/ppermute | solution.py:302
  90.4 6.8 %collective-permute-start.27 = (f32[128,128]{1,0:T(8,128)S(1)}, f32[128,128]{1,0:T(8,128)S(1)}, u32[]{:S(2)}, u32[]{:S(2)}) collective-permute-start(f32[128,128]{1,0:T(8,128)S(1)} %get-tuple-element.140), channel_id=1, source_target_pairs={{0,4},{4,0},{8,12},{12,8},{1,5},{5,1},{9,13},{13,9},{2,6},{6,2},{1... | collective-permute-start | bytes 196616 | tf_op jit(solution)/shard_map/ppermute | solution.py:302
  91.7 6.2 %collective-permute-start.28 = (f32[128,128]{1,0:T(8,128)S(1)}, f32[128,128]{1,0:T(8,128)S(1)}, u32[]{:S(2)}, u32[]{:S(2)}) collective-permute-start(f32[128,128]{1,0:T(8,128)S(1)} %get-tuple-element.141), channel_id=1, source_target_pairs={{0,8},{4,12},{8,0},{12,4},{1,9},{5,13},{9,1},{13,5},{2,10},{6,14},... | collective-permute-start | bytes 196616 | tf_op jit(solution)/shard_map/ppermute | solution.py:302
  93.0 6.2 %collective-permute-start.29 = (f32[128,128]{1,0:T(8,128)S(1)}, f32[128,128]{1,0:T(8,128)S(1)}, u32[]{:S(2)}, u32[]{:S(2)}) collective-permute-start(f32[128,128]{1,0:T(8,128)S(1)} %get-tuple-element.142), channel_id=1, source_target_pairs={{0,12},{4,8},{8,4},{12,0},{1,13},{5,9},{9,5},{13,1},{2,14},{6,10},... | collective-permute-start | bytes 196616 | tf_op jit(solution)/shard_map/ppermute | solution.py:302

commit v5 on v4

--- a/solution.py
+++ b/solution.py
@@ -10,7 +10,6 @@
 OUTER = 2
 INNER = 3
 STEP = 0.3
-LEADS = ((1, 3), (3, 1), (1, 2), (2, 1))
 F32 = jnp.float32
 BF16 = jnp.bfloat16
 PARAMS = pltpu.CompilerParams(vmem_limit_bytes=24 * 1024 * 1024)
@@ -42,11 +41,18 @@
     return lax.broadcasted_iota(jnp.int32, (rows, width), 0) + start < size
 
 
-def call(body, ins, in_specs, outs, out_specs, scratch=(), grid=(1,), flops=0, moved=0, alias=None, name=None):
+def call(body, ins, outs, in_specs=None, out_specs=None, scratch=(), grid=(), flops=0, moved=0, alias=None, name=None):
+    if in_specs is None:
+        in_specs = [SMEM if value.ndim == 1 else VMEM for value in ins]
+    if out_specs is None:
+        out_specs = [VMEM] * len(outs)
     return pl.pallas_call(
         body,
         out_shape=outs,
-        grid_spec=pl.GridSpec(grid=grid, in_specs=in_specs, out_specs=out_specs, scratch_shapes=list(scratch)),
+        grid=grid,
+        in_specs=in_specs,
+        out_specs=out_specs,
+        scratch_shapes=list(scratch),
         compiler_params=PARAMS,
         cost_estimate=pl.CostEstimate(flops=flops, bytes_accessed=moved, transcendentals=0),
         input_output_aliases=alias or {},
@@ -66,15 +72,17 @@
 
 SMEM = pl.BlockSpec(memory_space=pltpu.SMEM)
 HBM = pl.BlockSpec(memory_space=pltpu.HBM)
+VMEM = pl.BlockSpec(memory_space=pltpu.VMEM)
 
 
 def shape(rows, columns, dtype=F32):
     return jax.ShapeDtypeStruct((rows, columns), dtype)
 
 
-def first_kernel(wide, cap, peers_at, rows_at, operator_at, mult_at, *refs):
+def first_kernel(order, cap, peers_at, rows_at, operator_at, mult_at, *refs):
     unpack_all, unpack, high, low, image = refs[:5]
-    sends, (peers, rows, operator, mult, done) = refs[5:4 + wide], refs[4 + wide:]
+    n = len(order)
+    sends, (peers, rows, operator, mult, done) = refs[5:5 + n], refs[5 + n:]
     shared, width = image.shape
     copies = [
         pltpu.make_async_copy(source, target, done.at[i])
@@ -95,20 +103,23 @@
     ).astype(jnp.int32)
     wanted = jnp.broadcast_to(rows[...], (shared, shared)).T[:, :1]
     far = down[:, :1] ^ lax.axis_index("wide")
+    at = jnp.zeros_like(far)
+    for k, d in enumerate(order, 1):
+        at = jnp.where(far == d, k, at)
 
     def marks(key, columns):
         hit = key == lax.broadcasted_iota(jnp.int32, (shared, columns), 1)
         return jnp.where(hit, 1.0, 0.0).astype(BF16)
 
-    unpack_all[...] = marks(far * shared + wanted, unpack_all.shape[1])
+    unpack_all[...] = marks(at * shared + wanted, unpack_all.shape[1])
     unpack[...] = marks(
-        jnp.where(far == 0, wanted, shared + (far - 1) * cap + slot), unpack.shape[1]
+        jnp.where(at == 0, wanted, shared + (at - 1) * cap + slot), unpack.shape[1]
     )
     lane = lax.broadcasted_iota(jnp.int32, (shared, width), 1)
-    for d, out in enumerate(sends, 1):
+    for k, out in enumerate(sends, 1):
         out[shared:, :] = jnp.zeros((out.shape[0] - shared, width), F32)
         for c in range(-(-cap // width)):
-            hit = (far == d) & (slot == lane + c * width)
+            hit = (at == k) & (slot == lane + c * width)
             out[shared + c:shared + c + 1, :] = jnp.sum(
                 jnp.where(hit, wanted.astype(F32), 0.0), axis=0, keepdims=True
             )
@@ -169,7 +180,7 @@
     own = image[...]
     jump = own - arrived(recvs, own, unpack)
     alive = live(size[0], 0, *own.shape)
-    return jnp.where(alive, gap[...] - jump, 0.0), alive
+    return jnp.where(alive, gap[:own.shape[0], :] - jump, 0.0), alive
 
 
 def rest_first_kernel(pieces, given_parts, size, operator, *refs):
@@ -240,20 +251,21 @@
     recvs = refs[:n]
     image, unpack, gap, mult, modes, started, trial = refs[n:n + 7]
     residual, _ = shared_residual(recvs, image, unpack, gap, size)
-    coarse = started[...] + product(split(modes[...]), split(residual))
+    coarse = started[...] + product(split(modes[:, :image.shape[0]]), split(residual))
     for out in refs[n + 7:]:
         out[...] = coarse
-    trial[...] = mult[...] + STEP * residual
-
-
-def tile_kernel(n, m, high, low, *refs):
+    trial[...] = mult[:image.shape[0], :] + STEP * residual
+
+
+def tile_kernel(wide_order, narrow_order, high, low, *refs):
+    n, m = len(wide_order), len(narrow_order)
     blocks, outs, (gathered, parts) = refs[:n + 1], refs[n + 1:n + m + 2], refs[n + m + 2:]
     count = blocks[0].shape[0]
-    for d, ref in enumerate(blocks):
+    for d, ref in zip((0, *wide_order), blocks):
         at = pl.multiple_of((lax.axis_index("wide") ^ d) * count, count)
         gathered[pl.ds(at, count), :] = ref[...]
     parts[...] = product((high[...], low[...]), split(gathered[...]))
-    for d, out in enumerate(outs):
+    for d, out in zip((0, *narrow_order), outs):
         at = pl.multiple_of((lax.axis_index("narrow") ^ d) * count, count)
         out[...] = parts[pl.ds(at, count), :]
 
@@ -283,30 +295,43 @@
     image, unpack, gap, mult, floor, high, low, ahead, pack, mult_out, image_out = refs[n:n + 11]
     sends = refs[n + 11:]
     residual, alive = shared_residual(recvs, image, unpack, gap, size)
-    value = settle(mult[...] + STEP * residual, floor[...], alive)
+    shared = image.shape[0]
+    value = settle(mult[...] + STEP * residual, floor[:shared, :], alive)
     mult_out[...] = value
-    value = ahead[...] + product((high[...], low[...]), split(value))
+    value = ahead[...] + product((high[:, :shared], low[:, :shared]), split(value))
     image_out[...] = value
     send(cap, pack[...], value, sends)
 
 
 def last_kernel(n, size, *refs):
     recvs = refs[:n]
-    image, unpack, gap, mult, floor, _, _, mult_out, residual_out = refs[n:]
+    image, unpack, gap, mult, floor, _, _, mult_out, residual_out, settled, left, done = refs[n:]
+    shared = image.shape[0]
     residual, alive = shared_residual(recvs, image, unpack, gap, size)
-    mult_out[...] = settle(mult[...] + STEP * residual, floor[...], alive)
-    residual_out[...] = residual
+    left[...] = residual
+    first = pltpu.make_async_copy(left, residual_out.at[pl.ds(0, shared)], done.at[0])
+    first.start()
+    settled[...] = settle(mult[...] + STEP * residual, floor[:shared, :], alive)
+    second = pltpu.make_async_copy(settled, mult_out.at[pl.ds(0, shared)], done.at[1])
+    second.start()
+    first.wait()
+    second.wait()
 
 
 def swap(block, axis, count, d):
     return lax.ppermute(block, axis, [(i, i ^ d) for i in range(count)])
 
 
-def swap_all(blocks, axis, count, lead=()):
-    lead = [d for d in lead if d < count]
-    order = lead + [d for d in range(count - 1, 0, -1) if d not in lead]
-    got = {d: swap(blocks[d - 1], axis, count, d) for d in order}
-    return [got[d] for d in range(1, count)]
+def swap_all(blocks, axis, count, order):
+    return [swap(block, axis, count, d) for block, d in zip(blocks, order)]
+
+
+def middle_first(count):
+    return (count - 1, *range(1, count - 1))
+
+
+def far_first(count):
+    return tuple(range(count - 1, 0, -1))
 
 
 def local(
@@ -336,24 +361,23 @@
     listed = n * cap
     padded = -(-listed // 128) * 128
     size = interface_size
+    rows_order, coarse_order, part_order = middle_first(wide), far_first(wide), far_first(narrow)
     top = whole((shared, loads))
     sent = [shape(cap, loads)] * n
-    sent_specs = [whole((cap, loads))] * n
     full = 2 * order * loads
 
     list_rows = -(-(-(-cap // loads)) // 8) * 8
     unpack_all, unpack, top_high, top_low, image, *sends = call(
-        functools.partial(first_kernel, wide, cap),
-        (peer_list[0].reshape(1, shared), partner_row, operator, mult),
-        [HBM] * 4,
+        functools.partial(first_kernel, rows_order, cap),
+        tuple(
+            pltpu.with_memory_space_constraint(value, pltpu.HBM)
+            for value in (peer_list[0].reshape(1, shared), partner_row, operator, mult)
+        ),
         [shape(shared, wide * shared, BF16), shape(shared, shared + padded, BF16)]
         + [shape(shared, order, BF16)] * 2
         + [shape(shared, loads)]
         + [shape(shared + list_rows, loads)] * n,
-        [whole((shared, wide * shared)), whole((shared, shared + padded))]
-        + [whole((shared, order))] * 2
-        + [top]
-        + [whole((shared + list_rows, loads))] * n,
+        in_specs=[HBM] * 4,
         scratch=[
             pltpu.VMEM((1, shared), jnp.int32),
             pltpu.VMEM((1, shared), jnp.int32),
@@ -368,19 +392,15 @@
     floor, basis_high, basis_low, tile_high, tile_low = call(
         prepare_kernel,
         (contact_rows, modes, coarse_inverse),
-        [whole((1, order)), whole(modes.shape), whole(coarse_inverse.shape)],
         [shape(order, loads)] + [shape(order, count, BF16)] * 2 + [shape(*coarse_inverse.shape, BF16)] * 2,
-        [whole((order, loads))] + [whole((order, count))] * 2 + [whole(coarse_inverse.shape)] * 2,
         flops=full * count,
         moved=8 * coarse_inverse.size + 4 * full,
         name="prepare",
     )
     mults, mult_s = (mult,), mult
-    unpack_spec = whole(unpack.shape)
     for outer in range(OUTER):
         start = outer == 0
-        recvs = swap_all(sends, "wide", wide, (1,))
-        recv_spec = whole(sends[0].shape)
+        recvs = swap_all(sends, "wide", wide, rows_order)
         rest_ins = (*mults, mults[-1], gap, modes)
         rest_specs = [whole(piece.shape) for piece in mults] + [
             block((shared, loads), 1 if start else 0),
@@ -399,8 +419,8 @@
         trial_n, started, *parts = call(
             functools.partial(rest_first_kernel, len(mults), not start),
             ins + rest_ins,
+            rest_outs,
             specs + rest_specs,
-            rest_outs,
             rest_out_specs,
             scratch=[pltpu.VMEM((order, 2 * loads), BF16)],
             grid=(steps,),
@@ -415,33 +435,24 @@
             pack = call(
                 functools.partial(pack_kernel, n, cap),
                 tuple(recvs),
-                [recv_spec] * n,
                 [shape(padded, shared, BF16)],
-                [whole((padded, shared))],
                 flops=full,
                 moved=4 * padded * shared,
                 name="pack",
             )[0]
-            pack_spec = whole(pack.shape)
         trial_s, own, *coarse = call(
             functools.partial(coarse_kernel, n),
             (size, *recvs, image, marks, gap, mult_s, modes, started),
-            [SMEM] + [recv_spec] * n
-            + [top, whole(marks.shape), top, top, whole((count, shared)), whole((count, loads))],
             [shape(shared, loads)] + [shape(count, loads)] * wide,
-            [top] + [whole((count, loads))] * wide,
             flops=6 * shared * loads * unpack.shape[1],
             moved=2 * shared * unpack.shape[1],
             name="coarse",
         )
-        blocks = [own] + swap_all(coarse, "wide", wide, (3, 2) if start else (2, 3))
-        part_spec = whole((count, loads))
+        blocks = [own] + swap_all(coarse, "wide", wide, coarse_order)
         own, *parts = call(
-            functools.partial(tile_kernel, n, m),
+            functools.partial(tile_kernel, coarse_order, part_order),
             (tile_high, tile_low, *blocks),
-            [whole(coarse_inverse.shape)] * 2 + [part_spec] * wide,
             [shape(count, loads)] * narrow,
-            [part_spec] * narrow,
             scratch=[
                 pltpu.VMEM((wide * count, loads), F32),
                 pltpu.VMEM((narrow * count, loads), F32),
@@ -450,22 +461,18 @@
             moved=4 * coarse_inverse.size,
             name="tile",
         )
-        parts = [own] + swap_all(parts, "narrow", narrow, (1, 2) if start else (1, 3))
+        parts = [own] + swap_all(parts, "narrow", narrow, part_order)
         mult_s, mult_n, image, *sends = call(
             functools.partial(lift_kernel, n, m, cap),
             (size, *parts, basis_high, basis_low, trial_s, trial_n, floor, top_high, top_low, pack),
-            [SMEM] + [part_spec] * narrow
-            + [whole((order, count))] * 2 + [top, whole((rest, loads)), whole((order, loads))]
-            + [whole((shared, order))] * 2 + [pack_spec],
             [shape(shared, loads), shape(rest, loads), shape(shared, loads)] + sent,
-            [top, whole((rest, loads)), top] + sent_specs,
             flops=3 * full * shared,
             moved=4 * order * shared,
             name="lift",
         )
         for inner in range(1, INNER):
             last = outer == OUTER - 1 and inner == INNER - 1
-            recvs = swap_all(sends, "wide", wide, LEADS[2 * outer + inner - 1])
+            recvs = swap_all(sends, "wide", wide, rows_order)
             ins = (size, high, low, mult_s, mult_n, mult_n, gap, floor)
             specs = [
                 SMEM,
@@ -488,8 +495,8 @@
             rest_got = call(
                 functools.partial(rest_kernel, last),
                 ins,
+                outs,
                 specs,
-                outs,
                 out_specs,
                 scratch=[pltpu.VMEM((order, 2 * loads), BF16)],
                 grid=(steps,),
@@ -498,16 +505,20 @@
                 name="rest",
             )
             ins = (size, *recvs, image, unpack, gap, mult_s, floor)
-            specs = [SMEM] + sent_specs + [top, unpack_spec, top, top, top]
             if last:
                 return tuple(
                     out[None]
                     for out in call(
                         functools.partial(last_kernel, n),
                         ins + tuple(rest_got),
-                        specs + [pl.BlockSpec(memory_space=pl.ANY)] * 2,
                         [shape(order, loads)] * 2,
-                        [top] * 2,
+                        in_specs=[SMEM] + [VMEM] * (len(ins) - 1) + [HBM] * 2,
+                        out_specs=[HBM] * 2,
+                        scratch=[
+                            pltpu.VMEM((shared, loads), F32),
+                            pltpu.VMEM((shared, loads), F32),
+                            pltpu.SemaphoreType.DMA((2,)),
+                        ],
                         alias={len(ins): 0, len(ins) + 1: 1},
                         flops=6 * shared * loads * unpack.shape[1],
                         moved=2 * shared * unpack.shape[1],
@@ -515,13 +526,10 @@
                     )
                 )
             mult_n, ahead = rest_got
-            square = whole((shared, shared))
             mult_s, image, *sends = call(
                 functools.partial(sweep_kernel, n, cap),
                 ins + (top_high, top_low, ahead, pack),
-                specs + [square, square, top, pack_spec],
                 [shape(shared, loads)] * 2 + sent,
-                [top] * 2 + sent_specs,
                 flops=12 * shared * loads * unpack.shape[1],
                 moved=4 * shared * unpack.shape[1],
                 name="sweep",

time: 100 us -> 92.3 us (0.923)
  waiting for transfers between devices: 30.4 us -> 24.2 us
  local copies, waits for them, and re-layouts: 5.55 us -> 2.01 us
  Pallas kernels: 22.6 us -> 23.6 us
    ppermute x30, waiting for transfers between devices: 30.4 us -> 24.2 us  [swap(): return lax.ppermute(block, axis, [(i, i ^ d) for i in range(count)])]
    unnamed x20 -> x14, local copies, waits for them, and re-layouts: 5.55 us -> 2.01 us
  transfers between devices with their start and end apart: 30 -> 30, of which waited for: 17 -> 21; matrix products, arithmetic and copies ran while one was open for 0% -> 0% of each run, Pallas kernels for 15% -> 16%
where the time goes in v5:
time: 92.3 us; the launch traced here: 92.1 us
  starting transfers between devices  40.8 us (44%)
  waiting for transfers between devices  24.2 us (26%)
  Pallas kernels  23.6 us (26%)
  local copies, waits for them, and re-layouts  2.01 us (2%)
  between operations  1.55 us (2%)
    ppermute x30, starting transfers between devices, swap(): return lax.ppermute(block, axis, [(i, i ^ d) for i in range(count)])  40.8 us
    ppermute x30, waiting for transfers between devices, swap(): return lax.ppermute(block, axis, [(i, i ^ d) for i in range(count)])  24.2 us
    pallas_call x19, Pallas kernels, call(): pl.pallas_call(body, out_shape=outs, grid=grid, in_specs=in_specs, out_sp...  23.6 us
    unnamed x14, local copies, waits for them, and re-layouts  2.01 us
  transfers between devices with their start and end apart: 30, of which 21 were waited for; matrix products, arithmetic and copies ran while one was open for 0% of the time, Pallas kernels for 16%

profile of v5, /device:TPU:0, one launch (start us, length us, event | category | flops | bytes accessed | tf_op | source)
XLA Modules:
  0.0 92.1 jit_solution(10511569291070693149)
XLA Ops:
  0.7 2.1 %first.1 = (bf16[256,1024]{1,0:T(8,128)(2,1)S(1)}, bf16[256,640]{1,0:T(8,128)(2,1)S(1)}, bf16[256,1024]{1,0:T(8,128)(2,1)S(1)}, bf16[256,1024]{1,0:T(8,128)(2,1)...) custom-call(s32[1,256]{1,0:T(1,128)} %bitcast.32, ...), custom_call_target="tpu_custom_call" | custom-call | flops 201326592 | bytes 2097152 | tf_op jit(solution)/shard_map/first/pallas_call | solution.py:49
  2.7 5.1 %collective-permute-start = (f32[264,128]{1,0:T(8,128)S(1)}, f32[264,128]{1,0:T(8,128)S(1)}, u32[]{:S(2)}, u32[]{:S(2)}) collective-permute-start(f32[264,128]{1,0:T(8,128)S(1)} %get-tuple-element.78), channel_id=1, source_target_pairs={{0,12},{4,8},{8,4},{12,0},{1,13},{5,9},{9,5},{13,1},{2,14},{6,10},... | collective-permute-start | bytes 405512 | tf_op jit(solution)/shard_map/ppermute | solution.py:322
  7.8 0.6 collective-permute-start.2
  9.2 1.0 %copy-done.2 = f32[1,1024,128]{2,1,0:T(8,128)S(1)} copy-done((f32[1,1024,128]{2,1,0:T(8,128)S(1)}, f32[1,1024,128]{2,1,0:T(8,128)}, u32[]{:S(2)}) %copy-start.2) | copy-done | bytes 524312
  10.2 0.9 %copy-done.3 = f32[1,64,1024]{2,1,0:T(8,128)S(1)} copy-done((f32[1,64,1024]{2,1,0:T(8,128)S(1)}, f32[1,64,1024]{2,1,0:T(8,128)}, u32[]{:S(2)}) %copy-start.3) | copy-done | bytes 262168
  11.2 2.5 %rest_first.2 = (f32[768,128]{1,0:T(8,128)S(1)}, f32[64,128]{1,0:T(8,128)S(1)}, bf16[768,1024]{1,0:T(8,128)(2,1)S(1)}, bf16[768,1024]{1,0:T(8,128)(2,1)S(1)}) custom-call(s32[1]{0:T(128)S(6)} %copy.15.size, f32[1024,1024]{1,0:T(8,128)S(1)} %bitcast.20, f32[1024,128]{1,0:T(8,128)S(1)} %bitcast.22, f32[1024,128]{1,0:T(8,128)S(1)} %bitcast.23, ...), custom_call_target="tpu_custom_call" | custom-call | flops 603979776 | bytes 3145728 | tf_op jit(solution)/shard_map/rest_first/pallas_call | solution.py:49
  13.7 1.7 %collective-permute-done.1.refs_1_ = f32[264,128]{1,0:T(8,128)S(1)} collective-permute-done((f32[264,128]{1,0:T(8,128)S(1)}, f32[264,128]{1,0:T(8,128)S(1)}, u32[]{:S(2)}, u32[]{:S(2)}) %collective-permute-start.1) | collective-permute-done | bytes 135200 | tf_op jit(solution)/shard_map/ppermute | solution.py:322
  15.4 3.9 %collective-permute-done.2.refs_2_ = f32[264,128]{1,0:T(8,128)S(1)} collective-permute-done((f32[264,128]{1,0:T(8,128)S(1)}, f32[264,128]{1,0:T(8,128)S(1)}, u32[]{:S(2)}, u32[]{:S(2)}) %collective-permute-start.2) | collective-permute-done | bytes 135200 | tf_op jit(solution)/shard_map/ppermute | solution.py:322
  19.3 0.5 coarse.2
  19.8 2.5 %collective-permute-start.3 = (f32[64,128]{1,0:T(8,128)S(1)}, f32[64,128]{1,0:T(8,128)S(1)}, u32[]{:S(2)}, u32[]{:S(2)}) collective-permute-start(f32[64,128]{1,0:T(8,128)S(1)} %get-tuple-element.85), channel_id=1, source_target_pairs={{0,12},{4,8},{8,4},{12,0},{1,13},{5,9},{9,5},{13,1},{2,14},{6,10},... | collective-permute-start | bytes 98312 | tf_op jit(solution)/shard_map/ppermute | solution.py:322
  22.3 1.9 %collective-permute-start.5 = (f32[64,128]{1,0:T(8,128)S(1)}, f32[64,128]{1,0:T(8,128)S(1)}, u32[]{:S(2)}, u32[]{:S(2)}) collective-permute-start(f32[64,128]{1,0:T(8,128)S(1)} %get-tuple-element.87), channel_id=1, source_target_pairs={{0,4},{4,0},{8,12},{12,8},{1,5},{5,1},{9,13},{13,9},{2,6},{6,2},{1... | collective-permute-start | bytes 98312 | tf_op jit(solution)/shard_map/ppermute | solution.py:322
  24.2 0.4 prepare.1
  24.6 0.9 %collective-permute-done.3.refs_1_ = f32[64,128]{1,0:T(8,128)S(1)} collective-permute-done((f32[64,128]{1,0:T(8,128)S(1)}, f32[64,128]{1,0:T(8,128)S(1)}, u32[]{:S(2)}, u32[]{:S(2)}) %collective-permute-start.3) | collective-permute-done | bytes 32800 | tf_op jit(solution)/shard_map/ppermute | solution.py:322
  25.6 1.6 %collective-permute-done.4.refs_2_ = f32[64,128]{1,0:T(8,128)S(1)} collective-permute-done((f32[64,128]{1,0:T(8,128)S(1)}, f32[64,128]{1,0:T(8,128)S(1)}, u32[]{:S(2)}, u32[]{:S(2)}) %collective-permute-start.4) | collective-permute-done | bytes 32800 | tf_op jit(solution)/shard_map/ppermute | solution.py:322
  27.1 0.3 tile.4
  27.5 1.6 %collective-permute-start.7 = (f32[64,128]{1,0:T(8,128)S(1)}, f32[64,128]{1,0:T(8,128)S(1)}, u32[]{:S(2)}, u32[]{:S(2)}) collective-permute-start(f32[64,128]{1,0:T(8,128)S(1)} %get-tuple-element.90), channel_id=1, source_target_pairs={{0,2},{1,3},{2,0},{3,1},{4,6},{5,7},{6,4},{7,5},{8,10},{9,11},{10,... | collective-permute-start | bytes 98312 | tf_op jit(solution)/shard_map/ppermute | solution.py:322
  29.0 0.3 collective-permute-start.8
  29.3 0.1 pack.1.refs_11_
  29.5 1.6 %collective-permute-done.6.refs_1_ = f32[64,128]{1,0:T(8,128)S(1)} collective-permute-done((f32[64,128]{1,0:T(8,128)S(1)}, f32[64,128]{1,0:T(8,128)S(1)}, u32[]{:S(2)}, u32[]{:S(2)}) %collective-permute-start.6) | collective-permute-done | bytes 32800 | tf_op jit(solution)/shard_map/ppermute | solution.py:322
  31.1 0.4 collective-permute-done.7.refs_2_
  31.5 1.0 %lift.2 = (f32[256,128]{1,0:T(8,128)S(1)}, f32[768,128]{1,0:T(8,128)S(1)}, f32[256,128]{1,0:T(8,128)S(1)}, f32[128,128]{1,0:T(8,128)S(1)}, f32[128,128]{1,0:T(8,128)S(1)}, /*index=5*/f32[128,128]{1,0:T(8,128)S(1)}) custom-call(s32[1]{0:T(128)S(6)} %copy.15.size, f32[64,128]{1,0:T(8,128)S(1)} %get-tuple-element.88.refs_0_, ...), custom_call_target="tpu_custom_call" | custom-call | flops 201326592 | bytes 1048576 | tf_op jit(solution)/shard_map/lift/pallas_call | solution.py:49
  32.5 1.1 %collective-permute-start.10 = (f32[128,128]{1,0:T(8,128)S(1)}, f32[128,128]{1,0:T(8,128)S(1)}, u32[]{:S(2)}, u32[]{:S(2)}) collective-permute-start(f32[128,128]{1,0:T(8,128)S(1)} %get-tuple-element.100), channel_id=1, source_target_pairs={{0,4},{4,0},{8,12},{12,8},{1,5},{5,1},{9,13},{13,9},{2,6},{6,2},{1... | collective-permute-start | bytes 196616 | tf_op jit(solution)/shard_map/ppermute | solution.py:322
  33.6 1.4 %collective-permute-start.11 = (f32[128,128]{1,0:T(8,128)S(1)}, f32[128,128]{1,0:T(8,128)S(1)}, u32[]{:S(2)}, u32[]{:S(2)}) collective-permute-start(f32[128,128]{1,0:T(8,128)S(1)} %get-tuple-element.101), channel_id=1, source_target_pairs={{0,8},{4,12},{8,0},{12,4},{1,9},{5,13},{9,1},{13,5},{2,10},{6,14},... | collective-permute-start | bytes 196616 | tf_op jit(solution)/shard_map/ppermute | solution.py:322
  34.9 2.0 %collective-permute-start.9 = (f32[128,128]{1,0:T(8,128)S(1)}, f32[128,128]{1,0:T(8,128)S(1)}, u32[]{:S(2)}, u32[]{:S(2)}) collective-permute-start(f32[128,128]{1,0:T(8,128)S(1)} %get-tuple-element.99), channel_id=1, source_target_pairs={{0,12},{4,8},{8,4},{12,0},{1,13},{5,9},{9,5},{13,1},{2,14},{6,10},... | collective-permute-start | bytes 196616 | tf_op jit(solution)/shard_map/ppermute | solution.py:322
  37.0 2.3 %rest.4 = (f32[768,128]{1,0:T(8,128)S(1)}, f32[256,128]{1,0:T(8,128)S(1)}) custom-call(s32[1]{0:T(128)S(6)} %copy.15.size, bf16[768,1024]{1,0:T(8,128)(2,1)S(1)} %get-tuple-element.105.high.operator, bf16[768,1024]{1,0:T(8,128)(2,1)S(1)} %get-tuple-element.106.low.refs_0_, f32[256,128]{1,0:T(8,128)S(1)} %get-tuple-element.104.mult_s.refs_6_, ...), custom_call_target="tpu_custom_call" | custom-call | flops 805306368 | bytes 4194304 | tf_op jit(solution)/shard_map/rest/pallas_call | solution.py:49
  39.3 2.6 %collective-permute-done.11.refs_2_ = f32[128,128]{1,0:T(8,128)S(1)} collective-permute-done((f32[128,128]{1,0:T(8,128)S(1)}, f32[128,128]{1,0:T(8,128)S(1)}, u32[]{:S(2)}, u32[]{:S(2)}) %collective-permute-start.11) | collective-permute-done | bytes 65568 | tf_op jit(solution)/shard_map/ppermute | solution.py:322
  41.9 0.8 sweep.3
  42.8 2.1 %collective-permute-start.12 = (f32[128,128]{1,0:T(8,128)S(1)}, f32[128,128]{1,0:T(8,128)S(1)}, u32[]{:S(2)}, u32[]{:S(2)}) collective-permute-start(f32[128,128]{1,0:T(8,128)S(1)} %get-tuple-element.109), channel_id=1, source_target_pairs={{0,12},{4,8},{8,4},{12,0},{1,13},{5,9},{9,5},{13,1},{2,14},{6,10},... | collective-permute-start | bytes 196616 | tf_op jit(solution)/shard_map/ppermute | solution.py:322
  44.9 0.7 collective-permute-start.13
  45.7 1.6 %collective-permute-start.14 = (f32[128,128]{1,0:T(8,128)S(1)}, f32[128,128]{1,0:T(8,128)S(1)}, u32[]{:S(2)}, u32[]{:S(2)}) collective-permute-start(f32[128,128]{1,0:T(8,128)S(1)} %get-tuple-element.111), channel_id=1, source_target_pairs={{0,8},{4,12},{8,0},{12,4},{1,9},{5,13},{9,1},{13,5},{2,10},{6,14},... | collective-permute-start | bytes 196616 | tf_op jit(solution)/shard_map/ppermute | solution.py:322
  47.2 2.3 %rest.5 = (f32[768,128]{1,0:T(8,128)S(1)}, f32[256,128]{1,0:T(8,128)S(1)}) custom-call(s32[1]{0:T(128)S(6)} %copy.15.size, bf16[768,1024]{1,0:T(8,128)(2,1)S(1)} %get-tuple-element.105.high.operator, bf16[768,1024]{1,0:T(8,128)(2,1)S(1)} %get-tuple-element.106.low.refs_0_, f32[256,128]{1,0:T(8,128)S(1)} %get-tuple-element.113.mult_s.refs_6_, ...), custom_call_target="tpu_custom_call" | custom-call | flops 805306368 | bytes 4194304 | tf_op jit(solution)/shard_map/rest/pallas_call | solution.py:49
  49.6 0.5 collective-permute-done.13.refs_1_
  50.1 1.6 %collective-permute-done.14.refs_2_ = f32[128,128]{1,0:T(8,128)S(1)} collective-permute-done((f32[128,128]{1,0:T(8,128)S(1)}, f32[128,128]{1,0:T(8,128)S(1)}, u32[]{:S(2)}, u32[]{:S(2)}) %collective-permute-start.14) | collective-permute-done | bytes 65568 | tf_op jit(solution)/shard_map/ppermute | solution.py:322
  51.7 0.8 sweep.4
  52.6 2.3 %collective-permute-start.15 = (f32[128,128]{1,0:T(8,128)S(1)}, f32[128,128]{1,0:T(8,128)S(1)}, u32[]{:S(2)}, u32[]{:S(2)}) collective-permute-start(f32[128,128]{1,0:T(8,128)S(1)} %get-tuple-element.116), channel_id=1, source_target_pairs={{0,12},{4,8},{8,4},{12,0},{1,13},{5,9},{9,5},{13,1},{2,14},{6,10},... | collective-permute-start | bytes 196616 | tf_op jit(solution)/shard_map/ppermute | solution.py:322
  54.9 2.1 %collective-permute-start.17 = (f32[128,128]{1,0:T(8,128)S(1)}, f32[128,128]{1,0:T(8,128)S(1)}, u32[]{:S(2)}, u32[]{:S(2)}) collective-permute-start(f32[128,128]{1,0:T(8,128)S(1)} %get-tuple-element.118), channel_id=1, source_target_pairs={{0,8},{4,12},{8,0},{12,4},{1,9},{5,13},{9,1},{13,5},{2,10},{6,14},... | collective-permute-start | bytes 196616 | tf_op jit(solution)/shard_map/ppermute | solution.py:322
  57.0 2.2 %rest_first.3 = (f32[768,128]{1,0:T(8,128)S(1)}, f32[64,128]{1,0:T(8,128)S(1)}) custom-call(s32[1]{0:T(128)S(6)} %copy.15.size, bf16[768,1024]{1,0:T(8,128)(2,1)S(1)} %get-tuple-element.105.high.operator, bf16[768,1024]{1,0:T(8,128)(2,1)S(1)} %get-tuple-element.106.low.refs_0_, f32[256,128]{1,0:T(8,128)S(1)} %get-tuple-element.120.refs_1_.refs_6_, ...), custom_call_target="tpu_custom_call" | custom-call | flops 603979776 | bytes 3145728 | tf_op jit(solution)/shard_map/rest_first/pallas_call | solution.py:49
  59.3 0.8 collective-permute-done.16.refs_1_
  60.1 0.4 collective-permute-done.17.refs_2_
  60.5 0.5 coarse.3
  61.0 1.9 %collective-permute-start.18 = (f32[64,128]{1,0:T(8,128)S(1)}, f32[64,128]{1,0:T(8,128)S(1)}, u32[]{:S(2)}, u32[]{:S(2)}) collective-permute-start(f32[64,128]{1,0:T(8,128)S(1)} %get-tuple-element.124), channel_id=1, source_target_pairs={{0,12},{4,8},{8,4},{12,0},{1,13},{5,9},{9,5},{13,1},{2,14},{6,10},... | collective-permute-start | bytes 98312 | tf_op jit(solution)/shard_map/ppermute | solution.py:322
  62.9 1.2 %collective-permute-start.19 = (f32[64,128]{1,0:T(8,128)S(1)}, f32[64,128]{1,0:T(8,128)S(1)}, u32[]{:S(2)}, u32[]{:S(2)}) collective-permute-start(f32[64,128]{1,0:T(8,128)S(1)} %get-tuple-element.125), channel_id=1, source_target_pairs={{0,8},{4,12},{8,0},{12,4},{1,9},{5,13},{9,1},{13,5},{2,10},{6,14},... | collective-permute-start | bytes 98312 | tf_op jit(solution)/shard_map/ppermute | solution.py:322
  64.1 1.4 %collective-permute-start.20 = (f32[64,128]{1,0:T(8,128)S(1)}, f32[64,128]{1,0:T(8,128)S(1)}, u32[]{:S(2)}, u32[]{:S(2)}) collective-permute-start(f32[64,128]{1,0:T(8,128)S(1)} %get-tuple-element.126), channel_id=1, source_target_pairs={{0,4},{4,0},{8,12},{12,8},{1,5},{5,1},{9,13},{13,9},{2,6},{6,2},{1... | collective-permute-start | bytes 98312 | tf_op jit(solution)/shard_map/ppermute | solution.py:322
  65.4 1.3 %collective-permute-done.18.refs_1_ = f32[64,128]{1,0:T(8,128)S(1)} collective-permute-done((f32[64,128]{1,0:T(8,128)S(1)}, f32[64,128]{1,0:T(8,128)S(1)}, u32[]{:S(2)}, u32[]{:S(2)}) %collective-permute-start.18) | collective-permute-done | bytes 32800 | tf_op jit(solution)/shard_map/ppermute | solution.py:322
  66.7 1.2 %collective-permute-done.19.refs_2_ = f32[64,128]{1,0:T(8,128)S(1)} collective-permute-done((f32[64,128]{1,0:T(8,128)S(1)}, f32[64,128]{1,0:T(8,128)S(1)}, u32[]{:S(2)}, u32[]{:S(2)}) %collective-permute-start.19) | collective-permute-done | bytes 32800 | tf_op jit(solution)/shard_map/ppermute | solution.py:322
  67.9 0.3 collective-permute-done.20.refs_3_
  68.2 0.3 tile.5
  68.6 0.1 collective-permute-start.22
  68.7 1.8 %collective-permute-start.23 = (f32[64,128]{1,0:T(8,128)S(1)}, f32[64,128]{1,0:T(8,128)S(1)}, u32[]{:S(2)}, u32[]{:S(2)}) collective-permute-start(f32[64,128]{1,0:T(8,128)S(1)} %get-tuple-element.130), channel_id=1, source_target_pairs={{0,1},{1,0},{2,3},{3,2},{4,5},{5,4},{6,7},{7,6},{8,9},{9,8},{10,11... | collective-permute-start | bytes 98312 | tf_op jit(solution)/shard_map/ppermute | solution.py:322
  70.4 1.5 %collective-permute-done.21.refs_1_ = f32[64,128]{1,0:T(8,128)S(1)} collective-permute-done((f32[64,128]{1,0:T(8,128)S(1)}, f32[64,128]{1,0:T(8,128)S(1)}, u32[]{:S(2)}, u32[]{:S(2)}) %collective-permute-start.21) | collective-permute-done | bytes 32800 | tf_op jit(solution)/shard_map/ppermute | solution.py:322
  71.9 0.7 collective-permute-done.22.refs_2_
  72.6 1.0 %lift.3 = (f32[256,128]{1,0:T(8,128)S(1)}, f32[768,128]{1,0:T(8,128)S(1)}, f32[256,128]{1,0:T(8,128)S(1)}, f32[128,128]{1,0:T(8,128)S(1)}, f32[128,128]{1,0:T(8,128)S(1)}, /*index=5*/f32[128,128]{1,0:T(8,128)S(1)}) custom-call(s32[1]{0:T(128)S(6)} %copy.15.size, f32[64,128]{1,0:T(8,128)S(1)} %get-tuple-element.127.refs_0_, ...), custom_call_target="tpu_custom_call" | custom-call | flops 201326592 | bytes 1048576 | tf_op jit(solution)/shard_map/lift/pallas_call | solution.py:49
  73.6 1.9 %collective-permute-start.24 = (f32[128,128]{1,0:T(8,128)S(1)}, f32[128,128]{1,0:T(8,128)S(1)}, u32[]{:S(2)}, u32[]{:S(2)}) collective-permute-start(f32[128,128]{1,0:T(8,128)S(1)} %get-tuple-element.133), channel_id=1, source_target_pairs={{0,12},{4,8},{8,4},{12,0},{1,13},{5,9},{9,5},{13,1},{2,14},{6,10},... | collective-permute-start | bytes 196616 | tf_op jit(solution)/shard_map/ppermute | solution.py:322
  75.4 0.3 collective-permute-start.25
  75.7 2.3 %collective-permute-start.26 = (f32[128,128]{1,0:T(8,128)S(1)}, f32[128,128]{1,0:T(8,128)S(1)}, u32[]{:S(2)}, u32[]{:S(2)}) collective-permute-start(f32[128,128]{1,0:T(8,128)S(1)} %get-tuple-element.135), channel_id=1, source_target_pairs={{0,8},{4,12},{8,0},{12,4},{1,9},{5,13},{9,1},{13,5},{2,10},{6,14},... | collective-permute-start | bytes 196616 | tf_op jit(solution)/shard_map/ppermute | solution.py:322
  78.0 2.3 %rest.6 = (f32[768,128]{1,0:T(8,128)S(1)}, f32[256,128]{1,0:T(8,128)S(1)}) custom-call(s32[1]{0:T(128)S(6)} %copy.15.size, bf16[768,1024]{1,0:T(8,128)(2,1)S(1)} %get-tuple-element.105.high.operator, bf16[768,1024]{1,0:T(8,128)(2,1)S(1)} %get-tuple-element.106.low.refs_0_, f32[256,128]{1,0:T(8,128)S(1)} %get-tuple-element.137.mult_s.refs_6_, ...), custom_call_target="tpu_custom_call" | custom-call | flops 805306368 | bytes 4194304 | tf_op jit(solution)/shard_map/rest/pallas_call | solution.py:49
  80.4 0.5 collective-permute-done.25.refs_1_
  80.9 1.8 %collective-permute-done.26.refs_2_ = f32[128,128]{1,0:T(8,128)S(1)} collective-permute-done((f32[128,128]{1,0:T(8,128)S(1)}, f32[128,128]{1,0:T(8,128)S(1)}, u32[]{:S(2)}, u32[]{:S(2)}) %collective-permute-start.26) | collective-permute-done | bytes 65568 | tf_op jit(solution)/shard_map/ppermute | solution.py:322
  82.7 0.8 sweep.5
  83.5 1.9 %collective-permute-start.27 = (f32[128,128]{1,0:T(8,128)S(1)}, f32[128,128]{1,0:T(8,128)S(1)}, u32[]{:S(2)}, u32[]{:S(2)}) collective-permute-start(f32[128,128]{1,0:T(8,128)S(1)} %get-tuple-element.140), channel_id=1, source_target_pairs={{0,12},{4,8},{8,4},{12,0},{1,13},{5,9},{9,5},{13,1},{2,14},{6,10},... | collective-permute-start | bytes 196616 | tf_op jit(solution)/shard_map/ppermute | solution.py:322
  85.5 2.5 %collective-permute-start.29 = (f32[128,128]{1,0:T(8,128)S(1)}, f32[128,128]{1,0:T(8,128)S(1)}, u32[]{:S(2)}, u32[]{:S(2)}) collective-permute-start(f32[128,128]{1,0:T(8,128)S(1)} %get-tuple-element.142), channel_id=1, source_target_pairs={{0,8},{4,12},{8,0},{12,4},{1,9},{5,13},{9,1},{13,5},{2,10},{6,14},... | collective-permute-start | bytes 196616 | tf_op jit(solution)/shard_map/ppermute | solution.py:322
  88.0 2.4 %rest.7 = (f32[1024,128]{1,0:T(8,128)}, f32[1024,128]{1,0:T(8,128)}) custom-call(s32[1]{0:T(128)S(6)} %copy.15.size, bf16[768,1024]{1,0:T(8,128)(2,1)S(1)} %get-tuple-element.105.high.operator, bf16[768,1024]{1,0:T(8,128)(2,1)S(1)} %get-tuple-element.106.low.refs_0_, f32[256,128]{1,0:T(8,128)S(1)} %get-tuple-element.144.mult_s.refs_6_, ...), custom_call_target="tpu_custom_call" | custom-call | flops 805306368 | bytes 4194304 | tf_op jit(solution)/shard_map/rest/pallas_call | solution.py:49
  90.5 0.6 collective-permute-done.29.refs_2_
  91.1 1.0 %last.1 = (f32[1024,128]{1,0:T(8,128)}, f32[1024,128]{1,0:T(8,128)}) custom-call(s32[1]{0:T(128)S(6)} %copy.15.size, f32[128,128]{1,0:T(8,128)S(1)} %collective-permute-done.27.refs_0_, f32[128,128]{1,0:T(8,128)S(1)} %collective-permute-done.28.refs_1_, ...), custom_call_target="tpu_custom_call", output_to_operand_aliasing={{0}: (9, {}), {1}: (10, {})} | custom-call | flops 125829120 | bytes 327680 | tf_op jit(solution)/shard_map/last/pallas_call | solution.py:49
  (29 shorter events, 0.3 us)
Async XLA Ops:
  0.6 8.5 %copy-start = (f32[1,1024,128]{2,1,0:T(8,128)S(1)}, f32[1,1024,128]{2,1,0:T(8,128)}, u32[]{:S(2)}) copy-start(f32[1,1024,128]{2,1,0:T(8,128)} %param.12) | copy-start | bytes 1572868
  0.6 8.5 %copy-start.1 = (f32[1,1024,1024]{2,1,0:T(8,128)S(1)}, f32[1,1024,1024]{2,1,0:T(8,128)}, u32[]{:S(2)}) copy-start(f32[1,1024,1024]{2,1,0:T(8,128)} %param.9) | copy-start | bytes 12582916
  2.7 11.0 %collective-permute-start = (f32[264,128]{1,0:T(8,128)S(1)}, f32[264,128]{1,0:T(8,128)S(1)}, u32[]{:S(2)}, u32[]{:S(2)}) collective-permute-start(f32[264,128]{1,0:T(8,128)S(1)} %get-tuple-element.78), channel_id=1, source_target_pairs={{0,12},{4,8},{8,4},{12,0},{1,13},{5,9},{9,5},{13,1},{2,14},{6,10},... | collective-permute-start | bytes 405512 | tf_op jit(solution)/shard_map/ppermute | solution.py:322
  7.8 7.6 %collective-permute-start.1 = (f32[264,128]{1,0:T(8,128)S(1)}, f32[264,128]{1,0:T(8,128)S(1)}, u32[]{:S(2)}, u32[]{:S(2)}) collective-permute-start(f32[264,128]{1,0:T(8,128)S(1)} %get-tuple-element.79), channel_id=1, source_target_pairs={{0,4},{4,0},{8,12},{12,8},{1,5},{5,1},{9,13},{13,9},{2,6},{6,2},{1... | collective-permute-start | bytes 405512 | tf_op jit(solution)/shard_map/ppermute | solution.py:322
  7.8 11.4 %collective-permute-start.2 = (f32[264,128]{1,0:T(8,128)S(1)}, f32[264,128]{1,0:T(8,128)S(1)}, u32[]{:S(2)}, u32[]{:S(2)}) collective-permute-start(f32[264,128]{1,0:T(8,128)S(1)} %get-tuple-element.80), channel_id=1, source_target_pairs={{0,8},{4,12},{8,0},{12,4},{1,9},{5,13},{9,1},{13,5},{2,10},{6,14},... | collective-permute-start | bytes 405512 | tf_op jit(solution)/shard_map/ppermute | solution.py:322
  9.2 1.0 %copy-start.2 = (f32[1,1024,128]{2,1,0:T(8,128)S(1)}, f32[1,1024,128]{2,1,0:T(8,128)}, u32[]{:S(2)}) copy-start(f32[1,1024,128]{2,1,0:T(8,128)} %param.13) | copy-start | bytes 1572868
  10.2 0.9 %copy-start.3 = (f32[1,64,1024]{2,1,0:T(8,128)S(1)}, f32[1,64,1024]{2,1,0:T(8,128)}, u32[]{:S(2)}) copy-start(f32[1,64,1024]{2,1,0:T(8,128)} %param.11) | copy-start | bytes 786436
  13.7 10.5 %copy-start.5 = (f32[256,256]{1,0:T(8,128)S(1)}, f32[256,256]{1,0:T(8,128)}, u32[]{:S(2)}) copy-start(f32[256,256]{1,0:T(8,128)} %tile.3) | copy-start | bytes 786436
  13.7 10.5 %copy-start.6 = (s32[1,1024]{1,0:T(1,128)S(1)}, s32[1,1024]{1,0:T(1,128)}, u32[]{:S(2)}) copy-start(s32[1,1024]{1,0:T(1,128)} %contact.1) | copy-start | bytes 12292
  19.8 5.8 %collective-permute-start.3 = (f32[64,128]{1,0:T(8,128)S(1)}, f32[64,128]{1,0:T(8,128)S(1)}, u32[]{:S(2)}, u32[]{:S(2)}) collective-permute-start(f32[64,128]{1,0:T(8,128)S(1)} %get-tuple-element.85), channel_id=1, source_target_pairs={{0,12},{4,8},{8,4},{12,0},{1,13},{5,9},{9,5},{13,1},{2,14},{6,10},... | collective-permute-start | bytes 98312 | tf_op jit(solution)/shard_map/ppermute | solution.py:322
  22.3 4.8 %collective-permute-start.4 = (f32[64,128]{1,0:T(8,128)S(1)}, f32[64,128]{1,0:T(8,128)S(1)}, u32[]{:S(2)}, u32[]{:S(2)}) collective-permute-start(f32[64,128]{1,0:T(8,128)S(1)} %get-tuple-element.86), channel_id=1, source_target_pairs={{0,8},{4,12},{8,0},{12,4},{1,9},{5,13},{9,1},{13,5},{2,10},{6,14},... | collective-permute-start | bytes 98312 | tf_op jit(solution)/shard_map/ppermute | solution.py:322
  22.3 4.8 %collective-permute-start.5 = (f32[64,128]{1,0:T(8,128)S(1)}, f32[64,128]{1,0:T(8,128)S(1)}, u32[]{:S(2)}, u32[]{:S(2)}) collective-permute-start(f32[64,128]{1,0:T(8,128)S(1)} %get-tuple-element.87), channel_id=1, source_target_pairs={{0,4},{4,0},{8,12},{12,8},{1,5},{5,1},{9,13},{13,9},{2,6},{6,2},{1... | collective-permute-start | bytes 98312 | tf_op jit(solution)/shard_map/ppermute | solution.py:322
  27.4 3.7 %collective-permute-start.6 = (f32[64,128]{1,0:T(8,128)S(1)}, f32[64,128]{1,0:T(8,128)S(1)}, u32[]{:S(2)}, u32[]{:S(2)}) collective-permute-start(f32[64,128]{1,0:T(8,128)S(1)} %get-tuple-element.89), channel_id=1, source_target_pairs={{0,3},{1,2},{2,1},{3,0},{4,7},{5,6},{6,5},{7,4},{8,11},{9,10},{10,... | collective-permute-start | bytes 98312 | tf_op jit(solution)/shard_map/ppermute | solution.py:322
  27.5 4.0 %collective-permute-start.7 = (f32[64,128]{1,0:T(8,128)S(1)}, f32[64,128]{1,0:T(8,128)S(1)}, u32[]{:S(2)}, u32[]{:S(2)}) collective-permute-start(f32[64,128]{1,0:T(8,128)S(1)} %get-tuple-element.90), channel_id=1, source_target_pairs={{0,2},{1,3},{2,0},{3,1},{4,6},{5,7},{6,4},{7,5},{8,10},{9,11},{10,... | collective-permute-start | bytes 98312 | tf_op jit(solution)/shard_map/ppermute | solution.py:322
  29.0 2.5 %collective-permute-start.8 = (f32[64,128]{1,0:T(8,128)S(1)}, f32[64,128]{1,0:T(8,128)S(1)}, u32[]{:S(2)}, u32[]{:S(2)}) collective-permute-start(f32[64,128]{1,0:T(8,128)S(1)} %get-tuple-element.91), channel_id=1, source_target_pairs={{0,1},{1,0},{2,3},{3,2},{4,5},{5,4},{6,7},{7,6},{8,9},{9,8},{10,11... | collective-permute-start | bytes 98312 | tf_op jit(solution)/shard_map/ppermute | solution.py:322
  32.5 6.8 %collective-permute-start.10 = (f32[128,128]{1,0:T(8,128)S(1)}, f32[128,128]{1,0:T(8,128)S(1)}, u32[]{:S(2)}, u32[]{:S(2)}) collective-permute-start(f32[128,128]{1,0:T(8,128)S(1)} %get-tuple-element.100), channel_id=1, source_target_pairs={{0,4},{4,0},{8,12},{12,8},{1,5},{5,1},{9,13},{13,9},{2,6},{6,2},{1... | collective-permute-start | bytes 196616 | tf_op jit(solution)/shard_map/ppermute | solution.py:322
  33.6 8.4 %collective-permute-start.11 = (f32[128,128]{1,0:T(8,128)S(1)}, f32[128,128]{1,0:T(8,128)S(1)}, u32[]{:S(2)}, u32[]{:S(2)}) collective-permute-start(f32[128,128]{1,0:T(8,128)S(1)} %get-tuple-element.101), channel_id=1, source_target_pairs={{0,8},{4,12},{8,0},{12,4},{1,9},{5,13},{9,1},{13,5},{2,10},{6,14},... | collective-permute-start | bytes 196616 | tf_op jit(solution)/shard_map/ppermute | solution.py:322
  34.9 7.0 %collective-permute-start.9 = (f32[128,128]{1,0:T(8,128)S(1)}, f32[128,128]{1,0:T(8,128)S(1)}, u32[]{:S(2)}, u32[]{:S(2)}) collective-permute-start(f32[128,128]{1,0:T(8,128)S(1)} %get-tuple-element.99), channel_id=1, source_target_pairs={{0,12},{4,8},{8,4},{12,0},{1,13},{5,9},{9,5},{13,1},{2,14},{6,10},... | collective-permute-start | bytes 196616 | tf_op jit(solution)/shard_map/ppermute | solution.py:322
  42.8 6.8 %collective-permute-start.12 = (f32[128,128]{1,0:T(8,128)S(1)}, f32[128,128]{1,0:T(8,128)S(1)}, u32[]{:S(2)}, u32[]{:S(2)}) collective-permute-start(f32[128,128]{1,0:T(8,128)S(1)} %get-tuple-element.109), channel_id=1, source_target_pairs={{0,12},{4,8},{8,4},{12,0},{1,13},{5,9},{9,5},{13,1},{2,14},{6,10},... | collective-permute-start | bytes 196616 | tf_op jit(solution)/shard_map/ppermute | solution.py:322
  44.9 5.2 %collective-permute-start.13 = (f32[128,128]{1,0:T(8,128)S(1)}, f32[128,128]{1,0:T(8,128)S(1)}, u32[]{:S(2)}, u32[]{:S(2)}) collective-permute-start(f32[128,128]{1,0:T(8,128)S(1)} %get-tuple-element.110), channel_id=1, source_target_pairs={{0,4},{4,0},{8,12},{12,8},{1,5},{5,1},{9,13},{13,9},{2,6},{6,2},{1... | collective-permute-start | bytes 196616 | tf_op jit(solution)/shard_map/ppermute | solution.py:322
  45.7 6.1 %collective-permute-start.14 = (f32[128,128]{1,0:T(8,128)S(1)}, f32[128,128]{1,0:T(8,128)S(1)}, u32[]{:S(2)}, u32[]{:S(2)}) collective-permute-start(f32[128,128]{1,0:T(8,128)S(1)} %get-tuple-element.111), channel_id=1, source_target_pairs={{0,8},{4,12},{8,0},{12,4},{1,9},{5,13},{9,1},{13,5},{2,10},{6,14},... | collective-permute-start | bytes 196616 | tf_op jit(solution)/shard_map/ppermute | solution.py:322
  51.7 5.3 %copy-start.4 = (f32[1,64,1024]{2,1,0:T(8,128)S(1)}, f32[1,64,1024]{2,1,0:T(8,128)}, u32[]{:S(2)}) copy-start(f32[1,64,1024]{2,1,0:T(8,128)} %param.11) | copy-start | bytes 786436
  52.6 6.7 %collective-permute-start.15 = (f32[128,128]{1,0:T(8,128)S(1)}, f32[128,128]{1,0:T(8,128)S(1)}, u32[]{:S(2)}, u32[]{:S(2)}) collective-permute-start(f32[128,128]{1,0:T(8,128)S(1)} %get-tuple-element.116), channel_id=1, source_target_pairs={{0,12},{4,8},{8,4},{12,0},{1,13},{5,9},{9,5},{13,1},{2,14},{6,10},... | collective-permute-start | bytes 196616 | tf_op jit(solution)/shard_map/ppermute | solution.py:322
  54.9 5.2 %collective-permute-start.16 = (f32[128,128]{1,0:T(8,128)S(1)}, f32[128,128]{1,0:T(8,128)S(1)}, u32[]{:S(2)}, u32[]{:S(2)}) collective-permute-start(f32[128,128]{1,0:T(8,128)S(1)} %get-tuple-element.117), channel_id=1, source_target_pairs={{0,4},{4,0},{8,12},{12,8},{1,5},{5,1},{9,13},{13,9},{2,6},{6,2},{1... | collective-permute-start | bytes 196616 | tf_op jit(solution)/shard_map/ppermute | solution.py:322
  54.9 5.6 %collective-permute-start.17 = (f32[128,128]{1,0:T(8,128)S(1)}, f32[128,128]{1,0:T(8,128)S(1)}, u32[]{:S(2)}, u32[]{:S(2)}) collective-permute-start(f32[128,128]{1,0:T(8,128)S(1)} %get-tuple-element.118), channel_id=1, source_target_pairs={{0,8},{4,12},{8,0},{12,4},{1,9},{5,13},{9,1},{13,5},{2,10},{6,14},... | collective-permute-start | bytes 196616 | tf_op jit(solution)/shard_map/ppermute | solution.py:322
  61.0 5.8 %collective-permute-start.18 = (f32[64,128]{1,0:T(8,128)S(1)}, f32[64,128]{1,0:T(8,128)S(1)}, u32[]{:S(2)}, u32[]{:S(2)}) collective-permute-start(f32[64,128]{1,0:T(8,128)S(1)} %get-tuple-element.124), channel_id=1, source_target_pairs={{0,12},{4,8},{8,4},{12,0},{1,13},{5,9},{9,5},{13,1},{2,14},{6,10},... | collective-permute-start | bytes 98312 | tf_op jit(solution)/shard_map/ppermute | solution.py:322
  62.9 5.0 %collective-permute-start.19 = (f32[64,128]{1,0:T(8,128)S(1)}, f32[64,128]{1,0:T(8,128)S(1)}, u32[]{:S(2)}, u32[]{:S(2)}) collective-permute-start(f32[64,128]{1,0:T(8,128)S(1)} %get-tuple-element.125), channel_id=1, source_target_pairs={{0,8},{4,12},{8,0},{12,4},{1,9},{5,13},{9,1},{13,5},{2,10},{6,14},... | collective-permute-start | bytes 98312 | tf_op jit(solution)/shard_map/ppermute | solution.py:322
  64.1 4.2 %collective-permute-start.20 = (f32[64,128]{1,0:T(8,128)S(1)}, f32[64,128]{1,0:T(8,128)S(1)}, u32[]{:S(2)}, u32[]{:S(2)}) collective-permute-start(f32[64,128]{1,0:T(8,128)S(1)} %get-tuple-element.126), channel_id=1, source_target_pairs={{0,4},{4,0},{8,12},{12,8},{1,5},{5,1},{9,13},{13,9},{2,6},{6,2},{1... | collective-permute-start | bytes 98312 | tf_op jit(solution)/shard_map/ppermute | solution.py:322
  68.5 3.4 %collective-permute-start.21 = (f32[64,128]{1,0:T(8,128)S(1)}, f32[64,128]{1,0:T(8,128)S(1)}, u32[]{:S(2)}, u32[]{:S(2)}) collective-permute-start(f32[64,128]{1,0:T(8,128)S(1)} %get-tuple-element.128), channel_id=1, source_target_pairs={{0,3},{1,2},{2,1},{3,0},{4,7},{5,6},{6,5},{7,4},{8,11},{9,10},{10,... | collective-permute-start | bytes 98312 | tf_op jit(solution)/shard_map/ppermute | solution.py:322
  68.6 4.0 %collective-permute-start.22 = (f32[64,128]{1,0:T(8,128)S(1)}, f32[64,128]{1,0:T(8,128)S(1)}, u32[]{:S(2)}, u32[]{:S(2)}) collective-permute-start(f32[64,128]{1,0:T(8,128)S(1)} %get-tuple-element.129), channel_id=1, source_target_pairs={{0,2},{1,3},{2,0},{3,1},{4,6},{5,7},{6,4},{7,5},{8,10},{9,11},{10,... | collective-permute-start | bytes 98312 | tf_op jit(solution)/shard_map/ppermute | solution.py:322
  68.7 3.9 %collective-permute-start.23 = (f32[64,128]{1,0:T(8,128)S(1)}, f32[64,128]{1,0:T(8,128)S(1)}, u32[]{:S(2)}, u32[]{:S(2)}) collective-permute-start(f32[64,128]{1,0:T(8,128)S(1)} %get-tuple-element.130), channel_id=1, source_target_pairs={{0,1},{1,0},{2,3},{3,2},{4,5},{5,4},{6,7},{7,6},{8,9},{9,8},{10,11... | collective-permute-start | bytes 98312 | tf_op jit(solution)/shard_map/ppermute | solution.py:322
  73.6 6.8 %collective-permute-start.24 = (f32[128,128]{1,0:T(8,128)S(1)}, f32[128,128]{1,0:T(8,128)S(1)}, u32[]{:S(2)}, u32[]{:S(2)}) collective-permute-start(f32[128,128]{1,0:T(8,128)S(1)} %get-tuple-element.133), channel_id=1, source_target_pairs={{0,12},{4,8},{8,4},{12,0},{1,13},{5,9},{9,5},{13,1},{2,14},{6,10},... | collective-permute-start | bytes 196616 | tf_op jit(solution)/shard_map/ppermute | solution.py:322
  75.4 5.4 %collective-permute-start.25 = (f32[128,128]{1,0:T(8,128)S(1)}, f32[128,128]{1,0:T(8,128)S(1)}, u32[]{:S(2)}, u32[]{:S(2)}) collective-permute-start(f32[128,128]{1,0:T(8,128)S(1)} %get-tuple-element.134), channel_id=1, source_target_pairs={{0,4},{4,0},{8,12},{12,8},{1,5},{5,1},{9,13},{13,9},{2,6},{6,2},{1... | collective-permute-start | bytes 196616 | tf_op jit(solution)/shard_map/ppermute | solution.py:322
  75.7 6.9 %collective-permute-start.26 = (f32[128,128]{1,0:T(8,128)S(1)}, f32[128,128]{1,0:T(8,128)S(1)}, u32[]{:S(2)}, u32[]{:S(2)}) collective-permute-start(f32[128,128]{1,0:T(8,128)S(1)} %get-tuple-element.135), channel_id=1, source_target_pairs={{0,8},{4,12},{8,0},{12,4},{1,9},{5,13},{9,1},{13,5},{2,10},{6,14},... | collective-permute-start | bytes 196616 | tf_op jit(solution)/shard_map/ppermute | solution.py:322
  83.5 6.9 %collective-permute-start.27 = (f32[128,128]{1,0:T(8,128)S(1)}, f32[128,128]{1,0:T(8,128)S(1)}, u32[]{:S(2)}, u32[]{:S(2)}) collective-permute-start(f32[128,128]{1,0:T(8,128)S(1)} %get-tuple-element.140), channel_id=1, source_target_pairs={{0,12},{4,8},{8,4},{12,0},{1,13},{5,9},{9,5},{13,1},{2,14},{6,10},... | collective-permute-start | bytes 196616 | tf_op jit(solution)/shard_map/ppermute | solution.py:322
  85.4 5.0 %collective-permute-start.28 = (f32[128,128]{1,0:T(8,128)S(1)}, f32[128,128]{1,0:T(8,128)S(1)}, u32[]{:S(2)}, u32[]{:S(2)}) collective-permute-start(f32[128,128]{1,0:T(8,128)S(1)} %get-tuple-element.141), channel_id=1, source_target_pairs={{0,4},{4,0},{8,12},{12,8},{1,5},{5,1},{9,13},{13,9},{2,6},{6,2},{1... | collective-permute-start | bytes 196616 | tf_op jit(solution)/shard_map/ppermute | solution.py:322
  85.5 5.7 %collective-permute-start.29 = (f32[128,128]{1,0:T(8,128)S(1)}, f32[128,128]{1,0:T(8,128)S(1)}, u32[]{:S(2)}, u32[]{:S(2)}) collective-permute-start(f32[128,128]{1,0:T(8,128)S(1)} %get-tuple-element.142), channel_id=1, source_target_pairs={{0,8},{4,12},{8,0},{12,4},{1,9},{5,13},{9,1},{13,5},{2,10},{6,14},... | collective-permute-start | bytes 196616 | tf_op jit(solution)/shard_map/ppermute | solution.py:322

commit v6 on v5

--- a/solution.py
+++ b/solution.py
@@ -79,9 +79,9 @@
     return jax.ShapeDtypeStruct((rows, columns), dtype)
 
 
-def first_kernel(order, cap, peers_at, rows_at, operator_at, mult_at, *refs):
+def first_kernel(orders, cap, peers_at, rows_at, operator_at, mult_at, *refs):
     unpack_all, unpack, high, low, image = refs[:5]
-    n = len(order)
+    n = len(orders[0])
     sends, (peers, rows, operator, mult, done) = refs[5:5 + n], refs[5 + n:]
     shared, width = image.shape
     copies = [
@@ -104,8 +104,9 @@
     wanted = jnp.broadcast_to(rows[...], (shared, shared)).T[:, :1]
     far = down[:, :1] ^ lax.axis_index("wide")
     at = jnp.zeros_like(far)
-    for k, d in enumerate(order, 1):
-        at = jnp.where(far == d, k, at)
+    odd = lax.axis_index("narrow") % 2 == 1
+    for k, (even_d, odd_d) in enumerate(zip(*orders), 1):
+        at = jnp.where(far == jnp.where(odd, odd_d, even_d), k, at)
 
     def marks(key, columns):
         hit = key == lax.broadcasted_iota(jnp.int32, (shared, columns), 1)
@@ -326,8 +327,15 @@
     return [swap(block, axis, count, d) for block, d in zip(blocks, order)]
 
 
-def middle_first(count):
-    return (count - 1, *range(1, count - 1))
+def swap_rows(blocks, wide, narrow, orders):
+    return [
+        lax.ppermute(
+            block,
+            ("wide", "narrow"),
+            [(w * narrow + i, (w ^ ds[i % 2]) * narrow + i) for w in range(wide) for i in range(narrow)],
+        )
+        for block, ds in zip(blocks, zip(*orders))
+    ]
 
 
 def far_first(count):
@@ -361,14 +369,15 @@
     listed = n * cap
     padded = -(-listed // 128) * 128
     size = interface_size
-    rows_order, coarse_order, part_order = middle_first(wide), far_first(wide), far_first(narrow)
+    coarse_order, part_order = far_first(wide), far_first(narrow)
+    rows_orders = far_first(wide), tuple(range(1, wide))
     top = whole((shared, loads))
     sent = [shape(cap, loads)] * n
     full = 2 * order * loads
 
     list_rows = -(-(-(-cap // loads)) // 8) * 8
     unpack_all, unpack, top_high, top_low, image, *sends = call(
-        functools.partial(first_kernel, rows_order, cap),
+        functools.partial(first_kernel, rows_orders, cap),
         tuple(
             pltpu.with_memory_space_constraint(value, pltpu.HBM)
             for value in (peer_list[0].reshape(1, shared), partner_row, operator, mult)
@@ -400,7 +409,7 @@
     mults, mult_s = (mult,), mult
     for outer in range(OUTER):
         start = outer == 0
-        recvs = swap_all(sends, "wide", wide, rows_order)
+        recvs = swap_rows(sends, wide, narrow, rows_orders)
         rest_ins = (*mults, mults[-1], gap, modes)
         rest_specs = [whole(piece.shape) for piece in mults] + [
             block((shared, loads), 1 if start else 0),
@@ -472,7 +481,7 @@
         )
         for inner in range(1, INNER):
             last = outer == OUTER - 1 and inner == INNER - 1
-            recvs = swap_all(sends, "wide", wide, rows_order)
+            recvs = swap_rows(sends, wide, narrow, rows_orders)
             ins = (size, high, low, mult_s, mult_n, mult_n, gap, floor)
             specs = [
                 SMEM,

time: 92.3 us -> 95.8 us (1.038)
  waiting for transfers between devices: 24.2 us -> 27.7 us
    ppermute x30 -> x12, starting transfers between devices: 40.8 us -> 12.7 us  [swap(): return lax.ppermute(block, axis, [(i, i ^ d) for i in range(count)])]
    ppermute x0 -> x18, starting transfers between devices: none -> 28 us  [swap_rows(): lax.ppermute(block, ('wide', 'narrow'), [(w * narrow + i, (w ^ ds[i % 2])...]
    ppermute x0 -> x18, waiting for transfers between devices: none -> 18.6 us  [swap_rows(): lax.ppermute(block, ('wide', 'narrow'), [(w * narrow + i, (w ^ ds[i % 2])...]
    ppermute x30 -> x12, waiting for transfers between devices: 24.2 us -> 9.11 us  [swap(): return lax.ppermute(block, axis, [(i, i ^ d) for i in range(count)])]
  transfers between devices with their start and end apart: 30 -> 30, of which waited for: 21 -> 16; matrix products, arithmetic and copies ran while one was open for 0% -> 0% of each run, Pallas kernels for 16% -> 15%
where the time goes in v6:
time: 95.8 us; the launch traced here: 95.6 us
  starting transfers between devices  40.8 us (43%)
  waiting for transfers between devices  27.7 us (29%)
  Pallas kernels  23.6 us (25%)
  local copies, waits for them, and re-layouts  2.01 us (2%)
  between operations  1.54 us (2%)
    ppermute x18, starting transfers between devices, swap_rows(): lax.ppermute(block, ('wide', 'narrow'), [(w * narrow + i, (w ^ ds[i % 2])...  28 us
    pallas_call x19, Pallas kernels, call(): pl.pallas_call(body, out_shape=outs, grid=grid, in_specs=in_specs, out_sp...  23.6 us
    ppermute x18, waiting for transfers between devices, swap_rows(): lax.ppermute(block, ('wide', 'narrow'), [(w * narrow + i, (w ^ ds[i % 2])...  18.6 us
    ppermute x12, starting transfers between devices, swap(): return lax.ppermute(block, axis, [(i, i ^ d) for i in range(count)])  12.7 us
    ppermute x12, waiting for transfers between devices, swap(): return lax.ppermute(block, axis, [(i, i ^ d) for i in range(count)])  9.11 us
    unnamed x14, local copies, waits for them, and re-layouts  2.01 us
  transfers between devices with their start and end apart: 30, of which 16 were waited for; matrix products, arithmetic and copies ran while one was open for 0% of the time, Pallas kernels for 15%

profile of v6, /device:TPU:0, one launch (start us, length us, event | category | flops | bytes accessed | tf_op | source)
XLA Modules:
  0.0 95.6 jit_solution(12522910896084448399)
XLA Ops:
  0.7 2.1 %first.1 = (bf16[256,1024]{1,0:T(8,128)(2,1)S(1)}, bf16[256,640]{1,0:T(8,128)(2,1)S(1)}, bf16[256,1024]{1,0:T(8,128)(2,1)S(1)}, bf16[256,1024]{1,0:T(8,128)(2,1)...) custom-call(s32[1,256]{1,0:T(1,128)} %bitcast.32, ...), custom_call_target="tpu_custom_call" | custom-call | flops 201326592 | bytes 2097152 | tf_op jit(solution)/shard_map/first/pallas_call | solution.py:49
  2.7 5.1 %collective-permute-start = (f32[264,128]{1,0:T(8,128)S(1)}, f32[264,128]{1,0:T(8,128)S(1)}, u32[]{:S(2)}, u32[]{:S(2)}) collective-permute-start(f32[264,128]{1,0:T(8,128)S(1)} %get-tuple-element.78), channel_id=1, source_target_pairs={{0,12},{1,5},{2,14},{3,7},{4,8},{5,1},{6,10},{7,3},{8,4},{9,13},{1... | collective-permute-start | bytes 405512 | tf_op jit(solution)/shard_map/ppermute | solution.py:332
  7.8 0.6 collective-permute-start.2
  9.2 1.0 %copy-done.2 = f32[1,1024,128]{2,1,0:T(8,128)S(1)} copy-done((f32[1,1024,128]{2,1,0:T(8,128)S(1)}, f32[1,1024,128]{2,1,0:T(8,128)}, u32[]{:S(2)}) %copy-start.2) | copy-done | bytes 524312
  10.2 0.9 copy-done.3
  11.2 2.5 %rest_first.2 = (f32[768,128]{1,0:T(8,128)S(1)}, f32[64,128]{1,0:T(8,128)S(1)}, bf16[768,1024]{1,0:T(8,128)(2,1)S(1)}, bf16[768,1024]{1,0:T(8,128)(2,1)S(1)}) custom-call(s32[1]{0:T(128)S(6)} %copy.15.size, f32[1024,1024]{1,0:T(8,128)S(1)} %bitcast.20, f32[1024,128]{1,0:T(8,128)S(1)} %bitcast.22, f32[1024,128]{1,0:T(8,128)S(1)} %bitcast.23, ...), custom_call_target="tpu_custom_call" | custom-call | flops 603979776 | bytes 3145728 | tf_op jit(solution)/shard_map/rest_first/pallas_call | solution.py:49
  13.7 6.6 %collective-permute-done.1.refs_1_ = f32[264,128]{1,0:T(8,128)S(1)} collective-permute-done((f32[264,128]{1,0:T(8,128)S(1)}, f32[264,128]{1,0:T(8,128)S(1)}, u32[]{:S(2)}, u32[]{:S(2)}) %collective-permute-start.1) | collective-permute-done | bytes 135200 | tf_op jit(solution)/shard_map/ppermute | solution.py:332
  20.4 0.5 coarse.2
  20.9 2.6 %collective-permute-start.3 = (f32[64,128]{1,0:T(8,128)S(1)}, f32[64,128]{1,0:T(8,128)S(1)}, u32[]{:S(2)}, u32[]{:S(2)}) collective-permute-start(f32[64,128]{1,0:T(8,128)S(1)} %get-tuple-element.85), channel_id=1, source_target_pairs={{0,12},{4,8},{8,4},{12,0},{1,13},{5,9},{9,5},{13,1},{2,14},{6,10},... | collective-permute-start | bytes 98312 | tf_op jit(solution)/shard_map/ppermute | solution.py:323
  23.5 1.9 %collective-permute-start.5 = (f32[64,128]{1,0:T(8,128)S(1)}, f32[64,128]{1,0:T(8,128)S(1)}, u32[]{:S(2)}, u32[]{:S(2)}) collective-permute-start(f32[64,128]{1,0:T(8,128)S(1)} %get-tuple-element.87), channel_id=1, source_target_pairs={{0,4},{4,0},{8,12},{12,8},{1,5},{5,1},{9,13},{13,9},{2,6},{6,2},{1... | collective-permute-start | bytes 98312 | tf_op jit(solution)/shard_map/ppermute | solution.py:323
  25.3 0.4 prepare.1
  25.7 1.0 %collective-permute-done.3.refs_1_ = f32[64,128]{1,0:T(8,128)S(1)} collective-permute-done((f32[64,128]{1,0:T(8,128)S(1)}, f32[64,128]{1,0:T(8,128)S(1)}, u32[]{:S(2)}, u32[]{:S(2)}) %collective-permute-start.3) | collective-permute-done | bytes 32800 | tf_op jit(solution)/shard_map/ppermute | solution.py:323
  26.7 1.6 %collective-permute-done.4.refs_2_ = f32[64,128]{1,0:T(8,128)S(1)} collective-permute-done((f32[64,128]{1,0:T(8,128)S(1)}, f32[64,128]{1,0:T(8,128)S(1)}, u32[]{:S(2)}, u32[]{:S(2)}) %collective-permute-start.4) | collective-permute-done | bytes 32800 | tf_op jit(solution)/shard_map/ppermute | solution.py:323
  28.3 0.3 tile.4
  28.5 0.1 collective-permute-start.6
  28.6 1.6 %collective-permute-start.7 = (f32[64,128]{1,0:T(8,128)S(1)}, f32[64,128]{1,0:T(8,128)S(1)}, u32[]{:S(2)}, u32[]{:S(2)}) collective-permute-start(f32[64,128]{1,0:T(8,128)S(1)} %get-tuple-element.90), channel_id=1, source_target_pairs={{0,2},{1,3},{2,0},{3,1},{4,6},{5,7},{6,4},{7,5},{8,10},{9,11},{10,... | collective-permute-start | bytes 98312 | tf_op jit(solution)/shard_map/ppermute | solution.py:323
  30.2 0.3 collective-permute-start.8
  30.5 0.1 pack.1.refs_11_
  30.6 1.6 %collective-permute-done.6.refs_1_ = f32[64,128]{1,0:T(8,128)S(1)} collective-permute-done((f32[64,128]{1,0:T(8,128)S(1)}, f32[64,128]{1,0:T(8,128)S(1)}, u32[]{:S(2)}, u32[]{:S(2)}) %collective-permute-start.6) | collective-permute-done | bytes 32800 | tf_op jit(solution)/shard_map/ppermute | solution.py:323
  32.3 0.4 collective-permute-done.7.refs_2_
  32.7 1.0 %lift.2 = (f32[256,128]{1,0:T(8,128)S(1)}, f32[768,128]{1,0:T(8,128)S(1)}, f32[256,128]{1,0:T(8,128)S(1)}, f32[128,128]{1,0:T(8,128)S(1)}, f32[128,128]{1,0:T(8,128)S(1)}, /*index=5*/f32[128,128]{1,0:T(8,128)S(1)}) custom-call(s32[1]{0:T(128)S(6)} %copy.15.size, f32[64,128]{1,0:T(8,128)S(1)} %get-tuple-element.88.refs_0_, ...), custom_call_target="tpu_custom_call" | custom-call | flops 201326592 | bytes 1048576 | tf_op jit(solution)/shard_map/lift/pallas_call | solution.py:49
  33.6 2.1 %collective-permute-start.10 = (f32[128,128]{1,0:T(8,128)S(1)}, f32[128,128]{1,0:T(8,128)S(1)}, u32[]{:S(2)}, u32[]{:S(2)}) collective-permute-start(f32[128,128]{1,0:T(8,128)S(1)} %get-tuple-element.100), channel_id=1, source_target_pairs={{0,8},{1,9},{2,10},{3,11},{4,12},{5,13},{6,14},{7,15},{8,0},{9,1},... | collective-permute-start | bytes 196616 | tf_op jit(solution)/shard_map/ppermute | solution.py:332
  35.7 0.3 collective-permute-start.11
  36.1 2.0 %collective-permute-start.9 = (f32[128,128]{1,0:T(8,128)S(1)}, f32[128,128]{1,0:T(8,128)S(1)}, u32[]{:S(2)}, u32[]{:S(2)}) collective-permute-start(f32[128,128]{1,0:T(8,128)S(1)} %get-tuple-element.99), channel_id=1, source_target_pairs={{0,12},{1,5},{2,14},{3,7},{4,8},{5,1},{6,10},{7,3},{8,4},{9,13},{1... | collective-permute-start | bytes 196616 | tf_op jit(solution)/shard_map/ppermute | solution.py:332
  38.1 2.3 %rest.4 = (f32[768,128]{1,0:T(8,128)S(1)}, f32[256,128]{1,0:T(8,128)S(1)}) custom-call(s32[1]{0:T(128)S(6)} %copy.15.size, bf16[768,1024]{1,0:T(8,128)(2,1)S(1)} %get-tuple-element.105.high.operator, bf16[768,1024]{1,0:T(8,128)(2,1)S(1)} %get-tuple-element.106.low.refs_0_, f32[256,128]{1,0:T(8,128)S(1)} %get-tuple-element.104.mult_s.refs_6_, ...), custom_call_target="tpu_custom_call" | custom-call | flops 805306368 | bytes 4194304 | tf_op jit(solution)/shard_map/rest/pallas_call | solution.py:49
  40.4 1.1 %collective-permute-done.10.refs_1_ = f32[128,128]{1,0:T(8,128)S(1)} collective-permute-done((f32[128,128]{1,0:T(8,128)S(1)}, f32[128,128]{1,0:T(8,128)S(1)}, u32[]{:S(2)}, u32[]{:S(2)}) %collective-permute-start.10) | collective-permute-done | bytes 65568 | tf_op jit(solution)/shard_map/ppermute | solution.py:332
  41.5 1.4 %collective-permute-done.11.refs_2_ = f32[128,128]{1,0:T(8,128)S(1)} collective-permute-done((f32[128,128]{1,0:T(8,128)S(1)}, f32[128,128]{1,0:T(8,128)S(1)}, u32[]{:S(2)}, u32[]{:S(2)}) %collective-permute-start.11) | collective-permute-done | bytes 65568 | tf_op jit(solution)/shard_map/ppermute | solution.py:332
  42.9 0.8 sweep.3
  43.7 2.0 %collective-permute-start.12 = (f32[128,128]{1,0:T(8,128)S(1)}, f32[128,128]{1,0:T(8,128)S(1)}, u32[]{:S(2)}, u32[]{:S(2)}) collective-permute-start(f32[128,128]{1,0:T(8,128)S(1)} %get-tuple-element.109), channel_id=1, source_target_pairs={{0,12},{1,5},{2,14},{3,7},{4,8},{5,1},{6,10},{7,3},{8,4},{9,13},{1... | collective-permute-start | bytes 196616 | tf_op jit(solution)/shard_map/ppermute | solution.py:332
  45.7 0.4 collective-permute-start.13
  46.1 2.1 %collective-permute-start.14 = (f32[128,128]{1,0:T(8,128)S(1)}, f32[128,128]{1,0:T(8,128)S(1)}, u32[]{:S(2)}, u32[]{:S(2)}) collective-permute-start(f32[128,128]{1,0:T(8,128)S(1)} %get-tuple-element.111), channel_id=1, source_target_pairs={{0,4},{1,13},{2,6},{3,15},{4,0},{5,9},{6,2},{7,11},{8,12},{9,5},{1... | collective-permute-start | bytes 196616 | tf_op jit(solution)/shard_map/ppermute | solution.py:332
  48.2 2.3 %rest.5 = (f32[768,128]{1,0:T(8,128)S(1)}, f32[256,128]{1,0:T(8,128)S(1)}) custom-call(s32[1]{0:T(128)S(6)} %copy.15.size, bf16[768,1024]{1,0:T(8,128)(2,1)S(1)} %get-tuple-element.105.high.operator, bf16[768,1024]{1,0:T(8,128)(2,1)S(1)} %get-tuple-element.106.low.refs_0_, f32[256,128]{1,0:T(8,128)S(1)} %get-tuple-element.113.mult_s.refs_6_, ...), custom_call_target="tpu_custom_call" | custom-call | flops 805306368 | bytes 4194304 | tf_op jit(solution)/shard_map/rest/pallas_call | solution.py:49
  50.5 0.2 collective-permute-done.12.refs_0_
  50.7 2.4 %collective-permute-done.13.refs_1_ = f32[128,128]{1,0:T(8,128)S(1)} collective-permute-done((f32[128,128]{1,0:T(8,128)S(1)}, f32[128,128]{1,0:T(8,128)S(1)}, u32[]{:S(2)}, u32[]{:S(2)}) %collective-permute-start.13) | collective-permute-done | bytes 65568 | tf_op jit(solution)/shard_map/ppermute | solution.py:332
  53.1 0.8 sweep.4
  54.0 1.4 %collective-permute-start.15 = (f32[128,128]{1,0:T(8,128)S(1)}, f32[128,128]{1,0:T(8,128)S(1)}, u32[]{:S(2)}, u32[]{:S(2)}) collective-permute-start(f32[128,128]{1,0:T(8,128)S(1)} %get-tuple-element.116), channel_id=1, source_target_pairs={{0,12},{1,5},{2,14},{3,7},{4,8},{5,1},{6,10},{7,3},{8,4},{9,13},{1... | collective-permute-start | bytes 196616 | tf_op jit(solution)/shard_map/ppermute | solution.py:332
  55.4 3.0 %collective-permute-start.17 = (f32[128,128]{1,0:T(8,128)S(1)}, f32[128,128]{1,0:T(8,128)S(1)}, u32[]{:S(2)}, u32[]{:S(2)}) collective-permute-start(f32[128,128]{1,0:T(8,128)S(1)} %get-tuple-element.118), channel_id=1, source_target_pairs={{0,4},{1,13},{2,6},{3,15},{4,0},{5,9},{6,2},{7,11},{8,12},{9,5},{1... | collective-permute-start | bytes 196616 | tf_op jit(solution)/shard_map/ppermute | solution.py:332
  58.4 2.2 %rest_first.3 = (f32[768,128]{1,0:T(8,128)S(1)}, f32[64,128]{1,0:T(8,128)S(1)}) custom-call(s32[1]{0:T(128)S(6)} %copy.15.size, bf16[768,1024]{1,0:T(8,128)(2,1)S(1)} %get-tuple-element.105.high.operator, bf16[768,1024]{1,0:T(8,128)(2,1)S(1)} %get-tuple-element.106.low.refs_0_, f32[256,128]{1,0:T(8,128)S(1)} %get-tuple-element.120.refs_1_.refs_6_, ...), custom_call_target="tpu_custom_call" | custom-call | flops 603979776 | bytes 3145728 | tf_op jit(solution)/shard_map/rest_first/pallas_call | solution.py:49
  60.6 1.6 %collective-permute-done.16.refs_1_ = f32[128,128]{1,0:T(8,128)S(1)} collective-permute-done((f32[128,128]{1,0:T(8,128)S(1)}, f32[128,128]{1,0:T(8,128)S(1)}, u32[]{:S(2)}, u32[]{:S(2)}) %collective-permute-start.16) | collective-permute-done | bytes 65568 | tf_op jit(solution)/shard_map/ppermute | solution.py:332
  62.2 0.5 coarse.3
  62.7 1.8 %collective-permute-start.18 = (f32[64,128]{1,0:T(8,128)S(1)}, f32[64,128]{1,0:T(8,128)S(1)}, u32[]{:S(2)}, u32[]{:S(2)}) collective-permute-start(f32[64,128]{1,0:T(8,128)S(1)} %get-tuple-element.124), channel_id=1, source_target_pairs={{0,12},{4,8},{8,4},{12,0},{1,13},{5,9},{9,5},{13,1},{2,14},{6,10},... | collective-permute-start | bytes 98312 | tf_op jit(solution)/shard_map/ppermute | solution.py:323
  64.4 0.2 collective-permute-start.19
  64.7 2.5 %collective-permute-start.20 = (f32[64,128]{1,0:T(8,128)S(1)}, f32[64,128]{1,0:T(8,128)S(1)}, u32[]{:S(2)}, u32[]{:S(2)}) collective-permute-start(f32[64,128]{1,0:T(8,128)S(1)} %get-tuple-element.126), channel_id=1, source_target_pairs={{0,4},{4,0},{8,12},{12,8},{1,5},{5,1},{9,13},{13,9},{2,6},{6,2},{1... | collective-permute-start | bytes 98312 | tf_op jit(solution)/shard_map/ppermute | solution.py:323
  67.1 1.3 %collective-permute-done.18.refs_1_ = f32[64,128]{1,0:T(8,128)S(1)} collective-permute-done((f32[64,128]{1,0:T(8,128)S(1)}, f32[64,128]{1,0:T(8,128)S(1)}, u32[]{:S(2)}, u32[]{:S(2)}) %collective-permute-start.18) | collective-permute-done | bytes 32800 | tf_op jit(solution)/shard_map/ppermute | solution.py:323
  68.4 0.9 collective-permute-done.19.refs_2_
  69.3 0.0 collective-permute-done.20.refs_3_
  69.4 0.2 tile.5
  69.6 0.1 collective-permute-start.21
  69.7 1.2 %collective-permute-start.22 = (f32[64,128]{1,0:T(8,128)S(1)}, f32[64,128]{1,0:T(8,128)S(1)}, u32[]{:S(2)}, u32[]{:S(2)}) collective-permute-start(f32[64,128]{1,0:T(8,128)S(1)} %get-tuple-element.129), channel_id=1, source_target_pairs={{0,2},{1,3},{2,0},{3,1},{4,6},{5,7},{6,4},{7,5},{8,10},{9,11},{10,... | collective-permute-start | bytes 98312 | tf_op jit(solution)/shard_map/ppermute | solution.py:323
  70.9 0.6 collective-permute-start.23
  71.5 1.5 %collective-permute-done.21.refs_1_ = f32[64,128]{1,0:T(8,128)S(1)} collective-permute-done((f32[64,128]{1,0:T(8,128)S(1)}, f32[64,128]{1,0:T(8,128)S(1)}, u32[]{:S(2)}, u32[]{:S(2)}) %collective-permute-start.21) | collective-permute-done | bytes 32800 | tf_op jit(solution)/shard_map/ppermute | solution.py:323
  73.1 0.7 collective-permute-done.22.refs_2_
  73.8 1.0 %lift.3 = (f32[256,128]{1,0:T(8,128)S(1)}, f32[768,128]{1,0:T(8,128)S(1)}, f32[256,128]{1,0:T(8,128)S(1)}, f32[128,128]{1,0:T(8,128)S(1)}, f32[128,128]{1,0:T(8,128)S(1)}, /*index=5*/f32[128,128]{1,0:T(8,128)S(1)}) custom-call(s32[1]{0:T(128)S(6)} %copy.15.size, f32[64,128]{1,0:T(8,128)S(1)} %get-tuple-element.127.refs_0_, ...), custom_call_target="tpu_custom_call" | custom-call | flops 201326592 | bytes 1048576 | tf_op jit(solution)/shard_map/lift/pallas_call | solution.py:49
  74.8 2.3 %collective-permute-start.24 = (f32[128,128]{1,0:T(8,128)S(1)}, f32[128,128]{1,0:T(8,128)S(1)}, u32[]{:S(2)}, u32[]{:S(2)}) collective-permute-start(f32[128,128]{1,0:T(8,128)S(1)} %get-tuple-element.133), channel_id=1, source_target_pairs={{0,12},{1,5},{2,14},{3,7},{4,8},{5,1},{6,10},{7,3},{8,4},{9,13},{1... | collective-permute-start | bytes 196616 | tf_op jit(solution)/shard_map/ppermute | solution.py:332
  77.1 1.1 %collective-permute-start.25 = (f32[128,128]{1,0:T(8,128)S(1)}, f32[128,128]{1,0:T(8,128)S(1)}, u32[]{:S(2)}, u32[]{:S(2)}) collective-permute-start(f32[128,128]{1,0:T(8,128)S(1)} %get-tuple-element.134), channel_id=1, source_target_pairs={{0,8},{1,9},{2,10},{3,11},{4,12},{5,13},{6,14},{7,15},{8,0},{9,1},... | collective-permute-start | bytes 196616 | tf_op jit(solution)/shard_map/ppermute | solution.py:332
  78.2 1.1 %collective-permute-start.26 = (f32[128,128]{1,0:T(8,128)S(1)}, f32[128,128]{1,0:T(8,128)S(1)}, u32[]{:S(2)}, u32[]{:S(2)}) collective-permute-start(f32[128,128]{1,0:T(8,128)S(1)} %get-tuple-element.135), channel_id=1, source_target_pairs={{0,4},{1,13},{2,6},{3,15},{4,0},{5,9},{6,2},{7,11},{8,12},{9,5},{1... | collective-permute-start | bytes 196616 | tf_op jit(solution)/shard_map/ppermute | solution.py:332
  79.3 2.3 %rest.6 = (f32[768,128]{1,0:T(8,128)S(1)}, f32[256,128]{1,0:T(8,128)S(1)}) custom-call(s32[1]{0:T(128)S(6)} %copy.15.size, bf16[768,1024]{1,0:T(8,128)(2,1)S(1)} %get-tuple-element.105.high.operator, bf16[768,1024]{1,0:T(8,128)(2,1)S(1)} %get-tuple-element.106.low.refs_0_, f32[256,128]{1,0:T(8,128)S(1)} %get-tuple-element.137.mult_s.refs_6_, ...), custom_call_target="tpu_custom_call" | custom-call | flops 805306368 | bytes 4194304 | tf_op jit(solution)/shard_map/rest/pallas_call | solution.py:49
  81.6 3.5 %collective-permute-done.25.refs_1_ = f32[128,128]{1,0:T(8,128)S(1)} collective-permute-done((f32[128,128]{1,0:T(8,128)S(1)}, f32[128,128]{1,0:T(8,128)S(1)}, u32[]{:S(2)}, u32[]{:S(2)}) %collective-permute-start.25) | collective-permute-done | bytes 65568 | tf_op jit(solution)/shard_map/ppermute | solution.py:332
  85.1 0.8 sweep.5
  86.0 1.4 %collective-permute-start.27 = (f32[128,128]{1,0:T(8,128)S(1)}, f32[128,128]{1,0:T(8,128)S(1)}, u32[]{:S(2)}, u32[]{:S(2)}) collective-permute-start(f32[128,128]{1,0:T(8,128)S(1)} %get-tuple-element.140), channel_id=1, source_target_pairs={{0,12},{1,5},{2,14},{3,7},{4,8},{5,1},{6,10},{7,3},{8,4},{9,13},{1... | collective-permute-start | bytes 196616 | tf_op jit(solution)/shard_map/ppermute | solution.py:332
  87.4 3.1 %collective-permute-start.29 = (f32[128,128]{1,0:T(8,128)S(1)}, f32[128,128]{1,0:T(8,128)S(1)}, u32[]{:S(2)}, u32[]{:S(2)}) collective-permute-start(f32[128,128]{1,0:T(8,128)S(1)} %get-tuple-element.142), channel_id=1, source_target_pairs={{0,4},{1,13},{2,6},{3,15},{4,0},{5,9},{6,2},{7,11},{8,12},{9,5},{1... | collective-permute-start | bytes 196616 | tf_op jit(solution)/shard_map/ppermute | solution.py:332
  90.4 2.4 %rest.7 = (f32[1024,128]{1,0:T(8,128)}, f32[1024,128]{1,0:T(8,128)}) custom-call(s32[1]{0:T(128)S(6)} %copy.15.size, bf16[768,1024]{1,0:T(8,128)(2,1)S(1)} %get-tuple-element.105.high.operator, bf16[768,1024]{1,0:T(8,128)(2,1)S(1)} %get-tuple-element.106.low.refs_0_, f32[256,128]{1,0:T(8,128)S(1)} %get-tuple-element.144.mult_s.refs_6_, ...), custom_call_target="tpu_custom_call" | custom-call | flops 805306368 | bytes 4194304 | tf_op jit(solution)/shard_map/rest/pallas_call | solution.py:49
  92.8 1.8 %collective-permute-done.28.refs_1_ = f32[128,128]{1,0:T(8,128)S(1)} collective-permute-done((f32[128,128]{1,0:T(8,128)S(1)}, f32[128,128]{1,0:T(8,128)S(1)}, u32[]{:S(2)}, u32[]{:S(2)}) %collective-permute-start.28) | collective-permute-done | bytes 65568 | tf_op jit(solution)/shard_map/ppermute | solution.py:332
  94.6 1.0 %last.1 = (f32[1024,128]{1,0:T(8,128)}, f32[1024,128]{1,0:T(8,128)}) custom-call(s32[1]{0:T(128)S(6)} %copy.15.size, f32[128,128]{1,0:T(8,128)S(1)} %collective-permute-done.27.refs_0_, f32[128,128]{1,0:T(8,128)S(1)} %collective-permute-done.28.refs_1_, ...), custom_call_target="tpu_custom_call", output_to_operand_aliasing={{0}: (9, {}), {1}: (10, {})} | custom-call | flops 125829120 | bytes 327680 | tf_op jit(solution)/shard_map/last/pallas_call | solution.py:49
  (29 shorter events, 0.1 us)
Async XLA Ops:
  0.6 8.5 %copy-start = (f32[1,1024,128]{2,1,0:T(8,128)S(1)}, f32[1,1024,128]{2,1,0:T(8,128)}, u32[]{:S(2)}) copy-start(f32[1,1024,128]{2,1,0:T(8,128)} %param.12) | copy-start | bytes 1572868
  0.6 8.5 %copy-start.1 = (f32[1,1024,1024]{2,1,0:T(8,128)S(1)}, f32[1,1024,1024]{2,1,0:T(8,128)}, u32[]{:S(2)}) copy-start(f32[1,1024,1024]{2,1,0:T(8,128)} %param.9) | copy-start | bytes 12582916
  2.7 11.0 %collective-permute-start = (f32[264,128]{1,0:T(8,128)S(1)}, f32[264,128]{1,0:T(8,128)S(1)}, u32[]{:S(2)}, u32[]{:S(2)}) collective-permute-start(f32[264,128]{1,0:T(8,128)S(1)} %get-tuple-element.78), channel_id=1, source_target_pairs={{0,12},{1,5},{2,14},{3,7},{4,8},{5,1},{6,10},{7,3},{8,4},{9,13},{1... | collective-permute-start | bytes 405512 | tf_op jit(solution)/shard_map/ppermute | solution.py:332
  7.8 12.5 %collective-permute-start.1 = (f32[264,128]{1,0:T(8,128)S(1)}, f32[264,128]{1,0:T(8,128)S(1)}, u32[]{:S(2)}, u32[]{:S(2)}) collective-permute-start(f32[264,128]{1,0:T(8,128)S(1)} %get-tuple-element.79), channel_id=1, source_target_pairs={{0,8},{1,9},{2,10},{3,11},{4,12},{5,13},{6,14},{7,15},{8,0},{9,1},... | collective-permute-start | bytes 405512 | tf_op jit(solution)/shard_map/ppermute | solution.py:332
  7.8 12.5 %collective-permute-start.2 = (f32[264,128]{1,0:T(8,128)S(1)}, f32[264,128]{1,0:T(8,128)S(1)}, u32[]{:S(2)}, u32[]{:S(2)}) collective-permute-start(f32[264,128]{1,0:T(8,128)S(1)} %get-tuple-element.80), channel_id=1, source_target_pairs={{0,4},{1,13},{2,6},{3,15},{4,0},{5,9},{6,2},{7,11},{8,12},{9,5},{1... | collective-permute-start | bytes 405512 | tf_op jit(solution)/shard_map/ppermute | solution.py:332
  9.2 1.0 %copy-start.2 = (f32[1,1024,128]{2,1,0:T(8,128)S(1)}, f32[1,1024,128]{2,1,0:T(8,128)}, u32[]{:S(2)}) copy-start(f32[1,1024,128]{2,1,0:T(8,128)} %param.13) | copy-start | bytes 1572868
  10.2 0.9 copy-start.3
  13.7 11.6 %copy-start.5 = (f32[256,256]{1,0:T(8,128)S(1)}, f32[256,256]{1,0:T(8,128)}, u32[]{:S(2)}) copy-start(f32[256,256]{1,0:T(8,128)} %tile.3) | copy-start | bytes 786436
  13.7 11.6 %copy-start.6 = (s32[1,1024]{1,0:T(1,128)S(1)}, s32[1,1024]{1,0:T(1,128)}, u32[]{:S(2)}) copy-start(s32[1,1024]{1,0:T(1,128)} %contact.1) | copy-start | bytes 12292
  20.9 5.8 %collective-permute-start.3 = (f32[64,128]{1,0:T(8,128)S(1)}, f32[64,128]{1,0:T(8,128)S(1)}, u32[]{:S(2)}, u32[]{:S(2)}) collective-permute-start(f32[64,128]{1,0:T(8,128)S(1)} %get-tuple-element.85), channel_id=1, source_target_pairs={{0,12},{4,8},{8,4},{12,0},{1,13},{5,9},{9,5},{13,1},{2,14},{6,10},... | collective-permute-start | bytes 98312 | tf_op jit(solution)/shard_map/ppermute | solution.py:323
  23.5 4.8 %collective-permute-start.4 = (f32[64,128]{1,0:T(8,128)S(1)}, f32[64,128]{1,0:T(8,128)S(1)}, u32[]{:S(2)}, u32[]{:S(2)}) collective-permute-start(f32[64,128]{1,0:T(8,128)S(1)} %get-tuple-element.86), channel_id=1, source_target_pairs={{0,8},{4,12},{8,0},{12,4},{1,9},{5,13},{9,1},{13,5},{2,10},{6,14},... | collective-permute-start | bytes 98312 | tf_op jit(solution)/shard_map/ppermute | solution.py:323
  23.5 4.8 %collective-permute-start.5 = (f32[64,128]{1,0:T(8,128)S(1)}, f32[64,128]{1,0:T(8,128)S(1)}, u32[]{:S(2)}, u32[]{:S(2)}) collective-permute-start(f32[64,128]{1,0:T(8,128)S(1)} %get-tuple-element.87), channel_id=1, source_target_pairs={{0,4},{4,0},{8,12},{12,8},{1,5},{5,1},{9,13},{13,9},{2,6},{6,2},{1... | collective-permute-start | bytes 98312 | tf_op jit(solution)/shard_map/ppermute | solution.py:323
  28.5 3.7 %collective-permute-start.6 = (f32[64,128]{1,0:T(8,128)S(1)}, f32[64,128]{1,0:T(8,128)S(1)}, u32[]{:S(2)}, u32[]{:S(2)}) collective-permute-start(f32[64,128]{1,0:T(8,128)S(1)} %get-tuple-element.89), channel_id=1, source_target_pairs={{0,3},{1,2},{2,1},{3,0},{4,7},{5,6},{6,5},{7,4},{8,11},{9,10},{10,... | collective-permute-start | bytes 98312 | tf_op jit(solution)/shard_map/ppermute | solution.py:323
  28.6 4.0 %collective-permute-start.7 = (f32[64,128]{1,0:T(8,128)S(1)}, f32[64,128]{1,0:T(8,128)S(1)}, u32[]{:S(2)}, u32[]{:S(2)}) collective-permute-start(f32[64,128]{1,0:T(8,128)S(1)} %get-tuple-element.90), channel_id=1, source_target_pairs={{0,2},{1,3},{2,0},{3,1},{4,6},{5,7},{6,4},{7,5},{8,10},{9,11},{10,... | collective-permute-start | bytes 98312 | tf_op jit(solution)/shard_map/ppermute | solution.py:323
  30.2 2.5 %collective-permute-start.8 = (f32[64,128]{1,0:T(8,128)S(1)}, f32[64,128]{1,0:T(8,128)S(1)}, u32[]{:S(2)}, u32[]{:S(2)}) collective-permute-start(f32[64,128]{1,0:T(8,128)S(1)} %get-tuple-element.91), channel_id=1, source_target_pairs={{0,1},{1,0},{2,3},{3,2},{4,5},{5,4},{6,7},{7,6},{8,9},{9,8},{10,11... | collective-permute-start | bytes 98312 | tf_op jit(solution)/shard_map/ppermute | solution.py:323
  33.6 7.9 %collective-permute-start.10 = (f32[128,128]{1,0:T(8,128)S(1)}, f32[128,128]{1,0:T(8,128)S(1)}, u32[]{:S(2)}, u32[]{:S(2)}) collective-permute-start(f32[128,128]{1,0:T(8,128)S(1)} %get-tuple-element.100), channel_id=1, source_target_pairs={{0,8},{1,9},{2,10},{3,11},{4,12},{5,13},{6,14},{7,15},{8,0},{9,1},... | collective-permute-start | bytes 196616 | tf_op jit(solution)/shard_map/ppermute | solution.py:332
  35.7 7.2 %collective-permute-start.11 = (f32[128,128]{1,0:T(8,128)S(1)}, f32[128,128]{1,0:T(8,128)S(1)}, u32[]{:S(2)}, u32[]{:S(2)}) collective-permute-start(f32[128,128]{1,0:T(8,128)S(1)} %get-tuple-element.101), channel_id=1, source_target_pairs={{0,4},{1,13},{2,6},{3,15},{4,0},{5,9},{6,2},{7,11},{8,12},{9,5},{1... | collective-permute-start | bytes 196616 | tf_op jit(solution)/shard_map/ppermute | solution.py:332
  36.1 6.8 %collective-permute-start.9 = (f32[128,128]{1,0:T(8,128)S(1)}, f32[128,128]{1,0:T(8,128)S(1)}, u32[]{:S(2)}, u32[]{:S(2)}) collective-permute-start(f32[128,128]{1,0:T(8,128)S(1)} %get-tuple-element.99), channel_id=1, source_target_pairs={{0,12},{1,5},{2,14},{3,7},{4,8},{5,1},{6,10},{7,3},{8,4},{9,13},{1... | collective-permute-start | bytes 196616 | tf_op jit(solution)/shard_map/ppermute | solution.py:332
  43.7 7.0 %collective-permute-start.12 = (f32[128,128]{1,0:T(8,128)S(1)}, f32[128,128]{1,0:T(8,128)S(1)}, u32[]{:S(2)}, u32[]{:S(2)}) collective-permute-start(f32[128,128]{1,0:T(8,128)S(1)} %get-tuple-element.109), channel_id=1, source_target_pairs={{0,12},{1,5},{2,14},{3,7},{4,8},{5,1},{6,10},{7,3},{8,4},{9,13},{1... | collective-permute-start | bytes 196616 | tf_op jit(solution)/shard_map/ppermute | solution.py:332
  45.7 7.4 %collective-permute-start.13 = (f32[128,128]{1,0:T(8,128)S(1)}, f32[128,128]{1,0:T(8,128)S(1)}, u32[]{:S(2)}, u32[]{:S(2)}) collective-permute-start(f32[128,128]{1,0:T(8,128)S(1)} %get-tuple-element.110), channel_id=1, source_target_pairs={{0,8},{1,9},{2,10},{3,11},{4,12},{5,13},{6,14},{7,15},{8,0},{9,1},... | collective-permute-start | bytes 196616 | tf_op jit(solution)/shard_map/ppermute | solution.py:332
  46.1 7.0 %collective-permute-start.14 = (f32[128,128]{1,0:T(8,128)S(1)}, f32[128,128]{1,0:T(8,128)S(1)}, u32[]{:S(2)}, u32[]{:S(2)}) collective-permute-start(f32[128,128]{1,0:T(8,128)S(1)} %get-tuple-element.111), channel_id=1, source_target_pairs={{0,4},{1,13},{2,6},{3,15},{4,0},{5,9},{6,2},{7,11},{8,12},{9,5},{1... | collective-permute-start | bytes 196616 | tf_op jit(solution)/shard_map/ppermute | solution.py:332
  53.1 5.3 %copy-start.4 = (f32[1,64,1024]{2,1,0:T(8,128)S(1)}, f32[1,64,1024]{2,1,0:T(8,128)}, u32[]{:S(2)}) copy-start(f32[1,64,1024]{2,1,0:T(8,128)} %param.11) | copy-start | bytes 786436
  54.0 6.7 %collective-permute-start.15 = (f32[128,128]{1,0:T(8,128)S(1)}, f32[128,128]{1,0:T(8,128)S(1)}, u32[]{:S(2)}, u32[]{:S(2)}) collective-permute-start(f32[128,128]{1,0:T(8,128)S(1)} %get-tuple-element.116), channel_id=1, source_target_pairs={{0,12},{1,5},{2,14},{3,7},{4,8},{5,1},{6,10},{7,3},{8,4},{9,13},{1... | collective-permute-start | bytes 196616 | tf_op jit(solution)/shard_map/ppermute | solution.py:332
  55.4 6.8 %collective-permute-start.16 = (f32[128,128]{1,0:T(8,128)S(1)}, f32[128,128]{1,0:T(8,128)S(1)}, u32[]{:S(2)}, u32[]{:S(2)}) collective-permute-start(f32[128,128]{1,0:T(8,128)S(1)} %get-tuple-element.117), channel_id=1, source_target_pairs={{0,8},{1,9},{2,10},{3,11},{4,12},{5,13},{6,14},{7,15},{8,0},{9,1},... | collective-permute-start | bytes 196616 | tf_op jit(solution)/shard_map/ppermute | solution.py:332
  55.4 6.8 %collective-permute-start.17 = (f32[128,128]{1,0:T(8,128)S(1)}, f32[128,128]{1,0:T(8,128)S(1)}, u32[]{:S(2)}, u32[]{:S(2)}) collective-permute-start(f32[128,128]{1,0:T(8,128)S(1)} %get-tuple-element.118), channel_id=1, source_target_pairs={{0,4},{1,13},{2,6},{3,15},{4,0},{5,9},{6,2},{7,11},{8,12},{9,5},{1... | collective-permute-start | bytes 196616 | tf_op jit(solution)/shard_map/ppermute | solution.py:332
  62.7 5.8 %collective-permute-start.18 = (f32[64,128]{1,0:T(8,128)S(1)}, f32[64,128]{1,0:T(8,128)S(1)}, u32[]{:S(2)}, u32[]{:S(2)}) collective-permute-start(f32[64,128]{1,0:T(8,128)S(1)} %get-tuple-element.124), channel_id=1, source_target_pairs={{0,12},{4,8},{8,4},{12,0},{1,13},{5,9},{9,5},{13,1},{2,14},{6,10},... | collective-permute-start | bytes 98312 | tf_op jit(solution)/shard_map/ppermute | solution.py:323
  64.4 4.9 %collective-permute-start.19 = (f32[64,128]{1,0:T(8,128)S(1)}, f32[64,128]{1,0:T(8,128)S(1)}, u32[]{:S(2)}, u32[]{:S(2)}) collective-permute-start(f32[64,128]{1,0:T(8,128)S(1)} %get-tuple-element.125), channel_id=1, source_target_pairs={{0,8},{4,12},{8,0},{12,4},{1,9},{5,13},{9,1},{13,5},{2,10},{6,14},... | collective-permute-start | bytes 98312 | tf_op jit(solution)/shard_map/ppermute | solution.py:323
  64.7 4.7 %collective-permute-start.20 = (f32[64,128]{1,0:T(8,128)S(1)}, f32[64,128]{1,0:T(8,128)S(1)}, u32[]{:S(2)}, u32[]{:S(2)}) collective-permute-start(f32[64,128]{1,0:T(8,128)S(1)} %get-tuple-element.126), channel_id=1, source_target_pairs={{0,4},{4,0},{8,12},{12,8},{1,5},{5,1},{9,13},{13,9},{2,6},{6,2},{1... | collective-permute-start | bytes 98312 | tf_op jit(solution)/shard_map/ppermute | solution.py:323
  69.6 3.5 %collective-permute-start.21 = (f32[64,128]{1,0:T(8,128)S(1)}, f32[64,128]{1,0:T(8,128)S(1)}, u32[]{:S(2)}, u32[]{:S(2)}) collective-permute-start(f32[64,128]{1,0:T(8,128)S(1)} %get-tuple-element.128), channel_id=1, source_target_pairs={{0,3},{1,2},{2,1},{3,0},{4,7},{5,6},{6,5},{7,4},{8,11},{9,10},{10,... | collective-permute-start | bytes 98312 | tf_op jit(solution)/shard_map/ppermute | solution.py:323
  69.7 4.1 %collective-permute-start.22 = (f32[64,128]{1,0:T(8,128)S(1)}, f32[64,128]{1,0:T(8,128)S(1)}, u32[]{:S(2)}, u32[]{:S(2)}) collective-permute-start(f32[64,128]{1,0:T(8,128)S(1)} %get-tuple-element.129), channel_id=1, source_target_pairs={{0,2},{1,3},{2,0},{3,1},{4,6},{5,7},{6,4},{7,5},{8,10},{9,11},{10,... | collective-permute-start | bytes 98312 | tf_op jit(solution)/shard_map/ppermute | solution.py:323
  70.9 2.9 %collective-permute-start.23 = (f32[64,128]{1,0:T(8,128)S(1)}, f32[64,128]{1,0:T(8,128)S(1)}, u32[]{:S(2)}, u32[]{:S(2)}) collective-permute-start(f32[64,128]{1,0:T(8,128)S(1)} %get-tuple-element.130), channel_id=1, source_target_pairs={{0,1},{1,0},{2,3},{3,2},{4,5},{5,4},{6,7},{7,6},{8,9},{9,8},{10,11... | collective-permute-start | bytes 98312 | tf_op jit(solution)/shard_map/ppermute | solution.py:323
  74.8 6.8 %collective-permute-start.24 = (f32[128,128]{1,0:T(8,128)S(1)}, f32[128,128]{1,0:T(8,128)S(1)}, u32[]{:S(2)}, u32[]{:S(2)}) collective-permute-start(f32[128,128]{1,0:T(8,128)S(1)} %get-tuple-element.133), channel_id=1, source_target_pairs={{0,12},{1,5},{2,14},{3,7},{4,8},{5,1},{6,10},{7,3},{8,4},{9,13},{1... | collective-permute-start | bytes 196616 | tf_op jit(solution)/shard_map/ppermute | solution.py:332
  77.1 8.1 %collective-permute-start.25 = (f32[128,128]{1,0:T(8,128)S(1)}, f32[128,128]{1,0:T(8,128)S(1)}, u32[]{:S(2)}, u32[]{:S(2)}) collective-permute-start(f32[128,128]{1,0:T(8,128)S(1)} %get-tuple-element.134), channel_id=1, source_target_pairs={{0,8},{1,9},{2,10},{3,11},{4,12},{5,13},{6,14},{7,15},{8,0},{9,1},... | collective-permute-start | bytes 196616 | tf_op jit(solution)/shard_map/ppermute | solution.py:332
  78.2 7.0 %collective-permute-start.26 = (f32[128,128]{1,0:T(8,128)S(1)}, f32[128,128]{1,0:T(8,128)S(1)}, u32[]{:S(2)}, u32[]{:S(2)}) collective-permute-start(f32[128,128]{1,0:T(8,128)S(1)} %get-tuple-element.135), channel_id=1, source_target_pairs={{0,4},{1,13},{2,6},{3,15},{4,0},{5,9},{6,2},{7,11},{8,12},{9,5},{1... | collective-permute-start | bytes 196616 | tf_op jit(solution)/shard_map/ppermute | solution.py:332
  86.0 6.8 %collective-permute-start.27 = (f32[128,128]{1,0:T(8,128)S(1)}, f32[128,128]{1,0:T(8,128)S(1)}, u32[]{:S(2)}, u32[]{:S(2)}) collective-permute-start(f32[128,128]{1,0:T(8,128)S(1)} %get-tuple-element.140), channel_id=1, source_target_pairs={{0,12},{1,5},{2,14},{3,7},{4,8},{5,1},{6,10},{7,3},{8,4},{9,13},{1... | collective-permute-start | bytes 196616 | tf_op jit(solution)/shard_map/ppermute | solution.py:332
  87.4 7.2 %collective-permute-start.28 = (f32[128,128]{1,0:T(8,128)S(1)}, f32[128,128]{1,0:T(8,128)S(1)}, u32[]{:S(2)}, u32[]{:S(2)}) collective-permute-start(f32[128,128]{1,0:T(8,128)S(1)} %get-tuple-element.141), channel_id=1, source_target_pairs={{0,8},{1,9},{2,10},{3,11},{4,12},{5,13},{6,14},{7,15},{8,0},{9,1},... | collective-permute-start | bytes 196616 | tf_op jit(solution)/shard_map/ppermute | solution.py:332
  87.4 7.2 %collective-permute-start.29 = (f32[128,128]{1,0:T(8,128)S(1)}, f32[128,128]{1,0:T(8,128)S(1)}, u32[]{:S(2)}, u32[]{:S(2)}) collective-permute-start(f32[128,128]{1,0:T(8,128)S(1)} %get-tuple-element.142), channel_id=1, source_target_pairs={{0,4},{1,13},{2,6},{3,15},{4,0},{5,9},{6,2},{7,11},{8,12},{9,5},{1... | collective-permute-start | bytes 196616 | tf_op jit(solution)/shard_map/ppermute | solution.py:332

commit v7 on v5

v7 whole, which is shorter than its diff:
```python
import functools

import jax
import jax.numpy as jnp
from jax import lax
from jax.experimental import pallas as pl
from jax.experimental.pallas import tpu as pltpu
from jax.sharding import PartitionSpec as P

OUTER = 2
INNER = 3
STEP = 0.3
F32 = jnp.float32
BF16 = jnp.bfloat16
PARAMS = pltpu.CompilerParams(vmem_limit_bytes=24 * 1024 * 1024)


def split(value):
    high = value.astype(BF16)
    return high, (value - high.astype(F32)).astype(BF16)


def mm(left, right):
    return jnp.dot(left, right, preferred_element_type=F32)


def product(left, right):
    (left_high, left_low), (right_high, right_low) = left, right
    width = right_high.shape[1]
    both = mm(left_high, jnp.concatenate([right_high, right_low], axis=1))
    return both[:, :width] + (both[:, width:] + mm(left_low, right_high))


def pick(chosen, value):
    width = value.shape[1]
    both = mm(chosen, jnp.concatenate(split(value), axis=1))
    return both[:, :width] + both[:, width:]


def live(size, start, rows, width):
    return lax.broadcasted_iota(jnp.int32, (rows, width), 0) + start < size


def call(body, ins, outs, in_specs=None, out_specs=None, scratch=(), grid=(), flops=0, moved=0, alias=None, name=None):
    if in_specs is None:
        in_specs = [SMEM if value.ndim == 1 else VMEM for value in ins]
    if out_specs is None:
        out_specs = [VMEM] * len(outs)
    return pl.pallas_call(
        body,
        out_shape=outs,
        grid=grid,
        in_specs=in_specs,
        out_specs=out_specs,
        scratch_shapes=list(scratch),
        compiler_params=PARAMS,
        cost_estimate=pl.CostEstimate(flops=flops, bytes_accessed=moved, transcendentals=0),
        input_output_aliases=alias or {},
        name=name,
    )(*ins)


def whole(shape):
    return pl.BlockSpec(shape, lambda *i: (0,) * len(shape))


def block(shape, at=0, across=False):
    if across:
        return pl.BlockSpec(shape, lambda i: (0, i + at))
    return pl.BlockSpec(shape, lambda i: (i + at, 0))


SMEM = pl.BlockSpec(memory_space=pltpu.SMEM)
HBM = pl.BlockSpec(memory_space=pltpu.HBM)
VMEM = pl.BlockSpec(memory_space=pltpu.VMEM)


def shape(rows, columns, dtype=F32):
    return jax.ShapeDtypeStruct((rows, columns), dtype)


def first_kernel(n, cap, peers_at, rows_at, operator_at, mult_at, *refs):
    unpack_own, unpack_all, unpack, high, low, image = refs[:6]
    sends, (peers, rows, operator, mult, done) = refs[6:6 + n], refs[6 + n:]
    shared, width = image.shape
    copies = [
        pltpu.make_async_copy(source, target, done.at[i])
        for i, (source, target) in enumerate(
            ((peers_at, peers), (rows_at, rows), (mult_at, mult), (operator_at.at[pl.ds(0, shared)], operator))
        )
    ]
    for copy in copies:
        copy.start()
    copies[0].wait()
    copies[1].wait()
    across = jnp.broadcast_to(peers[...], (shared, shared))
    down = across.T
    first = lax.broadcasted_iota(jnp.int32, (shared, shared), 0)
    second = lax.broadcasted_iota(jnp.int32, (shared, shared), 1)
    slot = jnp.sum(
        jnp.where((across == down) & (second < first), 1.0, 0.0), axis=1, keepdims=True
    ).astype(jnp.int32)
    wanted = jnp.broadcast_to(rows[...], (shared, shared)).T[:, :1]
    far = down[:, :1] ^ lax.axis_index("wide")

    def marks(key, columns):
        hit = key == lax.broadcasted_iota(jnp.int32, (shared, columns), 1)
        return jnp.where(hit, 1.0, 0.0).astype(BF16)

    unpack_own[...] = marks(jnp.where(far == 0, wanted, -1), shared)
    unpack_all[...] = marks(jnp.where(far == 0, -1, (far - 1) * shared + wanted), unpack_all.shape[1])
    unpack[...] = marks(jnp.where(far == 0, -1, (far - 1) * cap + slot), unpack.shape[1])
    lane = lax.broadcasted_iota(jnp.int32, (shared, width), 1)
    for d, out in enumerate(sends, 1):
        out[shared:, :] = jnp.zeros((out.shape[0] - shared, width), F32)
        for c in range(-(-cap // width)):
            hit = (far == d) & (slot == lane + c * width)
            out[shared + c:shared + c + 1, :] = jnp.sum(
                jnp.where(hit, wanted.astype(F32), 0.0), axis=0, keepdims=True
            )
    copies[2].wait()
    copies[3].wait()
    parts = split(operator[...])
    high[...], low[...] = parts
    value = product(parts, split(mult[...]))
    image[...] = value
    for out in sends:
        out[:shared, :] = value


def pack_kernel(times, cap, *refs):
    n = len(times)
    recvs, (high, low, pack, stack_high, stack_low) = refs[:n], refs[n:]
    shared = pack.shape[1]
    width = recvs[0].shape[1]
    column = lax.broadcasted_iota(jnp.int32, (width, shared), 1).astype(F32)
    if n * cap < pack.shape[0]:
        pack[n * cap:, :] = jnp.zeros((pack.shape[0] - n * cap, shared), BF16)
    for d, recv in zip(times, recvs):
        for c in range(-(-cap // width)):
            wanted = jnp.broadcast_to(recv[shared + c:shared + c + 1, :], (shared, width)).T
            chosen = jnp.where(wanted == column, 1.0, 0.0).astype(BF16)
            size = min(width, cap - c * width)
            at = (d - 1) * cap + c * width
            pack[at:at + size, :] = chosen[:size]
    for source, stack in ((high, stack_high), (low, stack_low)):
        square = source[:, :shared]
        stack[:shared, :] = square
        stack[shared:, :] = mm(pack[...], square).astype(BF16)


def prepare_kernel(contact, modes, tile, floor, basis, tile_high, tile_low):
    order, width = floor.shape
    for at in range(0, order, width):
        flag = jnp.broadcast_to(contact[:, at:at + width], (width, width)).T
        floor[at:at + width, :] = jnp.where(flag == 1, 0.0, -jnp.inf)
    high, low = [part.astype(F32) for part in split(modes[...])]
    basis[...] = jnp.concatenate([high, high, low], axis=0).T.astype(BF16)
    tile_high[...], tile_low[...] = split(tile[...])


def send(cap, chosen, image, sends):
    picked = pick(chosen, image)
    for d, out in enumerate(sends):
        out[...] = picked[d * cap:(d + 1) * cap]


def arrived(times, recvs, shared, unpack):
    blocks = [recvs[times.index(d)][...][:shared] for d in sorted(times)]
    rows = sum(b.shape[0] for b in blocks)
    if rows < unpack.shape[1]:
        blocks.append(jnp.zeros((unpack.shape[1] - rows, blocks[0].shape[1]), F32))
    return pick(unpack[...], jnp.concatenate(blocks, axis=0))


def base_kernel(image, unpack_own, gap, base):
    own = image[...]
    base[...] = gap[:own.shape[0], :] - own + pick(unpack_own[...], own)


def settle(trial, floor, alive):
    return jnp.where(alive, jnp.maximum(trial, floor), 0.0)


def shared_residual(times, recvs, base, unpack, size):
    known = base[...]
    alive = live(size[0], 0, *known.shape)
    return jnp.where(alive, known + arrived(times, recvs, known.shape[0], unpack), 0.0), alive


def rest_start_kernel(size, operator, mult, mult_block, gap, modes, trial, coarse, high, low, halves):
    step = pl.program_id(0)
    rows, width = gap.shape

    @pl.when(step == 0)
    def _():
        halves[:, :width], halves[:, width:] = split(mult[...])
        coarse[...] = jnp.zeros_like(coarse)

    parts = split(operator[...])
    high[...], low[...] = parts
    both = mm(parts[0], halves[...])
    image = both[:, :width] + (both[:, width:] + mm(parts[1], halves[:, :width]))
    alive = live(size[0], (step + 1) * rows, rows, width)
    residual = jnp.where(alive, gap[...] - image, 0.0)
    trial[...] = mult_block[...] + STEP * residual
    coarse[...] += product(split(modes[...]), split(residual))


def rest_residual(size, high, low, mult_s, mult_n, gap):
    shared, (rows, width) = mult_s.shape[0], mult_n.shape
    mult = jnp.concatenate([mult_s[...], mult_n[...]], axis=0)
    image = product((high[...], low[...]), split(mult))
    alive = live(size[0], shared, rows, width)
    return jnp.where(alive, gap[shared:, :] - image, 0.0), alive


def rest_first_kernel(size, high, low, mult_s, mult_n, gap, modes, trial, coarse):
    residual, _ = rest_residual(size, high, low, mult_s, mult_n, gap)
    trial[...] = mult_n[...] + STEP * residual
    coarse[...] = product(split(modes[:, mult_s.shape[0]:]), split(residual))


def rest_kernel(size, high, low, mult_s, mult_n, gap, floor, top_high, top_low, pack, mult_out, ahead):
    shared = mult_s.shape[0]
    residual, alive = rest_residual(size, high, low, mult_s, mult_n, gap)
    mult = settle(mult_n[...] + STEP * residual, floor[shared:, :], alive)
    mult_out[...] = mult
    value = product((top_high[:, shared:], top_low[:, shared:]), split(mult))
    ahead[:shared, :] = value
    ahead[shared:, :] = pick(pack[...], value)


def rest_last_kernel(size, high, low, mult_s, mult_n, gap, floor, mult_out, residual_out, settled, left, done):
    shared, rows = mult_s.shape[0], mult_n.shape[0]
    residual, alive = rest_residual(size, high, low, mult_s, mult_n, gap)
    left[...] = residual
    settled[...] = settle(mult_n[...] + STEP * residual, floor[shared:, :], alive)
    copies = [
        pltpu.make_async_copy(source, target.at[pl.ds(shared, rows)], done.at[i])
        for i, (source, target) in enumerate(((left, residual_out), (settled, mult_out)))
    ]
    for copy in copies:
        copy.start()
    for copy in copies:
        copy.wait()


def coarse_kernel(times, size, *refs):
    n = len(times)
    recvs = refs[:n]
    base, unpack, mult, modes, started, trial = refs[n:n + 6]
    shared = base.shape[0]
    residual, _ = shared_residual(times, recvs, base, unpack, size)
    coarse = started[...] + product(split(modes[:, :shared]), split(residual))
    for out in refs[n + 6:]:
        out[...] = coarse
    trial[...] = mult[:shared, :] + STEP * residual


def tile_kernel(wide_order, narrow_order, high, low, *refs):
    n, m = len(wide_order), len(narrow_order)
    blocks, outs, (gathered, parts) = refs[:n + 1], refs[n + 1:n + m + 2], refs[n + m + 2:]
    count = blocks[0].shape[0]
    for d, ref in zip((0, *wide_order), blocks):
        at = pl.multiple_of((lax.axis_index("wide") ^ d) * count, count)
        gathered[pl.ds(at, count), :] = ref[...]
    parts[...] = product((high[...], low[...]), split(gathered[...]))
    for d, out in zip((0, *narrow_order), outs):
        at = pl.multiple_of((lax.axis_index("narrow") ^ d) * count, count)
        out[...] = parts[pl.ds(at, count), :]


def lift_kernel(n, m, cap, size, *refs):
    parts = refs[:m + 1]
    ins, (mult_s, mult_n, image), sends = refs[m + 1:m + 8], refs[m + 8:m + 11], refs[m + 11:]
    basis, trial_s, trial_n, floor, high, low, pack = ins
    solved = parts[0][...]
    for part in parts[1:]:
        solved = solved + part[...]
    shared, width = trial_s.shape
    order = floor.shape[0]
    high_part, low_part = split(solved)
    lifted = mm(basis[...], jnp.concatenate([high_part, low_part, high_part], axis=0))
    alive = live(size[0], 0, order, width)
    first = settle(trial_s[...] + lifted[:shared], floor[:shared], alive[:shared])
    rest = settle(trial_n[...] + lifted[shared:], floor[shared:], alive[shared:])
    mult_s[...] = first
    mult_n[...] = rest
    value = product((high[...], low[...]), split(jnp.concatenate([first, rest], axis=0)))
    image[...] = value
    send(cap, pack[...], value, sends)


def sweep_kernel(times, cap, size, *refs):
    n = len(times)
    recvs = refs[:n]
    base, unpack, mult, floor, high, low, ahead, mult_out, image_out = refs[n:n + 9]
    shared = base.shape[0]
    residual, alive = shared_residual(times, recvs, base, unpack, size)
    value = settle(mult[...] + STEP * residual, floor[:shared, :], alive)
    mult_out[...] = value
    both = ahead[...] + product((high[...], low[...]), split(value))
    image_out[...] = both[:shared]
    for d, out in enumerate(refs[n + 9:]):
        out[...] = both[shared + d * cap:shared + (d + 1) * cap]


def last_kernel(times, size, *refs):
    n = len(times)
    recvs = refs[:n]
    base, unpack, mult, floor, _, _, mult_out, residual_out, settled, left, done = refs[n:]
    shared = base.shape[0]
    residual, alive = shared_residual(times, recvs, base, unpack, size)
    left[...] = residual
    first = pltpu.make_async_copy(left, residual_out.at[pl.ds(0, shared)], done.at[0])
    first.start()
    settled[...] = settle(mult[...] + STEP * residual, floor[:shared, :], alive)
    second = pltpu.make_async_copy(settled, mult_out.at[pl.ds(0, shared)], done.at[1])
    second.start()
    first.wait()
    second.wait()


def swap(block, axis, count, d):
    return lax.ppermute(block, axis, [(i, i ^ d) for i in range(count)])


def swap_all(blocks, axis, count, order):
    return [swap(block, axis, count, d) for block, d in zip(blocks, order)]


def swap_rows(blocks, axis, count, times):
    return [swap(blocks[d - 1], axis, count, d) for d in times]


def half_first(count, back):
    half = count // 2
    others = [d for d in range(1, count) if d != half]
    return (half, *(others[::-1] if back else others))


def middle_first(count):
    return (count - 1, *range(1, count - 1))


def far_first(count):
    return tuple(range(count - 1, 0, -1))


def local(
    wide,
    narrow,
    operators,
    coarse_inverse,
    modes,
    gap,
    start_mult,
    peer_list,
    partner_row,
    interface_size,
    contact_rows,
):
    operator = operators[0]
    modes = modes[0]
    gap = gap[0]
    mult = start_mult[0]
    order, loads = mult.shape
    shared = partner_row.shape[1]
    count = modes.shape[0]
    rest = order - shared
    steps = rest // shared
    n, m = wide - 1, narrow - 1
    cap = 2 * shared // wide
    listed = n * cap
    padded = -(-listed // 128) * 128
    size = interface_size
    coarse_order, part_order = far_first(wide), far_first(narrow)
    half, half_back, middle = half_first(wide, False), half_first(wide, True), middle_first(wide)
    orders = ((half_back, half, middle), (half_back, half, half_back))
    sent = [shape(cap, loads)] * n
    full = 2 * order * loads

    list_rows = -(-(-(-cap // loads)) // 8) * 8
    unpack_own, unpack_all, unpack, top_high, top_low, image, *sends = call(
        functools.partial(first_kernel, n, cap),
        tuple(
            pltpu.with_memory_space_constraint(value, pltpu.HBM)
            for value in (peer_list[0].reshape(1, shared), partner_row, operator, mult)
        ),
        [shape(shared, shared, BF16), shape(shared, n * shared, BF16), shape(shared, padded, BF16)]
        + [shape(shared, order, BF16)] * 2
        + [shape(shared, loads)]
        + [shape(shared + list_rows, loads)] * n,
        in_specs=[HBM] * 4,
        scratch=[
            pltpu.VMEM((1, shared), jnp.int32),
            pltpu.VMEM((1, shared), jnp.int32),
            pltpu.VMEM((shared, order), F32),
            pltpu.VMEM((order, loads), F32),
            pltpu.SemaphoreType.DMA((4,)),
        ],
        flops=3 * full * shared,
        moved=8 * shared * order,
        name="first",
    )
    floor, basis, tile_high, tile_low = call(
        prepare_kernel,
        (contact_rows, modes, coarse_inverse),
        [shape(order, loads)] + [shape(order, 3 * count, BF16)] + [shape(*coarse_inverse.shape, BF16)] * 2,
        flops=full * count,
        moved=8 * coarse_inverse.size + 4 * full,
        name="prepare",
    )
    mult_s = mult
    scratch = [pltpu.VMEM((order, 2 * loads), BF16)]
    for outer in range(OUTER):
        times = orders[outer][0]
        recvs = swap_rows(sends, "wide", wide, times)
        base = call(
            base_kernel,
            (image, unpack_own, gap),
            [shape(shared, loads)],
            flops=4 * shared * shared * loads,
            moved=8 * shared * loads,
            name="base",
        )[0]
        if outer == 0:
            row_block, load_block = block((shared, order)), block((shared, loads))
            next_loads = block((shared, loads), 1)
            trial_n, started, high, low = call(
                rest_start_kernel,
                (size, operator, mult, mult, gap, modes),
                [shape(rest, loads), shape(count, loads)] + [shape(rest, order, BF16)] * 2,
                [
                    SMEM,
                    block((shared, order), 1),
                    whole((order, loads)),
                    next_loads,
                    next_loads,
                    block((count, shared), 1, across=True),
                ],
                [load_block, whole((count, loads)), row_block, row_block],
                scratch=scratch,
                grid=(steps,),
                flops=3 * full * rest,
                moved=8 * rest * order,
                name="rest_start",
            )
            marks = unpack_all
            pack, stack_high, stack_low = call(
                functools.partial(pack_kernel, times, cap),
                (*recvs, top_high, top_low),
                [shape(padded, shared, BF16)] + [shape(shared + padded, shared, BF16)] * 2,
                flops=8 * padded * shared * shared,
                moved=8 * padded * shared,
                name="pack",
            )
        else:
            trial_n, started = call(
                rest_first_kernel,
                (size, high, low, mult_s, mult_n, gap, modes),
                [shape(rest, loads), shape(count, loads)],
                flops=3 * full * rest,
                moved=4 * rest * order,
                name="rest_first",
            )
            marks = unpack
        trial_s, own, *coarse = call(
            functools.partial(coarse_kernel, times),
            (size, *recvs, base, marks, mult_s, modes, started),
            [shape(shared, loads)] + [shape(count, loads)] * wide,
            flops=6 * shared * loads * unpack.shape[1],
            moved=2 * shared * unpack.shape[1],
            name="coarse",
        )
        blocks = [own] + swap_all(coarse, "wide", wide, coarse_order)
        own, *parts = call(
            functools.partial(tile_kernel, coarse_order, part_order),
            (tile_high, tile_low, *blocks),
            [shape(count, loads)] * narrow,
            scratch=[
                pltpu.VMEM((wide * count, loads), F32),
                pltpu.VMEM((narrow * count, loads), F32),
            ],
            flops=6 * coarse_inverse.size * loads,
            moved=4 * coarse_inverse.size,
            name="tile",
        )
        parts = [own] + swap_all(parts, "narrow", narrow, part_order)
        mult_s, mult_n, image, *sends = call(
            functools.partial(lift_kernel, n, m, cap),
            (size, *parts, basis, trial_s, trial_n, floor, top_high, top_low, pack),
            [shape(shared, loads), shape(rest, loads), shape(shared, loads)] + sent,
            flops=3 * full * shared,
            moved=4 * order * shared,
            name="lift",
        )
        for inner in range(1, INNER):
            last = outer == OUTER - 1 and inner == INNER - 1
            times = orders[outer][inner]
            recvs = swap_rows(sends, "wide", wide, times)
            base = call(
                base_kernel,
                (image, unpack_own, gap),
                [shape(shared, loads)],
                flops=4 * shared * shared * loads,
                moved=8 * shared * loads,
                name="base",
            )[0]
            ins = (size, high, low, mult_s, mult_n, gap, floor)
            shadow = (size, *recvs, base, unpack, mult_s, floor)
            cost = dict(flops=6 * shared * loads * unpack.shape[1], moved=2 * shared * unpack.shape[1])
            if last:
                outs = call(
                    rest_last_kernel,
                    ins,
                    [shape(order, loads)] * 2,
                    out_specs=[HBM] * 2,
                    scratch=[pltpu.VMEM((rest, loads), F32)] * 2 + [pltpu.SemaphoreType.DMA((2,))],
                    flops=3 * full * rest,
                    moved=4 * rest * order,
                    name="rest_last",
                )
                outs = call(
                    functools.partial(last_kernel, times),
                    (*shadow, *outs),
                    [shape(order, loads)] * 2,
                    in_specs=[SMEM] + [VMEM] * (len(shadow) - 1) + [HBM] * 2,
                    out_specs=[HBM] * 2,
                    scratch=[pltpu.VMEM((shared, loads), F32)] * 2 + [pltpu.SemaphoreType.DMA((2,))],
                    alias={len(shadow): 0, len(shadow) + 1: 1},
                    name="last",
                    **cost,
                )
                return tuple(out[None] for out in outs)
            mult_n, ahead = call(
                rest_kernel,
                (*ins, top_high, top_low, pack),
                [shape(rest, loads), shape(shared + padded, loads)],
                flops=3 * full * order,
                moved=4 * order * order,
                name="rest",
            )
            mult_s, image, *sends = call(
                functools.partial(sweep_kernel, times, cap),
                (*shadow, stack_high, stack_low, ahead),
                [shape(shared, loads)] * 2 + sent,
                name="sweep",
                **cost,
            )


def solution(mesh):
    wide = mesh.shape["wide"]
    narrow = mesh.shape["narrow"]

    def body(*args):
        return local(wide, narrow, *args)

    return jax.shard_map(
        body,
        mesh=mesh,
        in_specs=(
            P(("groups", "wide", "narrow"), None, None),
            P(("groups", "wide"), "narrow"),
            P(("groups", "wide", "narrow"), None, None),
            P(("groups", "wide", "narrow"), None, None),
            P(("groups", "wide", "narrow"), None, None),
            P(("groups", "wide", "narrow"), None, None),
            P(("groups", "wide", "narrow"), None),
            P(("groups", "wide", "narrow")),
            P(("groups", "wide", "narrow"), None),
        ),
        out_specs=(
            P(("groups", "wide", "narrow"), None, None),
            P(("groups", "wide", "narrow"), None, None),
        ),
        check_vma=False,
    )
```

time: 92.3 us -> 90.5 us (0.980)
  waiting for transfers between devices: 24.2 us -> 30.2 us
  Pallas kernels: 23.6 us -> 19.3 us
  local copies, waits for them, and re-layouts: 2.01 us -> 0.03 us
  starting transfers between devices: 40.8 us -> 39.3 us
    ppermute x30, waiting for transfers between devices: 24.2 us -> 30.2 us  [swap(): return lax.ppermute(block, axis, [(i, i ^ d) for i in range(count)])]
    pallas_call x19 -> x25, Pallas kernels: 23.6 us -> 19.3 us  [call(): pl.pallas_call(body, out_shape=outs, grid=grid, in_specs=in_specs, out_sp...]
    unnamed x14 -> x12, local copies, waits for them, and re-layouts: 2.01 us -> 0.03 us
    ppermute x30, starting transfers between devices: 40.8 us -> 39.3 us  [swap(): return lax.ppermute(block, axis, [(i, i ^ d) for i in range(count)])]
  transfers between devices with their start and end apart: 30 -> 30, of which waited for: 21 -> 24; matrix products, arithmetic and copies ran while one was open for 0% -> 0% of each run, Pallas kernels for 16% -> 13%
where the time goes in v7:
time: 90.5 us; the launch traced here: 90.4 us
  starting transfers between devices  39.3 us (43%)
  waiting for transfers between devices  30.2 us (33%)
  Pallas kernels  19.3 us (21%)
  between operations  1.58 us (2%)
    ppermute x30, starting transfers between devices, swap(): return lax.ppermute(block, axis, [(i, i ^ d) for i in range(count)])  39.3 us
    ppermute x30, waiting for transfers between devices, swap(): return lax.ppermute(block, axis, [(i, i ^ d) for i in range(count)])  30.2 us
    pallas_call x25, Pallas kernels, call(): pl.pallas_call(body, out_shape=outs, grid=grid, in_specs=in_specs, out_sp...  19.3 us
  transfers between devices with their start and end apart: 30, of which 24 were waited for; matrix products, arithmetic and copies ran while one was open for 0% of the time, Pallas kernels for 13%

profile of v7, /device:TPU:0, one launch (start us, length us, event | category | flops | bytes accessed | tf_op | source)
XLA Modules:
  0.0 90.4 jit_solution(14118009379143995508)
XLA Ops:
  0.7 2.1 %first.1 = (bf16[256,256]{1,0:T(8,128)(2,1)S(1)}, bf16[256,768]{1,0:T(8,128)(2,1)S(1)}, bf16[256,384]{1,0:T(8,128)(2,1)S(1)}, bf16[256,1024]{1,0:T(8,128)(2,1)S(...) custom-call(s32[1,256]{1,0:T(1,128)} %bitcast.32, ...), custom_call_target="tpu_custom_call" | custom-call | flops 201326592 | bytes 2097152 | tf_op jit(solution)/shard_map/first/pallas_call | solution.py:49
  2.8 4.1 %collective-permute-start = (f32[264,128]{1,0:T(8,128)S(1)}, f32[264,128]{1,0:T(8,128)S(1)}, u32[]{:S(2)}, u32[]{:S(2)}) collective-permute-start(f32[264,128]{1,0:T(8,128)S(1)} %get-tuple-element.81), channel_id=1, source_target_pairs={{0,8},{4,12},{8,0},{12,4},{1,9},{5,13},{9,1},{13,5},{2,10},{6,14},... | collective-permute-start | bytes 405512 | tf_op jit(solution)/shard_map/ppermute | solution.py:326
  6.9 1.3 %collective-permute-start.1 = (f32[264,128]{1,0:T(8,128)S(1)}, f32[264,128]{1,0:T(8,128)S(1)}, u32[]{:S(2)}, u32[]{:S(2)}) collective-permute-start(f32[264,128]{1,0:T(8,128)S(1)} %get-tuple-element.82), channel_id=1, source_target_pairs={{0,12},{4,8},{8,4},{12,0},{1,13},{5,9},{9,5},{13,1},{2,14},{6,10},... | collective-permute-start | bytes 405512 | tf_op jit(solution)/shard_map/ppermute | solution.py:326
  9.3 2.0 %rest_start.1 = (f32[768,128]{1,0:T(8,128)S(1)}, f32[64,128]{1,0:T(8,128)S(1)}, bf16[768,1024]{1,0:T(8,128)(2,1)S(1)}, bf16[768,1024]{1,0:T(8,128)(2,1)S(1)}) custom-call(s32[1]{0:T(128)S(6)} %copy.15.size, f32[1024,1024]{1,0:T(8,128)S(1)} %bitcast.20, f32[1024,128]{1,0:T(8,128)S(1)} %bitcast.22, f32[1024,128]{1,0:T(8,128)S(1)} %bitcast.23, ...), custom_call_target="tpu_custom_call" | custom-call | flops 603979776 | bytes 6291456 | tf_op jit(solution)/shard_map/rest_start/pallas_call | solution.py:49
  11.4 5.7 %collective-permute-done.refs_0_ = f32[264,128]{1,0:T(8,128)S(1)} collective-permute-done((f32[264,128]{1,0:T(8,128)S(1)}, f32[264,128]{1,0:T(8,128)S(1)}, u32[]{:S(2)}, u32[]{:S(2)}) %collective-permute-start) | collective-permute-done | bytes 135200 | tf_op jit(solution)/shard_map/ppermute | solution.py:326
  17.1 0.5 collective-permute-done.2.refs_2_
  17.6 0.5 coarse.2
  18.1 3.6 %collective-permute-start.3 = (f32[64,128]{1,0:T(8,128)S(1)}, f32[64,128]{1,0:T(8,128)S(1)}, u32[]{:S(2)}, u32[]{:S(2)}) collective-permute-start(f32[64,128]{1,0:T(8,128)S(1)} %get-tuple-element.89), channel_id=1, source_target_pairs={{0,12},{4,8},{8,4},{12,0},{1,13},{5,9},{9,5},{13,1},{2,14},{6,10},... | collective-permute-start | bytes 98312 | tf_op jit(solution)/shard_map/ppermute | solution.py:326
  21.7 0.8 collective-permute-start.4
  22.4 0.5 collective-permute-start.5
  22.9 0.4 prepare.1
  23.3 0.6 collective-permute-done.3.refs_1_
  23.9 2.7 %collective-permute-done.4.refs_2_ = f32[64,128]{1,0:T(8,128)S(1)} collective-permute-done((f32[64,128]{1,0:T(8,128)S(1)}, f32[64,128]{1,0:T(8,128)S(1)}, u32[]{:S(2)}, u32[]{:S(2)}) %collective-permute-start.4) | collective-permute-done | bytes 32800 | tf_op jit(solution)/shard_map/ppermute | solution.py:326
  27.0 1.6 %collective-permute-start.7 = (f32[64,128]{1,0:T(8,128)S(1)}, f32[64,128]{1,0:T(8,128)S(1)}, u32[]{:S(2)}, u32[]{:S(2)}) collective-permute-start(f32[64,128]{1,0:T(8,128)S(1)} %get-tuple-element.94), channel_id=1, source_target_pairs={{0,2},{1,3},{2,0},{3,1},{4,6},{5,7},{6,4},{7,5},{8,10},{9,11},{10,... | collective-permute-start | bytes 98312 | tf_op jit(solution)/shard_map/ppermute | solution.py:326
  28.9 0.3 pack.1
  29.2 1.5 %collective-permute-done.6.refs_1_ = f32[64,128]{1,0:T(8,128)S(1)} collective-permute-done((f32[64,128]{1,0:T(8,128)S(1)}, f32[64,128]{1,0:T(8,128)S(1)}, u32[]{:S(2)}, u32[]{:S(2)}) %collective-permute-start.6) | collective-permute-done | bytes 32800 | tf_op jit(solution)/shard_map/ppermute | solution.py:326
  30.6 0.4 collective-permute-done.7.refs_2_
  31.1 1.0 %lift.2 = (f32[256,128]{1,0:T(8,128)S(1)}, f32[768,128]{1,0:T(8,128)S(1)}, f32[256,128]{1,0:T(8,128)S(1)}, f32[128,128]{1,0:T(8,128)S(1)}, f32[128,128]{1,0:T(8,128)S(1)}, /*index=5*/f32[128,128]{1,0:T(8,128)S(1)}) custom-call(s32[1]{0:T(128)S(6)} %copy.15.size, f32[64,128]{1,0:T(8,128)S(1)} %get-tuple-element.92.refs_0_, ...), custom_call_target="tpu_custom_call" | custom-call | flops 201326592 | bytes 1048576 | tf_op jit(solution)/shard_map/lift/pallas_call | solution.py:49
  32.1 1.9 %collective-permute-start.9 = (f32[128,128]{1,0:T(8,128)S(1)}, f32[128,128]{1,0:T(8,128)S(1)}, u32[]{:S(2)}, u32[]{:S(2)}) collective-permute-start(f32[128,128]{1,0:T(8,128)S(1)} %get-tuple-element.103), channel_id=1, source_target_pairs={{0,8},{4,12},{8,0},{12,4},{1,9},{5,13},{9,1},{13,5},{2,10},{6,14},... | collective-permute-start | bytes 196616 | tf_op jit(solution)/shard_map/ppermute | solution.py:326
  33.9 1.2 %collective-permute-start.10 = (f32[128,128]{1,0:T(8,128)S(1)}, f32[128,128]{1,0:T(8,128)S(1)}, u32[]{:S(2)}, u32[]{:S(2)}) collective-permute-start(f32[128,128]{1,0:T(8,128)S(1)} %get-tuple-element.104), channel_id=1, source_target_pairs={{0,4},{4,0},{8,12},{12,8},{1,5},{5,1},{9,13},{13,9},{2,6},{6,2},{1... | collective-permute-start | bytes 196616 | tf_op jit(solution)/shard_map/ppermute | solution.py:326
  35.2 1.3 %collective-permute-start.11 = (f32[128,128]{1,0:T(8,128)S(1)}, f32[128,128]{1,0:T(8,128)S(1)}, u32[]{:S(2)}, u32[]{:S(2)}) collective-permute-start(f32[128,128]{1,0:T(8,128)S(1)} %get-tuple-element.105), channel_id=1, source_target_pairs={{0,12},{4,8},{8,4},{12,0},{1,13},{5,9},{9,5},{13,1},{2,14},{6,10},... | collective-permute-start | bytes 196616 | tf_op jit(solution)/shard_map/ppermute | solution.py:326
  36.7 1.5 %rest.3 = (f32[768,128]{1,0:T(8,128)S(1)}, f32[640,128]{1,0:T(8,128)S(1)}) custom-call(s32[1]{0:T(128)S(6)} %copy.15.size, bf16[768,1024]{1,0:T(8,128)(2,1)S(1)} %get-tuple-element.111.high, bf16[768,1024]{1,0:T(8,128)(2,1)S(1)} %get-tuple-element.112.low, f32[256,128]{1,0:T(8,128)S(1)} %get-tuple-element.108.mult_s.refs_5_, ...), custom_call_target="tpu_custom_call" | custom-call | flops 805306368 | bytes 4194304 | tf_op jit(solution)/shard_map/rest/pallas_call | solution.py:49
  38.2 1.1 %collective-permute-done.9.refs_0_ = f32[128,128]{1,0:T(8,128)S(1)} collective-permute-done((f32[128,128]{1,0:T(8,128)S(1)}, f32[128,128]{1,0:T(8,128)S(1)}, u32[]{:S(2)}, u32[]{:S(2)}) %collective-permute-start.9) | collective-permute-done | bytes 65568 | tf_op jit(solution)/shard_map/ppermute | solution.py:326
  39.3 2.0 %collective-permute-done.11.refs_2_ = f32[128,128]{1,0:T(8,128)S(1)} collective-permute-done((f32[128,128]{1,0:T(8,128)S(1)}, f32[128,128]{1,0:T(8,128)S(1)}, u32[]{:S(2)}, u32[]{:S(2)}) %collective-permute-start.11) | collective-permute-done | bytes 65568 | tf_op jit(solution)/shard_map/ppermute | solution.py:326
  41.3 0.5 sweep.3
  41.8 1.8 %collective-permute-start.12 = (f32[128,128]{1,0:T(8,128)S(1)}, f32[128,128]{1,0:T(8,128)S(1)}, u32[]{:S(2)}, u32[]{:S(2)}) collective-permute-start(f32[128,128]{1,0:T(8,128)S(1)} %get-tuple-element.115), channel_id=1, source_target_pairs={{0,12},{4,8},{8,4},{12,0},{1,13},{5,9},{9,5},{13,1},{2,14},{6,10},... | collective-permute-start | bytes 196616 | tf_op jit(solution)/shard_map/ppermute | solution.py:326
  43.6 0.7 collective-permute-start.13
  44.3 2.0 %collective-permute-start.14 = (f32[128,128]{1,0:T(8,128)S(1)}, f32[128,128]{1,0:T(8,128)S(1)}, u32[]{:S(2)}, u32[]{:S(2)}) collective-permute-start(f32[128,128]{1,0:T(8,128)S(1)} %get-tuple-element.117), channel_id=1, source_target_pairs={{0,8},{4,12},{8,0},{12,4},{1,9},{5,13},{9,1},{13,5},{2,10},{6,14},... | collective-permute-start | bytes 196616 | tf_op jit(solution)/shard_map/ppermute | solution.py:326
  46.5 1.5 %rest.4 = (f32[768,128]{1,0:T(8,128)S(1)}, f32[640,128]{1,0:T(8,128)S(1)}) custom-call(s32[1]{0:T(128)S(6)} %copy.15.size, bf16[768,1024]{1,0:T(8,128)(2,1)S(1)} %get-tuple-element.111.high, bf16[768,1024]{1,0:T(8,128)(2,1)S(1)} %get-tuple-element.112.low, f32[256,128]{1,0:T(8,128)S(1)} %get-tuple-element.119.mult_s.refs_5_, ...), custom_call_target="tpu_custom_call" | custom-call | flops 805306368 | bytes 4194304 | tf_op jit(solution)/shard_map/rest/pallas_call | solution.py:49
  48.0 0.5 collective-permute-done.12.refs_0_
  48.5 0.6 collective-permute-done.13.refs_1_
  49.0 1.5 %collective-permute-done.14.refs_2_ = f32[128,128]{1,0:T(8,128)S(1)} collective-permute-done((f32[128,128]{1,0:T(8,128)S(1)}, f32[128,128]{1,0:T(8,128)S(1)}, u32[]{:S(2)}, u32[]{:S(2)}) %collective-permute-start.14) | collective-permute-done | bytes 65568 | tf_op jit(solution)/shard_map/ppermute | solution.py:326
  50.6 0.5 sweep.4
  51.1 1.1 %collective-permute-start.15 = (f32[128,128]{1,0:T(8,128)S(1)}, f32[128,128]{1,0:T(8,128)S(1)}, u32[]{:S(2)}, u32[]{:S(2)}) collective-permute-start(f32[128,128]{1,0:T(8,128)S(1)} %get-tuple-element.122), channel_id=1, source_target_pairs={{0,8},{4,12},{8,0},{12,4},{1,9},{5,13},{9,1},{13,5},{2,10},{6,14},... | collective-permute-start | bytes 196616 | tf_op jit(solution)/shard_map/ppermute | solution.py:326
  52.2 1.7 %collective-permute-start.16 = (f32[128,128]{1,0:T(8,128)S(1)}, f32[128,128]{1,0:T(8,128)S(1)}, u32[]{:S(2)}, u32[]{:S(2)}) collective-permute-start(f32[128,128]{1,0:T(8,128)S(1)} %get-tuple-element.123), channel_id=1, source_target_pairs={{0,12},{4,8},{8,4},{12,0},{1,13},{5,9},{9,5},{13,1},{2,14},{6,10},... | collective-permute-start | bytes 196616 | tf_op jit(solution)/shard_map/ppermute | solution.py:326
  53.9 0.8 collective-permute-start.17
  54.8 1.1 %rest_first.1 = (f32[768,128]{1,0:T(8,128)S(1)}, f32[64,128]{1,0:T(8,128)S(1)}) custom-call(s32[1]{0:T(128)S(6)} %copy.15.size, bf16[768,1024]{1,0:T(8,128)(2,1)S(1)} %get-tuple-element.111.high, bf16[768,1024]{1,0:T(8,128)(2,1)S(1)} %get-tuple-element.112.low, f32[256,128]{1,0:T(8,128)S(1)} %get-tuple-element.126.mult_s.refs_5_, ...), custom_call_target="tpu_custom_call" | custom-call | flops 603979776 | bytes 3145728 | tf_op jit(solution)/shard_map/rest_first/pallas_call | solution.py:49
  56.0 1.2 %collective-permute-done.15.refs_0_ = f32[128,128]{1,0:T(8,128)S(1)} collective-permute-done((f32[128,128]{1,0:T(8,128)S(1)}, f32[128,128]{1,0:T(8,128)S(1)}, u32[]{:S(2)}, u32[]{:S(2)}) %collective-permute-start.15) | collective-permute-done | bytes 65568 | tf_op jit(solution)/shard_map/ppermute | solution.py:326
  57.1 1.2 %collective-permute-done.16.refs_1_ = f32[128,128]{1,0:T(8,128)S(1)} collective-permute-done((f32[128,128]{1,0:T(8,128)S(1)}, f32[128,128]{1,0:T(8,128)S(1)}, u32[]{:S(2)}, u32[]{:S(2)}) %collective-permute-start.16) | collective-permute-done | bytes 65568 | tf_op jit(solution)/shard_map/ppermute | solution.py:326
  58.4 0.4 collective-permute-done.17.refs_2_
  58.8 0.4 coarse.3
  59.3 2.0 %collective-permute-start.18 = (f32[64,128]{1,0:T(8,128)S(1)}, f32[64,128]{1,0:T(8,128)S(1)}, u32[]{:S(2)}, u32[]{:S(2)}) collective-permute-start(f32[64,128]{1,0:T(8,128)S(1)} %get-tuple-element.130), channel_id=1, source_target_pairs={{0,12},{4,8},{8,4},{12,0},{1,13},{5,9},{9,5},{13,1},{2,14},{6,10},... | collective-permute-start | bytes 98312 | tf_op jit(solution)/shard_map/ppermute | solution.py:326
  61.2 2.5 %collective-permute-start.20 = (f32[64,128]{1,0:T(8,128)S(1)}, f32[64,128]{1,0:T(8,128)S(1)}, u32[]{:S(2)}, u32[]{:S(2)}) collective-permute-start(f32[64,128]{1,0:T(8,128)S(1)} %get-tuple-element.132), channel_id=1, source_target_pairs={{0,4},{4,0},{8,12},{12,8},{1,5},{5,1},{9,13},{13,9},{2,6},{6,2},{1... | collective-permute-start | bytes 98312 | tf_op jit(solution)/shard_map/ppermute | solution.py:326
  63.7 1.3 %collective-permute-done.18.refs_1_ = f32[64,128]{1,0:T(8,128)S(1)} collective-permute-done((f32[64,128]{1,0:T(8,128)S(1)}, f32[64,128]{1,0:T(8,128)S(1)}, u32[]{:S(2)}, u32[]{:S(2)}) %collective-permute-start.18) | collective-permute-done | bytes 32800 | tf_op jit(solution)/shard_map/ppermute | solution.py:326
  65.0 1.0 %collective-permute-done.19.refs_2_ = f32[64,128]{1,0:T(8,128)S(1)} collective-permute-done((f32[64,128]{1,0:T(8,128)S(1)}, f32[64,128]{1,0:T(8,128)S(1)}, u32[]{:S(2)}, u32[]{:S(2)}) %collective-permute-start.19) | collective-permute-done | bytes 32800 | tf_op jit(solution)/shard_map/ppermute | solution.py:326
  66.4 1.2 %collective-permute-start.22 = (f32[64,128]{1,0:T(8,128)S(1)}, f32[64,128]{1,0:T(8,128)S(1)}, u32[]{:S(2)}, u32[]{:S(2)}) collective-permute-start(f32[64,128]{1,0:T(8,128)S(1)} %get-tuple-element.135), channel_id=1, source_target_pairs={{0,2},{1,3},{2,0},{3,1},{4,6},{5,7},{6,4},{7,5},{8,10},{9,11},{10,... | collective-permute-start | bytes 98312 | tf_op jit(solution)/shard_map/ppermute | solution.py:326
  67.6 0.6 collective-permute-start.23
  68.2 1.5 %collective-permute-done.21.refs_1_ = f32[64,128]{1,0:T(8,128)S(1)} collective-permute-done((f32[64,128]{1,0:T(8,128)S(1)}, f32[64,128]{1,0:T(8,128)S(1)}, u32[]{:S(2)}, u32[]{:S(2)}) %collective-permute-start.21) | collective-permute-done | bytes 32800 | tf_op jit(solution)/shard_map/ppermute | solution.py:326
  69.7 0.8 collective-permute-done.22.refs_2_
  70.5 1.0 %lift.3 = (f32[256,128]{1,0:T(8,128)S(1)}, f32[768,128]{1,0:T(8,128)S(1)}, f32[256,128]{1,0:T(8,128)S(1)}, f32[128,128]{1,0:T(8,128)S(1)}, f32[128,128]{1,0:T(8,128)S(1)}, /*index=5*/f32[128,128]{1,0:T(8,128)S(1)}) custom-call(s32[1]{0:T(128)S(6)} %copy.15.size, f32[64,128]{1,0:T(8,128)S(1)} %get-tuple-element.133.refs_0_, ...), custom_call_target="tpu_custom_call" | custom-call | flops 201326592 | bytes 1048576 | tf_op jit(solution)/shard_map/lift/pallas_call | solution.py:49
  71.5 2.1 %collective-permute-start.24 = (f32[128,128]{1,0:T(8,128)S(1)}, f32[128,128]{1,0:T(8,128)S(1)}, u32[]{:S(2)}, u32[]{:S(2)}) collective-permute-start(f32[128,128]{1,0:T(8,128)S(1)} %get-tuple-element.139), channel_id=1, source_target_pairs={{0,8},{4,12},{8,0},{12,4},{1,9},{5,13},{9,1},{13,5},{2,10},{6,14},... | collective-permute-start | bytes 196616 | tf_op jit(solution)/shard_map/ppermute | solution.py:326
  73.6 0.5 collective-permute-start.25
  74.1 1.9 %collective-permute-start.26 = (f32[128,128]{1,0:T(8,128)S(1)}, f32[128,128]{1,0:T(8,128)S(1)}, u32[]{:S(2)}, u32[]{:S(2)}) collective-permute-start(f32[128,128]{1,0:T(8,128)S(1)} %get-tuple-element.141), channel_id=1, source_target_pairs={{0,12},{4,8},{8,4},{12,0},{1,13},{5,9},{9,5},{13,1},{2,14},{6,10},... | collective-permute-start | bytes 196616 | tf_op jit(solution)/shard_map/ppermute | solution.py:326
  76.2 1.5 %rest.5 = (f32[768,128]{1,0:T(8,128)S(1)}, f32[640,128]{1,0:T(8,128)S(1)}) custom-call(s32[1]{0:T(128)S(6)} %copy.15.size, bf16[768,1024]{1,0:T(8,128)(2,1)S(1)} %get-tuple-element.111.high, bf16[768,1024]{1,0:T(8,128)(2,1)S(1)} %get-tuple-element.112.low, f32[256,128]{1,0:T(8,128)S(1)} %get-tuple-element.143.mult_s.refs_5_, ...), custom_call_target="tpu_custom_call" | custom-call | flops 805306368 | bytes 4194304 | tf_op jit(solution)/shard_map/rest/pallas_call | solution.py:49
  77.7 1.1 %collective-permute-done.24.refs_0_ = f32[128,128]{1,0:T(8,128)S(1)} collective-permute-done((f32[128,128]{1,0:T(8,128)S(1)}, f32[128,128]{1,0:T(8,128)S(1)}, u32[]{:S(2)}, u32[]{:S(2)}) %collective-permute-start.24) | collective-permute-done | bytes 65568 | tf_op jit(solution)/shard_map/ppermute | solution.py:326
  78.7 1.7 %collective-permute-done.26.refs_2_ = f32[128,128]{1,0:T(8,128)S(1)} collective-permute-done((f32[128,128]{1,0:T(8,128)S(1)}, f32[128,128]{1,0:T(8,128)S(1)}, u32[]{:S(2)}, u32[]{:S(2)}) %collective-permute-start.26) | collective-permute-done | bytes 65568 | tf_op jit(solution)/shard_map/ppermute | solution.py:326
  80.5 0.5 sweep.5
  81.0 1.6 %collective-permute-start.27 = (f32[128,128]{1,0:T(8,128)S(1)}, f32[128,128]{1,0:T(8,128)S(1)}, u32[]{:S(2)}, u32[]{:S(2)}) collective-permute-start(f32[128,128]{1,0:T(8,128)S(1)} %get-tuple-element.146), channel_id=1, source_target_pairs={{0,8},{4,12},{8,0},{12,4},{1,9},{5,13},{9,1},{13,5},{2,10},{6,14},... | collective-permute-start | bytes 196616 | tf_op jit(solution)/shard_map/ppermute | solution.py:326
  82.6 1.9 %collective-permute-start.28 = (f32[128,128]{1,0:T(8,128)S(1)}, f32[128,128]{1,0:T(8,128)S(1)}, u32[]{:S(2)}, u32[]{:S(2)}) collective-permute-start(f32[128,128]{1,0:T(8,128)S(1)} %get-tuple-element.147), channel_id=1, source_target_pairs={{0,12},{4,8},{8,4},{12,0},{1,13},{5,9},{9,5},{13,1},{2,14},{6,10},... | collective-permute-start | bytes 196616 | tf_op jit(solution)/shard_map/ppermute | solution.py:326
  84.8 1.9 %rest_last.1 = (f32[1024,128]{1,0:T(8,128)}, f32[1024,128]{1,0:T(8,128)}) custom-call(s32[1]{0:T(128)S(6)} %copy.15.size, bf16[768,1024]{1,0:T(8,128)(2,1)S(1)} %get-tuple-element.111.high, bf16[768,1024]{1,0:T(8,128)(2,1)S(1)} %get-tuple-element.112.low, f32[256,128]{1,0:T(8,128)S(1)} %get-tuple-element.150.mult_s.refs_5_, ...), custom_call_target="tpu_custom_call" | custom-call | flops 603979776 | bytes 3145728 | tf_op jit(solution)/shard_map/rest_last/pallas_call | solution.py:49
  86.6 1.1 %collective-permute-done.27.refs_0_ = f32[128,128]{1,0:T(8,128)S(1)} collective-permute-done((f32[128,128]{1,0:T(8,128)S(1)}, f32[128,128]{1,0:T(8,128)S(1)}, u32[]{:S(2)}, u32[]{:S(2)}) %collective-permute-start.27) | collective-permute-done | bytes 65568 | tf_op jit(solution)/shard_map/ppermute | solution.py:326
  87.8 1.2 %collective-permute-done.28.refs_1_ = f32[128,128]{1,0:T(8,128)S(1)} collective-permute-done((f32[128,128]{1,0:T(8,128)S(1)}, f32[128,128]{1,0:T(8,128)S(1)}, u32[]{:S(2)}, u32[]{:S(2)}) %collective-permute-start.28) | collective-permute-done | bytes 65568 | tf_op jit(solution)/shard_map/ppermute | solution.py:326
  89.0 0.4 collective-permute-done.29.refs_2_
  89.4 0.9 %last.1 = (f32[1024,128]{1,0:T(8,128)}, f32[1024,128]{1,0:T(8,128)}) custom-call(s32[1]{0:T(128)S(6)} %copy.15.size, f32[128,128]{1,0:T(8,128)S(1)} %collective-permute-done.27.refs_0_, f32[128,128]{1,0:T(8,128)S(1)} %collective-permute-done.28.refs_1_, ...), custom_call_target="tpu_custom_call", output_to_operand_aliasing={{0}: (8, {}), {1}: (9, {})} | custom-call | flops 75497472 | bytes 196608 | tf_op jit(solution)/shard_map/last/pallas_call | solution.py:49
  (33 shorter events, 2.5 us)
Async XLA Ops:
  0.6 8.5 %copy-start = (f32[1,1024,128]{2,1,0:T(8,128)S(1)}, f32[1,1024,128]{2,1,0:T(8,128)}, u32[]{:S(2)}) copy-start(f32[1,1024,128]{2,1,0:T(8,128)} %param.12) | copy-start | bytes 1572868
  0.6 8.7 %copy-start.1 = (f32[1,1024,1024]{2,1,0:T(8,128)S(1)}, f32[1,1024,1024]{2,1,0:T(8,128)}, u32[]{:S(2)}) copy-start(f32[1,1024,1024]{2,1,0:T(8,128)} %param.9) | copy-start | bytes 12582916
  0.7 8.7 %copy-start.2 = (f32[1,1024,128]{2,1,0:T(8,128)S(1)}, f32[1,1024,128]{2,1,0:T(8,128)}, u32[]{:S(2)}) copy-start(f32[1,1024,128]{2,1,0:T(8,128)} %param.13) | copy-start | bytes 1572868
  0.7 8.7 %copy-start.3 = (f32[1,64,1024]{2,1,0:T(8,128)S(1)}, f32[1,64,1024]{2,1,0:T(8,128)}, u32[]{:S(2)}) copy-start(f32[1,64,1024]{2,1,0:T(8,128)} %param.11) | copy-start | bytes 786436
  2.8 14.4 %collective-permute-start = (f32[264,128]{1,0:T(8,128)S(1)}, f32[264,128]{1,0:T(8,128)S(1)}, u32[]{:S(2)}, u32[]{:S(2)}) collective-permute-start(f32[264,128]{1,0:T(8,128)S(1)} %get-tuple-element.81), channel_id=1, source_target_pairs={{0,8},{4,12},{8,0},{12,4},{1,9},{5,13},{9,1},{13,5},{2,10},{6,14},... | collective-permute-start | bytes 405512 | tf_op jit(solution)/shard_map/ppermute | solution.py:326
  6.9 10.3 %collective-permute-start.1 = (f32[264,128]{1,0:T(8,128)S(1)}, f32[264,128]{1,0:T(8,128)S(1)}, u32[]{:S(2)}, u32[]{:S(2)}) collective-permute-start(f32[264,128]{1,0:T(8,128)S(1)} %get-tuple-element.82), channel_id=1, source_target_pairs={{0,12},{4,8},{8,4},{12,0},{1,13},{5,9},{9,5},{13,1},{2,14},{6,10},... | collective-permute-start | bytes 405512 | tf_op jit(solution)/shard_map/ppermute | solution.py:326
  8.2 9.4 %collective-permute-start.2 = (f32[264,128]{1,0:T(8,128)S(1)}, f32[264,128]{1,0:T(8,128)S(1)}, u32[]{:S(2)}, u32[]{:S(2)}) collective-permute-start(f32[264,128]{1,0:T(8,128)S(1)} %get-tuple-element.83), channel_id=1, source_target_pairs={{0,4},{4,0},{8,12},{12,8},{1,5},{5,1},{9,13},{13,9},{2,6},{6,2},{1... | collective-permute-start | bytes 405512 | tf_op jit(solution)/shard_map/ppermute | solution.py:326
  11.3 11.6 %copy-start.4 = (f32[256,256]{1,0:T(8,128)S(1)}, f32[256,256]{1,0:T(8,128)}, u32[]{:S(2)}) copy-start(f32[256,256]{1,0:T(8,128)} %tile.3) | copy-start | bytes 786436
  11.3 11.6 %copy-start.5 = (s32[1,1024]{1,0:T(1,128)S(1)}, s32[1,1024]{1,0:T(1,128)}, u32[]{:S(2)}) copy-start(s32[1,1024]{1,0:T(1,128)} %contact.1) | copy-start | bytes 12292
  18.1 5.8 %collective-permute-start.3 = (f32[64,128]{1,0:T(8,128)S(1)}, f32[64,128]{1,0:T(8,128)S(1)}, u32[]{:S(2)}, u32[]{:S(2)}) collective-permute-start(f32[64,128]{1,0:T(8,128)S(1)} %get-tuple-element.89), channel_id=1, source_target_pairs={{0,12},{4,8},{8,4},{12,0},{1,13},{5,9},{9,5},{13,1},{2,14},{6,10},... | collective-permute-start | bytes 98312 | tf_op jit(solution)/shard_map/ppermute | solution.py:326
  21.7 4.9 %collective-permute-start.4 = (f32[64,128]{1,0:T(8,128)S(1)}, f32[64,128]{1,0:T(8,128)S(1)}, u32[]{:S(2)}, u32[]{:S(2)}) collective-permute-start(f32[64,128]{1,0:T(8,128)S(1)} %get-tuple-element.90), channel_id=1, source_target_pairs={{0,8},{4,12},{8,0},{12,4},{1,9},{5,13},{9,1},{13,5},{2,10},{6,14},... | collective-permute-start | bytes 98312 | tf_op jit(solution)/shard_map/ppermute | solution.py:326
  22.4 4.3 %collective-permute-start.5 = (f32[64,128]{1,0:T(8,128)S(1)}, f32[64,128]{1,0:T(8,128)S(1)}, u32[]{:S(2)}, u32[]{:S(2)}) collective-permute-start(f32[64,128]{1,0:T(8,128)S(1)} %get-tuple-element.91), channel_id=1, source_target_pairs={{0,4},{4,0},{8,12},{12,8},{1,5},{5,1},{9,13},{13,9},{2,6},{6,2},{1... | collective-permute-start | bytes 98312 | tf_op jit(solution)/shard_map/ppermute | solution.py:326
  26.9 3.7 %collective-permute-start.6 = (f32[64,128]{1,0:T(8,128)S(1)}, f32[64,128]{1,0:T(8,128)S(1)}, u32[]{:S(2)}, u32[]{:S(2)}) collective-permute-start(f32[64,128]{1,0:T(8,128)S(1)} %get-tuple-element.93), channel_id=1, source_target_pairs={{0,3},{1,2},{2,1},{3,0},{4,7},{5,6},{6,5},{7,4},{8,11},{9,10},{10,... | collective-permute-start | bytes 98312 | tf_op jit(solution)/shard_map/ppermute | solution.py:326
  27.0 4.0 %collective-permute-start.7 = (f32[64,128]{1,0:T(8,128)S(1)}, f32[64,128]{1,0:T(8,128)S(1)}, u32[]{:S(2)}, u32[]{:S(2)}) collective-permute-start(f32[64,128]{1,0:T(8,128)S(1)} %get-tuple-element.94), channel_id=1, source_target_pairs={{0,2},{1,3},{2,0},{3,1},{4,6},{5,7},{6,4},{7,5},{8,10},{9,11},{10,... | collective-permute-start | bytes 98312 | tf_op jit(solution)/shard_map/ppermute | solution.py:326
  28.6 2.5 %collective-permute-start.8 = (f32[64,128]{1,0:T(8,128)S(1)}, f32[64,128]{1,0:T(8,128)S(1)}, u32[]{:S(2)}, u32[]{:S(2)}) collective-permute-start(f32[64,128]{1,0:T(8,128)S(1)} %get-tuple-element.95), channel_id=1, source_target_pairs={{0,1},{1,0},{2,3},{3,2},{4,5},{5,4},{6,7},{7,6},{8,9},{9,8},{10,11... | collective-permute-start | bytes 98312 | tf_op jit(solution)/shard_map/ppermute | solution.py:326
  32.1 7.2 %collective-permute-start.9 = (f32[128,128]{1,0:T(8,128)S(1)}, f32[128,128]{1,0:T(8,128)S(1)}, u32[]{:S(2)}, u32[]{:S(2)}) collective-permute-start(f32[128,128]{1,0:T(8,128)S(1)} %get-tuple-element.103), channel_id=1, source_target_pairs={{0,8},{4,12},{8,0},{12,4},{1,9},{5,13},{9,1},{13,5},{2,10},{6,14},... | collective-permute-start | bytes 196616 | tf_op jit(solution)/shard_map/ppermute | solution.py:326
  33.9 5.3 %collective-permute-start.10 = (f32[128,128]{1,0:T(8,128)S(1)}, f32[128,128]{1,0:T(8,128)S(1)}, u32[]{:S(2)}, u32[]{:S(2)}) collective-permute-start(f32[128,128]{1,0:T(8,128)S(1)} %get-tuple-element.104), channel_id=1, source_target_pairs={{0,4},{4,0},{8,12},{12,8},{1,5},{5,1},{9,13},{13,9},{2,6},{6,2},{1... | collective-permute-start | bytes 196616 | tf_op jit(solution)/shard_map/ppermute | solution.py:326
  35.2 6.1 %collective-permute-start.11 = (f32[128,128]{1,0:T(8,128)S(1)}, f32[128,128]{1,0:T(8,128)S(1)}, u32[]{:S(2)}, u32[]{:S(2)}) collective-permute-start(f32[128,128]{1,0:T(8,128)S(1)} %get-tuple-element.105), channel_id=1, source_target_pairs={{0,12},{4,8},{8,4},{12,0},{1,13},{5,9},{9,5},{13,1},{2,14},{6,10},... | collective-permute-start | bytes 196616 | tf_op jit(solution)/shard_map/ppermute | solution.py:326
  41.8 6.6 %collective-permute-start.12 = (f32[128,128]{1,0:T(8,128)S(1)}, f32[128,128]{1,0:T(8,128)S(1)}, u32[]{:S(2)}, u32[]{:S(2)}) collective-permute-start(f32[128,128]{1,0:T(8,128)S(1)} %get-tuple-element.115), channel_id=1, source_target_pairs={{0,12},{4,8},{8,4},{12,0},{1,13},{5,9},{9,5},{13,1},{2,14},{6,10},... | collective-permute-start | bytes 196616 | tf_op jit(solution)/shard_map/ppermute | solution.py:326
  43.6 5.4 %collective-permute-start.13 = (f32[128,128]{1,0:T(8,128)S(1)}, f32[128,128]{1,0:T(8,128)S(1)}, u32[]{:S(2)}, u32[]{:S(2)}) collective-permute-start(f32[128,128]{1,0:T(8,128)S(1)} %get-tuple-element.116), channel_id=1, source_target_pairs={{0,4},{4,0},{8,12},{12,8},{1,5},{5,1},{9,13},{13,9},{2,6},{6,2},{1... | collective-permute-start | bytes 196616 | tf_op jit(solution)/shard_map/ppermute | solution.py:326
  44.3 6.2 %collective-permute-start.14 = (f32[128,128]{1,0:T(8,128)S(1)}, f32[128,128]{1,0:T(8,128)S(1)}, u32[]{:S(2)}, u32[]{:S(2)}) collective-permute-start(f32[128,128]{1,0:T(8,128)S(1)} %get-tuple-element.117), channel_id=1, source_target_pairs={{0,8},{4,12},{8,0},{12,4},{1,9},{5,13},{9,1},{13,5},{2,10},{6,14},... | collective-permute-start | bytes 196616 | tf_op jit(solution)/shard_map/ppermute | solution.py:326
  51.1 6.1 %collective-permute-start.15 = (f32[128,128]{1,0:T(8,128)S(1)}, f32[128,128]{1,0:T(8,128)S(1)}, u32[]{:S(2)}, u32[]{:S(2)}) collective-permute-start(f32[128,128]{1,0:T(8,128)S(1)} %get-tuple-element.122), channel_id=1, source_target_pairs={{0,8},{4,12},{8,0},{12,4},{1,9},{5,13},{9,1},{13,5},{2,10},{6,14},... | collective-permute-start | bytes 196616 | tf_op jit(solution)/shard_map/ppermute | solution.py:326
  52.2 6.2 %collective-permute-start.16 = (f32[128,128]{1,0:T(8,128)S(1)}, f32[128,128]{1,0:T(8,128)S(1)}, u32[]{:S(2)}, u32[]{:S(2)}) collective-permute-start(f32[128,128]{1,0:T(8,128)S(1)} %get-tuple-element.123), channel_id=1, source_target_pairs={{0,12},{4,8},{8,4},{12,0},{1,13},{5,9},{9,5},{13,1},{2,14},{6,10},... | collective-permute-start | bytes 196616 | tf_op jit(solution)/shard_map/ppermute | solution.py:326
  53.9 5.0 %collective-permute-start.17 = (f32[128,128]{1,0:T(8,128)S(1)}, f32[128,128]{1,0:T(8,128)S(1)}, u32[]{:S(2)}, u32[]{:S(2)}) collective-permute-start(f32[128,128]{1,0:T(8,128)S(1)} %get-tuple-element.124), channel_id=1, source_target_pairs={{0,4},{4,0},{8,12},{12,8},{1,5},{5,1},{9,13},{13,9},{2,6},{6,2},{1... | collective-permute-start | bytes 196616 | tf_op jit(solution)/shard_map/ppermute | solution.py:326
  59.3 5.8 %collective-permute-start.18 = (f32[64,128]{1,0:T(8,128)S(1)}, f32[64,128]{1,0:T(8,128)S(1)}, u32[]{:S(2)}, u32[]{:S(2)}) collective-permute-start(f32[64,128]{1,0:T(8,128)S(1)} %get-tuple-element.130), channel_id=1, source_target_pairs={{0,12},{4,8},{8,4},{12,0},{1,13},{5,9},{9,5},{13,1},{2,14},{6,10},... | collective-permute-start | bytes 98312 | tf_op jit(solution)/shard_map/ppermute | solution.py:326
  61.2 4.8 %collective-permute-start.19 = (f32[64,128]{1,0:T(8,128)S(1)}, f32[64,128]{1,0:T(8,128)S(1)}, u32[]{:S(2)}, u32[]{:S(2)}) collective-permute-start(f32[64,128]{1,0:T(8,128)S(1)} %get-tuple-element.131), channel_id=1, source_target_pairs={{0,8},{4,12},{8,0},{12,4},{1,9},{5,13},{9,1},{13,5},{2,10},{6,14},... | collective-permute-start | bytes 98312 | tf_op jit(solution)/shard_map/ppermute | solution.py:326
  61.2 4.8 %collective-permute-start.20 = (f32[64,128]{1,0:T(8,128)S(1)}, f32[64,128]{1,0:T(8,128)S(1)}, u32[]{:S(2)}, u32[]{:S(2)}) collective-permute-start(f32[64,128]{1,0:T(8,128)S(1)} %get-tuple-element.132), channel_id=1, source_target_pairs={{0,4},{4,0},{8,12},{12,8},{1,5},{5,1},{9,13},{13,9},{2,6},{6,2},{1... | collective-permute-start | bytes 98312 | tf_op jit(solution)/shard_map/ppermute | solution.py:326
  66.3 3.4 %collective-permute-start.21 = (f32[64,128]{1,0:T(8,128)S(1)}, f32[64,128]{1,0:T(8,128)S(1)}, u32[]{:S(2)}, u32[]{:S(2)}) collective-permute-start(f32[64,128]{1,0:T(8,128)S(1)} %get-tuple-element.134), channel_id=1, source_target_pairs={{0,3},{1,2},{2,1},{3,0},{4,7},{5,6},{6,5},{7,4},{8,11},{9,10},{10,... | collective-permute-start | bytes 98312 | tf_op jit(solution)/shard_map/ppermute | solution.py:326
  66.4 4.1 %collective-permute-start.22 = (f32[64,128]{1,0:T(8,128)S(1)}, f32[64,128]{1,0:T(8,128)S(1)}, u32[]{:S(2)}, u32[]{:S(2)}) collective-permute-start(f32[64,128]{1,0:T(8,128)S(1)} %get-tuple-element.135), channel_id=1, source_target_pairs={{0,2},{1,3},{2,0},{3,1},{4,6},{5,7},{6,4},{7,5},{8,10},{9,11},{10,... | collective-permute-start | bytes 98312 | tf_op jit(solution)/shard_map/ppermute | solution.py:326
  67.6 2.9 %collective-permute-start.23 = (f32[64,128]{1,0:T(8,128)S(1)}, f32[64,128]{1,0:T(8,128)S(1)}, u32[]{:S(2)}, u32[]{:S(2)}) collective-permute-start(f32[64,128]{1,0:T(8,128)S(1)} %get-tuple-element.136), channel_id=1, source_target_pairs={{0,1},{1,0},{2,3},{3,2},{4,5},{5,4},{6,7},{7,6},{8,9},{9,8},{10,11... | collective-permute-start | bytes 98312 | tf_op jit(solution)/shard_map/ppermute | solution.py:326
  71.5 7.2 %collective-permute-start.24 = (f32[128,128]{1,0:T(8,128)S(1)}, f32[128,128]{1,0:T(8,128)S(1)}, u32[]{:S(2)}, u32[]{:S(2)}) collective-permute-start(f32[128,128]{1,0:T(8,128)S(1)} %get-tuple-element.139), channel_id=1, source_target_pairs={{0,8},{4,12},{8,0},{12,4},{1,9},{5,13},{9,1},{13,5},{2,10},{6,14},... | collective-permute-start | bytes 196616 | tf_op jit(solution)/shard_map/ppermute | solution.py:326
  73.6 5.1 %collective-permute-start.25 = (f32[128,128]{1,0:T(8,128)S(1)}, f32[128,128]{1,0:T(8,128)S(1)}, u32[]{:S(2)}, u32[]{:S(2)}) collective-permute-start(f32[128,128]{1,0:T(8,128)S(1)} %get-tuple-element.140), channel_id=1, source_target_pairs={{0,4},{4,0},{8,12},{12,8},{1,5},{5,1},{9,13},{13,9},{2,6},{6,2},{1... | collective-permute-start | bytes 196616 | tf_op jit(solution)/shard_map/ppermute | solution.py:326
  74.1 6.4 %collective-permute-start.26 = (f32[128,128]{1,0:T(8,128)S(1)}, f32[128,128]{1,0:T(8,128)S(1)}, u32[]{:S(2)}, u32[]{:S(2)}) collective-permute-start(f32[128,128]{1,0:T(8,128)S(1)} %get-tuple-element.141), channel_id=1, source_target_pairs={{0,12},{4,8},{8,4},{12,0},{1,13},{5,9},{9,5},{13,1},{2,14},{6,10},... | collective-permute-start | bytes 196616 | tf_op jit(solution)/shard_map/ppermute | solution.py:326
  81.0 6.8 %collective-permute-start.27 = (f32[128,128]{1,0:T(8,128)S(1)}, f32[128,128]{1,0:T(8,128)S(1)}, u32[]{:S(2)}, u32[]{:S(2)}) collective-permute-start(f32[128,128]{1,0:T(8,128)S(1)} %get-tuple-element.146), channel_id=1, source_target_pairs={{0,8},{4,12},{8,0},{12,4},{1,9},{5,13},{9,1},{13,5},{2,10},{6,14},... | collective-permute-start | bytes 196616 | tf_op jit(solution)/shard_map/ppermute | solution.py:326
  82.6 6.4 %collective-permute-start.28 = (f32[128,128]{1,0:T(8,128)S(1)}, f32[128,128]{1,0:T(8,128)S(1)}, u32[]{:S(2)}, u32[]{:S(2)}) collective-permute-start(f32[128,128]{1,0:T(8,128)S(1)} %get-tuple-element.147), channel_id=1, source_target_pairs={{0,12},{4,8},{8,4},{12,0},{1,13},{5,9},{9,5},{13,1},{2,14},{6,10},... | collective-permute-start | bytes 196616 | tf_op jit(solution)/shard_map/ppermute | solution.py:326
  84.5 5.0 %collective-permute-start.29 = (f32[128,128]{1,0:T(8,128)S(1)}, f32[128,128]{1,0:T(8,128)S(1)}, u32[]{:S(2)}, u32[]{:S(2)}) collective-permute-start(f32[128,128]{1,0:T(8,128)S(1)} %get-tuple-element.148), channel_id=1, source_target_pairs={{0,4},{4,0},{8,12},{12,8},{1,5},{5,1},{9,13},{13,9},{2,6},{6,2},{1... | collective-permute-start | bytes 196616 | tf_op jit(solution)/shard_map/ppermute | solution.py:326

commit v8 on v7

--- a/solution.py
+++ b/solution.py
@@ -79,9 +79,22 @@
     return jax.ShapeDtypeStruct((rows, columns), dtype)
 
 
+def places(peers, rows):
+    shared = peers.shape[1]
+    across = jnp.broadcast_to(peers[...], (shared, shared))
+    down = across.T
+    first = lax.broadcasted_iota(jnp.int32, (shared, shared), 0)
+    second = lax.broadcasted_iota(jnp.int32, (shared, shared), 1)
+    slot = jnp.sum(
+        jnp.where((across == down) & (second < first), 1.0, 0.0), axis=1, keepdims=True
+    ).astype(jnp.int32)
+    wanted = jnp.broadcast_to(rows[...], (shared, shared)).T[:, :1]
+    return down[:, :1] ^ lax.axis_index("wide"), slot, wanted
+
+
 def first_kernel(n, cap, peers_at, rows_at, operator_at, mult_at, *refs):
-    unpack_own, unpack_all, unpack, high, low, image = refs[:6]
-    sends, (peers, rows, operator, mult, done) = refs[6:6 + n], refs[6 + n:]
+    high, low, image = refs[:3]
+    sends, (peers, rows, operator, mult, done) = refs[3:3 + n], refs[3 + n:]
     shared, width = image.shape
     copies = [
         pltpu.make_async_copy(source, target, done.at[i])
@@ -93,30 +106,15 @@
         copy.start()
     copies[0].wait()
     copies[1].wait()
-    across = jnp.broadcast_to(peers[...], (shared, shared))
-    down = across.T
-    first = lax.broadcasted_iota(jnp.int32, (shared, shared), 0)
-    second = lax.broadcasted_iota(jnp.int32, (shared, shared), 1)
-    slot = jnp.sum(
-        jnp.where((across == down) & (second < first), 1.0, 0.0), axis=1, keepdims=True
-    ).astype(jnp.int32)
-    wanted = jnp.broadcast_to(rows[...], (shared, shared)).T[:, :1]
-    far = down[:, :1] ^ lax.axis_index("wide")
-
-    def marks(key, columns):
-        hit = key == lax.broadcasted_iota(jnp.int32, (shared, columns), 1)
-        return jnp.where(hit, 1.0, 0.0).astype(BF16)
-
-    unpack_own[...] = marks(jnp.where(far == 0, wanted, -1), shared)
-    unpack_all[...] = marks(jnp.where(far == 0, -1, (far - 1) * shared + wanted), unpack_all.shape[1])
-    unpack[...] = marks(jnp.where(far == 0, -1, (far - 1) * cap + slot), unpack.shape[1])
+    far, slot, wanted = places(peers, rows)
+    wanted = wanted.astype(F32)
     lane = lax.broadcasted_iota(jnp.int32, (shared, width), 1)
     for d, out in enumerate(sends, 1):
         out[shared:, :] = jnp.zeros((out.shape[0] - shared, width), F32)
         for c in range(-(-cap // width)):
             hit = (far == d) & (slot == lane + c * width)
             out[shared + c:shared + c + 1, :] = jnp.sum(
-                jnp.where(hit, wanted.astype(F32), 0.0), axis=0, keepdims=True
+                jnp.where(hit, wanted, 0.0), axis=0, keepdims=True
             )
     copies[2].wait()
     copies[3].wait()
@@ -126,6 +124,18 @@
     image[...] = value
     for out in sends:
         out[:shared, :] = value
+
+
+def marks_kernel(cap, peers, rows, unpack_own, unpack_all, unpack):
+    far, slot, wanted = places(peers, rows)
+    shared = peers.shape[1]
+    for key, out in (
+        (jnp.where(far == 0, wanted, -1), unpack_own),
+        (jnp.where(far == 0, -1, (far - 1) * shared + wanted), unpack_all),
+        (jnp.where(far == 0, -1, (far - 1) * cap + slot), unpack),
+    ):
+        hit = key == lax.broadcasted_iota(jnp.int32, out.shape, 1)
+        out[...] = jnp.where(hit, 1.0, 0.0).astype(BF16)
 
 
 def pack_kernel(times, cap, *refs):
@@ -281,13 +291,19 @@
     shared, width = trial_s.shape
     order = floor.shape[0]
     high_part, low_part = split(solved)
-    lifted = mm(basis[...], jnp.concatenate([high_part, low_part, high_part], axis=0))
-    alive = live(size[0], 0, order, width)
-    first = settle(trial_s[...] + lifted[:shared], floor[:shared], alive[:shared])
-    rest = settle(trial_n[...] + lifted[shared:], floor[shared:], alive[shared:])
-    mult_s[...] = first
-    mult_n[...] = rest
-    value = product((high[...], low[...]), split(jnp.concatenate([first, rest], axis=0)))
+    solved = jnp.concatenate([high_part, low_part, high_part], axis=0)
+    shared, width = trial_s.shape
+    value = jnp.zeros((shared, width), F32)
+    for at in range(0, floor.shape[0], shared):
+        here = slice(at, at + shared)
+        trial = trial_s[...] if at == 0 else trial_n[at - shared:at, :]
+        alive = live(size[0], at, shared, width)
+        mult = settle(trial + mm(basis[here, :], solved), floor[here, :], alive)
+        if at == 0:
+            mult_s[...] = mult
+        else:
+            mult_n[at - shared:at, :] = mult
+        value = value + product((high[:, here], low[:, here]), split(mult))
     image[...] = value
     send(cap, pack[...], value, sends)
 
@@ -334,10 +350,9 @@
     return [swap(blocks[d - 1], axis, count, d) for d in times]
 
 
-def half_first(count, back):
+def half_first(count):
     half = count // 2
-    others = [d for d in range(1, count) if d != half]
-    return (half, *(others[::-1] if back else others))
+    return (half, *(d for d in range(count - 1, 0, -1) if d != half))
 
 
 def middle_first(count):
@@ -375,21 +390,18 @@
     listed = n * cap
     padded = -(-listed // 128) * 128
     size = interface_size
-    coarse_order, part_order = far_first(wide), far_first(narrow)
-    half, half_back, middle = half_first(wide, False), half_first(wide, True), middle_first(wide)
-    orders = ((half_back, half, middle), (half_back, half, half_back))
+    part_order = far_first(narrow)
+    half_back, middle = half_first(wide), middle_first(wide)
+    orders = ((middle, half_back, half_back), (half_back, far_first(wide), half_back))
     sent = [shape(cap, loads)] * n
     full = 2 * order * loads
 
     list_rows = -(-(-(-cap // loads)) // 8) * 8
-    unpack_own, unpack_all, unpack, top_high, top_low, image, *sends = call(
+    pairs = peer_list[0].reshape(1, shared), partner_row
+    top_high, top_low, image, *sends = call(
         functools.partial(first_kernel, n, cap),
-        tuple(
-            pltpu.with_memory_space_constraint(value, pltpu.HBM)
-            for value in (peer_list[0].reshape(1, shared), partner_row, operator, mult)
-        ),
-        [shape(shared, shared, BF16), shape(shared, n * shared, BF16), shape(shared, padded, BF16)]
-        + [shape(shared, order, BF16)] * 2
+        tuple(pltpu.with_memory_space_constraint(value, pltpu.HBM) for value in (*pairs, operator, mult)),
+        [shape(shared, order, BF16)] * 2
         + [shape(shared, loads)]
         + [shape(shared + list_rows, loads)] * n,
         in_specs=[HBM] * 4,
@@ -403,6 +415,14 @@
         flops=3 * full * shared,
         moved=8 * shared * order,
         name="first",
+    )
+    unpack_own, unpack_all, unpack = call(
+        functools.partial(marks_kernel, cap),
+        pairs,
+        [shape(shared, shared, BF16), shape(shared, n * shared, BF16), shape(shared, padded, BF16)],
+        flops=8 * shared * shared * wide,
+        moved=2 * shared * shared * wide,
+        name="marks",
     )
     floor, basis, tile_high, tile_low = call(
         prepare_kernel,
@@ -474,6 +494,7 @@
             moved=2 * shared * unpack.shape[1],
             name="coarse",
         )
+        coarse_order = half_back if outer == 0 else far_first(wide)
         blocks = [own] + swap_all(coarse, "wide", wide, coarse_order)
         own, *parts = call(
             functools.partial(tile_kernel, coarse_order, part_order),

time: 90.5 us -> 91.7 us (1.013)
  starting transfers between devices: 39.3 us -> 36.3 us
  waiting for transfers between devices: 30.2 us -> 31.7 us
  local copies, waits for them, and re-layouts: 0.03 us -> 1.38 us
  Pallas kernels: 19.3 us -> 20.5 us
    ppermute x30, starting transfers between devices: 39.3 us -> 36.3 us  [swap(): return lax.ppermute(block, axis, [(i, i ^ d) for i in range(count)])]
    ppermute x30, waiting for transfers between devices: 30.2 us -> 31.7 us  [swap(): return lax.ppermute(block, axis, [(i, i ^ d) for i in range(count)])]
    unnamed x12 -> x16, local copies, waits for them, and re-layouts: 0.03 us -> 1.38 us
    pallas_call x25 -> x26, Pallas kernels: 19.3 us -> 20.5 us  [call(): pl.pallas_call(body, out_shape=outs, grid=grid, in_specs=in_specs, out_sp...]
  transfers between devices with their start and end apart: 30 -> 30, of which waited for: 24 -> 22; matrix products, arithmetic and copies ran while one was open for 0% -> 0% of each run, Pallas kernels for 13% -> 13%
where the time goes in v8:
time: 91.7 us; the launch traced here: 91.5 us
  starting transfers between devices  36.3 us (40%)
  waiting for transfers between devices  31.7 us (35%)
  Pallas kernels  20.5 us (22%)
  between operations  1.61 us (2%)
  local copies, waits for them, and re-layouts  1.38 us (2%)
    ppermute x30, starting transfers between devices, swap(): return lax.ppermute(block, axis, [(i, i ^ d) for i in range(count)])  36.3 us
    ppermute x30, waiting for transfers between devices, swap(): return lax.ppermute(block, axis, [(i, i ^ d) for i in range(count)])  31.7 us
    pallas_call x26, Pallas kernels, call(): pl.pallas_call(body, out_shape=outs, grid=grid, in_specs=in_specs, out_sp...  20.5 us
  transfers between devices with their start and end apart: 30, of which 22 were waited for; matrix products, arithmetic and copies ran while one was open for 0% of the time, Pallas kernels for 13%

profile of v8, /device:TPU:0, one launch (start us, length us, event | category | flops | bytes accessed | tf_op | source)
XLA Modules:
  0.0 91.5 jit_solution(12700463646390140854)
XLA Ops:
  0.7 2.1 %first.1 = (bf16[256,1024]{1,0:T(8,128)(2,1)S(1)}, bf16[256,1024]{1,0:T(8,128)(2,1)S(1)}, f32[256,128]{1,0:T(8,128)S(1)}, f32[264,128]{1,0:T(8,128)S(1)}, f32[26...) custom-call(s32[1,256]{1,0:T(1,128)} %bitcast.30, s32[1,256]{1,0:T(1,128)} %rows.1, f32[1024,1024]{1,0:T(8,128)} %bitcast.19, ...), custom_call_target="tpu_custom_call" | custom-call | flops 201326592 | bytes 2097152 | tf_op jit(solution)/shard_map/first/pallas_call | solution.py:49
  2.7 5.1 %collective-permute-start = (f32[264,128]{1,0:T(8,128)S(1)}, f32[264,128]{1,0:T(8,128)S(1)}, u32[]{:S(2)}, u32[]{:S(2)}) collective-permute-start(f32[264,128]{1,0:T(8,128)S(1)} %get-tuple-element.81), channel_id=1, source_target_pairs={{0,12},{4,8},{8,4},{12,0},{1,13},{5,9},{9,5},{13,1},{2,14},{6,10},... | collective-permute-start | bytes 405512 | tf_op jit(solution)/shard_map/ppermute | solution.py:342
  7.9 0.6 collective-permute-start.2
  9.2 0.7 copy-done.6
  9.8 0.7 copy-done.7
  10.5 0.4 marks.1
  11.1 2.0 %rest_start.1 = (f32[768,128]{1,0:T(8,128)S(1)}, f32[64,128]{1,0:T(8,128)S(1)}, bf16[768,1024]{1,0:T(8,128)(2,1)S(1)}, bf16[768,1024]{1,0:T(8,128)(2,1)S(1)}) custom-call(s32[1]{0:T(128)S(6)} %copy.15.size, f32[1024,1024]{1,0:T(8,128)S(1)} %bitcast.20, f32[1024,128]{1,0:T(8,128)S(1)} %bitcast.22, f32[1024,128]{1,0:T(8,128)S(1)} %bitcast.23, ...), custom_call_target="tpu_custom_call" | custom-call | flops 603979776 | bytes 6291456 | tf_op jit(solution)/shard_map/rest_start/pallas_call | solution.py:49
  13.2 2.3 %collective-permute-done.1.refs_1_ = f32[264,128]{1,0:T(8,128)S(1)} collective-permute-done((f32[264,128]{1,0:T(8,128)S(1)}, f32[264,128]{1,0:T(8,128)S(1)}, u32[]{:S(2)}, u32[]{:S(2)}) %collective-permute-start.1) | collective-permute-done | bytes 135200 | tf_op jit(solution)/shard_map/ppermute | solution.py:342
  15.4 3.9 %collective-permute-done.2.refs_2_ = f32[264,128]{1,0:T(8,128)S(1)} collective-permute-done((f32[264,128]{1,0:T(8,128)S(1)}, f32[264,128]{1,0:T(8,128)S(1)}, u32[]{:S(2)}, u32[]{:S(2)}) %collective-permute-start.2) | collective-permute-done | bytes 135200 | tf_op jit(solution)/shard_map/ppermute | solution.py:342
  19.3 0.5 coarse.2
  19.7 0.8 collective-permute-start.3
  20.5 1.8 %collective-permute-start.4 = (f32[64,128]{1,0:T(8,128)S(1)}, f32[64,128]{1,0:T(8,128)S(1)}, u32[]{:S(2)}, u32[]{:S(2)}) collective-permute-start(f32[64,128]{1,0:T(8,128)S(1)} %get-tuple-element.90), channel_id=1, source_target_pairs={{0,12},{4,8},{8,4},{12,0},{1,13},{5,9},{9,5},{13,1},{2,14},{6,10},... | collective-permute-start | bytes 98312 | tf_op jit(solution)/shard_map/ppermute | solution.py:342
  22.4 0.9 %collective-permute-start.5 = (f32[64,128]{1,0:T(8,128)S(1)}, f32[64,128]{1,0:T(8,128)S(1)}, u32[]{:S(2)}, u32[]{:S(2)}) collective-permute-start(f32[64,128]{1,0:T(8,128)S(1)} %get-tuple-element.91), channel_id=1, source_target_pairs={{0,4},{4,0},{8,12},{12,8},{1,5},{5,1},{9,13},{13,9},{2,6},{6,2},{1... | collective-permute-start | bytes 98312 | tf_op jit(solution)/shard_map/ppermute | solution.py:342
  23.3 0.4 prepare.1
  23.7 1.1 %collective-permute-done.3.refs_1_ = f32[64,128]{1,0:T(8,128)S(1)} collective-permute-done((f32[64,128]{1,0:T(8,128)S(1)}, f32[64,128]{1,0:T(8,128)S(1)}, u32[]{:S(2)}, u32[]{:S(2)}) %collective-permute-start.3) | collective-permute-done | bytes 32800 | tf_op jit(solution)/shard_map/ppermute | solution.py:342
  24.8 1.7 %collective-permute-done.4.refs_2_ = f32[64,128]{1,0:T(8,128)S(1)} collective-permute-done((f32[64,128]{1,0:T(8,128)S(1)}, f32[64,128]{1,0:T(8,128)S(1)}, u32[]{:S(2)}, u32[]{:S(2)}) %collective-permute-start.4) | collective-permute-done | bytes 32800 | tf_op jit(solution)/shard_map/ppermute | solution.py:342
  26.6 0.3 tile.4
  27.0 1.6 %collective-permute-start.7 = (f32[64,128]{1,0:T(8,128)S(1)}, f32[64,128]{1,0:T(8,128)S(1)}, u32[]{:S(2)}, u32[]{:S(2)}) collective-permute-start(f32[64,128]{1,0:T(8,128)S(1)} %get-tuple-element.94), channel_id=1, source_target_pairs={{0,2},{1,3},{2,0},{3,1},{4,6},{5,7},{6,4},{7,5},{8,10},{9,11},{10,... | collective-permute-start | bytes 98312 | tf_op jit(solution)/shard_map/ppermute | solution.py:342
  28.5 0.3 collective-permute-start.8
  28.8 0.3 pack.1
  29.1 1.5 %collective-permute-done.6.refs_1_ = f32[64,128]{1,0:T(8,128)S(1)} collective-permute-done((f32[64,128]{1,0:T(8,128)S(1)}, f32[64,128]{1,0:T(8,128)S(1)}, u32[]{:S(2)}, u32[]{:S(2)}) %collective-permute-start.6) | collective-permute-done | bytes 32800 | tf_op jit(solution)/shard_map/ppermute | solution.py:342
  30.6 0.4 collective-permute-done.7.refs_2_
  31.0 1.4 %lift.2 = (f32[256,128]{1,0:T(8,128)S(1)}, f32[768,128]{1,0:T(8,128)S(1)}, f32[256,128]{1,0:T(8,128)S(1)}, f32[128,128]{1,0:T(8,128)S(1)}, f32[128,128]{1,0:T(8,128)S(1)}, /*index=5*/f32[128,128]{1,0:T(8,128)S(1)}) custom-call(s32[1]{0:T(128)S(6)} %copy.15.size, f32[64,128]{1,0:T(8,128)S(1)} %get-tuple-element.92.refs_0_, ...), custom_call_target="tpu_custom_call" | custom-call | flops 201326592 | bytes 1048576 | tf_op jit(solution)/shard_map/lift/pallas_call | solution.py:49
  32.4 1.7 %collective-permute-start.9 = (f32[128,128]{1,0:T(8,128)S(1)}, f32[128,128]{1,0:T(8,128)S(1)}, u32[]{:S(2)}, u32[]{:S(2)}) collective-permute-start(f32[128,128]{1,0:T(8,128)S(1)} %get-tuple-element.103), channel_id=1, source_target_pairs={{0,8},{4,12},{8,0},{12,4},{1,9},{5,13},{9,1},{13,5},{2,10},{6,14},... | collective-permute-start | bytes 196616 | tf_op jit(solution)/shard_map/ppermute | solution.py:342
  34.1 1.3 %collective-permute-start.10 = (f32[128,128]{1,0:T(8,128)S(1)}, f32[128,128]{1,0:T(8,128)S(1)}, u32[]{:S(2)}, u32[]{:S(2)}) collective-permute-start(f32[128,128]{1,0:T(8,128)S(1)} %get-tuple-element.104), channel_id=1, source_target_pairs={{0,12},{4,8},{8,4},{12,0},{1,13},{5,9},{9,5},{13,1},{2,14},{6,10},... | collective-permute-start | bytes 196616 | tf_op jit(solution)/shard_map/ppermute | solution.py:342
  35.5 0.5 collective-permute-start.11
  36.2 1.5 %rest.3 = (f32[768,128]{1,0:T(8,128)S(1)}, f32[640,128]{1,0:T(8,128)S(1)}) custom-call(s32[1]{0:T(128)S(6)} %copy.15.size, bf16[768,1024]{1,0:T(8,128)(2,1)S(1)} %get-tuple-element.111.high, bf16[768,1024]{1,0:T(8,128)(2,1)S(1)} %get-tuple-element.112.low, f32[256,128]{1,0:T(8,128)S(1)} %get-tuple-element.108.mult_s.refs_5_, ...), custom_call_target="tpu_custom_call" | custom-call | flops 805306368 | bytes 4194304 | tf_op jit(solution)/shard_map/rest/pallas_call | solution.py:49
  37.7 3.0 %collective-permute-done.9.refs_0_ = f32[128,128]{1,0:T(8,128)S(1)} collective-permute-done((f32[128,128]{1,0:T(8,128)S(1)}, f32[128,128]{1,0:T(8,128)S(1)}, u32[]{:S(2)}, u32[]{:S(2)}) %collective-permute-start.9) | collective-permute-done | bytes 65568 | tf_op jit(solution)/shard_map/ppermute | solution.py:342
  40.7 1.2 %collective-permute-done.11.refs_2_ = f32[128,128]{1,0:T(8,128)S(1)} collective-permute-done((f32[128,128]{1,0:T(8,128)S(1)}, f32[128,128]{1,0:T(8,128)S(1)}, u32[]{:S(2)}, u32[]{:S(2)}) %collective-permute-start.11) | collective-permute-done | bytes 65568 | tf_op jit(solution)/shard_map/ppermute | solution.py:342
  41.9 0.5 sweep.3
  42.4 1.0 %collective-permute-start.12 = (f32[128,128]{1,0:T(8,128)S(1)}, f32[128,128]{1,0:T(8,128)S(1)}, u32[]{:S(2)}, u32[]{:S(2)}) collective-permute-start(f32[128,128]{1,0:T(8,128)S(1)} %get-tuple-element.115), channel_id=1, source_target_pairs={{0,8},{4,12},{8,0},{12,4},{1,9},{5,13},{9,1},{13,5},{2,10},{6,14},... | collective-permute-start | bytes 196616 | tf_op jit(solution)/shard_map/ppermute | solution.py:342
  43.5 2.1 %collective-permute-start.13 = (f32[128,128]{1,0:T(8,128)S(1)}, f32[128,128]{1,0:T(8,128)S(1)}, u32[]{:S(2)}, u32[]{:S(2)}) collective-permute-start(f32[128,128]{1,0:T(8,128)S(1)} %get-tuple-element.116), channel_id=1, source_target_pairs={{0,12},{4,8},{8,4},{12,0},{1,13},{5,9},{9,5},{13,1},{2,14},{6,10},... | collective-permute-start | bytes 196616 | tf_op jit(solution)/shard_map/ppermute | solution.py:342
  45.5 0.5 collective-permute-start.14
  46.2 1.5 %rest.4 = (f32[768,128]{1,0:T(8,128)S(1)}, f32[640,128]{1,0:T(8,128)S(1)}) custom-call(s32[1]{0:T(128)S(6)} %copy.15.size, bf16[768,1024]{1,0:T(8,128)(2,1)S(1)} %get-tuple-element.111.high, bf16[768,1024]{1,0:T(8,128)(2,1)S(1)} %get-tuple-element.112.low, f32[256,128]{1,0:T(8,128)S(1)} %get-tuple-element.119.mult_s.refs_5_, ...), custom_call_target="tpu_custom_call" | custom-call | flops 805306368 | bytes 4194304 | tf_op jit(solution)/shard_map/rest/pallas_call | solution.py:49
  47.7 2.8 %collective-permute-done.12.refs_0_ = f32[128,128]{1,0:T(8,128)S(1)} collective-permute-done((f32[128,128]{1,0:T(8,128)S(1)}, f32[128,128]{1,0:T(8,128)S(1)}, u32[]{:S(2)}, u32[]{:S(2)}) %collective-permute-start.12) | collective-permute-done | bytes 65568 | tf_op jit(solution)/shard_map/ppermute | solution.py:342
  50.5 0.6 collective-permute-done.14.refs_2_
  51.1 0.5 sweep.4
  51.7 1.0 %collective-permute-start.15 = (f32[128,128]{1,0:T(8,128)S(1)}, f32[128,128]{1,0:T(8,128)S(1)}, u32[]{:S(2)}, u32[]{:S(2)}) collective-permute-start(f32[128,128]{1,0:T(8,128)S(1)} %get-tuple-element.122), channel_id=1, source_target_pairs={{0,8},{4,12},{8,0},{12,4},{1,9},{5,13},{9,1},{13,5},{2,10},{6,14},... | collective-permute-start | bytes 196616 | tf_op jit(solution)/shard_map/ppermute | solution.py:342
  52.7 2.5 %collective-permute-start.16 = (f32[128,128]{1,0:T(8,128)S(1)}, f32[128,128]{1,0:T(8,128)S(1)}, u32[]{:S(2)}, u32[]{:S(2)}) collective-permute-start(f32[128,128]{1,0:T(8,128)S(1)} %get-tuple-element.123), channel_id=1, source_target_pairs={{0,12},{4,8},{8,4},{12,0},{1,13},{5,9},{9,5},{13,1},{2,14},{6,10},... | collective-permute-start | bytes 196616 | tf_op jit(solution)/shard_map/ppermute | solution.py:342
  55.4 1.1 %rest_first.1 = (f32[768,128]{1,0:T(8,128)S(1)}, f32[64,128]{1,0:T(8,128)S(1)}) custom-call(s32[1]{0:T(128)S(6)} %copy.15.size, bf16[768,1024]{1,0:T(8,128)(2,1)S(1)} %get-tuple-element.111.high, bf16[768,1024]{1,0:T(8,128)(2,1)S(1)} %get-tuple-element.112.low, f32[256,128]{1,0:T(8,128)S(1)} %get-tuple-element.126.mult_s.refs_5_, ...), custom_call_target="tpu_custom_call" | custom-call | flops 603979776 | bytes 3145728 | tf_op jit(solution)/shard_map/rest_first/pallas_call | solution.py:49
  56.6 3.1 %collective-permute-done.15.refs_0_ = f32[128,128]{1,0:T(8,128)S(1)} collective-permute-done((f32[128,128]{1,0:T(8,128)S(1)}, f32[128,128]{1,0:T(8,128)S(1)}, u32[]{:S(2)}, u32[]{:S(2)}) %collective-permute-start.15) | collective-permute-done | bytes 65568 | tf_op jit(solution)/shard_map/ppermute | solution.py:342
  59.7 0.6 collective-permute-done.17.refs_2_
  60.2 0.4 coarse.3
  60.7 1.4 %collective-permute-start.18 = (f32[64,128]{1,0:T(8,128)S(1)}, f32[64,128]{1,0:T(8,128)S(1)}, u32[]{:S(2)}, u32[]{:S(2)}) collective-permute-start(f32[64,128]{1,0:T(8,128)S(1)} %get-tuple-element.130), channel_id=1, source_target_pairs={{0,12},{4,8},{8,4},{12,0},{1,13},{5,9},{9,5},{13,1},{2,14},{6,10},... | collective-permute-start | bytes 98312 | tf_op jit(solution)/shard_map/ppermute | solution.py:342
  62.1 0.8 collective-permute-start.19
  62.9 2.2 %collective-permute-start.20 = (f32[64,128]{1,0:T(8,128)S(1)}, f32[64,128]{1,0:T(8,128)S(1)}, u32[]{:S(2)}, u32[]{:S(2)}) collective-permute-start(f32[64,128]{1,0:T(8,128)S(1)} %get-tuple-element.132), channel_id=1, source_target_pairs={{0,4},{4,0},{8,12},{12,8},{1,5},{5,1},{9,13},{13,9},{2,6},{6,2},{1... | collective-permute-start | bytes 98312 | tf_op jit(solution)/shard_map/ppermute | solution.py:342
  65.1 1.3 %collective-permute-done.18.refs_1_ = f32[64,128]{1,0:T(8,128)S(1)} collective-permute-done((f32[64,128]{1,0:T(8,128)S(1)}, f32[64,128]{1,0:T(8,128)S(1)}, u32[]{:S(2)}, u32[]{:S(2)}) %collective-permute-start.18) | collective-permute-done | bytes 32800 | tf_op jit(solution)/shard_map/ppermute | solution.py:342
  66.4 0.8 collective-permute-done.19.refs_2_
  67.8 1.8 %collective-permute-start.23 = (f32[64,128]{1,0:T(8,128)S(1)}, f32[64,128]{1,0:T(8,128)S(1)}, u32[]{:S(2)}, u32[]{:S(2)}) collective-permute-start(f32[64,128]{1,0:T(8,128)S(1)} %get-tuple-element.136), channel_id=1, source_target_pairs={{0,1},{1,0},{2,3},{3,2},{4,5},{5,4},{6,7},{7,6},{8,9},{9,8},{10,11... | collective-permute-start | bytes 98312 | tf_op jit(solution)/shard_map/ppermute | solution.py:342
  69.5 1.5 %collective-permute-done.21.refs_1_ = f32[64,128]{1,0:T(8,128)S(1)} collective-permute-done((f32[64,128]{1,0:T(8,128)S(1)}, f32[64,128]{1,0:T(8,128)S(1)}, u32[]{:S(2)}, u32[]{:S(2)}) %collective-permute-start.21) | collective-permute-done | bytes 32800 | tf_op jit(solution)/shard_map/ppermute | solution.py:342
  71.0 0.7 collective-permute-done.22.refs_2_
  71.7 1.4 %lift.3 = (f32[256,128]{1,0:T(8,128)S(1)}, f32[768,128]{1,0:T(8,128)S(1)}, f32[256,128]{1,0:T(8,128)S(1)}, f32[128,128]{1,0:T(8,128)S(1)}, f32[128,128]{1,0:T(8,128)S(1)}, /*index=5*/f32[128,128]{1,0:T(8,128)S(1)}) custom-call(s32[1]{0:T(128)S(6)} %copy.15.size, f32[64,128]{1,0:T(8,128)S(1)} %get-tuple-element.133.refs_0_, ...), custom_call_target="tpu_custom_call" | custom-call | flops 201326592 | bytes 1048576 | tf_op jit(solution)/shard_map/lift/pallas_call | solution.py:49
  73.2 2.1 %collective-permute-start.24 = (f32[128,128]{1,0:T(8,128)S(1)}, f32[128,128]{1,0:T(8,128)S(1)}, u32[]{:S(2)}, u32[]{:S(2)}) collective-permute-start(f32[128,128]{1,0:T(8,128)S(1)} %get-tuple-element.139), channel_id=1, source_target_pairs={{0,12},{4,8},{8,4},{12,0},{1,13},{5,9},{9,5},{13,1},{2,14},{6,10},... | collective-permute-start | bytes 196616 | tf_op jit(solution)/shard_map/ppermute | solution.py:342
  75.3 1.1 %collective-permute-start.25 = (f32[128,128]{1,0:T(8,128)S(1)}, f32[128,128]{1,0:T(8,128)S(1)}, u32[]{:S(2)}, u32[]{:S(2)}) collective-permute-start(f32[128,128]{1,0:T(8,128)S(1)} %get-tuple-element.140), channel_id=1, source_target_pairs={{0,8},{4,12},{8,0},{12,4},{1,9},{5,13},{9,1},{13,5},{2,10},{6,14},... | collective-permute-start | bytes 196616 | tf_op jit(solution)/shard_map/ppermute | solution.py:342
  76.4 1.2 %collective-permute-start.26 = (f32[128,128]{1,0:T(8,128)S(1)}, f32[128,128]{1,0:T(8,128)S(1)}, u32[]{:S(2)}, u32[]{:S(2)}) collective-permute-start(f32[128,128]{1,0:T(8,128)S(1)} %get-tuple-element.141), channel_id=1, source_target_pairs={{0,4},{4,0},{8,12},{12,8},{1,5},{5,1},{9,13},{13,9},{2,6},{6,2},{1... | collective-permute-start | bytes 196616 | tf_op jit(solution)/shard_map/ppermute | solution.py:342
  77.8 1.5 %rest.5 = (f32[768,128]{1,0:T(8,128)S(1)}, f32[640,128]{1,0:T(8,128)S(1)}) custom-call(s32[1]{0:T(128)S(6)} %copy.15.size, bf16[768,1024]{1,0:T(8,128)(2,1)S(1)} %get-tuple-element.111.high, bf16[768,1024]{1,0:T(8,128)(2,1)S(1)} %get-tuple-element.112.low, f32[256,128]{1,0:T(8,128)S(1)} %get-tuple-element.143.mult_s.refs_5_, ...), custom_call_target="tpu_custom_call" | custom-call | flops 805306368 | bytes 4194304 | tf_op jit(solution)/shard_map/rest/pallas_call | solution.py:49
  79.3 0.4 collective-permute-done.24.refs_0_
  79.8 2.7 %collective-permute-done.25.refs_1_ = f32[128,128]{1,0:T(8,128)S(1)} collective-permute-done((f32[128,128]{1,0:T(8,128)S(1)}, f32[128,128]{1,0:T(8,128)S(1)}, u32[]{:S(2)}, u32[]{:S(2)}) %collective-permute-start.25) | collective-permute-done | bytes 65568 | tf_op jit(solution)/shard_map/ppermute | solution.py:342
  82.4 0.5 sweep.5
  83.0 2.2 %collective-permute-start.28 = (f32[128,128]{1,0:T(8,128)S(1)}, f32[128,128]{1,0:T(8,128)S(1)}, u32[]{:S(2)}, u32[]{:S(2)}) collective-permute-start(f32[128,128]{1,0:T(8,128)S(1)} %get-tuple-element.147), channel_id=1, source_target_pairs={{0,12},{4,8},{8,4},{12,0},{1,13},{5,9},{9,5},{13,1},{2,14},{6,10},... | collective-permute-start | bytes 196616 | tf_op jit(solution)/shard_map/ppermute | solution.py:342
  85.2 1.3 %collective-permute-start.29 = (f32[128,128]{1,0:T(8,128)S(1)}, f32[128,128]{1,0:T(8,128)S(1)}, u32[]{:S(2)}, u32[]{:S(2)}) collective-permute-start(f32[128,128]{1,0:T(8,128)S(1)} %get-tuple-element.148), channel_id=1, source_target_pairs={{0,4},{4,0},{8,12},{12,8},{1,5},{5,1},{9,13},{13,9},{2,6},{6,2},{1... | collective-permute-start | bytes 196616 | tf_op jit(solution)/shard_map/ppermute | solution.py:342
  86.7 1.9 %rest_last.1 = (f32[1024,128]{1,0:T(8,128)}, f32[1024,128]{1,0:T(8,128)}) custom-call(s32[1]{0:T(128)S(6)} %copy.15.size, bf16[768,1024]{1,0:T(8,128)(2,1)S(1)} %get-tuple-element.111.high, bf16[768,1024]{1,0:T(8,128)(2,1)S(1)} %get-tuple-element.112.low, f32[256,128]{1,0:T(8,128)S(1)} %get-tuple-element.150.mult_s.refs_5_, ...), custom_call_target="tpu_custom_call" | custom-call | flops 603979776 | bytes 3145728 | tf_op jit(solution)/shard_map/rest_last/pallas_call | solution.py:49
  88.6 1.7 %collective-permute-done.27.refs_0_ = f32[128,128]{1,0:T(8,128)S(1)} collective-permute-done((f32[128,128]{1,0:T(8,128)S(1)}, f32[128,128]{1,0:T(8,128)S(1)}, u32[]{:S(2)}, u32[]{:S(2)}) %collective-permute-start.27) | collective-permute-done | bytes 65568 | tf_op jit(solution)/shard_map/ppermute | solution.py:342
  90.6 0.9 %last.1 = (f32[1024,128]{1,0:T(8,128)}, f32[1024,128]{1,0:T(8,128)}) custom-call(s32[1]{0:T(128)S(6)} %copy.15.size, f32[128,128]{1,0:T(8,128)S(1)} %collective-permute-done.27.refs_0_, f32[128,128]{1,0:T(8,128)S(1)} %collective-permute-done.28.refs_1_, ...), custom_call_target="tpu_custom_call", output_to_operand_aliasing={{0}: (8, {}), {1}: (9, {})} | custom-call | flops 75497472 | bytes 196608 | tf_op jit(solution)/shard_map/last/pallas_call | solution.py:49
  (38 shorter events, 2.3 us)
Async XLA Ops:
  0.6 10.3 %copy-start = (f32[1,1024,128]{2,1,0:T(8,128)S(1)}, f32[1,1024,128]{2,1,0:T(8,128)}, u32[]{:S(2)}) copy-start(f32[1,1024,128]{2,1,0:T(8,128)} %param.12) | copy-start | bytes 1572868
  0.6 10.5 %copy-start.1 = (f32[1,1024,1024]{2,1,0:T(8,128)S(1)}, f32[1,1024,1024]{2,1,0:T(8,128)}, u32[]{:S(2)}) copy-start(f32[1,1024,1024]{2,1,0:T(8,128)} %param.9) | copy-start | bytes 12582916
  0.7 10.5 %copy-start.2 = (f32[1,1024,128]{2,1,0:T(8,128)S(1)}, f32[1,1024,128]{2,1,0:T(8,128)}, u32[]{:S(2)}) copy-start(f32[1,1024,128]{2,1,0:T(8,128)} %param.13) | copy-start | bytes 1572868
  0.7 10.5 %copy-start.3 = (f32[1,64,1024]{2,1,0:T(8,128)S(1)}, f32[1,64,1024]{2,1,0:T(8,128)}, u32[]{:S(2)}) copy-start(f32[1,64,1024]{2,1,0:T(8,128)} %param.11) | copy-start | bytes 786436
  2.7 10.4 %collective-permute-start = (f32[264,128]{1,0:T(8,128)S(1)}, f32[264,128]{1,0:T(8,128)S(1)}, u32[]{:S(2)}, u32[]{:S(2)}) collective-permute-start(f32[264,128]{1,0:T(8,128)S(1)} %get-tuple-element.81), channel_id=1, source_target_pairs={{0,12},{4,8},{8,4},{12,0},{1,13},{5,9},{9,5},{13,1},{2,14},{6,10},... | collective-permute-start | bytes 405512 | tf_op jit(solution)/shard_map/ppermute | solution.py:342
  7.9 7.6 %collective-permute-start.1 = (f32[264,128]{1,0:T(8,128)S(1)}, f32[264,128]{1,0:T(8,128)S(1)}, u32[]{:S(2)}, u32[]{:S(2)}) collective-permute-start(f32[264,128]{1,0:T(8,128)S(1)} %get-tuple-element.82), channel_id=1, source_target_pairs={{0,4},{4,0},{8,12},{12,8},{1,5},{5,1},{9,13},{13,9},{2,6},{6,2},{1... | collective-permute-start | bytes 405512 | tf_op jit(solution)/shard_map/ppermute | solution.py:342
  7.9 11.4 %collective-permute-start.2 = (f32[264,128]{1,0:T(8,128)S(1)}, f32[264,128]{1,0:T(8,128)S(1)}, u32[]{:S(2)}, u32[]{:S(2)}) collective-permute-start(f32[264,128]{1,0:T(8,128)S(1)} %get-tuple-element.83), channel_id=1, source_target_pairs={{0,8},{4,12},{8,0},{12,4},{1,9},{5,13},{9,1},{13,5},{2,10},{6,14},... | collective-permute-start | bytes 405512 | tf_op jit(solution)/shard_map/ppermute | solution.py:342
  9.2 0.7 copy-start.6
  9.8 0.7 copy-start.7
  13.1 10.2 %copy-start.4 = (f32[256,256]{1,0:T(8,128)S(1)}, f32[256,256]{1,0:T(8,128)}, u32[]{:S(2)}) copy-start(f32[256,256]{1,0:T(8,128)} %tile.3) | copy-start | bytes 786436
  13.2 10.1 %copy-start.5 = (s32[1,1024]{1,0:T(1,128)S(1)}, s32[1,1024]{1,0:T(1,128)}, u32[]{:S(2)}) copy-start(s32[1,1024]{1,0:T(1,128)} %contact.1) | copy-start | bytes 12292
  19.7 5.0 %collective-permute-start.3 = (f32[64,128]{1,0:T(8,128)S(1)}, f32[64,128]{1,0:T(8,128)S(1)}, u32[]{:S(2)}, u32[]{:S(2)}) collective-permute-start(f32[64,128]{1,0:T(8,128)S(1)} %get-tuple-element.89), channel_id=1, source_target_pairs={{0,8},{4,12},{8,0},{12,4},{1,9},{5,13},{9,1},{13,5},{2,10},{6,14},... | collective-permute-start | bytes 98312 | tf_op jit(solution)/shard_map/ppermute | solution.py:342
  20.5 5.9 %collective-permute-start.4 = (f32[64,128]{1,0:T(8,128)S(1)}, f32[64,128]{1,0:T(8,128)S(1)}, u32[]{:S(2)}, u32[]{:S(2)}) collective-permute-start(f32[64,128]{1,0:T(8,128)S(1)} %get-tuple-element.90), channel_id=1, source_target_pairs={{0,12},{4,8},{8,4},{12,0},{1,13},{5,9},{9,5},{13,1},{2,14},{6,10},... | collective-permute-start | bytes 98312 | tf_op jit(solution)/shard_map/ppermute | solution.py:342
  22.4 4.3 %collective-permute-start.5 = (f32[64,128]{1,0:T(8,128)S(1)}, f32[64,128]{1,0:T(8,128)S(1)}, u32[]{:S(2)}, u32[]{:S(2)}) collective-permute-start(f32[64,128]{1,0:T(8,128)S(1)} %get-tuple-element.91), channel_id=1, source_target_pairs={{0,4},{4,0},{8,12},{12,8},{1,5},{5,1},{9,13},{13,9},{2,6},{6,2},{1... | collective-permute-start | bytes 98312 | tf_op jit(solution)/shard_map/ppermute | solution.py:342
  26.9 3.7 %collective-permute-start.6 = (f32[64,128]{1,0:T(8,128)S(1)}, f32[64,128]{1,0:T(8,128)S(1)}, u32[]{:S(2)}, u32[]{:S(2)}) collective-permute-start(f32[64,128]{1,0:T(8,128)S(1)} %get-tuple-element.93), channel_id=1, source_target_pairs={{0,3},{1,2},{2,1},{3,0},{4,7},{5,6},{6,5},{7,4},{8,11},{9,10},{10,... | collective-permute-start | bytes 98312 | tf_op jit(solution)/shard_map/ppermute | solution.py:342
  27.0 4.0 %collective-permute-start.7 = (f32[64,128]{1,0:T(8,128)S(1)}, f32[64,128]{1,0:T(8,128)S(1)}, u32[]{:S(2)}, u32[]{:S(2)}) collective-permute-start(f32[64,128]{1,0:T(8,128)S(1)} %get-tuple-element.94), channel_id=1, source_target_pairs={{0,2},{1,3},{2,0},{3,1},{4,6},{5,7},{6,4},{7,5},{8,10},{9,11},{10,... | collective-permute-start | bytes 98312 | tf_op jit(solution)/shard_map/ppermute | solution.py:342
  28.5 2.5 %collective-permute-start.8 = (f32[64,128]{1,0:T(8,128)S(1)}, f32[64,128]{1,0:T(8,128)S(1)}, u32[]{:S(2)}, u32[]{:S(2)}) collective-permute-start(f32[64,128]{1,0:T(8,128)S(1)} %get-tuple-element.95), channel_id=1, source_target_pairs={{0,1},{1,0},{2,3},{3,2},{4,5},{5,4},{6,7},{7,6},{8,9},{9,8},{10,11... | collective-permute-start | bytes 98312 | tf_op jit(solution)/shard_map/ppermute | solution.py:342
  32.4 8.3 %collective-permute-start.9 = (f32[128,128]{1,0:T(8,128)S(1)}, f32[128,128]{1,0:T(8,128)S(1)}, u32[]{:S(2)}, u32[]{:S(2)}) collective-permute-start(f32[128,128]{1,0:T(8,128)S(1)} %get-tuple-element.103), channel_id=1, source_target_pairs={{0,8},{4,12},{8,0},{12,4},{1,9},{5,13},{9,1},{13,5},{2,10},{6,14},... | collective-permute-start | bytes 196616 | tf_op jit(solution)/shard_map/ppermute | solution.py:342
  34.1 6.6 %collective-permute-start.10 = (f32[128,128]{1,0:T(8,128)S(1)}, f32[128,128]{1,0:T(8,128)S(1)}, u32[]{:S(2)}, u32[]{:S(2)}) collective-permute-start(f32[128,128]{1,0:T(8,128)S(1)} %get-tuple-element.104), channel_id=1, source_target_pairs={{0,12},{4,8},{8,4},{12,0},{1,13},{5,9},{9,5},{13,1},{2,14},{6,10},... | collective-permute-start | bytes 196616 | tf_op jit(solution)/shard_map/ppermute | solution.py:342
  35.5 6.4 %collective-permute-start.11 = (f32[128,128]{1,0:T(8,128)S(1)}, f32[128,128]{1,0:T(8,128)S(1)}, u32[]{:S(2)}, u32[]{:S(2)}) collective-permute-start(f32[128,128]{1,0:T(8,128)S(1)} %get-tuple-element.105), channel_id=1, source_target_pairs={{0,4},{4,0},{8,12},{12,8},{1,5},{5,1},{9,13},{13,9},{2,6},{6,2},{1... | collective-permute-start | bytes 196616 | tf_op jit(solution)/shard_map/ppermute | solution.py:342
  42.4 8.1 %collective-permute-start.12 = (f32[128,128]{1,0:T(8,128)S(1)}, f32[128,128]{1,0:T(8,128)S(1)}, u32[]{:S(2)}, u32[]{:S(2)}) collective-permute-start(f32[128,128]{1,0:T(8,128)S(1)} %get-tuple-element.115), channel_id=1, source_target_pairs={{0,8},{4,12},{8,0},{12,4},{1,9},{5,13},{9,1},{13,5},{2,10},{6,14},... | collective-permute-start | bytes 196616 | tf_op jit(solution)/shard_map/ppermute | solution.py:342
  43.5 7.1 %collective-permute-start.13 = (f32[128,128]{1,0:T(8,128)S(1)}, f32[128,128]{1,0:T(8,128)S(1)}, u32[]{:S(2)}, u32[]{:S(2)}) collective-permute-start(f32[128,128]{1,0:T(8,128)S(1)} %get-tuple-element.116), channel_id=1, source_target_pairs={{0,12},{4,8},{8,4},{12,0},{1,13},{5,9},{9,5},{13,1},{2,14},{6,10},... | collective-permute-start | bytes 196616 | tf_op jit(solution)/shard_map/ppermute | solution.py:342
  45.5 5.6 %collective-permute-start.14 = (f32[128,128]{1,0:T(8,128)S(1)}, f32[128,128]{1,0:T(8,128)S(1)}, u32[]{:S(2)}, u32[]{:S(2)}) collective-permute-start(f32[128,128]{1,0:T(8,128)S(1)} %get-tuple-element.117), channel_id=1, source_target_pairs={{0,4},{4,0},{8,12},{12,8},{1,5},{5,1},{9,13},{13,9},{2,6},{6,2},{1... | collective-permute-start | bytes 196616 | tf_op jit(solution)/shard_map/ppermute | solution.py:342
  51.7 8.0 %collective-permute-start.15 = (f32[128,128]{1,0:T(8,128)S(1)}, f32[128,128]{1,0:T(8,128)S(1)}, u32[]{:S(2)}, u32[]{:S(2)}) collective-permute-start(f32[128,128]{1,0:T(8,128)S(1)} %get-tuple-element.122), channel_id=1, source_target_pairs={{0,8},{4,12},{8,0},{12,4},{1,9},{5,13},{9,1},{13,5},{2,10},{6,14},... | collective-permute-start | bytes 196616 | tf_op jit(solution)/shard_map/ppermute | solution.py:342
  52.7 7.0 %collective-permute-start.16 = (f32[128,128]{1,0:T(8,128)S(1)}, f32[128,128]{1,0:T(8,128)S(1)}, u32[]{:S(2)}, u32[]{:S(2)}) collective-permute-start(f32[128,128]{1,0:T(8,128)S(1)} %get-tuple-element.123), channel_id=1, source_target_pairs={{0,12},{4,8},{8,4},{12,0},{1,13},{5,9},{9,5},{13,1},{2,14},{6,10},... | collective-permute-start | bytes 196616 | tf_op jit(solution)/shard_map/ppermute | solution.py:342
  55.2 5.1 %collective-permute-start.17 = (f32[128,128]{1,0:T(8,128)S(1)}, f32[128,128]{1,0:T(8,128)S(1)}, u32[]{:S(2)}, u32[]{:S(2)}) collective-permute-start(f32[128,128]{1,0:T(8,128)S(1)} %get-tuple-element.124), channel_id=1, source_target_pairs={{0,4},{4,0},{8,12},{12,8},{1,5},{5,1},{9,13},{13,9},{2,6},{6,2},{1... | collective-permute-start | bytes 196616 | tf_op jit(solution)/shard_map/ppermute | solution.py:342
  60.7 5.8 %collective-permute-start.18 = (f32[64,128]{1,0:T(8,128)S(1)}, f32[64,128]{1,0:T(8,128)S(1)}, u32[]{:S(2)}, u32[]{:S(2)}) collective-permute-start(f32[64,128]{1,0:T(8,128)S(1)} %get-tuple-element.130), channel_id=1, source_target_pairs={{0,12},{4,8},{8,4},{12,0},{1,13},{5,9},{9,5},{13,1},{2,14},{6,10},... | collective-permute-start | bytes 98312 | tf_op jit(solution)/shard_map/ppermute | solution.py:342
  62.1 5.2 %collective-permute-start.19 = (f32[64,128]{1,0:T(8,128)S(1)}, f32[64,128]{1,0:T(8,128)S(1)}, u32[]{:S(2)}, u32[]{:S(2)}) collective-permute-start(f32[64,128]{1,0:T(8,128)S(1)} %get-tuple-element.131), channel_id=1, source_target_pairs={{0,8},{4,12},{8,0},{12,4},{1,9},{5,13},{9,1},{13,5},{2,10},{6,14},... | collective-permute-start | bytes 98312 | tf_op jit(solution)/shard_map/ppermute | solution.py:342
  62.9 4.5 %collective-permute-start.20 = (f32[64,128]{1,0:T(8,128)S(1)}, f32[64,128]{1,0:T(8,128)S(1)}, u32[]{:S(2)}, u32[]{:S(2)}) collective-permute-start(f32[64,128]{1,0:T(8,128)S(1)} %get-tuple-element.132), channel_id=1, source_target_pairs={{0,4},{4,0},{8,12},{12,8},{1,5},{5,1},{9,13},{13,9},{2,6},{6,2},{1... | collective-permute-start | bytes 98312 | tf_op jit(solution)/shard_map/ppermute | solution.py:342
  67.6 3.4 %collective-permute-start.21 = (f32[64,128]{1,0:T(8,128)S(1)}, f32[64,128]{1,0:T(8,128)S(1)}, u32[]{:S(2)}, u32[]{:S(2)}) collective-permute-start(f32[64,128]{1,0:T(8,128)S(1)} %get-tuple-element.134), channel_id=1, source_target_pairs={{0,3},{1,2},{2,1},{3,0},{4,7},{5,6},{6,5},{7,4},{8,11},{9,10},{10,... | collective-permute-start | bytes 98312 | tf_op jit(solution)/shard_map/ppermute | solution.py:342
  67.7 4.0 %collective-permute-start.22 = (f32[64,128]{1,0:T(8,128)S(1)}, f32[64,128]{1,0:T(8,128)S(1)}, u32[]{:S(2)}, u32[]{:S(2)}) collective-permute-start(f32[64,128]{1,0:T(8,128)S(1)} %get-tuple-element.135), channel_id=1, source_target_pairs={{0,2},{1,3},{2,0},{3,1},{4,6},{5,7},{6,4},{7,5},{8,10},{9,11},{10,... | collective-permute-start | bytes 98312 | tf_op jit(solution)/shard_map/ppermute | solution.py:342
  67.8 4.0 %collective-permute-start.23 = (f32[64,128]{1,0:T(8,128)S(1)}, f32[64,128]{1,0:T(8,128)S(1)}, u32[]{:S(2)}, u32[]{:S(2)}) collective-permute-start(f32[64,128]{1,0:T(8,128)S(1)} %get-tuple-element.136), channel_id=1, source_target_pairs={{0,1},{1,0},{2,3},{3,2},{4,5},{5,4},{6,7},{7,6},{8,9},{9,8},{10,11... | collective-permute-start | bytes 98312 | tf_op jit(solution)/shard_map/ppermute | solution.py:342
  73.2 6.6 %collective-permute-start.24 = (f32[128,128]{1,0:T(8,128)S(1)}, f32[128,128]{1,0:T(8,128)S(1)}, u32[]{:S(2)}, u32[]{:S(2)}) collective-permute-start(f32[128,128]{1,0:T(8,128)S(1)} %get-tuple-element.139), channel_id=1, source_target_pairs={{0,12},{4,8},{8,4},{12,0},{1,13},{5,9},{9,5},{13,1},{2,14},{6,10},... | collective-permute-start | bytes 196616 | tf_op jit(solution)/shard_map/ppermute | solution.py:342
  75.3 7.2 %collective-permute-start.25 = (f32[128,128]{1,0:T(8,128)S(1)}, f32[128,128]{1,0:T(8,128)S(1)}, u32[]{:S(2)}, u32[]{:S(2)}) collective-permute-start(f32[128,128]{1,0:T(8,128)S(1)} %get-tuple-element.140), channel_id=1, source_target_pairs={{0,8},{4,12},{8,0},{12,4},{1,9},{5,13},{9,1},{13,5},{2,10},{6,14},... | collective-permute-start | bytes 196616 | tf_op jit(solution)/shard_map/ppermute | solution.py:342
  76.4 6.0 %collective-permute-start.26 = (f32[128,128]{1,0:T(8,128)S(1)}, f32[128,128]{1,0:T(8,128)S(1)}, u32[]{:S(2)}, u32[]{:S(2)}) collective-permute-start(f32[128,128]{1,0:T(8,128)S(1)} %get-tuple-element.141), channel_id=1, source_target_pairs={{0,4},{4,0},{8,12},{12,8},{1,5},{5,1},{9,13},{13,9},{2,6},{6,2},{1... | collective-permute-start | bytes 196616 | tf_op jit(solution)/shard_map/ppermute | solution.py:342
  83.0 7.3 %collective-permute-start.27 = (f32[128,128]{1,0:T(8,128)S(1)}, f32[128,128]{1,0:T(8,128)S(1)}, u32[]{:S(2)}, u32[]{:S(2)}) collective-permute-start(f32[128,128]{1,0:T(8,128)S(1)} %get-tuple-element.146), channel_id=1, source_target_pairs={{0,8},{4,12},{8,0},{12,4},{1,9},{5,13},{9,1},{13,5},{2,10},{6,14},... | collective-permute-start | bytes 196616 | tf_op jit(solution)/shard_map/ppermute | solution.py:342
  83.0 7.3 %collective-permute-start.28 = (f32[128,128]{1,0:T(8,128)S(1)}, f32[128,128]{1,0:T(8,128)S(1)}, u32[]{:S(2)}, u32[]{:S(2)}) collective-permute-start(f32[128,128]{1,0:T(8,128)S(1)} %get-tuple-element.147), channel_id=1, source_target_pairs={{0,12},{4,8},{8,4},{12,0},{1,13},{5,9},{9,5},{13,1},{2,14},{6,10},... | collective-permute-start | bytes 196616 | tf_op jit(solution)/shard_map/ppermute | solution.py:342
  85.2 5.3 %collective-permute-start.29 = (f32[128,128]{1,0:T(8,128)S(1)}, f32[128,128]{1,0:T(8,128)S(1)}, u32[]{:S(2)}, u32[]{:S(2)}) collective-permute-start(f32[128,128]{1,0:T(8,128)S(1)} %get-tuple-element.148), channel_id=1, source_target_pairs={{0,4},{4,0},{8,12},{12,8},{1,5},{5,1},{9,13},{13,9},{2,6},{6,2},{1... | collective-permute-start | bytes 196616 | tf_op jit(solution)/shard_map/ppermute | solution.py:342

commit v9 on v8

--- a/solution.py
+++ b/solution.py
@@ -24,11 +24,14 @@
     return jnp.dot(left, right, preferred_element_type=F32)
 
 
+def stack(value):
+    return jnp.concatenate(split(value), axis=0)
+
+
 def product(left, right):
-    (left_high, left_low), (right_high, right_low) = left, right
-    width = right_high.shape[1]
-    both = mm(left_high, jnp.concatenate([right_high, right_low], axis=1))
-    return both[:, :width] + (both[:, width:] + mm(left_low, right_high))
+    rows, width = left.shape[0] // 2, right.shape[1]
+    both = mm(left, jnp.concatenate(split(right), axis=1))
+    return both[:rows, :width] + (both[:rows, width:] + both[rows:, :width] + both[rows:, width:])
 
 
 def pick(chosen, value):
@@ -93,13 +96,16 @@
 
 
 def first_kernel(n, cap, peers_at, rows_at, operator_at, mult_at, *refs):
-    high, low, image = refs[:3]
-    sends, (peers, rows, operator, mult, done) = refs[3:3 + n], refs[3 + n:]
+    top, image = refs[:2]
+    sends, (peers, rows, operator, mult, done) = refs[2:2 + n], refs[2 + n:]
     shared, width = image.shape
+    order = mult.shape[0]
+    halves = [pl.ds(at, order // 2) for at in (0, order // 2)]
     copies = [
         pltpu.make_async_copy(source, target, done.at[i])
         for i, (source, target) in enumerate(
-            ((peers_at, peers), (rows_at, rows), (mult_at, mult), (operator_at.at[pl.ds(0, shared)], operator))
+            [(peers_at, peers), (rows_at, rows), (mult_at, mult)]
+            + [(operator_at.at[pl.ds(0, shared), half], operator.at[:, half]) for half in halves]
         )
     ]
     for copy in copies:
@@ -117,10 +123,12 @@
                 jnp.where(hit, wanted, 0.0), axis=0, keepdims=True
             )
     copies[2].wait()
-    copies[3].wait()
-    parts = split(operator[...])
-    high[...], low[...] = parts
-    value = product(parts, split(mult[...]))
+    value = jnp.zeros((shared, width), F32)
+    for copy, half in zip(copies[3:], halves):
+        copy.wait()
+        parts = stack(operator[:, half])
+        top[:, half] = parts
+        value = value + product(parts, mult[half, :])
     image[...] = value
     for out in sends:
         out[:shared, :] = value
@@ -140,7 +148,7 @@
 
 def pack_kernel(times, cap, *refs):
     n = len(times)
-    recvs, (high, low, pack, stack_high, stack_low) = refs[:n], refs[n:]
+    recvs, (top, pack, square) = refs[:n], refs[n:]
     shared = pack.shape[1]
     width = recvs[0].shape[1]
     column = lax.broadcasted_iota(jnp.int32, (width, shared), 1).astype(F32)
@@ -153,20 +161,21 @@
             size = min(width, cap - c * width)
             at = (d - 1) * cap + c * width
             pack[at:at + size, :] = chosen[:size]
-    for source, stack in ((high, stack_high), (low, stack_low)):
-        square = source[:, :shared]
-        stack[:shared, :] = square
-        stack[shared:, :] = mm(pack[...], square).astype(BF16)
-
-
-def prepare_kernel(contact, modes, tile, floor, basis, tile_high, tile_low):
+    half = square.shape[0] // 2
+    for i in range(2):
+        part = top[i * shared:(i + 1) * shared, :shared]
+        square[i * half:i * half + shared, :] = part
+        square[i * half + shared:(i + 1) * half, :] = mm(pack[...], part).astype(BF16)
+
+
+def prepare_kernel(contact, modes, tile, floor, basis, tile_parts):
     order, width = floor.shape
     for at in range(0, order, width):
         flag = jnp.broadcast_to(contact[:, at:at + width], (width, width)).T
         floor[at:at + width, :] = jnp.where(flag == 1, 0.0, -jnp.inf)
     high, low = [part.astype(F32) for part in split(modes[...])]
     basis[...] = jnp.concatenate([high, high, low], axis=0).T.astype(BF16)
-    tile_high[...], tile_low[...] = split(tile[...])
+    tile_parts[...] = stack(tile[...])
 
 
 def send(cap, chosen, image, sends):
@@ -198,7 +207,7 @@
     return jnp.where(alive, known + arrived(times, recvs, known.shape[0], unpack), 0.0), alive
 
 
-def rest_start_kernel(size, operator, mult, mult_block, gap, modes, trial, coarse, high, low, halves):
+def rest_start_kernel(size, operator, mult, mult_block, gap, modes, trial, coarse, parts, halves):
     step = pl.program_id(0)
     rows, width = gap.shape
 
@@ -207,43 +216,43 @@
         halves[:, :width], halves[:, width:] = split(mult[...])
         coarse[...] = jnp.zeros_like(coarse)
 
-    parts = split(operator[...])
-    high[...], low[...] = parts
-    both = mm(parts[0], halves[...])
-    image = both[:, :width] + (both[:, width:] + mm(parts[1], halves[:, :width]))
+    high, low = split(operator[...])
+    parts[0], parts[1] = high, low
+    both = mm(jnp.concatenate([high, low], axis=0), halves[...])
+    image = both[:rows, :width] + (both[:rows, width:] + both[rows:, :width] + both[rows:, width:])
     alive = live(size[0], (step + 1) * rows, rows, width)
     residual = jnp.where(alive, gap[...] - image, 0.0)
     trial[...] = mult_block[...] + STEP * residual
-    coarse[...] += product(split(modes[...]), split(residual))
-
-
-def rest_residual(size, high, low, mult_s, mult_n, gap):
+    coarse[...] += product(stack(modes[...]), residual)
+
+
+def rest_residual(size, parts, mult_s, mult_n, gap):
     shared, (rows, width) = mult_s.shape[0], mult_n.shape
     mult = jnp.concatenate([mult_s[...], mult_n[...]], axis=0)
-    image = product((high[...], low[...]), split(mult))
+    image = product(parts[...].reshape(2 * rows, parts.shape[2]), mult)
     alive = live(size[0], shared, rows, width)
     return jnp.where(alive, gap[shared:, :] - image, 0.0), alive
 
 
-def rest_first_kernel(size, high, low, mult_s, mult_n, gap, modes, trial, coarse):
-    residual, _ = rest_residual(size, high, low, mult_s, mult_n, gap)
+def rest_first_kernel(size, parts, mult_s, mult_n, gap, modes, trial, coarse):
+    residual, _ = rest_residual(size, parts, mult_s, mult_n, gap)
     trial[...] = mult_n[...] + STEP * residual
-    coarse[...] = product(split(modes[:, mult_s.shape[0]:]), split(residual))
-
-
-def rest_kernel(size, high, low, mult_s, mult_n, gap, floor, top_high, top_low, pack, mult_out, ahead):
+    coarse[...] = product(stack(modes[:, mult_s.shape[0]:]), residual)
+
+
+def rest_kernel(size, parts, mult_s, mult_n, gap, floor, top, pack, mult_out, ahead):
     shared = mult_s.shape[0]
-    residual, alive = rest_residual(size, high, low, mult_s, mult_n, gap)
+    residual, alive = rest_residual(size, parts, mult_s, mult_n, gap)
     mult = settle(mult_n[...] + STEP * residual, floor[shared:, :], alive)
     mult_out[...] = mult
-    value = product((top_high[:, shared:], top_low[:, shared:]), split(mult))
+    value = product(top[:, shared:], mult)
     ahead[:shared, :] = value
     ahead[shared:, :] = pick(pack[...], value)
 
 
-def rest_last_kernel(size, high, low, mult_s, mult_n, gap, floor, mult_out, residual_out, settled, left, done):
+def rest_last_kernel(size, parts, mult_s, mult_n, gap, floor, mult_out, residual_out, settled, left, done):
     shared, rows = mult_s.shape[0], mult_n.shape[0]
-    residual, alive = rest_residual(size, high, low, mult_s, mult_n, gap)
+    residual, alive = rest_residual(size, parts, mult_s, mult_n, gap)
     left[...] = residual
     settled[...] = settle(mult_n[...] + STEP * residual, floor[shared:, :], alive)
     copies = [
@@ -262,20 +271,20 @@
     base, unpack, mult, modes, started, trial = refs[n:n + 6]
     shared = base.shape[0]
     residual, _ = shared_residual(times, recvs, base, unpack, size)
-    coarse = started[...] + product(split(modes[:, :shared]), split(residual))
+    coarse = started[...] + product(stack(modes[:, :shared]), residual)
     for out in refs[n + 6:]:
         out[...] = coarse
     trial[...] = mult[:shared, :] + STEP * residual
 
 
-def tile_kernel(wide_order, narrow_order, high, low, *refs):
+def tile_kernel(wide_order, narrow_order, tile, *refs):
     n, m = len(wide_order), len(narrow_order)
     blocks, outs, (gathered, parts) = refs[:n + 1], refs[n + 1:n + m + 2], refs[n + m + 2:]
     count = blocks[0].shape[0]
     for d, ref in zip((0, *wide_order), blocks):
         at = pl.multiple_of((lax.axis_index("wide") ^ d) * count, count)
         gathered[pl.ds(at, count), :] = ref[...]
-    parts[...] = product((high[...], low[...]), split(gathered[...]))
+    parts[...] = product(tile[...], gathered[...])
     for d, out in zip((0, *narrow_order), outs):
         at = pl.multiple_of((lax.axis_index("narrow") ^ d) * count, count)
         out[...] = parts[pl.ds(at, count), :]
@@ -283,27 +292,22 @@
 
 def lift_kernel(n, m, cap, size, *refs):
     parts = refs[:m + 1]
-    ins, (mult_s, mult_n, image), sends = refs[m + 1:m + 8], refs[m + 8:m + 11], refs[m + 11:]
-    basis, trial_s, trial_n, floor, high, low, pack = ins
+    ins, (mult_s, mult_n, image), sends = refs[m + 1:m + 7], refs[m + 7:m + 10], refs[m + 10:]
+    basis, trial_s, trial_n, floor, top, pack = ins
     solved = parts[0][...]
     for part in parts[1:]:
         solved = solved + part[...]
     shared, width = trial_s.shape
     order = floor.shape[0]
-    high_part, low_part = split(solved)
-    solved = jnp.concatenate([high_part, low_part, high_part], axis=0)
+    high, low = split(solved)
+    lifted = mm(basis[...], jnp.concatenate([high, low, high], axis=0))
     shared, width = trial_s.shape
-    value = jnp.zeros((shared, width), F32)
-    for at in range(0, floor.shape[0], shared):
-        here = slice(at, at + shared)
-        trial = trial_s[...] if at == 0 else trial_n[at - shared:at, :]
-        alive = live(size[0], at, shared, width)
-        mult = settle(trial + mm(basis[here, :], solved), floor[here, :], alive)
-        if at == 0:
-            mult_s[...] = mult
-        else:
-            mult_n[at - shared:at, :] = mult
-        value = value + product((high[:, here], low[:, here]), split(mult))
+    alive = live(size[0], 0, floor.shape[0], width)
+    first = settle(trial_s[...] + lifted[:shared], floor[:shared, :], alive[:shared])
+    rest = settle(trial_n[...] + lifted[shared:], floor[shared:, :], alive[shared:])
+    mult_s[...] = first
+    mult_n[...] = rest
+    value = product(top[...], jnp.concatenate([first, rest], axis=0))
     image[...] = value
     send(cap, pack[...], value, sends)
 
@@ -311,14 +315,14 @@
 def sweep_kernel(times, cap, size, *refs):
     n = len(times)
     recvs = refs[:n]
-    base, unpack, mult, floor, high, low, ahead, mult_out, image_out = refs[n:n + 9]
+    base, unpack, mult, floor, square, ahead, mult_out, image_out = refs[n:n + 8]
     shared = base.shape[0]
     residual, alive = shared_residual(times, recvs, base, unpack, size)
     value = settle(mult[...] + STEP * residual, floor[:shared, :], alive)
     mult_out[...] = value
-    both = ahead[...] + product((high[...], low[...]), split(value))
+    both = ahead[...] + product(square[...], value)
     image_out[...] = both[:shared]
-    for d, out in enumerate(refs[n + 9:]):
+    for d, out in enumerate(refs[n + 8:]):
         out[...] = both[shared + d * cap:shared + (d + 1) * cap]
 
 
@@ -392,17 +396,16 @@
     size = interface_size
     part_order = far_first(narrow)
     half_back, middle = half_first(wide), middle_first(wide)
-    orders = ((middle, half_back, half_back), (half_back, far_first(wide), half_back))
+    orders = ((middle, half_back, middle), (half_back, half_back, half_back))
     sent = [shape(cap, loads)] * n
     full = 2 * order * loads
 
     list_rows = -(-(-(-cap // loads)) // 8) * 8
     pairs = peer_list[0].reshape(1, shared), partner_row
-    top_high, top_low, image, *sends = call(
+    top, image, *sends = call(
         functools.partial(first_kernel, n, cap),
         tuple(pltpu.with_memory_space_constraint(value, pltpu.HBM) for value in (*pairs, operator, mult)),
-        [shape(shared, order, BF16)] * 2
-        + [shape(shared, loads)]
+        [shape(2 * shared, order, BF16), shape(shared, loads)]
         + [shape(shared + list_rows, loads)] * n,
         in_specs=[HBM] * 4,
         scratch=[
@@ -410,7 +413,7 @@
             pltpu.VMEM((1, shared), jnp.int32),
             pltpu.VMEM((shared, order), F32),
             pltpu.VMEM((order, loads), F32),
-            pltpu.SemaphoreType.DMA((4,)),
+            pltpu.SemaphoreType.DMA((5,)),
         ],
         flops=3 * full * shared,
         moved=8 * shared * order,
@@ -424,10 +427,10 @@
         moved=2 * shared * shared * wide,
         name="marks",
     )
-    floor, basis, tile_high, tile_low = call(
+    floor, basis, tile_parts = call(
         prepare_kernel,
         (contact_rows, modes, coarse_inverse),
-        [shape(order, loads)] + [shape(order, 3 * count, BF16)] + [shape(*coarse_inverse.shape, BF16)] * 2,
+        [shape(order, loads)] + [shape(order, 3 * count, BF16)] + [shape(2 * narrow * count, wide * count, BF16)],
         flops=full * count,
         moved=8 * coarse_inverse.size + 4 * full,
         name="prepare",
@@ -446,12 +449,11 @@
             name="base",
         )[0]
         if outer == 0:
-            row_block, load_block = block((shared, order)), block((shared, loads))
             next_loads = block((shared, loads), 1)
-            trial_n, started, high, low = call(
+            trial_n, started, parts = call(
                 rest_start_kernel,
                 (size, operator, mult, mult, gap, modes),
-                [shape(rest, loads), shape(count, loads)] + [shape(rest, order, BF16)] * 2,
+                [shape(rest, loads), shape(count, loads), jax.ShapeDtypeStruct((2, rest, order), BF16)],
                 [
                     SMEM,
                     block((shared, order), 1),
@@ -460,7 +462,11 @@
                     next_loads,
                     block((count, shared), 1, across=True),
                 ],
-                [load_block, whole((count, loads)), row_block, row_block],
+                [
+                    block((shared, loads)),
+                    whole((count, loads)),
+                    pl.BlockSpec((2, shared, order), lambda i: (0, i, 0)),
+                ],
                 scratch=scratch,
                 grid=(steps,),
                 flops=3 * full * rest,
@@ -468,10 +474,10 @@
                 name="rest_start",
             )
             marks = unpack_all
-            pack, stack_high, stack_low = call(
+            pack, square = call(
                 functools.partial(pack_kernel, times, cap),
-                (*recvs, top_high, top_low),
-                [shape(padded, shared, BF16)] + [shape(shared + padded, shared, BF16)] * 2,
+                (*recvs, top),
+                [shape(padded, shared, BF16), shape(2 * (shared + padded), shared, BF16)],
                 flops=8 * padded * shared * shared,
                 moved=8 * padded * shared,
                 name="pack",
@@ -479,7 +485,7 @@
         else:
             trial_n, started = call(
                 rest_first_kernel,
-                (size, high, low, mult_s, mult_n, gap, modes),
+                (size, parts, mult_s, mult_n, gap, modes),
                 [shape(rest, loads), shape(count, loads)],
                 flops=3 * full * rest,
                 moved=4 * rest * order,
@@ -496,9 +502,9 @@
         )
         coarse_order = half_back if outer == 0 else far_first(wide)
         blocks = [own] + swap_all(coarse, "wide", wide, coarse_order)
-        own, *parts = call(
+        own, *shares = call(
             functools.partial(tile_kernel, coarse_order, part_order),
-            (tile_high, tile_low, *blocks),
+            (tile_parts, *blocks),
             [shape(count, loads)] * narrow,
             scratch=[
                 pltpu.VMEM((wide * count, loads), F32),
@@ -508,10 +514,10 @@
             moved=4 * coarse_inverse.size,
             name="tile",
         )
-        parts = [own] + swap_all(parts, "narrow", narrow, part_order)
+        shares = [own] + swap_all(shares, "narrow", narrow, part_order)
         mult_s, mult_n, image, *sends = call(
             functools.partial(lift_kernel, n, m, cap),
-            (size, *parts, basis, trial_s, trial_n, floor, top_high, top_low, pack),
+            (size, *shares, basis, trial_s, trial_n, floor, top, pack),
             [shape(shared, loads), shape(rest, loads), shape(shared, loads)] + sent,
             flops=3 * full * shared,
             moved=4 * order * shared,
@@ -529,7 +535,7 @@
                 moved=8 * shared * loads,
                 name="base",
             )[0]
-            ins = (size, high, low, mult_s, mult_n, gap, floor)
+            ins = (size, parts, mult_s, mult_n, gap, floor)
             shadow = (size, *recvs, base, unpack, mult_s, floor)
             cost = dict(flops=6 * shared * loads * unpack.shape[1], moved=2 * shared * unpack.shape[1])
             if last:
@@ -557,7 +563,7 @@
                 return tuple(out[None] for out in outs)
             mult_n, ahead = call(
                 rest_kernel,
-                (*ins, top_high, top_low, pack),
+                (*ins, top, pack),
                 [shape(rest, loads), shape(shared + padded, loads)],
                 flops=3 * full * order,
                 moved=4 * order * order,
@@ -565,7 +571,7 @@
             )
             mult_s, image, *sends = call(
                 functools.partial(sweep_kernel, times, cap),
-                (*shadow, stack_high, stack_low, ahead),
+                (*shadow, square, ahead),
                 [shape(shared, loads)] * 2 + sent,
                 name="sweep",
                 **cost,

time: 91.7 us -> 91.6 us (level)
  Pallas kernels: 20.5 us -> 22.1 us
  local copies, waits for them, and re-layouts: 1.38 us -> 0.04 us
  waiting for transfers between devices: 31.7 us -> 30.7 us
    pallas_call x26, Pallas kernels: 20.5 us -> 22.1 us  [call(): pl.pallas_call(body, out_shape=outs, grid=grid, in_specs=in_specs, out_sp...]
    unnamed x16, local copies, waits for them, and re-layouts: 1.38 us -> 0.04 us
    ppermute x30, waiting for transfers between devices: 31.7 us -> 30.7 us  [swap(): return lax.ppermute(block, axis, [(i, i ^ d) for i in range(count)])]
  transfers between devices with their start and end apart: 30 -> 30, of which waited for: 22 -> 24; matrix products, arithmetic and copies ran while one was open for 0% -> 0% of each run, Pallas kernels for 13% -> 15%
where the time goes in v9:
time: 91.6 us; the launch traced here: 91.4 us
  starting transfers between devices  36.7 us (40%)
  waiting for transfers between devices  30.7 us (34%)
  Pallas kernels  22.1 us (24%)
  between operations  1.79 us (2%)
    ppermute x30, starting transfers between devices, swap(): return lax.ppermute(block, axis, [(i, i ^ d) for i in range(count)])  36.7 us
    ppermute x30, waiting for transfers between devices, swap(): return lax.ppermute(block, axis, [(i, i ^ d) for i in range(count)])  30.7 us
    pallas_call x26, Pallas kernels, call(): pl.pallas_call(body, out_shape=outs, grid=grid, in_specs=in_specs, out_sp...  22.1 us
  transfers between devices with their start and end apart: 30, of which 24 were waited for; matrix products, arithmetic and copies ran while one was open for 0% of the time, Pallas kernels for 15%

profile of v9, /device:TPU:0, one launch (start us, length us, event | category | flops | bytes accessed | tf_op | source)
XLA Modules:
  0.0 91.4 jit_solution(18012569851437164742)
XLA Ops:
  0.7 2.3 %first.1 = (bf16[512,1024]{1,0:T(8,128)(2,1)S(1)}, f32[256,128]{1,0:T(8,128)S(1)}, f32[264,128]{1,0:T(8,128)S(1)}, f32[264,128]{1,0:T(8,128)S(1)}, f32[264,128]{1,0:T(8,128)S(1)}) custom-call(s32[1,256]{1,0:T(1,128)} %bitcast.30, s32[1,256]{1,0:T(1,128)} %rows.1, f32[1024,1024]{1,0:T(8,128)} %bitcast.19, f32[1024,128]{1,0:T(8,128)} %bitcast.21), custom_call_target="tpu_custom_call" | custom-call | flops 201326592 | bytes 2097152 | tf_op jit(solution)/shard_map/first/pallas_call | solution.py:52
  3.0 5.1 %collective-permute-start = (f32[264,128]{1,0:T(8,128)S(1)}, f32[264,128]{1,0:T(8,128)S(1)}, u32[]{:S(2)}, u32[]{:S(2)}) collective-permute-start(f32[264,128]{1,0:T(8,128)S(1)} %get-tuple-element.76), channel_id=1, source_target_pairs={{0,12},{4,8},{8,4},{12,0},{1,13},{5,9},{9,5},{13,1},{2,14},{6,10},... | collective-permute-start | bytes 405512 | tf_op jit(solution)/shard_map/ppermute | solution.py:346
  8.1 0.6 collective-permute-start.2
  9.4 0.4 marks.1
  10.1 2.5 %rest_start.1 = (f32[768,128]{1,0:T(8,128)S(1)}, f32[64,128]{1,0:T(8,128)S(1)}, bf16[2,768,1024]{2,1,0:T(8,128)(2,1)S(1)}) custom-call(s32[1]{0:T(128)S(6)} %copy.15.size, f32[1024,1024]{1,0:T(8,128)S(1)} %bitcast.20, f32[1024,128]{1,0:T(8,128)S(1)} %bitcast.22, f32[1024,128]{1,0:T(8,128)S(1)} %bitcast.23, f32[1024,128]{1,0:T(8,128)S(1)} %bitcast.8, ...), custom_call_target="tpu_custom_call" | custom-call | flops 603979776 | bytes 6291456 | tf_op jit(solution)/shard_map/rest_start/pallas_call | solution.py:52
  12.6 3.1 %collective-permute-done.1.refs_1_ = f32[264,128]{1,0:T(8,128)S(1)} collective-permute-done((f32[264,128]{1,0:T(8,128)S(1)}, f32[264,128]{1,0:T(8,128)S(1)}, u32[]{:S(2)}, u32[]{:S(2)}) %collective-permute-start.1) | collective-permute-done | bytes 135200 | tf_op jit(solution)/shard_map/ppermute | solution.py:346
  15.7 3.9 %collective-permute-done.2.refs_2_ = f32[264,128]{1,0:T(8,128)S(1)} collective-permute-done((f32[264,128]{1,0:T(8,128)S(1)}, f32[264,128]{1,0:T(8,128)S(1)}, u32[]{:S(2)}, u32[]{:S(2)}) %collective-permute-start.2) | collective-permute-done | bytes 135200 | tf_op jit(solution)/shard_map/ppermute | solution.py:346
  19.5 0.5 coarse.2
  20.0 0.8 collective-permute-start.3
  20.8 1.8 %collective-permute-start.4 = (f32[64,128]{1,0:T(8,128)S(1)}, f32[64,128]{1,0:T(8,128)S(1)}, u32[]{:S(2)}, u32[]{:S(2)}) collective-permute-start(f32[64,128]{1,0:T(8,128)S(1)} %get-tuple-element.85), channel_id=1, source_target_pairs={{0,12},{4,8},{8,4},{12,0},{1,13},{5,9},{9,5},{13,1},{2,14},{6,10},... | collective-permute-start | bytes 98312 | tf_op jit(solution)/shard_map/ppermute | solution.py:346
  22.6 0.9 %collective-permute-start.5 = (f32[64,128]{1,0:T(8,128)S(1)}, f32[64,128]{1,0:T(8,128)S(1)}, u32[]{:S(2)}, u32[]{:S(2)}) collective-permute-start(f32[64,128]{1,0:T(8,128)S(1)} %get-tuple-element.86), channel_id=1, source_target_pairs={{0,4},{4,0},{8,12},{12,8},{1,5},{5,1},{9,13},{13,9},{2,6},{6,2},{1... | collective-permute-start | bytes 98312 | tf_op jit(solution)/shard_map/ppermute | solution.py:346
  23.6 0.4 prepare.1
  24.0 1.1 %collective-permute-done.3.refs_1_ = f32[64,128]{1,0:T(8,128)S(1)} collective-permute-done((f32[64,128]{1,0:T(8,128)S(1)}, f32[64,128]{1,0:T(8,128)S(1)}, u32[]{:S(2)}, u32[]{:S(2)}) %collective-permute-start.3) | collective-permute-done | bytes 32800 | tf_op jit(solution)/shard_map/ppermute | solution.py:346
  25.0 1.7 %collective-permute-done.4.refs_2_ = f32[64,128]{1,0:T(8,128)S(1)} collective-permute-done((f32[64,128]{1,0:T(8,128)S(1)}, f32[64,128]{1,0:T(8,128)S(1)}, u32[]{:S(2)}, u32[]{:S(2)}) %collective-permute-start.4) | collective-permute-done | bytes 32800 | tf_op jit(solution)/shard_map/ppermute | solution.py:346
  27.2 1.6 %collective-permute-start.7 = (f32[64,128]{1,0:T(8,128)S(1)}, f32[64,128]{1,0:T(8,128)S(1)}, u32[]{:S(2)}, u32[]{:S(2)}) collective-permute-start(f32[64,128]{1,0:T(8,128)S(1)} %get-tuple-element.89), channel_id=1, source_target_pairs={{0,2},{1,3},{2,0},{3,1},{4,6},{5,7},{6,4},{7,5},{8,10},{9,11},{10,... | collective-permute-start | bytes 98312 | tf_op jit(solution)/shard_map/ppermute | solution.py:346
  29.1 0.3 pack.1
  29.4 1.5 %collective-permute-done.6.refs_1_ = f32[64,128]{1,0:T(8,128)S(1)} collective-permute-done((f32[64,128]{1,0:T(8,128)S(1)}, f32[64,128]{1,0:T(8,128)S(1)}, u32[]{:S(2)}, u32[]{:S(2)}) %collective-permute-start.6) | collective-permute-done | bytes 32800 | tf_op jit(solution)/shard_map/ppermute | solution.py:346
  30.9 0.4 collective-permute-done.7.refs_2_
  31.3 1.0 %lift.2 = (f32[256,128]{1,0:T(8,128)S(1)}, f32[768,128]{1,0:T(8,128)S(1)}, f32[256,128]{1,0:T(8,128)S(1)}, f32[128,128]{1,0:T(8,128)S(1)}, f32[128,128]{1,0:T(8,128)S(1)}, /*index=5*/f32[128,128]{1,0:T(8,128)S(1)}) custom-call(s32[1]{0:T(128)S(6)} %copy.15.size, f32[64,128]{1,0:T(8,128)S(1)} %get-tuple-element.87.refs_0_, ...), custom_call_target="tpu_custom_call" | custom-call | flops 201326592 | bytes 1048576 | tf_op jit(solution)/shard_map/lift/pallas_call | solution.py:52
  32.3 1.7 %collective-permute-start.9 = (f32[128,128]{1,0:T(8,128)S(1)}, f32[128,128]{1,0:T(8,128)S(1)}, u32[]{:S(2)}, u32[]{:S(2)}) collective-permute-start(f32[128,128]{1,0:T(8,128)S(1)} %get-tuple-element.97), channel_id=1, source_target_pairs={{0,8},{4,12},{8,0},{12,4},{1,9},{5,13},{9,1},{13,5},{2,10},{6,14},... | collective-permute-start | bytes 196616 | tf_op jit(solution)/shard_map/ppermute | solution.py:346
  34.0 1.4 %collective-permute-start.10 = (f32[128,128]{1,0:T(8,128)S(1)}, f32[128,128]{1,0:T(8,128)S(1)}, u32[]{:S(2)}, u32[]{:S(2)}) collective-permute-start(f32[128,128]{1,0:T(8,128)S(1)} %get-tuple-element.98), channel_id=1, source_target_pairs={{0,12},{4,8},{8,4},{12,0},{1,13},{5,9},{9,5},{13,1},{2,14},{6,10},... | collective-permute-start | bytes 196616 | tf_op jit(solution)/shard_map/ppermute | solution.py:346
  35.3 0.5 collective-permute-start.11
  36.1 1.9 %rest.3 = (f32[768,128]{1,0:T(8,128)S(1)}, f32[640,128]{1,0:T(8,128)S(1)}) custom-call(s32[1]{0:T(128)S(6)} %copy.15.size, bf16[2,768,1024]{2,1,0:T(8,128)(2,1)S(1)} %get-tuple-element.104.parts, f32[256,128]{1,0:T(8,128)S(1)} %get-tuple-element.102.mult_s.refs_5_, f32[768,128]{1,0:T(8,128)S(1)} %get-tuple-element.105.mult_n, f32[1024,128]{1,0:T(8,128)S(1)} %bitcast.10, ...), custom_call_target="tpu_custom_call" | custom-call | flops 805306368 | bytes 4194304 | tf_op jit(solution)/shard_map/rest/pallas_call | solution.py:52
  37.9 2.6 %collective-permute-done.9.refs_0_ = f32[128,128]{1,0:T(8,128)S(1)} collective-permute-done((f32[128,128]{1,0:T(8,128)S(1)}, f32[128,128]{1,0:T(8,128)S(1)}, u32[]{:S(2)}, u32[]{:S(2)}) %collective-permute-start.9) | collective-permute-done | bytes 65568 | tf_op jit(solution)/shard_map/ppermute | solution.py:346
  40.6 1.2 %collective-permute-done.11.refs_2_ = f32[128,128]{1,0:T(8,128)S(1)} collective-permute-done((f32[128,128]{1,0:T(8,128)S(1)}, f32[128,128]{1,0:T(8,128)S(1)}, u32[]{:S(2)}, u32[]{:S(2)}) %collective-permute-start.11) | collective-permute-done | bytes 65568 | tf_op jit(solution)/shard_map/ppermute | solution.py:346
  41.8 0.7 sweep.3
  42.4 1.7 %collective-permute-start.12 = (f32[128,128]{1,0:T(8,128)S(1)}, f32[128,128]{1,0:T(8,128)S(1)}, u32[]{:S(2)}, u32[]{:S(2)}) collective-permute-start(f32[128,128]{1,0:T(8,128)S(1)} %get-tuple-element.107), channel_id=1, source_target_pairs={{0,12},{4,8},{8,4},{12,0},{1,13},{5,9},{9,5},{13,1},{2,14},{6,10},... | collective-permute-start | bytes 196616 | tf_op jit(solution)/shard_map/ppermute | solution.py:346
  44.2 2.7 %collective-permute-start.14 = (f32[128,128]{1,0:T(8,128)S(1)}, f32[128,128]{1,0:T(8,128)S(1)}, u32[]{:S(2)}, u32[]{:S(2)}) collective-permute-start(f32[128,128]{1,0:T(8,128)S(1)} %get-tuple-element.109), channel_id=1, source_target_pairs={{0,8},{4,12},{8,0},{12,4},{1,9},{5,13},{9,1},{13,5},{2,10},{6,14},... | collective-permute-start | bytes 196616 | tf_op jit(solution)/shard_map/ppermute | solution.py:346
  47.1 1.9 %rest.4 = (f32[768,128]{1,0:T(8,128)S(1)}, f32[640,128]{1,0:T(8,128)S(1)}) custom-call(s32[1]{0:T(128)S(6)} %copy.15.size, bf16[2,768,1024]{2,1,0:T(8,128)(2,1)S(1)} %get-tuple-element.104.parts, f32[256,128]{1,0:T(8,128)S(1)} %get-tuple-element.111.mult_s.refs_5_, f32[768,128]{1,0:T(8,128)S(1)} %get-tuple-element.112.mult_n, f32[1024,128]{1,0:T(8,128)S(1)} %bitcast.12, ...), custom_call_target="tpu_custom_call" | custom-call | flops 805306368 | bytes 4194304 | tf_op jit(solution)/shard_map/rest/pallas_call | solution.py:52
  49.0 0.3 collective-permute-done.12.refs_0_
  49.3 1.2 %collective-permute-done.13.refs_1_ = f32[128,128]{1,0:T(8,128)S(1)} collective-permute-done((f32[128,128]{1,0:T(8,128)S(1)}, f32[128,128]{1,0:T(8,128)S(1)}, u32[]{:S(2)}, u32[]{:S(2)}) %collective-permute-start.13) | collective-permute-done | bytes 65568 | tf_op jit(solution)/shard_map/ppermute | solution.py:346
  50.5 0.7 collective-permute-done.14.refs_2_
  51.1 0.7 sweep.4
  51.8 1.0 %collective-permute-start.15 = (f32[128,128]{1,0:T(8,128)S(1)}, f32[128,128]{1,0:T(8,128)S(1)}, u32[]{:S(2)}, u32[]{:S(2)}) collective-permute-start(f32[128,128]{1,0:T(8,128)S(1)} %get-tuple-element.114), channel_id=1, source_target_pairs={{0,8},{4,12},{8,0},{12,4},{1,9},{5,13},{9,1},{13,5},{2,10},{6,14},... | collective-permute-start | bytes 196616 | tf_op jit(solution)/shard_map/ppermute | solution.py:346
  52.8 1.9 %collective-permute-start.16 = (f32[128,128]{1,0:T(8,128)S(1)}, f32[128,128]{1,0:T(8,128)S(1)}, u32[]{:S(2)}, u32[]{:S(2)}) collective-permute-start(f32[128,128]{1,0:T(8,128)S(1)} %get-tuple-element.115), channel_id=1, source_target_pairs={{0,12},{4,8},{8,4},{12,0},{1,13},{5,9},{9,5},{13,1},{2,14},{6,10},... | collective-permute-start | bytes 196616 | tf_op jit(solution)/shard_map/ppermute | solution.py:346
  54.7 0.6 collective-permute-start.17
  55.6 1.2 %rest_first.1 = (f32[768,128]{1,0:T(8,128)S(1)}, f32[64,128]{1,0:T(8,128)S(1)}) custom-call(s32[1]{0:T(128)S(6)} %copy.15.size, bf16[2,768,1024]{2,1,0:T(8,128)(2,1)S(1)} %get-tuple-element.104.parts, f32[256,128]{1,0:T(8,128)S(1)} %get-tuple-element.118.mult_s.refs_5_, f32[768,128]{1,0:T(8,128)S(1)} %get-tuple-element.119.mult_n, f32[1024,128]{1,0:T(8,128)S(1)} %bitcast.14, ...), custom_call_target="tpu_custom_call" | custom-call | flops 603979776 | bytes 3145728 | tf_op jit(solution)/shard_map/rest_first/pallas_call | solution.py:52
  56.8 1.2 %collective-permute-done.15.refs_0_ = f32[128,128]{1,0:T(8,128)S(1)} collective-permute-done((f32[128,128]{1,0:T(8,128)S(1)}, f32[128,128]{1,0:T(8,128)S(1)}, u32[]{:S(2)}, u32[]{:S(2)}) %collective-permute-start.15) | collective-permute-done | bytes 65568 | tf_op jit(solution)/shard_map/ppermute | solution.py:346
  57.9 1.1 %collective-permute-done.16.refs_1_ = f32[128,128]{1,0:T(8,128)S(1)} collective-permute-done((f32[128,128]{1,0:T(8,128)S(1)}, f32[128,128]{1,0:T(8,128)S(1)}, u32[]{:S(2)}, u32[]{:S(2)}) %collective-permute-start.16) | collective-permute-done | bytes 65568 | tf_op jit(solution)/shard_map/ppermute | solution.py:346
  59.0 0.6 collective-permute-done.17.refs_2_
  59.7 0.4 coarse.3
  60.1 2.0 %collective-permute-start.18 = (f32[64,128]{1,0:T(8,128)S(1)}, f32[64,128]{1,0:T(8,128)S(1)}, u32[]{:S(2)}, u32[]{:S(2)}) collective-permute-start(f32[64,128]{1,0:T(8,128)S(1)} %get-tuple-element.122), channel_id=1, source_target_pairs={{0,12},{4,8},{8,4},{12,0},{1,13},{5,9},{9,5},{13,1},{2,14},{6,10},... | collective-permute-start | bytes 98312 | tf_op jit(solution)/shard_map/ppermute | solution.py:346
  62.1 2.5 %collective-permute-start.20 = (f32[64,128]{1,0:T(8,128)S(1)}, f32[64,128]{1,0:T(8,128)S(1)}, u32[]{:S(2)}, u32[]{:S(2)}) collective-permute-start(f32[64,128]{1,0:T(8,128)S(1)} %get-tuple-element.124), channel_id=1, source_target_pairs={{0,4},{4,0},{8,12},{12,8},{1,5},{5,1},{9,13},{13,9},{2,6},{6,2},{1... | collective-permute-start | bytes 98312 | tf_op jit(solution)/shard_map/ppermute | solution.py:346
  64.6 1.3 %collective-permute-done.18.refs_1_ = f32[64,128]{1,0:T(8,128)S(1)} collective-permute-done((f32[64,128]{1,0:T(8,128)S(1)}, f32[64,128]{1,0:T(8,128)S(1)}, u32[]{:S(2)}, u32[]{:S(2)}) %collective-permute-start.18) | collective-permute-done | bytes 32800 | tf_op jit(solution)/shard_map/ppermute | solution.py:346
  65.9 1.0 %collective-permute-done.19.refs_2_ = f32[64,128]{1,0:T(8,128)S(1)} collective-permute-done((f32[64,128]{1,0:T(8,128)S(1)}, f32[64,128]{1,0:T(8,128)S(1)}, u32[]{:S(2)}, u32[]{:S(2)}) %collective-permute-start.19) | collective-permute-done | bytes 32800 | tf_op jit(solution)/shard_map/ppermute | solution.py:346
  67.2 0.8 collective-permute-start.22
  68.0 1.1 %collective-permute-start.23 = (f32[64,128]{1,0:T(8,128)S(1)}, f32[64,128]{1,0:T(8,128)S(1)}, u32[]{:S(2)}, u32[]{:S(2)}) collective-permute-start(f32[64,128]{1,0:T(8,128)S(1)} %get-tuple-element.128), channel_id=1, source_target_pairs={{0,1},{1,0},{2,3},{3,2},{4,5},{5,4},{6,7},{7,6},{8,9},{9,8},{10,11... | collective-permute-start | bytes 98312 | tf_op jit(solution)/shard_map/ppermute | solution.py:346
  69.1 1.5 %collective-permute-done.21.refs_1_ = f32[64,128]{1,0:T(8,128)S(1)} collective-permute-done((f32[64,128]{1,0:T(8,128)S(1)}, f32[64,128]{1,0:T(8,128)S(1)}, u32[]{:S(2)}, u32[]{:S(2)}) %collective-permute-start.21) | collective-permute-done | bytes 32800 | tf_op jit(solution)/shard_map/ppermute | solution.py:346
  70.6 0.8 collective-permute-done.22.refs_2_
  71.4 1.0 %lift.3 = (f32[256,128]{1,0:T(8,128)S(1)}, f32[768,128]{1,0:T(8,128)S(1)}, f32[256,128]{1,0:T(8,128)S(1)}, f32[128,128]{1,0:T(8,128)S(1)}, f32[128,128]{1,0:T(8,128)S(1)}, /*index=5*/f32[128,128]{1,0:T(8,128)S(1)}) custom-call(s32[1]{0:T(128)S(6)} %copy.15.size, f32[64,128]{1,0:T(8,128)S(1)} %get-tuple-element.125.refs_0_, ...), custom_call_target="tpu_custom_call" | custom-call | flops 201326592 | bytes 1048576 | tf_op jit(solution)/shard_map/lift/pallas_call | solution.py:52
  72.4 2.1 %collective-permute-start.24 = (f32[128,128]{1,0:T(8,128)S(1)}, f32[128,128]{1,0:T(8,128)S(1)}, u32[]{:S(2)}, u32[]{:S(2)}) collective-permute-start(f32[128,128]{1,0:T(8,128)S(1)} %get-tuple-element.131), channel_id=1, source_target_pairs={{0,8},{4,12},{8,0},{12,4},{1,9},{5,13},{9,1},{13,5},{2,10},{6,14},... | collective-permute-start | bytes 196616 | tf_op jit(solution)/shard_map/ppermute | solution.py:346
  74.5 1.9 %collective-permute-start.25 = (f32[128,128]{1,0:T(8,128)S(1)}, f32[128,128]{1,0:T(8,128)S(1)}, u32[]{:S(2)}, u32[]{:S(2)}) collective-permute-start(f32[128,128]{1,0:T(8,128)S(1)} %get-tuple-element.132), channel_id=1, source_target_pairs={{0,12},{4,8},{8,4},{12,0},{1,13},{5,9},{9,5},{13,1},{2,14},{6,10},... | collective-permute-start | bytes 196616 | tf_op jit(solution)/shard_map/ppermute | solution.py:346
  76.6 1.9 %rest.5 = (f32[768,128]{1,0:T(8,128)S(1)}, f32[640,128]{1,0:T(8,128)S(1)}) custom-call(s32[1]{0:T(128)S(6)} %copy.15.size, bf16[2,768,1024]{2,1,0:T(8,128)(2,1)S(1)} %get-tuple-element.104.parts, f32[256,128]{1,0:T(8,128)S(1)} %get-tuple-element.135.mult_s.refs_5_, f32[768,128]{1,0:T(8,128)S(1)} %get-tuple-element.136.mult_n, f32[1024,128]{1,0:T(8,128)S(1)} %bitcast.16, ...), custom_call_target="tpu_custom_call" | custom-call | flops 805306368 | bytes 4194304 | tf_op jit(solution)/shard_map/rest/pallas_call | solution.py:52
  78.5 1.8 %collective-permute-done.24.refs_0_ = f32[128,128]{1,0:T(8,128)S(1)} collective-permute-done((f32[128,128]{1,0:T(8,128)S(1)}, f32[128,128]{1,0:T(8,128)S(1)}, u32[]{:S(2)}, u32[]{:S(2)}) %collective-permute-start.24) | collective-permute-done | bytes 65568 | tf_op jit(solution)/shard_map/ppermute | solution.py:346
  80.3 0.6 collective-permute-done.25.refs_1_
  80.9 0.7 collective-permute-done.26.refs_2_
  81.6 0.7 sweep.5
  82.3 1.0 %collective-permute-start.27 = (f32[128,128]{1,0:T(8,128)S(1)}, f32[128,128]{1,0:T(8,128)S(1)}, u32[]{:S(2)}, u32[]{:S(2)}) collective-permute-start(f32[128,128]{1,0:T(8,128)S(1)} %get-tuple-element.138), channel_id=1, source_target_pairs={{0,8},{4,12},{8,0},{12,4},{1,9},{5,13},{9,1},{13,5},{2,10},{6,14},... | collective-permute-start | bytes 196616 | tf_op jit(solution)/shard_map/ppermute | solution.py:346
  83.2 1.9 %collective-permute-start.28 = (f32[128,128]{1,0:T(8,128)S(1)}, f32[128,128]{1,0:T(8,128)S(1)}, u32[]{:S(2)}, u32[]{:S(2)}) collective-permute-start(f32[128,128]{1,0:T(8,128)S(1)} %get-tuple-element.139), channel_id=1, source_target_pairs={{0,12},{4,8},{8,4},{12,0},{1,13},{5,9},{9,5},{13,1},{2,14},{6,10},... | collective-permute-start | bytes 196616 | tf_op jit(solution)/shard_map/ppermute | solution.py:346
  85.1 0.7 collective-permute-start.29
  86.0 1.9 %rest_last.1 = (f32[1024,128]{1,0:T(8,128)}, f32[1024,128]{1,0:T(8,128)}) custom-call(s32[1]{0:T(128)S(6)} %copy.15.size, bf16[2,768,1024]{2,1,0:T(8,128)(2,1)S(1)} %get-tuple-element.104.parts, f32[256,128]{1,0:T(8,128)S(1)} %get-tuple-element.142.mult_s.refs_5_, f32[768,128]{1,0:T(8,128)S(1)} %get-tuple-element.143.mult_n, f32[1024,128]{1,0:T(8,128)S(1)} %bitcast.18, ...), custom_call_target="tpu_custom_call" | custom-call | flops 603979776 | bytes 3145728 | tf_op jit(solution)/shard_map/rest_last/pallas_call | solution.py:52
  87.9 1.7 %collective-permute-done.27.refs_0_ = f32[128,128]{1,0:T(8,128)S(1)} collective-permute-done((f32[128,128]{1,0:T(8,128)S(1)}, f32[128,128]{1,0:T(8,128)S(1)}, u32[]{:S(2)}, u32[]{:S(2)}) %collective-permute-start.27) | collective-permute-done | bytes 65568 | tf_op jit(solution)/shard_map/ppermute | solution.py:346
  89.7 0.6 collective-permute-done.29.refs_2_
  90.3 0.9 %last.1 = (f32[1024,128]{1,0:T(8,128)}, f32[1024,128]{1,0:T(8,128)}) custom-call(s32[1]{0:T(128)S(6)} %copy.15.size, f32[128,128]{1,0:T(8,128)S(1)} %collective-permute-done.27.refs_0_, f32[128,128]{1,0:T(8,128)S(1)} %collective-permute-done.28.refs_1_, ...), custom_call_target="tpu_custom_call", output_to_operand_aliasing={{0}: (8, {}), {1}: (9, {})} | custom-call | flops 75497472 | bytes 196608 | tf_op jit(solution)/shard_map/last/pallas_call | solution.py:52
  (38 shorter events, 2.3 us)
Async XLA Ops:
  0.6 8.8 %copy-start.7 = (s32[1,256]{1,0:T(1,128)S(1)}, s32[1,256]{1,0:T(1,128)}, u32[]{:S(2)}) copy-start(s32[1,256]{1,0:T(1,128)} %rows.1) | copy-start | bytes 3076
  0.6 8.8 %copy-start.6 = (s32[1,256,1]{1,2,0:T(1,128)S(1)}, s32[1,256,1]{1,2,0:T(1,128)}, u32[]{:S(2)}) copy-start(s32[1,256,1]{1,2,0:T(1,128)} %param.14) | copy-start | bytes 3076
  0.7 9.4 %copy-start.1 = (f32[1,1024,1024]{2,1,0:T(8,128)S(1)}, f32[1,1024,1024]{2,1,0:T(8,128)}, u32[]{:S(2)}) copy-start(f32[1,1024,1024]{2,1,0:T(8,128)} %param.9) | copy-start | bytes 12582916
  0.7 9.2 %copy-start = (f32[1,1024,128]{2,1,0:T(8,128)S(1)}, f32[1,1024,128]{2,1,0:T(8,128)}, u32[]{:S(2)}) copy-start(f32[1,1024,128]{2,1,0:T(8,128)} %param.12) | copy-start | bytes 1572868
  0.7 9.4 %copy-start.2 = (f32[1,1024,128]{2,1,0:T(8,128)S(1)}, f32[1,1024,128]{2,1,0:T(8,128)}, u32[]{:S(2)}) copy-start(f32[1,1024,128]{2,1,0:T(8,128)} %param.13) | copy-start | bytes 1572868
  0.7 9.4 %copy-start.3 = (f32[1,64,1024]{2,1,0:T(8,128)S(1)}, f32[1,64,1024]{2,1,0:T(8,128)}, u32[]{:S(2)}) copy-start(f32[1,64,1024]{2,1,0:T(8,128)} %param.11) | copy-start | bytes 786436
  3.0 9.6 %collective-permute-start = (f32[264,128]{1,0:T(8,128)S(1)}, f32[264,128]{1,0:T(8,128)S(1)}, u32[]{:S(2)}, u32[]{:S(2)}) collective-permute-start(f32[264,128]{1,0:T(8,128)S(1)} %get-tuple-element.76), channel_id=1, source_target_pairs={{0,12},{4,8},{8,4},{12,0},{1,13},{5,9},{9,5},{13,1},{2,14},{6,10},... | collective-permute-start | bytes 405512 | tf_op jit(solution)/shard_map/ppermute | solution.py:346
  8.1 7.6 %collective-permute-start.1 = (f32[264,128]{1,0:T(8,128)S(1)}, f32[264,128]{1,0:T(8,128)S(1)}, u32[]{:S(2)}, u32[]{:S(2)}) collective-permute-start(f32[264,128]{1,0:T(8,128)S(1)} %get-tuple-element.77), channel_id=1, source_target_pairs={{0,4},{4,0},{8,12},{12,8},{1,5},{5,1},{9,13},{13,9},{2,6},{6,2},{1... | collective-permute-start | bytes 405512 | tf_op jit(solution)/shard_map/ppermute | solution.py:346
  8.1 11.4 %collective-permute-start.2 = (f32[264,128]{1,0:T(8,128)S(1)}, f32[264,128]{1,0:T(8,128)S(1)}, u32[]{:S(2)}, u32[]{:S(2)}) collective-permute-start(f32[264,128]{1,0:T(8,128)S(1)} %get-tuple-element.78), channel_id=1, source_target_pairs={{0,8},{4,12},{8,0},{12,4},{1,9},{5,13},{9,1},{13,5},{2,10},{6,14},... | collective-permute-start | bytes 405512 | tf_op jit(solution)/shard_map/ppermute | solution.py:346
  9.8 13.7 %copy-start.4 = (f32[256,256]{1,0:T(8,128)S(1)}, f32[256,256]{1,0:T(8,128)}, u32[]{:S(2)}) copy-start(f32[256,256]{1,0:T(8,128)} %tile.3) | copy-start | bytes 786436
  9.8 13.7 %copy-start.5 = (s32[1,1024]{1,0:T(1,128)S(1)}, s32[1,1024]{1,0:T(1,128)}, u32[]{:S(2)}) copy-start(s32[1,1024]{1,0:T(1,128)} %contact.1) | copy-start | bytes 12292
  20.0 5.0 %collective-permute-start.3 = (f32[64,128]{1,0:T(8,128)S(1)}, f32[64,128]{1,0:T(8,128)S(1)}, u32[]{:S(2)}, u32[]{:S(2)}) collective-permute-start(f32[64,128]{1,0:T(8,128)S(1)} %get-tuple-element.84), channel_id=1, source_target_pairs={{0,8},{4,12},{8,0},{12,4},{1,9},{5,13},{9,1},{13,5},{2,10},{6,14},... | collective-permute-start | bytes 98312 | tf_op jit(solution)/shard_map/ppermute | solution.py:346
  20.8 5.9 %collective-permute-start.4 = (f32[64,128]{1,0:T(8,128)S(1)}, f32[64,128]{1,0:T(8,128)S(1)}, u32[]{:S(2)}, u32[]{:S(2)}) collective-permute-start(f32[64,128]{1,0:T(8,128)S(1)} %get-tuple-element.85), channel_id=1, source_target_pairs={{0,12},{4,8},{8,4},{12,0},{1,13},{5,9},{9,5},{13,1},{2,14},{6,10},... | collective-permute-start | bytes 98312 | tf_op jit(solution)/shard_map/ppermute | solution.py:346
  22.6 4.3 %collective-permute-start.5 = (f32[64,128]{1,0:T(8,128)S(1)}, f32[64,128]{1,0:T(8,128)S(1)}, u32[]{:S(2)}, u32[]{:S(2)}) collective-permute-start(f32[64,128]{1,0:T(8,128)S(1)} %get-tuple-element.86), channel_id=1, source_target_pairs={{0,4},{4,0},{8,12},{12,8},{1,5},{5,1},{9,13},{13,9},{2,6},{6,2},{1... | collective-permute-start | bytes 98312 | tf_op jit(solution)/shard_map/ppermute | solution.py:346
  27.2 3.7 %collective-permute-start.6 = (f32[64,128]{1,0:T(8,128)S(1)}, f32[64,128]{1,0:T(8,128)S(1)}, u32[]{:S(2)}, u32[]{:S(2)}) collective-permute-start(f32[64,128]{1,0:T(8,128)S(1)} %get-tuple-element.88), channel_id=1, source_target_pairs={{0,3},{1,2},{2,1},{3,0},{4,7},{5,6},{6,5},{7,4},{8,11},{9,10},{10,... | collective-permute-start | bytes 98312 | tf_op jit(solution)/shard_map/ppermute | solution.py:346
  27.2 4.0 %collective-permute-start.7 = (f32[64,128]{1,0:T(8,128)S(1)}, f32[64,128]{1,0:T(8,128)S(1)}, u32[]{:S(2)}, u32[]{:S(2)}) collective-permute-start(f32[64,128]{1,0:T(8,128)S(1)} %get-tuple-element.89), channel_id=1, source_target_pairs={{0,2},{1,3},{2,0},{3,1},{4,6},{5,7},{6,4},{7,5},{8,10},{9,11},{10,... | collective-permute-start | bytes 98312 | tf_op jit(solution)/shard_map/ppermute | solution.py:346
  28.8 2.5 %collective-permute-start.8 = (f32[64,128]{1,0:T(8,128)S(1)}, f32[64,128]{1,0:T(8,128)S(1)}, u32[]{:S(2)}, u32[]{:S(2)}) collective-permute-start(f32[64,128]{1,0:T(8,128)S(1)} %get-tuple-element.90), channel_id=1, source_target_pairs={{0,1},{1,0},{2,3},{3,2},{4,5},{5,4},{6,7},{7,6},{8,9},{9,8},{10,11... | collective-permute-start | bytes 98312 | tf_op jit(solution)/shard_map/ppermute | solution.py:346
  32.3 8.3 %collective-permute-start.9 = (f32[128,128]{1,0:T(8,128)S(1)}, f32[128,128]{1,0:T(8,128)S(1)}, u32[]{:S(2)}, u32[]{:S(2)}) collective-permute-start(f32[128,128]{1,0:T(8,128)S(1)} %get-tuple-element.97), channel_id=1, source_target_pairs={{0,8},{4,12},{8,0},{12,4},{1,9},{5,13},{9,1},{13,5},{2,10},{6,14},... | collective-permute-start | bytes 196616 | tf_op jit(solution)/shard_map/ppermute | solution.py:346
  34.0 6.6 %collective-permute-start.10 = (f32[128,128]{1,0:T(8,128)S(1)}, f32[128,128]{1,0:T(8,128)S(1)}, u32[]{:S(2)}, u32[]{:S(2)}) collective-permute-start(f32[128,128]{1,0:T(8,128)S(1)} %get-tuple-element.98), channel_id=1, source_target_pairs={{0,12},{4,8},{8,4},{12,0},{1,13},{5,9},{9,5},{13,1},{2,14},{6,10},... | collective-permute-start | bytes 196616 | tf_op jit(solution)/shard_map/ppermute | solution.py:346
  35.3 6.4 %collective-permute-start.11 = (f32[128,128]{1,0:T(8,128)S(1)}, f32[128,128]{1,0:T(8,128)S(1)}, u32[]{:S(2)}, u32[]{:S(2)}) collective-permute-start(f32[128,128]{1,0:T(8,128)S(1)} %get-tuple-element.99), channel_id=1, source_target_pairs={{0,4},{4,0},{8,12},{12,8},{1,5},{5,1},{9,13},{13,9},{2,6},{6,2},{1... | collective-permute-start | bytes 196616 | tf_op jit(solution)/shard_map/ppermute | solution.py:346
  42.4 6.8 %collective-permute-start.12 = (f32[128,128]{1,0:T(8,128)S(1)}, f32[128,128]{1,0:T(8,128)S(1)}, u32[]{:S(2)}, u32[]{:S(2)}) collective-permute-start(f32[128,128]{1,0:T(8,128)S(1)} %get-tuple-element.107), channel_id=1, source_target_pairs={{0,12},{4,8},{8,4},{12,0},{1,13},{5,9},{9,5},{13,1},{2,14},{6,10},... | collective-permute-start | bytes 196616 | tf_op jit(solution)/shard_map/ppermute | solution.py:346
  44.1 6.3 %collective-permute-start.13 = (f32[128,128]{1,0:T(8,128)S(1)}, f32[128,128]{1,0:T(8,128)S(1)}, u32[]{:S(2)}, u32[]{:S(2)}) collective-permute-start(f32[128,128]{1,0:T(8,128)S(1)} %get-tuple-element.108), channel_id=1, source_target_pairs={{0,4},{4,0},{8,12},{12,8},{1,5},{5,1},{9,13},{13,9},{2,6},{6,2},{1... | collective-permute-start | bytes 196616 | tf_op jit(solution)/shard_map/ppermute | solution.py:346
  44.2 7.0 %collective-permute-start.14 = (f32[128,128]{1,0:T(8,128)S(1)}, f32[128,128]{1,0:T(8,128)S(1)}, u32[]{:S(2)}, u32[]{:S(2)}) collective-permute-start(f32[128,128]{1,0:T(8,128)S(1)} %get-tuple-element.109), channel_id=1, source_target_pairs={{0,8},{4,12},{8,0},{12,4},{1,9},{5,13},{9,1},{13,5},{2,10},{6,14},... | collective-permute-start | bytes 196616 | tf_op jit(solution)/shard_map/ppermute | solution.py:346
  51.8 6.1 %collective-permute-start.15 = (f32[128,128]{1,0:T(8,128)S(1)}, f32[128,128]{1,0:T(8,128)S(1)}, u32[]{:S(2)}, u32[]{:S(2)}) collective-permute-start(f32[128,128]{1,0:T(8,128)S(1)} %get-tuple-element.114), channel_id=1, source_target_pairs={{0,8},{4,12},{8,0},{12,4},{1,9},{5,13},{9,1},{13,5},{2,10},{6,14},... | collective-permute-start | bytes 196616 | tf_op jit(solution)/shard_map/ppermute | solution.py:346
  52.8 6.2 %collective-permute-start.16 = (f32[128,128]{1,0:T(8,128)S(1)}, f32[128,128]{1,0:T(8,128)S(1)}, u32[]{:S(2)}, u32[]{:S(2)}) collective-permute-start(f32[128,128]{1,0:T(8,128)S(1)} %get-tuple-element.115), channel_id=1, source_target_pairs={{0,12},{4,8},{8,4},{12,0},{1,13},{5,9},{9,5},{13,1},{2,14},{6,10},... | collective-permute-start | bytes 196616 | tf_op jit(solution)/shard_map/ppermute | solution.py:346
  54.7 4.9 %collective-permute-start.17 = (f32[128,128]{1,0:T(8,128)S(1)}, f32[128,128]{1,0:T(8,128)S(1)}, u32[]{:S(2)}, u32[]{:S(2)}) collective-permute-start(f32[128,128]{1,0:T(8,128)S(1)} %get-tuple-element.116), channel_id=1, source_target_pairs={{0,4},{4,0},{8,12},{12,8},{1,5},{5,1},{9,13},{13,9},{2,6},{6,2},{1... | collective-permute-start | bytes 196616 | tf_op jit(solution)/shard_map/ppermute | solution.py:346
  60.1 5.8 %collective-permute-start.18 = (f32[64,128]{1,0:T(8,128)S(1)}, f32[64,128]{1,0:T(8,128)S(1)}, u32[]{:S(2)}, u32[]{:S(2)}) collective-permute-start(f32[64,128]{1,0:T(8,128)S(1)} %get-tuple-element.122), channel_id=1, source_target_pairs={{0,12},{4,8},{8,4},{12,0},{1,13},{5,9},{9,5},{13,1},{2,14},{6,10},... | collective-permute-start | bytes 98312 | tf_op jit(solution)/shard_map/ppermute | solution.py:346
  62.1 4.8 %collective-permute-start.19 = (f32[64,128]{1,0:T(8,128)S(1)}, f32[64,128]{1,0:T(8,128)S(1)}, u32[]{:S(2)}, u32[]{:S(2)}) collective-permute-start(f32[64,128]{1,0:T(8,128)S(1)} %get-tuple-element.123), channel_id=1, source_target_pairs={{0,8},{4,12},{8,0},{12,4},{1,9},{5,13},{9,1},{13,5},{2,10},{6,14},... | collective-permute-start | bytes 98312 | tf_op jit(solution)/shard_map/ppermute | solution.py:346
  62.1 4.8 %collective-permute-start.20 = (f32[64,128]{1,0:T(8,128)S(1)}, f32[64,128]{1,0:T(8,128)S(1)}, u32[]{:S(2)}, u32[]{:S(2)}) collective-permute-start(f32[64,128]{1,0:T(8,128)S(1)} %get-tuple-element.124), channel_id=1, source_target_pairs={{0,4},{4,0},{8,12},{12,8},{1,5},{5,1},{9,13},{13,9},{2,6},{6,2},{1... | collective-permute-start | bytes 98312 | tf_op jit(solution)/shard_map/ppermute | solution.py:346
  67.2 3.4 %collective-permute-start.21 = (f32[64,128]{1,0:T(8,128)S(1)}, f32[64,128]{1,0:T(8,128)S(1)}, u32[]{:S(2)}, u32[]{:S(2)}) collective-permute-start(f32[64,128]{1,0:T(8,128)S(1)} %get-tuple-element.126), channel_id=1, source_target_pairs={{0,3},{1,2},{2,1},{3,0},{4,7},{5,6},{6,5},{7,4},{8,11},{9,10},{10,... | collective-permute-start | bytes 98312 | tf_op jit(solution)/shard_map/ppermute | solution.py:346
  67.2 4.1 %collective-permute-start.22 = (f32[64,128]{1,0:T(8,128)S(1)}, f32[64,128]{1,0:T(8,128)S(1)}, u32[]{:S(2)}, u32[]{:S(2)}) collective-permute-start(f32[64,128]{1,0:T(8,128)S(1)} %get-tuple-element.127), channel_id=1, source_target_pairs={{0,2},{1,3},{2,0},{3,1},{4,6},{5,7},{6,4},{7,5},{8,10},{9,11},{10,... | collective-permute-start | bytes 98312 | tf_op jit(solution)/shard_map/ppermute | solution.py:346
  68.0 3.3 %collective-permute-start.23 = (f32[64,128]{1,0:T(8,128)S(1)}, f32[64,128]{1,0:T(8,128)S(1)}, u32[]{:S(2)}, u32[]{:S(2)}) collective-permute-start(f32[64,128]{1,0:T(8,128)S(1)} %get-tuple-element.128), channel_id=1, source_target_pairs={{0,1},{1,0},{2,3},{3,2},{4,5},{5,4},{6,7},{7,6},{8,9},{9,8},{10,11... | collective-permute-start | bytes 98312 | tf_op jit(solution)/shard_map/ppermute | solution.py:346
  72.4 7.9 %collective-permute-start.24 = (f32[128,128]{1,0:T(8,128)S(1)}, f32[128,128]{1,0:T(8,128)S(1)}, u32[]{:S(2)}, u32[]{:S(2)}) collective-permute-start(f32[128,128]{1,0:T(8,128)S(1)} %get-tuple-element.131), channel_id=1, source_target_pairs={{0,8},{4,12},{8,0},{12,4},{1,9},{5,13},{9,1},{13,5},{2,10},{6,14},... | collective-permute-start | bytes 196616 | tf_op jit(solution)/shard_map/ppermute | solution.py:346
  74.5 6.4 %collective-permute-start.25 = (f32[128,128]{1,0:T(8,128)S(1)}, f32[128,128]{1,0:T(8,128)S(1)}, u32[]{:S(2)}, u32[]{:S(2)}) collective-permute-start(f32[128,128]{1,0:T(8,128)S(1)} %get-tuple-element.132), channel_id=1, source_target_pairs={{0,12},{4,8},{8,4},{12,0},{1,13},{5,9},{9,5},{13,1},{2,14},{6,10},... | collective-permute-start | bytes 196616 | tf_op jit(solution)/shard_map/ppermute | solution.py:346
  76.4 5.2 %collective-permute-start.26 = (f32[128,128]{1,0:T(8,128)S(1)}, f32[128,128]{1,0:T(8,128)S(1)}, u32[]{:S(2)}, u32[]{:S(2)}) collective-permute-start(f32[128,128]{1,0:T(8,128)S(1)} %get-tuple-element.133), channel_id=1, source_target_pairs={{0,4},{4,0},{8,12},{12,8},{1,5},{5,1},{9,13},{13,9},{2,6},{6,2},{1... | collective-permute-start | bytes 196616 | tf_op jit(solution)/shard_map/ppermute | solution.py:346
  82.3 7.4 %collective-permute-start.27 = (f32[128,128]{1,0:T(8,128)S(1)}, f32[128,128]{1,0:T(8,128)S(1)}, u32[]{:S(2)}, u32[]{:S(2)}) collective-permute-start(f32[128,128]{1,0:T(8,128)S(1)} %get-tuple-element.138), channel_id=1, source_target_pairs={{0,8},{4,12},{8,0},{12,4},{1,9},{5,13},{9,1},{13,5},{2,10},{6,14},... | collective-permute-start | bytes 196616 | tf_op jit(solution)/shard_map/ppermute | solution.py:346
  83.2 6.4 %collective-permute-start.28 = (f32[128,128]{1,0:T(8,128)S(1)}, f32[128,128]{1,0:T(8,128)S(1)}, u32[]{:S(2)}, u32[]{:S(2)}) collective-permute-start(f32[128,128]{1,0:T(8,128)S(1)} %get-tuple-element.139), channel_id=1, source_target_pairs={{0,12},{4,8},{8,4},{12,0},{1,13},{5,9},{9,5},{13,1},{2,14},{6,10},... | collective-permute-start | bytes 196616 | tf_op jit(solution)/shard_map/ppermute | solution.py:346
  85.1 5.2 %collective-permute-start.29 = (f32[128,128]{1,0:T(8,128)S(1)}, f32[128,128]{1,0:T(8,128)S(1)}, u32[]{:S(2)}, u32[]{:S(2)}) collective-permute-start(f32[128,128]{1,0:T(8,128)S(1)} %get-tuple-element.140), channel_id=1, source_target_pairs={{0,4},{4,0},{8,12},{12,8},{1,5},{5,1},{9,13},{13,9},{2,6},{6,2},{1... | collective-permute-start | bytes 196616 | tf_op jit(solution)/shard_map/ppermute | solution.py:346

commit v10 on v7

--- a/solution.py
+++ b/solution.py
@@ -221,7 +221,11 @@
     coarse[...] = product(split(modes[:, mult_s.shape[0]:]), split(residual))
 
 
-def rest_kernel(size, high, low, mult_s, mult_n, gap, floor, top_high, top_low, pack, mult_out, ahead):
+def early():
+    return lax.axis_index("narrow") % 2 == 1
+
+
+def rest_update(size, high, low, mult_s, mult_n, gap, floor, top_high, top_low, pack, mult_out, ahead):
     shared = mult_s.shape[0]
     residual, alive = rest_residual(size, high, low, mult_s, mult_n, gap)
     mult = settle(mult_n[...] + STEP * residual, floor[shared:, :], alive)
@@ -229,6 +233,19 @@
     value = product((top_high[:, shared:], top_low[:, shared:]), split(mult))
     ahead[:shared, :] = value
     ahead[shared:, :] = pick(pack[...], value)
+
+
+def rest_late_kernel(*refs):
+    ins, (mult_done, ahead_done, mult_out, ahead) = refs[:-4], refs[-4:]
+
+    @pl.when(early())
+    def _():
+        mult_out[...] = mult_done[...]
+        ahead[...] = ahead_done[...]
+
+    @pl.when(jnp.logical_not(early()))
+    def _():
+        rest_update(*ins, mult_out, ahead)
 
 
 def rest_last_kernel(size, high, low, mult_s, mult_n, gap, floor, mult_out, residual_out, settled, left, done):
@@ -273,8 +290,9 @@
 
 def lift_kernel(n, m, cap, size, *refs):
     parts = refs[:m + 1]
-    ins, (mult_s, mult_n, image), sends = refs[m + 1:m + 8], refs[m + 8:m + 11], refs[m + 11:]
-    basis, trial_s, trial_n, floor, high, low, pack = ins
+    ins, outs, sends = refs[m + 1:m + 11], refs[m + 11:m + 16], refs[m + 16:]
+    basis, trial_s, trial_n, floor, high, low, pack, rest_high, rest_low, gap = ins
+    mult_s, mult_n, image, mult_done, ahead_done = outs
     solved = parts[0][...]
     for part in parts[1:]:
         solved = solved + part[...]
@@ -290,6 +308,12 @@
     value = product((high[...], low[...]), split(jnp.concatenate([first, rest], axis=0)))
     image[...] = value
     send(cap, pack[...], value, sends)
+
+    @pl.when(early())
+    def _():
+        rest_update(
+            size, rest_high, rest_low, mult_s, mult_n, gap, floor, high, low, pack, mult_done, ahead_done
+        )
 
 
 def sweep_kernel(times, cap, size, *refs):
@@ -377,7 +401,7 @@
     size = interface_size
     coarse_order, part_order = far_first(wide), far_first(narrow)
     half, half_back, middle = half_first(wide, False), half_first(wide, True), middle_first(wide)
-    orders = ((half_back, half, middle), (half_back, half, half_back))
+    orders = ((middle, half, middle), (half_back, half, half_back))
     sent = [shape(cap, loads)] * n
     full = 2 * order * loads
 
@@ -488,10 +512,12 @@
             name="tile",
         )
         parts = [own] + swap_all(parts, "narrow", narrow, part_order)
-        mult_s, mult_n, image, *sends = call(
+        mult_s, mult_n, image, mult_done, ahead_done, *sends = call(
             functools.partial(lift_kernel, n, m, cap),
-            (size, *parts, basis, trial_s, trial_n, floor, top_high, top_low, pack),
-            [shape(shared, loads), shape(rest, loads), shape(shared, loads)] + sent,
+            (size, *parts, basis, trial_s, trial_n, floor, top_high, top_low, pack, high, low, gap),
+            [shape(shared, loads), shape(rest, loads), shape(shared, loads)]
+            + [shape(rest, loads), shape(shared + padded, loads)]
+            + sent,
             flops=3 * full * shared,
             moved=4 * order * shared,
             name="lift",
@@ -535,8 +561,8 @@
                 )
                 return tuple(out[None] for out in outs)
             mult_n, ahead = call(
-                rest_kernel,
-                (*ins, top_high, top_low, pack),
+                rest_late_kernel if inner == 1 else rest_update,
+                (*ins, top_high, top_low, pack) + ((mult_done, ahead_done) if inner == 1 else ()),
                 [shape(rest, loads), shape(shared + padded, loads)],
                 flops=3 * full * order,
                 moved=4 * order * order,

time: 90.5 us -> 93.2 us (1.030)
  waiting for transfers between devices: 30.2 us -> 32.8 us
    ppermute x30, waiting for transfers between devices: 30.2 us -> 32.8 us  [swap(): return lax.ppermute(block, axis, [(i, i ^ d) for i in range(count)])]
  transfers between devices with their start and end apart: 30 -> 30, of which waited for: 24 -> 23; matrix products, arithmetic and copies ran while one was open for 0% -> 0% of each run, Pallas kernels for 13% -> 12%
where the time goes in v10:
time: 93.2 us; the launch traced here: 93.1 us
  starting transfers between devices  39 us (42%)
  waiting for transfers between devices  32.8 us (35%)
  Pallas kernels  19.5 us (21%)
  between operations  1.75 us (2%)
    ppermute x30, starting transfers between devices, swap(): return lax.ppermute(block, axis, [(i, i ^ d) for i in range(count)])  39 us
    ppermute x30, waiting for transfers between devices, swap(): return lax.ppermute(block, axis, [(i, i ^ d) for i in range(count)])  32.8 us
    pallas_call x25, Pallas kernels, call(): pl.pallas_call(body, out_shape=outs, grid=grid, in_specs=in_specs, out_sp...  19.5 us
  transfers between devices with their start and end apart: 30, of which 23 were waited for; matrix products, arithmetic and copies ran while one was open for 0% of the time, Pallas kernels for 12%

profile of v10, /device:TPU:0, one launch (start us, length us, event | category | flops | bytes accessed | tf_op | source)
XLA Modules:
  0.0 93.1 jit_solution(3921380282553438409)
XLA Ops:
  0.7 2.1 %first.1 = (bf16[256,256]{1,0:T(8,128)(2,1)S(1)}, bf16[256,768]{1,0:T(8,128)(2,1)S(1)}, bf16[256,384]{1,0:T(8,128)(2,1)S(1)}, bf16[256,1024]{1,0:T(8,128)(2,1)S(...) custom-call(s32[1,256]{1,0:T(1,128)} %bitcast.34, ...), custom_call_target="tpu_custom_call" | custom-call | flops 201326592 | bytes 2097152 | tf_op jit(solution)/shard_map/first/pallas_call | solution.py:49
  2.8 5.1 %collective-permute-start = (f32[264,128]{1,0:T(8,128)S(1)}, f32[264,128]{1,0:T(8,128)S(1)}, u32[]{:S(2)}, u32[]{:S(2)}) collective-permute-start(f32[264,128]{1,0:T(8,128)S(1)} %get-tuple-element.85), channel_id=1, source_target_pairs={{0,12},{4,8},{8,4},{12,0},{1,13},{5,9},{9,5},{13,1},{2,14},{6,10},... | collective-permute-start | bytes 405512 | tf_op jit(solution)/shard_map/ppermute | solution.py:350
  7.9 0.6 collective-permute-start.2
  9.4 2.0 %rest_start.1 = (f32[768,128]{1,0:T(8,128)S(1)}, f32[64,128]{1,0:T(8,128)S(1)}, bf16[768,1024]{1,0:T(8,128)(2,1)S(1)}, bf16[768,1024]{1,0:T(8,128)(2,1)S(1)}) custom-call(s32[1]{0:T(128)S(6)} %copy.15.size.refs_0_, f32[1024,1024]{1,0:T(8,128)S(1)} %bitcast.22, f32[1024,128]{1,0:T(8,128)S(1)} %bitcast.24, f32[1024,128]{1,0:T(8,128)S(1)} %bitcast.25, ...), custom_call_target="tpu_custom_call" | custom-call | flops 603979776 | bytes 6291456 | tf_op jit(solution)/shard_map/rest_start/pallas_call | solution.py:49
  11.4 0.9 collective-permute-done.refs_0_
  12.3 3.1 %collective-permute-done.1.refs_1_ = f32[264,128]{1,0:T(8,128)S(1)} collective-permute-done((f32[264,128]{1,0:T(8,128)S(1)}, f32[264,128]{1,0:T(8,128)S(1)}, u32[]{:S(2)}, u32[]{:S(2)}) %collective-permute-start.1) | collective-permute-done | bytes 135200 | tf_op jit(solution)/shard_map/ppermute | solution.py:350
  15.4 3.8 %collective-permute-done.2.refs_2_ = f32[264,128]{1,0:T(8,128)S(1)} collective-permute-done((f32[264,128]{1,0:T(8,128)S(1)}, f32[264,128]{1,0:T(8,128)S(1)}, u32[]{:S(2)}, u32[]{:S(2)}) %collective-permute-start.2) | collective-permute-done | bytes 135200 | tf_op jit(solution)/shard_map/ppermute | solution.py:350
  19.3 0.5 coarse.2
  19.8 2.5 %collective-permute-start.3 = (f32[64,128]{1,0:T(8,128)S(1)}, f32[64,128]{1,0:T(8,128)S(1)}, u32[]{:S(2)}, u32[]{:S(2)}) collective-permute-start(f32[64,128]{1,0:T(8,128)S(1)} %get-tuple-element.93), channel_id=1, source_target_pairs={{0,12},{4,8},{8,4},{12,0},{1,13},{5,9},{9,5},{13,1},{2,14},{6,10},... | collective-permute-start | bytes 98312 | tf_op jit(solution)/shard_map/ppermute | solution.py:350
  22.3 1.9 %collective-permute-start.5 = (f32[64,128]{1,0:T(8,128)S(1)}, f32[64,128]{1,0:T(8,128)S(1)}, u32[]{:S(2)}, u32[]{:S(2)}) collective-permute-start(f32[64,128]{1,0:T(8,128)S(1)} %get-tuple-element.95), channel_id=1, source_target_pairs={{0,4},{4,0},{8,12},{12,8},{1,5},{5,1},{9,13},{13,9},{2,6},{6,2},{1... | collective-permute-start | bytes 98312 | tf_op jit(solution)/shard_map/ppermute | solution.py:350
  24.2 0.4 prepare.1
  24.6 0.9 collective-permute-done.3.refs_1_
  25.5 1.6 %collective-permute-done.4.refs_2_ = f32[64,128]{1,0:T(8,128)S(1)} collective-permute-done((f32[64,128]{1,0:T(8,128)S(1)}, f32[64,128]{1,0:T(8,128)S(1)}, u32[]{:S(2)}, u32[]{:S(2)}) %collective-permute-start.4) | collective-permute-done | bytes 32800 | tf_op jit(solution)/shard_map/ppermute | solution.py:350
  27.4 1.6 %collective-permute-start.7 = (f32[64,128]{1,0:T(8,128)S(1)}, f32[64,128]{1,0:T(8,128)S(1)}, u32[]{:S(2)}, u32[]{:S(2)}) collective-permute-start(f32[64,128]{1,0:T(8,128)S(1)} %get-tuple-element.98), channel_id=1, source_target_pairs={{0,2},{1,3},{2,0},{3,1},{4,6},{5,7},{6,4},{7,5},{8,10},{9,11},{10,... | collective-permute-start | bytes 98312 | tf_op jit(solution)/shard_map/ppermute | solution.py:350
  29.0 0.3 collective-permute-start.8
  29.3 0.3 pack.1
  29.6 1.5 %collective-permute-done.6.refs_1_ = f32[64,128]{1,0:T(8,128)S(1)} collective-permute-done((f32[64,128]{1,0:T(8,128)S(1)}, f32[64,128]{1,0:T(8,128)S(1)}, u32[]{:S(2)}, u32[]{:S(2)}) %collective-permute-start.6) | collective-permute-done | bytes 32800 | tf_op jit(solution)/shard_map/ppermute | solution.py:350
  31.1 0.4 collective-permute-done.7.refs_2_
  31.5 1.0 %lift.2 = (f32[256,128]{1,0:T(8,128)S(1)}, f32[768,128]{1,0:T(8,128)S(1)}, f32[256,128]{1,0:T(8,128)S(1)}, f32[768,128]{1,0:T(8,128)S(1)}, f32[640,128]{1,0:T(8,...) custom-call(s32[1]{0:T(128)S(6)} %copy.15.size.refs_0_, ...), custom_call_target="tpu_custom_call" | custom-call | flops 201326592 | bytes 1048576 | tf_op jit(solution)/shard_map/lift/pallas_call | solution.py:49
  32.5 2.1 %collective-permute-start.9 = (f32[128,128]{1,0:T(8,128)S(1)}, f32[128,128]{1,0:T(8,128)S(1)}, u32[]{:S(2)}, u32[]{:S(2)}) collective-permute-start(f32[128,128]{1,0:T(8,128)S(1)} %get-tuple-element.109), channel_id=1, source_target_pairs={{0,8},{4,12},{8,0},{12,4},{1,9},{5,13},{9,1},{13,5},{2,10},{6,14},... | collective-permute-start | bytes 196616 | tf_op jit(solution)/shard_map/ppermute | solution.py:350
  34.6 0.3 collective-permute-start.10
  34.9 2.0 %collective-permute-start.11 = (f32[128,128]{1,0:T(8,128)S(1)}, f32[128,128]{1,0:T(8,128)S(1)}, u32[]{:S(2)}, u32[]{:S(2)}) collective-permute-start(f32[128,128]{1,0:T(8,128)S(1)} %get-tuple-element.111), channel_id=1, source_target_pairs={{0,12},{4,8},{8,4},{12,0},{1,13},{5,9},{9,5},{13,1},{2,14},{6,10},... | collective-permute-start | bytes 196616 | tf_op jit(solution)/shard_map/ppermute | solution.py:350
  37.1 1.5 %rest.3 = (f32[768,128]{1,0:T(8,128)S(1)}, f32[640,128]{1,0:T(8,128)S(1)}) custom-call(s32[1]{0:T(128)S(6)} %copy.15.size.refs_0_, bf16[768,1024]{1,0:T(8,128)(2,1)S(1)} %get-tuple-element.107.refs_11_.refs_1_.high, bf16[768,1024]{1,0:T(8,128)(2,1)S(1)} %get-tuple-element.108.refs_12_.refs_2_.low, f32[256,128]{1,0:T(8,128)S(1)} %get-tuple-element.114.refs_3_.refs_5_, ...), custom_call_target="tpu_custom_call" | custom-call | flops 805306368 | bytes 4194304 | tf_op jit(solution)/shard_map/rest/pallas_call | solution.py:49
  38.6 0.4 collective-permute-done.9.refs_0_
  39.0 1.0 %collective-permute-done.10.refs_1_ = f32[128,128]{1,0:T(8,128)S(1)} collective-permute-done((f32[128,128]{1,0:T(8,128)S(1)}, f32[128,128]{1,0:T(8,128)S(1)}, u32[]{:S(2)}, u32[]{:S(2)}) %collective-permute-start.10) | collective-permute-done | bytes 65568 | tf_op jit(solution)/shard_map/ppermute | solution.py:350
  40.1 1.7 %collective-permute-done.11.refs_2_ = f32[128,128]{1,0:T(8,128)S(1)} collective-permute-done((f32[128,128]{1,0:T(8,128)S(1)}, f32[128,128]{1,0:T(8,128)S(1)}, u32[]{:S(2)}, u32[]{:S(2)}) %collective-permute-start.11) | collective-permute-done | bytes 65568 | tf_op jit(solution)/shard_map/ppermute | solution.py:350
  41.8 0.5 sweep.3
  42.3 2.1 %collective-permute-start.12 = (f32[128,128]{1,0:T(8,128)S(1)}, f32[128,128]{1,0:T(8,128)S(1)}, u32[]{:S(2)}, u32[]{:S(2)}) collective-permute-start(f32[128,128]{1,0:T(8,128)S(1)} %get-tuple-element.121), channel_id=1, source_target_pairs={{0,12},{4,8},{8,4},{12,0},{1,13},{5,9},{9,5},{13,1},{2,14},{6,10},... | collective-permute-start | bytes 196616 | tf_op jit(solution)/shard_map/ppermute | solution.py:350
  44.7 2.1 %collective-permute-start.14 = (f32[128,128]{1,0:T(8,128)S(1)}, f32[128,128]{1,0:T(8,128)S(1)}, u32[]{:S(2)}, u32[]{:S(2)}) collective-permute-start(f32[128,128]{1,0:T(8,128)S(1)} %get-tuple-element.123), channel_id=1, source_target_pairs={{0,8},{4,12},{8,0},{12,4},{1,9},{5,13},{9,1},{13,5},{2,10},{6,14},... | collective-permute-start | bytes 196616 | tf_op jit(solution)/shard_map/ppermute | solution.py:350
  46.9 1.5 %rest.4 = (f32[768,128]{1,0:T(8,128)S(1)}, f32[640,128]{1,0:T(8,128)S(1)}) custom-call(s32[1]{0:T(128)S(6)} %copy.15.size.refs_0_, bf16[768,1024]{1,0:T(8,128)(2,1)S(1)} %get-tuple-element.107.refs_11_.refs_1_.high, bf16[768,1024]{1,0:T(8,128)(2,1)S(1)} %get-tuple-element.108.refs_12_.refs_2_.low, f32[256,128]{1,0:T(8,128)S(1)} %get-tuple-element.125.mult_s.refs_5_, ...), custom_call_target="tpu_custom_call" | custom-call | flops 805306368 | bytes 4194304 | tf_op jit(solution)/shard_map/rest/pallas_call | solution.py:49
  48.4 0.5 collective-permute-done.12.refs_0_
  48.9 1.7 %collective-permute-done.13.refs_1_ = f32[128,128]{1,0:T(8,128)S(1)} collective-permute-done((f32[128,128]{1,0:T(8,128)S(1)}, f32[128,128]{1,0:T(8,128)S(1)}, u32[]{:S(2)}, u32[]{:S(2)}) %collective-permute-start.13) | collective-permute-done | bytes 65568 | tf_op jit(solution)/shard_map/ppermute | solution.py:350
  50.6 0.9 %collective-permute-done.14.refs_2_ = f32[128,128]{1,0:T(8,128)S(1)} collective-permute-done((f32[128,128]{1,0:T(8,128)S(1)}, f32[128,128]{1,0:T(8,128)S(1)}, u32[]{:S(2)}, u32[]{:S(2)}) %collective-permute-start.14) | collective-permute-done | bytes 65568 | tf_op jit(solution)/shard_map/ppermute | solution.py:350
  51.6 0.5 sweep.4
  52.1 0.9 collective-permute-start.15
  52.9 1.6 %collective-permute-start.16 = (f32[128,128]{1,0:T(8,128)S(1)}, f32[128,128]{1,0:T(8,128)S(1)}, u32[]{:S(2)}, u32[]{:S(2)}) collective-permute-start(f32[128,128]{1,0:T(8,128)S(1)} %get-tuple-element.129), channel_id=1, source_target_pairs={{0,12},{4,8},{8,4},{12,0},{1,13},{5,9},{9,5},{13,1},{2,14},{6,10},... | collective-permute-start | bytes 196616 | tf_op jit(solution)/shard_map/ppermute | solution.py:350
  54.6 1.1 %collective-permute-start.17 = (f32[128,128]{1,0:T(8,128)S(1)}, f32[128,128]{1,0:T(8,128)S(1)}, u32[]{:S(2)}, u32[]{:S(2)}) collective-permute-start(f32[128,128]{1,0:T(8,128)S(1)} %get-tuple-element.130), channel_id=1, source_target_pairs={{0,4},{4,0},{8,12},{12,8},{1,5},{5,1},{9,13},{13,9},{2,6},{6,2},{1... | collective-permute-start | bytes 196616 | tf_op jit(solution)/shard_map/ppermute | solution.py:350
  55.8 1.1 %rest_first.1 = (f32[768,128]{1,0:T(8,128)S(1)}, f32[64,128]{1,0:T(8,128)S(1)}) custom-call(s32[1]{0:T(128)S(6)} %copy.15.size.refs_0_, bf16[768,1024]{1,0:T(8,128)(2,1)S(1)} %get-tuple-element.107.refs_11_.refs_1_.high, bf16[768,1024]{1,0:T(8,128)(2,1)S(1)} %get-tuple-element.108.refs_12_.refs_2_.low, f32[256,128]{1,0:T(8,128)S(1)} %get-tuple-element.132.mult_s.refs_5_, ...), custom_call_target="tpu_custom_call" | custom-call | flops 603979776 | bytes 3145728 | tf_op jit(solution)/shard_map/rest_first/pallas_call | solution.py:49
  57.0 2.6 %collective-permute-done.15.refs_0_ = f32[128,128]{1,0:T(8,128)S(1)} collective-permute-done((f32[128,128]{1,0:T(8,128)S(1)}, f32[128,128]{1,0:T(8,128)S(1)}, u32[]{:S(2)}, u32[]{:S(2)}) %collective-permute-start.15) | collective-permute-done | bytes 65568 | tf_op jit(solution)/shard_map/ppermute | solution.py:350
  59.6 0.4 collective-permute-done.17.refs_2_
  60.0 0.4 coarse.3
  60.4 1.8 %collective-permute-start.18 = (f32[64,128]{1,0:T(8,128)S(1)}, f32[64,128]{1,0:T(8,128)S(1)}, u32[]{:S(2)}, u32[]{:S(2)}) collective-permute-start(f32[64,128]{1,0:T(8,128)S(1)} %get-tuple-element.136), channel_id=1, source_target_pairs={{0,12},{4,8},{8,4},{12,0},{1,13},{5,9},{9,5},{13,1},{2,14},{6,10},... | collective-permute-start | bytes 98312 | tf_op jit(solution)/shard_map/ppermute | solution.py:350
  62.2 0.6 collective-permute-start.19
  62.8 2.1 %collective-permute-start.20 = (f32[64,128]{1,0:T(8,128)S(1)}, f32[64,128]{1,0:T(8,128)S(1)}, u32[]{:S(2)}, u32[]{:S(2)}) collective-permute-start(f32[64,128]{1,0:T(8,128)S(1)} %get-tuple-element.138), channel_id=1, source_target_pairs={{0,4},{4,0},{8,12},{12,8},{1,5},{5,1},{9,13},{13,9},{2,6},{6,2},{1... | collective-permute-start | bytes 98312 | tf_op jit(solution)/shard_map/ppermute | solution.py:350
  64.9 1.3 %collective-permute-done.18.refs_1_ = f32[64,128]{1,0:T(8,128)S(1)} collective-permute-done((f32[64,128]{1,0:T(8,128)S(1)}, f32[64,128]{1,0:T(8,128)S(1)}, u32[]{:S(2)}, u32[]{:S(2)}) %collective-permute-start.18) | collective-permute-done | bytes 32800 | tf_op jit(solution)/shard_map/ppermute | solution.py:350
  66.2 0.9 collective-permute-done.19.refs_2_
  67.5 1.4 %collective-permute-start.22 = (f32[64,128]{1,0:T(8,128)S(1)}, f32[64,128]{1,0:T(8,128)S(1)}, u32[]{:S(2)}, u32[]{:S(2)}) collective-permute-start(f32[64,128]{1,0:T(8,128)S(1)} %get-tuple-element.141), channel_id=1, source_target_pairs={{0,2},{1,3},{2,0},{3,1},{4,6},{5,7},{6,4},{7,5},{8,10},{9,11},{10,... | collective-permute-start | bytes 98312 | tf_op jit(solution)/shard_map/ppermute | solution.py:350
  68.9 0.4 collective-permute-start.23
  69.3 1.8 %collective-permute-done.21.refs_1_ = f32[64,128]{1,0:T(8,128)S(1)} collective-permute-done((f32[64,128]{1,0:T(8,128)S(1)}, f32[64,128]{1,0:T(8,128)S(1)}, u32[]{:S(2)}, u32[]{:S(2)}) %collective-permute-start.21) | collective-permute-done | bytes 32800 | tf_op jit(solution)/shard_map/ppermute | solution.py:350
  71.1 0.4 collective-permute-done.22.refs_2_
  71.5 1.2 %lift.3 = (f32[256,128]{1,0:T(8,128)S(1)}, f32[768,128]{1,0:T(8,128)S(1)}, f32[256,128]{1,0:T(8,128)S(1)}, f32[768,128]{1,0:T(8,128)S(1)}, f32[640,128]{1,0:T(8,...) custom-call(s32[1]{0:T(128)S(6)} %copy.15.size.refs_0_, ...), custom_call_target="tpu_custom_call" | custom-call | flops 201326592 | bytes 1048576 | tf_op jit(solution)/shard_map/lift/pallas_call | solution.py:49
  72.6 2.0 %collective-permute-start.24 = (f32[128,128]{1,0:T(8,128)S(1)}, f32[128,128]{1,0:T(8,128)S(1)}, u32[]{:S(2)}, u32[]{:S(2)}) collective-permute-start(f32[128,128]{1,0:T(8,128)S(1)} %get-tuple-element.145), channel_id=1, source_target_pairs={{0,8},{4,12},{8,0},{12,4},{1,9},{5,13},{9,1},{13,5},{2,10},{6,14},... | collective-permute-start | bytes 196616 | tf_op jit(solution)/shard_map/ppermute | solution.py:350
  74.6 0.6 collective-permute-start.25
  75.3 1.8 %collective-permute-start.26 = (f32[128,128]{1,0:T(8,128)S(1)}, f32[128,128]{1,0:T(8,128)S(1)}, u32[]{:S(2)}, u32[]{:S(2)}) collective-permute-start(f32[128,128]{1,0:T(8,128)S(1)} %get-tuple-element.147), channel_id=1, source_target_pairs={{0,12},{4,8},{8,4},{12,0},{1,13},{5,9},{9,5},{13,1},{2,14},{6,10},... | collective-permute-start | bytes 196616 | tf_op jit(solution)/shard_map/ppermute | solution.py:350
  77.3 1.5 %rest.5 = (f32[768,128]{1,0:T(8,128)S(1)}, f32[640,128]{1,0:T(8,128)S(1)}) custom-call(s32[1]{0:T(128)S(6)} %copy.15.size.refs_0_, bf16[768,1024]{1,0:T(8,128)(2,1)S(1)} %get-tuple-element.107.refs_11_.refs_1_.high, bf16[768,1024]{1,0:T(8,128)(2,1)S(1)} %get-tuple-element.108.refs_12_.refs_2_.low, f32[256,128]{1,0:T(8,128)S(1)} %get-tuple-element.149.refs_3_.refs_5_, ...), custom_call_target="tpu_custom_call" | custom-call | flops 805306368 | bytes 4194304 | tf_op jit(solution)/shard_map/rest/pallas_call | solution.py:49
  78.8 0.9 collective-permute-done.25.refs_1_
  79.7 2.4 %collective-permute-done.26.refs_2_ = f32[128,128]{1,0:T(8,128)S(1)} collective-permute-done((f32[128,128]{1,0:T(8,128)S(1)}, f32[128,128]{1,0:T(8,128)S(1)}, u32[]{:S(2)}, u32[]{:S(2)}) %collective-permute-start.26) | collective-permute-done | bytes 65568 | tf_op jit(solution)/shard_map/ppermute | solution.py:350
  82.1 0.5 sweep.5
  82.7 1.8 %collective-permute-start.27 = (f32[128,128]{1,0:T(8,128)S(1)}, f32[128,128]{1,0:T(8,128)S(1)}, u32[]{:S(2)}, u32[]{:S(2)}) collective-permute-start(f32[128,128]{1,0:T(8,128)S(1)} %get-tuple-element.154), channel_id=1, source_target_pairs={{0,8},{4,12},{8,0},{12,4},{1,9},{5,13},{9,1},{13,5},{2,10},{6,14},... | collective-permute-start | bytes 196616 | tf_op jit(solution)/shard_map/ppermute | solution.py:350
  84.5 1.7 %collective-permute-start.28 = (f32[128,128]{1,0:T(8,128)S(1)}, f32[128,128]{1,0:T(8,128)S(1)}, u32[]{:S(2)}, u32[]{:S(2)}) collective-permute-start(f32[128,128]{1,0:T(8,128)S(1)} %get-tuple-element.155), channel_id=1, source_target_pairs={{0,12},{4,8},{8,4},{12,0},{1,13},{5,9},{9,5},{13,1},{2,14},{6,10},... | collective-permute-start | bytes 196616 | tf_op jit(solution)/shard_map/ppermute | solution.py:350
  86.5 1.9 %rest_last.1 = (f32[1024,128]{1,0:T(8,128)}, f32[1024,128]{1,0:T(8,128)}) custom-call(s32[1]{0:T(128)S(6)} %copy.15.size.refs_0_, bf16[768,1024]{1,0:T(8,128)(2,1)S(1)} %get-tuple-element.107.refs_11_.refs_1_.high, bf16[768,1024]{1,0:T(8,128)(2,1)S(1)} %get-tuple-element.108.refs_12_.refs_2_.low, f32[256,128]{1,0:T(8,128)S(1)} %get-tuple-element.158.mult_s.refs_5_, ...), custom_call_target="tpu_custom_call" | custom-call | flops 603979776 | bytes 3145728 | tf_op jit(solution)/shard_map/rest_last/pallas_call | solution.py:49
  88.4 2.9 %collective-permute-done.27.refs_0_ = f32[128,128]{1,0:T(8,128)S(1)} collective-permute-done((f32[128,128]{1,0:T(8,128)S(1)}, f32[128,128]{1,0:T(8,128)S(1)}, u32[]{:S(2)}, u32[]{:S(2)}) %collective-permute-start.27) | collective-permute-done | bytes 65568 | tf_op jit(solution)/shard_map/ppermute | solution.py:350
  91.2 0.7 collective-permute-done.29.refs_2_
  92.0 0.9 %last.1 = (f32[1024,128]{1,0:T(8,128)}, f32[1024,128]{1,0:T(8,128)}) custom-call(s32[1]{0:T(128)S(6)} %copy.15.size.refs_0_, f32[128,128]{1,0:T(8,128)S(1)} %collective-permute-done.27.refs_0_, f32[128,128]{1,0:T(8,128)S(1)} %collective-permute-done.28.refs_1_, ...), custom_call_target="tpu_custom_call", output_to_operand_aliasing={{0}: (8, {}), {1}: (9, {})} | custom-call | flops 75497472 | bytes 196608 | tf_op jit(solution)/shard_map/last/pallas_call | solution.py:49
  (33 shorter events, 2.1 us)
Async XLA Ops:
  0.6 8.5 %copy-start = (f32[1,1024,128]{2,1,0:T(8,128)S(1)}, f32[1,1024,128]{2,1,0:T(8,128)}, u32[]{:S(2)}) copy-start(f32[1,1024,128]{2,1,0:T(8,128)} %param.12) | copy-start | bytes 1572868
  0.6 8.7 %copy-start.1 = (f32[1,1024,1024]{2,1,0:T(8,128)S(1)}, f32[1,1024,1024]{2,1,0:T(8,128)}, u32[]{:S(2)}) copy-start(f32[1,1024,1024]{2,1,0:T(8,128)} %param.9) | copy-start | bytes 12582916
  0.7 8.7 %copy-start.2 = (f32[1,1024,128]{2,1,0:T(8,128)S(1)}, f32[1,1024,128]{2,1,0:T(8,128)}, u32[]{:S(2)}) copy-start(f32[1,1024,128]{2,1,0:T(8,128)} %param.13) | copy-start | bytes 1572868
  0.7 8.7 %copy-start.3 = (f32[1,64,1024]{2,1,0:T(8,128)S(1)}, f32[1,64,1024]{2,1,0:T(8,128)}, u32[]{:S(2)}) copy-start(f32[1,64,1024]{2,1,0:T(8,128)} %param.11) | copy-start | bytes 786436
  2.8 9.6 %collective-permute-start = (f32[264,128]{1,0:T(8,128)S(1)}, f32[264,128]{1,0:T(8,128)S(1)}, u32[]{:S(2)}, u32[]{:S(2)}) collective-permute-start(f32[264,128]{1,0:T(8,128)S(1)} %get-tuple-element.85), channel_id=1, source_target_pairs={{0,12},{4,8},{8,4},{12,0},{1,13},{5,9},{9,5},{13,1},{2,14},{6,10},... | collective-permute-start | bytes 405512 | tf_op jit(solution)/shard_map/ppermute | solution.py:350
  7.9 7.6 %collective-permute-start.1 = (f32[264,128]{1,0:T(8,128)S(1)}, f32[264,128]{1,0:T(8,128)S(1)}, u32[]{:S(2)}, u32[]{:S(2)}) collective-permute-start(f32[264,128]{1,0:T(8,128)S(1)} %get-tuple-element.86), channel_id=1, source_target_pairs={{0,4},{4,0},{8,12},{12,8},{1,5},{5,1},{9,13},{13,9},{2,6},{6,2},{1... | collective-permute-start | bytes 405512 | tf_op jit(solution)/shard_map/ppermute | solution.py:350
  7.9 11.4 %collective-permute-start.2 = (f32[264,128]{1,0:T(8,128)S(1)}, f32[264,128]{1,0:T(8,128)S(1)}, u32[]{:S(2)}, u32[]{:S(2)}) collective-permute-start(f32[264,128]{1,0:T(8,128)S(1)} %get-tuple-element.87), channel_id=1, source_target_pairs={{0,8},{4,12},{8,0},{12,4},{1,9},{5,13},{9,1},{13,5},{2,10},{6,14},... | collective-permute-start | bytes 405512 | tf_op jit(solution)/shard_map/ppermute | solution.py:350
  11.4 12.8 %copy-start.4 = (f32[256,256]{1,0:T(8,128)S(1)}, f32[256,256]{1,0:T(8,128)}, u32[]{:S(2)}) copy-start(f32[256,256]{1,0:T(8,128)} %tile.3) | copy-start | bytes 786436
  11.4 12.8 %copy-start.5 = (s32[1,1024]{1,0:T(1,128)S(1)}, s32[1,1024]{1,0:T(1,128)}, u32[]{:S(2)}) copy-start(s32[1,1024]{1,0:T(1,128)} %contact.1) | copy-start | bytes 12292
  19.8 5.8 %collective-permute-start.3 = (f32[64,128]{1,0:T(8,128)S(1)}, f32[64,128]{1,0:T(8,128)S(1)}, u32[]{:S(2)}, u32[]{:S(2)}) collective-permute-start(f32[64,128]{1,0:T(8,128)S(1)} %get-tuple-element.93), channel_id=1, source_target_pairs={{0,12},{4,8},{8,4},{12,0},{1,13},{5,9},{9,5},{13,1},{2,14},{6,10},... | collective-permute-start | bytes 98312 | tf_op jit(solution)/shard_map/ppermute | solution.py:350
  22.3 4.8 %collective-permute-start.4 = (f32[64,128]{1,0:T(8,128)S(1)}, f32[64,128]{1,0:T(8,128)S(1)}, u32[]{:S(2)}, u32[]{:S(2)}) collective-permute-start(f32[64,128]{1,0:T(8,128)S(1)} %get-tuple-element.94), channel_id=1, source_target_pairs={{0,8},{4,12},{8,0},{12,4},{1,9},{5,13},{9,1},{13,5},{2,10},{6,14},... | collective-permute-start | bytes 98312 | tf_op jit(solution)/shard_map/ppermute | solution.py:350
  22.3 4.8 %collective-permute-start.5 = (f32[64,128]{1,0:T(8,128)S(1)}, f32[64,128]{1,0:T(8,128)S(1)}, u32[]{:S(2)}, u32[]{:S(2)}) collective-permute-start(f32[64,128]{1,0:T(8,128)S(1)} %get-tuple-element.95), channel_id=1, source_target_pairs={{0,4},{4,0},{8,12},{12,8},{1,5},{5,1},{9,13},{13,9},{2,6},{6,2},{1... | collective-permute-start | bytes 98312 | tf_op jit(solution)/shard_map/ppermute | solution.py:350
  27.4 3.7 %collective-permute-start.6 = (f32[64,128]{1,0:T(8,128)S(1)}, f32[64,128]{1,0:T(8,128)S(1)}, u32[]{:S(2)}, u32[]{:S(2)}) collective-permute-start(f32[64,128]{1,0:T(8,128)S(1)} %get-tuple-element.97), channel_id=1, source_target_pairs={{0,3},{1,2},{2,1},{3,0},{4,7},{5,6},{6,5},{7,4},{8,11},{9,10},{10,... | collective-permute-start | bytes 98312 | tf_op jit(solution)/shard_map/ppermute | solution.py:350
  27.4 4.0 %collective-permute-start.7 = (f32[64,128]{1,0:T(8,128)S(1)}, f32[64,128]{1,0:T(8,128)S(1)}, u32[]{:S(2)}, u32[]{:S(2)}) collective-permute-start(f32[64,128]{1,0:T(8,128)S(1)} %get-tuple-element.98), channel_id=1, source_target_pairs={{0,2},{1,3},{2,0},{3,1},{4,6},{5,7},{6,4},{7,5},{8,10},{9,11},{10,... | collective-permute-start | bytes 98312 | tf_op jit(solution)/shard_map/ppermute | solution.py:350
  29.0 2.5 %collective-permute-start.8 = (f32[64,128]{1,0:T(8,128)S(1)}, f32[64,128]{1,0:T(8,128)S(1)}, u32[]{:S(2)}, u32[]{:S(2)}) collective-permute-start(f32[64,128]{1,0:T(8,128)S(1)} %get-tuple-element.99), channel_id=1, source_target_pairs={{0,1},{1,0},{2,3},{3,2},{4,5},{5,4},{6,7},{7,6},{8,9},{9,8},{10,11... | collective-permute-start | bytes 98312 | tf_op jit(solution)/shard_map/ppermute | solution.py:350
  32.5 6.6 %collective-permute-start.9 = (f32[128,128]{1,0:T(8,128)S(1)}, f32[128,128]{1,0:T(8,128)S(1)}, u32[]{:S(2)}, u32[]{:S(2)}) collective-permute-start(f32[128,128]{1,0:T(8,128)S(1)} %get-tuple-element.109), channel_id=1, source_target_pairs={{0,8},{4,12},{8,0},{12,4},{1,9},{5,13},{9,1},{13,5},{2,10},{6,14},... | collective-permute-start | bytes 196616 | tf_op jit(solution)/shard_map/ppermute | solution.py:350
  34.6 5.5 %collective-permute-start.10 = (f32[128,128]{1,0:T(8,128)S(1)}, f32[128,128]{1,0:T(8,128)S(1)}, u32[]{:S(2)}, u32[]{:S(2)}) collective-permute-start(f32[128,128]{1,0:T(8,128)S(1)} %get-tuple-element.110), channel_id=1, source_target_pairs={{0,4},{4,0},{8,12},{12,8},{1,5},{5,1},{9,13},{13,9},{2,6},{6,2},{1... | collective-permute-start | bytes 196616 | tf_op jit(solution)/shard_map/ppermute | solution.py:350
  34.9 6.8 %collective-permute-start.11 = (f32[128,128]{1,0:T(8,128)S(1)}, f32[128,128]{1,0:T(8,128)S(1)}, u32[]{:S(2)}, u32[]{:S(2)}) collective-permute-start(f32[128,128]{1,0:T(8,128)S(1)} %get-tuple-element.111), channel_id=1, source_target_pairs={{0,12},{4,8},{8,4},{12,0},{1,13},{5,9},{9,5},{13,1},{2,14},{6,10},... | collective-permute-start | bytes 196616 | tf_op jit(solution)/shard_map/ppermute | solution.py:350
  42.3 6.6 %collective-permute-start.12 = (f32[128,128]{1,0:T(8,128)S(1)}, f32[128,128]{1,0:T(8,128)S(1)}, u32[]{:S(2)}, u32[]{:S(2)}) collective-permute-start(f32[128,128]{1,0:T(8,128)S(1)} %get-tuple-element.121), channel_id=1, source_target_pairs={{0,12},{4,8},{8,4},{12,0},{1,13},{5,9},{9,5},{13,1},{2,14},{6,10},... | collective-permute-start | bytes 196616 | tf_op jit(solution)/shard_map/ppermute | solution.py:350
  44.4 6.2 %collective-permute-start.13 = (f32[128,128]{1,0:T(8,128)S(1)}, f32[128,128]{1,0:T(8,128)S(1)}, u32[]{:S(2)}, u32[]{:S(2)}) collective-permute-start(f32[128,128]{1,0:T(8,128)S(1)} %get-tuple-element.122), channel_id=1, source_target_pairs={{0,4},{4,0},{8,12},{12,8},{1,5},{5,1},{9,13},{13,9},{2,6},{6,2},{1... | collective-permute-start | bytes 196616 | tf_op jit(solution)/shard_map/ppermute | solution.py:350
  44.7 6.9 %collective-permute-start.14 = (f32[128,128]{1,0:T(8,128)S(1)}, f32[128,128]{1,0:T(8,128)S(1)}, u32[]{:S(2)}, u32[]{:S(2)}) collective-permute-start(f32[128,128]{1,0:T(8,128)S(1)} %get-tuple-element.123), channel_id=1, source_target_pairs={{0,8},{4,12},{8,0},{12,4},{1,9},{5,13},{9,1},{13,5},{2,10},{6,14},... | collective-permute-start | bytes 196616 | tf_op jit(solution)/shard_map/ppermute | solution.py:350
  52.1 7.5 %collective-permute-start.15 = (f32[128,128]{1,0:T(8,128)S(1)}, f32[128,128]{1,0:T(8,128)S(1)}, u32[]{:S(2)}, u32[]{:S(2)}) collective-permute-start(f32[128,128]{1,0:T(8,128)S(1)} %get-tuple-element.128), channel_id=1, source_target_pairs={{0,8},{4,12},{8,0},{12,4},{1,9},{5,13},{9,1},{13,5},{2,10},{6,14},... | collective-permute-start | bytes 196616 | tf_op jit(solution)/shard_map/ppermute | solution.py:350
  52.9 6.7 %collective-permute-start.16 = (f32[128,128]{1,0:T(8,128)S(1)}, f32[128,128]{1,0:T(8,128)S(1)}, u32[]{:S(2)}, u32[]{:S(2)}) collective-permute-start(f32[128,128]{1,0:T(8,128)S(1)} %get-tuple-element.129), channel_id=1, source_target_pairs={{0,12},{4,8},{8,4},{12,0},{1,13},{5,9},{9,5},{13,1},{2,14},{6,10},... | collective-permute-start | bytes 196616 | tf_op jit(solution)/shard_map/ppermute | solution.py:350
  54.6 5.4 %collective-permute-start.17 = (f32[128,128]{1,0:T(8,128)S(1)}, f32[128,128]{1,0:T(8,128)S(1)}, u32[]{:S(2)}, u32[]{:S(2)}) collective-permute-start(f32[128,128]{1,0:T(8,128)S(1)} %get-tuple-element.130), channel_id=1, source_target_pairs={{0,4},{4,0},{8,12},{12,8},{1,5},{5,1},{9,13},{13,9},{2,6},{6,2},{1... | collective-permute-start | bytes 196616 | tf_op jit(solution)/shard_map/ppermute | solution.py:350
  60.4 5.8 %collective-permute-start.18 = (f32[64,128]{1,0:T(8,128)S(1)}, f32[64,128]{1,0:T(8,128)S(1)}, u32[]{:S(2)}, u32[]{:S(2)}) collective-permute-start(f32[64,128]{1,0:T(8,128)S(1)} %get-tuple-element.136), channel_id=1, source_target_pairs={{0,12},{4,8},{8,4},{12,0},{1,13},{5,9},{9,5},{13,1},{2,14},{6,10},... | collective-permute-start | bytes 98312 | tf_op jit(solution)/shard_map/ppermute | solution.py:350
  62.2 4.9 %collective-permute-start.19 = (f32[64,128]{1,0:T(8,128)S(1)}, f32[64,128]{1,0:T(8,128)S(1)}, u32[]{:S(2)}, u32[]{:S(2)}) collective-permute-start(f32[64,128]{1,0:T(8,128)S(1)} %get-tuple-element.137), channel_id=1, source_target_pairs={{0,8},{4,12},{8,0},{12,4},{1,9},{5,13},{9,1},{13,5},{2,10},{6,14},... | collective-permute-start | bytes 98312 | tf_op jit(solution)/shard_map/ppermute | solution.py:350
  62.8 4.3 %collective-permute-start.20 = (f32[64,128]{1,0:T(8,128)S(1)}, f32[64,128]{1,0:T(8,128)S(1)}, u32[]{:S(2)}, u32[]{:S(2)}) collective-permute-start(f32[64,128]{1,0:T(8,128)S(1)} %get-tuple-element.138), channel_id=1, source_target_pairs={{0,4},{4,0},{8,12},{12,8},{1,5},{5,1},{9,13},{13,9},{2,6},{6,2},{1... | collective-permute-start | bytes 98312 | tf_op jit(solution)/shard_map/ppermute | solution.py:350
  67.4 3.7 %collective-permute-start.21 = (f32[64,128]{1,0:T(8,128)S(1)}, f32[64,128]{1,0:T(8,128)S(1)}, u32[]{:S(2)}, u32[]{:S(2)}) collective-permute-start(f32[64,128]{1,0:T(8,128)S(1)} %get-tuple-element.140), channel_id=1, source_target_pairs={{0,3},{1,2},{2,1},{3,0},{4,7},{5,6},{6,5},{7,4},{8,11},{9,10},{10,... | collective-permute-start | bytes 98312 | tf_op jit(solution)/shard_map/ppermute | solution.py:350
  67.5 4.0 %collective-permute-start.22 = (f32[64,128]{1,0:T(8,128)S(1)}, f32[64,128]{1,0:T(8,128)S(1)}, u32[]{:S(2)}, u32[]{:S(2)}) collective-permute-start(f32[64,128]{1,0:T(8,128)S(1)} %get-tuple-element.141), channel_id=1, source_target_pairs={{0,2},{1,3},{2,0},{3,1},{4,6},{5,7},{6,4},{7,5},{8,10},{9,11},{10,... | collective-permute-start | bytes 98312 | tf_op jit(solution)/shard_map/ppermute | solution.py:350
  68.9 2.5 %collective-permute-start.23 = (f32[64,128]{1,0:T(8,128)S(1)}, f32[64,128]{1,0:T(8,128)S(1)}, u32[]{:S(2)}, u32[]{:S(2)}) collective-permute-start(f32[64,128]{1,0:T(8,128)S(1)} %get-tuple-element.142), channel_id=1, source_target_pairs={{0,1},{1,0},{2,3},{3,2},{4,5},{5,4},{6,7},{7,6},{8,9},{9,8},{10,11... | collective-permute-start | bytes 98312 | tf_op jit(solution)/shard_map/ppermute | solution.py:350
  72.6 6.2 %collective-permute-start.24 = (f32[128,128]{1,0:T(8,128)S(1)}, f32[128,128]{1,0:T(8,128)S(1)}, u32[]{:S(2)}, u32[]{:S(2)}) collective-permute-start(f32[128,128]{1,0:T(8,128)S(1)} %get-tuple-element.145), channel_id=1, source_target_pairs={{0,8},{4,12},{8,0},{12,4},{1,9},{5,13},{9,1},{13,5},{2,10},{6,14},... | collective-permute-start | bytes 196616 | tf_op jit(solution)/shard_map/ppermute | solution.py:350
  74.6 5.1 %collective-permute-start.25 = (f32[128,128]{1,0:T(8,128)S(1)}, f32[128,128]{1,0:T(8,128)S(1)}, u32[]{:S(2)}, u32[]{:S(2)}) collective-permute-start(f32[128,128]{1,0:T(8,128)S(1)} %get-tuple-element.146), channel_id=1, source_target_pairs={{0,4},{4,0},{8,12},{12,8},{1,5},{5,1},{9,13},{13,9},{2,6},{6,2},{1... | collective-permute-start | bytes 196616 | tf_op jit(solution)/shard_map/ppermute | solution.py:350
  75.3 6.9 %collective-permute-start.26 = (f32[128,128]{1,0:T(8,128)S(1)}, f32[128,128]{1,0:T(8,128)S(1)}, u32[]{:S(2)}, u32[]{:S(2)}) collective-permute-start(f32[128,128]{1,0:T(8,128)S(1)} %get-tuple-element.147), channel_id=1, source_target_pairs={{0,12},{4,8},{8,4},{12,0},{1,13},{5,9},{9,5},{13,1},{2,14},{6,10},... | collective-permute-start | bytes 196616 | tf_op jit(solution)/shard_map/ppermute | solution.py:350
  82.7 8.6 %collective-permute-start.27 = (f32[128,128]{1,0:T(8,128)S(1)}, f32[128,128]{1,0:T(8,128)S(1)}, u32[]{:S(2)}, u32[]{:S(2)}) collective-permute-start(f32[128,128]{1,0:T(8,128)S(1)} %get-tuple-element.154), channel_id=1, source_target_pairs={{0,8},{4,12},{8,0},{12,4},{1,9},{5,13},{9,1},{13,5},{2,10},{6,14},... | collective-permute-start | bytes 196616 | tf_op jit(solution)/shard_map/ppermute | solution.py:350
  84.5 6.7 %collective-permute-start.28 = (f32[128,128]{1,0:T(8,128)S(1)}, f32[128,128]{1,0:T(8,128)S(1)}, u32[]{:S(2)}, u32[]{:S(2)}) collective-permute-start(f32[128,128]{1,0:T(8,128)S(1)} %get-tuple-element.155), channel_id=1, source_target_pairs={{0,12},{4,8},{8,4},{12,0},{1,13},{5,9},{9,5},{13,1},{2,14},{6,10},... | collective-permute-start | bytes 196616 | tf_op jit(solution)/shard_map/ppermute | solution.py:350
  86.3 5.7 %collective-permute-start.29 = (f32[128,128]{1,0:T(8,128)S(1)}, f32[128,128]{1,0:T(8,128)S(1)}, u32[]{:S(2)}, u32[]{:S(2)}) collective-permute-start(f32[128,128]{1,0:T(8,128)S(1)} %get-tuple-element.156), channel_id=1, source_target_pairs={{0,4},{4,0},{8,12},{12,8},{1,5},{5,1},{9,13},{13,9},{2,6},{6,2},{1... | collective-permute-start | bytes 196616 | tf_op jit(solution)/shard_map/ppermute | solution.py:350

commit v11 on v7

--- a/solution.py
+++ b/solution.py
@@ -77,6 +77,10 @@
 
 def shape(rows, columns, dtype=F32):
     return jax.ShapeDtypeStruct((rows, columns), dtype)
+
+
+def by_line(even, odd):
+    return even if odd is even else jnp.where(lax.axis_index("narrow") % 2 == 1, odd, even)
 
 
 def first_kernel(n, cap, peers_at, rows_at, operator_at, mult_at, *refs):
@@ -129,14 +133,14 @@
 
 
 def pack_kernel(times, cap, *refs):
-    n = len(times)
+    n = len(times[0])
     recvs, (high, low, pack, stack_high, stack_low) = refs[:n], refs[n:]
     shared = pack.shape[1]
     width = recvs[0].shape[1]
     column = lax.broadcasted_iota(jnp.int32, (width, shared), 1).astype(F32)
     if n * cap < pack.shape[0]:
         pack[n * cap:, :] = jnp.zeros((pack.shape[0] - n * cap, shared), BF16)
-    for d, recv in zip(times, recvs):
+    for d, recv in zip(times[0], recvs):
         for c in range(-(-cap // width)):
             wanted = jnp.broadcast_to(recv[shared + c:shared + c + 1, :], (shared, width)).T
             chosen = jnp.where(wanted == column, 1.0, 0.0).astype(BF16)
@@ -159,14 +163,16 @@
     tile_high[...], tile_low[...] = split(tile[...])
 
 
-def send(cap, chosen, image, sends):
+def send(times, cap, chosen, image, sends):
     picked = pick(chosen, image)
-    for d, out in enumerate(sends):
-        out[...] = picked[d * cap:(d + 1) * cap]
+    rows = [picked[at:at + cap] for at in range(0, len(sends) * cap, cap)]
+    for out, (even, odd) in zip(sends, zip(*times)):
+        out[...] = by_line(rows[even - 1], rows[odd - 1])
 
 
 def arrived(times, recvs, shared, unpack):
-    blocks = [recvs[times.index(d)][...][:shared] for d in sorted(times)]
+    got = [recv[...][:shared] for recv in recvs]
+    blocks = [by_line(*(got[line.index(d)] for line in times)) for d in sorted(times[0])]
     rows = sum(b.shape[0] for b in blocks)
     if rows < unpack.shape[1]:
         blocks.append(jnp.zeros((unpack.shape[1] - rows, blocks[0].shape[1]), F32))
@@ -247,7 +253,7 @@
 
 
 def coarse_kernel(times, size, *refs):
-    n = len(times)
+    n = len(times[0])
     recvs = refs[:n]
     base, unpack, mult, modes, started, trial = refs[n:n + 6]
     shared = base.shape[0]
@@ -271,7 +277,7 @@
         out[...] = parts[pl.ds(at, count), :]
 
 
-def lift_kernel(n, m, cap, size, *refs):
+def lift_kernel(times, m, cap, size, *refs):
     parts = refs[:m + 1]
     ins, (mult_s, mult_n, image), sends = refs[m + 1:m + 8], refs[m + 8:m + 11], refs[m + 11:]
     basis, trial_s, trial_n, floor, high, low, pack = ins
@@ -289,11 +295,11 @@
     mult_n[...] = rest
     value = product((high[...], low[...]), split(jnp.concatenate([first, rest], axis=0)))
     image[...] = value
-    send(cap, pack[...], value, sends)
+    send(times, cap, pack[...], value, sends)
 
 
 def sweep_kernel(times, cap, size, *refs):
-    n = len(times)
+    n = len(times[0])
     recvs = refs[:n]
     base, unpack, mult, floor, high, low, ahead, mult_out, image_out = refs[n:n + 9]
     shared = base.shape[0]
@@ -307,7 +313,7 @@
 
 
 def last_kernel(times, size, *refs):
-    n = len(times)
+    n = len(times[0])
     recvs = refs[:n]
     base, unpack, mult, floor, _, _, mult_out, residual_out, settled, left, done = refs[n:]
     shared = base.shape[0]
@@ -330,14 +336,24 @@
     return [swap(block, axis, count, d) for block, d in zip(blocks, order)]
 
 
-def swap_rows(blocks, axis, count, times):
-    return [swap(blocks[d - 1], axis, count, d) for d in times]
-
-
-def half_first(count, back):
+def swap_rows(blocks, wide, narrow, times):
+    return [
+        lax.ppermute(
+            block,
+            ("wide", "narrow"),
+            [(w * narrow + i, (w ^ ds[i % 2]) * narrow + i) for w in range(wide) for i in range(narrow)],
+        )
+        for block, ds in zip(blocks, zip(*times))
+    ]
+
+
+def half_first(count):
     half = count // 2
-    others = [d for d in range(1, count) if d != half]
-    return (half, *(others[::-1] if back else others))
+    return (half, *(d for d in range(count - 1, 0, -1) if d != half))
+
+
+def sorted_by(blocks, times):
+    return [blocks[d - 1] for d in times[0]]
 
 
 def middle_first(count):
@@ -376,8 +392,9 @@
     padded = -(-listed // 128) * 128
     size = interface_size
     coarse_order, part_order = far_first(wide), far_first(narrow)
-    half, half_back, middle = half_first(wide, False), half_first(wide, True), middle_first(wide)
-    orders = ((half_back, half, middle), (half_back, half, half_back))
+    middle, half = middle_first(wide), half_first(wide)
+    both, apart = (half, half), (tuple(range(1, wide)), half)
+    orders = (((middle, middle), apart, both), (both, apart, both))
     sent = [shape(cap, loads)] * n
     full = 2 * order * loads
 
@@ -416,7 +433,7 @@
     scratch = [pltpu.VMEM((order, 2 * loads), BF16)]
     for outer in range(OUTER):
         times = orders[outer][0]
-        recvs = swap_rows(sends, "wide", wide, times)
+        recvs = swap_rows(sorted_by(sends, times), wide, narrow, times)
         base = call(
             base_kernel,
             (image, unpack_own, gap),
@@ -489,7 +506,7 @@
         )
         parts = [own] + swap_all(parts, "narrow", narrow, part_order)
         mult_s, mult_n, image, *sends = call(
-            functools.partial(lift_kernel, n, m, cap),
+            functools.partial(lift_kernel, orders[outer][1], m, cap),
             (size, *parts, basis, trial_s, trial_n, floor, top_high, top_low, pack),
             [shape(shared, loads), shape(rest, loads), shape(shared, loads)] + sent,
             flops=3 * full * shared,
@@ -499,7 +516,9 @@
         for inner in range(1, INNER):
             last = outer == OUTER - 1 and inner == INNER - 1
             times = orders[outer][inner]
-            recvs = swap_rows(sends, "wide", wide, times)
+            if inner > 1:
+                sends = sorted_by(sends, times)
+            recvs = swap_rows(sends, wide, narrow, times)
             base = call(
                 base_kernel,
                 (image, unpack_own, gap),

time: 90.5 us -> 90.7 us (level)
  waiting for transfers between devices: 30.2 us -> 31.4 us
  starting transfers between devices: 39.3 us -> 38.2 us
    ppermute x30 -> x12, starting transfers between devices: 39.3 us -> 12.7 us  [swap(): return lax.ppermute(block, axis, [(i, i ^ d) for i in range(count)])]
    ppermute x0 -> x18, starting transfers between devices: none -> 25.5 us  [swap_rows(): lax.ppermute(block, ('wide', 'narrow'), [(w * narrow + i, (w ^ ds[i % 2])...]
    ppermute x0 -> x18, waiting for transfers between devices: none -> 22.3 us  [swap_rows(): lax.ppermute(block, ('wide', 'narrow'), [(w * narrow + i, (w ^ ds[i % 2])...]
    ppermute x30 -> x12, waiting for transfers between devices: 30.2 us -> 9.13 us  [swap(): return lax.ppermute(block, axis, [(i, i ^ d) for i in range(count)])]
  transfers between devices with their start and end apart: 30 -> 30, of which waited for: 24 -> 23; matrix products, arithmetic and copies ran while one was open for 0% -> 0% of each run, Pallas kernels for 13% -> 13%
where the time goes in v11:
time: 90.7 us; the launch traced here: 90.5 us
  starting transfers between devices  38.2 us (42%)
  waiting for transfers between devices  31.4 us (35%)
  Pallas kernels  19.3 us (21%)
  between operations  1.59 us (2%)
    ppermute x18, starting transfers between devices, swap_rows(): lax.ppermute(block, ('wide', 'narrow'), [(w * narrow + i, (w ^ ds[i % 2])...  25.5 us
    ppermute x18, waiting for transfers between devices, swap_rows(): lax.ppermute(block, ('wide', 'narrow'), [(w * narrow + i, (w ^ ds[i % 2])...  22.3 us
    pallas_call x25, Pallas kernels, call(): pl.pallas_call(body, out_shape=outs, grid=grid, in_specs=in_specs, out_sp...  19.3 us
    ppermute x12, starting transfers between devices, swap(): return lax.ppermute(block, axis, [(i, i ^ d) for i in range(count)])  12.7 us
    ppermute x12, waiting for transfers between devices, swap(): return lax.ppermute(block, axis, [(i, i ^ d) for i in range(count)])  9.13 us
  transfers between devices with their start and end apart: 30, of which 23 were waited for; matrix products, arithmetic and copies ran while one was open for 0% of the time, Pallas kernels for 13%

profile of v11, /device:TPU:0, one launch (start us, length us, event | category | flops | bytes accessed | tf_op | source)
XLA Modules:
  0.0 90.5 jit_solution(5390642089488073572)
XLA Ops:
  0.7 2.1 %first.1 = (bf16[256,256]{1,0:T(8,128)(2,1)S(1)}, bf16[256,768]{1,0:T(8,128)(2,1)S(1)}, bf16[256,384]{1,0:T(8,128)(2,1)S(1)}, bf16[256,1024]{1,0:T(8,128)(2,1)S(...) custom-call(s32[1,256]{1,0:T(1,128)} %bitcast.32, ...), custom_call_target="tpu_custom_call" | custom-call | flops 201326592 | bytes 2097152 | tf_op jit(solution)/shard_map/first/pallas_call | solution.py:49
  2.8 5.1 %collective-permute-start = (f32[264,128]{1,0:T(8,128)S(1)}, f32[264,128]{1,0:T(8,128)S(1)}, u32[]{:S(2)}, u32[]{:S(2)}) collective-permute-start(f32[264,128]{1,0:T(8,128)S(1)} %get-tuple-element.81), channel_id=1, source_target_pairs={{0,12},{1,13},{2,14},{3,15},{4,8},{5,9},{6,10},{7,11},{8,4},{9,5},... | collective-permute-start | bytes 405512 | tf_op jit(solution)/shard_map/ppermute | solution.py:341
  7.9 0.6 collective-permute-start.2
  9.4 2.0 %rest_start.1 = (f32[768,128]{1,0:T(8,128)S(1)}, f32[64,128]{1,0:T(8,128)S(1)}, bf16[768,1024]{1,0:T(8,128)(2,1)S(1)}, bf16[768,1024]{1,0:T(8,128)(2,1)S(1)}) custom-call(s32[1]{0:T(128)S(6)} %copy.15.size, f32[1024,1024]{1,0:T(8,128)S(1)} %bitcast.20, f32[1024,128]{1,0:T(8,128)S(1)} %bitcast.22, f32[1024,128]{1,0:T(8,128)S(1)} %bitcast.23, ...), custom_call_target="tpu_custom_call" | custom-call | flops 603979776 | bytes 6291456 | tf_op jit(solution)/shard_map/rest_start/pallas_call | solution.py:49
  11.4 0.9 collective-permute-done.refs_0_
  12.3 3.1 %collective-permute-done.1.refs_1_ = f32[264,128]{1,0:T(8,128)S(1)} collective-permute-done((f32[264,128]{1,0:T(8,128)S(1)}, f32[264,128]{1,0:T(8,128)S(1)}, u32[]{:S(2)}, u32[]{:S(2)}) %collective-permute-start.1) | collective-permute-done | bytes 135200 | tf_op jit(solution)/shard_map/ppermute | solution.py:341
  15.4 3.9 %collective-permute-done.2.refs_2_ = f32[264,128]{1,0:T(8,128)S(1)} collective-permute-done((f32[264,128]{1,0:T(8,128)S(1)}, f32[264,128]{1,0:T(8,128)S(1)}, u32[]{:S(2)}, u32[]{:S(2)}) %collective-permute-start.2) | collective-permute-done | bytes 135200 | tf_op jit(solution)/shard_map/ppermute | solution.py:341
  19.3 0.4 coarse.2
  19.7 2.5 %collective-permute-start.3 = (f32[64,128]{1,0:T(8,128)S(1)}, f32[64,128]{1,0:T(8,128)S(1)}, u32[]{:S(2)}, u32[]{:S(2)}) collective-permute-start(f32[64,128]{1,0:T(8,128)S(1)} %get-tuple-element.89), channel_id=1, source_target_pairs={{0,12},{4,8},{8,4},{12,0},{1,13},{5,9},{9,5},{13,1},{2,14},{6,10},... | collective-permute-start | bytes 98312 | tf_op jit(solution)/shard_map/ppermute | solution.py:332
  22.3 1.9 %collective-permute-start.5 = (f32[64,128]{1,0:T(8,128)S(1)}, f32[64,128]{1,0:T(8,128)S(1)}, u32[]{:S(2)}, u32[]{:S(2)}) collective-permute-start(f32[64,128]{1,0:T(8,128)S(1)} %get-tuple-element.91), channel_id=1, source_target_pairs={{0,4},{4,0},{8,12},{12,8},{1,5},{5,1},{9,13},{13,9},{2,6},{6,2},{1... | collective-permute-start | bytes 98312 | tf_op jit(solution)/shard_map/ppermute | solution.py:332
  24.2 0.4 prepare.1
  24.6 0.9 %collective-permute-done.3.refs_1_ = f32[64,128]{1,0:T(8,128)S(1)} collective-permute-done((f32[64,128]{1,0:T(8,128)S(1)}, f32[64,128]{1,0:T(8,128)S(1)}, u32[]{:S(2)}, u32[]{:S(2)}) %collective-permute-start.3) | collective-permute-done | bytes 32800 | tf_op jit(solution)/shard_map/ppermute | solution.py:332
  25.5 1.6 %collective-permute-done.4.refs_2_ = f32[64,128]{1,0:T(8,128)S(1)} collective-permute-done((f32[64,128]{1,0:T(8,128)S(1)}, f32[64,128]{1,0:T(8,128)S(1)}, u32[]{:S(2)}, u32[]{:S(2)}) %collective-permute-start.4) | collective-permute-done | bytes 32800 | tf_op jit(solution)/shard_map/ppermute | solution.py:332
  27.1 0.3 tile.4
  27.4 1.5 %collective-permute-start.7 = (f32[64,128]{1,0:T(8,128)S(1)}, f32[64,128]{1,0:T(8,128)S(1)}, u32[]{:S(2)}, u32[]{:S(2)}) collective-permute-start(f32[64,128]{1,0:T(8,128)S(1)} %get-tuple-element.94), channel_id=1, source_target_pairs={{0,2},{1,3},{2,0},{3,1},{4,6},{5,7},{6,4},{7,5},{8,10},{9,11},{10,... | collective-permute-start | bytes 98312 | tf_op jit(solution)/shard_map/ppermute | solution.py:332
  29.0 0.3 collective-permute-start.8
  29.3 0.3 pack.1
  29.6 1.5 %collective-permute-done.6.refs_1_ = f32[64,128]{1,0:T(8,128)S(1)} collective-permute-done((f32[64,128]{1,0:T(8,128)S(1)}, f32[64,128]{1,0:T(8,128)S(1)}, u32[]{:S(2)}, u32[]{:S(2)}) %collective-permute-start.6) | collective-permute-done | bytes 32800 | tf_op jit(solution)/shard_map/ppermute | solution.py:332
  31.1 0.4 collective-permute-done.7.refs_2_
  31.5 1.0 %lift.2 = (f32[256,128]{1,0:T(8,128)S(1)}, f32[768,128]{1,0:T(8,128)S(1)}, f32[256,128]{1,0:T(8,128)S(1)}, f32[128,128]{1,0:T(8,128)S(1)}, f32[128,128]{1,0:T(8,128)S(1)}, /*index=5*/f32[128,128]{1,0:T(8,128)S(1)}) custom-call(s32[1]{0:T(128)S(6)} %copy.15.size, f32[64,128]{1,0:T(8,128)S(1)} %get-tuple-element.92.refs_0_, ...), custom_call_target="tpu_custom_call" | custom-call | flops 201326592 | bytes 1048576 | tf_op jit(solution)/shard_map/lift/pallas_call | solution.py:49
  32.5 1.1 %collective-permute-start.9 = (f32[128,128]{1,0:T(8,128)S(1)}, f32[128,128]{1,0:T(8,128)S(1)}, u32[]{:S(2)}, u32[]{:S(2)}) collective-permute-start(f32[128,128]{1,0:T(8,128)S(1)} %get-tuple-element.103), channel_id=1, source_target_pairs={{0,4},{1,9},{2,6},{3,11},{4,0},{5,13},{6,2},{7,15},{8,12},{9,1},{1... | collective-permute-start | bytes 196616 | tf_op jit(solution)/shard_map/ppermute | solution.py:341
  33.6 1.4 %collective-permute-start.10 = (f32[128,128]{1,0:T(8,128)S(1)}, f32[128,128]{1,0:T(8,128)S(1)}, u32[]{:S(2)}, u32[]{:S(2)}) collective-permute-start(f32[128,128]{1,0:T(8,128)S(1)} %get-tuple-element.104), channel_id=1, source_target_pairs={{0,8},{1,13},{2,10},{3,15},{4,12},{5,9},{6,14},{7,11},{8,0},{9,5},... | collective-permute-start | bytes 196616 | tf_op jit(solution)/shard_map/ppermute | solution.py:341
  34.9 2.0 %collective-permute-start.11 = (f32[128,128]{1,0:T(8,128)S(1)}, f32[128,128]{1,0:T(8,128)S(1)}, u32[]{:S(2)}, u32[]{:S(2)}) collective-permute-start(f32[128,128]{1,0:T(8,128)S(1)} %get-tuple-element.105), channel_id=1, source_target_pairs={{0,12},{1,5},{2,14},{3,7},{4,8},{5,1},{6,10},{7,3},{8,4},{9,13},{1... | collective-permute-start | bytes 196616 | tf_op jit(solution)/shard_map/ppermute | solution.py:341
  37.1 1.5 %rest.3 = (f32[768,128]{1,0:T(8,128)S(1)}, f32[640,128]{1,0:T(8,128)S(1)}) custom-call(s32[1]{0:T(128)S(6)} %copy.15.size, bf16[768,1024]{1,0:T(8,128)(2,1)S(1)} %get-tuple-element.111.high, bf16[768,1024]{1,0:T(8,128)(2,1)S(1)} %get-tuple-element.112.low, f32[256,128]{1,0:T(8,128)S(1)} %get-tuple-element.108.mult_s.refs_5_, ...), custom_call_target="tpu_custom_call" | custom-call | flops 805306368 | bytes 4194304 | tf_op jit(solution)/shard_map/rest/pallas_call | solution.py:49
  38.6 2.2 %collective-permute-done.10.refs_1_ = f32[128,128]{1,0:T(8,128)S(1)} collective-permute-done((f32[128,128]{1,0:T(8,128)S(1)}, f32[128,128]{1,0:T(8,128)S(1)}, u32[]{:S(2)}, u32[]{:S(2)}) %collective-permute-start.10) | collective-permute-done | bytes 65568 | tf_op jit(solution)/shard_map/ppermute | solution.py:341
  40.8 0.5 collective-permute-done.11.refs_2_
  41.4 0.5 sweep.3
  41.9 1.7 %collective-permute-start.12 = (f32[128,128]{1,0:T(8,128)S(1)}, f32[128,128]{1,0:T(8,128)S(1)}, u32[]{:S(2)}, u32[]{:S(2)}) collective-permute-start(f32[128,128]{1,0:T(8,128)S(1)} %get-tuple-element.115), channel_id=1, source_target_pairs={{0,8},{1,9},{2,10},{3,11},{4,12},{5,13},{6,14},{7,15},{8,0},{9,1},... | collective-permute-start | bytes 196616 | tf_op jit(solution)/shard_map/ppermute | solution.py:341
  43.6 1.9 %collective-permute-start.13 = (f32[128,128]{1,0:T(8,128)S(1)}, f32[128,128]{1,0:T(8,128)S(1)}, u32[]{:S(2)}, u32[]{:S(2)}) collective-permute-start(f32[128,128]{1,0:T(8,128)S(1)} %get-tuple-element.116), channel_id=1, source_target_pairs={{0,12},{1,13},{2,14},{3,15},{4,8},{5,9},{6,10},{7,11},{8,4},{9,5},... | collective-permute-start | bytes 196616 | tf_op jit(solution)/shard_map/ppermute | solution.py:341
  45.7 1.5 %rest.4 = (f32[768,128]{1,0:T(8,128)S(1)}, f32[640,128]{1,0:T(8,128)S(1)}) custom-call(s32[1]{0:T(128)S(6)} %copy.15.size, bf16[768,1024]{1,0:T(8,128)(2,1)S(1)} %get-tuple-element.111.high, bf16[768,1024]{1,0:T(8,128)(2,1)S(1)} %get-tuple-element.112.low, f32[256,128]{1,0:T(8,128)S(1)} %get-tuple-element.119.mult_s.refs_5_, ...), custom_call_target="tpu_custom_call" | custom-call | flops 805306368 | bytes 4194304 | tf_op jit(solution)/shard_map/rest/pallas_call | solution.py:49
  47.2 1.6 %collective-permute-done.12.refs_0_ = f32[128,128]{1,0:T(8,128)S(1)} collective-permute-done((f32[128,128]{1,0:T(8,128)S(1)}, f32[128,128]{1,0:T(8,128)S(1)}, u32[]{:S(2)}, u32[]{:S(2)}) %collective-permute-start.12) | collective-permute-done | bytes 65568 | tf_op jit(solution)/shard_map/ppermute | solution.py:341
  48.9 1.0 %collective-permute-done.13.refs_1_ = f32[128,128]{1,0:T(8,128)S(1)} collective-permute-done((f32[128,128]{1,0:T(8,128)S(1)}, f32[128,128]{1,0:T(8,128)S(1)}, u32[]{:S(2)}, u32[]{:S(2)}) %collective-permute-start.13) | collective-permute-done | bytes 65568 | tf_op jit(solution)/shard_map/ppermute | solution.py:341
  49.9 0.6 collective-permute-done.14.refs_2_
  50.5 0.5 sweep.4
  51.0 1.0 %collective-permute-start.15 = (f32[128,128]{1,0:T(8,128)S(1)}, f32[128,128]{1,0:T(8,128)S(1)}, u32[]{:S(2)}, u32[]{:S(2)}) collective-permute-start(f32[128,128]{1,0:T(8,128)S(1)} %get-tuple-element.122), channel_id=1, source_target_pairs={{0,8},{1,9},{2,10},{3,11},{4,12},{5,13},{6,14},{7,15},{8,0},{9,1},... | collective-permute-start | bytes 196616 | tf_op jit(solution)/shard_map/ppermute | solution.py:341
  52.0 1.8 %collective-permute-start.16 = (f32[128,128]{1,0:T(8,128)S(1)}, f32[128,128]{1,0:T(8,128)S(1)}, u32[]{:S(2)}, u32[]{:S(2)}) collective-permute-start(f32[128,128]{1,0:T(8,128)S(1)} %get-tuple-element.123), channel_id=1, source_target_pairs={{0,12},{1,13},{2,14},{3,15},{4,8},{5,9},{6,10},{7,11},{8,4},{9,5},... | collective-permute-start | bytes 196616 | tf_op jit(solution)/shard_map/ppermute | solution.py:341
  53.8 0.8 collective-permute-start.17
  54.7 1.1 %rest_first.1 = (f32[768,128]{1,0:T(8,128)S(1)}, f32[64,128]{1,0:T(8,128)S(1)}) custom-call(s32[1]{0:T(128)S(6)} %copy.15.size, bf16[768,1024]{1,0:T(8,128)(2,1)S(1)} %get-tuple-element.111.high, bf16[768,1024]{1,0:T(8,128)(2,1)S(1)} %get-tuple-element.112.low, f32[256,128]{1,0:T(8,128)S(1)} %get-tuple-element.126.mult_s.refs_5_, ...), custom_call_target="tpu_custom_call" | custom-call | flops 603979776 | bytes 3145728 | tf_op jit(solution)/shard_map/rest_first/pallas_call | solution.py:49
  55.9 0.9 %collective-permute-done.15.refs_0_ = f32[128,128]{1,0:T(8,128)S(1)} collective-permute-done((f32[128,128]{1,0:T(8,128)S(1)}, f32[128,128]{1,0:T(8,128)S(1)}, u32[]{:S(2)}, u32[]{:S(2)}) %collective-permute-start.15) | collective-permute-done | bytes 65568 | tf_op jit(solution)/shard_map/ppermute | solution.py:341
  56.8 1.4 %collective-permute-done.16.refs_1_ = f32[128,128]{1,0:T(8,128)S(1)} collective-permute-done((f32[128,128]{1,0:T(8,128)S(1)}, f32[128,128]{1,0:T(8,128)S(1)}, u32[]{:S(2)}, u32[]{:S(2)}) %collective-permute-start.16) | collective-permute-done | bytes 65568 | tf_op jit(solution)/shard_map/ppermute | solution.py:341
  58.2 0.5 collective-permute-done.17.refs_2_
  58.7 0.4 coarse.3
  59.2 2.0 %collective-permute-start.18 = (f32[64,128]{1,0:T(8,128)S(1)}, f32[64,128]{1,0:T(8,128)S(1)}, u32[]{:S(2)}, u32[]{:S(2)}) collective-permute-start(f32[64,128]{1,0:T(8,128)S(1)} %get-tuple-element.130), channel_id=1, source_target_pairs={{0,12},{4,8},{8,4},{12,0},{1,13},{5,9},{9,5},{13,1},{2,14},{6,10},... | collective-permute-start | bytes 98312 | tf_op jit(solution)/shard_map/ppermute | solution.py:332
  61.2 2.5 %collective-permute-start.20 = (f32[64,128]{1,0:T(8,128)S(1)}, f32[64,128]{1,0:T(8,128)S(1)}, u32[]{:S(2)}, u32[]{:S(2)}) collective-permute-start(f32[64,128]{1,0:T(8,128)S(1)} %get-tuple-element.132), channel_id=1, source_target_pairs={{0,4},{4,0},{8,12},{12,8},{1,5},{5,1},{9,13},{13,9},{2,6},{6,2},{1... | collective-permute-start | bytes 98312 | tf_op jit(solution)/shard_map/ppermute | solution.py:332
  63.6 1.3 %collective-permute-done.18.refs_1_ = f32[64,128]{1,0:T(8,128)S(1)} collective-permute-done((f32[64,128]{1,0:T(8,128)S(1)}, f32[64,128]{1,0:T(8,128)S(1)}, u32[]{:S(2)}, u32[]{:S(2)}) %collective-permute-start.18) | collective-permute-done | bytes 32800 | tf_op jit(solution)/shard_map/ppermute | solution.py:332
  65.0 1.0 %collective-permute-done.19.refs_2_ = f32[64,128]{1,0:T(8,128)S(1)} collective-permute-done((f32[64,128]{1,0:T(8,128)S(1)}, f32[64,128]{1,0:T(8,128)S(1)}, u32[]{:S(2)}, u32[]{:S(2)}) %collective-permute-start.19) | collective-permute-done | bytes 32800 | tf_op jit(solution)/shard_map/ppermute | solution.py:332
  66.3 1.1 %collective-permute-start.22 = (f32[64,128]{1,0:T(8,128)S(1)}, f32[64,128]{1,0:T(8,128)S(1)}, u32[]{:S(2)}, u32[]{:S(2)}) collective-permute-start(f32[64,128]{1,0:T(8,128)S(1)} %get-tuple-element.135), channel_id=1, source_target_pairs={{0,2},{1,3},{2,0},{3,1},{4,6},{5,7},{6,4},{7,5},{8,10},{9,11},{10,... | collective-permute-start | bytes 98312 | tf_op jit(solution)/shard_map/ppermute | solution.py:332
  67.4 0.8 collective-permute-start.23
  68.2 1.5 %collective-permute-done.21.refs_1_ = f32[64,128]{1,0:T(8,128)S(1)} collective-permute-done((f32[64,128]{1,0:T(8,128)S(1)}, f32[64,128]{1,0:T(8,128)S(1)}, u32[]{:S(2)}, u32[]{:S(2)}) %collective-permute-start.21) | collective-permute-done | bytes 32800 | tf_op jit(solution)/shard_map/ppermute | solution.py:332
  69.6 0.9 %collective-permute-done.22.refs_2_ = f32[64,128]{1,0:T(8,128)S(1)} collective-permute-done((f32[64,128]{1,0:T(8,128)S(1)}, f32[64,128]{1,0:T(8,128)S(1)}, u32[]{:S(2)}, u32[]{:S(2)}) %collective-permute-start.22) | collective-permute-done | bytes 32800 | tf_op jit(solution)/shard_map/ppermute | solution.py:332
  70.6 1.0 %lift.3 = (f32[256,128]{1,0:T(8,128)S(1)}, f32[768,128]{1,0:T(8,128)S(1)}, f32[256,128]{1,0:T(8,128)S(1)}, f32[128,128]{1,0:T(8,128)S(1)}, f32[128,128]{1,0:T(8,128)S(1)}, /*index=5*/f32[128,128]{1,0:T(8,128)S(1)}) custom-call(s32[1]{0:T(128)S(6)} %copy.15.size, f32[64,128]{1,0:T(8,128)S(1)} %get-tuple-element.133.refs_0_, ...), custom_call_target="tpu_custom_call" | custom-call | flops 201326592 | bytes 1048576 | tf_op jit(solution)/shard_map/lift/pallas_call | solution.py:49
  71.6 1.7 %collective-permute-start.24 = (f32[128,128]{1,0:T(8,128)S(1)}, f32[128,128]{1,0:T(8,128)S(1)}, u32[]{:S(2)}, u32[]{:S(2)}) collective-permute-start(f32[128,128]{1,0:T(8,128)S(1)} %get-tuple-element.139), channel_id=1, source_target_pairs={{0,4},{1,9},{2,6},{3,11},{4,0},{5,13},{6,2},{7,15},{8,12},{9,1},{1... | collective-permute-start | bytes 196616 | tf_op jit(solution)/shard_map/ppermute | solution.py:341
  73.2 0.9 collective-permute-start.25
  74.1 1.9 %collective-permute-start.26 = (f32[128,128]{1,0:T(8,128)S(1)}, f32[128,128]{1,0:T(8,128)S(1)}, u32[]{:S(2)}, u32[]{:S(2)}) collective-permute-start(f32[128,128]{1,0:T(8,128)S(1)} %get-tuple-element.141), channel_id=1, source_target_pairs={{0,12},{1,5},{2,14},{3,7},{4,8},{5,1},{6,10},{7,3},{8,4},{9,13},{1... | collective-permute-start | bytes 196616 | tf_op jit(solution)/shard_map/ppermute | solution.py:341
  76.2 1.5 %rest.5 = (f32[768,128]{1,0:T(8,128)S(1)}, f32[640,128]{1,0:T(8,128)S(1)}) custom-call(s32[1]{0:T(128)S(6)} %copy.15.size, bf16[768,1024]{1,0:T(8,128)(2,1)S(1)} %get-tuple-element.111.high, bf16[768,1024]{1,0:T(8,128)(2,1)S(1)} %get-tuple-element.112.low, f32[256,128]{1,0:T(8,128)S(1)} %get-tuple-element.143.mult_s.refs_5_, ...), custom_call_target="tpu_custom_call" | custom-call | flops 805306368 | bytes 4194304 | tf_op jit(solution)/shard_map/rest/pallas_call | solution.py:49
  77.7 2.8 %collective-permute-done.25.refs_1_ = f32[128,128]{1,0:T(8,128)S(1)} collective-permute-done((f32[128,128]{1,0:T(8,128)S(1)}, f32[128,128]{1,0:T(8,128)S(1)}, u32[]{:S(2)}, u32[]{:S(2)}) %collective-permute-start.25) | collective-permute-done | bytes 65568 | tf_op jit(solution)/shard_map/ppermute | solution.py:341
  80.5 0.5 sweep.5
  81.1 1.7 %collective-permute-start.27 = (f32[128,128]{1,0:T(8,128)S(1)}, f32[128,128]{1,0:T(8,128)S(1)}, u32[]{:S(2)}, u32[]{:S(2)}) collective-permute-start(f32[128,128]{1,0:T(8,128)S(1)} %get-tuple-element.146), channel_id=1, source_target_pairs={{0,8},{1,9},{2,10},{3,11},{4,12},{5,13},{6,14},{7,15},{8,0},{9,1},... | collective-permute-start | bytes 196616 | tf_op jit(solution)/shard_map/ppermute | solution.py:341
  82.8 1.9 %collective-permute-start.28 = (f32[128,128]{1,0:T(8,128)S(1)}, f32[128,128]{1,0:T(8,128)S(1)}, u32[]{:S(2)}, u32[]{:S(2)}) collective-permute-start(f32[128,128]{1,0:T(8,128)S(1)} %get-tuple-element.147), channel_id=1, source_target_pairs={{0,12},{1,13},{2,14},{3,15},{4,8},{5,9},{6,10},{7,11},{8,4},{9,5},... | collective-permute-start | bytes 196616 | tf_op jit(solution)/shard_map/ppermute | solution.py:341
  84.9 1.9 %rest_last.1 = (f32[1024,128]{1,0:T(8,128)}, f32[1024,128]{1,0:T(8,128)}) custom-call(s32[1]{0:T(128)S(6)} %copy.15.size, bf16[768,1024]{1,0:T(8,128)(2,1)S(1)} %get-tuple-element.111.high, bf16[768,1024]{1,0:T(8,128)(2,1)S(1)} %get-tuple-element.112.low, f32[256,128]{1,0:T(8,128)S(1)} %get-tuple-element.150.mult_s.refs_5_, ...), custom_call_target="tpu_custom_call" | custom-call | flops 603979776 | bytes 3145728 | tf_op jit(solution)/shard_map/rest_last/pallas_call | solution.py:49
  86.8 0.5 collective-permute-done.27.refs_0_
  87.3 1.6 %collective-permute-done.28.refs_1_ = f32[128,128]{1,0:T(8,128)S(1)} collective-permute-done((f32[128,128]{1,0:T(8,128)S(1)}, f32[128,128]{1,0:T(8,128)S(1)}, u32[]{:S(2)}, u32[]{:S(2)}) %collective-permute-start.28) | collective-permute-done | bytes 65568 | tf_op jit(solution)/shard_map/ppermute | solution.py:341
  88.9 0.6 collective-permute-done.29.refs_2_
  89.6 0.9 %last.1 = (f32[1024,128]{1,0:T(8,128)}, f32[1024,128]{1,0:T(8,128)}) custom-call(s32[1]{0:T(128)S(6)} %copy.15.size, f32[128,128]{1,0:T(8,128)S(1)} %collective-permute-done.27.refs_0_, f32[128,128]{1,0:T(8,128)S(1)} %collective-permute-done.28.refs_1_, ...), custom_call_target="tpu_custom_call", output_to_operand_aliasing={{0}: (8, {}), {1}: (9, {})} | custom-call | flops 75497472 | bytes 196608 | tf_op jit(solution)/shard_map/last/pallas_call | solution.py:49
  (33 shorter events, 1.6 us)
Async XLA Ops:
  0.6 8.5 %copy-start = (f32[1,1024,128]{2,1,0:T(8,128)S(1)}, f32[1,1024,128]{2,1,0:T(8,128)}, u32[]{:S(2)}) copy-start(f32[1,1024,128]{2,1,0:T(8,128)} %param.12) | copy-start | bytes 1572868
  0.6 8.7 %copy-start.1 = (f32[1,1024,1024]{2,1,0:T(8,128)S(1)}, f32[1,1024,1024]{2,1,0:T(8,128)}, u32[]{:S(2)}) copy-start(f32[1,1024,1024]{2,1,0:T(8,128)} %param.9) | copy-start | bytes 12582916
  0.7 8.7 %copy-start.2 = (f32[1,1024,128]{2,1,0:T(8,128)S(1)}, f32[1,1024,128]{2,1,0:T(8,128)}, u32[]{:S(2)}) copy-start(f32[1,1024,128]{2,1,0:T(8,128)} %param.13) | copy-start | bytes 1572868
  0.7 8.7 %copy-start.3 = (f32[1,64,1024]{2,1,0:T(8,128)S(1)}, f32[1,64,1024]{2,1,0:T(8,128)}, u32[]{:S(2)}) copy-start(f32[1,64,1024]{2,1,0:T(8,128)} %param.11) | copy-start | bytes 786436
  2.8 9.6 %collective-permute-start = (f32[264,128]{1,0:T(8,128)S(1)}, f32[264,128]{1,0:T(8,128)S(1)}, u32[]{:S(2)}, u32[]{:S(2)}) collective-permute-start(f32[264,128]{1,0:T(8,128)S(1)} %get-tuple-element.81), channel_id=1, source_target_pairs={{0,12},{1,13},{2,14},{3,15},{4,8},{5,9},{6,10},{7,11},{8,4},{9,5},... | collective-permute-start | bytes 405512 | tf_op jit(solution)/shard_map/ppermute | solution.py:341
  7.9 7.6 %collective-permute-start.1 = (f32[264,128]{1,0:T(8,128)S(1)}, f32[264,128]{1,0:T(8,128)S(1)}, u32[]{:S(2)}, u32[]{:S(2)}) collective-permute-start(f32[264,128]{1,0:T(8,128)S(1)} %get-tuple-element.82), channel_id=1, source_target_pairs={{0,4},{1,5},{2,6},{3,7},{4,0},{5,1},{6,2},{7,3},{8,12},{9,13},{10,... | collective-permute-start | bytes 405512 | tf_op jit(solution)/shard_map/ppermute | solution.py:341
  7.9 11.4 %collective-permute-start.2 = (f32[264,128]{1,0:T(8,128)S(1)}, f32[264,128]{1,0:T(8,128)S(1)}, u32[]{:S(2)}, u32[]{:S(2)}) collective-permute-start(f32[264,128]{1,0:T(8,128)S(1)} %get-tuple-element.83), channel_id=1, source_target_pairs={{0,8},{1,9},{2,10},{3,11},{4,12},{5,13},{6,14},{7,15},{8,0},{9,1},... | collective-permute-start | bytes 405512 | tf_op jit(solution)/shard_map/ppermute | solution.py:341
  11.4 12.8 %copy-start.4 = (f32[256,256]{1,0:T(8,128)S(1)}, f32[256,256]{1,0:T(8,128)}, u32[]{:S(2)}) copy-start(f32[256,256]{1,0:T(8,128)} %tile.3) | copy-start | bytes 786436
  11.4 12.8 %copy-start.5 = (s32[1,1024]{1,0:T(1,128)S(1)}, s32[1,1024]{1,0:T(1,128)}, u32[]{:S(2)}) copy-start(s32[1,1024]{1,0:T(1,128)} %contact.1) | copy-start | bytes 12292
  19.7 5.8 %collective-permute-start.3 = (f32[64,128]{1,0:T(8,128)S(1)}, f32[64,128]{1,0:T(8,128)S(1)}, u32[]{:S(2)}, u32[]{:S(2)}) collective-permute-start(f32[64,128]{1,0:T(8,128)S(1)} %get-tuple-element.89), channel_id=1, source_target_pairs={{0,12},{4,8},{8,4},{12,0},{1,13},{5,9},{9,5},{13,1},{2,14},{6,10},... | collective-permute-start | bytes 98312 | tf_op jit(solution)/shard_map/ppermute | solution.py:332
  22.3 4.8 %collective-permute-start.4 = (f32[64,128]{1,0:T(8,128)S(1)}, f32[64,128]{1,0:T(8,128)S(1)}, u32[]{:S(2)}, u32[]{:S(2)}) collective-permute-start(f32[64,128]{1,0:T(8,128)S(1)} %get-tuple-element.90), channel_id=1, source_target_pairs={{0,8},{4,12},{8,0},{12,4},{1,9},{5,13},{9,1},{13,5},{2,10},{6,14},... | collective-permute-start | bytes 98312 | tf_op jit(solution)/shard_map/ppermute | solution.py:332
  22.3 4.8 %collective-permute-start.5 = (f32[64,128]{1,0:T(8,128)S(1)}, f32[64,128]{1,0:T(8,128)S(1)}, u32[]{:S(2)}, u32[]{:S(2)}) collective-permute-start(f32[64,128]{1,0:T(8,128)S(1)} %get-tuple-element.91), channel_id=1, source_target_pairs={{0,4},{4,0},{8,12},{12,8},{1,5},{5,1},{9,13},{13,9},{2,6},{6,2},{1... | collective-permute-start | bytes 98312 | tf_op jit(solution)/shard_map/ppermute | solution.py:332
  27.4 3.7 %collective-permute-start.6 = (f32[64,128]{1,0:T(8,128)S(1)}, f32[64,128]{1,0:T(8,128)S(1)}, u32[]{:S(2)}, u32[]{:S(2)}) collective-permute-start(f32[64,128]{1,0:T(8,128)S(1)} %get-tuple-element.93), channel_id=1, source_target_pairs={{0,3},{1,2},{2,1},{3,0},{4,7},{5,6},{6,5},{7,4},{8,11},{9,10},{10,... | collective-permute-start | bytes 98312 | tf_op jit(solution)/shard_map/ppermute | solution.py:332
  27.4 4.0 %collective-permute-start.7 = (f32[64,128]{1,0:T(8,128)S(1)}, f32[64,128]{1,0:T(8,128)S(1)}, u32[]{:S(2)}, u32[]{:S(2)}) collective-permute-start(f32[64,128]{1,0:T(8,128)S(1)} %get-tuple-element.94), channel_id=1, source_target_pairs={{0,2},{1,3},{2,0},{3,1},{4,6},{5,7},{6,4},{7,5},{8,10},{9,11},{10,... | collective-permute-start | bytes 98312 | tf_op jit(solution)/shard_map/ppermute | solution.py:332
  29.0 2.5 %collective-permute-start.8 = (f32[64,128]{1,0:T(8,128)S(1)}, f32[64,128]{1,0:T(8,128)S(1)}, u32[]{:S(2)}, u32[]{:S(2)}) collective-permute-start(f32[64,128]{1,0:T(8,128)S(1)} %get-tuple-element.95), channel_id=1, source_target_pairs={{0,1},{1,0},{2,3},{3,2},{4,5},{5,4},{6,7},{7,6},{8,9},{9,8},{10,11... | collective-permute-start | bytes 98312 | tf_op jit(solution)/shard_map/ppermute | solution.py:332
  32.5 6.1 %collective-permute-start.9 = (f32[128,128]{1,0:T(8,128)S(1)}, f32[128,128]{1,0:T(8,128)S(1)}, u32[]{:S(2)}, u32[]{:S(2)}) collective-permute-start(f32[128,128]{1,0:T(8,128)S(1)} %get-tuple-element.103), channel_id=1, source_target_pairs={{0,4},{1,9},{2,6},{3,11},{4,0},{5,13},{6,2},{7,15},{8,12},{9,1},{1... | collective-permute-start | bytes 196616 | tf_op jit(solution)/shard_map/ppermute | solution.py:341
  33.6 7.3 %collective-permute-start.10 = (f32[128,128]{1,0:T(8,128)S(1)}, f32[128,128]{1,0:T(8,128)S(1)}, u32[]{:S(2)}, u32[]{:S(2)}) collective-permute-start(f32[128,128]{1,0:T(8,128)S(1)} %get-tuple-element.104), channel_id=1, source_target_pairs={{0,8},{1,13},{2,10},{3,15},{4,12},{5,9},{6,14},{7,11},{8,0},{9,5},... | collective-permute-start | bytes 196616 | tf_op jit(solution)/shard_map/ppermute | solution.py:341
  34.9 6.5 %collective-permute-start.11 = (f32[128,128]{1,0:T(8,128)S(1)}, f32[128,128]{1,0:T(8,128)S(1)}, u32[]{:S(2)}, u32[]{:S(2)}) collective-permute-start(f32[128,128]{1,0:T(8,128)S(1)} %get-tuple-element.105), channel_id=1, source_target_pairs={{0,12},{1,5},{2,14},{3,7},{4,8},{5,1},{6,10},{7,3},{8,4},{9,13},{1... | collective-permute-start | bytes 196616 | tf_op jit(solution)/shard_map/ppermute | solution.py:341
  41.9 6.9 %collective-permute-start.12 = (f32[128,128]{1,0:T(8,128)S(1)}, f32[128,128]{1,0:T(8,128)S(1)}, u32[]{:S(2)}, u32[]{:S(2)}) collective-permute-start(f32[128,128]{1,0:T(8,128)S(1)} %get-tuple-element.115), channel_id=1, source_target_pairs={{0,8},{1,9},{2,10},{3,11},{4,12},{5,13},{6,14},{7,15},{8,0},{9,1},... | collective-permute-start | bytes 196616 | tf_op jit(solution)/shard_map/ppermute | solution.py:341
  43.6 6.2 %collective-permute-start.13 = (f32[128,128]{1,0:T(8,128)S(1)}, f32[128,128]{1,0:T(8,128)S(1)}, u32[]{:S(2)}, u32[]{:S(2)}) collective-permute-start(f32[128,128]{1,0:T(8,128)S(1)} %get-tuple-element.116), channel_id=1, source_target_pairs={{0,12},{1,13},{2,14},{3,15},{4,8},{5,9},{6,10},{7,11},{8,4},{9,5},... | collective-permute-start | bytes 196616 | tf_op jit(solution)/shard_map/ppermute | solution.py:341
  45.5 5.0 %collective-permute-start.14 = (f32[128,128]{1,0:T(8,128)S(1)}, f32[128,128]{1,0:T(8,128)S(1)}, u32[]{:S(2)}, u32[]{:S(2)}) collective-permute-start(f32[128,128]{1,0:T(8,128)S(1)} %get-tuple-element.117), channel_id=1, source_target_pairs={{0,4},{1,5},{2,6},{3,7},{4,0},{5,1},{6,2},{7,3},{8,12},{9,13},{10,... | collective-permute-start | bytes 196616 | tf_op jit(solution)/shard_map/ppermute | solution.py:341
  51.0 5.8 %collective-permute-start.15 = (f32[128,128]{1,0:T(8,128)S(1)}, f32[128,128]{1,0:T(8,128)S(1)}, u32[]{:S(2)}, u32[]{:S(2)}) collective-permute-start(f32[128,128]{1,0:T(8,128)S(1)} %get-tuple-element.122), channel_id=1, source_target_pairs={{0,8},{1,9},{2,10},{3,11},{4,12},{5,13},{6,14},{7,15},{8,0},{9,1},... | collective-permute-start | bytes 196616 | tf_op jit(solution)/shard_map/ppermute | solution.py:341
  52.0 6.3 %collective-permute-start.16 = (f32[128,128]{1,0:T(8,128)S(1)}, f32[128,128]{1,0:T(8,128)S(1)}, u32[]{:S(2)}, u32[]{:S(2)}) collective-permute-start(f32[128,128]{1,0:T(8,128)S(1)} %get-tuple-element.123), channel_id=1, source_target_pairs={{0,12},{1,13},{2,14},{3,15},{4,8},{5,9},{6,10},{7,11},{8,4},{9,5},... | collective-permute-start | bytes 196616 | tf_op jit(solution)/shard_map/ppermute | solution.py:341
  53.8 5.0 %collective-permute-start.17 = (f32[128,128]{1,0:T(8,128)S(1)}, f32[128,128]{1,0:T(8,128)S(1)}, u32[]{:S(2)}, u32[]{:S(2)}) collective-permute-start(f32[128,128]{1,0:T(8,128)S(1)} %get-tuple-element.124), channel_id=1, source_target_pairs={{0,4},{1,5},{2,6},{3,7},{4,0},{5,1},{6,2},{7,3},{8,12},{9,13},{10,... | collective-permute-start | bytes 196616 | tf_op jit(solution)/shard_map/ppermute | solution.py:341
  59.2 5.8 %collective-permute-start.18 = (f32[64,128]{1,0:T(8,128)S(1)}, f32[64,128]{1,0:T(8,128)S(1)}, u32[]{:S(2)}, u32[]{:S(2)}) collective-permute-start(f32[64,128]{1,0:T(8,128)S(1)} %get-tuple-element.130), channel_id=1, source_target_pairs={{0,12},{4,8},{8,4},{12,0},{1,13},{5,9},{9,5},{13,1},{2,14},{6,10},... | collective-permute-start | bytes 98312 | tf_op jit(solution)/shard_map/ppermute | solution.py:332
  61.1 4.8 %collective-permute-start.19 = (f32[64,128]{1,0:T(8,128)S(1)}, f32[64,128]{1,0:T(8,128)S(1)}, u32[]{:S(2)}, u32[]{:S(2)}) collective-permute-start(f32[64,128]{1,0:T(8,128)S(1)} %get-tuple-element.131), channel_id=1, source_target_pairs={{0,8},{4,12},{8,0},{12,4},{1,9},{5,13},{9,1},{13,5},{2,10},{6,14},... | collective-permute-start | bytes 98312 | tf_op jit(solution)/shard_map/ppermute | solution.py:332
  61.2 4.8 %collective-permute-start.20 = (f32[64,128]{1,0:T(8,128)S(1)}, f32[64,128]{1,0:T(8,128)S(1)}, u32[]{:S(2)}, u32[]{:S(2)}) collective-permute-start(f32[64,128]{1,0:T(8,128)S(1)} %get-tuple-element.132), channel_id=1, source_target_pairs={{0,4},{4,0},{8,12},{12,8},{1,5},{5,1},{9,13},{13,9},{2,6},{6,2},{1... | collective-permute-start | bytes 98312 | tf_op jit(solution)/shard_map/ppermute | solution.py:332
  66.2 3.4 %collective-permute-start.21 = (f32[64,128]{1,0:T(8,128)S(1)}, f32[64,128]{1,0:T(8,128)S(1)}, u32[]{:S(2)}, u32[]{:S(2)}) collective-permute-start(f32[64,128]{1,0:T(8,128)S(1)} %get-tuple-element.134), channel_id=1, source_target_pairs={{0,3},{1,2},{2,1},{3,0},{4,7},{5,6},{6,5},{7,4},{8,11},{9,10},{10,... | collective-permute-start | bytes 98312 | tf_op jit(solution)/shard_map/ppermute | solution.py:332
  66.3 4.3 %collective-permute-start.22 = (f32[64,128]{1,0:T(8,128)S(1)}, f32[64,128]{1,0:T(8,128)S(1)}, u32[]{:S(2)}, u32[]{:S(2)}) collective-permute-start(f32[64,128]{1,0:T(8,128)S(1)} %get-tuple-element.135), channel_id=1, source_target_pairs={{0,2},{1,3},{2,0},{3,1},{4,6},{5,7},{6,4},{7,5},{8,10},{9,11},{10,... | collective-permute-start | bytes 98312 | tf_op jit(solution)/shard_map/ppermute | solution.py:332
  67.4 3.2 %collective-permute-start.23 = (f32[64,128]{1,0:T(8,128)S(1)}, f32[64,128]{1,0:T(8,128)S(1)}, u32[]{:S(2)}, u32[]{:S(2)}) collective-permute-start(f32[64,128]{1,0:T(8,128)S(1)} %get-tuple-element.136), channel_id=1, source_target_pairs={{0,1},{1,0},{2,3},{3,2},{4,5},{5,4},{6,7},{7,6},{8,9},{9,8},{10,11... | collective-permute-start | bytes 98312 | tf_op jit(solution)/shard_map/ppermute | solution.py:332
  71.6 6.1 %collective-permute-start.24 = (f32[128,128]{1,0:T(8,128)S(1)}, f32[128,128]{1,0:T(8,128)S(1)}, u32[]{:S(2)}, u32[]{:S(2)}) collective-permute-start(f32[128,128]{1,0:T(8,128)S(1)} %get-tuple-element.139), channel_id=1, source_target_pairs={{0,4},{1,9},{2,6},{3,11},{4,0},{5,13},{6,2},{7,15},{8,12},{9,1},{1... | collective-permute-start | bytes 196616 | tf_op jit(solution)/shard_map/ppermute | solution.py:341
  73.2 7.3 %collective-permute-start.25 = (f32[128,128]{1,0:T(8,128)S(1)}, f32[128,128]{1,0:T(8,128)S(1)}, u32[]{:S(2)}, u32[]{:S(2)}) collective-permute-start(f32[128,128]{1,0:T(8,128)S(1)} %get-tuple-element.140), channel_id=1, source_target_pairs={{0,8},{1,13},{2,10},{3,15},{4,12},{5,9},{6,14},{7,11},{8,0},{9,5},... | collective-permute-start | bytes 196616 | tf_op jit(solution)/shard_map/ppermute | solution.py:341
  74.1 6.4 %collective-permute-start.26 = (f32[128,128]{1,0:T(8,128)S(1)}, f32[128,128]{1,0:T(8,128)S(1)}, u32[]{:S(2)}, u32[]{:S(2)}) collective-permute-start(f32[128,128]{1,0:T(8,128)S(1)} %get-tuple-element.141), channel_id=1, source_target_pairs={{0,12},{1,5},{2,14},{3,7},{4,8},{5,1},{6,10},{7,3},{8,4},{9,13},{1... | collective-permute-start | bytes 196616 | tf_op jit(solution)/shard_map/ppermute | solution.py:341
  81.1 6.2 %collective-permute-start.27 = (f32[128,128]{1,0:T(8,128)S(1)}, f32[128,128]{1,0:T(8,128)S(1)}, u32[]{:S(2)}, u32[]{:S(2)}) collective-permute-start(f32[128,128]{1,0:T(8,128)S(1)} %get-tuple-element.146), channel_id=1, source_target_pairs={{0,8},{1,9},{2,10},{3,11},{4,12},{5,13},{6,14},{7,15},{8,0},{9,1},... | collective-permute-start | bytes 196616 | tf_op jit(solution)/shard_map/ppermute | solution.py:341
  82.8 6.1 %collective-permute-start.28 = (f32[128,128]{1,0:T(8,128)S(1)}, f32[128,128]{1,0:T(8,128)S(1)}, u32[]{:S(2)}, u32[]{:S(2)}) collective-permute-start(f32[128,128]{1,0:T(8,128)S(1)} %get-tuple-element.147), channel_id=1, source_target_pairs={{0,12},{1,13},{2,14},{3,15},{4,8},{5,9},{6,10},{7,11},{8,4},{9,5},... | collective-permute-start | bytes 196616 | tf_op jit(solution)/shard_map/ppermute | solution.py:341
  84.7 4.8 %collective-permute-start.29 = (f32[128,128]{1,0:T(8,128)S(1)}, f32[128,128]{1,0:T(8,128)S(1)}, u32[]{:S(2)}, u32[]{:S(2)}) collective-permute-start(f32[128,128]{1,0:T(8,128)S(1)} %get-tuple-element.148), channel_id=1, source_target_pairs={{0,4},{1,5},{2,6},{3,7},{4,0},{5,1},{6,2},{7,3},{8,12},{9,13},{10,... | collective-permute-start | bytes 196616 | tf_op jit(solution)/shard_map/ppermute | solution.py:341

commit v12 on v8

--- a/solution.py
+++ b/solution.py
@@ -92,10 +92,9 @@
     return down[:, :1] ^ lax.axis_index("wide"), slot, wanted
 
 
-def first_kernel(n, cap, peers_at, rows_at, operator_at, mult_at, *refs):
-    high, low, image = refs[:3]
-    sends, (peers, rows, operator, mult, done) = refs[3:3 + n], refs[3 + n:]
-    shared, width = image.shape
+def lists_kernel(n, peers_at, rows_at, operator_at, mult_at, operator, mult, *refs):
+    lists, (peers, rows, done) = refs[:n], refs[n:]
+    shared = operator.shape[0]
     copies = [
         pltpu.make_async_copy(source, target, done.at[i])
         for i, (source, target) in enumerate(
@@ -108,30 +107,25 @@
     copies[1].wait()
     far, slot, wanted = places(peers, rows)
     wanted = wanted.astype(F32)
-    lane = lax.broadcasted_iota(jnp.int32, (shared, width), 1)
-    for d, out in enumerate(sends, 1):
-        out[shared:, :] = jnp.zeros((out.shape[0] - shared, width), F32)
-        for c in range(-(-cap // width)):
-            hit = (far == d) & (slot == lane + c * width)
-            out[shared + c:shared + c + 1, :] = jnp.sum(
-                jnp.where(hit, wanted, 0.0), axis=0, keepdims=True
-            )
+    lane = lax.broadcasted_iota(jnp.int32, (shared, mult.shape[1]), 1)
+    for d, out in enumerate(lists, 1):
+        for c in range(out.shape[0]):
+            hit = (far == d) & (slot == lane + c * out.shape[1])
+            out[c:c + 1, :] = jnp.sum(jnp.where(hit, wanted, 0.0), axis=0, keepdims=True)
     copies[2].wait()
     copies[3].wait()
+
+
+def first_kernel(operator, mult, high, low, image):
     parts = split(operator[...])
     high[...], low[...] = parts
-    value = product(parts, split(mult[...]))
-    image[...] = value
-    for out in sends:
-        out[:shared, :] = value
-
-
-def marks_kernel(cap, peers, rows, unpack_own, unpack_all, unpack):
+    image[...] = product(parts, split(mult[...]))
+
+
+def marks_kernel(cap, peers, rows, unpack_own, unpack):
     far, slot, wanted = places(peers, rows)
-    shared = peers.shape[1]
     for key, out in (
         (jnp.where(far == 0, wanted, -1), unpack_own),
-        (jnp.where(far == 0, -1, (far - 1) * shared + wanted), unpack_all),
         (jnp.where(far == 0, -1, (far - 1) * cap + slot), unpack),
     ):
         hit = key == lax.broadcasted_iota(jnp.int32, out.shape, 1)
@@ -140,19 +134,23 @@
 
 def pack_kernel(times, cap, *refs):
     n = len(times)
-    recvs, (high, low, pack, stack_high, stack_low) = refs[:n], refs[n:]
-    shared = pack.shape[1]
-    width = recvs[0].shape[1]
+    lists, (image, pack), sends = refs[:n], refs[n:n + 2], refs[n + 2:]
+    shared, width = image.shape
     column = lax.broadcasted_iota(jnp.int32, (width, shared), 1).astype(F32)
     if n * cap < pack.shape[0]:
         pack[n * cap:, :] = jnp.zeros((pack.shape[0] - n * cap, shared), BF16)
-    for d, recv in zip(times, recvs):
+    for d, asked in zip(times, lists):
         for c in range(-(-cap // width)):
-            wanted = jnp.broadcast_to(recv[shared + c:shared + c + 1, :], (shared, width)).T
+            wanted = jnp.broadcast_to(asked[c:c + 1, :], (shared, width)).T
             chosen = jnp.where(wanted == column, 1.0, 0.0).astype(BF16)
             size = min(width, cap - c * width)
             at = (d - 1) * cap + c * width
             pack[at:at + size, :] = chosen[:size]
+    send(cap, pack[...], image[...], sends)
+
+
+def square_kernel(high, low, pack, stack_high, stack_low):
+    shared = pack.shape[1]
     for source, stack in ((high, stack_high), (low, stack_low)):
         square = source[:, :shared]
         stack[:shared, :] = square
@@ -175,8 +173,8 @@
         out[...] = picked[d * cap:(d + 1) * cap]
 
 
-def arrived(times, recvs, shared, unpack):
-    blocks = [recvs[times.index(d)][...][:shared] for d in sorted(times)]
+def arrived(times, recvs, unpack):
+    blocks = [recvs[times.index(d)][...] for d in sorted(times)]
     rows = sum(b.shape[0] for b in blocks)
     if rows < unpack.shape[1]:
         blocks.append(jnp.zeros((unpack.shape[1] - rows, blocks[0].shape[1]), F32))
@@ -195,7 +193,7 @@
 def shared_residual(times, recvs, base, unpack, size):
     known = base[...]
     alive = live(size[0], 0, *known.shape)
-    return jnp.where(alive, known + arrived(times, recvs, known.shape[0], unpack), 0.0), alive
+    return jnp.where(alive, known + arrived(times, recvs, unpack), 0.0), alive
 
 
 def rest_start_kernel(size, operator, mult, mult_block, gap, modes, trial, coarse, high, low, halves):
@@ -291,19 +289,13 @@
     shared, width = trial_s.shape
     order = floor.shape[0]
     high_part, low_part = split(solved)
-    solved = jnp.concatenate([high_part, low_part, high_part], axis=0)
-    shared, width = trial_s.shape
-    value = jnp.zeros((shared, width), F32)
-    for at in range(0, floor.shape[0], shared):
-        here = slice(at, at + shared)
-        trial = trial_s[...] if at == 0 else trial_n[at - shared:at, :]
-        alive = live(size[0], at, shared, width)
-        mult = settle(trial + mm(basis[here, :], solved), floor[here, :], alive)
-        if at == 0:
-            mult_s[...] = mult
-        else:
-            mult_n[at - shared:at, :] = mult
-        value = value + product((high[:, here], low[:, here]), split(mult))
+    lifted = mm(basis[...], jnp.concatenate([high_part, low_part, high_part], axis=0))
+    alive = live(size[0], 0, order, width)
+    first = settle(trial_s[...] + lifted[:shared], floor[:shared], alive[:shared])
+    rest = settle(trial_n[...] + lifted[shared:], floor[shared:], alive[shared:])
+    mult_s[...] = first
+    mult_n[...] = rest
+    value = product((high[...], low[...]), split(jnp.concatenate([first, rest], axis=0)))
     image[...] = value
     send(cap, pack[...], value, sends)
 
@@ -353,10 +345,6 @@
 def half_first(count):
     half = count // 2
     return (half, *(d for d in range(count - 1, 0, -1) if d != half))
-
-
-def middle_first(count):
-    return (count - 1, *range(1, count - 1))
 
 
 def far_first(count):
@@ -390,36 +378,55 @@
     listed = n * cap
     padded = -(-listed // 128) * 128
     size = interface_size
-    part_order = far_first(narrow)
-    half_back, middle = half_first(wide), middle_first(wide)
-    orders = ((middle, half_back, half_back), (half_back, far_first(wide), half_back))
+    coarse_order, part_order, times = far_first(wide), far_first(narrow), half_first(wide)
     sent = [shape(cap, loads)] * n
     full = 2 * order * loads
 
     list_rows = -(-(-(-cap // loads)) // 8) * 8
     pairs = peer_list[0].reshape(1, shared), partner_row
-    top_high, top_low, image, *sends = call(
-        functools.partial(first_kernel, n, cap),
+    operator_top, mult_near, *lists = call(
+        functools.partial(lists_kernel, n),
         tuple(pltpu.with_memory_space_constraint(value, pltpu.HBM) for value in (*pairs, operator, mult)),
-        [shape(shared, order, BF16)] * 2
-        + [shape(shared, loads)]
-        + [shape(shared + list_rows, loads)] * n,
+        [shape(shared, order), shape(order, loads)] + [shape(list_rows, loads)] * n,
         in_specs=[HBM] * 4,
         scratch=[
             pltpu.VMEM((1, shared), jnp.int32),
             pltpu.VMEM((1, shared), jnp.int32),
-            pltpu.VMEM((shared, order), F32),
-            pltpu.VMEM((order, loads), F32),
             pltpu.SemaphoreType.DMA((4,)),
         ],
+        flops=8 * shared * shared,
+        moved=8 * shared * order,
+        name="lists",
+    )
+    lists = swap_rows(lists, "wide", wide, times)
+    top_high, top_low, image = call(
+        first_kernel,
+        (operator_top, mult_near),
+        [shape(shared, order, BF16)] * 2 + [shape(shared, loads)],
         flops=3 * full * shared,
         moved=8 * shared * order,
         name="first",
     )
-    unpack_own, unpack_all, unpack = call(
+    pack, *sends = call(
+        functools.partial(pack_kernel, times, cap),
+        (*lists, image),
+        [shape(padded, shared, BF16)] + sent,
+        flops=4 * padded * shared * loads,
+        moved=4 * padded * shared,
+        name="pack",
+    )
+    stack_high, stack_low = call(
+        square_kernel,
+        (top_high, top_low, pack),
+        [shape(shared + padded, shared, BF16)] * 2,
+        flops=4 * padded * shared * shared,
+        moved=8 * padded * shared,
+        name="square",
+    )
+    unpack_own, unpack = call(
         functools.partial(marks_kernel, cap),
         pairs,
-        [shape(shared, shared, BF16), shape(shared, n * shared, BF16), shape(shared, padded, BF16)],
+        [shape(shared, shared, BF16), shape(shared, padded, BF16)],
         flops=8 * shared * shared * wide,
         moved=2 * shared * shared * wide,
         name="marks",
@@ -435,7 +442,6 @@
     mult_s = mult
     scratch = [pltpu.VMEM((order, 2 * loads), BF16)]
     for outer in range(OUTER):
-        times = orders[outer][0]
         recvs = swap_rows(sends, "wide", wide, times)
         base = call(
             base_kernel,
@@ -450,7 +456,7 @@
             next_loads = block((shared, loads), 1)
             trial_n, started, high, low = call(
                 rest_start_kernel,
-                (size, operator, mult, mult, gap, modes),
+                (size, pltpu.with_memory_space_constraint(operator, pltpu.HBM), mult, mult, gap, modes),
                 [shape(rest, loads), shape(count, loads)] + [shape(rest, order, BF16)] * 2,
                 [
                     SMEM,
@@ -467,15 +473,6 @@
                 moved=8 * rest * order,
                 name="rest_start",
             )
-            marks = unpack_all
-            pack, stack_high, stack_low = call(
-                functools.partial(pack_kernel, times, cap),
-                (*recvs, top_high, top_low),
-                [shape(padded, shared, BF16)] + [shape(shared + padded, shared, BF16)] * 2,
-                flops=8 * padded * shared * shared,
-                moved=8 * padded * shared,
-                name="pack",
-            )
         else:
             trial_n, started = call(
                 rest_first_kernel,
@@ -485,16 +482,14 @@
                 moved=4 * rest * order,
                 name="rest_first",
             )
-            marks = unpack
         trial_s, own, *coarse = call(
             functools.partial(coarse_kernel, times),
-            (size, *recvs, base, marks, mult_s, modes, started),
+            (size, *recvs, base, unpack, mult_s, modes, started),
             [shape(shared, loads)] + [shape(count, loads)] * wide,
             flops=6 * shared * loads * unpack.shape[1],
             moved=2 * shared * unpack.shape[1],
             name="coarse",
         )
-        coarse_order = half_back if outer == 0 else far_first(wide)
         blocks = [own] + swap_all(coarse, "wide", wide, coarse_order)
         own, *parts = call(
             functools.partial(tile_kernel, coarse_order, part_order),
@@ -519,7 +514,6 @@
         )
         for inner in range(1, INNER):
             last = outer == OUTER - 1 and inner == INNER - 1
-            times = orders[outer][inner]
             recvs = swap_rows(sends, "wide", wide, times)
             base = call(
                 base_kernel,

time: 91.7 us -> 92.3 us (level)
  starting transfers between devices: 36.3 us -> 40.2 us
  waiting for transfers between devices: 31.7 us -> 28.8 us
  local copies, waits for them, and re-layouts: 1.38 us -> 0.04 us
    ppermute x30 -> x33, starting transfers between devices: 36.3 us -> 40.2 us  [swap(): return lax.ppermute(block, axis, [(i, i ^ d) for i in range(count)])]
    ppermute x30 -> x33, waiting for transfers between devices: 31.7 us -> 28.8 us  [swap(): return lax.ppermute(block, axis, [(i, i ^ d) for i in range(count)])]
    unnamed x16 -> x14, local copies, waits for them, and re-layouts: 1.38 us -> 0.04 us
    pallas_call x26 -> x28, Pallas kernels: 20.5 us -> 21.4 us  [call(): pl.pallas_call(body, out_shape=outs, grid=grid, in_specs=in_specs, out_sp...]
  transfers between devices with their start and end apart: 30 -> 33, of which waited for: 22 -> 21; matrix products, arithmetic and copies ran while one was open for 0% -> 0% of each run, Pallas kernels for 13% -> 15%
where the time goes in v12:
time: 92.3 us; the launch traced here: 92.1 us
  starting transfers between devices  40.2 us (44%)
  waiting for transfers between devices  28.8 us (31%)
  Pallas kernels  21.4 us (23%)
  between operations  1.64 us (2%)
    ppermute x33, starting transfers between devices, swap(): return lax.ppermute(block, axis, [(i, i ^ d) for i in range(count)])  40.2 us
    ppermute x33, waiting for transfers between devices, swap(): return lax.ppermute(block, axis, [(i, i ^ d) for i in range(count)])  28.8 us
    pallas_call x28, Pallas kernels, call(): pl.pallas_call(body, out_shape=outs, grid=grid, in_specs=in_specs, out_sp...  21.4 us
  transfers between devices with their start and end apart: 33, of which 21 were waited for; matrix products, arithmetic and copies ran while one was open for 0% of the time, Pallas kernels for 15%

profile of v12, /device:TPU:0, one launch (start us, length us, event | category | flops | bytes accessed | tf_op | source)
XLA Modules:
  0.0 92.1 jit_solution(10446418714545928503)
XLA Ops:
  0.6 1.5 %lists.1 = (f32[256,1024]{1,0:T(8,128)S(1)}, f32[1024,128]{1,0:T(8,128)S(1)}, f32[8,128]{1,0:T(8,128)S(1)}, f32[8,128]{1,0:T(8,128)S(1)}, f32[8,128]{1,0:T(8,128)S(1)}) custom-call(s32[1,256]{1,0:T(1,128)} %bitcast.28, s32[1,256]{1,0:T(1,128)} %rows.1, f32[1024,1024]{1,0:T(8,128)} %bitcast.30, f32[1024,128]{1,0:T(8,128)} %bitcast.19), custom_call_target="tpu_custom_call" | custom-call | flops 524288 | bytes 2097152 | tf_op jit(solution)/shard_map/lists/pallas_call | solution.py:49
  2.2 4.1 %collective-permute-start = (f32[8,128]{1,0:T(8,128)S(1)}, f32[8,128]{1,0:T(8,128)S(1)}, u32[]{:S(2)}, u32[]{:S(2)}) collective-permute-start(f32[8,128]{1,0:T(8,128)S(1)} %get-tuple-element.85), channel_id=1, source_target_pairs={{0,8},{4,12},{8,0},{12,4},{1,9},{5,13},{9,1},{13,5},{2,10},{6,14},... | collective-permute-start | bytes 12296 | tf_op jit(solution)/shard_map/ppermute | solution.py:334
  6.3 1.3 %collective-permute-start.1 = (f32[8,128]{1,0:T(8,128)S(1)}, f32[8,128]{1,0:T(8,128)S(1)}, u32[]{:S(2)}, u32[]{:S(2)}) collective-permute-start(f32[8,128]{1,0:T(8,128)S(1)} %get-tuple-element.86), channel_id=1, source_target_pairs={{0,12},{4,8},{8,4},{12,0},{1,13},{5,9},{9,5},{13,1},{2,14},{6,10},... | collective-permute-start | bytes 12296 | tf_op jit(solution)/shard_map/ppermute | solution.py:334
  7.8 0.5 first.1
  8.3 3.4 %collective-permute-done.1.refs_1_ = f32[8,128]{1,0:T(8,128)S(1)} collective-permute-done((f32[8,128]{1,0:T(8,128)S(1)}, f32[8,128]{1,0:T(8,128)S(1)}, u32[]{:S(2)}, u32[]{:S(2)}) %collective-permute-start.1) | collective-permute-done | bytes 4128 | tf_op jit(solution)/shard_map/ppermute | solution.py:334
  11.9 1.3 %collective-permute-start.3 = (f32[128,128]{1,0:T(8,128)S(1)}, f32[128,128]{1,0:T(8,128)S(1)}, u32[]{:S(2)}, u32[]{:S(2)}) collective-permute-start(f32[128,128]{1,0:T(8,128)S(1)} %get-tuple-element.91), channel_id=1, source_target_pairs={{0,8},{4,12},{8,0},{12,4},{1,9},{5,13},{9,1},{13,5},{2,10},{6,14},... | collective-permute-start | bytes 196616 | tf_op jit(solution)/shard_map/ppermute | solution.py:334
  13.2 0.9 collective-permute-start.4
  14.1 1.3 %collective-permute-start.5 = (f32[128,128]{1,0:T(8,128)S(1)}, f32[128,128]{1,0:T(8,128)S(1)}, u32[]{:S(2)}, u32[]{:S(2)}) collective-permute-start(f32[128,128]{1,0:T(8,128)S(1)} %get-tuple-element.93), channel_id=1, source_target_pairs={{0,4},{4,0},{8,12},{12,8},{1,5},{5,1},{9,13},{13,9},{2,6},{6,2},{1... | collective-permute-start | bytes 196616 | tf_op jit(solution)/shard_map/ppermute | solution.py:334
  16.2 0.3 marks.1
  16.7 3.8 %rest_start.1 = (f32[768,128]{1,0:T(8,128)S(1)}, f32[64,128]{1,0:T(8,128)S(1)}, bf16[768,1024]{1,0:T(8,128)(2,1)S(1)}, bf16[768,1024]{1,0:T(8,128)(2,1)S(1)}) custom-call(s32[1]{0:T(128)S(6)} %copy.15.size, f32[1024,1024]{1,0:T(8,128)} %bitcast.31, f32[1024,128]{1,0:T(8,128)S(1)} %bitcast.20, f32[1024,128]{1,0:T(8,128)S(1)} %bitcast.21, ...), custom_call_target="tpu_custom_call" | custom-call | flops 603979776 | bytes 6291456 | tf_op jit(solution)/shard_map/rest_start/pallas_call | solution.py:49
  20.6 0.4 coarse.2
  21.0 2.1 %collective-permute-start.6 = (f32[64,128]{1,0:T(8,128)S(1)}, f32[64,128]{1,0:T(8,128)S(1)}, u32[]{:S(2)}, u32[]{:S(2)}) collective-permute-start(f32[64,128]{1,0:T(8,128)S(1)} %get-tuple-element.98), channel_id=1, source_target_pairs={{0,12},{4,8},{8,4},{12,0},{1,13},{5,9},{9,5},{13,1},{2,14},{6,10},... | collective-permute-start | bytes 98312 | tf_op jit(solution)/shard_map/ppermute | solution.py:334
  23.3 2.2 %collective-permute-start.8 = (f32[64,128]{1,0:T(8,128)S(1)}, f32[64,128]{1,0:T(8,128)S(1)}, u32[]{:S(2)}, u32[]{:S(2)}) collective-permute-start(f32[64,128]{1,0:T(8,128)S(1)} %get-tuple-element.100), channel_id=1, source_target_pairs={{0,4},{4,0},{8,12},{12,8},{1,5},{5,1},{9,13},{13,9},{2,6},{6,2},{1... | collective-permute-start | bytes 98312 | tf_op jit(solution)/shard_map/ppermute | solution.py:334
  25.5 0.4 prepare.1
  25.9 0.9 %collective-permute-done.6.refs_1_ = f32[64,128]{1,0:T(8,128)S(1)} collective-permute-done((f32[64,128]{1,0:T(8,128)S(1)}, f32[64,128]{1,0:T(8,128)S(1)}, u32[]{:S(2)}, u32[]{:S(2)}) %collective-permute-start.6) | collective-permute-done | bytes 32800 | tf_op jit(solution)/shard_map/ppermute | solution.py:334
  26.8 1.5 %collective-permute-done.7.refs_2_ = f32[64,128]{1,0:T(8,128)S(1)} collective-permute-done((f32[64,128]{1,0:T(8,128)S(1)}, f32[64,128]{1,0:T(8,128)S(1)}, u32[]{:S(2)}, u32[]{:S(2)}) %collective-permute-start.7) | collective-permute-done | bytes 32800 | tf_op jit(solution)/shard_map/ppermute | solution.py:334
  28.6 1.6 %collective-permute-start.10 = (f32[64,128]{1,0:T(8,128)S(1)}, f32[64,128]{1,0:T(8,128)S(1)}, u32[]{:S(2)}, u32[]{:S(2)}) collective-permute-start(f32[64,128]{1,0:T(8,128)S(1)} %get-tuple-element.103), channel_id=1, source_target_pairs={{0,2},{1,3},{2,0},{3,1},{4,6},{5,7},{6,4},{7,5},{8,10},{9,11},{10,... | collective-permute-start | bytes 98312 | tf_op jit(solution)/shard_map/ppermute | solution.py:334
  30.2 0.3 collective-permute-start.11
  30.7 1.5 %collective-permute-done.9.refs_1_ = f32[64,128]{1,0:T(8,128)S(1)} collective-permute-done((f32[64,128]{1,0:T(8,128)S(1)}, f32[64,128]{1,0:T(8,128)S(1)}, u32[]{:S(2)}, u32[]{:S(2)}) %collective-permute-start.9) | collective-permute-done | bytes 32800 | tf_op jit(solution)/shard_map/ppermute | solution.py:334
  32.3 0.4 collective-permute-done.10.refs_2_
  32.7 1.0 %lift.2 = (f32[256,128]{1,0:T(8,128)S(1)}, f32[768,128]{1,0:T(8,128)S(1)}, f32[256,128]{1,0:T(8,128)S(1)}, f32[128,128]{1,0:T(8,128)S(1)}, f32[128,128]{1,0:T(8,128)S(1)}, /*index=5*/f32[128,128]{1,0:T(8,128)S(1)}) custom-call(s32[1]{0:T(128)S(6)} %copy.15.size, f32[64,128]{1,0:T(8,128)S(1)} %get-tuple-element.101.refs_0_, ...), custom_call_target="tpu_custom_call" | custom-call | flops 201326592 | bytes 1048576 | tf_op jit(solution)/shard_map/lift/pallas_call | solution.py:49
  33.7 1.7 %collective-permute-start.12 = (f32[128,128]{1,0:T(8,128)S(1)}, f32[128,128]{1,0:T(8,128)S(1)}, u32[]{:S(2)}, u32[]{:S(2)}) collective-permute-start(f32[128,128]{1,0:T(8,128)S(1)} %get-tuple-element.112), channel_id=1, source_target_pairs={{0,8},{4,12},{8,0},{12,4},{1,9},{5,13},{9,1},{13,5},{2,10},{6,14},... | collective-permute-start | bytes 196616 | tf_op jit(solution)/shard_map/ppermute | solution.py:334
  35.4 1.8 %collective-permute-start.13 = (f32[128,128]{1,0:T(8,128)S(1)}, f32[128,128]{1,0:T(8,128)S(1)}, u32[]{:S(2)}, u32[]{:S(2)}) collective-permute-start(f32[128,128]{1,0:T(8,128)S(1)} %get-tuple-element.113), channel_id=1, source_target_pairs={{0,12},{4,8},{8,4},{12,0},{1,13},{5,9},{9,5},{13,1},{2,14},{6,10},... | collective-permute-start | bytes 196616 | tf_op jit(solution)/shard_map/ppermute | solution.py:334
  37.4 1.5 %rest.3 = (f32[768,128]{1,0:T(8,128)S(1)}, f32[640,128]{1,0:T(8,128)S(1)}) custom-call(s32[1]{0:T(128)S(6)} %copy.15.size, bf16[768,1024]{1,0:T(8,128)(2,1)S(1)} %get-tuple-element.119.high, bf16[768,1024]{1,0:T(8,128)(2,1)S(1)} %get-tuple-element.120.low, f32[256,128]{1,0:T(8,128)S(1)} %get-tuple-element.116.mult_s.refs_5_, ...), custom_call_target="tpu_custom_call" | custom-call | flops 805306368 | bytes 4194304 | tf_op jit(solution)/shard_map/rest/pallas_call | solution.py:49
  38.9 3.4 %collective-permute-done.12.refs_0_ = f32[128,128]{1,0:T(8,128)S(1)} collective-permute-done((f32[128,128]{1,0:T(8,128)S(1)}, f32[128,128]{1,0:T(8,128)S(1)}, u32[]{:S(2)}, u32[]{:S(2)}) %collective-permute-start.12) | collective-permute-done | bytes 65568 | tf_op jit(solution)/shard_map/ppermute | solution.py:334
  42.3 0.8 collective-permute-done.14.refs_2_
  43.1 0.5 sweep.3
  43.6 1.0 %collective-permute-start.15 = (f32[128,128]{1,0:T(8,128)S(1)}, f32[128,128]{1,0:T(8,128)S(1)}, u32[]{:S(2)}, u32[]{:S(2)}) collective-permute-start(f32[128,128]{1,0:T(8,128)S(1)} %get-tuple-element.123), channel_id=1, source_target_pairs={{0,8},{4,12},{8,0},{12,4},{1,9},{5,13},{9,1},{13,5},{2,10},{6,14},... | collective-permute-start | bytes 196616 | tf_op jit(solution)/shard_map/ppermute | solution.py:334
  44.6 2.0 %collective-permute-start.16 = (f32[128,128]{1,0:T(8,128)S(1)}, f32[128,128]{1,0:T(8,128)S(1)}, u32[]{:S(2)}, u32[]{:S(2)}) collective-permute-start(f32[128,128]{1,0:T(8,128)S(1)} %get-tuple-element.124), channel_id=1, source_target_pairs={{0,12},{4,8},{8,4},{12,0},{1,13},{5,9},{9,5},{13,1},{2,14},{6,10},... | collective-permute-start | bytes 196616 | tf_op jit(solution)/shard_map/ppermute | solution.py:334
  46.7 0.5 collective-permute-start.17
  47.4 1.5 %rest.4 = (f32[768,128]{1,0:T(8,128)S(1)}, f32[640,128]{1,0:T(8,128)S(1)}) custom-call(s32[1]{0:T(128)S(6)} %copy.15.size, bf16[768,1024]{1,0:T(8,128)(2,1)S(1)} %get-tuple-element.119.high, bf16[768,1024]{1,0:T(8,128)(2,1)S(1)} %get-tuple-element.120.low, f32[256,128]{1,0:T(8,128)S(1)} %get-tuple-element.127.mult_s.refs_5_, ...), custom_call_target="tpu_custom_call" | custom-call | flops 805306368 | bytes 4194304 | tf_op jit(solution)/shard_map/rest/pallas_call | solution.py:49
  48.9 2.8 %collective-permute-done.15.refs_0_ = f32[128,128]{1,0:T(8,128)S(1)} collective-permute-done((f32[128,128]{1,0:T(8,128)S(1)}, f32[128,128]{1,0:T(8,128)S(1)}, u32[]{:S(2)}, u32[]{:S(2)}) %collective-permute-start.15) | collective-permute-done | bytes 65568 | tf_op jit(solution)/shard_map/ppermute | solution.py:334
  51.7 0.3 collective-permute-done.17.refs_2_
  52.0 0.5 sweep.4
  52.5 1.4 %collective-permute-start.18 = (f32[128,128]{1,0:T(8,128)S(1)}, f32[128,128]{1,0:T(8,128)S(1)}, u32[]{:S(2)}, u32[]{:S(2)}) collective-permute-start(f32[128,128]{1,0:T(8,128)S(1)} %get-tuple-element.130), channel_id=1, source_target_pairs={{0,8},{4,12},{8,0},{12,4},{1,9},{5,13},{9,1},{13,5},{2,10},{6,14},... | collective-permute-start | bytes 196616 | tf_op jit(solution)/shard_map/ppermute | solution.py:334
  53.9 2.0 %collective-permute-start.19 = (f32[128,128]{1,0:T(8,128)S(1)}, f32[128,128]{1,0:T(8,128)S(1)}, u32[]{:S(2)}, u32[]{:S(2)}) collective-permute-start(f32[128,128]{1,0:T(8,128)S(1)} %get-tuple-element.131), channel_id=1, source_target_pairs={{0,12},{4,8},{8,4},{12,0},{1,13},{5,9},{9,5},{13,1},{2,14},{6,10},... | collective-permute-start | bytes 196616 | tf_op jit(solution)/shard_map/ppermute | solution.py:334
  56.3 1.1 %rest_first.1 = (f32[768,128]{1,0:T(8,128)S(1)}, f32[64,128]{1,0:T(8,128)S(1)}) custom-call(s32[1]{0:T(128)S(6)} %copy.15.size, bf16[768,1024]{1,0:T(8,128)(2,1)S(1)} %get-tuple-element.119.high, bf16[768,1024]{1,0:T(8,128)(2,1)S(1)} %get-tuple-element.120.low, f32[256,128]{1,0:T(8,128)S(1)} %get-tuple-element.134.mult_s.refs_5_, ...), custom_call_target="tpu_custom_call" | custom-call | flops 603979776 | bytes 3145728 | tf_op jit(solution)/shard_map/rest_first/pallas_call | solution.py:49
  57.4 1.7 %collective-permute-done.18.refs_0_ = f32[128,128]{1,0:T(8,128)S(1)} collective-permute-done((f32[128,128]{1,0:T(8,128)S(1)}, f32[128,128]{1,0:T(8,128)S(1)}, u32[]{:S(2)}, u32[]{:S(2)}) %collective-permute-start.18) | collective-permute-done | bytes 65568 | tf_op jit(solution)/shard_map/ppermute | solution.py:334
  59.1 0.9 %collective-permute-done.19.refs_1_ = f32[128,128]{1,0:T(8,128)S(1)} collective-permute-done((f32[128,128]{1,0:T(8,128)S(1)}, f32[128,128]{1,0:T(8,128)S(1)}, u32[]{:S(2)}, u32[]{:S(2)}) %collective-permute-start.19) | collective-permute-done | bytes 65568 | tf_op jit(solution)/shard_map/ppermute | solution.py:334
  60.1 0.6 collective-permute-done.20.refs_2_
  60.7 0.4 coarse.3
  61.2 2.0 %collective-permute-start.21 = (f32[64,128]{1,0:T(8,128)S(1)}, f32[64,128]{1,0:T(8,128)S(1)}, u32[]{:S(2)}, u32[]{:S(2)}) collective-permute-start(f32[64,128]{1,0:T(8,128)S(1)} %get-tuple-element.138), channel_id=1, source_target_pairs={{0,12},{4,8},{8,4},{12,0},{1,13},{5,9},{9,5},{13,1},{2,14},{6,10},... | collective-permute-start | bytes 98312 | tf_op jit(solution)/shard_map/ppermute | solution.py:334
  63.2 2.4 %collective-permute-start.23 = (f32[64,128]{1,0:T(8,128)S(1)}, f32[64,128]{1,0:T(8,128)S(1)}, u32[]{:S(2)}, u32[]{:S(2)}) collective-permute-start(f32[64,128]{1,0:T(8,128)S(1)} %get-tuple-element.140), channel_id=1, source_target_pairs={{0,4},{4,0},{8,12},{12,8},{1,5},{5,1},{9,13},{13,9},{2,6},{6,2},{1... | collective-permute-start | bytes 98312 | tf_op jit(solution)/shard_map/ppermute | solution.py:334
  65.6 1.3 %collective-permute-done.21.refs_1_ = f32[64,128]{1,0:T(8,128)S(1)} collective-permute-done((f32[64,128]{1,0:T(8,128)S(1)}, f32[64,128]{1,0:T(8,128)S(1)}, u32[]{:S(2)}, u32[]{:S(2)}) %collective-permute-start.21) | collective-permute-done | bytes 32800 | tf_op jit(solution)/shard_map/ppermute | solution.py:334
  66.9 1.1 %collective-permute-done.22.refs_2_ = f32[64,128]{1,0:T(8,128)S(1)} collective-permute-done((f32[64,128]{1,0:T(8,128)S(1)}, f32[64,128]{1,0:T(8,128)S(1)}, u32[]{:S(2)}, u32[]{:S(2)}) %collective-permute-start.22) | collective-permute-done | bytes 32800 | tf_op jit(solution)/shard_map/ppermute | solution.py:334
  68.3 0.3 collective-permute-start.25
  68.7 1.5 %collective-permute-start.26 = (f32[64,128]{1,0:T(8,128)S(1)}, f32[64,128]{1,0:T(8,128)S(1)}, u32[]{:S(2)}, u32[]{:S(2)}) collective-permute-start(f32[64,128]{1,0:T(8,128)S(1)} %get-tuple-element.144), channel_id=1, source_target_pairs={{0,1},{1,0},{2,3},{3,2},{4,5},{5,4},{6,7},{7,6},{8,9},{9,8},{10,11... | collective-permute-start | bytes 98312 | tf_op jit(solution)/shard_map/ppermute | solution.py:334
  70.2 1.5 %collective-permute-done.24.refs_1_ = f32[64,128]{1,0:T(8,128)S(1)} collective-permute-done((f32[64,128]{1,0:T(8,128)S(1)}, f32[64,128]{1,0:T(8,128)S(1)}, u32[]{:S(2)}, u32[]{:S(2)}) %collective-permute-start.24) | collective-permute-done | bytes 32800 | tf_op jit(solution)/shard_map/ppermute | solution.py:334
  71.7 0.7 collective-permute-done.25.refs_2_
  72.4 1.0 %lift.3 = (f32[256,128]{1,0:T(8,128)S(1)}, f32[768,128]{1,0:T(8,128)S(1)}, f32[256,128]{1,0:T(8,128)S(1)}, f32[128,128]{1,0:T(8,128)S(1)}, f32[128,128]{1,0:T(8,128)S(1)}, /*index=5*/f32[128,128]{1,0:T(8,128)S(1)}) custom-call(s32[1]{0:T(128)S(6)} %copy.15.size, f32[64,128]{1,0:T(8,128)S(1)} %get-tuple-element.141.refs_0_, ...), custom_call_target="tpu_custom_call" | custom-call | flops 201326592 | bytes 1048576 | tf_op jit(solution)/shard_map/lift/pallas_call | solution.py:49
  73.4 2.1 %collective-permute-start.27 = (f32[128,128]{1,0:T(8,128)S(1)}, f32[128,128]{1,0:T(8,128)S(1)}, u32[]{:S(2)}, u32[]{:S(2)}) collective-permute-start(f32[128,128]{1,0:T(8,128)S(1)} %get-tuple-element.147), channel_id=1, source_target_pairs={{0,8},{4,12},{8,0},{12,4},{1,9},{5,13},{9,1},{13,5},{2,10},{6,14},... | collective-permute-start | bytes 196616 | tf_op jit(solution)/shard_map/ppermute | solution.py:334
  75.5 1.9 %collective-permute-start.28 = (f32[128,128]{1,0:T(8,128)S(1)}, f32[128,128]{1,0:T(8,128)S(1)}, u32[]{:S(2)}, u32[]{:S(2)}) collective-permute-start(f32[128,128]{1,0:T(8,128)S(1)} %get-tuple-element.148), channel_id=1, source_target_pairs={{0,12},{4,8},{8,4},{12,0},{1,13},{5,9},{9,5},{13,1},{2,14},{6,10},... | collective-permute-start | bytes 196616 | tf_op jit(solution)/shard_map/ppermute | solution.py:334
  77.5 1.5 %rest.5 = (f32[768,128]{1,0:T(8,128)S(1)}, f32[640,128]{1,0:T(8,128)S(1)}) custom-call(s32[1]{0:T(128)S(6)} %copy.15.size, bf16[768,1024]{1,0:T(8,128)(2,1)S(1)} %get-tuple-element.119.high, bf16[768,1024]{1,0:T(8,128)(2,1)S(1)} %get-tuple-element.120.low, f32[256,128]{1,0:T(8,128)S(1)} %get-tuple-element.151.mult_s.refs_5_, ...), custom_call_target="tpu_custom_call" | custom-call | flops 805306368 | bytes 4194304 | tf_op jit(solution)/shard_map/rest/pallas_call | solution.py:49
  79.0 2.2 %collective-permute-done.27.refs_0_ = f32[128,128]{1,0:T(8,128)S(1)} collective-permute-done((f32[128,128]{1,0:T(8,128)S(1)}, f32[128,128]{1,0:T(8,128)S(1)}, u32[]{:S(2)}, u32[]{:S(2)}) %collective-permute-start.27) | collective-permute-done | bytes 65568 | tf_op jit(solution)/shard_map/ppermute | solution.py:334
  81.2 0.7 collective-permute-done.28.refs_1_
  81.8 0.7 collective-permute-done.29.refs_2_
  82.6 0.5 sweep.5
  83.1 1.0 %collective-permute-start.30 = (f32[128,128]{1,0:T(8,128)S(1)}, f32[128,128]{1,0:T(8,128)S(1)}, u32[]{:S(2)}, u32[]{:S(2)}) collective-permute-start(f32[128,128]{1,0:T(8,128)S(1)} %get-tuple-element.154), channel_id=1, source_target_pairs={{0,8},{4,12},{8,0},{12,4},{1,9},{5,13},{9,1},{13,5},{2,10},{6,14},... | collective-permute-start | bytes 196616 | tf_op jit(solution)/shard_map/ppermute | solution.py:334
  84.1 1.9 %collective-permute-start.31 = (f32[128,128]{1,0:T(8,128)S(1)}, f32[128,128]{1,0:T(8,128)S(1)}, u32[]{:S(2)}, u32[]{:S(2)}) collective-permute-start(f32[128,128]{1,0:T(8,128)S(1)} %get-tuple-element.155), channel_id=1, source_target_pairs={{0,12},{4,8},{8,4},{12,0},{1,13},{5,9},{9,5},{13,1},{2,14},{6,10},... | collective-permute-start | bytes 196616 | tf_op jit(solution)/shard_map/ppermute | solution.py:334
  86.0 0.7 collective-permute-start.32
  86.9 1.9 %rest_last.1 = (f32[1024,128]{1,0:T(8,128)}, f32[1024,128]{1,0:T(8,128)}) custom-call(s32[1]{0:T(128)S(6)} %copy.15.size, bf16[768,1024]{1,0:T(8,128)(2,1)S(1)} %get-tuple-element.119.high, bf16[768,1024]{1,0:T(8,128)(2,1)S(1)} %get-tuple-element.120.low, f32[256,128]{1,0:T(8,128)S(1)} %get-tuple-element.158.mult_s.refs_5_, ...), custom_call_target="tpu_custom_call" | custom-call | flops 603979776 | bytes 3145728 | tf_op jit(solution)/shard_map/rest_last/pallas_call | solution.py:49
  88.8 1.7 %collective-permute-done.30.refs_0_ = f32[128,128]{1,0:T(8,128)S(1)} collective-permute-done((f32[128,128]{1,0:T(8,128)S(1)}, f32[128,128]{1,0:T(8,128)S(1)}, u32[]{:S(2)}, u32[]{:S(2)}) %collective-permute-start.30) | collective-permute-done | bytes 65568 | tf_op jit(solution)/shard_map/ppermute | solution.py:334
  90.5 0.6 collective-permute-done.32.refs_2_
  91.1 0.9 %last.1 = (f32[1024,128]{1,0:T(8,128)}, f32[1024,128]{1,0:T(8,128)}) custom-call(s32[1]{0:T(128)S(6)} %copy.15.size, f32[128,128]{1,0:T(8,128)S(1)} %collective-permute-done.30.refs_0_, f32[128,128]{1,0:T(8,128)S(1)} %collective-permute-done.31.refs_1_, ...), custom_call_target="tpu_custom_call", output_to_operand_aliasing={{0}: (8, {}), {1}: (9, {})} | custom-call | flops 75497472 | bytes 196608 | tf_op jit(solution)/shard_map/last/pallas_call | solution.py:49
  (44 shorter events, 3.0 us)
Async XLA Ops:
  2.1 14.0 %copy-start.5 = (s32[1,256,1]{1,2,0:T(1,128)S(1)}, s32[1,256,1]{1,2,0:T(1,128)}, u32[]{:S(2)}) copy-start(s32[1,256,1]{1,2,0:T(1,128)} %param.14) | copy-start | bytes 3076
  2.1 14.0 %copy-start.6 = (s32[1,256]{1,0:T(1,128)S(1)}, s32[1,256]{1,0:T(1,128)}, u32[]{:S(2)}) copy-start(s32[1,256]{1,0:T(1,128)} %rows.1) | copy-start | bytes 3076
  2.1 14.3 %copy-start = (f32[1,1024,128]{2,1,0:T(8,128)S(1)}, f32[1,1024,128]{2,1,0:T(8,128)}, u32[]{:S(2)}) copy-start(f32[1,1024,128]{2,1,0:T(8,128)} %param.12) | copy-start | bytes 1572868
  2.1 14.5 %copy-start.1 = (f32[1,1024,128]{2,1,0:T(8,128)S(1)}, f32[1,1024,128]{2,1,0:T(8,128)}, u32[]{:S(2)}) copy-start(f32[1,1024,128]{2,1,0:T(8,128)} %param.13) | copy-start | bytes 1572868
  2.1 14.5 %copy-start.2 = (f32[1,64,1024]{2,1,0:T(8,128)S(1)}, f32[1,64,1024]{2,1,0:T(8,128)}, u32[]{:S(2)}) copy-start(f32[1,64,1024]{2,1,0:T(8,128)} %param.11) | copy-start | bytes 786436
  2.2 6.1 %collective-permute-start = (f32[8,128]{1,0:T(8,128)S(1)}, f32[8,128]{1,0:T(8,128)S(1)}, u32[]{:S(2)}, u32[]{:S(2)}) collective-permute-start(f32[8,128]{1,0:T(8,128)S(1)} %get-tuple-element.85), channel_id=1, source_target_pairs={{0,8},{4,12},{8,0},{12,4},{1,9},{5,13},{9,1},{13,5},{2,10},{6,14},... | collective-permute-start | bytes 12296 | tf_op jit(solution)/shard_map/ppermute | solution.py:334
  6.3 5.4 %collective-permute-start.1 = (f32[8,128]{1,0:T(8,128)S(1)}, f32[8,128]{1,0:T(8,128)S(1)}, u32[]{:S(2)}, u32[]{:S(2)}) collective-permute-start(f32[8,128]{1,0:T(8,128)S(1)} %get-tuple-element.86), channel_id=1, source_target_pairs={{0,12},{4,8},{8,4},{12,0},{1,13},{5,9},{9,5},{13,1},{2,14},{6,10},... | collective-permute-start | bytes 12296 | tf_op jit(solution)/shard_map/ppermute | solution.py:334
  7.6 4.1 %collective-permute-start.2 = (f32[8,128]{1,0:T(8,128)S(1)}, f32[8,128]{1,0:T(8,128)S(1)}, u32[]{:S(2)}, u32[]{:S(2)}) collective-permute-start(f32[8,128]{1,0:T(8,128)S(1)} %get-tuple-element.87), channel_id=1, source_target_pairs={{0,4},{4,0},{8,12},{12,8},{1,5},{5,1},{9,13},{13,9},{2,6},{6,2},{1... | collective-permute-start | bytes 12296 | tf_op jit(solution)/shard_map/ppermute | solution.py:334
  11.9 8.6 %collective-permute-start.3 = (f32[128,128]{1,0:T(8,128)S(1)}, f32[128,128]{1,0:T(8,128)S(1)}, u32[]{:S(2)}, u32[]{:S(2)}) collective-permute-start(f32[128,128]{1,0:T(8,128)S(1)} %get-tuple-element.91), channel_id=1, source_target_pairs={{0,8},{4,12},{8,0},{12,4},{1,9},{5,13},{9,1},{13,5},{2,10},{6,14},... | collective-permute-start | bytes 196616 | tf_op jit(solution)/shard_map/ppermute | solution.py:334
  13.2 7.3 %collective-permute-start.4 = (f32[128,128]{1,0:T(8,128)S(1)}, f32[128,128]{1,0:T(8,128)S(1)}, u32[]{:S(2)}, u32[]{:S(2)}) collective-permute-start(f32[128,128]{1,0:T(8,128)S(1)} %get-tuple-element.92), channel_id=1, source_target_pairs={{0,12},{4,8},{8,4},{12,0},{1,13},{5,9},{9,5},{13,1},{2,14},{6,10},... | collective-permute-start | bytes 196616 | tf_op jit(solution)/shard_map/ppermute | solution.py:334
  14.1 6.4 %collective-permute-start.5 = (f32[128,128]{1,0:T(8,128)S(1)}, f32[128,128]{1,0:T(8,128)S(1)}, u32[]{:S(2)}, u32[]{:S(2)}) collective-permute-start(f32[128,128]{1,0:T(8,128)S(1)} %get-tuple-element.93), channel_id=1, source_target_pairs={{0,4},{4,0},{8,12},{12,8},{1,5},{5,1},{9,13},{13,9},{2,6},{6,2},{1... | collective-permute-start | bytes 196616 | tf_op jit(solution)/shard_map/ppermute | solution.py:334
  16.7 8.8 %copy-start.3 = (f32[256,256]{1,0:T(8,128)S(1)}, f32[256,256]{1,0:T(8,128)}, u32[]{:S(2)}) copy-start(f32[256,256]{1,0:T(8,128)} %tile.3) | copy-start | bytes 786436
  16.7 8.8 %copy-start.4 = (s32[1,1024]{1,0:T(1,128)S(1)}, s32[1,1024]{1,0:T(1,128)}, u32[]{:S(2)}) copy-start(s32[1,1024]{1,0:T(1,128)} %contact.1) | copy-start | bytes 12292
  21.0 5.8 %collective-permute-start.6 = (f32[64,128]{1,0:T(8,128)S(1)}, f32[64,128]{1,0:T(8,128)S(1)}, u32[]{:S(2)}, u32[]{:S(2)}) collective-permute-start(f32[64,128]{1,0:T(8,128)S(1)} %get-tuple-element.98), channel_id=1, source_target_pairs={{0,12},{4,8},{8,4},{12,0},{1,13},{5,9},{9,5},{13,1},{2,14},{6,10},... | collective-permute-start | bytes 98312 | tf_op jit(solution)/shard_map/ppermute | solution.py:334
  23.1 5.2 %collective-permute-start.7 = (f32[64,128]{1,0:T(8,128)S(1)}, f32[64,128]{1,0:T(8,128)S(1)}, u32[]{:S(2)}, u32[]{:S(2)}) collective-permute-start(f32[64,128]{1,0:T(8,128)S(1)} %get-tuple-element.99), channel_id=1, source_target_pairs={{0,8},{4,12},{8,0},{12,4},{1,9},{5,13},{9,1},{13,5},{2,10},{6,14},... | collective-permute-start | bytes 98312 | tf_op jit(solution)/shard_map/ppermute | solution.py:334
  23.3 5.0 %collective-permute-start.8 = (f32[64,128]{1,0:T(8,128)S(1)}, f32[64,128]{1,0:T(8,128)S(1)}, u32[]{:S(2)}, u32[]{:S(2)}) collective-permute-start(f32[64,128]{1,0:T(8,128)S(1)} %get-tuple-element.100), channel_id=1, source_target_pairs={{0,4},{4,0},{8,12},{12,8},{1,5},{5,1},{9,13},{13,9},{2,6},{6,2},{1... | collective-permute-start | bytes 98312 | tf_op jit(solution)/shard_map/ppermute | solution.py:334
  28.5 3.7 %collective-permute-start.9 = (f32[64,128]{1,0:T(8,128)S(1)}, f32[64,128]{1,0:T(8,128)S(1)}, u32[]{:S(2)}, u32[]{:S(2)}) collective-permute-start(f32[64,128]{1,0:T(8,128)S(1)} %get-tuple-element.102), channel_id=1, source_target_pairs={{0,3},{1,2},{2,1},{3,0},{4,7},{5,6},{6,5},{7,4},{8,11},{9,10},{10,... | collective-permute-start | bytes 98312 | tf_op jit(solution)/shard_map/ppermute | solution.py:334
  28.6 4.0 %collective-permute-start.10 = (f32[64,128]{1,0:T(8,128)S(1)}, f32[64,128]{1,0:T(8,128)S(1)}, u32[]{:S(2)}, u32[]{:S(2)}) collective-permute-start(f32[64,128]{1,0:T(8,128)S(1)} %get-tuple-element.103), channel_id=1, source_target_pairs={{0,2},{1,3},{2,0},{3,1},{4,6},{5,7},{6,4},{7,5},{8,10},{9,11},{10,... | collective-permute-start | bytes 98312 | tf_op jit(solution)/shard_map/ppermute | solution.py:334
  30.2 2.5 %collective-permute-start.11 = (f32[64,128]{1,0:T(8,128)S(1)}, f32[64,128]{1,0:T(8,128)S(1)}, u32[]{:S(2)}, u32[]{:S(2)}) collective-permute-start(f32[64,128]{1,0:T(8,128)S(1)} %get-tuple-element.104), channel_id=1, source_target_pairs={{0,1},{1,0},{2,3},{3,2},{4,5},{5,4},{6,7},{7,6},{8,9},{9,8},{10,11... | collective-permute-start | bytes 98312 | tf_op jit(solution)/shard_map/ppermute | solution.py:334
  33.7 8.7 %collective-permute-start.12 = (f32[128,128]{1,0:T(8,128)S(1)}, f32[128,128]{1,0:T(8,128)S(1)}, u32[]{:S(2)}, u32[]{:S(2)}) collective-permute-start(f32[128,128]{1,0:T(8,128)S(1)} %get-tuple-element.112), channel_id=1, source_target_pairs={{0,8},{4,12},{8,0},{12,4},{1,9},{5,13},{9,1},{13,5},{2,10},{6,14},... | collective-permute-start | bytes 196616 | tf_op jit(solution)/shard_map/ppermute | solution.py:334
  35.4 6.9 %collective-permute-start.13 = (f32[128,128]{1,0:T(8,128)S(1)}, f32[128,128]{1,0:T(8,128)S(1)}, u32[]{:S(2)}, u32[]{:S(2)}) collective-permute-start(f32[128,128]{1,0:T(8,128)S(1)} %get-tuple-element.113), channel_id=1, source_target_pairs={{0,12},{4,8},{8,4},{12,0},{1,13},{5,9},{9,5},{13,1},{2,14},{6,10},... | collective-permute-start | bytes 196616 | tf_op jit(solution)/shard_map/ppermute | solution.py:334
  37.2 5.9 %collective-permute-start.14 = (f32[128,128]{1,0:T(8,128)S(1)}, f32[128,128]{1,0:T(8,128)S(1)}, u32[]{:S(2)}, u32[]{:S(2)}) collective-permute-start(f32[128,128]{1,0:T(8,128)S(1)} %get-tuple-element.114), channel_id=1, source_target_pairs={{0,4},{4,0},{8,12},{12,8},{1,5},{5,1},{9,13},{13,9},{2,6},{6,2},{1... | collective-permute-start | bytes 196616 | tf_op jit(solution)/shard_map/ppermute | solution.py:334
  43.6 8.0 %collective-permute-start.15 = (f32[128,128]{1,0:T(8,128)S(1)}, f32[128,128]{1,0:T(8,128)S(1)}, u32[]{:S(2)}, u32[]{:S(2)}) collective-permute-start(f32[128,128]{1,0:T(8,128)S(1)} %get-tuple-element.123), channel_id=1, source_target_pairs={{0,8},{4,12},{8,0},{12,4},{1,9},{5,13},{9,1},{13,5},{2,10},{6,14},... | collective-permute-start | bytes 196616 | tf_op jit(solution)/shard_map/ppermute | solution.py:334
  44.6 7.0 %collective-permute-start.16 = (f32[128,128]{1,0:T(8,128)S(1)}, f32[128,128]{1,0:T(8,128)S(1)}, u32[]{:S(2)}, u32[]{:S(2)}) collective-permute-start(f32[128,128]{1,0:T(8,128)S(1)} %get-tuple-element.124), channel_id=1, source_target_pairs={{0,12},{4,8},{8,4},{12,0},{1,13},{5,9},{9,5},{13,1},{2,14},{6,10},... | collective-permute-start | bytes 196616 | tf_op jit(solution)/shard_map/ppermute | solution.py:334
  46.7 5.3 %collective-permute-start.17 = (f32[128,128]{1,0:T(8,128)S(1)}, f32[128,128]{1,0:T(8,128)S(1)}, u32[]{:S(2)}, u32[]{:S(2)}) collective-permute-start(f32[128,128]{1,0:T(8,128)S(1)} %get-tuple-element.125), channel_id=1, source_target_pairs={{0,4},{4,0},{8,12},{12,8},{1,5},{5,1},{9,13},{13,9},{2,6},{6,2},{1... | collective-permute-start | bytes 196616 | tf_op jit(solution)/shard_map/ppermute | solution.py:334
  52.5 6.6 %collective-permute-start.18 = (f32[128,128]{1,0:T(8,128)S(1)}, f32[128,128]{1,0:T(8,128)S(1)}, u32[]{:S(2)}, u32[]{:S(2)}) collective-permute-start(f32[128,128]{1,0:T(8,128)S(1)} %get-tuple-element.130), channel_id=1, source_target_pairs={{0,8},{4,12},{8,0},{12,4},{1,9},{5,13},{9,1},{13,5},{2,10},{6,14},... | collective-permute-start | bytes 196616 | tf_op jit(solution)/shard_map/ppermute | solution.py:334
  53.9 6.2 %collective-permute-start.19 = (f32[128,128]{1,0:T(8,128)S(1)}, f32[128,128]{1,0:T(8,128)S(1)}, u32[]{:S(2)}, u32[]{:S(2)}) collective-permute-start(f32[128,128]{1,0:T(8,128)S(1)} %get-tuple-element.131), channel_id=1, source_target_pairs={{0,12},{4,8},{8,4},{12,0},{1,13},{5,9},{9,5},{13,1},{2,14},{6,10},... | collective-permute-start | bytes 196616 | tf_op jit(solution)/shard_map/ppermute | solution.py:334
  55.9 4.8 %collective-permute-start.20 = (f32[128,128]{1,0:T(8,128)S(1)}, f32[128,128]{1,0:T(8,128)S(1)}, u32[]{:S(2)}, u32[]{:S(2)}) collective-permute-start(f32[128,128]{1,0:T(8,128)S(1)} %get-tuple-element.132), channel_id=1, source_target_pairs={{0,4},{4,0},{8,12},{12,8},{1,5},{5,1},{9,13},{13,9},{2,6},{6,2},{1... | collective-permute-start | bytes 196616 | tf_op jit(solution)/shard_map/ppermute | solution.py:334
  61.2 5.8 %collective-permute-start.21 = (f32[64,128]{1,0:T(8,128)S(1)}, f32[64,128]{1,0:T(8,128)S(1)}, u32[]{:S(2)}, u32[]{:S(2)}) collective-permute-start(f32[64,128]{1,0:T(8,128)S(1)} %get-tuple-element.138), channel_id=1, source_target_pairs={{0,12},{4,8},{8,4},{12,0},{1,13},{5,9},{9,5},{13,1},{2,14},{6,10},... | collective-permute-start | bytes 98312 | tf_op jit(solution)/shard_map/ppermute | solution.py:334
  63.2 4.8 %collective-permute-start.22 = (f32[64,128]{1,0:T(8,128)S(1)}, f32[64,128]{1,0:T(8,128)S(1)}, u32[]{:S(2)}, u32[]{:S(2)}) collective-permute-start(f32[64,128]{1,0:T(8,128)S(1)} %get-tuple-element.139), channel_id=1, source_target_pairs={{0,8},{4,12},{8,0},{12,4},{1,9},{5,13},{9,1},{13,5},{2,10},{6,14},... | collective-permute-start | bytes 98312 | tf_op jit(solution)/shard_map/ppermute | solution.py:334
  63.2 4.8 %collective-permute-start.23 = (f32[64,128]{1,0:T(8,128)S(1)}, f32[64,128]{1,0:T(8,128)S(1)}, u32[]{:S(2)}, u32[]{:S(2)}) collective-permute-start(f32[64,128]{1,0:T(8,128)S(1)} %get-tuple-element.140), channel_id=1, source_target_pairs={{0,4},{4,0},{8,12},{12,8},{1,5},{5,1},{9,13},{13,9},{2,6},{6,2},{1... | collective-permute-start | bytes 98312 | tf_op jit(solution)/shard_map/ppermute | solution.py:334
  68.3 3.4 %collective-permute-start.24 = (f32[64,128]{1,0:T(8,128)S(1)}, f32[64,128]{1,0:T(8,128)S(1)}, u32[]{:S(2)}, u32[]{:S(2)}) collective-permute-start(f32[64,128]{1,0:T(8,128)S(1)} %get-tuple-element.142), channel_id=1, source_target_pairs={{0,3},{1,2},{2,1},{3,0},{4,7},{5,6},{6,5},{7,4},{8,11},{9,10},{10,... | collective-permute-start | bytes 98312 | tf_op jit(solution)/shard_map/ppermute | solution.py:334
  68.3 4.0 %collective-permute-start.25 = (f32[64,128]{1,0:T(8,128)S(1)}, f32[64,128]{1,0:T(8,128)S(1)}, u32[]{:S(2)}, u32[]{:S(2)}) collective-permute-start(f32[64,128]{1,0:T(8,128)S(1)} %get-tuple-element.143), channel_id=1, source_target_pairs={{0,2},{1,3},{2,0},{3,1},{4,6},{5,7},{6,4},{7,5},{8,10},{9,11},{10,... | collective-permute-start | bytes 98312 | tf_op jit(solution)/shard_map/ppermute | solution.py:334
  68.7 3.7 %collective-permute-start.26 = (f32[64,128]{1,0:T(8,128)S(1)}, f32[64,128]{1,0:T(8,128)S(1)}, u32[]{:S(2)}, u32[]{:S(2)}) collective-permute-start(f32[64,128]{1,0:T(8,128)S(1)} %get-tuple-element.144), channel_id=1, source_target_pairs={{0,1},{1,0},{2,3},{3,2},{4,5},{5,4},{6,7},{7,6},{8,9},{9,8},{10,11... | collective-permute-start | bytes 98312 | tf_op jit(solution)/shard_map/ppermute | solution.py:334
  73.4 7.8 %collective-permute-start.27 = (f32[128,128]{1,0:T(8,128)S(1)}, f32[128,128]{1,0:T(8,128)S(1)}, u32[]{:S(2)}, u32[]{:S(2)}) collective-permute-start(f32[128,128]{1,0:T(8,128)S(1)} %get-tuple-element.147), channel_id=1, source_target_pairs={{0,8},{4,12},{8,0},{12,4},{1,9},{5,13},{9,1},{13,5},{2,10},{6,14},... | collective-permute-start | bytes 196616 | tf_op jit(solution)/shard_map/ppermute | solution.py:334
  75.5 6.4 %collective-permute-start.28 = (f32[128,128]{1,0:T(8,128)S(1)}, f32[128,128]{1,0:T(8,128)S(1)}, u32[]{:S(2)}, u32[]{:S(2)}) collective-permute-start(f32[128,128]{1,0:T(8,128)S(1)} %get-tuple-element.148), channel_id=1, source_target_pairs={{0,12},{4,8},{8,4},{12,0},{1,13},{5,9},{9,5},{13,1},{2,14},{6,10},... | collective-permute-start | bytes 196616 | tf_op jit(solution)/shard_map/ppermute | solution.py:334
  77.3 5.2 %collective-permute-start.29 = (f32[128,128]{1,0:T(8,128)S(1)}, f32[128,128]{1,0:T(8,128)S(1)}, u32[]{:S(2)}, u32[]{:S(2)}) collective-permute-start(f32[128,128]{1,0:T(8,128)S(1)} %get-tuple-element.149), channel_id=1, source_target_pairs={{0,4},{4,0},{8,12},{12,8},{1,5},{5,1},{9,13},{13,9},{2,6},{6,2},{1... | collective-permute-start | bytes 196616 | tf_op jit(solution)/shard_map/ppermute | solution.py:334
  83.1 7.4 %collective-permute-start.30 = (f32[128,128]{1,0:T(8,128)S(1)}, f32[128,128]{1,0:T(8,128)S(1)}, u32[]{:S(2)}, u32[]{:S(2)}) collective-permute-start(f32[128,128]{1,0:T(8,128)S(1)} %get-tuple-element.154), channel_id=1, source_target_pairs={{0,8},{4,12},{8,0},{12,4},{1,9},{5,13},{9,1},{13,5},{2,10},{6,14},... | collective-permute-start | bytes 196616 | tf_op jit(solution)/shard_map/ppermute | solution.py:334
  84.1 6.4 %collective-permute-start.31 = (f32[128,128]{1,0:T(8,128)S(1)}, f32[128,128]{1,0:T(8,128)S(1)}, u32[]{:S(2)}, u32[]{:S(2)}) collective-permute-start(f32[128,128]{1,0:T(8,128)S(1)} %get-tuple-element.155), channel_id=1, source_target_pairs={{0,12},{4,8},{8,4},{12,0},{1,13},{5,9},{9,5},{13,1},{2,14},{6,10},... | collective-permute-start | bytes 196616 | tf_op jit(solution)/shard_map/ppermute | solution.py:334
  86.0 5.2 %collective-permute-start.32 = (f32[128,128]{1,0:T(8,128)S(1)}, f32[128,128]{1,0:T(8,128)S(1)}, u32[]{:S(2)}, u32[]{:S(2)}) collective-permute-start(f32[128,128]{1,0:T(8,128)S(1)} %get-tuple-element.156), channel_id=1, source_target_pairs={{0,4},{4,0},{8,12},{12,8},{1,5},{5,1},{9,13},{13,9},{2,6},{6,2},{1... | collective-permute-start | bytes 196616 | tf_op jit(solution)/shard_map/ppermute | solution.py:334

commit v13 on v7

--- a/solution.py
+++ b/solution.py
@@ -80,8 +80,8 @@
 
 
 def first_kernel(n, cap, peers_at, rows_at, operator_at, mult_at, *refs):
-    unpack_own, unpack_all, unpack, high, low, image = refs[:6]
-    sends, (peers, rows, operator, mult, done) = refs[6:6 + n], refs[6 + n:]
+    unpack_own, unpack_all, unpack_near, unpack_far, high, low, image = refs[:7]
+    sends, (peers, rows, operator, mult, done) = refs[7:7 + n], refs[7 + n:]
     shared, width = image.shape
     copies = [
         pltpu.make_async_copy(source, target, done.at[i])
@@ -109,7 +109,8 @@
 
     unpack_own[...] = marks(jnp.where(far == 0, wanted, -1), shared)
     unpack_all[...] = marks(jnp.where(far == 0, -1, (far - 1) * shared + wanted), unpack_all.shape[1])
-    unpack[...] = marks(jnp.where(far == 0, -1, (far - 1) * cap + slot), unpack.shape[1])
+    unpack_near[...] = marks(jnp.where(far == 1, slot, -1), unpack_near.shape[1])
+    unpack_far[...] = marks(jnp.where(far > 1, (far - 2) * cap + slot, -1), unpack_far.shape[1])
     lane = lax.broadcasted_iota(jnp.int32, (shared, width), 1)
     for d, out in enumerate(sends, 1):
         out[shared:, :] = jnp.zeros((out.shape[0] - shared, width), F32)
@@ -178,6 +179,11 @@
     base[...] = gap[:own.shape[0], :] - own + pick(unpack_own[...], own)
 
 
+def far_kernel(times, *refs):
+    recvs, (known, unpack, base) = refs[:len(times)], refs[len(times):]
+    base[...] = known[...] + arrived(times, recvs, known.shape[0], unpack)
+
+
 def settle(trial, floor, alive):
     return jnp.where(alive, jnp.maximum(trial, floor), 0.0)
 
@@ -248,8 +254,8 @@
 
 def coarse_kernel(times, size, *refs):
     n = len(times)
-    recvs = refs[:n]
-    base, unpack, mult, modes, started, trial = refs[n:n + 6]
+    base, recvs = refs[0], refs[1:n + 1]
+    unpack, mult, modes, started, trial = refs[n + 1:n + 6]
     shared = base.shape[0]
     residual, _ = shared_residual(times, recvs, base, unpack, size)
     coarse = started[...] + product(split(modes[:, :shared]), split(residual))
@@ -294,8 +300,8 @@
 
 def sweep_kernel(times, cap, size, *refs):
     n = len(times)
-    recvs = refs[:n]
-    base, unpack, mult, floor, high, low, ahead, mult_out, image_out = refs[n:n + 9]
+    base, recvs = refs[0], refs[1:n + 1]
+    unpack, mult, floor, high, low, ahead, mult_out, image_out = refs[n + 1:n + 9]
     shared = base.shape[0]
     residual, alive = shared_residual(times, recvs, base, unpack, size)
     value = settle(mult[...] + STEP * residual, floor[:shared, :], alive)
@@ -308,8 +314,8 @@
 
 def last_kernel(times, size, *refs):
     n = len(times)
-    recvs = refs[:n]
-    base, unpack, mult, floor, _, _, mult_out, residual_out, settled, left, done = refs[n:]
+    base, recvs = refs[0], refs[1:n + 1]
+    unpack, mult, floor, _, _, mult_out, residual_out, settled, left, done = refs[n + 1:]
     shared = base.shape[0]
     residual, alive = shared_residual(times, recvs, base, unpack, size)
     left[...] = residual
@@ -334,10 +340,9 @@
     return [swap(blocks[d - 1], axis, count, d) for d in times]
 
 
-def half_first(count, back):
+def half_first(count):
     half = count // 2
-    others = [d for d in range(1, count) if d != half]
-    return (half, *(others[::-1] if back else others))
+    return (half, *(d for d in range(count - 1, 1, -1) if d != half), *((1,) if half > 1 else ()))
 
 
 def middle_first(count):
@@ -376,19 +381,19 @@
     padded = -(-listed // 128) * 128
     size = interface_size
     coarse_order, part_order = far_first(wide), far_first(narrow)
-    half, half_back, middle = half_first(wide, False), half_first(wide, True), middle_first(wide)
-    orders = ((half_back, half, middle), (half_back, half, half_back))
+    far_times, padded_near = half_first(wide), -(-cap // 128) * 128
+    padded_far = max(128, -(-(n - 1) * cap // 128) * 128)
     sent = [shape(cap, loads)] * n
     full = 2 * order * loads
 
     list_rows = -(-(-(-cap // loads)) // 8) * 8
-    unpack_own, unpack_all, unpack, top_high, top_low, image, *sends = call(
+    unpack_own, unpack_all, unpack_near, unpack_far, top_high, top_low, image, *sends = call(
         functools.partial(first_kernel, n, cap),
         tuple(
             pltpu.with_memory_space_constraint(value, pltpu.HBM)
             for value in (peer_list[0].reshape(1, shared), partner_row, operator, mult)
         ),
-        [shape(shared, shared, BF16), shape(shared, n * shared, BF16), shape(shared, padded, BF16)]
+        [shape(shared, width, BF16) for width in (shared, n * shared, padded_near, padded_far)]
         + [shape(shared, order, BF16)] * 2
         + [shape(shared, loads)]
         + [shape(shared + list_rows, loads)] * n,
@@ -412,10 +417,22 @@
         moved=8 * coarse_inverse.size + 4 * full,
         name="prepare",
     )
+    def add_far(recvs, times, base):
+        if n > 1:
+            base = call(
+                functools.partial(far_kernel, times[:-1]),
+                (*recvs[:-1], base, unpack_far),
+                [shape(shared, loads)],
+                flops=4 * shared * loads * padded_far,
+                moved=2 * shared * padded_far,
+                name="far",
+            )[0]
+        return recvs[-1:], times[-1:], base, unpack_near
+
     mult_s = mult
     scratch = [pltpu.VMEM((order, 2 * loads), BF16)]
     for outer in range(OUTER):
-        times = orders[outer][0]
+        times = middle_first(wide) if outer == 0 else far_times
         recvs = swap_rows(sends, "wide", wide, times)
         base = call(
             base_kernel,
@@ -430,7 +447,7 @@
             next_loads = block((shared, loads), 1)
             trial_n, started, high, low = call(
                 rest_start_kernel,
-                (size, operator, mult, mult, gap, modes),
+                (size, pltpu.with_memory_space_constraint(operator, pltpu.HBM), mult, mult, gap, modes),
                 [shape(rest, loads), shape(count, loads)] + [shape(rest, order, BF16)] * 2,
                 [
                     SMEM,
@@ -465,13 +482,13 @@
                 moved=4 * rest * order,
                 name="rest_first",
             )
-            marks = unpack
+            recvs, times, base, marks = add_far(recvs, times, base)
         trial_s, own, *coarse = call(
             functools.partial(coarse_kernel, times),
-            (size, *recvs, base, marks, mult_s, modes, started),
+            (size, base, *recvs, marks, mult_s, modes, started),
             [shape(shared, loads)] + [shape(count, loads)] * wide,
-            flops=6 * shared * loads * unpack.shape[1],
-            moved=2 * shared * unpack.shape[1],
+            flops=6 * shared * loads * padded,
+            moved=2 * shared * padded,
             name="coarse",
         )
         blocks = [own] + swap_all(coarse, "wide", wide, coarse_order)
@@ -498,7 +515,7 @@
         )
         for inner in range(1, INNER):
             last = outer == OUTER - 1 and inner == INNER - 1
-            times = orders[outer][inner]
+            times = far_times
             recvs = swap_rows(sends, "wide", wide, times)
             base = call(
                 base_kernel,
@@ -509,8 +526,9 @@
                 name="base",
             )[0]
             ins = (size, high, low, mult_s, mult_n, gap, floor)
-            shadow = (size, *recvs, base, unpack, mult_s, floor)
-            cost = dict(flops=6 * shared * loads * unpack.shape[1], moved=2 * shared * unpack.shape[1])
+            recvs, times, base, marks = add_far(recvs, times, base)
+            shadow = (size, base, *recvs, marks, mult_s, floor)
+            cost = dict(flops=6 * shared * loads * padded, moved=2 * shared * padded)
             if last:
                 outs = call(
                     rest_last_kernel,

time: 90.5 us -> 91.6 us (1.012)
  Pallas kernels: 19.3 us -> 21.8 us
  starting transfers between devices: 39.3 us -> 37.1 us
    pallas_call x25 -> x30, Pallas kernels: 19.3 us -> 21.8 us  [call(): pl.pallas_call(body, out_shape=outs, grid=grid, in_specs=in_specs, out_sp...]
    ppermute x30, starting transfers between devices: 39.3 us -> 37.1 us  [swap(): return lax.ppermute(block, axis, [(i, i ^ d) for i in range(count)])]
  transfers between devices with their start and end apart: 30 -> 30, of which waited for: 24 -> 23; matrix products, arithmetic and copies ran while one was open for 0% -> 0% of each run, Pallas kernels for 13% -> 15%
where the time goes in v13:
time: 91.6 us; the launch traced here: 91.4 us
  starting transfers between devices  37.1 us (41%)
  waiting for transfers between devices  30.8 us (34%)
  Pallas kernels  21.8 us (24%)
  between operations  1.61 us (2%)
    ppermute x30, starting transfers between devices, swap(): return lax.ppermute(block, axis, [(i, i ^ d) for i in range(count)])  37.1 us
    ppermute x30, waiting for transfers between devices, swap(): return lax.ppermute(block, axis, [(i, i ^ d) for i in range(count)])  30.8 us
    pallas_call x30, Pallas kernels, call(): pl.pallas_call(body, out_shape=outs, grid=grid, in_specs=in_specs, out_sp...  21.8 us
  transfers between devices with their start and end apart: 30, of which 23 were waited for; matrix products, arithmetic and copies ran while one was open for 0% of the time, Pallas kernels for 15%

profile of v13, /device:TPU:0, one launch (start us, length us, event | category | flops | bytes accessed | tf_op | source)
XLA Modules:
  0.0 91.4 jit_solution(3863695691134320200)
XLA Ops:
  0.7 2.0 %first.1 = (bf16[256,256]{1,0:T(8,128)(2,1)S(1)}, bf16[256,768]{1,0:T(8,128)(2,1)S(1)}, bf16[256,128]{1,0:T(8,128)(2,1)S(1)}, bf16[256,256]{1,0:T(8,128)(2,1)S(1...) custom-call(s32[1,256]{1,0:T(1,128)} %bitcast.32, ...), custom_call_target="tpu_custom_call" | custom-call | flops 201326592 | bytes 2097152 | tf_op jit(solution)/shard_map/first/pallas_call | solution.py:49
  2.7 5.1 %collective-permute-start = (f32[264,128]{1,0:T(8,128)S(1)}, f32[264,128]{1,0:T(8,128)S(1)}, u32[]{:S(2)}, u32[]{:S(2)}) collective-permute-start(f32[264,128]{1,0:T(8,128)S(1)} %get-tuple-element.84), channel_id=1, source_target_pairs={{0,12},{4,8},{8,4},{12,0},{1,13},{5,9},{9,5},{13,1},{2,14},{6,10},... | collective-permute-start | bytes 405512 | tf_op jit(solution)/shard_map/ppermute | solution.py:332
  7.8 0.6 collective-permute-start.2
  9.3 3.8 %rest_start.1 = (f32[768,128]{1,0:T(8,128)S(1)}, f32[64,128]{1,0:T(8,128)S(1)}, bf16[768,1024]{1,0:T(8,128)(2,1)S(1)}, bf16[768,1024]{1,0:T(8,128)(2,1)S(1)}) custom-call(s32[1]{0:T(128)S(6)} %copy.15.size, f32[1024,1024]{1,0:T(8,128)} %bitcast.29, f32[1024,128]{1,0:T(8,128)S(1)} %bitcast.20, f32[1024,128]{1,0:T(8,128)S(1)} %bitcast.21, ...), custom_call_target="tpu_custom_call" | custom-call | flops 603979776 | bytes 6291456 | tf_op jit(solution)/shard_map/rest_start/pallas_call | solution.py:49
  13.2 2.2 %collective-permute-done.1.refs_2_.refs_1_ = f32[264,128]{1,0:T(8,128)S(1)} collective-permute-done((f32[264,128]{1,0:T(8,128)S(1)}, f32[264,128]{1,0:T(8,128)S(1)}, u32[]{:S(2)}, u32[]{:S(2)}) %collective-permute-start.1) | collective-permute-done | bytes 135200 | tf_op jit(solution)/shard_map/ppermute | solution.py:332
  15.4 3.9 %collective-permute-done.2.refs_3_.refs_2_ = f32[264,128]{1,0:T(8,128)S(1)} collective-permute-done((f32[264,128]{1,0:T(8,128)S(1)}, f32[264,128]{1,0:T(8,128)S(1)}, u32[]{:S(2)}, u32[]{:S(2)}) %collective-permute-start.2) | collective-permute-done | bytes 135200 | tf_op jit(solution)/shard_map/ppermute | solution.py:332
  19.2 0.5 coarse.2
  19.7 2.5 %collective-permute-start.3 = (f32[64,128]{1,0:T(8,128)S(1)}, f32[64,128]{1,0:T(8,128)S(1)}, u32[]{:S(2)}, u32[]{:S(2)}) collective-permute-start(f32[64,128]{1,0:T(8,128)S(1)} %get-tuple-element.90), channel_id=1, source_target_pairs={{0,12},{4,8},{8,4},{12,0},{1,13},{5,9},{9,5},{13,1},{2,14},{6,10},... | collective-permute-start | bytes 98312 | tf_op jit(solution)/shard_map/ppermute | solution.py:332
  22.2 1.9 %collective-permute-start.5 = (f32[64,128]{1,0:T(8,128)S(1)}, f32[64,128]{1,0:T(8,128)S(1)}, u32[]{:S(2)}, u32[]{:S(2)}) collective-permute-start(f32[64,128]{1,0:T(8,128)S(1)} %get-tuple-element.92), channel_id=1, source_target_pairs={{0,4},{4,0},{8,12},{12,8},{1,5},{5,1},{9,13},{13,9},{2,6},{6,2},{1... | collective-permute-start | bytes 98312 | tf_op jit(solution)/shard_map/ppermute | solution.py:332
  24.1 0.4 prepare.1
  24.5 0.9 %collective-permute-done.3.refs_1_ = f32[64,128]{1,0:T(8,128)S(1)} collective-permute-done((f32[64,128]{1,0:T(8,128)S(1)}, f32[64,128]{1,0:T(8,128)S(1)}, u32[]{:S(2)}, u32[]{:S(2)}) %collective-permute-start.3) | collective-permute-done | bytes 32800 | tf_op jit(solution)/shard_map/ppermute | solution.py:332
  25.5 1.6 %collective-permute-done.4.refs_2_ = f32[64,128]{1,0:T(8,128)S(1)} collective-permute-done((f32[64,128]{1,0:T(8,128)S(1)}, f32[64,128]{1,0:T(8,128)S(1)}, u32[]{:S(2)}, u32[]{:S(2)}) %collective-permute-start.4) | collective-permute-done | bytes 32800 | tf_op jit(solution)/shard_map/ppermute | solution.py:332
  27.0 0.3 tile.4
  27.4 1.6 %collective-permute-start.7 = (f32[64,128]{1,0:T(8,128)S(1)}, f32[64,128]{1,0:T(8,128)S(1)}, u32[]{:S(2)}, u32[]{:S(2)}) collective-permute-start(f32[64,128]{1,0:T(8,128)S(1)} %get-tuple-element.95), channel_id=1, source_target_pairs={{0,2},{1,3},{2,0},{3,1},{4,6},{5,7},{6,4},{7,5},{8,10},{9,11},{10,... | collective-permute-start | bytes 98312 | tf_op jit(solution)/shard_map/ppermute | solution.py:332
  28.9 0.3 collective-permute-start.8
  29.2 0.3 pack.1
  29.5 1.5 %collective-permute-done.6.refs_1_ = f32[64,128]{1,0:T(8,128)S(1)} collective-permute-done((f32[64,128]{1,0:T(8,128)S(1)}, f32[64,128]{1,0:T(8,128)S(1)}, u32[]{:S(2)}, u32[]{:S(2)}) %collective-permute-start.6) | collective-permute-done | bytes 32800 | tf_op jit(solution)/shard_map/ppermute | solution.py:332
  31.0 0.4 collective-permute-done.7.refs_2_
  31.4 1.0 %lift.2 = (f32[256,128]{1,0:T(8,128)S(1)}, f32[768,128]{1,0:T(8,128)S(1)}, f32[256,128]{1,0:T(8,128)S(1)}, f32[128,128]{1,0:T(8,128)S(1)}, f32[128,128]{1,0:T(8,128)S(1)}, /*index=5*/f32[128,128]{1,0:T(8,128)S(1)}) custom-call(s32[1]{0:T(128)S(6)} %copy.15.size, f32[64,128]{1,0:T(8,128)S(1)} %get-tuple-element.93.refs_0_, ...), custom_call_target="tpu_custom_call" | custom-call | flops 201326592 | bytes 1048576 | tf_op jit(solution)/shard_map/lift/pallas_call | solution.py:49
  32.4 2.1 %collective-permute-start.9 = (f32[128,128]{1,0:T(8,128)S(1)}, f32[128,128]{1,0:T(8,128)S(1)}, u32[]{:S(2)}, u32[]{:S(2)}) collective-permute-start(f32[128,128]{1,0:T(8,128)S(1)} %get-tuple-element.104), channel_id=1, source_target_pairs={{0,8},{4,12},{8,0},{12,4},{1,9},{5,13},{9,1},{13,5},{2,10},{6,14},... | collective-permute-start | bytes 196616 | tf_op jit(solution)/shard_map/ppermute | solution.py:332
  34.5 1.3 %collective-permute-start.10 = (f32[128,128]{1,0:T(8,128)S(1)}, f32[128,128]{1,0:T(8,128)S(1)}, u32[]{:S(2)}, u32[]{:S(2)}) collective-permute-start(f32[128,128]{1,0:T(8,128)S(1)} %get-tuple-element.105), channel_id=1, source_target_pairs={{0,12},{4,8},{8,4},{12,0},{1,13},{5,9},{9,5},{13,1},{2,14},{6,10},... | collective-permute-start | bytes 196616 | tf_op jit(solution)/shard_map/ppermute | solution.py:332
  36.2 1.5 %rest.3 = (f32[768,128]{1,0:T(8,128)S(1)}, f32[640,128]{1,0:T(8,128)S(1)}) custom-call(s32[1]{0:T(128)S(6)} %copy.15.size, bf16[768,1024]{1,0:T(8,128)(2,1)S(1)} %get-tuple-element.113.high, bf16[768,1024]{1,0:T(8,128)(2,1)S(1)} %get-tuple-element.114.low, f32[256,128]{1,0:T(8,128)S(1)} %get-tuple-element.110.mult_s.refs_3_, ...), custom_call_target="tpu_custom_call" | custom-call | flops 805306368 | bytes 4194304 | tf_op jit(solution)/shard_map/rest/pallas_call | solution.py:49
  37.7 3.0 %collective-permute-done.9.refs_0_ = f32[128,128]{1,0:T(8,128)S(1)} collective-permute-done((f32[128,128]{1,0:T(8,128)S(1)}, f32[128,128]{1,0:T(8,128)S(1)}, u32[]{:S(2)}, u32[]{:S(2)}) %collective-permute-start.9) | collective-permute-done | bytes 65568 | tf_op jit(solution)/shard_map/ppermute | solution.py:332
  40.7 0.3 collective-permute-done.10.refs_1_
  41.3 0.6 collective-permute-done.11.refs_1_
  41.9 0.5 sweep.3
  42.4 1.2 %collective-permute-start.12 = (f32[128,128]{1,0:T(8,128)S(1)}, f32[128,128]{1,0:T(8,128)S(1)}, u32[]{:S(2)}, u32[]{:S(2)}) collective-permute-start(f32[128,128]{1,0:T(8,128)S(1)} %get-tuple-element.117), channel_id=1, source_target_pairs={{0,8},{4,12},{8,0},{12,4},{1,9},{5,13},{9,1},{13,5},{2,10},{6,14},... | collective-permute-start | bytes 196616 | tf_op jit(solution)/shard_map/ppermute | solution.py:332
  43.6 2.0 %collective-permute-start.13 = (f32[128,128]{1,0:T(8,128)S(1)}, f32[128,128]{1,0:T(8,128)S(1)}, u32[]{:S(2)}, u32[]{:S(2)}) collective-permute-start(f32[128,128]{1,0:T(8,128)S(1)} %get-tuple-element.118), channel_id=1, source_target_pairs={{0,12},{4,8},{8,4},{12,0},{1,13},{5,9},{9,5},{13,1},{2,14},{6,10},... | collective-permute-start | bytes 196616 | tf_op jit(solution)/shard_map/ppermute | solution.py:332
  45.8 0.4 collective-permute-start.14
  46.2 1.5 %rest.4 = (f32[768,128]{1,0:T(8,128)S(1)}, f32[640,128]{1,0:T(8,128)S(1)}) custom-call(s32[1]{0:T(128)S(6)} %copy.15.size, bf16[768,1024]{1,0:T(8,128)(2,1)S(1)} %get-tuple-element.113.high, bf16[768,1024]{1,0:T(8,128)(2,1)S(1)} %get-tuple-element.114.low, f32[256,128]{1,0:T(8,128)S(1)} %get-tuple-element.121.mult_s.refs_3_, ...), custom_call_target="tpu_custom_call" | custom-call | flops 805306368 | bytes 4194304 | tf_op jit(solution)/shard_map/rest/pallas_call | solution.py:49
  47.7 2.8 %collective-permute-done.12.refs_0_ = f32[128,128]{1,0:T(8,128)S(1)} collective-permute-done((f32[128,128]{1,0:T(8,128)S(1)}, f32[128,128]{1,0:T(8,128)S(1)}, u32[]{:S(2)}, u32[]{:S(2)}) %collective-permute-start.12) | collective-permute-done | bytes 65568 | tf_op jit(solution)/shard_map/ppermute | solution.py:332
  50.7 0.2 collective-permute-done.14.refs_1_
  50.9 0.5 sweep.4
  51.4 1.6 %collective-permute-start.15 = (f32[128,128]{1,0:T(8,128)S(1)}, f32[128,128]{1,0:T(8,128)S(1)}, u32[]{:S(2)}, u32[]{:S(2)}) collective-permute-start(f32[128,128]{1,0:T(8,128)S(1)} %get-tuple-element.124), channel_id=1, source_target_pairs={{0,8},{4,12},{8,0},{12,4},{1,9},{5,13},{9,1},{13,5},{2,10},{6,14},... | collective-permute-start | bytes 196616 | tf_op jit(solution)/shard_map/ppermute | solution.py:332
  53.1 2.1 %collective-permute-start.16 = (f32[128,128]{1,0:T(8,128)S(1)}, f32[128,128]{1,0:T(8,128)S(1)}, u32[]{:S(2)}, u32[]{:S(2)}) collective-permute-start(f32[128,128]{1,0:T(8,128)S(1)} %get-tuple-element.125), channel_id=1, source_target_pairs={{0,12},{4,8},{8,4},{12,0},{1,13},{5,9},{9,5},{13,1},{2,14},{6,10},... | collective-permute-start | bytes 196616 | tf_op jit(solution)/shard_map/ppermute | solution.py:332
  55.3 1.1 %rest_first.1 = (f32[768,128]{1,0:T(8,128)S(1)}, f32[64,128]{1,0:T(8,128)S(1)}) custom-call(s32[1]{0:T(128)S(6)} %copy.15.size, bf16[768,1024]{1,0:T(8,128)(2,1)S(1)} %get-tuple-element.113.high, bf16[768,1024]{1,0:T(8,128)(2,1)S(1)} %get-tuple-element.114.low, f32[256,128]{1,0:T(8,128)S(1)} %get-tuple-element.128.mult_s.refs_3_, ...), custom_call_target="tpu_custom_call" | custom-call | flops 603979776 | bytes 3145728 | tf_op jit(solution)/shard_map/rest_first/pallas_call | solution.py:49
  56.5 1.7 %collective-permute-done.15.refs_0_ = f32[128,128]{1,0:T(8,128)S(1)} collective-permute-done((f32[128,128]{1,0:T(8,128)S(1)}, f32[128,128]{1,0:T(8,128)S(1)}, u32[]{:S(2)}, u32[]{:S(2)}) %collective-permute-start.15) | collective-permute-done | bytes 65568 | tf_op jit(solution)/shard_map/ppermute | solution.py:332
  58.2 1.3 %collective-permute-done.16.refs_1_ = f32[128,128]{1,0:T(8,128)S(1)} collective-permute-done((f32[128,128]{1,0:T(8,128)S(1)}, f32[128,128]{1,0:T(8,128)S(1)}, u32[]{:S(2)}, u32[]{:S(2)}) %collective-permute-start.16) | collective-permute-done | bytes 65568 | tf_op jit(solution)/shard_map/ppermute | solution.py:332
  59.7 0.3 collective-permute-done.17.refs_1_
  60.0 0.4 coarse.3
  60.4 1.9 %collective-permute-start.18 = (f32[64,128]{1,0:T(8,128)S(1)}, f32[64,128]{1,0:T(8,128)S(1)}, u32[]{:S(2)}, u32[]{:S(2)}) collective-permute-start(f32[64,128]{1,0:T(8,128)S(1)} %get-tuple-element.132), channel_id=1, source_target_pairs={{0,12},{4,8},{8,4},{12,0},{1,13},{5,9},{9,5},{13,1},{2,14},{6,10},... | collective-permute-start | bytes 98312 | tf_op jit(solution)/shard_map/ppermute | solution.py:332
  62.3 2.5 %collective-permute-start.20 = (f32[64,128]{1,0:T(8,128)S(1)}, f32[64,128]{1,0:T(8,128)S(1)}, u32[]{:S(2)}, u32[]{:S(2)}) collective-permute-start(f32[64,128]{1,0:T(8,128)S(1)} %get-tuple-element.134), channel_id=1, source_target_pairs={{0,4},{4,0},{8,12},{12,8},{1,5},{5,1},{9,13},{13,9},{2,6},{6,2},{1... | collective-permute-start | bytes 98312 | tf_op jit(solution)/shard_map/ppermute | solution.py:332
  64.8 1.3 %collective-permute-done.18.refs_1_ = f32[64,128]{1,0:T(8,128)S(1)} collective-permute-done((f32[64,128]{1,0:T(8,128)S(1)}, f32[64,128]{1,0:T(8,128)S(1)}, u32[]{:S(2)}, u32[]{:S(2)}) %collective-permute-start.18) | collective-permute-done | bytes 32800 | tf_op jit(solution)/shard_map/ppermute | solution.py:332
  66.1 1.0 %collective-permute-done.19.refs_2_ = f32[64,128]{1,0:T(8,128)S(1)} collective-permute-done((f32[64,128]{1,0:T(8,128)S(1)}, f32[64,128]{1,0:T(8,128)S(1)}, u32[]{:S(2)}, u32[]{:S(2)}) %collective-permute-start.19) | collective-permute-done | bytes 32800 | tf_op jit(solution)/shard_map/ppermute | solution.py:332
  67.1 0.3 tile.5
  67.4 0.6 collective-permute-start.22
  68.0 1.3 %collective-permute-start.23 = (f32[64,128]{1,0:T(8,128)S(1)}, f32[64,128]{1,0:T(8,128)S(1)}, u32[]{:S(2)}, u32[]{:S(2)}) collective-permute-start(f32[64,128]{1,0:T(8,128)S(1)} %get-tuple-element.138), channel_id=1, source_target_pairs={{0,1},{1,0},{2,3},{3,2},{4,5},{5,4},{6,7},{7,6},{8,9},{9,8},{10,11... | collective-permute-start | bytes 98312 | tf_op jit(solution)/shard_map/ppermute | solution.py:332
  69.3 1.5 %collective-permute-done.21.refs_1_ = f32[64,128]{1,0:T(8,128)S(1)} collective-permute-done((f32[64,128]{1,0:T(8,128)S(1)}, f32[64,128]{1,0:T(8,128)S(1)}, u32[]{:S(2)}, u32[]{:S(2)}) %collective-permute-start.21) | collective-permute-done | bytes 32800 | tf_op jit(solution)/shard_map/ppermute | solution.py:332
  70.8 0.7 collective-permute-done.22.refs_2_
  71.5 1.0 %lift.3 = (f32[256,128]{1,0:T(8,128)S(1)}, f32[768,128]{1,0:T(8,128)S(1)}, f32[256,128]{1,0:T(8,128)S(1)}, f32[128,128]{1,0:T(8,128)S(1)}, f32[128,128]{1,0:T(8,128)S(1)}, /*index=5*/f32[128,128]{1,0:T(8,128)S(1)}) custom-call(s32[1]{0:T(128)S(6)} %copy.15.size, f32[64,128]{1,0:T(8,128)S(1)} %get-tuple-element.135.refs_0_, ...), custom_call_target="tpu_custom_call" | custom-call | flops 201326592 | bytes 1048576 | tf_op jit(solution)/shard_map/lift/pallas_call | solution.py:49
  72.5 2.1 %collective-permute-start.24 = (f32[128,128]{1,0:T(8,128)S(1)}, f32[128,128]{1,0:T(8,128)S(1)}, u32[]{:S(2)}, u32[]{:S(2)}) collective-permute-start(f32[128,128]{1,0:T(8,128)S(1)} %get-tuple-element.141), channel_id=1, source_target_pairs={{0,8},{4,12},{8,0},{12,4},{1,9},{5,13},{9,1},{13,5},{2,10},{6,14},... | collective-permute-start | bytes 196616 | tf_op jit(solution)/shard_map/ppermute | solution.py:332
  74.6 2.0 %collective-permute-start.25 = (f32[128,128]{1,0:T(8,128)S(1)}, f32[128,128]{1,0:T(8,128)S(1)}, u32[]{:S(2)}, u32[]{:S(2)}) collective-permute-start(f32[128,128]{1,0:T(8,128)S(1)} %get-tuple-element.142), channel_id=1, source_target_pairs={{0,12},{4,8},{8,4},{12,0},{1,13},{5,9},{9,5},{13,1},{2,14},{6,10},... | collective-permute-start | bytes 196616 | tf_op jit(solution)/shard_map/ppermute | solution.py:332
  76.8 1.5 %rest.5 = (f32[768,128]{1,0:T(8,128)S(1)}, f32[640,128]{1,0:T(8,128)S(1)}) custom-call(s32[1]{0:T(128)S(6)} %copy.15.size, bf16[768,1024]{1,0:T(8,128)(2,1)S(1)} %get-tuple-element.113.high, bf16[768,1024]{1,0:T(8,128)(2,1)S(1)} %get-tuple-element.114.low, f32[256,128]{1,0:T(8,128)S(1)} %get-tuple-element.145.mult_s.refs_3_, ...), custom_call_target="tpu_custom_call" | custom-call | flops 805306368 | bytes 4194304 | tf_op jit(solution)/shard_map/rest/pallas_call | solution.py:49
  78.3 2.1 %collective-permute-done.24.refs_0_ = f32[128,128]{1,0:T(8,128)S(1)} collective-permute-done((f32[128,128]{1,0:T(8,128)S(1)}, f32[128,128]{1,0:T(8,128)S(1)}, u32[]{:S(2)}, u32[]{:S(2)}) %collective-permute-start.24) | collective-permute-done | bytes 65568 | tf_op jit(solution)/shard_map/ppermute | solution.py:332
  80.5 0.6 collective-permute-done.25.refs_1_
  81.2 0.7 collective-permute-done.26.refs_1_
  81.9 0.5 sweep.5
  82.4 1.0 %collective-permute-start.27 = (f32[128,128]{1,0:T(8,128)S(1)}, f32[128,128]{1,0:T(8,128)S(1)}, u32[]{:S(2)}, u32[]{:S(2)}) collective-permute-start(f32[128,128]{1,0:T(8,128)S(1)} %get-tuple-element.148), channel_id=1, source_target_pairs={{0,8},{4,12},{8,0},{12,4},{1,9},{5,13},{9,1},{13,5},{2,10},{6,14},... | collective-permute-start | bytes 196616 | tf_op jit(solution)/shard_map/ppermute | solution.py:332
  83.4 1.9 %collective-permute-start.28 = (f32[128,128]{1,0:T(8,128)S(1)}, f32[128,128]{1,0:T(8,128)S(1)}, u32[]{:S(2)}, u32[]{:S(2)}) collective-permute-start(f32[128,128]{1,0:T(8,128)S(1)} %get-tuple-element.149), channel_id=1, source_target_pairs={{0,12},{4,8},{8,4},{12,0},{1,13},{5,9},{9,5},{13,1},{2,14},{6,10},... | collective-permute-start | bytes 196616 | tf_op jit(solution)/shard_map/ppermute | solution.py:332
  85.3 0.6 collective-permute-start.29
  86.1 1.9 %rest_last.1 = (f32[1024,128]{1,0:T(8,128)}, f32[1024,128]{1,0:T(8,128)}) custom-call(s32[1]{0:T(128)S(6)} %copy.15.size, bf16[768,1024]{1,0:T(8,128)(2,1)S(1)} %get-tuple-element.113.high, bf16[768,1024]{1,0:T(8,128)(2,1)S(1)} %get-tuple-element.114.low, f32[256,128]{1,0:T(8,128)S(1)} %get-tuple-element.152.mult_s.refs_3_, ...), custom_call_target="tpu_custom_call" | custom-call | flops 603979776 | bytes 3145728 | tf_op jit(solution)/shard_map/rest_last/pallas_call | solution.py:49
  88.0 1.9 %collective-permute-done.27.refs_0_ = f32[128,128]{1,0:T(8,128)S(1)} collective-permute-done((f32[128,128]{1,0:T(8,128)S(1)}, f32[128,128]{1,0:T(8,128)S(1)}, u32[]{:S(2)}, u32[]{:S(2)}) %collective-permute-start.27) | collective-permute-done | bytes 65568 | tf_op jit(solution)/shard_map/ppermute | solution.py:332
  90.1 0.4 collective-permute-done.29.refs_1_
  90.5 0.9 last.1
  (36 shorter events, 2.5 us)
Async XLA Ops:
  0.6 8.5 %copy-start = (f32[1,1024,128]{2,1,0:T(8,128)S(1)}, f32[1,1024,128]{2,1,0:T(8,128)}, u32[]{:S(2)}) copy-start(f32[1,1024,128]{2,1,0:T(8,128)} %param.12) | copy-start | bytes 1572868
  0.6 8.7 %copy-start.1 = (f32[1,1024,128]{2,1,0:T(8,128)S(1)}, f32[1,1024,128]{2,1,0:T(8,128)}, u32[]{:S(2)}) copy-start(f32[1,1024,128]{2,1,0:T(8,128)} %param.13) | copy-start | bytes 1572868
  0.7 8.7 %copy-start.2 = (f32[1,64,1024]{2,1,0:T(8,128)S(1)}, f32[1,64,1024]{2,1,0:T(8,128)}, u32[]{:S(2)}) copy-start(f32[1,64,1024]{2,1,0:T(8,128)} %param.11) | copy-start | bytes 786436
  2.7 10.5 %collective-permute-start = (f32[264,128]{1,0:T(8,128)S(1)}, f32[264,128]{1,0:T(8,128)S(1)}, u32[]{:S(2)}, u32[]{:S(2)}) collective-permute-start(f32[264,128]{1,0:T(8,128)S(1)} %get-tuple-element.84), channel_id=1, source_target_pairs={{0,12},{4,8},{8,4},{12,0},{1,13},{5,9},{9,5},{13,1},{2,14},{6,10},... | collective-permute-start | bytes 405512 | tf_op jit(solution)/shard_map/ppermute | solution.py:332
  7.8 7.6 %collective-permute-start.1 = (f32[264,128]{1,0:T(8,128)S(1)}, f32[264,128]{1,0:T(8,128)S(1)}, u32[]{:S(2)}, u32[]{:S(2)}) collective-permute-start(f32[264,128]{1,0:T(8,128)S(1)} %get-tuple-element.85), channel_id=1, source_target_pairs={{0,4},{4,0},{8,12},{12,8},{1,5},{5,1},{9,13},{13,9},{2,6},{6,2},{1... | collective-permute-start | bytes 405512 | tf_op jit(solution)/shard_map/ppermute | solution.py:332
  7.8 11.4 %collective-permute-start.2 = (f32[264,128]{1,0:T(8,128)S(1)}, f32[264,128]{1,0:T(8,128)S(1)}, u32[]{:S(2)}, u32[]{:S(2)}) collective-permute-start(f32[264,128]{1,0:T(8,128)S(1)} %get-tuple-element.86), channel_id=1, source_target_pairs={{0,8},{4,12},{8,0},{12,4},{1,9},{5,13},{9,1},{13,5},{2,10},{6,14},... | collective-permute-start | bytes 405512 | tf_op jit(solution)/shard_map/ppermute | solution.py:332
  13.1 11.0 %copy-start.3 = (f32[256,256]{1,0:T(8,128)S(1)}, f32[256,256]{1,0:T(8,128)}, u32[]{:S(2)}) copy-start(f32[256,256]{1,0:T(8,128)} %tile.3) | copy-start | bytes 786436
  13.1 11.0 %copy-start.4 = (s32[1,1024]{1,0:T(1,128)S(1)}, s32[1,1024]{1,0:T(1,128)}, u32[]{:S(2)}) copy-start(s32[1,1024]{1,0:T(1,128)} %contact.1) | copy-start | bytes 12292
  19.7 5.8 %collective-permute-start.3 = (f32[64,128]{1,0:T(8,128)S(1)}, f32[64,128]{1,0:T(8,128)S(1)}, u32[]{:S(2)}, u32[]{:S(2)}) collective-permute-start(f32[64,128]{1,0:T(8,128)S(1)} %get-tuple-element.90), channel_id=1, source_target_pairs={{0,12},{4,8},{8,4},{12,0},{1,13},{5,9},{9,5},{13,1},{2,14},{6,10},... | collective-permute-start | bytes 98312 | tf_op jit(solution)/shard_map/ppermute | solution.py:332
  22.2 4.8 %collective-permute-start.4 = (f32[64,128]{1,0:T(8,128)S(1)}, f32[64,128]{1,0:T(8,128)S(1)}, u32[]{:S(2)}, u32[]{:S(2)}) collective-permute-start(f32[64,128]{1,0:T(8,128)S(1)} %get-tuple-element.91), channel_id=1, source_target_pairs={{0,8},{4,12},{8,0},{12,4},{1,9},{5,13},{9,1},{13,5},{2,10},{6,14},... | collective-permute-start | bytes 98312 | tf_op jit(solution)/shard_map/ppermute | solution.py:332
  22.2 4.8 %collective-permute-start.5 = (f32[64,128]{1,0:T(8,128)S(1)}, f32[64,128]{1,0:T(8,128)S(1)}, u32[]{:S(2)}, u32[]{:S(2)}) collective-permute-start(f32[64,128]{1,0:T(8,128)S(1)} %get-tuple-element.92), channel_id=1, source_target_pairs={{0,4},{4,0},{8,12},{12,8},{1,5},{5,1},{9,13},{13,9},{2,6},{6,2},{1... | collective-permute-start | bytes 98312 | tf_op jit(solution)/shard_map/ppermute | solution.py:332
  27.3 3.7 %collective-permute-start.6 = (f32[64,128]{1,0:T(8,128)S(1)}, f32[64,128]{1,0:T(8,128)S(1)}, u32[]{:S(2)}, u32[]{:S(2)}) collective-permute-start(f32[64,128]{1,0:T(8,128)S(1)} %get-tuple-element.94), channel_id=1, source_target_pairs={{0,3},{1,2},{2,1},{3,0},{4,7},{5,6},{6,5},{7,4},{8,11},{9,10},{10,... | collective-permute-start | bytes 98312 | tf_op jit(solution)/shard_map/ppermute | solution.py:332
  27.4 4.0 %collective-permute-start.7 = (f32[64,128]{1,0:T(8,128)S(1)}, f32[64,128]{1,0:T(8,128)S(1)}, u32[]{:S(2)}, u32[]{:S(2)}) collective-permute-start(f32[64,128]{1,0:T(8,128)S(1)} %get-tuple-element.95), channel_id=1, source_target_pairs={{0,2},{1,3},{2,0},{3,1},{4,6},{5,7},{6,4},{7,5},{8,10},{9,11},{10,... | collective-permute-start | bytes 98312 | tf_op jit(solution)/shard_map/ppermute | solution.py:332
  28.9 2.5 %collective-permute-start.8 = (f32[64,128]{1,0:T(8,128)S(1)}, f32[64,128]{1,0:T(8,128)S(1)}, u32[]{:S(2)}, u32[]{:S(2)}) collective-permute-start(f32[64,128]{1,0:T(8,128)S(1)} %get-tuple-element.96), channel_id=1, source_target_pairs={{0,1},{1,0},{2,3},{3,2},{4,5},{5,4},{6,7},{7,6},{8,9},{9,8},{10,11... | collective-permute-start | bytes 98312 | tf_op jit(solution)/shard_map/ppermute | solution.py:332
  32.4 8.3 %collective-permute-start.9 = (f32[128,128]{1,0:T(8,128)S(1)}, f32[128,128]{1,0:T(8,128)S(1)}, u32[]{:S(2)}, u32[]{:S(2)}) collective-permute-start(f32[128,128]{1,0:T(8,128)S(1)} %get-tuple-element.104), channel_id=1, source_target_pairs={{0,8},{4,12},{8,0},{12,4},{1,9},{5,13},{9,1},{13,5},{2,10},{6,14},... | collective-permute-start | bytes 196616 | tf_op jit(solution)/shard_map/ppermute | solution.py:332
  34.5 6.6 %collective-permute-start.10 = (f32[128,128]{1,0:T(8,128)S(1)}, f32[128,128]{1,0:T(8,128)S(1)}, u32[]{:S(2)}, u32[]{:S(2)}) collective-permute-start(f32[128,128]{1,0:T(8,128)S(1)} %get-tuple-element.105), channel_id=1, source_target_pairs={{0,12},{4,8},{8,4},{12,0},{1,13},{5,9},{9,5},{13,1},{2,14},{6,10},... | collective-permute-start | bytes 196616 | tf_op jit(solution)/shard_map/ppermute | solution.py:332
  36.1 5.9 %collective-permute-start.11 = (f32[128,128]{1,0:T(8,128)S(1)}, f32[128,128]{1,0:T(8,128)S(1)}, u32[]{:S(2)}, u32[]{:S(2)}) collective-permute-start(f32[128,128]{1,0:T(8,128)S(1)} %get-tuple-element.108), channel_id=1, source_target_pairs={{0,4},{4,0},{8,12},{12,8},{1,5},{5,1},{9,13},{13,9},{2,6},{6,2},{1... | collective-permute-start | bytes 196616 | tf_op jit(solution)/shard_map/ppermute | solution.py:332
  42.4 8.1 %collective-permute-start.12 = (f32[128,128]{1,0:T(8,128)S(1)}, f32[128,128]{1,0:T(8,128)S(1)}, u32[]{:S(2)}, u32[]{:S(2)}) collective-permute-start(f32[128,128]{1,0:T(8,128)S(1)} %get-tuple-element.117), channel_id=1, source_target_pairs={{0,8},{4,12},{8,0},{12,4},{1,9},{5,13},{9,1},{13,5},{2,10},{6,14},... | collective-permute-start | bytes 196616 | tf_op jit(solution)/shard_map/ppermute | solution.py:332
  43.6 6.9 %collective-permute-start.13 = (f32[128,128]{1,0:T(8,128)S(1)}, f32[128,128]{1,0:T(8,128)S(1)}, u32[]{:S(2)}, u32[]{:S(2)}) collective-permute-start(f32[128,128]{1,0:T(8,128)S(1)} %get-tuple-element.118), channel_id=1, source_target_pairs={{0,12},{4,8},{8,4},{12,0},{1,13},{5,9},{9,5},{13,1},{2,14},{6,10},... | collective-permute-start | bytes 196616 | tf_op jit(solution)/shard_map/ppermute | solution.py:332
  45.8 5.1 %collective-permute-start.14 = (f32[128,128]{1,0:T(8,128)S(1)}, f32[128,128]{1,0:T(8,128)S(1)}, u32[]{:S(2)}, u32[]{:S(2)}) collective-permute-start(f32[128,128]{1,0:T(8,128)S(1)} %get-tuple-element.120), channel_id=1, source_target_pairs={{0,4},{4,0},{8,12},{12,8},{1,5},{5,1},{9,13},{13,9},{2,6},{6,2},{1... | collective-permute-start | bytes 196616 | tf_op jit(solution)/shard_map/ppermute | solution.py:332
  51.4 6.8 %collective-permute-start.15 = (f32[128,128]{1,0:T(8,128)S(1)}, f32[128,128]{1,0:T(8,128)S(1)}, u32[]{:S(2)}, u32[]{:S(2)}) collective-permute-start(f32[128,128]{1,0:T(8,128)S(1)} %get-tuple-element.124), channel_id=1, source_target_pairs={{0,8},{4,12},{8,0},{12,4},{1,9},{5,13},{9,1},{13,5},{2,10},{6,14},... | collective-permute-start | bytes 196616 | tf_op jit(solution)/shard_map/ppermute | solution.py:332
  53.1 6.5 %collective-permute-start.16 = (f32[128,128]{1,0:T(8,128)S(1)}, f32[128,128]{1,0:T(8,128)S(1)}, u32[]{:S(2)}, u32[]{:S(2)}) collective-permute-start(f32[128,128]{1,0:T(8,128)S(1)} %get-tuple-element.125), channel_id=1, source_target_pairs={{0,12},{4,8},{8,4},{12,0},{1,13},{5,9},{9,5},{13,1},{2,14},{6,10},... | collective-permute-start | bytes 196616 | tf_op jit(solution)/shard_map/ppermute | solution.py:332
  55.2 4.9 %collective-permute-start.17 = (f32[128,128]{1,0:T(8,128)S(1)}, f32[128,128]{1,0:T(8,128)S(1)}, u32[]{:S(2)}, u32[]{:S(2)}) collective-permute-start(f32[128,128]{1,0:T(8,128)S(1)} %get-tuple-element.127), channel_id=1, source_target_pairs={{0,4},{4,0},{8,12},{12,8},{1,5},{5,1},{9,13},{13,9},{2,6},{6,2},{1... | collective-permute-start | bytes 196616 | tf_op jit(solution)/shard_map/ppermute | solution.py:332
  60.4 5.8 %collective-permute-start.18 = (f32[64,128]{1,0:T(8,128)S(1)}, f32[64,128]{1,0:T(8,128)S(1)}, u32[]{:S(2)}, u32[]{:S(2)}) collective-permute-start(f32[64,128]{1,0:T(8,128)S(1)} %get-tuple-element.132), channel_id=1, source_target_pairs={{0,12},{4,8},{8,4},{12,0},{1,13},{5,9},{9,5},{13,1},{2,14},{6,10},... | collective-permute-start | bytes 98312 | tf_op jit(solution)/shard_map/ppermute | solution.py:332
  62.3 4.8 %collective-permute-start.19 = (f32[64,128]{1,0:T(8,128)S(1)}, f32[64,128]{1,0:T(8,128)S(1)}, u32[]{:S(2)}, u32[]{:S(2)}) collective-permute-start(f32[64,128]{1,0:T(8,128)S(1)} %get-tuple-element.133), channel_id=1, source_target_pairs={{0,8},{4,12},{8,0},{12,4},{1,9},{5,13},{9,1},{13,5},{2,10},{6,14},... | collective-permute-start | bytes 98312 | tf_op jit(solution)/shard_map/ppermute | solution.py:332
  62.3 4.8 %collective-permute-start.20 = (f32[64,128]{1,0:T(8,128)S(1)}, f32[64,128]{1,0:T(8,128)S(1)}, u32[]{:S(2)}, u32[]{:S(2)}) collective-permute-start(f32[64,128]{1,0:T(8,128)S(1)} %get-tuple-element.134), channel_id=1, source_target_pairs={{0,4},{4,0},{8,12},{12,8},{1,5},{5,1},{9,13},{13,9},{2,6},{6,2},{1... | collective-permute-start | bytes 98312 | tf_op jit(solution)/shard_map/ppermute | solution.py:332
  67.4 3.4 %collective-permute-start.21 = (f32[64,128]{1,0:T(8,128)S(1)}, f32[64,128]{1,0:T(8,128)S(1)}, u32[]{:S(2)}, u32[]{:S(2)}) collective-permute-start(f32[64,128]{1,0:T(8,128)S(1)} %get-tuple-element.136), channel_id=1, source_target_pairs={{0,3},{1,2},{2,1},{3,0},{4,7},{5,6},{6,5},{7,4},{8,11},{9,10},{10,... | collective-permute-start | bytes 98312 | tf_op jit(solution)/shard_map/ppermute | solution.py:332
  67.4 4.0 %collective-permute-start.22 = (f32[64,128]{1,0:T(8,128)S(1)}, f32[64,128]{1,0:T(8,128)S(1)}, u32[]{:S(2)}, u32[]{:S(2)}) collective-permute-start(f32[64,128]{1,0:T(8,128)S(1)} %get-tuple-element.137), channel_id=1, source_target_pairs={{0,2},{1,3},{2,0},{3,1},{4,6},{5,7},{6,4},{7,5},{8,10},{9,11},{10,... | collective-permute-start | bytes 98312 | tf_op jit(solution)/shard_map/ppermute | solution.py:332
  68.0 3.5 %collective-permute-start.23 = (f32[64,128]{1,0:T(8,128)S(1)}, f32[64,128]{1,0:T(8,128)S(1)}, u32[]{:S(2)}, u32[]{:S(2)}) collective-permute-start(f32[64,128]{1,0:T(8,128)S(1)} %get-tuple-element.138), channel_id=1, source_target_pairs={{0,1},{1,0},{2,3},{3,2},{4,5},{5,4},{6,7},{7,6},{8,9},{9,8},{10,11... | collective-permute-start | bytes 98312 | tf_op jit(solution)/shard_map/ppermute | solution.py:332
  72.5 8.0 %collective-permute-start.24 = (f32[128,128]{1,0:T(8,128)S(1)}, f32[128,128]{1,0:T(8,128)S(1)}, u32[]{:S(2)}, u32[]{:S(2)}) collective-permute-start(f32[128,128]{1,0:T(8,128)S(1)} %get-tuple-element.141), channel_id=1, source_target_pairs={{0,8},{4,12},{8,0},{12,4},{1,9},{5,13},{9,1},{13,5},{2,10},{6,14},... | collective-permute-start | bytes 196616 | tf_op jit(solution)/shard_map/ppermute | solution.py:332
  74.6 6.5 %collective-permute-start.25 = (f32[128,128]{1,0:T(8,128)S(1)}, f32[128,128]{1,0:T(8,128)S(1)}, u32[]{:S(2)}, u32[]{:S(2)}) collective-permute-start(f32[128,128]{1,0:T(8,128)S(1)} %get-tuple-element.142), channel_id=1, source_target_pairs={{0,12},{4,8},{8,4},{12,0},{1,13},{5,9},{9,5},{13,1},{2,14},{6,10},... | collective-permute-start | bytes 196616 | tf_op jit(solution)/shard_map/ppermute | solution.py:332
  76.7 5.1 %collective-permute-start.26 = (f32[128,128]{1,0:T(8,128)S(1)}, f32[128,128]{1,0:T(8,128)S(1)}, u32[]{:S(2)}, u32[]{:S(2)}) collective-permute-start(f32[128,128]{1,0:T(8,128)S(1)} %get-tuple-element.144), channel_id=1, source_target_pairs={{0,4},{4,0},{8,12},{12,8},{1,5},{5,1},{9,13},{13,9},{2,6},{6,2},{1... | collective-permute-start | bytes 196616 | tf_op jit(solution)/shard_map/ppermute | solution.py:332
  82.4 7.5 %collective-permute-start.27 = (f32[128,128]{1,0:T(8,128)S(1)}, f32[128,128]{1,0:T(8,128)S(1)}, u32[]{:S(2)}, u32[]{:S(2)}) collective-permute-start(f32[128,128]{1,0:T(8,128)S(1)} %get-tuple-element.148), channel_id=1, source_target_pairs={{0,8},{4,12},{8,0},{12,4},{1,9},{5,13},{9,1},{13,5},{2,10},{6,14},... | collective-permute-start | bytes 196616 | tf_op jit(solution)/shard_map/ppermute | solution.py:332
  83.4 6.6 %collective-permute-start.28 = (f32[128,128]{1,0:T(8,128)S(1)}, f32[128,128]{1,0:T(8,128)S(1)}, u32[]{:S(2)}, u32[]{:S(2)}) collective-permute-start(f32[128,128]{1,0:T(8,128)S(1)} %get-tuple-element.149), channel_id=1, source_target_pairs={{0,12},{4,8},{8,4},{12,0},{1,13},{5,9},{9,5},{13,1},{2,14},{6,10},... | collective-permute-start | bytes 196616 | tf_op jit(solution)/shard_map/ppermute | solution.py:332
  85.3 5.2 %collective-permute-start.29 = (f32[128,128]{1,0:T(8,128)S(1)}, f32[128,128]{1,0:T(8,128)S(1)}, u32[]{:S(2)}, u32[]{:S(2)}) collective-permute-start(f32[128,128]{1,0:T(8,128)S(1)} %get-tuple-element.151), channel_id=1, source_target_pairs={{0,4},{4,0},{8,12},{12,8},{1,5},{5,1},{9,13},{13,9},{2,6},{6,2},{1... | collective-permute-start | bytes 196616 | tf_op jit(solution)/shard_map/ppermute | solution.py:332

commit v14 on v7

--- a/solution.py
+++ b/solution.py
@@ -130,7 +130,7 @@
 
 def pack_kernel(times, cap, *refs):
     n = len(times)
-    recvs, (high, low, pack, stack_high, stack_low) = refs[:n], refs[n:]
+    recvs, (high, low, pack, pack_high, pack_low) = refs[:n], refs[n:]
     shared = pack.shape[1]
     width = recvs[0].shape[1]
     column = lax.broadcasted_iota(jnp.int32, (width, shared), 1).astype(F32)
@@ -143,10 +143,8 @@
             size = min(width, cap - c * width)
             at = (d - 1) * cap + c * width
             pack[at:at + size, :] = chosen[:size]
-    for source, stack in ((high, stack_high), (low, stack_low)):
-        square = source[:, :shared]
-        stack[:shared, :] = square
-        stack[shared:, :] = mm(pack[...], square).astype(BF16)
+    for source, picked in ((high, pack_high), (low, pack_low)):
+        picked[...] = mm(pack[...], source[:, :shared]).astype(BF16)
 
 
 def prepare_kernel(contact, modes, tile, floor, basis, tile_high, tile_low):
@@ -176,6 +174,12 @@
 def base_kernel(image, unpack_own, gap, base):
     own = image[...]
     base[...] = gap[:own.shape[0], :] - own + pick(unpack_own[...], own)
+
+
+def image_base_kernel(ahead, high, low, mult, unpack_own, gap, base):
+    shared = mult.shape[0]
+    own = ahead[:shared, :] + product((high[:, :shared], low[:, :shared]), split(mult[...]))
+    base[...] = gap[:shared, :] - own + pick(unpack_own[...], own)
 
 
 def settle(trial, floor, alive):
@@ -295,15 +299,14 @@
 def sweep_kernel(times, cap, size, *refs):
     n = len(times)
     recvs = refs[:n]
-    base, unpack, mult, floor, high, low, ahead, mult_out, image_out = refs[n:n + 9]
+    base, unpack, mult, floor, high, low, ahead, mult_out = refs[n:n + 8]
     shared = base.shape[0]
     residual, alive = shared_residual(times, recvs, base, unpack, size)
     value = settle(mult[...] + STEP * residual, floor[:shared, :], alive)
     mult_out[...] = value
-    both = ahead[...] + product((high[...], low[...]), split(value))
-    image_out[...] = both[:shared]
-    for d, out in enumerate(refs[n + 9:]):
-        out[...] = both[shared + d * cap:shared + (d + 1) * cap]
+    rows = ahead[shared:, :] + product((high[...], low[...]), split(value))
+    for d, out in enumerate(refs[n + 8:]):
+        out[...] = rows[d * cap:(d + 1) * cap]
 
 
 def last_kernel(times, size, *refs):
@@ -334,10 +337,9 @@
     return [swap(blocks[d - 1], axis, count, d) for d in times]
 
 
-def half_first(count, back):
+def half_first(count):
     half = count // 2
-    others = [d for d in range(1, count) if d != half]
-    return (half, *(others[::-1] if back else others))
+    return (half, *(d for d in range(count - 1, 0, -1) if d != half))
 
 
 def middle_first(count):
@@ -376,8 +378,8 @@
     padded = -(-listed // 128) * 128
     size = interface_size
     coarse_order, part_order = far_first(wide), far_first(narrow)
-    half, half_back, middle = half_first(wide, False), half_first(wide, True), middle_first(wide)
-    orders = ((half_back, half, middle), (half_back, half, half_back))
+    middle, half = middle_first(wide), half_first(wide)
+    orders = ((middle, half, half), (half, half, half))
     sent = [shape(cap, loads)] * n
     full = 2 * order * loads
 
@@ -412,19 +414,23 @@
         moved=8 * coarse_inverse.size + 4 * full,
         name="prepare",
     )
+    def base_of(known):
+        ins = (image,) if known else (ahead, top_high, top_low, mult_s)
+        return call(
+            base_kernel if known else image_base_kernel,
+            (*ins, unpack_own, gap),
+            [shape(shared, loads)],
+            flops=10 * shared * shared * loads,
+            moved=8 * shared * loads,
+            name="base",
+        )[0]
+
     mult_s = mult
     scratch = [pltpu.VMEM((order, 2 * loads), BF16)]
     for outer in range(OUTER):
         times = orders[outer][0]
         recvs = swap_rows(sends, "wide", wide, times)
-        base = call(
-            base_kernel,
-            (image, unpack_own, gap),
-            [shape(shared, loads)],
-            flops=4 * shared * shared * loads,
-            moved=8 * shared * loads,
-            name="base",
-        )[0]
+        base = base_of(outer == 0)
         if outer == 0:
             row_block, load_block = block((shared, order)), block((shared, loads))
             next_loads = block((shared, loads), 1)
@@ -448,10 +454,10 @@
                 name="rest_start",
             )
             marks = unpack_all
-            pack, stack_high, stack_low = call(
+            pack, pack_high, pack_low = call(
                 functools.partial(pack_kernel, times, cap),
                 (*recvs, top_high, top_low),
-                [shape(padded, shared, BF16)] + [shape(shared + padded, shared, BF16)] * 2,
+                [shape(padded, shared, BF16)] * 3,
                 flops=8 * padded * shared * shared,
                 moved=8 * padded * shared,
                 name="pack",
@@ -500,14 +506,7 @@
             last = outer == OUTER - 1 and inner == INNER - 1
             times = orders[outer][inner]
             recvs = swap_rows(sends, "wide", wide, times)
-            base = call(
-                base_kernel,
-                (image, unpack_own, gap),
-                [shape(shared, loads)],
-                flops=4 * shared * shared * loads,
-                moved=8 * shared * loads,
-                name="base",
-            )[0]
+            base = base_of(inner == 1)
             ins = (size, high, low, mult_s, mult_n, gap, floor)
             shadow = (size, *recvs, base, unpack, mult_s, floor)
             cost = dict(flops=6 * shared * loads * unpack.shape[1], moved=2 * shared * unpack.shape[1])
@@ -542,10 +541,10 @@
                 moved=4 * order * order,
                 name="rest",
             )
-            mult_s, image, *sends = call(
+            mult_s, *sends = call(
                 functools.partial(sweep_kernel, times, cap),
-                (*shadow, stack_high, stack_low, ahead),
-                [shape(shared, loads)] * 2 + sent,
+                (*shadow, pack_high, pack_low, ahead),
+                [shape(shared, loads)] + sent,
                 name="sweep",
                 **cost,
             )

time: 90.5 us -> 91.3 us (level)
  starting transfers between devices: 39.3 us -> 36.7 us
  waiting for transfers between devices: 30.2 us -> 32.5 us
  Pallas kernels: 19.3 us -> 20.3 us
    ppermute x30, starting transfers between devices: 39.3 us -> 36.7 us  [swap(): return lax.ppermute(block, axis, [(i, i ^ d) for i in range(count)])]
    ppermute x30, waiting for transfers between devices: 30.2 us -> 32.5 us  [swap(): return lax.ppermute(block, axis, [(i, i ^ d) for i in range(count)])]
    pallas_call x25, Pallas kernels: 19.3 us -> 20.3 us  [call(): pl.pallas_call(body, out_shape=outs, grid=grid, in_specs=in_specs, out_sp...]
where the time goes in v14:
time: 91.3 us; the launch traced here: 91.1 us
  starting transfers between devices  36.7 us (40%)
  waiting for transfers between devices  32.5 us (36%)
  Pallas kernels  20.3 us (22%)
  between operations  1.58 us (2%)
    ppermute x30, starting transfers between devices, swap(): return lax.ppermute(block, axis, [(i, i ^ d) for i in range(count)])  36.7 us
    ppermute x30, waiting for transfers between devices, swap(): return lax.ppermute(block, axis, [(i, i ^ d) for i in range(count)])  32.5 us
    pallas_call x25, Pallas kernels, call(): pl.pallas_call(body, out_shape=outs, grid=grid, in_specs=in_specs, out_sp...  20.3 us
  transfers between devices with their start and end apart: 30, of which 24 were waited for; matrix products, arithmetic and copies ran while one was open for 0% of the time, Pallas kernels for 13%

profile of v14, /device:TPU:0, one launch (start us, length us, event | category | flops | bytes accessed | tf_op | source)
XLA Modules:
  0.0 91.1 jit_solution(10803651851855902280)
XLA Ops:
  0.7 2.1 %first.1 = (bf16[256,256]{1,0:T(8,128)(2,1)S(1)}, bf16[256,768]{1,0:T(8,128)(2,1)S(1)}, bf16[256,384]{1,0:T(8,128)(2,1)S(1)}, bf16[256,1024]{1,0:T(8,128)(2,1)S(...) custom-call(s32[1,256]{1,0:T(1,128)} %bitcast.32, ...), custom_call_target="tpu_custom_call" | custom-call | flops 201326592 | bytes 2097152 | tf_op jit(solution)/shard_map/first/pallas_call | solution.py:49
  2.8 5.1 %collective-permute-start = (f32[264,128]{1,0:T(8,128)S(1)}, f32[264,128]{1,0:T(8,128)S(1)}, u32[]{:S(2)}, u32[]{:S(2)}) collective-permute-start(f32[264,128]{1,0:T(8,128)S(1)} %get-tuple-element.78), channel_id=1, source_target_pairs={{0,12},{4,8},{8,4},{12,0},{1,13},{5,9},{9,5},{13,1},{2,14},{6,10},... | collective-permute-start | bytes 405512 | tf_op jit(solution)/shard_map/ppermute | solution.py:329
  7.9 0.6 collective-permute-start.2
  9.4 2.0 %rest_start.1 = (f32[768,128]{1,0:T(8,128)S(1)}, f32[64,128]{1,0:T(8,128)S(1)}, bf16[768,1024]{1,0:T(8,128)(2,1)S(1)}, bf16[768,1024]{1,0:T(8,128)(2,1)S(1)}) custom-call(s32[1]{0:T(128)S(6)} %copy.15.size, f32[1024,1024]{1,0:T(8,128)S(1)} %bitcast.20, f32[1024,128]{1,0:T(8,128)S(1)} %bitcast.22, f32[1024,128]{1,0:T(8,128)S(1)} %bitcast.23, ...), custom_call_target="tpu_custom_call" | custom-call | flops 603979776 | bytes 6291456 | tf_op jit(solution)/shard_map/rest_start/pallas_call | solution.py:49
  11.4 0.9 collective-permute-done.refs_0_
  12.3 3.1 %collective-permute-done.1.refs_1_ = f32[264,128]{1,0:T(8,128)S(1)} collective-permute-done((f32[264,128]{1,0:T(8,128)S(1)}, f32[264,128]{1,0:T(8,128)S(1)}, u32[]{:S(2)}, u32[]{:S(2)}) %collective-permute-start.1) | collective-permute-done | bytes 135200 | tf_op jit(solution)/shard_map/ppermute | solution.py:329
  15.4 3.9 %collective-permute-done.2.refs_2_ = f32[264,128]{1,0:T(8,128)S(1)} collective-permute-done((f32[264,128]{1,0:T(8,128)S(1)}, f32[264,128]{1,0:T(8,128)S(1)}, u32[]{:S(2)}, u32[]{:S(2)}) %collective-permute-start.2) | collective-permute-done | bytes 135200 | tf_op jit(solution)/shard_map/ppermute | solution.py:329
  19.3 0.5 coarse.2
  19.8 2.5 %collective-permute-start.3 = (f32[64,128]{1,0:T(8,128)S(1)}, f32[64,128]{1,0:T(8,128)S(1)}, u32[]{:S(2)}, u32[]{:S(2)}) collective-permute-start(f32[64,128]{1,0:T(8,128)S(1)} %get-tuple-element.86), channel_id=1, source_target_pairs={{0,12},{4,8},{8,4},{12,0},{1,13},{5,9},{9,5},{13,1},{2,14},{6,10},... | collective-permute-start | bytes 98312 | tf_op jit(solution)/shard_map/ppermute | solution.py:329
  22.3 1.9 %collective-permute-start.5 = (f32[64,128]{1,0:T(8,128)S(1)}, f32[64,128]{1,0:T(8,128)S(1)}, u32[]{:S(2)}, u32[]{:S(2)}) collective-permute-start(f32[64,128]{1,0:T(8,128)S(1)} %get-tuple-element.88), channel_id=1, source_target_pairs={{0,4},{4,0},{8,12},{12,8},{1,5},{5,1},{9,13},{13,9},{2,6},{6,2},{1... | collective-permute-start | bytes 98312 | tf_op jit(solution)/shard_map/ppermute | solution.py:329
  24.2 0.4 prepare.1
  24.6 0.9 %collective-permute-done.3.refs_1_ = f32[64,128]{1,0:T(8,128)S(1)} collective-permute-done((f32[64,128]{1,0:T(8,128)S(1)}, f32[64,128]{1,0:T(8,128)S(1)}, u32[]{:S(2)}, u32[]{:S(2)}) %collective-permute-start.3) | collective-permute-done | bytes 32800 | tf_op jit(solution)/shard_map/ppermute | solution.py:329
  25.5 1.6 %collective-permute-done.4.refs_2_ = f32[64,128]{1,0:T(8,128)S(1)} collective-permute-done((f32[64,128]{1,0:T(8,128)S(1)}, f32[64,128]{1,0:T(8,128)S(1)}, u32[]{:S(2)}, u32[]{:S(2)}) %collective-permute-start.4) | collective-permute-done | bytes 32800 | tf_op jit(solution)/shard_map/ppermute | solution.py:329
  27.4 1.6 %collective-permute-start.7 = (f32[64,128]{1,0:T(8,128)S(1)}, f32[64,128]{1,0:T(8,128)S(1)}, u32[]{:S(2)}, u32[]{:S(2)}) collective-permute-start(f32[64,128]{1,0:T(8,128)S(1)} %get-tuple-element.91), channel_id=1, source_target_pairs={{0,2},{1,3},{2,0},{3,1},{4,6},{5,7},{6,4},{7,5},{8,10},{9,11},{10,... | collective-permute-start | bytes 98312 | tf_op jit(solution)/shard_map/ppermute | solution.py:329
  29.0 0.3 collective-permute-start.8
  29.3 0.3 pack.1
  29.6 1.5 %collective-permute-done.6.refs_1_ = f32[64,128]{1,0:T(8,128)S(1)} collective-permute-done((f32[64,128]{1,0:T(8,128)S(1)}, f32[64,128]{1,0:T(8,128)S(1)}, u32[]{:S(2)}, u32[]{:S(2)}) %collective-permute-start.6) | collective-permute-done | bytes 32800 | tf_op jit(solution)/shard_map/ppermute | solution.py:329
  31.1 0.4 collective-permute-done.7.refs_2_
  31.5 1.0 %lift.2 = (f32[256,128]{1,0:T(8,128)S(1)}, f32[768,128]{1,0:T(8,128)S(1)}, f32[256,128]{1,0:T(8,128)S(1)}, f32[128,128]{1,0:T(8,128)S(1)}, f32[128,128]{1,0:T(8,128)S(1)}, /*index=5*/f32[128,128]{1,0:T(8,128)S(1)}) custom-call(s32[1]{0:T(128)S(6)} %copy.15.size, f32[64,128]{1,0:T(8,128)S(1)} %get-tuple-element.89.refs_0_, ...), custom_call_target="tpu_custom_call" | custom-call | flops 201326592 | bytes 1048576 | tf_op jit(solution)/shard_map/lift/pallas_call | solution.py:49
  32.5 2.1 %collective-permute-start.9 = (f32[128,128]{1,0:T(8,128)S(1)}, f32[128,128]{1,0:T(8,128)S(1)}, u32[]{:S(2)}, u32[]{:S(2)}) collective-permute-start(f32[128,128]{1,0:T(8,128)S(1)} %get-tuple-element.100), channel_id=1, source_target_pairs={{0,8},{4,12},{8,0},{12,4},{1,9},{5,13},{9,1},{13,5},{2,10},{6,14},... | collective-permute-start | bytes 196616 | tf_op jit(solution)/shard_map/ppermute | solution.py:329
  34.6 1.4 %collective-permute-start.10 = (f32[128,128]{1,0:T(8,128)S(1)}, f32[128,128]{1,0:T(8,128)S(1)}, u32[]{:S(2)}, u32[]{:S(2)}) collective-permute-start(f32[128,128]{1,0:T(8,128)S(1)} %get-tuple-element.101), channel_id=1, source_target_pairs={{0,12},{4,8},{8,4},{12,0},{1,13},{5,9},{9,5},{13,1},{2,14},{6,10},... | collective-permute-start | bytes 196616 | tf_op jit(solution)/shard_map/ppermute | solution.py:329
  36.2 1.5 %rest.3 = (f32[768,128]{1,0:T(8,128)S(1)}, f32[640,128]{1,0:T(8,128)S(1)}) custom-call(s32[1]{0:T(128)S(6)} %copy.15.size, bf16[768,1024]{1,0:T(8,128)(2,1)S(1)} %get-tuple-element.108.high, bf16[768,1024]{1,0:T(8,128)(2,1)S(1)} %get-tuple-element.109.low, f32[256,128]{1,0:T(8,128)S(1)} %get-tuple-element.105.mult_s.refs_5_, ...), custom_call_target="tpu_custom_call" | custom-call | flops 805306368 | bytes 4194304 | tf_op jit(solution)/shard_map/rest/pallas_call | solution.py:49
  37.7 3.1 %collective-permute-done.9.refs_0_ = f32[128,128]{1,0:T(8,128)S(1)} collective-permute-done((f32[128,128]{1,0:T(8,128)S(1)}, f32[128,128]{1,0:T(8,128)S(1)}, u32[]{:S(2)}, u32[]{:S(2)}) %collective-permute-start.9) | collective-permute-done | bytes 65568 | tf_op jit(solution)/shard_map/ppermute | solution.py:329
  40.8 0.3 collective-permute-done.10.refs_1_
  41.1 0.8 collective-permute-done.11.refs_2_
  41.9 0.6 sweep.3
  42.5 1.0 %collective-permute-start.12 = (f32[128,128]{1,0:T(8,128)S(1)}, f32[128,128]{1,0:T(8,128)S(1)}, u32[]{:S(2)}, u32[]{:S(2)}) collective-permute-start(f32[128,128]{1,0:T(8,128)S(1)} %get-tuple-element.112), channel_id=1, source_target_pairs={{0,8},{4,12},{8,0},{12,4},{1,9},{5,13},{9,1},{13,5},{2,10},{6,14},... | collective-permute-start | bytes 196616 | tf_op jit(solution)/shard_map/ppermute | solution.py:329
  43.6 2.0 %collective-permute-start.13 = (f32[128,128]{1,0:T(8,128)S(1)}, f32[128,128]{1,0:T(8,128)S(1)}, u32[]{:S(2)}, u32[]{:S(2)}) collective-permute-start(f32[128,128]{1,0:T(8,128)S(1)} %get-tuple-element.113), channel_id=1, source_target_pairs={{0,12},{4,8},{8,4},{12,0},{1,13},{5,9},{9,5},{13,1},{2,14},{6,10},... | collective-permute-start | bytes 196616 | tf_op jit(solution)/shard_map/ppermute | solution.py:329
  45.6 0.5 collective-permute-start.14
  46.1 0.5 base.8.refs_3_
  46.6 1.5 %rest.4 = (f32[768,128]{1,0:T(8,128)S(1)}, f32[640,128]{1,0:T(8,128)S(1)}) custom-call(s32[1]{0:T(128)S(6)} %copy.15.size, bf16[768,1024]{1,0:T(8,128)(2,1)S(1)} %get-tuple-element.108.high, bf16[768,1024]{1,0:T(8,128)(2,1)S(1)} %get-tuple-element.109.low, f32[256,128]{1,0:T(8,128)S(1)} %get-tuple-element.115.mult.mult_s.refs_5_, ...), custom_call_target="tpu_custom_call" | custom-call | flops 805306368 | bytes 4194304 | tf_op jit(solution)/shard_map/rest/pallas_call | solution.py:49
  48.1 2.5 %collective-permute-done.12.refs_0_ = f32[128,128]{1,0:T(8,128)S(1)} collective-permute-done((f32[128,128]{1,0:T(8,128)S(1)}, f32[128,128]{1,0:T(8,128)S(1)}, u32[]{:S(2)}, u32[]{:S(2)}) %collective-permute-start.12) | collective-permute-done | bytes 65568 | tf_op jit(solution)/shard_map/ppermute | solution.py:329
  50.9 0.6 sweep.4
  51.5 1.4 %collective-permute-start.15 = (f32[128,128]{1,0:T(8,128)S(1)}, f32[128,128]{1,0:T(8,128)S(1)}, u32[]{:S(2)}, u32[]{:S(2)}) collective-permute-start(f32[128,128]{1,0:T(8,128)S(1)} %get-tuple-element.118), channel_id=1, source_target_pairs={{0,8},{4,12},{8,0},{12,4},{1,9},{5,13},{9,1},{13,5},{2,10},{6,14},... | collective-permute-start | bytes 196616 | tf_op jit(solution)/shard_map/ppermute | solution.py:329
  52.9 2.1 %collective-permute-start.16 = (f32[128,128]{1,0:T(8,128)S(1)}, f32[128,128]{1,0:T(8,128)S(1)}, u32[]{:S(2)}, u32[]{:S(2)}) collective-permute-start(f32[128,128]{1,0:T(8,128)S(1)} %get-tuple-element.119), channel_id=1, source_target_pairs={{0,12},{4,8},{8,4},{12,0},{1,13},{5,9},{9,5},{13,1},{2,14},{6,10},... | collective-permute-start | bytes 196616 | tf_op jit(solution)/shard_map/ppermute | solution.py:329
  55.0 0.5 base.9.refs_3_
  55.5 1.1 %rest_first.1 = (f32[768,128]{1,0:T(8,128)S(1)}, f32[64,128]{1,0:T(8,128)S(1)}) custom-call(s32[1]{0:T(128)S(6)} %copy.15.size, bf16[768,1024]{1,0:T(8,128)(2,1)S(1)} %get-tuple-element.108.high, bf16[768,1024]{1,0:T(8,128)(2,1)S(1)} %get-tuple-element.109.low, f32[256,128]{1,0:T(8,128)S(1)} %get-tuple-element.121.mult.mult_s.refs_5_, ...), custom_call_target="tpu_custom_call" | custom-call | flops 603979776 | bytes 3145728 | tf_op jit(solution)/shard_map/rest_first/pallas_call | solution.py:49
  56.7 1.5 %collective-permute-done.15.refs_0_ = f32[128,128]{1,0:T(8,128)S(1)} collective-permute-done((f32[128,128]{1,0:T(8,128)S(1)}, f32[128,128]{1,0:T(8,128)S(1)}, u32[]{:S(2)}, u32[]{:S(2)}) %collective-permute-start.15) | collective-permute-done | bytes 65568 | tf_op jit(solution)/shard_map/ppermute | solution.py:329
  58.1 0.9 %collective-permute-done.16.refs_1_ = f32[128,128]{1,0:T(8,128)S(1)} collective-permute-done((f32[128,128]{1,0:T(8,128)S(1)}, f32[128,128]{1,0:T(8,128)S(1)}, u32[]{:S(2)}, u32[]{:S(2)}) %collective-permute-start.16) | collective-permute-done | bytes 65568 | tf_op jit(solution)/shard_map/ppermute | solution.py:329
  59.1 0.6 collective-permute-done.17.refs_2_
  59.7 0.4 coarse.3
  60.1 2.0 %collective-permute-start.18 = (f32[64,128]{1,0:T(8,128)S(1)}, f32[64,128]{1,0:T(8,128)S(1)}, u32[]{:S(2)}, u32[]{:S(2)}) collective-permute-start(f32[64,128]{1,0:T(8,128)S(1)} %get-tuple-element.125), channel_id=1, source_target_pairs={{0,12},{4,8},{8,4},{12,0},{1,13},{5,9},{9,5},{13,1},{2,14},{6,10},... | collective-permute-start | bytes 98312 | tf_op jit(solution)/shard_map/ppermute | solution.py:329
  62.2 2.4 %collective-permute-start.20 = (f32[64,128]{1,0:T(8,128)S(1)}, f32[64,128]{1,0:T(8,128)S(1)}, u32[]{:S(2)}, u32[]{:S(2)}) collective-permute-start(f32[64,128]{1,0:T(8,128)S(1)} %get-tuple-element.127), channel_id=1, source_target_pairs={{0,4},{4,0},{8,12},{12,8},{1,5},{5,1},{9,13},{13,9},{2,6},{6,2},{1... | collective-permute-start | bytes 98312 | tf_op jit(solution)/shard_map/ppermute | solution.py:329
  64.6 1.3 %collective-permute-done.18.refs_1_ = f32[64,128]{1,0:T(8,128)S(1)} collective-permute-done((f32[64,128]{1,0:T(8,128)S(1)}, f32[64,128]{1,0:T(8,128)S(1)}, u32[]{:S(2)}, u32[]{:S(2)}) %collective-permute-start.18) | collective-permute-done | bytes 32800 | tf_op jit(solution)/shard_map/ppermute | solution.py:329
  65.9 1.1 %collective-permute-done.19.refs_2_ = f32[64,128]{1,0:T(8,128)S(1)} collective-permute-done((f32[64,128]{1,0:T(8,128)S(1)}, f32[64,128]{1,0:T(8,128)S(1)}, u32[]{:S(2)}, u32[]{:S(2)}) %collective-permute-start.19) | collective-permute-done | bytes 32800 | tf_op jit(solution)/shard_map/ppermute | solution.py:329
  67.5 1.6 %collective-permute-start.23 = (f32[64,128]{1,0:T(8,128)S(1)}, f32[64,128]{1,0:T(8,128)S(1)}, u32[]{:S(2)}, u32[]{:S(2)}) collective-permute-start(f32[64,128]{1,0:T(8,128)S(1)} %get-tuple-element.131), channel_id=1, source_target_pairs={{0,1},{1,0},{2,3},{3,2},{4,5},{5,4},{6,7},{7,6},{8,9},{9,8},{10,11... | collective-permute-start | bytes 98312 | tf_op jit(solution)/shard_map/ppermute | solution.py:329
  69.2 1.5 %collective-permute-done.21.refs_1_ = f32[64,128]{1,0:T(8,128)S(1)} collective-permute-done((f32[64,128]{1,0:T(8,128)S(1)}, f32[64,128]{1,0:T(8,128)S(1)}, u32[]{:S(2)}, u32[]{:S(2)}) %collective-permute-start.21) | collective-permute-done | bytes 32800 | tf_op jit(solution)/shard_map/ppermute | solution.py:329
  70.7 0.7 collective-permute-done.22.refs_2_
  71.4 1.0 %lift.3 = (f32[256,128]{1,0:T(8,128)S(1)}, f32[768,128]{1,0:T(8,128)S(1)}, f32[256,128]{1,0:T(8,128)S(1)}, f32[128,128]{1,0:T(8,128)S(1)}, f32[128,128]{1,0:T(8,128)S(1)}, /*index=5*/f32[128,128]{1,0:T(8,128)S(1)}) custom-call(s32[1]{0:T(128)S(6)} %copy.15.size, f32[64,128]{1,0:T(8,128)S(1)} %get-tuple-element.128.refs_0_, ...), custom_call_target="tpu_custom_call" | custom-call | flops 201326592 | bytes 1048576 | tf_op jit(solution)/shard_map/lift/pallas_call | solution.py:49
  72.4 2.1 %collective-permute-start.24 = (f32[128,128]{1,0:T(8,128)S(1)}, f32[128,128]{1,0:T(8,128)S(1)}, u32[]{:S(2)}, u32[]{:S(2)}) collective-permute-start(f32[128,128]{1,0:T(8,128)S(1)} %get-tuple-element.134), channel_id=1, source_target_pairs={{0,8},{4,12},{8,0},{12,4},{1,9},{5,13},{9,1},{13,5},{2,10},{6,14},... | collective-permute-start | bytes 196616 | tf_op jit(solution)/shard_map/ppermute | solution.py:329
  74.5 1.9 %collective-permute-start.25 = (f32[128,128]{1,0:T(8,128)S(1)}, f32[128,128]{1,0:T(8,128)S(1)}, u32[]{:S(2)}, u32[]{:S(2)}) collective-permute-start(f32[128,128]{1,0:T(8,128)S(1)} %get-tuple-element.135), channel_id=1, source_target_pairs={{0,12},{4,8},{8,4},{12,0},{1,13},{5,9},{9,5},{13,1},{2,14},{6,10},... | collective-permute-start | bytes 196616 | tf_op jit(solution)/shard_map/ppermute | solution.py:329
  76.5 1.5 %rest.5 = (f32[768,128]{1,0:T(8,128)S(1)}, f32[640,128]{1,0:T(8,128)S(1)}) custom-call(s32[1]{0:T(128)S(6)} %copy.15.size, bf16[768,1024]{1,0:T(8,128)(2,1)S(1)} %get-tuple-element.108.high, bf16[768,1024]{1,0:T(8,128)(2,1)S(1)} %get-tuple-element.109.low, f32[256,128]{1,0:T(8,128)S(1)} %get-tuple-element.138.mult_s.refs_5_, ...), custom_call_target="tpu_custom_call" | custom-call | flops 805306368 | bytes 4194304 | tf_op jit(solution)/shard_map/rest/pallas_call | solution.py:49
  78.0 2.1 %collective-permute-done.24.refs_0_ = f32[128,128]{1,0:T(8,128)S(1)} collective-permute-done((f32[128,128]{1,0:T(8,128)S(1)}, f32[128,128]{1,0:T(8,128)S(1)}, u32[]{:S(2)}, u32[]{:S(2)}) %collective-permute-start.24) | collective-permute-done | bytes 65568 | tf_op jit(solution)/shard_map/ppermute | solution.py:329
  80.2 0.7 collective-permute-done.25.refs_1_
  80.8 0.8 collective-permute-done.26.refs_2_
  81.6 0.6 sweep.5
  82.2 0.9 %collective-permute-start.27 = (f32[128,128]{1,0:T(8,128)S(1)}, f32[128,128]{1,0:T(8,128)S(1)}, u32[]{:S(2)}, u32[]{:S(2)}) collective-permute-start(f32[128,128]{1,0:T(8,128)S(1)} %get-tuple-element.141), channel_id=1, source_target_pairs={{0,8},{4,12},{8,0},{12,4},{1,9},{5,13},{9,1},{13,5},{2,10},{6,14},... | collective-permute-start | bytes 196616 | tf_op jit(solution)/shard_map/ppermute | solution.py:329
  83.1 1.9 %collective-permute-start.28 = (f32[128,128]{1,0:T(8,128)S(1)}, f32[128,128]{1,0:T(8,128)S(1)}, u32[]{:S(2)}, u32[]{:S(2)}) collective-permute-start(f32[128,128]{1,0:T(8,128)S(1)} %get-tuple-element.142), channel_id=1, source_target_pairs={{0,12},{4,8},{8,4},{12,0},{1,13},{5,9},{9,5},{13,1},{2,14},{6,10},... | collective-permute-start | bytes 196616 | tf_op jit(solution)/shard_map/ppermute | solution.py:329
  85.0 0.7 collective-permute-start.29
  85.7 0.5 base.11.refs_3_
  86.2 1.9 %rest_last.1 = (f32[1024,128]{1,0:T(8,128)}, f32[1024,128]{1,0:T(8,128)}) custom-call(s32[1]{0:T(128)S(6)} %copy.15.size, bf16[768,1024]{1,0:T(8,128)(2,1)S(1)} %get-tuple-element.108.high, bf16[768,1024]{1,0:T(8,128)(2,1)S(1)} %get-tuple-element.109.low, f32[256,128]{1,0:T(8,128)S(1)} %get-tuple-element.144.mult.mult_s.refs_5_, ...), custom_call_target="tpu_custom_call" | custom-call | flops 603979776 | bytes 3145728 | tf_op jit(solution)/shard_map/rest_last/pallas_call | solution.py:49
  88.1 1.4 %collective-permute-done.27.refs_0_ = f32[128,128]{1,0:T(8,128)S(1)} collective-permute-done((f32[128,128]{1,0:T(8,128)S(1)}, f32[128,128]{1,0:T(8,128)S(1)}, u32[]{:S(2)}, u32[]{:S(2)}) %collective-permute-start.27) | collective-permute-done | bytes 65568 | tf_op jit(solution)/shard_map/ppermute | solution.py:329
  89.5 0.6 collective-permute-done.29.refs_2_
  90.2 0.9 %last.1 = (f32[1024,128]{1,0:T(8,128)}, f32[1024,128]{1,0:T(8,128)}) custom-call(s32[1]{0:T(128)S(6)} %copy.15.size, f32[128,128]{1,0:T(8,128)S(1)} %collective-permute-done.27.refs_0_, f32[128,128]{1,0:T(8,128)S(1)} %collective-permute-done.28.refs_1_, ...), custom_call_target="tpu_custom_call", output_to_operand_aliasing={{0}: (8, {}), {1}: (9, {})} | custom-call | flops 75497472 | bytes 196608 | tf_op jit(solution)/shard_map/last/pallas_call | solution.py:49
  (33 shorter events, 1.9 us)
Async XLA Ops:
  0.6 8.5 %copy-start = (f32[1,1024,128]{2,1,0:T(8,128)S(1)}, f32[1,1024,128]{2,1,0:T(8,128)}, u32[]{:S(2)}) copy-start(f32[1,1024,128]{2,1,0:T(8,128)} %param.12) | copy-start | bytes 1572868
  0.6 8.7 %copy-start.1 = (f32[1,1024,1024]{2,1,0:T(8,128)S(1)}, f32[1,1024,1024]{2,1,0:T(8,128)}, u32[]{:S(2)}) copy-start(f32[1,1024,1024]{2,1,0:T(8,128)} %param.9) | copy-start | bytes 12582916
  0.7 8.7 %copy-start.2 = (f32[1,1024,128]{2,1,0:T(8,128)S(1)}, f32[1,1024,128]{2,1,0:T(8,128)}, u32[]{:S(2)}) copy-start(f32[1,1024,128]{2,1,0:T(8,128)} %param.13) | copy-start | bytes 1572868
  0.7 8.7 %copy-start.3 = (f32[1,64,1024]{2,1,0:T(8,128)S(1)}, f32[1,64,1024]{2,1,0:T(8,128)}, u32[]{:S(2)}) copy-start(f32[1,64,1024]{2,1,0:T(8,128)} %param.11) | copy-start | bytes 786436
  2.8 9.6 %collective-permute-start = (f32[264,128]{1,0:T(8,128)S(1)}, f32[264,128]{1,0:T(8,128)S(1)}, u32[]{:S(2)}, u32[]{:S(2)}) collective-permute-start(f32[264,128]{1,0:T(8,128)S(1)} %get-tuple-element.78), channel_id=1, source_target_pairs={{0,12},{4,8},{8,4},{12,0},{1,13},{5,9},{9,5},{13,1},{2,14},{6,10},... | collective-permute-start | bytes 405512 | tf_op jit(solution)/shard_map/ppermute | solution.py:329
  7.9 7.6 %collective-permute-start.1 = (f32[264,128]{1,0:T(8,128)S(1)}, f32[264,128]{1,0:T(8,128)S(1)}, u32[]{:S(2)}, u32[]{:S(2)}) collective-permute-start(f32[264,128]{1,0:T(8,128)S(1)} %get-tuple-element.79), channel_id=1, source_target_pairs={{0,4},{4,0},{8,12},{12,8},{1,5},{5,1},{9,13},{13,9},{2,6},{6,2},{1... | collective-permute-start | bytes 405512 | tf_op jit(solution)/shard_map/ppermute | solution.py:329
  7.9 11.4 %collective-permute-start.2 = (f32[264,128]{1,0:T(8,128)S(1)}, f32[264,128]{1,0:T(8,128)S(1)}, u32[]{:S(2)}, u32[]{:S(2)}) collective-permute-start(f32[264,128]{1,0:T(8,128)S(1)} %get-tuple-element.80), channel_id=1, source_target_pairs={{0,8},{4,12},{8,0},{12,4},{1,9},{5,13},{9,1},{13,5},{2,10},{6,14},... | collective-permute-start | bytes 405512 | tf_op jit(solution)/shard_map/ppermute | solution.py:329
  11.4 12.8 %copy-start.4 = (f32[256,256]{1,0:T(8,128)S(1)}, f32[256,256]{1,0:T(8,128)}, u32[]{:S(2)}) copy-start(f32[256,256]{1,0:T(8,128)} %tile.3) | copy-start | bytes 786436
  11.4 12.8 %copy-start.5 = (s32[1,1024]{1,0:T(1,128)S(1)}, s32[1,1024]{1,0:T(1,128)}, u32[]{:S(2)}) copy-start(s32[1,1024]{1,0:T(1,128)} %contact.1) | copy-start | bytes 12292
  19.8 5.8 %collective-permute-start.3 = (f32[64,128]{1,0:T(8,128)S(1)}, f32[64,128]{1,0:T(8,128)S(1)}, u32[]{:S(2)}, u32[]{:S(2)}) collective-permute-start(f32[64,128]{1,0:T(8,128)S(1)} %get-tuple-element.86), channel_id=1, source_target_pairs={{0,12},{4,8},{8,4},{12,0},{1,13},{5,9},{9,5},{13,1},{2,14},{6,10},... | collective-permute-start | bytes 98312 | tf_op jit(solution)/shard_map/ppermute | solution.py:329
  22.3 4.8 %collective-permute-start.4 = (f32[64,128]{1,0:T(8,128)S(1)}, f32[64,128]{1,0:T(8,128)S(1)}, u32[]{:S(2)}, u32[]{:S(2)}) collective-permute-start(f32[64,128]{1,0:T(8,128)S(1)} %get-tuple-element.87), channel_id=1, source_target_pairs={{0,8},{4,12},{8,0},{12,4},{1,9},{5,13},{9,1},{13,5},{2,10},{6,14},... | collective-permute-start | bytes 98312 | tf_op jit(solution)/shard_map/ppermute | solution.py:329
  22.3 4.8 %collective-permute-start.5 = (f32[64,128]{1,0:T(8,128)S(1)}, f32[64,128]{1,0:T(8,128)S(1)}, u32[]{:S(2)}, u32[]{:S(2)}) collective-permute-start(f32[64,128]{1,0:T(8,128)S(1)} %get-tuple-element.88), channel_id=1, source_target_pairs={{0,4},{4,0},{8,12},{12,8},{1,5},{5,1},{9,13},{13,9},{2,6},{6,2},{1... | collective-permute-start | bytes 98312 | tf_op jit(solution)/shard_map/ppermute | solution.py:329
  27.4 3.7 %collective-permute-start.6 = (f32[64,128]{1,0:T(8,128)S(1)}, f32[64,128]{1,0:T(8,128)S(1)}, u32[]{:S(2)}, u32[]{:S(2)}) collective-permute-start(f32[64,128]{1,0:T(8,128)S(1)} %get-tuple-element.90), channel_id=1, source_target_pairs={{0,3},{1,2},{2,1},{3,0},{4,7},{5,6},{6,5},{7,4},{8,11},{9,10},{10,... | collective-permute-start | bytes 98312 | tf_op jit(solution)/shard_map/ppermute | solution.py:329
  27.4 4.0 %collective-permute-start.7 = (f32[64,128]{1,0:T(8,128)S(1)}, f32[64,128]{1,0:T(8,128)S(1)}, u32[]{:S(2)}, u32[]{:S(2)}) collective-permute-start(f32[64,128]{1,0:T(8,128)S(1)} %get-tuple-element.91), channel_id=1, source_target_pairs={{0,2},{1,3},{2,0},{3,1},{4,6},{5,7},{6,4},{7,5},{8,10},{9,11},{10,... | collective-permute-start | bytes 98312 | tf_op jit(solution)/shard_map/ppermute | solution.py:329
  29.0 2.5 %collective-permute-start.8 = (f32[64,128]{1,0:T(8,128)S(1)}, f32[64,128]{1,0:T(8,128)S(1)}, u32[]{:S(2)}, u32[]{:S(2)}) collective-permute-start(f32[64,128]{1,0:T(8,128)S(1)} %get-tuple-element.92), channel_id=1, source_target_pairs={{0,1},{1,0},{2,3},{3,2},{4,5},{5,4},{6,7},{7,6},{8,9},{9,8},{10,11... | collective-permute-start | bytes 98312 | tf_op jit(solution)/shard_map/ppermute | solution.py:329
  32.5 8.3 %collective-permute-start.9 = (f32[128,128]{1,0:T(8,128)S(1)}, f32[128,128]{1,0:T(8,128)S(1)}, u32[]{:S(2)}, u32[]{:S(2)}) collective-permute-start(f32[128,128]{1,0:T(8,128)S(1)} %get-tuple-element.100), channel_id=1, source_target_pairs={{0,8},{4,12},{8,0},{12,4},{1,9},{5,13},{9,1},{13,5},{2,10},{6,14},... | collective-permute-start | bytes 196616 | tf_op jit(solution)/shard_map/ppermute | solution.py:329
  34.6 6.6 %collective-permute-start.10 = (f32[128,128]{1,0:T(8,128)S(1)}, f32[128,128]{1,0:T(8,128)S(1)}, u32[]{:S(2)}, u32[]{:S(2)}) collective-permute-start(f32[128,128]{1,0:T(8,128)S(1)} %get-tuple-element.101), channel_id=1, source_target_pairs={{0,12},{4,8},{8,4},{12,0},{1,13},{5,9},{9,5},{13,1},{2,14},{6,10},... | collective-permute-start | bytes 196616 | tf_op jit(solution)/shard_map/ppermute | solution.py:329
  35.9 6.0 %collective-permute-start.11 = (f32[128,128]{1,0:T(8,128)S(1)}, f32[128,128]{1,0:T(8,128)S(1)}, u32[]{:S(2)}, u32[]{:S(2)}) collective-permute-start(f32[128,128]{1,0:T(8,128)S(1)} %get-tuple-element.102), channel_id=1, source_target_pairs={{0,4},{4,0},{8,12},{12,8},{1,5},{5,1},{9,13},{13,9},{2,6},{6,2},{1... | collective-permute-start | bytes 196616 | tf_op jit(solution)/shard_map/ppermute | solution.py:329
  42.5 8.1 %collective-permute-start.12 = (f32[128,128]{1,0:T(8,128)S(1)}, f32[128,128]{1,0:T(8,128)S(1)}, u32[]{:S(2)}, u32[]{:S(2)}) collective-permute-start(f32[128,128]{1,0:T(8,128)S(1)} %get-tuple-element.112), channel_id=1, source_target_pairs={{0,8},{4,12},{8,0},{12,4},{1,9},{5,13},{9,1},{13,5},{2,10},{6,14},... | collective-permute-start | bytes 196616 | tf_op jit(solution)/shard_map/ppermute | solution.py:329
  43.6 7.0 %collective-permute-start.13 = (f32[128,128]{1,0:T(8,128)S(1)}, f32[128,128]{1,0:T(8,128)S(1)}, u32[]{:S(2)}, u32[]{:S(2)}) collective-permute-start(f32[128,128]{1,0:T(8,128)S(1)} %get-tuple-element.113), channel_id=1, source_target_pairs={{0,12},{4,8},{8,4},{12,0},{1,13},{5,9},{9,5},{13,1},{2,14},{6,10},... | collective-permute-start | bytes 196616 | tf_op jit(solution)/shard_map/ppermute | solution.py:329
  45.6 5.3 %collective-permute-start.14 = (f32[128,128]{1,0:T(8,128)S(1)}, f32[128,128]{1,0:T(8,128)S(1)}, u32[]{:S(2)}, u32[]{:S(2)}) collective-permute-start(f32[128,128]{1,0:T(8,128)S(1)} %get-tuple-element.114), channel_id=1, source_target_pairs={{0,4},{4,0},{8,12},{12,8},{1,5},{5,1},{9,13},{13,9},{2,6},{6,2},{1... | collective-permute-start | bytes 196616 | tf_op jit(solution)/shard_map/ppermute | solution.py:329
  51.5 6.6 %collective-permute-start.15 = (f32[128,128]{1,0:T(8,128)S(1)}, f32[128,128]{1,0:T(8,128)S(1)}, u32[]{:S(2)}, u32[]{:S(2)}) collective-permute-start(f32[128,128]{1,0:T(8,128)S(1)} %get-tuple-element.118), channel_id=1, source_target_pairs={{0,8},{4,12},{8,0},{12,4},{1,9},{5,13},{9,1},{13,5},{2,10},{6,14},... | collective-permute-start | bytes 196616 | tf_op jit(solution)/shard_map/ppermute | solution.py:329
  52.9 6.2 %collective-permute-start.16 = (f32[128,128]{1,0:T(8,128)S(1)}, f32[128,128]{1,0:T(8,128)S(1)}, u32[]{:S(2)}, u32[]{:S(2)}) collective-permute-start(f32[128,128]{1,0:T(8,128)S(1)} %get-tuple-element.119), channel_id=1, source_target_pairs={{0,12},{4,8},{8,4},{12,0},{1,13},{5,9},{9,5},{13,1},{2,14},{6,10},... | collective-permute-start | bytes 196616 | tf_op jit(solution)/shard_map/ppermute | solution.py:329
  55.0 4.7 %collective-permute-start.17 = (f32[128,128]{1,0:T(8,128)S(1)}, f32[128,128]{1,0:T(8,128)S(1)}, u32[]{:S(2)}, u32[]{:S(2)}) collective-permute-start(f32[128,128]{1,0:T(8,128)S(1)} %get-tuple-element.120), channel_id=1, source_target_pairs={{0,4},{4,0},{8,12},{12,8},{1,5},{5,1},{9,13},{13,9},{2,6},{6,2},{1... | collective-permute-start | bytes 196616 | tf_op jit(solution)/shard_map/ppermute | solution.py:329
  60.1 5.8 %collective-permute-start.18 = (f32[64,128]{1,0:T(8,128)S(1)}, f32[64,128]{1,0:T(8,128)S(1)}, u32[]{:S(2)}, u32[]{:S(2)}) collective-permute-start(f32[64,128]{1,0:T(8,128)S(1)} %get-tuple-element.125), channel_id=1, source_target_pairs={{0,12},{4,8},{8,4},{12,0},{1,13},{5,9},{9,5},{13,1},{2,14},{6,10},... | collective-permute-start | bytes 98312 | tf_op jit(solution)/shard_map/ppermute | solution.py:329
  62.2 4.8 %collective-permute-start.19 = (f32[64,128]{1,0:T(8,128)S(1)}, f32[64,128]{1,0:T(8,128)S(1)}, u32[]{:S(2)}, u32[]{:S(2)}) collective-permute-start(f32[64,128]{1,0:T(8,128)S(1)} %get-tuple-element.126), channel_id=1, source_target_pairs={{0,8},{4,12},{8,0},{12,4},{1,9},{5,13},{9,1},{13,5},{2,10},{6,14},... | collective-permute-start | bytes 98312 | tf_op jit(solution)/shard_map/ppermute | solution.py:329
  62.2 4.8 %collective-permute-start.20 = (f32[64,128]{1,0:T(8,128)S(1)}, f32[64,128]{1,0:T(8,128)S(1)}, u32[]{:S(2)}, u32[]{:S(2)}) collective-permute-start(f32[64,128]{1,0:T(8,128)S(1)} %get-tuple-element.127), channel_id=1, source_target_pairs={{0,4},{4,0},{8,12},{12,8},{1,5},{5,1},{9,13},{13,9},{2,6},{6,2},{1... | collective-permute-start | bytes 98312 | tf_op jit(solution)/shard_map/ppermute | solution.py:329
  67.3 3.4 %collective-permute-start.21 = (f32[64,128]{1,0:T(8,128)S(1)}, f32[64,128]{1,0:T(8,128)S(1)}, u32[]{:S(2)}, u32[]{:S(2)}) collective-permute-start(f32[64,128]{1,0:T(8,128)S(1)} %get-tuple-element.129), channel_id=1, source_target_pairs={{0,3},{1,2},{2,1},{3,0},{4,7},{5,6},{6,5},{7,4},{8,11},{9,10},{10,... | collective-permute-start | bytes 98312 | tf_op jit(solution)/shard_map/ppermute | solution.py:329
  67.3 4.0 %collective-permute-start.22 = (f32[64,128]{1,0:T(8,128)S(1)}, f32[64,128]{1,0:T(8,128)S(1)}, u32[]{:S(2)}, u32[]{:S(2)}) collective-permute-start(f32[64,128]{1,0:T(8,128)S(1)} %get-tuple-element.130), channel_id=1, source_target_pairs={{0,2},{1,3},{2,0},{3,1},{4,6},{5,7},{6,4},{7,5},{8,10},{9,11},{10,... | collective-permute-start | bytes 98312 | tf_op jit(solution)/shard_map/ppermute | solution.py:329
  67.5 3.8 %collective-permute-start.23 = (f32[64,128]{1,0:T(8,128)S(1)}, f32[64,128]{1,0:T(8,128)S(1)}, u32[]{:S(2)}, u32[]{:S(2)}) collective-permute-start(f32[64,128]{1,0:T(8,128)S(1)} %get-tuple-element.131), channel_id=1, source_target_pairs={{0,1},{1,0},{2,3},{3,2},{4,5},{5,4},{6,7},{7,6},{8,9},{9,8},{10,11... | collective-permute-start | bytes 98312 | tf_op jit(solution)/shard_map/ppermute | solution.py:329
  72.4 7.8 %collective-permute-start.24 = (f32[128,128]{1,0:T(8,128)S(1)}, f32[128,128]{1,0:T(8,128)S(1)}, u32[]{:S(2)}, u32[]{:S(2)}) collective-permute-start(f32[128,128]{1,0:T(8,128)S(1)} %get-tuple-element.134), channel_id=1, source_target_pairs={{0,8},{4,12},{8,0},{12,4},{1,9},{5,13},{9,1},{13,5},{2,10},{6,14},... | collective-permute-start | bytes 196616 | tf_op jit(solution)/shard_map/ppermute | solution.py:329
  74.5 6.4 %collective-permute-start.25 = (f32[128,128]{1,0:T(8,128)S(1)}, f32[128,128]{1,0:T(8,128)S(1)}, u32[]{:S(2)}, u32[]{:S(2)}) collective-permute-start(f32[128,128]{1,0:T(8,128)S(1)} %get-tuple-element.135), channel_id=1, source_target_pairs={{0,12},{4,8},{8,4},{12,0},{1,13},{5,9},{9,5},{13,1},{2,14},{6,10},... | collective-permute-start | bytes 196616 | tf_op jit(solution)/shard_map/ppermute | solution.py:329
  76.3 5.3 %collective-permute-start.26 = (f32[128,128]{1,0:T(8,128)S(1)}, f32[128,128]{1,0:T(8,128)S(1)}, u32[]{:S(2)}, u32[]{:S(2)}) collective-permute-start(f32[128,128]{1,0:T(8,128)S(1)} %get-tuple-element.136), channel_id=1, source_target_pairs={{0,4},{4,0},{8,12},{12,8},{1,5},{5,1},{9,13},{13,9},{2,6},{6,2},{1... | collective-permute-start | bytes 196616 | tf_op jit(solution)/shard_map/ppermute | solution.py:329
  82.2 7.3 %collective-permute-start.27 = (f32[128,128]{1,0:T(8,128)S(1)}, f32[128,128]{1,0:T(8,128)S(1)}, u32[]{:S(2)}, u32[]{:S(2)}) collective-permute-start(f32[128,128]{1,0:T(8,128)S(1)} %get-tuple-element.141), channel_id=1, source_target_pairs={{0,8},{4,12},{8,0},{12,4},{1,9},{5,13},{9,1},{13,5},{2,10},{6,14},... | collective-permute-start | bytes 196616 | tf_op jit(solution)/shard_map/ppermute | solution.py:329
  83.1 6.4 %collective-permute-start.28 = (f32[128,128]{1,0:T(8,128)S(1)}, f32[128,128]{1,0:T(8,128)S(1)}, u32[]{:S(2)}, u32[]{:S(2)}) collective-permute-start(f32[128,128]{1,0:T(8,128)S(1)} %get-tuple-element.142), channel_id=1, source_target_pairs={{0,12},{4,8},{8,4},{12,0},{1,13},{5,9},{9,5},{13,1},{2,14},{6,10},... | collective-permute-start | bytes 196616 | tf_op jit(solution)/shard_map/ppermute | solution.py:329
  85.0 5.2 %collective-permute-start.29 = (f32[128,128]{1,0:T(8,128)S(1)}, f32[128,128]{1,0:T(8,128)S(1)}, u32[]{:S(2)}, u32[]{:S(2)}) collective-permute-start(f32[128,128]{1,0:T(8,128)S(1)} %get-tuple-element.143), channel_id=1, source_target_pairs={{0,4},{4,0},{8,12},{12,8},{1,5},{5,1},{9,13},{13,9},{2,6},{6,2},{1... | collective-permute-start | bytes 196616 | tf_op jit(solution)/shard_map/ppermute | solution.py:329

commit v15 on v7

--- a/solution.py
+++ b/solution.py
@@ -375,9 +375,9 @@
     listed = n * cap
     padded = -(-listed // 128) * 128
     size = interface_size
-    coarse_order, part_order = far_first(wide), far_first(narrow)
+    coarse_order, part_order = half_first(wide, True), far_first(narrow)
     half, half_back, middle = half_first(wide, False), half_first(wide, True), middle_first(wide)
-    orders = ((half_back, half, middle), (half_back, half, half_back))
+    orders = ((middle, half, half_back), (half_back, half, half_back))
     sent = [shape(cap, loads)] * n
     full = 2 * order * loads
 

time: 90.5 us -> 89.7 us (level)
  starting transfers between devices: 39.3 us -> 36.6 us
  waiting for transfers between devices: 30.2 us -> 32 us
    ppermute x30, starting transfers between devices: 39.3 us -> 36.6 us  [swap(): return lax.ppermute(block, axis, [(i, i ^ d) for i in range(count)])]
    ppermute x30, waiting for transfers between devices: 30.2 us -> 32 us  [swap(): return lax.ppermute(block, axis, [(i, i ^ d) for i in range(count)])]
  transfers between devices with their start and end apart: 30 -> 30, of which waited for: 24 -> 26; matrix products, arithmetic and copies ran while one was open for 0% -> 0% of each run, Pallas kernels for 13% -> 13%
where the time goes in v15:
time: 89.7 us; the launch traced here: 89.6 us
  starting transfers between devices  36.6 us (41%)
  waiting for transfers between devices  32 us (36%)
  Pallas kernels  19.3 us (22%)
  between operations  1.58 us (2%)
    ppermute x30, starting transfers between devices, swap(): return lax.ppermute(block, axis, [(i, i ^ d) for i in range(count)])  36.6 us
    ppermute x30, waiting for transfers between devices, swap(): return lax.ppermute(block, axis, [(i, i ^ d) for i in range(count)])  32 us
    pallas_call x25, Pallas kernels, call(): pl.pallas_call(body, out_shape=outs, grid=grid, in_specs=in_specs, out_sp...  19.3 us
  transfers between devices with their start and end apart: 30, of which 26 were waited for; matrix products, arithmetic and copies ran while one was open for 0% of the time, Pallas kernels for 13%

profile of v15, /device:TPU:0, one launch (start us, length us, event | category | flops | bytes accessed | tf_op | source)
XLA Modules:
  0.0 89.6 jit_solution(4019738332379001946)
XLA Ops:
  0.7 2.1 %first.1 = (bf16[256,256]{1,0:T(8,128)(2,1)S(1)}, bf16[256,768]{1,0:T(8,128)(2,1)S(1)}, bf16[256,384]{1,0:T(8,128)(2,1)S(1)}, bf16[256,1024]{1,0:T(8,128)(2,1)S(...) custom-call(s32[1,256]{1,0:T(1,128)} %bitcast.32, ...), custom_call_target="tpu_custom_call" | custom-call | flops 201326592 | bytes 2097152 | tf_op jit(solution)/shard_map/first/pallas_call | solution.py:49
  2.8 5.1 %collective-permute-start = (f32[264,128]{1,0:T(8,128)S(1)}, f32[264,128]{1,0:T(8,128)S(1)}, u32[]{:S(2)}, u32[]{:S(2)}) collective-permute-start(f32[264,128]{1,0:T(8,128)S(1)} %get-tuple-element.81), channel_id=1, source_target_pairs={{0,12},{4,8},{8,4},{12,0},{1,13},{5,9},{9,5},{13,1},{2,14},{6,10},... | collective-permute-start | bytes 405512 | tf_op jit(solution)/shard_map/ppermute | solution.py:326
  7.9 0.6 collective-permute-start.2
  9.4 2.0 %rest_start.1 = (f32[768,128]{1,0:T(8,128)S(1)}, f32[64,128]{1,0:T(8,128)S(1)}, bf16[768,1024]{1,0:T(8,128)(2,1)S(1)}, bf16[768,1024]{1,0:T(8,128)(2,1)S(1)}) custom-call(s32[1]{0:T(128)S(6)} %copy.15.size, f32[1024,1024]{1,0:T(8,128)S(1)} %bitcast.20, f32[1024,128]{1,0:T(8,128)S(1)} %bitcast.22, f32[1024,128]{1,0:T(8,128)S(1)} %bitcast.23, ...), custom_call_target="tpu_custom_call" | custom-call | flops 603979776 | bytes 6291456 | tf_op jit(solution)/shard_map/rest_start/pallas_call | solution.py:49
  11.4 0.9 collective-permute-done.refs_0_
  12.3 3.1 %collective-permute-done.1.refs_1_ = f32[264,128]{1,0:T(8,128)S(1)} collective-permute-done((f32[264,128]{1,0:T(8,128)S(1)}, f32[264,128]{1,0:T(8,128)S(1)}, u32[]{:S(2)}, u32[]{:S(2)}) %collective-permute-start.1) | collective-permute-done | bytes 135200 | tf_op jit(solution)/shard_map/ppermute | solution.py:326
  15.4 3.9 %collective-permute-done.2.refs_2_ = f32[264,128]{1,0:T(8,128)S(1)} collective-permute-done((f32[264,128]{1,0:T(8,128)S(1)}, f32[264,128]{1,0:T(8,128)S(1)}, u32[]{:S(2)}, u32[]{:S(2)}) %collective-permute-start.2) | collective-permute-done | bytes 135200 | tf_op jit(solution)/shard_map/ppermute | solution.py:326
  19.3 0.4 coarse.2
  19.7 0.8 collective-permute-start.3
  20.6 1.8 %collective-permute-start.4 = (f32[64,128]{1,0:T(8,128)S(1)}, f32[64,128]{1,0:T(8,128)S(1)}, u32[]{:S(2)}, u32[]{:S(2)}) collective-permute-start(f32[64,128]{1,0:T(8,128)S(1)} %get-tuple-element.90), channel_id=1, source_target_pairs={{0,12},{4,8},{8,4},{12,0},{1,13},{5,9},{9,5},{13,1},{2,14},{6,10},... | collective-permute-start | bytes 98312 | tf_op jit(solution)/shard_map/ppermute | solution.py:326
  22.4 0.9 %collective-permute-start.5 = (f32[64,128]{1,0:T(8,128)S(1)}, f32[64,128]{1,0:T(8,128)S(1)}, u32[]{:S(2)}, u32[]{:S(2)}) collective-permute-start(f32[64,128]{1,0:T(8,128)S(1)} %get-tuple-element.91), channel_id=1, source_target_pairs={{0,4},{4,0},{8,12},{12,8},{1,5},{5,1},{9,13},{13,9},{2,6},{6,2},{1... | collective-permute-start | bytes 98312 | tf_op jit(solution)/shard_map/ppermute | solution.py:326
  23.3 0.4 prepare.1
  23.7 1.1 %collective-permute-done.3.refs_1_ = f32[64,128]{1,0:T(8,128)S(1)} collective-permute-done((f32[64,128]{1,0:T(8,128)S(1)}, f32[64,128]{1,0:T(8,128)S(1)}, u32[]{:S(2)}, u32[]{:S(2)}) %collective-permute-start.3) | collective-permute-done | bytes 32800 | tf_op jit(solution)/shard_map/ppermute | solution.py:326
  24.8 1.7 %collective-permute-done.4.refs_2_ = f32[64,128]{1,0:T(8,128)S(1)} collective-permute-done((f32[64,128]{1,0:T(8,128)S(1)}, f32[64,128]{1,0:T(8,128)S(1)}, u32[]{:S(2)}, u32[]{:S(2)}) %collective-permute-start.4) | collective-permute-done | bytes 32800 | tf_op jit(solution)/shard_map/ppermute | solution.py:326
  27.0 1.6 %collective-permute-start.7 = (f32[64,128]{1,0:T(8,128)S(1)}, f32[64,128]{1,0:T(8,128)S(1)}, u32[]{:S(2)}, u32[]{:S(2)}) collective-permute-start(f32[64,128]{1,0:T(8,128)S(1)} %get-tuple-element.94), channel_id=1, source_target_pairs={{0,2},{1,3},{2,0},{3,1},{4,6},{5,7},{6,4},{7,5},{8,10},{9,11},{10,... | collective-permute-start | bytes 98312 | tf_op jit(solution)/shard_map/ppermute | solution.py:326
  29.1 1.5 %collective-permute-done.6.refs_1_ = f32[64,128]{1,0:T(8,128)S(1)} collective-permute-done((f32[64,128]{1,0:T(8,128)S(1)}, f32[64,128]{1,0:T(8,128)S(1)}, u32[]{:S(2)}, u32[]{:S(2)}) %collective-permute-start.6) | collective-permute-done | bytes 32800 | tf_op jit(solution)/shard_map/ppermute | solution.py:326
  30.6 0.4 collective-permute-done.7.refs_2_
  31.0 1.0 %lift.2 = (f32[256,128]{1,0:T(8,128)S(1)}, f32[768,128]{1,0:T(8,128)S(1)}, f32[256,128]{1,0:T(8,128)S(1)}, f32[128,128]{1,0:T(8,128)S(1)}, f32[128,128]{1,0:T(8,128)S(1)}, /*index=5*/f32[128,128]{1,0:T(8,128)S(1)}) custom-call(s32[1]{0:T(128)S(6)} %copy.15.size, f32[64,128]{1,0:T(8,128)S(1)} %get-tuple-element.92.refs_0_, ...), custom_call_target="tpu_custom_call" | custom-call | flops 201326592 | bytes 1048576 | tf_op jit(solution)/shard_map/lift/pallas_call | solution.py:49
  32.0 1.7 %collective-permute-start.9 = (f32[128,128]{1,0:T(8,128)S(1)}, f32[128,128]{1,0:T(8,128)S(1)}, u32[]{:S(2)}, u32[]{:S(2)}) collective-permute-start(f32[128,128]{1,0:T(8,128)S(1)} %get-tuple-element.103), channel_id=1, source_target_pairs={{0,8},{4,12},{8,0},{12,4},{1,9},{5,13},{9,1},{13,5},{2,10},{6,14},... | collective-permute-start | bytes 196616 | tf_op jit(solution)/shard_map/ppermute | solution.py:326
  33.7 0.8 collective-permute-start.10
  34.4 2.0 %collective-permute-start.11 = (f32[128,128]{1,0:T(8,128)S(1)}, f32[128,128]{1,0:T(8,128)S(1)}, u32[]{:S(2)}, u32[]{:S(2)}) collective-permute-start(f32[128,128]{1,0:T(8,128)S(1)} %get-tuple-element.105), channel_id=1, source_target_pairs={{0,12},{4,8},{8,4},{12,0},{1,13},{5,9},{9,5},{13,1},{2,14},{6,10},... | collective-permute-start | bytes 196616 | tf_op jit(solution)/shard_map/ppermute | solution.py:326
  36.6 1.5 %rest.3 = (f32[768,128]{1,0:T(8,128)S(1)}, f32[640,128]{1,0:T(8,128)S(1)}) custom-call(s32[1]{0:T(128)S(6)} %copy.15.size, bf16[768,1024]{1,0:T(8,128)(2,1)S(1)} %get-tuple-element.111.high, bf16[768,1024]{1,0:T(8,128)(2,1)S(1)} %get-tuple-element.112.low, f32[256,128]{1,0:T(8,128)S(1)} %get-tuple-element.108.mult_s.refs_5_, ...), custom_call_target="tpu_custom_call" | custom-call | flops 805306368 | bytes 4194304 | tf_op jit(solution)/shard_map/rest/pallas_call | solution.py:49
  38.1 1.4 %collective-permute-done.9.refs_0_ = f32[128,128]{1,0:T(8,128)S(1)} collective-permute-done((f32[128,128]{1,0:T(8,128)S(1)}, f32[128,128]{1,0:T(8,128)S(1)}, u32[]{:S(2)}, u32[]{:S(2)}) %collective-permute-start.9) | collective-permute-done | bytes 65568 | tf_op jit(solution)/shard_map/ppermute | solution.py:326
  39.6 0.6 collective-permute-done.10.refs_1_
  40.1 0.4 collective-permute-done.11.refs_2_
  40.6 0.5 sweep.3
  41.1 1.9 %collective-permute-start.12 = (f32[128,128]{1,0:T(8,128)S(1)}, f32[128,128]{1,0:T(8,128)S(1)}, u32[]{:S(2)}, u32[]{:S(2)}) collective-permute-start(f32[128,128]{1,0:T(8,128)S(1)} %get-tuple-element.115), channel_id=1, source_target_pairs={{0,8},{4,12},{8,0},{12,4},{1,9},{5,13},{9,1},{13,5},{2,10},{6,14},... | collective-permute-start | bytes 196616 | tf_op jit(solution)/shard_map/ppermute | solution.py:326
  43.0 2.0 %collective-permute-start.13 = (f32[128,128]{1,0:T(8,128)S(1)}, f32[128,128]{1,0:T(8,128)S(1)}, u32[]{:S(2)}, u32[]{:S(2)}) collective-permute-start(f32[128,128]{1,0:T(8,128)S(1)} %get-tuple-element.116), channel_id=1, source_target_pairs={{0,12},{4,8},{8,4},{12,0},{1,13},{5,9},{9,5},{13,1},{2,14},{6,10},... | collective-permute-start | bytes 196616 | tf_op jit(solution)/shard_map/ppermute | solution.py:326
  45.2 1.5 %rest.4 = (f32[768,128]{1,0:T(8,128)S(1)}, f32[640,128]{1,0:T(8,128)S(1)}) custom-call(s32[1]{0:T(128)S(6)} %copy.15.size, bf16[768,1024]{1,0:T(8,128)(2,1)S(1)} %get-tuple-element.111.high, bf16[768,1024]{1,0:T(8,128)(2,1)S(1)} %get-tuple-element.112.low, f32[256,128]{1,0:T(8,128)S(1)} %get-tuple-element.119.mult_s.refs_5_, ...), custom_call_target="tpu_custom_call" | custom-call | flops 805306368 | bytes 4194304 | tf_op jit(solution)/shard_map/rest/pallas_call | solution.py:49
  46.7 1.9 %collective-permute-done.12.refs_0_ = f32[128,128]{1,0:T(8,128)S(1)} collective-permute-done((f32[128,128]{1,0:T(8,128)S(1)}, f32[128,128]{1,0:T(8,128)S(1)}, u32[]{:S(2)}, u32[]{:S(2)}) %collective-permute-start.12) | collective-permute-done | bytes 65568 | tf_op jit(solution)/shard_map/ppermute | solution.py:326
  48.6 0.9 collective-permute-done.13.refs_1_
  49.5 0.6 collective-permute-done.14.refs_2_
  50.2 0.5 sweep.4
  50.7 0.8 collective-permute-start.15
  51.5 1.9 %collective-permute-start.16 = (f32[128,128]{1,0:T(8,128)S(1)}, f32[128,128]{1,0:T(8,128)S(1)}, u32[]{:S(2)}, u32[]{:S(2)}) collective-permute-start(f32[128,128]{1,0:T(8,128)S(1)} %get-tuple-element.123), channel_id=1, source_target_pairs={{0,12},{4,8},{8,4},{12,0},{1,13},{5,9},{9,5},{13,1},{2,14},{6,10},... | collective-permute-start | bytes 196616 | tf_op jit(solution)/shard_map/ppermute | solution.py:326
  53.4 0.8 collective-permute-start.17
  54.4 1.1 %rest_first.1 = (f32[768,128]{1,0:T(8,128)S(1)}, f32[64,128]{1,0:T(8,128)S(1)}) custom-call(s32[1]{0:T(128)S(6)} %copy.15.size, bf16[768,1024]{1,0:T(8,128)(2,1)S(1)} %get-tuple-element.111.high, bf16[768,1024]{1,0:T(8,128)(2,1)S(1)} %get-tuple-element.112.low, f32[256,128]{1,0:T(8,128)S(1)} %get-tuple-element.126.mult_s.refs_5_, ...), custom_call_target="tpu_custom_call" | custom-call | flops 603979776 | bytes 3145728 | tf_op jit(solution)/shard_map/rest_first/pallas_call | solution.py:49
  55.6 2.4 %collective-permute-done.15.refs_0_ = f32[128,128]{1,0:T(8,128)S(1)} collective-permute-done((f32[128,128]{1,0:T(8,128)S(1)}, f32[128,128]{1,0:T(8,128)S(1)}, u32[]{:S(2)}, u32[]{:S(2)}) %collective-permute-start.15) | collective-permute-done | bytes 65568 | tf_op jit(solution)/shard_map/ppermute | solution.py:326
  58.0 0.6 collective-permute-done.17.refs_2_
  58.7 0.4 coarse.3
  59.1 0.4 collective-permute-start.18
  59.5 2.6 %collective-permute-start.19 = (f32[64,128]{1,0:T(8,128)S(1)}, f32[64,128]{1,0:T(8,128)S(1)}, u32[]{:S(2)}, u32[]{:S(2)}) collective-permute-start(f32[64,128]{1,0:T(8,128)S(1)} %get-tuple-element.131), channel_id=1, source_target_pairs={{0,12},{4,8},{8,4},{12,0},{1,13},{5,9},{9,5},{13,1},{2,14},{6,10},... | collective-permute-start | bytes 98312 | tf_op jit(solution)/shard_map/ppermute | solution.py:326
  62.1 0.6 collective-permute-start.20
  62.7 1.7 %collective-permute-done.18.refs_1_ = f32[64,128]{1,0:T(8,128)S(1)} collective-permute-done((f32[64,128]{1,0:T(8,128)S(1)}, f32[64,128]{1,0:T(8,128)S(1)}, u32[]{:S(2)}, u32[]{:S(2)}) %collective-permute-start.18) | collective-permute-done | bytes 32800 | tf_op jit(solution)/shard_map/ppermute | solution.py:326
  64.4 0.9 collective-permute-done.19.refs_2_
  65.2 0.8 collective-permute-done.20.refs_3_
  66.7 1.5 %collective-permute-start.23 = (f32[64,128]{1,0:T(8,128)S(1)}, f32[64,128]{1,0:T(8,128)S(1)}, u32[]{:S(2)}, u32[]{:S(2)}) collective-permute-start(f32[64,128]{1,0:T(8,128)S(1)} %get-tuple-element.136), channel_id=1, source_target_pairs={{0,1},{1,0},{2,3},{3,2},{4,5},{5,4},{6,7},{7,6},{8,9},{9,8},{10,11... | collective-permute-start | bytes 98312 | tf_op jit(solution)/shard_map/ppermute | solution.py:326
  68.2 1.5 %collective-permute-done.21.refs_1_ = f32[64,128]{1,0:T(8,128)S(1)} collective-permute-done((f32[64,128]{1,0:T(8,128)S(1)}, f32[64,128]{1,0:T(8,128)S(1)}, u32[]{:S(2)}, u32[]{:S(2)}) %collective-permute-start.21) | collective-permute-done | bytes 32800 | tf_op jit(solution)/shard_map/ppermute | solution.py:326
  69.7 0.7 collective-permute-done.22.refs_2_
  70.4 1.0 %lift.3 = (f32[256,128]{1,0:T(8,128)S(1)}, f32[768,128]{1,0:T(8,128)S(1)}, f32[256,128]{1,0:T(8,128)S(1)}, f32[128,128]{1,0:T(8,128)S(1)}, f32[128,128]{1,0:T(8,128)S(1)}, /*index=5*/f32[128,128]{1,0:T(8,128)S(1)}) custom-call(s32[1]{0:T(128)S(6)} %copy.15.size, f32[64,128]{1,0:T(8,128)S(1)} %get-tuple-element.133.refs_0_, ...), custom_call_target="tpu_custom_call" | custom-call | flops 201326592 | bytes 1048576 | tf_op jit(solution)/shard_map/lift/pallas_call | solution.py:49
  71.4 0.8 collective-permute-start.24
  72.2 1.6 %collective-permute-start.25 = (f32[128,128]{1,0:T(8,128)S(1)}, f32[128,128]{1,0:T(8,128)S(1)}, u32[]{:S(2)}, u32[]{:S(2)}) collective-permute-start(f32[128,128]{1,0:T(8,128)S(1)} %get-tuple-element.140), channel_id=1, source_target_pairs={{0,4},{4,0},{8,12},{12,8},{1,5},{5,1},{9,13},{13,9},{2,6},{6,2},{1... | collective-permute-start | bytes 196616 | tf_op jit(solution)/shard_map/ppermute | solution.py:326
  73.8 2.0 %collective-permute-start.26 = (f32[128,128]{1,0:T(8,128)S(1)}, f32[128,128]{1,0:T(8,128)S(1)}, u32[]{:S(2)}, u32[]{:S(2)}) collective-permute-start(f32[128,128]{1,0:T(8,128)S(1)} %get-tuple-element.141), channel_id=1, source_target_pairs={{0,12},{4,8},{8,4},{12,0},{1,13},{5,9},{9,5},{13,1},{2,14},{6,10},... | collective-permute-start | bytes 196616 | tf_op jit(solution)/shard_map/ppermute | solution.py:326
  76.1 1.5 %rest.5 = (f32[768,128]{1,0:T(8,128)S(1)}, f32[640,128]{1,0:T(8,128)S(1)}) custom-call(s32[1]{0:T(128)S(6)} %copy.15.size, bf16[768,1024]{1,0:T(8,128)(2,1)S(1)} %get-tuple-element.111.high, bf16[768,1024]{1,0:T(8,128)(2,1)S(1)} %get-tuple-element.112.low, f32[256,128]{1,0:T(8,128)S(1)} %get-tuple-element.143.mult_s.refs_5_, ...), custom_call_target="tpu_custom_call" | custom-call | flops 805306368 | bytes 4194304 | tf_op jit(solution)/shard_map/rest/pallas_call | solution.py:49
  77.5 1.0 %collective-permute-done.24.refs_0_ = f32[128,128]{1,0:T(8,128)S(1)} collective-permute-done((f32[128,128]{1,0:T(8,128)S(1)}, f32[128,128]{1,0:T(8,128)S(1)}, u32[]{:S(2)}, u32[]{:S(2)}) %collective-permute-start.24) | collective-permute-done | bytes 65568 | tf_op jit(solution)/shard_map/ppermute | solution.py:326
  78.6 1.4 %collective-permute-done.26.refs_2_ = f32[128,128]{1,0:T(8,128)S(1)} collective-permute-done((f32[128,128]{1,0:T(8,128)S(1)}, f32[128,128]{1,0:T(8,128)S(1)}, u32[]{:S(2)}, u32[]{:S(2)}) %collective-permute-start.26) | collective-permute-done | bytes 65568 | tf_op jit(solution)/shard_map/ppermute | solution.py:326
  80.0 0.5 sweep.5
  80.5 1.3 %collective-permute-start.27 = (f32[128,128]{1,0:T(8,128)S(1)}, f32[128,128]{1,0:T(8,128)S(1)}, u32[]{:S(2)}, u32[]{:S(2)}) collective-permute-start(f32[128,128]{1,0:T(8,128)S(1)} %get-tuple-element.146), channel_id=1, source_target_pairs={{0,8},{4,12},{8,0},{12,4},{1,9},{5,13},{9,1},{13,5},{2,10},{6,14},... | collective-permute-start | bytes 196616 | tf_op jit(solution)/shard_map/ppermute | solution.py:326
  81.8 2.1 %collective-permute-start.28 = (f32[128,128]{1,0:T(8,128)S(1)}, f32[128,128]{1,0:T(8,128)S(1)}, u32[]{:S(2)}, u32[]{:S(2)}) collective-permute-start(f32[128,128]{1,0:T(8,128)S(1)} %get-tuple-element.147), channel_id=1, source_target_pairs={{0,12},{4,8},{8,4},{12,0},{1,13},{5,9},{9,5},{13,1},{2,14},{6,10},... | collective-permute-start | bytes 196616 | tf_op jit(solution)/shard_map/ppermute | solution.py:326
  84.2 1.9 %rest_last.1 = (f32[1024,128]{1,0:T(8,128)}, f32[1024,128]{1,0:T(8,128)}) custom-call(s32[1]{0:T(128)S(6)} %copy.15.size, bf16[768,1024]{1,0:T(8,128)(2,1)S(1)} %get-tuple-element.111.high, bf16[768,1024]{1,0:T(8,128)(2,1)S(1)} %get-tuple-element.112.low, f32[256,128]{1,0:T(8,128)S(1)} %get-tuple-element.150.mult_s.refs_5_, ...), custom_call_target="tpu_custom_call" | custom-call | flops 603979776 | bytes 3145728 | tf_op jit(solution)/shard_map/rest_last/pallas_call | solution.py:49
  86.1 1.0 %collective-permute-done.27.refs_0_ = f32[128,128]{1,0:T(8,128)S(1)} collective-permute-done((f32[128,128]{1,0:T(8,128)S(1)}, f32[128,128]{1,0:T(8,128)S(1)}, u32[]{:S(2)}, u32[]{:S(2)}) %collective-permute-start.27) | collective-permute-done | bytes 65568 | tf_op jit(solution)/shard_map/ppermute | solution.py:326
  87.1 0.9 collective-permute-done.28.refs_1_
  88.0 0.7 collective-permute-done.29.refs_2_
  88.6 0.9 %last.1 = (f32[1024,128]{1,0:T(8,128)}, f32[1024,128]{1,0:T(8,128)}) custom-call(s32[1]{0:T(128)S(6)} %copy.15.size, f32[128,128]{1,0:T(8,128)S(1)} %collective-permute-done.27.refs_0_, f32[128,128]{1,0:T(8,128)S(1)} %collective-permute-done.28.refs_1_, ...), custom_call_target="tpu_custom_call", output_to_operand_aliasing={{0}: (8, {}), {1}: (9, {})} | custom-call | flops 75497472 | bytes 196608 | tf_op jit(solution)/shard_map/last/pallas_call | solution.py:49
  (33 shorter events, 3.0 us)
Async XLA Ops:
  0.6 8.5 %copy-start = (f32[1,1024,128]{2,1,0:T(8,128)S(1)}, f32[1,1024,128]{2,1,0:T(8,128)}, u32[]{:S(2)}) copy-start(f32[1,1024,128]{2,1,0:T(8,128)} %param.12) | copy-start | bytes 1572868
  0.6 8.7 %copy-start.1 = (f32[1,1024,1024]{2,1,0:T(8,128)S(1)}, f32[1,1024,1024]{2,1,0:T(8,128)}, u32[]{:S(2)}) copy-start(f32[1,1024,1024]{2,1,0:T(8,128)} %param.9) | copy-start | bytes 12582916
  0.7 8.7 %copy-start.2 = (f32[1,1024,128]{2,1,0:T(8,128)S(1)}, f32[1,1024,128]{2,1,0:T(8,128)}, u32[]{:S(2)}) copy-start(f32[1,1024,128]{2,1,0:T(8,128)} %param.13) | copy-start | bytes 1572868
  0.7 8.7 %copy-start.3 = (f32[1,64,1024]{2,1,0:T(8,128)S(1)}, f32[1,64,1024]{2,1,0:T(8,128)}, u32[]{:S(2)}) copy-start(f32[1,64,1024]{2,1,0:T(8,128)} %param.11) | copy-start | bytes 786436
  2.8 9.6 %collective-permute-start = (f32[264,128]{1,0:T(8,128)S(1)}, f32[264,128]{1,0:T(8,128)S(1)}, u32[]{:S(2)}, u32[]{:S(2)}) collective-permute-start(f32[264,128]{1,0:T(8,128)S(1)} %get-tuple-element.81), channel_id=1, source_target_pairs={{0,12},{4,8},{8,4},{12,0},{1,13},{5,9},{9,5},{13,1},{2,14},{6,10},... | collective-permute-start | bytes 405512 | tf_op jit(solution)/shard_map/ppermute | solution.py:326
  7.9 7.6 %collective-permute-start.1 = (f32[264,128]{1,0:T(8,128)S(1)}, f32[264,128]{1,0:T(8,128)S(1)}, u32[]{:S(2)}, u32[]{:S(2)}) collective-permute-start(f32[264,128]{1,0:T(8,128)S(1)} %get-tuple-element.82), channel_id=1, source_target_pairs={{0,4},{4,0},{8,12},{12,8},{1,5},{5,1},{9,13},{13,9},{2,6},{6,2},{1... | collective-permute-start | bytes 405512 | tf_op jit(solution)/shard_map/ppermute | solution.py:326
  7.9 11.4 %collective-permute-start.2 = (f32[264,128]{1,0:T(8,128)S(1)}, f32[264,128]{1,0:T(8,128)S(1)}, u32[]{:S(2)}, u32[]{:S(2)}) collective-permute-start(f32[264,128]{1,0:T(8,128)S(1)} %get-tuple-element.83), channel_id=1, source_target_pairs={{0,8},{4,12},{8,0},{12,4},{1,9},{5,13},{9,1},{13,5},{2,10},{6,14},... | collective-permute-start | bytes 405512 | tf_op jit(solution)/shard_map/ppermute | solution.py:326
  11.4 11.9 %copy-start.4 = (f32[256,256]{1,0:T(8,128)S(1)}, f32[256,256]{1,0:T(8,128)}, u32[]{:S(2)}) copy-start(f32[256,256]{1,0:T(8,128)} %tile.3) | copy-start | bytes 786436
  11.4 11.9 %copy-start.5 = (s32[1,1024]{1,0:T(1,128)S(1)}, s32[1,1024]{1,0:T(1,128)}, u32[]{:S(2)}) copy-start(s32[1,1024]{1,0:T(1,128)} %contact.1) | copy-start | bytes 12292
  19.7 5.0 %collective-permute-start.3 = (f32[64,128]{1,0:T(8,128)S(1)}, f32[64,128]{1,0:T(8,128)S(1)}, u32[]{:S(2)}, u32[]{:S(2)}) collective-permute-start(f32[64,128]{1,0:T(8,128)S(1)} %get-tuple-element.89), channel_id=1, source_target_pairs={{0,8},{4,12},{8,0},{12,4},{1,9},{5,13},{9,1},{13,5},{2,10},{6,14},... | collective-permute-start | bytes 98312 | tf_op jit(solution)/shard_map/ppermute | solution.py:326
  20.6 5.9 %collective-permute-start.4 = (f32[64,128]{1,0:T(8,128)S(1)}, f32[64,128]{1,0:T(8,128)S(1)}, u32[]{:S(2)}, u32[]{:S(2)}) collective-permute-start(f32[64,128]{1,0:T(8,128)S(1)} %get-tuple-element.90), channel_id=1, source_target_pairs={{0,12},{4,8},{8,4},{12,0},{1,13},{5,9},{9,5},{13,1},{2,14},{6,10},... | collective-permute-start | bytes 98312 | tf_op jit(solution)/shard_map/ppermute | solution.py:326
  22.4 4.3 %collective-permute-start.5 = (f32[64,128]{1,0:T(8,128)S(1)}, f32[64,128]{1,0:T(8,128)S(1)}, u32[]{:S(2)}, u32[]{:S(2)}) collective-permute-start(f32[64,128]{1,0:T(8,128)S(1)} %get-tuple-element.91), channel_id=1, source_target_pairs={{0,4},{4,0},{8,12},{12,8},{1,5},{5,1},{9,13},{13,9},{2,6},{6,2},{1... | collective-permute-start | bytes 98312 | tf_op jit(solution)/shard_map/ppermute | solution.py:326
  26.9 3.7 %collective-permute-start.6 = (f32[64,128]{1,0:T(8,128)S(1)}, f32[64,128]{1,0:T(8,128)S(1)}, u32[]{:S(2)}, u32[]{:S(2)}) collective-permute-start(f32[64,128]{1,0:T(8,128)S(1)} %get-tuple-element.93), channel_id=1, source_target_pairs={{0,3},{1,2},{2,1},{3,0},{4,7},{5,6},{6,5},{7,4},{8,11},{9,10},{10,... | collective-permute-start | bytes 98312 | tf_op jit(solution)/shard_map/ppermute | solution.py:326
  27.0 4.0 %collective-permute-start.7 = (f32[64,128]{1,0:T(8,128)S(1)}, f32[64,128]{1,0:T(8,128)S(1)}, u32[]{:S(2)}, u32[]{:S(2)}) collective-permute-start(f32[64,128]{1,0:T(8,128)S(1)} %get-tuple-element.94), channel_id=1, source_target_pairs={{0,2},{1,3},{2,0},{3,1},{4,6},{5,7},{6,4},{7,5},{8,10},{9,11},{10,... | collective-permute-start | bytes 98312 | tf_op jit(solution)/shard_map/ppermute | solution.py:326
  28.5 2.5 %collective-permute-start.8 = (f32[64,128]{1,0:T(8,128)S(1)}, f32[64,128]{1,0:T(8,128)S(1)}, u32[]{:S(2)}, u32[]{:S(2)}) collective-permute-start(f32[64,128]{1,0:T(8,128)S(1)} %get-tuple-element.95), channel_id=1, source_target_pairs={{0,1},{1,0},{2,3},{3,2},{4,5},{5,4},{6,7},{7,6},{8,9},{9,8},{10,11... | collective-permute-start | bytes 98312 | tf_op jit(solution)/shard_map/ppermute | solution.py:326
  32.0 7.6 %collective-permute-start.9 = (f32[128,128]{1,0:T(8,128)S(1)}, f32[128,128]{1,0:T(8,128)S(1)}, u32[]{:S(2)}, u32[]{:S(2)}) collective-permute-start(f32[128,128]{1,0:T(8,128)S(1)} %get-tuple-element.103), channel_id=1, source_target_pairs={{0,8},{4,12},{8,0},{12,4},{1,9},{5,13},{9,1},{13,5},{2,10},{6,14},... | collective-permute-start | bytes 196616 | tf_op jit(solution)/shard_map/ppermute | solution.py:326
  33.7 6.5 %collective-permute-start.10 = (f32[128,128]{1,0:T(8,128)S(1)}, f32[128,128]{1,0:T(8,128)S(1)}, u32[]{:S(2)}, u32[]{:S(2)}) collective-permute-start(f32[128,128]{1,0:T(8,128)S(1)} %get-tuple-element.104), channel_id=1, source_target_pairs={{0,4},{4,0},{8,12},{12,8},{1,5},{5,1},{9,13},{13,9},{2,6},{6,2},{1... | collective-permute-start | bytes 196616 | tf_op jit(solution)/shard_map/ppermute | solution.py:326
  34.4 6.1 %collective-permute-start.11 = (f32[128,128]{1,0:T(8,128)S(1)}, f32[128,128]{1,0:T(8,128)S(1)}, u32[]{:S(2)}, u32[]{:S(2)}) collective-permute-start(f32[128,128]{1,0:T(8,128)S(1)} %get-tuple-element.105), channel_id=1, source_target_pairs={{0,12},{4,8},{8,4},{12,0},{1,13},{5,9},{9,5},{13,1},{2,14},{6,10},... | collective-permute-start | bytes 196616 | tf_op jit(solution)/shard_map/ppermute | solution.py:326
  41.1 7.5 %collective-permute-start.12 = (f32[128,128]{1,0:T(8,128)S(1)}, f32[128,128]{1,0:T(8,128)S(1)}, u32[]{:S(2)}, u32[]{:S(2)}) collective-permute-start(f32[128,128]{1,0:T(8,128)S(1)} %get-tuple-element.115), channel_id=1, source_target_pairs={{0,8},{4,12},{8,0},{12,4},{1,9},{5,13},{9,1},{13,5},{2,10},{6,14},... | collective-permute-start | bytes 196616 | tf_op jit(solution)/shard_map/ppermute | solution.py:326
  43.0 6.5 %collective-permute-start.13 = (f32[128,128]{1,0:T(8,128)S(1)}, f32[128,128]{1,0:T(8,128)S(1)}, u32[]{:S(2)}, u32[]{:S(2)}) collective-permute-start(f32[128,128]{1,0:T(8,128)S(1)} %get-tuple-element.116), channel_id=1, source_target_pairs={{0,12},{4,8},{8,4},{12,0},{1,13},{5,9},{9,5},{13,1},{2,14},{6,10},... | collective-permute-start | bytes 196616 | tf_op jit(solution)/shard_map/ppermute | solution.py:326
  45.0 5.1 %collective-permute-start.14 = (f32[128,128]{1,0:T(8,128)S(1)}, f32[128,128]{1,0:T(8,128)S(1)}, u32[]{:S(2)}, u32[]{:S(2)}) collective-permute-start(f32[128,128]{1,0:T(8,128)S(1)} %get-tuple-element.117), channel_id=1, source_target_pairs={{0,4},{4,0},{8,12},{12,8},{1,5},{5,1},{9,13},{13,9},{2,6},{6,2},{1... | collective-permute-start | bytes 196616 | tf_op jit(solution)/shard_map/ppermute | solution.py:326
  50.7 7.3 %collective-permute-start.15 = (f32[128,128]{1,0:T(8,128)S(1)}, f32[128,128]{1,0:T(8,128)S(1)}, u32[]{:S(2)}, u32[]{:S(2)}) collective-permute-start(f32[128,128]{1,0:T(8,128)S(1)} %get-tuple-element.122), channel_id=1, source_target_pairs={{0,8},{4,12},{8,0},{12,4},{1,9},{5,13},{9,1},{13,5},{2,10},{6,14},... | collective-permute-start | bytes 196616 | tf_op jit(solution)/shard_map/ppermute | solution.py:326
  51.5 6.6 %collective-permute-start.16 = (f32[128,128]{1,0:T(8,128)S(1)}, f32[128,128]{1,0:T(8,128)S(1)}, u32[]{:S(2)}, u32[]{:S(2)}) collective-permute-start(f32[128,128]{1,0:T(8,128)S(1)} %get-tuple-element.123), channel_id=1, source_target_pairs={{0,12},{4,8},{8,4},{12,0},{1,13},{5,9},{9,5},{13,1},{2,14},{6,10},... | collective-permute-start | bytes 196616 | tf_op jit(solution)/shard_map/ppermute | solution.py:326
  53.4 5.3 %collective-permute-start.17 = (f32[128,128]{1,0:T(8,128)S(1)}, f32[128,128]{1,0:T(8,128)S(1)}, u32[]{:S(2)}, u32[]{:S(2)}) collective-permute-start(f32[128,128]{1,0:T(8,128)S(1)} %get-tuple-element.124), channel_id=1, source_target_pairs={{0,4},{4,0},{8,12},{12,8},{1,5},{5,1},{9,13},{13,9},{2,6},{6,2},{1... | collective-permute-start | bytes 196616 | tf_op jit(solution)/shard_map/ppermute | solution.py:326
  59.1 5.2 %collective-permute-start.18 = (f32[64,128]{1,0:T(8,128)S(1)}, f32[64,128]{1,0:T(8,128)S(1)}, u32[]{:S(2)}, u32[]{:S(2)}) collective-permute-start(f32[64,128]{1,0:T(8,128)S(1)} %get-tuple-element.130), channel_id=1, source_target_pairs={{0,8},{4,12},{8,0},{12,4},{1,9},{5,13},{9,1},{13,5},{2,10},{6,14},... | collective-permute-start | bytes 98312 | tf_op jit(solution)/shard_map/ppermute | solution.py:326
  59.5 5.7 %collective-permute-start.19 = (f32[64,128]{1,0:T(8,128)S(1)}, f32[64,128]{1,0:T(8,128)S(1)}, u32[]{:S(2)}, u32[]{:S(2)}) collective-permute-start(f32[64,128]{1,0:T(8,128)S(1)} %get-tuple-element.131), channel_id=1, source_target_pairs={{0,12},{4,8},{8,4},{12,0},{1,13},{5,9},{9,5},{13,1},{2,14},{6,10},... | collective-permute-start | bytes 98312 | tf_op jit(solution)/shard_map/ppermute | solution.py:326
  62.1 3.9 %collective-permute-start.20 = (f32[64,128]{1,0:T(8,128)S(1)}, f32[64,128]{1,0:T(8,128)S(1)}, u32[]{:S(2)}, u32[]{:S(2)}) collective-permute-start(f32[64,128]{1,0:T(8,128)S(1)} %get-tuple-element.132), channel_id=1, source_target_pairs={{0,4},{4,0},{8,12},{12,8},{1,5},{5,1},{9,13},{13,9},{2,6},{6,2},{1... | collective-permute-start | bytes 98312 | tf_op jit(solution)/shard_map/ppermute | solution.py:326
  66.3 3.4 %collective-permute-start.21 = (f32[64,128]{1,0:T(8,128)S(1)}, f32[64,128]{1,0:T(8,128)S(1)}, u32[]{:S(2)}, u32[]{:S(2)}) collective-permute-start(f32[64,128]{1,0:T(8,128)S(1)} %get-tuple-element.134), channel_id=1, source_target_pairs={{0,3},{1,2},{2,1},{3,0},{4,7},{5,6},{6,5},{7,4},{8,11},{9,10},{10,... | collective-permute-start | bytes 98312 | tf_op jit(solution)/shard_map/ppermute | solution.py:326
  66.4 4.0 %collective-permute-start.22 = (f32[64,128]{1,0:T(8,128)S(1)}, f32[64,128]{1,0:T(8,128)S(1)}, u32[]{:S(2)}, u32[]{:S(2)}) collective-permute-start(f32[64,128]{1,0:T(8,128)S(1)} %get-tuple-element.135), channel_id=1, source_target_pairs={{0,2},{1,3},{2,0},{3,1},{4,6},{5,7},{6,4},{7,5},{8,10},{9,11},{10,... | collective-permute-start | bytes 98312 | tf_op jit(solution)/shard_map/ppermute | solution.py:326
  66.7 3.7 %collective-permute-start.23 = (f32[64,128]{1,0:T(8,128)S(1)}, f32[64,128]{1,0:T(8,128)S(1)}, u32[]{:S(2)}, u32[]{:S(2)}) collective-permute-start(f32[64,128]{1,0:T(8,128)S(1)} %get-tuple-element.136), channel_id=1, source_target_pairs={{0,1},{1,0},{2,3},{3,2},{4,5},{5,4},{6,7},{7,6},{8,9},{9,8},{10,11... | collective-permute-start | bytes 98312 | tf_op jit(solution)/shard_map/ppermute | solution.py:326
  71.4 7.2 %collective-permute-start.24 = (f32[128,128]{1,0:T(8,128)S(1)}, f32[128,128]{1,0:T(8,128)S(1)}, u32[]{:S(2)}, u32[]{:S(2)}) collective-permute-start(f32[128,128]{1,0:T(8,128)S(1)} %get-tuple-element.139), channel_id=1, source_target_pairs={{0,8},{4,12},{8,0},{12,4},{1,9},{5,13},{9,1},{13,5},{2,10},{6,14},... | collective-permute-start | bytes 196616 | tf_op jit(solution)/shard_map/ppermute | solution.py:326
  72.2 6.3 %collective-permute-start.25 = (f32[128,128]{1,0:T(8,128)S(1)}, f32[128,128]{1,0:T(8,128)S(1)}, u32[]{:S(2)}, u32[]{:S(2)}) collective-permute-start(f32[128,128]{1,0:T(8,128)S(1)} %get-tuple-element.140), channel_id=1, source_target_pairs={{0,4},{4,0},{8,12},{12,8},{1,5},{5,1},{9,13},{13,9},{2,6},{6,2},{1... | collective-permute-start | bytes 196616 | tf_op jit(solution)/shard_map/ppermute | solution.py:326
  73.8 6.1 %collective-permute-start.26 = (f32[128,128]{1,0:T(8,128)S(1)}, f32[128,128]{1,0:T(8,128)S(1)}, u32[]{:S(2)}, u32[]{:S(2)}) collective-permute-start(f32[128,128]{1,0:T(8,128)S(1)} %get-tuple-element.141), channel_id=1, source_target_pairs={{0,12},{4,8},{8,4},{12,0},{1,13},{5,9},{9,5},{13,1},{2,14},{6,10},... | collective-permute-start | bytes 196616 | tf_op jit(solution)/shard_map/ppermute | solution.py:326
  80.5 6.6 %collective-permute-start.27 = (f32[128,128]{1,0:T(8,128)S(1)}, f32[128,128]{1,0:T(8,128)S(1)}, u32[]{:S(2)}, u32[]{:S(2)}) collective-permute-start(f32[128,128]{1,0:T(8,128)S(1)} %get-tuple-element.146), channel_id=1, source_target_pairs={{0,8},{4,12},{8,0},{12,4},{1,9},{5,13},{9,1},{13,5},{2,10},{6,14},... | collective-permute-start | bytes 196616 | tf_op jit(solution)/shard_map/ppermute | solution.py:326
  81.8 6.1 %collective-permute-start.28 = (f32[128,128]{1,0:T(8,128)S(1)}, f32[128,128]{1,0:T(8,128)S(1)}, u32[]{:S(2)}, u32[]{:S(2)}) collective-permute-start(f32[128,128]{1,0:T(8,128)S(1)} %get-tuple-element.147), channel_id=1, source_target_pairs={{0,12},{4,8},{8,4},{12,0},{1,13},{5,9},{9,5},{13,1},{2,14},{6,10},... | collective-permute-start | bytes 196616 | tf_op jit(solution)/shard_map/ppermute | solution.py:326
  84.0 4.7 %collective-permute-start.29 = (f32[128,128]{1,0:T(8,128)S(1)}, f32[128,128]{1,0:T(8,128)S(1)}, u32[]{:S(2)}, u32[]{:S(2)}) collective-permute-start(f32[128,128]{1,0:T(8,128)S(1)} %get-tuple-element.148), channel_id=1, source_target_pairs={{0,4},{4,0},{8,12},{12,8},{1,5},{5,1},{9,13},{13,9},{2,6},{6,2},{1... | collective-permute-start | bytes 196616 | tf_op jit(solution)/shard_map/ppermute | solution.py:326

commit v16 on v15

--- a/solution.py
+++ b/solution.py
@@ -81,7 +81,7 @@
 
 def first_kernel(n, cap, peers_at, rows_at, operator_at, mult_at, *refs):
     unpack_own, unpack_all, unpack, high, low, image = refs[:6]
-    sends, (peers, rows, operator, mult, done) = refs[6:6 + n], refs[6 + n:]
+    message, peers, rows, operator, mult, done = refs[6:]
     shared, width = image.shape
     copies = [
         pltpu.make_async_copy(source, target, done.at[i])
@@ -111,26 +111,27 @@
     unpack_all[...] = marks(jnp.where(far == 0, -1, (far - 1) * shared + wanted), unpack_all.shape[1])
     unpack[...] = marks(jnp.where(far == 0, -1, (far - 1) * cap + slot), unpack.shape[1])
     lane = lax.broadcasted_iota(jnp.int32, (shared, width), 1)
-    for d, out in enumerate(sends, 1):
-        out[shared:, :] = jnp.zeros((out.shape[0] - shared, width), F32)
-        for c in range(-(-cap // width)):
-            hit = (far == d) & (slot == lane + c * width)
-            out[shared + c:shared + c + 1, :] = jnp.sum(
-                jnp.where(hit, wanted.astype(F32), 0.0), axis=0, keepdims=True
-            )
+    message[shared:, :] = jnp.zeros((message.shape[0] - shared, width), F32)
+    chunks = -(-cap // width)
+    for k in range(n * chunks):
+        d, c = k // chunks + 1, k % chunks
+        hit = (far == d) & (slot == lane + c * width)
+        message[shared + k:shared + k + 1, :] = jnp.sum(
+            jnp.where(hit, wanted.astype(F32), 0.0), axis=0, keepdims=True
+        )
     copies[2].wait()
     copies[3].wait()
     parts = split(operator[...])
     high[...], low[...] = parts
     value = product(parts, split(mult[...]))
     image[...] = value
-    for out in sends:
-        out[:shared, :] = value
-
-
-def pack_kernel(times, cap, *refs):
+    message[:shared, :] = value
+
+
+def pack_kernel(times, relayed, cap, *refs):
     n = len(times)
-    recvs, (high, low, pack, stack_high, stack_low) = refs[:n], refs[n:]
+    recvs, refs = refs[:n + relayed], refs[n + relayed:]
+    recvs, (high, low, pack, stack_high, stack_low) = merged(recvs, relayed), refs
     shared = pack.shape[1]
     width = recvs[0].shape[1]
     column = lax.broadcasted_iota(jnp.int32, (width, shared), 1).astype(F32)
@@ -138,7 +139,8 @@
         pack[n * cap:, :] = jnp.zeros((pack.shape[0] - n * cap, shared), BF16)
     for d, recv in zip(times, recvs):
         for c in range(-(-cap // width)):
-            wanted = jnp.broadcast_to(recv[shared + c:shared + c + 1, :], (shared, width)).T
+            k = shared + (d - 1) * -(-cap // width) + c
+            wanted = jnp.broadcast_to(recv[k:k + 1, :], (shared, width)).T
             chosen = jnp.where(wanted == column, 1.0, 0.0).astype(BF16)
             size = min(width, cap - c * width)
             at = (d - 1) * cap + c * width
@@ -165,17 +167,26 @@
         out[...] = picked[d * cap:(d + 1) * cap]
 
 
+def merged(recvs, relayed):
+    blocks = [recv[...] for recv in recvs]
+    if relayed:
+        place = lax.axis_index("wide")
+        outer = (place == 0) | (place == lax.axis_size("wide") - 1)
+        blocks[-2:] = [jnp.where(outer, blocks[-1], blocks[-2])]
+    return blocks
+
+
 def arrived(times, recvs, shared, unpack):
-    blocks = [recvs[times.index(d)][...][:shared] for d in sorted(times)]
+    blocks = [recvs[times.index(d)][:shared] for d in sorted(times)]
     rows = sum(b.shape[0] for b in blocks)
     if rows < unpack.shape[1]:
         blocks.append(jnp.zeros((unpack.shape[1] - rows, blocks[0].shape[1]), F32))
     return pick(unpack[...], jnp.concatenate(blocks, axis=0))
 
 
-def base_kernel(image, unpack_own, gap, base):
+def base_of(image, unpack_own, gap):
     own = image[...]
-    base[...] = gap[:own.shape[0], :] - own + pick(unpack_own[...], own)
+    return gap[:own.shape[0], :] - own + pick(unpack_own[...], own)
 
 
 def settle(trial, floor, alive):
@@ -188,7 +199,9 @@
     return jnp.where(alive, known + arrived(times, recvs, known.shape[0], unpack), 0.0), alive
 
 
-def rest_start_kernel(size, operator, mult, mult_block, gap, modes, trial, coarse, high, low, halves):
+def rest_start_kernel(
+    size, operator, mult, mult_block, gap, modes, image, unpack_own, top_gap, trial, coarse, high, low, base, halves
+):
     step = pl.program_id(0)
     rows, width = gap.shape
 
@@ -196,6 +209,7 @@
     def _():
         halves[:, :width], halves[:, width:] = split(mult[...])
         coarse[...] = jnp.zeros_like(coarse)
+        base[...] = base_of(image, unpack_own, top_gap)
 
     parts = split(operator[...])
     high[...], low[...] = parts
@@ -215,14 +229,18 @@
     return jnp.where(alive, gap[shared:, :] - image, 0.0), alive
 
 
-def rest_first_kernel(size, high, low, mult_s, mult_n, gap, modes, trial, coarse):
+def rest_first_kernel(size, high, low, mult_s, mult_n, gap, image, unpack_own, modes, trial, coarse, base):
     residual, _ = rest_residual(size, high, low, mult_s, mult_n, gap)
+    base[...] = base_of(image, unpack_own, gap)
     trial[...] = mult_n[...] + STEP * residual
     coarse[...] = product(split(modes[:, mult_s.shape[0]:]), split(residual))
 
 
-def rest_kernel(size, high, low, mult_s, mult_n, gap, floor, top_high, top_low, pack, mult_out, ahead):
+def rest_kernel(
+    size, high, low, mult_s, mult_n, gap, image, unpack_own, floor, top_high, top_low, pack, mult_out, ahead, base
+):
     shared = mult_s.shape[0]
+    base[...] = base_of(image, unpack_own, gap)
     residual, alive = rest_residual(size, high, low, mult_s, mult_n, gap)
     mult = settle(mult_n[...] + STEP * residual, floor[shared:, :], alive)
     mult_out[...] = mult
@@ -231,10 +249,13 @@
     ahead[shared:, :] = pick(pack[...], value)
 
 
-def rest_last_kernel(size, high, low, mult_s, mult_n, gap, floor, mult_out, residual_out, settled, left, done):
+def rest_last_kernel(
+    size, high, low, mult_s, mult_n, gap, image, unpack_own, floor, mult_out, residual_out, base, settled, left, done
+):
     shared, rows = mult_s.shape[0], mult_n.shape[0]
     residual, alive = rest_residual(size, high, low, mult_s, mult_n, gap)
     left[...] = residual
+    base[...] = base_of(image, unpack_own, gap)
     settled[...] = settle(mult_n[...] + STEP * residual, floor[shared:, :], alive)
     copies = [
         pltpu.make_async_copy(source, target.at[pl.ds(shared, rows)], done.at[i])
@@ -246,9 +267,9 @@
         copy.wait()
 
 
-def coarse_kernel(times, size, *refs):
-    n = len(times)
-    recvs = refs[:n]
+def coarse_kernel(times, relayed, size, *refs):
+    n = len(times) + relayed
+    recvs = merged(refs[:n], relayed)
     base, unpack, mult, modes, started, trial = refs[n:n + 6]
     shared = base.shape[0]
     residual, _ = shared_residual(times, recvs, base, unpack, size)
@@ -294,7 +315,7 @@
 
 def sweep_kernel(times, cap, size, *refs):
     n = len(times)
-    recvs = refs[:n]
+    recvs = merged(refs[:n], False)
     base, unpack, mult, floor, high, low, ahead, mult_out, image_out = refs[n:n + 9]
     shared = base.shape[0]
     residual, alive = shared_residual(times, recvs, base, unpack, size)
@@ -308,7 +329,7 @@
 
 def last_kernel(times, size, *refs):
     n = len(times)
-    recvs = refs[:n]
+    recvs = merged(refs[:n], False)
     base, unpack, mult, floor, _, _, mult_out, residual_out, settled, left, done = refs[n:]
     shared = base.shape[0]
     residual, alive = shared_residual(times, recvs, base, unpack, size)
@@ -332,6 +353,16 @@
 
 def swap_rows(blocks, axis, count, times):
     return [swap(blocks[d - 1], axis, count, d) for d in times]
+
+
+def swap_all_rows(block, axis):
+    crossed = swap(block, axis, 4, 3)
+    return [
+        crossed,
+        swap(block, axis, 4, 1),
+        lax.ppermute(block, axis, [(0, 2), (3, 1)]),
+        lax.ppermute(crossed, axis, [(2, 3), (1, 0)]),
+    ]
 
 
 def half_first(count, back):
@@ -381,8 +412,8 @@
     sent = [shape(cap, loads)] * n
     full = 2 * order * loads
 
-    list_rows = -(-(-(-cap // loads)) // 8) * 8
-    unpack_own, unpack_all, unpack, top_high, top_low, image, *sends = call(
+    list_rows = -(-n * -(-cap // loads) // 8) * 8
+    unpack_own, unpack_all, unpack, top_high, top_low, image, message = call(
         functools.partial(first_kernel, n, cap),
         tuple(
             pltpu.with_memory_space_constraint(value, pltpu.HBM)
@@ -391,7 +422,7 @@
         [shape(shared, shared, BF16), shape(shared, n * shared, BF16), shape(shared, padded, BF16)]
         + [shape(shared, order, BF16)] * 2
         + [shape(shared, loads)]
-        + [shape(shared + list_rows, loads)] * n,
+        + [shape(shared + list_rows, loads)],
         in_specs=[HBM] * 4,
         scratch=[
             pltpu.VMEM((1, shared), jnp.int32),
@@ -416,22 +447,18 @@
     scratch = [pltpu.VMEM((order, 2 * loads), BF16)]
     for outer in range(OUTER):
         times = orders[outer][0]
-        recvs = swap_rows(sends, "wide", wide, times)
-        base = call(
-            base_kernel,
-            (image, unpack_own, gap),
-            [shape(shared, loads)],
-            flops=4 * shared * shared * loads,
-            moved=8 * shared * loads,
-            name="base",
-        )[0]
+        relayed = outer == 0 and wide == 4
+        if relayed:
+            recvs = swap_all_rows(message, "wide")
+        else:
+            recvs = swap_rows([message] * n if outer == 0 else sends, "wide", wide, times)
         if outer == 0:
             row_block, load_block = block((shared, order)), block((shared, loads))
             next_loads = block((shared, loads), 1)
-            trial_n, started, high, low = call(
+            trial_n, started, high, low, base = call(
                 rest_start_kernel,
-                (size, operator, mult, mult, gap, modes),
-                [shape(rest, loads), shape(count, loads)] + [shape(rest, order, BF16)] * 2,
+                (size, operator, mult, mult, gap, modes, image, unpack_own, gap),
+                [shape(rest, loads), shape(count, loads)] + [shape(rest, order, BF16)] * 2 + [shape(shared, loads)],
                 [
                     SMEM,
                     block((shared, order), 1),
@@ -439,8 +466,11 @@
                     next_loads,
                     next_loads,
                     block((count, shared), 1, across=True),
+                    whole((shared, loads)),
+                    whole((shared, shared)),
+                    whole((shared, loads)),
                 ],
-                [load_block, whole((count, loads)), row_block, row_block],
+                [load_block, whole((count, loads)), row_block, row_block, whole((shared, loads))],
                 scratch=scratch,
                 grid=(steps,),
                 flops=3 * full * rest,
@@ -449,7 +479,7 @@
             )
             marks = unpack_all
             pack, stack_high, stack_low = call(
-                functools.partial(pack_kernel, times, cap),
+                functools.partial(pack_kernel, times, relayed, cap),
                 (*recvs, top_high, top_low),
                 [shape(padded, shared, BF16)] + [shape(shared + padded, shared, BF16)] * 2,
                 flops=8 * padded * shared * shared,
@@ -457,17 +487,17 @@
                 name="pack",
             )
         else:
-            trial_n, started = call(
+            trial_n, started, base = call(
                 rest_first_kernel,
-                (size, high, low, mult_s, mult_n, gap, modes),
-                [shape(rest, loads), shape(count, loads)],
+                (size, high, low, mult_s, mult_n, gap, image, unpack_own, modes),
+                [shape(rest, loads), shape(count, loads), shape(shared, loads)],
                 flops=3 * full * rest,
                 moved=4 * rest * order,
                 name="rest_first",
             )
             marks = unpack
         trial_s, own, *coarse = call(
-            functools.partial(coarse_kernel, times),
+            functools.partial(coarse_kernel, times, relayed),
             (size, *recvs, base, marks, mult_s, modes, started),
             [shape(shared, loads)] + [shape(count, loads)] * wide,
             flops=6 * shared * loads * unpack.shape[1],
@@ -500,28 +530,20 @@
             last = outer == OUTER - 1 and inner == INNER - 1
             times = orders[outer][inner]
             recvs = swap_rows(sends, "wide", wide, times)
-            base = call(
-                base_kernel,
-                (image, unpack_own, gap),
-                [shape(shared, loads)],
-                flops=4 * shared * shared * loads,
-                moved=8 * shared * loads,
-                name="base",
-            )[0]
-            ins = (size, high, low, mult_s, mult_n, gap, floor)
-            shadow = (size, *recvs, base, unpack, mult_s, floor)
+            ins = (size, high, low, mult_s, mult_n, gap, image, unpack_own, floor)
             cost = dict(flops=6 * shared * loads * unpack.shape[1], moved=2 * shared * unpack.shape[1])
             if last:
-                outs = call(
+                *outs, base = call(
                     rest_last_kernel,
                     ins,
-                    [shape(order, loads)] * 2,
-                    out_specs=[HBM] * 2,
+                    [shape(order, loads)] * 2 + [shape(shared, loads)],
+                    out_specs=[HBM] * 2 + [VMEM],
                     scratch=[pltpu.VMEM((rest, loads), F32)] * 2 + [pltpu.SemaphoreType.DMA((2,))],
                     flops=3 * full * rest,
                     moved=4 * rest * order,
                     name="rest_last",
                 )
+                shadow = (size, *recvs, base, unpack, mult_s, floor)
                 outs = call(
                     functools.partial(last_kernel, times),
                     (*shadow, *outs),
@@ -534,14 +556,16 @@
                     **cost,
                 )
                 return tuple(out[None] for out in outs)
-            mult_n, ahead = call(
+            next_n, ahead, base = call(
                 rest_kernel,
                 (*ins, top_high, top_low, pack),
-                [shape(rest, loads), shape(shared + padded, loads)],
+                [shape(rest, loads), shape(shared + padded, loads), shape(shared, loads)],
                 flops=3 * full * order,
                 moved=4 * order * order,
                 name="rest",
             )
+            mult_n = next_n
+            shadow = (size, *recvs, base, unpack, mult_s, floor)
             mult_s, image, *sends = call(
                 functools.partial(sweep_kernel, times, cap),
                 (*shadow, stack_high, stack_low, ahead),

time: 89.7 us -> 93 us (1.037)
  starting transfers between devices: 36.6 us -> 40.9 us
  waiting for transfers between devices: 32 us -> 29.7 us
  local copies, waits for them, and re-layouts: 0.03 us -> 2.01 us
    ppermute x0 -> x2, starting transfers between devices: none -> 3.82 us  [the longest x1 2.54 us: swap_all_rows(): lax.ppermute(block, axis, [(0, 2), (3, 1)])]
    ppermute x30 -> x29, waiting for transfers between devices: 32 us -> 29 us  [swap(): return lax.ppermute(block, axis, [(i, i ^ d) for i in range(count)])]
    unnamed x12 -> x14, local copies, waits for them, and re-layouts: 0.03 us -> 2.01 us
    pallas_call x25 -> x19, Pallas kernels: 19.3 us -> 18.5 us  [call(): pl.pallas_call(body, out_shape=outs, grid=grid, in_specs=in_specs, out_sp...]
    ppermute x30 -> x29, starting transfers between devices: 36.6 us -> 37.1 us  [swap(): return lax.ppermute(block, axis, [(i, i ^ d) for i in range(count)])]
  transfers between devices with their start and end apart: 30 -> 31, of which waited for: 26 -> 23; matrix products, arithmetic and copies ran while one was open for 0% -> 0% of each run, Pallas kernels for 13% -> 11%
where the time goes in v16:
time: 93 us; the launch traced here: 92.7 us
  starting transfers between devices  40.9 us (44%)
  waiting for transfers between devices  29.7 us (32%)
  Pallas kernels  18.5 us (20%)
  local copies, waits for them, and re-layouts  2.01 us (2%)
  between operations  1.56 us (2%)
    ppermute x29, starting transfers between devices, swap(): return lax.ppermute(block, axis, [(i, i ^ d) for i in range(count)])  37.1 us
    ppermute x29, waiting for transfers between devices, swap(): return lax.ppermute(block, axis, [(i, i ^ d) for i in range(count)])  29 us
    pallas_call x19, Pallas kernels, call(): pl.pallas_call(body, out_shape=outs, grid=grid, in_specs=in_specs, out_sp...  18.5 us
    ppermute x1, starting transfers between devices, swap_all_rows(): lax.ppermute(block, axis, [(0, 2), (3, 1)])  2.54 us
    unnamed x14, local copies, waits for them, and re-layouts  2.01 us
  transfers between devices with their start and end apart: 31, of which 23 were waited for; matrix products, arithmetic and copies ran while one was open for 0% of the time, Pallas kernels for 11%

profile of v16, /device:TPU:0, one launch (start us, length us, event | category | flops | bytes accessed | tf_op | source)
XLA Modules:
  0.0 92.7 jit_solution(16228239294055775577)
XLA Ops:
  0.7 2.1 %first.1 = (bf16[256,256]{1,0:T(8,128)(2,1)S(1)}, bf16[256,768]{1,0:T(8,128)(2,1)S(1)}, bf16[256,384]{1,0:T(8,128)(2,1)S(1)}, bf16[256,1024]{1,0:T(8,128)(2,1)S(...) custom-call(s32[1,256]{1,0:T(1,128)} %bitcast.27, s32[1,256]{1,0:T(1,128)} %rows_at.1, ...), custom_call_target="tpu_custom_call" | custom-call | flops 201326592 | bytes 2097152 | tf_op jit(solution)/shard_map/first/pallas_call | solution.py:49
  2.7 5.1 %collective-permute-start = (f32[264,128]{1,0:T(8,128)S(1)}, f32[264,128]{1,0:T(8,128)S(1)}, u32[]{:S(2)}, u32[]{:S(2)}) collective-permute-start(f32[264,128]{1,0:T(8,128)S(1)} %get-tuple-element.85), channel_id=1, source_target_pairs={{0,12},{4,8},{8,4},{12,0},{1,13},{5,9},{9,5},{13,1},{2,14},{6,10},... | collective-permute-start | bytes 405512 | tf_op jit(solution)/shard_map/ppermute | solution.py:347
  7.8 2.5 %collective-permute-start.2 = (f32[264,128]{1,0:T(8,128)S(1)}, f32[264,128]{1,0:T(8,128)S(1)}, u32[]{:S(2)}, u32[]{:S(2)}) collective-permute-start(f32[264,128]{1,0:T(8,128)S(1)} %get-tuple-element.85), channel_id=1, source_target_pairs={{0,8},{12,4},{1,9},{13,5},{2,10},{14,6},{3,11},{15,7},{16,24},{28,... | collective-permute-start | bytes 405512 | tf_op jit(solution)/shard_map/ppermute | solution.py:363
  10.4 1.9 %collective-permute-done.refs_0_ = f32[264,128]{1,0:T(8,128)S(1)} collective-permute-done((f32[264,128]{1,0:T(8,128)S(1)}, f32[264,128]{1,0:T(8,128)S(1)}, u32[]{:S(2)}, u32[]{:S(2)}) %collective-permute-start) | collective-permute-done | bytes 135200 | tf_op jit(solution)/shard_map/ppermute | solution.py:347
  12.3 1.3 %collective-permute-start.3 = (f32[264,128]{1,0:T(8,128)S(1)}, f32[264,128]{1,0:T(8,128)S(1)}, u32[]{:S(2)}, u32[]{:S(2)}) collective-permute-start(f32[264,128]{1,0:T(8,128)S(1)} %collective-permute-done.refs_0_), channel_id=1, source_target_pairs={{8,12},{4,0},{9,13},{5,1},{10,14},{6,2},{11,15},{7,3},{24,28},{20,... | collective-permute-start | bytes 405512 | tf_op jit(solution)/shard_map/ppermute | solution.py:364
  14.3 1.0 %copy-done.2 = f32[1,1024,128]{2,1,0:T(8,128)S(1)} copy-done((f32[1,1024,128]{2,1,0:T(8,128)S(1)}, f32[1,1024,128]{2,1,0:T(8,128)}, u32[]{:S(2)}) %copy-start.2) | copy-done | bytes 524312
  15.3 0.9 %copy-done.3 = f32[1,64,1024]{2,1,0:T(8,128)S(1)} copy-done((f32[1,64,1024]{2,1,0:T(8,128)S(1)}, f32[1,64,1024]{2,1,0:T(8,128)}, u32[]{:S(2)}) %copy-start.3) | copy-done | bytes 262168
  16.3 2.2 %rest_start.1 = (f32[768,128]{1,0:T(8,128)S(1)}, f32[64,128]{1,0:T(8,128)S(1)}, bf16[768,1024]{1,0:T(8,128)(2,1)S(1)}, bf16[768,1024]{1,0:T(8,128)(2,1)S(1)}, f32[256,128]{1,0:T(8,128)S(1)}) custom-call(s32[1]{0:T(128)S(6)} %copy.15.size, f32[1024,1024]{1,0:T(8,128)S(1)} %bitcast.15, f32[1024,128]{1,0:T(8,128)S(1)} %bitcast.17, f32[1024,128]{1,0:T(8,128)S(1)} %bitcast.18, ...), custom_call_target="tpu_custom_call" | custom-call | flops 603979776 | bytes 6291456 | tf_op jit(solution)/shard_map/rest_start/pallas_call | solution.py:49
  18.5 0.7 collective-permute-done.3.refs_3_
  19.2 0.5 coarse.2
  19.7 4.4 %collective-permute-start.4 = (f32[64,128]{1,0:T(8,128)S(1)}, f32[64,128]{1,0:T(8,128)S(1)}, u32[]{:S(2)}, u32[]{:S(2)}) collective-permute-start(f32[64,128]{1,0:T(8,128)S(1)} %get-tuple-element.92), channel_id=1, source_target_pairs={{0,8},{4,12},{8,0},{12,4},{1,9},{5,13},{9,1},{13,5},{2,10},{6,14},... | collective-permute-start | bytes 98312 | tf_op jit(solution)/shard_map/ppermute | solution.py:347
  24.1 0.6 collective-permute-start.6
  24.7 0.4 prepare.1
  25.1 1.6 %collective-permute-done.4.refs_1_ = f32[64,128]{1,0:T(8,128)S(1)} collective-permute-done((f32[64,128]{1,0:T(8,128)S(1)}, f32[64,128]{1,0:T(8,128)S(1)}, u32[]{:S(2)}, u32[]{:S(2)}) %collective-permute-start.4) | collective-permute-done | bytes 32800 | tf_op jit(solution)/shard_map/ppermute | solution.py:347
  26.7 3.1 %collective-permute-done.5.refs_2_ = f32[64,128]{1,0:T(8,128)S(1)} collective-permute-done((f32[64,128]{1,0:T(8,128)S(1)}, f32[64,128]{1,0:T(8,128)S(1)}, u32[]{:S(2)}, u32[]{:S(2)}) %collective-permute-start.5) | collective-permute-done | bytes 32800 | tf_op jit(solution)/shard_map/ppermute | solution.py:347
  30.1 1.6 %collective-permute-start.8 = (f32[64,128]{1,0:T(8,128)S(1)}, f32[64,128]{1,0:T(8,128)S(1)}, u32[]{:S(2)}, u32[]{:S(2)}) collective-permute-start(f32[64,128]{1,0:T(8,128)S(1)} %get-tuple-element.97), channel_id=1, source_target_pairs={{0,2},{1,3},{2,0},{3,1},{4,6},{5,7},{6,4},{7,5},{8,10},{9,11},{10,... | collective-permute-start | bytes 98312 | tf_op jit(solution)/shard_map/ppermute | solution.py:347
  32.0 0.3 pack.1
  32.3 1.5 %collective-permute-done.7.refs_1_ = f32[64,128]{1,0:T(8,128)S(1)} collective-permute-done((f32[64,128]{1,0:T(8,128)S(1)}, f32[64,128]{1,0:T(8,128)S(1)}, u32[]{:S(2)}, u32[]{:S(2)}) %collective-permute-start.7) | collective-permute-done | bytes 32800 | tf_op jit(solution)/shard_map/ppermute | solution.py:347
  33.8 0.4 collective-permute-done.8.refs_2_
  34.2 1.0 %lift.2 = (f32[256,128]{1,0:T(8,128)S(1)}, f32[768,128]{1,0:T(8,128)S(1)}, f32[256,128]{1,0:T(8,128)S(1)}, f32[128,128]{1,0:T(8,128)S(1)}, f32[128,128]{1,0:T(8,128)S(1)}, /*index=5*/f32[128,128]{1,0:T(8,128)S(1)}) custom-call(s32[1]{0:T(128)S(6)} %copy.15.size, f32[64,128]{1,0:T(8,128)S(1)} %get-tuple-element.95.refs_0_, ...), custom_call_target="tpu_custom_call" | custom-call | flops 201326592 | bytes 1048576 | tf_op jit(solution)/shard_map/lift/pallas_call | solution.py:49
  35.2 1.0 %collective-permute-start.10 = (f32[128,128]{1,0:T(8,128)S(1)}, f32[128,128]{1,0:T(8,128)S(1)}, u32[]{:S(2)}, u32[]{:S(2)}) collective-permute-start(f32[128,128]{1,0:T(8,128)S(1)} %get-tuple-element.106), channel_id=1, source_target_pairs={{0,8},{4,12},{8,0},{12,4},{1,9},{5,13},{9,1},{13,5},{2,10},{6,14},... | collective-permute-start | bytes 196616 | tf_op jit(solution)/shard_map/ppermute | solution.py:347
  36.1 1.7 %collective-permute-start.11 = (f32[128,128]{1,0:T(8,128)S(1)}, f32[128,128]{1,0:T(8,128)S(1)}, u32[]{:S(2)}, u32[]{:S(2)}) collective-permute-start(f32[128,128]{1,0:T(8,128)S(1)} %get-tuple-element.107), channel_id=1, source_target_pairs={{0,4},{4,0},{8,12},{12,8},{1,5},{5,1},{9,13},{13,9},{2,6},{6,2},{1... | collective-permute-start | bytes 196616 | tf_op jit(solution)/shard_map/ppermute | solution.py:347
  37.8 1.8 %collective-permute-start.12 = (f32[128,128]{1,0:T(8,128)S(1)}, f32[128,128]{1,0:T(8,128)S(1)}, u32[]{:S(2)}, u32[]{:S(2)}) collective-permute-start(f32[128,128]{1,0:T(8,128)S(1)} %get-tuple-element.108), channel_id=1, source_target_pairs={{0,12},{4,8},{8,4},{12,0},{1,13},{5,9},{9,5},{13,1},{2,14},{6,10},... | collective-permute-start | bytes 196616 | tf_op jit(solution)/shard_map/ppermute | solution.py:347
  39.6 1.5 %rest.3 = (f32[768,128]{1,0:T(8,128)S(1)}, f32[640,128]{1,0:T(8,128)S(1)}, f32[256,128]{1,0:T(8,128)S(1)}) custom-call(s32[1]{0:T(128)S(6)} %copy.15.size, bf16[768,1024]{1,0:T(8,128)(2,1)S(1)} %get-tuple-element.109.high, bf16[768,1024]{1,0:T(8,128)(2,1)S(1)} %get-tuple-element.110.low, f32[256,128]{1,0:T(8,128)S(1)} %get-tuple-element.111.mult_s.refs_5_, ...), custom_call_target="tpu_custom_call" | custom-call | flops 805306368 | bytes 4194304 | tf_op jit(solution)/shard_map/rest/pallas_call | solution.py:49
  41.4 0.4 collective-permute-done.11.refs_1_
  41.8 2.2 %collective-permute-done.12.refs_2_ = f32[128,128]{1,0:T(8,128)S(1)} collective-permute-done((f32[128,128]{1,0:T(8,128)S(1)}, f32[128,128]{1,0:T(8,128)S(1)}, u32[]{:S(2)}, u32[]{:S(2)}) %collective-permute-start.12) | collective-permute-done | bytes 65568 | tf_op jit(solution)/shard_map/ppermute | solution.py:347
  43.9 0.5 sweep.3
  44.5 1.7 %collective-permute-start.13 = (f32[128,128]{1,0:T(8,128)S(1)}, f32[128,128]{1,0:T(8,128)S(1)}, u32[]{:S(2)}, u32[]{:S(2)}) collective-permute-start(f32[128,128]{1,0:T(8,128)S(1)} %get-tuple-element.119), channel_id=1, source_target_pairs={{0,8},{4,12},{8,0},{12,4},{1,9},{5,13},{9,1},{13,5},{2,10},{6,14},... | collective-permute-start | bytes 196616 | tf_op jit(solution)/shard_map/ppermute | solution.py:347
  46.2 1.4 %collective-permute-start.14 = (f32[128,128]{1,0:T(8,128)S(1)}, f32[128,128]{1,0:T(8,128)S(1)}, u32[]{:S(2)}, u32[]{:S(2)}) collective-permute-start(f32[128,128]{1,0:T(8,128)S(1)} %get-tuple-element.120), channel_id=1, source_target_pairs={{0,12},{4,8},{8,4},{12,0},{1,13},{5,9},{9,5},{13,1},{2,14},{6,10},... | collective-permute-start | bytes 196616 | tf_op jit(solution)/shard_map/ppermute | solution.py:347
  47.6 0.4 collective-permute-start.15
  48.0 1.5 %rest.4 = (f32[768,128]{1,0:T(8,128)S(1)}, f32[640,128]{1,0:T(8,128)S(1)}, f32[256,128]{1,0:T(8,128)S(1)}) custom-call(s32[1]{0:T(128)S(6)} %copy.15.size, bf16[768,1024]{1,0:T(8,128)(2,1)S(1)} %get-tuple-element.109.high, bf16[768,1024]{1,0:T(8,128)(2,1)S(1)} %get-tuple-element.110.low, f32[256,128]{1,0:T(8,128)S(1)} %get-tuple-element.122.mult_s.refs_5_, ...), custom_call_target="tpu_custom_call" | custom-call | flops 805306368 | bytes 4194304 | tf_op jit(solution)/shard_map/rest/pallas_call | solution.py:49
  49.6 1.8 %collective-permute-done.13.refs_0_ = f32[128,128]{1,0:T(8,128)S(1)} collective-permute-done((f32[128,128]{1,0:T(8,128)S(1)}, f32[128,128]{1,0:T(8,128)S(1)}, u32[]{:S(2)}, u32[]{:S(2)}) %collective-permute-start.13) | collective-permute-done | bytes 65568 | tf_op jit(solution)/shard_map/ppermute | solution.py:347
  51.4 1.1 %collective-permute-done.14.refs_1_ = f32[128,128]{1,0:T(8,128)S(1)} collective-permute-done((f32[128,128]{1,0:T(8,128)S(1)}, f32[128,128]{1,0:T(8,128)S(1)}, u32[]{:S(2)}, u32[]{:S(2)}) %collective-permute-start.14) | collective-permute-done | bytes 65568 | tf_op jit(solution)/shard_map/ppermute | solution.py:347
  52.5 0.7 collective-permute-done.15.refs_2_
  53.2 0.5 sweep.4
  53.7 0.9 collective-permute-start.16
  54.6 1.7 %collective-permute-start.17 = (f32[128,128]{1,0:T(8,128)S(1)}, f32[128,128]{1,0:T(8,128)S(1)}, u32[]{:S(2)}, u32[]{:S(2)}) collective-permute-start(f32[128,128]{1,0:T(8,128)S(1)} %get-tuple-element.128), channel_id=1, source_target_pairs={{0,12},{4,8},{8,4},{12,0},{1,13},{5,9},{9,5},{13,1},{2,14},{6,10},... | collective-permute-start | bytes 196616 | tf_op jit(solution)/shard_map/ppermute | solution.py:347
  56.3 1.0 %collective-permute-start.18 = (f32[128,128]{1,0:T(8,128)S(1)}, f32[128,128]{1,0:T(8,128)S(1)}, u32[]{:S(2)}, u32[]{:S(2)}) collective-permute-start(f32[128,128]{1,0:T(8,128)S(1)} %get-tuple-element.129), channel_id=1, source_target_pairs={{0,4},{4,0},{8,12},{12,8},{1,5},{5,1},{9,13},{13,9},{2,6},{6,2},{1... | collective-permute-start | bytes 196616 | tf_op jit(solution)/shard_map/ppermute | solution.py:347
  57.3 1.1 %rest_first.1 = (f32[768,128]{1,0:T(8,128)S(1)}, f32[64,128]{1,0:T(8,128)S(1)}, f32[256,128]{1,0:T(8,128)S(1)}) custom-call(s32[1]{0:T(128)S(6)} %copy.15.size, bf16[768,1024]{1,0:T(8,128)(2,1)S(1)} %get-tuple-element.109.high, bf16[768,1024]{1,0:T(8,128)(2,1)S(1)} %get-tuple-element.110.low, f32[256,128]{1,0:T(8,128)S(1)} %get-tuple-element.130.mult_s.refs_5_, ...), custom_call_target="tpu_custom_call" | custom-call | flops 603979776 | bytes 3145728 | tf_op jit(solution)/shard_map/rest_first/pallas_call | solution.py:49
  58.4 2.9 %collective-permute-done.16.refs_0_ = f32[128,128]{1,0:T(8,128)S(1)} collective-permute-done((f32[128,128]{1,0:T(8,128)S(1)}, f32[128,128]{1,0:T(8,128)S(1)}, u32[]{:S(2)}, u32[]{:S(2)}) %collective-permute-start.16) | collective-permute-done | bytes 65568 | tf_op jit(solution)/shard_map/ppermute | solution.py:347
  61.3 0.4 collective-permute-done.18.refs_2_
  61.7 0.4 coarse.3
  62.1 1.4 %collective-permute-start.19 = (f32[64,128]{1,0:T(8,128)S(1)}, f32[64,128]{1,0:T(8,128)S(1)}, u32[]{:S(2)}, u32[]{:S(2)}) collective-permute-start(f32[64,128]{1,0:T(8,128)S(1)} %get-tuple-element.136), channel_id=1, source_target_pairs={{0,8},{4,12},{8,0},{12,4},{1,9},{5,13},{9,1},{13,5},{2,10},{6,14},... | collective-permute-start | bytes 98312 | tf_op jit(solution)/shard_map/ppermute | solution.py:347
  63.6 1.9 %collective-permute-start.20 = (f32[64,128]{1,0:T(8,128)S(1)}, f32[64,128]{1,0:T(8,128)S(1)}, u32[]{:S(2)}, u32[]{:S(2)}) collective-permute-start(f32[64,128]{1,0:T(8,128)S(1)} %get-tuple-element.137), channel_id=1, source_target_pairs={{0,12},{4,8},{8,4},{12,0},{1,13},{5,9},{9,5},{13,1},{2,14},{6,10},... | collective-permute-start | bytes 98312 | tf_op jit(solution)/shard_map/ppermute | solution.py:347
  65.7 2.0 %collective-permute-done.19.refs_1_ = f32[64,128]{1,0:T(8,128)S(1)} collective-permute-done((f32[64,128]{1,0:T(8,128)S(1)}, f32[64,128]{1,0:T(8,128)S(1)}, u32[]{:S(2)}, u32[]{:S(2)}) %collective-permute-start.19) | collective-permute-done | bytes 32800 | tf_op jit(solution)/shard_map/ppermute | solution.py:347
  67.7 1.6 %collective-permute-done.20.refs_2_ = f32[64,128]{1,0:T(8,128)S(1)} collective-permute-done((f32[64,128]{1,0:T(8,128)S(1)}, f32[64,128]{1,0:T(8,128)S(1)}, u32[]{:S(2)}, u32[]{:S(2)}) %collective-permute-start.20) | collective-permute-done | bytes 32800 | tf_op jit(solution)/shard_map/ppermute | solution.py:347
  69.3 0.3 collective-permute-done.21.refs_3_
  70.0 1.8 %collective-permute-start.24 = (f32[64,128]{1,0:T(8,128)S(1)}, f32[64,128]{1,0:T(8,128)S(1)}, u32[]{:S(2)}, u32[]{:S(2)}) collective-permute-start(f32[64,128]{1,0:T(8,128)S(1)} %get-tuple-element.142), channel_id=1, source_target_pairs={{0,1},{1,0},{2,3},{3,2},{4,5},{5,4},{6,7},{7,6},{8,9},{9,8},{10,11... | collective-permute-start | bytes 98312 | tf_op jit(solution)/shard_map/ppermute | solution.py:347
  71.8 1.5 %collective-permute-done.22.refs_1_ = f32[64,128]{1,0:T(8,128)S(1)} collective-permute-done((f32[64,128]{1,0:T(8,128)S(1)}, f32[64,128]{1,0:T(8,128)S(1)}, u32[]{:S(2)}, u32[]{:S(2)}) %collective-permute-start.22) | collective-permute-done | bytes 32800 | tf_op jit(solution)/shard_map/ppermute | solution.py:347
  73.3 0.7 collective-permute-done.23.refs_2_
  74.0 1.0 %lift.3 = (f32[256,128]{1,0:T(8,128)S(1)}, f32[768,128]{1,0:T(8,128)S(1)}, f32[256,128]{1,0:T(8,128)S(1)}, f32[128,128]{1,0:T(8,128)S(1)}, f32[128,128]{1,0:T(8,128)S(1)}, /*index=5*/f32[128,128]{1,0:T(8,128)S(1)}) custom-call(s32[1]{0:T(128)S(6)} %copy.15.size, f32[64,128]{1,0:T(8,128)S(1)} %get-tuple-element.139.refs_0_, ...), custom_call_target="tpu_custom_call" | custom-call | flops 201326592 | bytes 1048576 | tf_op jit(solution)/shard_map/lift/pallas_call | solution.py:49
  75.0 0.6 collective-permute-start.25
  75.6 1.9 %collective-permute-start.26 = (f32[128,128]{1,0:T(8,128)S(1)}, f32[128,128]{1,0:T(8,128)S(1)}, u32[]{:S(2)}, u32[]{:S(2)}) collective-permute-start(f32[128,128]{1,0:T(8,128)S(1)} %get-tuple-element.146), channel_id=1, source_target_pairs={{0,4},{4,0},{8,12},{12,8},{1,5},{5,1},{9,13},{13,9},{2,6},{6,2},{1... | collective-permute-start | bytes 196616 | tf_op jit(solution)/shard_map/ppermute | solution.py:347
  77.5 1.9 %collective-permute-start.27 = (f32[128,128]{1,0:T(8,128)S(1)}, f32[128,128]{1,0:T(8,128)S(1)}, u32[]{:S(2)}, u32[]{:S(2)}) collective-permute-start(f32[128,128]{1,0:T(8,128)S(1)} %get-tuple-element.147), channel_id=1, source_target_pairs={{0,12},{4,8},{8,4},{12,0},{1,13},{5,9},{9,5},{13,1},{2,14},{6,10},... | collective-permute-start | bytes 196616 | tf_op jit(solution)/shard_map/ppermute | solution.py:347
  79.4 1.5 %rest.5 = (f32[768,128]{1,0:T(8,128)S(1)}, f32[640,128]{1,0:T(8,128)S(1)}, f32[256,128]{1,0:T(8,128)S(1)}) custom-call(s32[1]{0:T(128)S(6)} %copy.15.size, bf16[768,1024]{1,0:T(8,128)(2,1)S(1)} %get-tuple-element.109.high, bf16[768,1024]{1,0:T(8,128)(2,1)S(1)} %get-tuple-element.110.low, f32[256,128]{1,0:T(8,128)S(1)} %get-tuple-element.148.mult_s.refs_5_, ...), custom_call_target="tpu_custom_call" | custom-call | flops 805306368 | bytes 4194304 | tf_op jit(solution)/shard_map/rest/pallas_call | solution.py:49
  81.2 2.4 %collective-permute-done.27.refs_2_ = f32[128,128]{1,0:T(8,128)S(1)} collective-permute-done((f32[128,128]{1,0:T(8,128)S(1)}, f32[128,128]{1,0:T(8,128)S(1)}, u32[]{:S(2)}, u32[]{:S(2)}) %collective-permute-start.27) | collective-permute-done | bytes 65568 | tf_op jit(solution)/shard_map/ppermute | solution.py:347
  83.6 0.5 sweep.5
  84.1 0.4 collective-permute-start.28
  84.5 1.9 %collective-permute-start.29 = (f32[128,128]{1,0:T(8,128)S(1)}, f32[128,128]{1,0:T(8,128)S(1)}, u32[]{:S(2)}, u32[]{:S(2)}) collective-permute-start(f32[128,128]{1,0:T(8,128)S(1)} %get-tuple-element.154), channel_id=1, source_target_pairs={{0,12},{4,8},{8,4},{12,0},{1,13},{5,9},{9,5},{13,1},{2,14},{6,10},... | collective-permute-start | bytes 196616 | tf_op jit(solution)/shard_map/ppermute | solution.py:347
  86.4 1.3 %collective-permute-start.30 = (f32[128,128]{1,0:T(8,128)S(1)}, f32[128,128]{1,0:T(8,128)S(1)}, u32[]{:S(2)}, u32[]{:S(2)}) collective-permute-start(f32[128,128]{1,0:T(8,128)S(1)} %get-tuple-element.155), channel_id=1, source_target_pairs={{0,4},{4,0},{8,12},{12,8},{1,5},{5,1},{9,13},{13,9},{2,6},{6,2},{1... | collective-permute-start | bytes 196616 | tf_op jit(solution)/shard_map/ppermute | solution.py:347
  87.6 1.9 %rest_last.1 = (f32[1024,128]{1,0:T(8,128)}, f32[1024,128]{1,0:T(8,128)}, f32[256,128]{1,0:T(8,128)S(1)}) custom-call(s32[1]{0:T(128)S(6)} %copy.15.size, bf16[768,1024]{1,0:T(8,128)(2,1)S(1)} %get-tuple-element.109.high, bf16[768,1024]{1,0:T(8,128)(2,1)S(1)} %get-tuple-element.110.low, f32[256,128]{1,0:T(8,128)S(1)} %get-tuple-element.156.mult_s.refs_5_, ...), custom_call_target="tpu_custom_call" | custom-call | flops 603979776 | bytes 3145728 | tf_op jit(solution)/shard_map/rest_last/pallas_call | solution.py:49
  89.6 1.8 %collective-permute-done.28.refs_0_ = f32[128,128]{1,0:T(8,128)S(1)} collective-permute-done((f32[128,128]{1,0:T(8,128)S(1)}, f32[128,128]{1,0:T(8,128)S(1)}, u32[]{:S(2)}, u32[]{:S(2)}) %collective-permute-start.28) | collective-permute-done | bytes 65568 | tf_op jit(solution)/shard_map/ppermute | solution.py:347
  91.3 0.5 collective-permute-done.30.refs_2_
  91.8 0.9 %last.1 = (f32[1024,128]{1,0:T(8,128)}, f32[1024,128]{1,0:T(8,128)}) custom-call(s32[1]{0:T(128)S(6)} %copy.15.size, f32[128,128]{1,0:T(8,128)S(1)} %collective-permute-done.28.refs_0_, f32[128,128]{1,0:T(8,128)S(1)} %collective-permute-done.29.refs_1_, ...), custom_call_target="tpu_custom_call", output_to_operand_aliasing={{0}: (8, {}), {1}: (9, {})} | custom-call | flops 75497472 | bytes 196608 | tf_op jit(solution)/shard_map/last/pallas_call | solution.py:49
  (31 shorter events, 1.7 us)
Async XLA Ops:
  0.6 13.6 %copy-start = (f32[1,1024,128]{2,1,0:T(8,128)S(1)}, f32[1,1024,128]{2,1,0:T(8,128)}, u32[]{:S(2)}) copy-start(f32[1,1024,128]{2,1,0:T(8,128)} %param.12) | copy-start | bytes 1572868
  0.6 13.6 %copy-start.1 = (f32[1,1024,1024]{2,1,0:T(8,128)S(1)}, f32[1,1024,1024]{2,1,0:T(8,128)}, u32[]{:S(2)}) copy-start(f32[1,1024,1024]{2,1,0:T(8,128)} %param.9) | copy-start | bytes 12582916
  2.7 9.6 %collective-permute-start = (f32[264,128]{1,0:T(8,128)S(1)}, f32[264,128]{1,0:T(8,128)S(1)}, u32[]{:S(2)}, u32[]{:S(2)}) collective-permute-start(f32[264,128]{1,0:T(8,128)S(1)} %get-tuple-element.85), channel_id=1, source_target_pairs={{0,12},{4,8},{8,4},{12,0},{1,13},{5,9},{9,5},{13,1},{2,14},{6,10},... | collective-permute-start | bytes 405512 | tf_op jit(solution)/shard_map/ppermute | solution.py:347
  7.8 10.7 %collective-permute-start.1 = (f32[264,128]{1,0:T(8,128)S(1)}, f32[264,128]{1,0:T(8,128)S(1)}, u32[]{:S(2)}, u32[]{:S(2)}) collective-permute-start(f32[264,128]{1,0:T(8,128)S(1)} %get-tuple-element.85), channel_id=1, source_target_pairs={{0,4},{4,0},{8,12},{12,8},{1,5},{5,1},{9,13},{13,9},{2,6},{6,2},{1... | collective-permute-start | bytes 405512 | tf_op jit(solution)/shard_map/ppermute | solution.py:347
  7.8 10.7 %collective-permute-start.2 = (f32[264,128]{1,0:T(8,128)S(1)}, f32[264,128]{1,0:T(8,128)S(1)}, u32[]{:S(2)}, u32[]{:S(2)}) collective-permute-start(f32[264,128]{1,0:T(8,128)S(1)} %get-tuple-element.85), channel_id=1, source_target_pairs={{0,8},{12,4},{1,9},{13,5},{2,10},{14,6},{3,11},{15,7},{16,24},{28,... | collective-permute-start | bytes 405512 | tf_op jit(solution)/shard_map/ppermute | solution.py:363
  12.3 6.9 %collective-permute-start.3 = (f32[264,128]{1,0:T(8,128)S(1)}, f32[264,128]{1,0:T(8,128)S(1)}, u32[]{:S(2)}, u32[]{:S(2)}) collective-permute-start(f32[264,128]{1,0:T(8,128)S(1)} %collective-permute-done.refs_0_), channel_id=1, source_target_pairs={{8,12},{4,0},{9,13},{5,1},{10,14},{6,2},{11,15},{7,3},{24,28},{20,... | collective-permute-start | bytes 405512 | tf_op jit(solution)/shard_map/ppermute | solution.py:364
  14.3 1.0 %copy-start.2 = (f32[1,1024,128]{2,1,0:T(8,128)S(1)}, f32[1,1024,128]{2,1,0:T(8,128)}, u32[]{:S(2)}) copy-start(f32[1,1024,128]{2,1,0:T(8,128)} %param.13) | copy-start | bytes 1572868
  15.3 0.9 %copy-start.3 = (f32[1,64,1024]{2,1,0:T(8,128)S(1)}, f32[1,64,1024]{2,1,0:T(8,128)}, u32[]{:S(2)}) copy-start(f32[1,64,1024]{2,1,0:T(8,128)} %param.11) | copy-start | bytes 786436
  18.5 6.2 %copy-start.5 = (f32[256,256]{1,0:T(8,128)S(1)}, f32[256,256]{1,0:T(8,128)}, u32[]{:S(2)}) copy-start(f32[256,256]{1,0:T(8,128)} %tile.3) | copy-start | bytes 786436
  18.5 6.2 %copy-start.6 = (s32[1,1024]{1,0:T(1,128)S(1)}, s32[1,1024]{1,0:T(1,128)}, u32[]{:S(2)}) copy-start(s32[1,1024]{1,0:T(1,128)} %contact.1) | copy-start | bytes 12292
  19.7 7.0 %collective-permute-start.4 = (f32[64,128]{1,0:T(8,128)S(1)}, f32[64,128]{1,0:T(8,128)S(1)}, u32[]{:S(2)}, u32[]{:S(2)}) collective-permute-start(f32[64,128]{1,0:T(8,128)S(1)} %get-tuple-element.92), channel_id=1, source_target_pairs={{0,8},{4,12},{8,0},{12,4},{1,9},{5,13},{9,1},{13,5},{2,10},{6,14},... | collective-permute-start | bytes 98312 | tf_op jit(solution)/shard_map/ppermute | solution.py:347
  24.1 5.7 %collective-permute-start.5 = (f32[64,128]{1,0:T(8,128)S(1)}, f32[64,128]{1,0:T(8,128)S(1)}, u32[]{:S(2)}, u32[]{:S(2)}) collective-permute-start(f32[64,128]{1,0:T(8,128)S(1)} %get-tuple-element.93), channel_id=1, source_target_pairs={{0,12},{4,8},{8,4},{12,0},{1,13},{5,9},{9,5},{13,1},{2,14},{6,10},... | collective-permute-start | bytes 98312 | tf_op jit(solution)/shard_map/ppermute | solution.py:347
  24.1 5.7 %collective-permute-start.6 = (f32[64,128]{1,0:T(8,128)S(1)}, f32[64,128]{1,0:T(8,128)S(1)}, u32[]{:S(2)}, u32[]{:S(2)}) collective-permute-start(f32[64,128]{1,0:T(8,128)S(1)} %get-tuple-element.94), channel_id=1, source_target_pairs={{0,4},{4,0},{8,12},{12,8},{1,5},{5,1},{9,13},{13,9},{2,6},{6,2},{1... | collective-permute-start | bytes 98312 | tf_op jit(solution)/shard_map/ppermute | solution.py:347
  30.1 3.7 %collective-permute-start.7 = (f32[64,128]{1,0:T(8,128)S(1)}, f32[64,128]{1,0:T(8,128)S(1)}, u32[]{:S(2)}, u32[]{:S(2)}) collective-permute-start(f32[64,128]{1,0:T(8,128)S(1)} %get-tuple-element.96), channel_id=1, source_target_pairs={{0,3},{1,2},{2,1},{3,0},{4,7},{5,6},{6,5},{7,4},{8,11},{9,10},{10,... | collective-permute-start | bytes 98312 | tf_op jit(solution)/shard_map/ppermute | solution.py:347
  30.1 4.0 %collective-permute-start.8 = (f32[64,128]{1,0:T(8,128)S(1)}, f32[64,128]{1,0:T(8,128)S(1)}, u32[]{:S(2)}, u32[]{:S(2)}) collective-permute-start(f32[64,128]{1,0:T(8,128)S(1)} %get-tuple-element.97), channel_id=1, source_target_pairs={{0,2},{1,3},{2,0},{3,1},{4,6},{5,7},{6,4},{7,5},{8,10},{9,11},{10,... | collective-permute-start | bytes 98312 | tf_op jit(solution)/shard_map/ppermute | solution.py:347
  31.7 2.5 %collective-permute-start.9 = (f32[64,128]{1,0:T(8,128)S(1)}, f32[64,128]{1,0:T(8,128)S(1)}, u32[]{:S(2)}, u32[]{:S(2)}) collective-permute-start(f32[64,128]{1,0:T(8,128)S(1)} %get-tuple-element.98), channel_id=1, source_target_pairs={{0,1},{1,0},{2,3},{3,2},{4,5},{5,4},{6,7},{7,6},{8,9},{9,8},{10,11... | collective-permute-start | bytes 98312 | tf_op jit(solution)/shard_map/ppermute | solution.py:347
  35.2 6.2 %collective-permute-start.10 = (f32[128,128]{1,0:T(8,128)S(1)}, f32[128,128]{1,0:T(8,128)S(1)}, u32[]{:S(2)}, u32[]{:S(2)}) collective-permute-start(f32[128,128]{1,0:T(8,128)S(1)} %get-tuple-element.106), channel_id=1, source_target_pairs={{0,8},{4,12},{8,0},{12,4},{1,9},{5,13},{9,1},{13,5},{2,10},{6,14},... | collective-permute-start | bytes 196616 | tf_op jit(solution)/shard_map/ppermute | solution.py:347
  36.1 5.6 %collective-permute-start.11 = (f32[128,128]{1,0:T(8,128)S(1)}, f32[128,128]{1,0:T(8,128)S(1)}, u32[]{:S(2)}, u32[]{:S(2)}) collective-permute-start(f32[128,128]{1,0:T(8,128)S(1)} %get-tuple-element.107), channel_id=1, source_target_pairs={{0,4},{4,0},{8,12},{12,8},{1,5},{5,1},{9,13},{13,9},{2,6},{6,2},{1... | collective-permute-start | bytes 196616 | tf_op jit(solution)/shard_map/ppermute | solution.py:347
  37.8 6.1 %collective-permute-start.12 = (f32[128,128]{1,0:T(8,128)S(1)}, f32[128,128]{1,0:T(8,128)S(1)}, u32[]{:S(2)}, u32[]{:S(2)}) collective-permute-start(f32[128,128]{1,0:T(8,128)S(1)} %get-tuple-element.108), channel_id=1, source_target_pairs={{0,12},{4,8},{8,4},{12,0},{1,13},{5,9},{9,5},{13,1},{2,14},{6,10},... | collective-permute-start | bytes 196616 | tf_op jit(solution)/shard_map/ppermute | solution.py:347
  44.5 6.9 %collective-permute-start.13 = (f32[128,128]{1,0:T(8,128)S(1)}, f32[128,128]{1,0:T(8,128)S(1)}, u32[]{:S(2)}, u32[]{:S(2)}) collective-permute-start(f32[128,128]{1,0:T(8,128)S(1)} %get-tuple-element.119), channel_id=1, source_target_pairs={{0,8},{4,12},{8,0},{12,4},{1,9},{5,13},{9,1},{13,5},{2,10},{6,14},... | collective-permute-start | bytes 196616 | tf_op jit(solution)/shard_map/ppermute | solution.py:347
  46.2 6.3 %collective-permute-start.14 = (f32[128,128]{1,0:T(8,128)S(1)}, f32[128,128]{1,0:T(8,128)S(1)}, u32[]{:S(2)}, u32[]{:S(2)}) collective-permute-start(f32[128,128]{1,0:T(8,128)S(1)} %get-tuple-element.120), channel_id=1, source_target_pairs={{0,12},{4,8},{8,4},{12,0},{1,13},{5,9},{9,5},{13,1},{2,14},{6,10},... | collective-permute-start | bytes 196616 | tf_op jit(solution)/shard_map/ppermute | solution.py:347
  47.6 5.6 %collective-permute-start.15 = (f32[128,128]{1,0:T(8,128)S(1)}, f32[128,128]{1,0:T(8,128)S(1)}, u32[]{:S(2)}, u32[]{:S(2)}) collective-permute-start(f32[128,128]{1,0:T(8,128)S(1)} %get-tuple-element.121), channel_id=1, source_target_pairs={{0,4},{4,0},{8,12},{12,8},{1,5},{5,1},{9,13},{13,9},{2,6},{6,2},{1... | collective-permute-start | bytes 196616 | tf_op jit(solution)/shard_map/ppermute | solution.py:347
  49.6 7.7 %copy-start.4 = (f32[1,64,1024]{2,1,0:T(8,128)S(1)}, f32[1,64,1024]{2,1,0:T(8,128)}, u32[]{:S(2)}) copy-start(f32[1,64,1024]{2,1,0:T(8,128)} %param.11) | copy-start | bytes 786436
  53.7 7.6 %collective-permute-start.16 = (f32[128,128]{1,0:T(8,128)S(1)}, f32[128,128]{1,0:T(8,128)S(1)}, u32[]{:S(2)}, u32[]{:S(2)}) collective-permute-start(f32[128,128]{1,0:T(8,128)S(1)} %get-tuple-element.127), channel_id=1, source_target_pairs={{0,8},{4,12},{8,0},{12,4},{1,9},{5,13},{9,1},{13,5},{2,10},{6,14},... | collective-permute-start | bytes 196616 | tf_op jit(solution)/shard_map/ppermute | solution.py:347
  54.6 6.7 %collective-permute-start.17 = (f32[128,128]{1,0:T(8,128)S(1)}, f32[128,128]{1,0:T(8,128)S(1)}, u32[]{:S(2)}, u32[]{:S(2)}) collective-permute-start(f32[128,128]{1,0:T(8,128)S(1)} %get-tuple-element.128), channel_id=1, source_target_pairs={{0,12},{4,8},{8,4},{12,0},{1,13},{5,9},{9,5},{13,1},{2,14},{6,10},... | collective-permute-start | bytes 196616 | tf_op jit(solution)/shard_map/ppermute | solution.py:347
  56.3 5.4 %collective-permute-start.18 = (f32[128,128]{1,0:T(8,128)S(1)}, f32[128,128]{1,0:T(8,128)S(1)}, u32[]{:S(2)}, u32[]{:S(2)}) collective-permute-start(f32[128,128]{1,0:T(8,128)S(1)} %get-tuple-element.129), channel_id=1, source_target_pairs={{0,4},{4,0},{8,12},{12,8},{1,5},{5,1},{9,13},{13,9},{2,6},{6,2},{1... | collective-permute-start | bytes 196616 | tf_op jit(solution)/shard_map/ppermute | solution.py:347
  62.1 5.6 %collective-permute-start.19 = (f32[64,128]{1,0:T(8,128)S(1)}, f32[64,128]{1,0:T(8,128)S(1)}, u32[]{:S(2)}, u32[]{:S(2)}) collective-permute-start(f32[64,128]{1,0:T(8,128)S(1)} %get-tuple-element.136), channel_id=1, source_target_pairs={{0,8},{4,12},{8,0},{12,4},{1,9},{5,13},{9,1},{13,5},{2,10},{6,14},... | collective-permute-start | bytes 98312 | tf_op jit(solution)/shard_map/ppermute | solution.py:347
  63.6 5.7 %collective-permute-start.20 = (f32[64,128]{1,0:T(8,128)S(1)}, f32[64,128]{1,0:T(8,128)S(1)}, u32[]{:S(2)}, u32[]{:S(2)}) collective-permute-start(f32[64,128]{1,0:T(8,128)S(1)} %get-tuple-element.137), channel_id=1, source_target_pairs={{0,12},{4,8},{8,4},{12,0},{1,13},{5,9},{9,5},{13,1},{2,14},{6,10},... | collective-permute-start | bytes 98312 | tf_op jit(solution)/shard_map/ppermute | solution.py:347
  65.4 4.2 %collective-permute-start.21 = (f32[64,128]{1,0:T(8,128)S(1)}, f32[64,128]{1,0:T(8,128)S(1)}, u32[]{:S(2)}, u32[]{:S(2)}) collective-permute-start(f32[64,128]{1,0:T(8,128)S(1)} %get-tuple-element.138), channel_id=1, source_target_pairs={{0,4},{4,0},{8,12},{12,8},{1,5},{5,1},{9,13},{13,9},{2,6},{6,2},{1... | collective-permute-start | bytes 98312 | tf_op jit(solution)/shard_map/ppermute | solution.py:347
  69.9 3.4 %collective-permute-start.22 = (f32[64,128]{1,0:T(8,128)S(1)}, f32[64,128]{1,0:T(8,128)S(1)}, u32[]{:S(2)}, u32[]{:S(2)}) collective-permute-start(f32[64,128]{1,0:T(8,128)S(1)} %get-tuple-element.140), channel_id=1, source_target_pairs={{0,3},{1,2},{2,1},{3,0},{4,7},{5,6},{6,5},{7,4},{8,11},{9,10},{10,... | collective-permute-start | bytes 98312 | tf_op jit(solution)/shard_map/ppermute | solution.py:347
  70.0 4.0 %collective-permute-start.23 = (f32[64,128]{1,0:T(8,128)S(1)}, f32[64,128]{1,0:T(8,128)S(1)}, u32[]{:S(2)}, u32[]{:S(2)}) collective-permute-start(f32[64,128]{1,0:T(8,128)S(1)} %get-tuple-element.141), channel_id=1, source_target_pairs={{0,2},{1,3},{2,0},{3,1},{4,6},{5,7},{6,4},{7,5},{8,10},{9,11},{10,... | collective-permute-start | bytes 98312 | tf_op jit(solution)/shard_map/ppermute | solution.py:347
  70.0 4.0 %collective-permute-start.24 = (f32[64,128]{1,0:T(8,128)S(1)}, f32[64,128]{1,0:T(8,128)S(1)}, u32[]{:S(2)}, u32[]{:S(2)}) collective-permute-start(f32[64,128]{1,0:T(8,128)S(1)} %get-tuple-element.142), channel_id=1, source_target_pairs={{0,1},{1,0},{2,3},{3,2},{4,5},{5,4},{6,7},{7,6},{8,9},{9,8},{10,11... | collective-permute-start | bytes 98312 | tf_op jit(solution)/shard_map/ppermute | solution.py:347
  75.0 6.2 %collective-permute-start.25 = (f32[128,128]{1,0:T(8,128)S(1)}, f32[128,128]{1,0:T(8,128)S(1)}, u32[]{:S(2)}, u32[]{:S(2)}) collective-permute-start(f32[128,128]{1,0:T(8,128)S(1)} %get-tuple-element.145), channel_id=1, source_target_pairs={{0,8},{4,12},{8,0},{12,4},{1,9},{5,13},{9,1},{13,5},{2,10},{6,14},... | collective-permute-start | bytes 196616 | tf_op jit(solution)/shard_map/ppermute | solution.py:347
  75.6 5.5 %collective-permute-start.26 = (f32[128,128]{1,0:T(8,128)S(1)}, f32[128,128]{1,0:T(8,128)S(1)}, u32[]{:S(2)}, u32[]{:S(2)}) collective-permute-start(f32[128,128]{1,0:T(8,128)S(1)} %get-tuple-element.146), channel_id=1, source_target_pairs={{0,4},{4,0},{8,12},{12,8},{1,5},{5,1},{9,13},{13,9},{2,6},{6,2},{1... | collective-permute-start | bytes 196616 | tf_op jit(solution)/shard_map/ppermute | solution.py:347
  77.5 6.1 %collective-permute-start.27 = (f32[128,128]{1,0:T(8,128)S(1)}, f32[128,128]{1,0:T(8,128)S(1)}, u32[]{:S(2)}, u32[]{:S(2)}) collective-permute-start(f32[128,128]{1,0:T(8,128)S(1)} %get-tuple-element.147), channel_id=1, source_target_pairs={{0,12},{4,8},{8,4},{12,0},{1,13},{5,9},{9,5},{13,1},{2,14},{6,10},... | collective-permute-start | bytes 196616 | tf_op jit(solution)/shard_map/ppermute | solution.py:347
  84.1 7.2 %collective-permute-start.28 = (f32[128,128]{1,0:T(8,128)S(1)}, f32[128,128]{1,0:T(8,128)S(1)}, u32[]{:S(2)}, u32[]{:S(2)}) collective-permute-start(f32[128,128]{1,0:T(8,128)S(1)} %get-tuple-element.153), channel_id=1, source_target_pairs={{0,8},{4,12},{8,0},{12,4},{1,9},{5,13},{9,1},{13,5},{2,10},{6,14},... | collective-permute-start | bytes 196616 | tf_op jit(solution)/shard_map/ppermute | solution.py:347
  84.5 6.9 %collective-permute-start.29 = (f32[128,128]{1,0:T(8,128)S(1)}, f32[128,128]{1,0:T(8,128)S(1)}, u32[]{:S(2)}, u32[]{:S(2)}) collective-permute-start(f32[128,128]{1,0:T(8,128)S(1)} %get-tuple-element.154), channel_id=1, source_target_pairs={{0,12},{4,8},{8,4},{12,0},{1,13},{5,9},{9,5},{13,1},{2,14},{6,10},... | collective-permute-start | bytes 196616 | tf_op jit(solution)/shard_map/ppermute | solution.py:347
  86.4 5.4 %collective-permute-start.30 = (f32[128,128]{1,0:T(8,128)S(1)}, f32[128,128]{1,0:T(8,128)S(1)}, u32[]{:S(2)}, u32[]{:S(2)}) collective-permute-start(f32[128,128]{1,0:T(8,128)S(1)} %get-tuple-element.155), channel_id=1, source_target_pairs={{0,4},{4,0},{8,12},{12,8},{1,5},{5,1},{9,13},{13,9},{2,6},{6,2},{1... | collective-permute-start | bytes 196616 | tf_op jit(solution)/shard_map/ppermute | solution.py:347

commit v17 on v15

--- a/solution.py
+++ b/solution.py
@@ -83,12 +83,11 @@
     unpack_own, unpack_all, unpack, high, low, image = refs[:6]
     sends, (peers, rows, operator, mult, done) = refs[6:6 + n], refs[6 + n:]
     shared, width = image.shape
-    copies = [
-        pltpu.make_async_copy(source, target, done.at[i])
-        for i, (source, target) in enumerate(
-            ((peers_at, peers), (rows_at, rows), (mult_at, mult), (operator_at.at[pl.ds(0, shared)], operator))
-        )
-    ]
+    pieces = [(peers_at, peers), (rows_at, rows)]
+    for source, target, count in ((mult_at, mult, 2), (operator_at, operator, 4)):
+        step = target.shape[0] // count
+        pieces += [(source.at[pl.ds(k * step, step)], target.at[pl.ds(k * step, step)]) for k in range(count)]
+    copies = [pltpu.make_async_copy(source, target, done.at[i]) for i, (source, target) in enumerate(pieces)]
     for copy in copies:
         copy.start()
     copies[0].wait()
@@ -118,8 +117,8 @@
             out[shared + c:shared + c + 1, :] = jnp.sum(
                 jnp.where(hit, wanted.astype(F32), 0.0), axis=0, keepdims=True
             )
-    copies[2].wait()
-    copies[3].wait()
+    for copy in copies[2:]:
+        copy.wait()
     parts = split(operator[...])
     high[...], low[...] = parts
     value = product(parts, split(mult[...]))
@@ -273,7 +272,7 @@
 
 def lift_kernel(n, m, cap, size, *refs):
     parts = refs[:m + 1]
-    ins, (mult_s, mult_n, image), sends = refs[m + 1:m + 8], refs[m + 8:m + 11], refs[m + 11:]
+    ins, (mult_s, mult_n, image), sends, halves = refs[m + 1:m + 8], refs[m + 8:m + 11], refs[m + 11:-1], refs[-1]
     basis, trial_s, trial_n, floor, high, low, pack = ins
     solved = parts[0][...]
     for part in parts[1:]:
@@ -281,13 +280,20 @@
     shared, width = trial_s.shape
     order = floor.shape[0]
     high_part, low_part = split(solved)
-    lifted = mm(basis[...], jnp.concatenate([high_part, low_part, high_part], axis=0))
-    alive = live(size[0], 0, order, width)
-    first = settle(trial_s[...] + lifted[:shared], floor[:shared], alive[:shared])
-    rest = settle(trial_n[...] + lifted[shared:], floor[shared:], alive[shared:])
-    mult_s[...] = first
-    mult_n[...] = rest
-    value = product((high[...], low[...]), split(jnp.concatenate([first, rest], axis=0)))
+    solved = jnp.concatenate([high_part, low_part, high_part], axis=0)
+    shared, width = trial_s.shape
+    for at in range(0, floor.shape[0], shared):
+        rows = slice(at, at + shared)
+        trial = trial_s[...] if at == 0 else trial_n[at - shared:at, :]
+        alive = live(size[0], at, shared, width)
+        mult = settle(trial + mm(basis[rows, :], solved), floor[rows, :], alive)
+        if at == 0:
+            mult_s[...] = mult
+        else:
+            mult_n[at - shared:at, :] = mult
+        halves[rows, :width], halves[rows, width:] = split(mult)
+    both = mm(high[...], halves[...])
+    value = both[:, :width] + (both[:, width:] + mm(low[...], halves[:, :width]))
     image[...] = value
     send(cap, pack[...], value, sends)
 
@@ -398,7 +404,7 @@
             pltpu.VMEM((1, shared), jnp.int32),
             pltpu.VMEM((shared, order), F32),
             pltpu.VMEM((order, loads), F32),
-            pltpu.SemaphoreType.DMA((4,)),
+            pltpu.SemaphoreType.DMA((8,)),
         ],
         flops=3 * full * shared,
         moved=8 * shared * order,
@@ -494,6 +500,7 @@
             [shape(shared, loads), shape(rest, loads), shape(shared, loads)] + sent,
             flops=3 * full * shared,
             moved=4 * order * shared,
+            scratch=scratch,
             name="lift",
         )
         for inner in range(1, INNER):

time: 89.7 us -> 89.5 us (level)
  no operation moved by 1% of the time
where the time goes in v17:
time: 89.5 us; the launch traced here: 89.3 us
  starting transfers between devices  36.7 us (41%)
  waiting for transfers between devices  32.1 us (36%)
  Pallas kernels  19 us (21%)
  between operations  1.57 us (2%)
    ppermute x30, starting transfers between devices, swap(): return lax.ppermute(block, axis, [(i, i ^ d) for i in range(count)])  36.7 us
    ppermute x30, waiting for transfers between devices, swap(): return lax.ppermute(block, axis, [(i, i ^ d) for i in range(count)])  32.1 us
    pallas_call x25, Pallas kernels, call(): pl.pallas_call(body, out_shape=outs, grid=grid, in_specs=in_specs, out_sp...  19 us
  transfers between devices with their start and end apart: 30, of which 26 were waited for; matrix products, arithmetic and copies ran while one was open for 0% of the time, Pallas kernels for 13%

profile of v17, /device:TPU:0, one launch (start us, length us, event | category | flops | bytes accessed | tf_op | source)
XLA Modules:
  0.0 89.3 jit_solution(13648725831887249432)
XLA Ops:
  0.7 2.1 %first.1 = (bf16[256,256]{1,0:T(8,128)(2,1)S(1)}, bf16[256,768]{1,0:T(8,128)(2,1)S(1)}, bf16[256,384]{1,0:T(8,128)(2,1)S(1)}, bf16[256,1024]{1,0:T(8,128)(2,1)S(...) custom-call(s32[1,256]{1,0:T(1,128)} %bitcast.32, ...), custom_call_target="tpu_custom_call" | custom-call | flops 201326592 | bytes 2097152 | tf_op jit(solution)/shard_map/first/pallas_call | solution.py:49
  2.7 5.1 %collective-permute-start = (f32[264,128]{1,0:T(8,128)S(1)}, f32[264,128]{1,0:T(8,128)S(1)}, u32[]{:S(2)}, u32[]{:S(2)}) collective-permute-start(f32[264,128]{1,0:T(8,128)S(1)} %get-tuple-element.81), channel_id=1, source_target_pairs={{0,12},{4,8},{8,4},{12,0},{1,13},{5,9},{9,5},{13,1},{2,14},{6,10},... | collective-permute-start | bytes 405512 | tf_op jit(solution)/shard_map/ppermute | solution.py:332
  7.9 0.6 collective-permute-start.2
  9.4 2.0 %rest_start.1 = (f32[768,128]{1,0:T(8,128)S(1)}, f32[64,128]{1,0:T(8,128)S(1)}, bf16[768,1024]{1,0:T(8,128)(2,1)S(1)}, bf16[768,1024]{1,0:T(8,128)(2,1)S(1)}) custom-call(s32[1]{0:T(128)S(6)} %copy.15.size, f32[1024,1024]{1,0:T(8,128)S(1)} %bitcast.20, f32[1024,128]{1,0:T(8,128)S(1)} %bitcast.22, f32[1024,128]{1,0:T(8,128)S(1)} %bitcast.23, ...), custom_call_target="tpu_custom_call" | custom-call | flops 603979776 | bytes 6291456 | tf_op jit(solution)/shard_map/rest_start/pallas_call | solution.py:49
  11.4 0.9 collective-permute-done.refs_0_
  12.3 3.1 %collective-permute-done.1.refs_1_ = f32[264,128]{1,0:T(8,128)S(1)} collective-permute-done((f32[264,128]{1,0:T(8,128)S(1)}, f32[264,128]{1,0:T(8,128)S(1)}, u32[]{:S(2)}, u32[]{:S(2)}) %collective-permute-start.1) | collective-permute-done | bytes 135200 | tf_op jit(solution)/shard_map/ppermute | solution.py:332
  15.4 3.9 %collective-permute-done.2.refs_2_ = f32[264,128]{1,0:T(8,128)S(1)} collective-permute-done((f32[264,128]{1,0:T(8,128)S(1)}, f32[264,128]{1,0:T(8,128)S(1)}, u32[]{:S(2)}, u32[]{:S(2)}) %collective-permute-start.2) | collective-permute-done | bytes 135200 | tf_op jit(solution)/shard_map/ppermute | solution.py:332
  19.3 0.5 coarse.2
  19.7 0.8 collective-permute-start.3
  20.5 1.8 %collective-permute-start.4 = (f32[64,128]{1,0:T(8,128)S(1)}, f32[64,128]{1,0:T(8,128)S(1)}, u32[]{:S(2)}, u32[]{:S(2)}) collective-permute-start(f32[64,128]{1,0:T(8,128)S(1)} %get-tuple-element.90), channel_id=1, source_target_pairs={{0,12},{4,8},{8,4},{12,0},{1,13},{5,9},{9,5},{13,1},{2,14},{6,10},... | collective-permute-start | bytes 98312 | tf_op jit(solution)/shard_map/ppermute | solution.py:332
  22.4 0.9 %collective-permute-start.5 = (f32[64,128]{1,0:T(8,128)S(1)}, f32[64,128]{1,0:T(8,128)S(1)}, u32[]{:S(2)}, u32[]{:S(2)}) collective-permute-start(f32[64,128]{1,0:T(8,128)S(1)} %get-tuple-element.91), channel_id=1, source_target_pairs={{0,4},{4,0},{8,12},{12,8},{1,5},{5,1},{9,13},{13,9},{2,6},{6,2},{1... | collective-permute-start | bytes 98312 | tf_op jit(solution)/shard_map/ppermute | solution.py:332
  23.3 0.4 prepare.1
  23.7 1.1 %collective-permute-done.3.refs_1_ = f32[64,128]{1,0:T(8,128)S(1)} collective-permute-done((f32[64,128]{1,0:T(8,128)S(1)}, f32[64,128]{1,0:T(8,128)S(1)}, u32[]{:S(2)}, u32[]{:S(2)}) %collective-permute-start.3) | collective-permute-done | bytes 32800 | tf_op jit(solution)/shard_map/ppermute | solution.py:332
  24.8 1.7 %collective-permute-done.4.refs_2_ = f32[64,128]{1,0:T(8,128)S(1)} collective-permute-done((f32[64,128]{1,0:T(8,128)S(1)}, f32[64,128]{1,0:T(8,128)S(1)}, u32[]{:S(2)}, u32[]{:S(2)}) %collective-permute-start.4) | collective-permute-done | bytes 32800 | tf_op jit(solution)/shard_map/ppermute | solution.py:332
  27.0 1.6 %collective-permute-start.7 = (f32[64,128]{1,0:T(8,128)S(1)}, f32[64,128]{1,0:T(8,128)S(1)}, u32[]{:S(2)}, u32[]{:S(2)}) collective-permute-start(f32[64,128]{1,0:T(8,128)S(1)} %get-tuple-element.94), channel_id=1, source_target_pairs={{0,2},{1,3},{2,0},{3,1},{4,6},{5,7},{6,4},{7,5},{8,10},{9,11},{10,... | collective-permute-start | bytes 98312 | tf_op jit(solution)/shard_map/ppermute | solution.py:332
  29.1 1.5 %collective-permute-done.6.refs_1_ = f32[64,128]{1,0:T(8,128)S(1)} collective-permute-done((f32[64,128]{1,0:T(8,128)S(1)}, f32[64,128]{1,0:T(8,128)S(1)}, u32[]{:S(2)}, u32[]{:S(2)}) %collective-permute-start.6) | collective-permute-done | bytes 32800 | tf_op jit(solution)/shard_map/ppermute | solution.py:332
  30.6 0.4 collective-permute-done.7.refs_2_
  31.0 0.9 lift.2
  31.9 1.7 %collective-permute-start.9 = (f32[128,128]{1,0:T(8,128)S(1)}, f32[128,128]{1,0:T(8,128)S(1)}, u32[]{:S(2)}, u32[]{:S(2)}) collective-permute-start(f32[128,128]{1,0:T(8,128)S(1)} %get-tuple-element.103), channel_id=1, source_target_pairs={{0,8},{4,12},{8,0},{12,4},{1,9},{5,13},{9,1},{13,5},{2,10},{6,14},... | collective-permute-start | bytes 196616 | tf_op jit(solution)/shard_map/ppermute | solution.py:332
  33.5 0.8 collective-permute-start.10
  34.3 2.0 %collective-permute-start.11 = (f32[128,128]{1,0:T(8,128)S(1)}, f32[128,128]{1,0:T(8,128)S(1)}, u32[]{:S(2)}, u32[]{:S(2)}) collective-permute-start(f32[128,128]{1,0:T(8,128)S(1)} %get-tuple-element.105), channel_id=1, source_target_pairs={{0,12},{4,8},{8,4},{12,0},{1,13},{5,9},{9,5},{13,1},{2,14},{6,10},... | collective-permute-start | bytes 196616 | tf_op jit(solution)/shard_map/ppermute | solution.py:332
  36.5 1.5 %rest.3 = (f32[768,128]{1,0:T(8,128)S(1)}, f32[640,128]{1,0:T(8,128)S(1)}) custom-call(s32[1]{0:T(128)S(6)} %copy.15.size, bf16[768,1024]{1,0:T(8,128)(2,1)S(1)} %get-tuple-element.111.high, bf16[768,1024]{1,0:T(8,128)(2,1)S(1)} %get-tuple-element.112.low, f32[256,128]{1,0:T(8,128)S(1)} %get-tuple-element.108.mult_s.refs_5_, ...), custom_call_target="tpu_custom_call" | custom-call | flops 805306368 | bytes 4194304 | tf_op jit(solution)/shard_map/rest/pallas_call | solution.py:49
  38.0 1.4 %collective-permute-done.9.refs_0_ = f32[128,128]{1,0:T(8,128)S(1)} collective-permute-done((f32[128,128]{1,0:T(8,128)S(1)}, f32[128,128]{1,0:T(8,128)S(1)}, u32[]{:S(2)}, u32[]{:S(2)}) %collective-permute-start.9) | collective-permute-done | bytes 65568 | tf_op jit(solution)/shard_map/ppermute | solution.py:332
  39.4 0.7 collective-permute-done.10.refs_1_
  40.1 0.3 collective-permute-done.11.refs_2_
  40.4 0.5 sweep.3
  40.9 1.9 %collective-permute-start.12 = (f32[128,128]{1,0:T(8,128)S(1)}, f32[128,128]{1,0:T(8,128)S(1)}, u32[]{:S(2)}, u32[]{:S(2)}) collective-permute-start(f32[128,128]{1,0:T(8,128)S(1)} %get-tuple-element.115), channel_id=1, source_target_pairs={{0,8},{4,12},{8,0},{12,4},{1,9},{5,13},{9,1},{13,5},{2,10},{6,14},... | collective-permute-start | bytes 196616 | tf_op jit(solution)/shard_map/ppermute | solution.py:332
  42.9 2.0 %collective-permute-start.13 = (f32[128,128]{1,0:T(8,128)S(1)}, f32[128,128]{1,0:T(8,128)S(1)}, u32[]{:S(2)}, u32[]{:S(2)}) collective-permute-start(f32[128,128]{1,0:T(8,128)S(1)} %get-tuple-element.116), channel_id=1, source_target_pairs={{0,12},{4,8},{8,4},{12,0},{1,13},{5,9},{9,5},{13,1},{2,14},{6,10},... | collective-permute-start | bytes 196616 | tf_op jit(solution)/shard_map/ppermute | solution.py:332
  45.1 1.5 %rest.4 = (f32[768,128]{1,0:T(8,128)S(1)}, f32[640,128]{1,0:T(8,128)S(1)}) custom-call(s32[1]{0:T(128)S(6)} %copy.15.size, bf16[768,1024]{1,0:T(8,128)(2,1)S(1)} %get-tuple-element.111.high, bf16[768,1024]{1,0:T(8,128)(2,1)S(1)} %get-tuple-element.112.low, f32[256,128]{1,0:T(8,128)S(1)} %get-tuple-element.119.mult_s.refs_5_, ...), custom_call_target="tpu_custom_call" | custom-call | flops 805306368 | bytes 4194304 | tf_op jit(solution)/shard_map/rest/pallas_call | solution.py:49
  46.6 1.9 %collective-permute-done.12.refs_0_ = f32[128,128]{1,0:T(8,128)S(1)} collective-permute-done((f32[128,128]{1,0:T(8,128)S(1)}, f32[128,128]{1,0:T(8,128)S(1)}, u32[]{:S(2)}, u32[]{:S(2)}) %collective-permute-start.12) | collective-permute-done | bytes 65568 | tf_op jit(solution)/shard_map/ppermute | solution.py:332
  48.5 0.9 %collective-permute-done.13.refs_1_ = f32[128,128]{1,0:T(8,128)S(1)} collective-permute-done((f32[128,128]{1,0:T(8,128)S(1)}, f32[128,128]{1,0:T(8,128)S(1)}, u32[]{:S(2)}, u32[]{:S(2)}) %collective-permute-start.13) | collective-permute-done | bytes 65568 | tf_op jit(solution)/shard_map/ppermute | solution.py:332
  49.4 0.6 collective-permute-done.14.refs_2_
  50.0 0.5 sweep.4
  50.6 0.8 collective-permute-start.15
  51.3 1.9 %collective-permute-start.16 = (f32[128,128]{1,0:T(8,128)S(1)}, f32[128,128]{1,0:T(8,128)S(1)}, u32[]{:S(2)}, u32[]{:S(2)}) collective-permute-start(f32[128,128]{1,0:T(8,128)S(1)} %get-tuple-element.123), channel_id=1, source_target_pairs={{0,12},{4,8},{8,4},{12,0},{1,13},{5,9},{9,5},{13,1},{2,14},{6,10},... | collective-permute-start | bytes 196616 | tf_op jit(solution)/shard_map/ppermute | solution.py:332
  53.3 0.8 collective-permute-start.17
  54.3 1.1 %rest_first.1 = (f32[768,128]{1,0:T(8,128)S(1)}, f32[64,128]{1,0:T(8,128)S(1)}) custom-call(s32[1]{0:T(128)S(6)} %copy.15.size, bf16[768,1024]{1,0:T(8,128)(2,1)S(1)} %get-tuple-element.111.high, bf16[768,1024]{1,0:T(8,128)(2,1)S(1)} %get-tuple-element.112.low, f32[256,128]{1,0:T(8,128)S(1)} %get-tuple-element.126.mult_s.refs_5_, ...), custom_call_target="tpu_custom_call" | custom-call | flops 603979776 | bytes 3145728 | tf_op jit(solution)/shard_map/rest_first/pallas_call | solution.py:49
  55.5 2.5 %collective-permute-done.15.refs_0_ = f32[128,128]{1,0:T(8,128)S(1)} collective-permute-done((f32[128,128]{1,0:T(8,128)S(1)}, f32[128,128]{1,0:T(8,128)S(1)}, u32[]{:S(2)}, u32[]{:S(2)}) %collective-permute-start.15) | collective-permute-done | bytes 65568 | tf_op jit(solution)/shard_map/ppermute | solution.py:332
  57.9 0.6 collective-permute-done.17.refs_2_
  58.6 0.4 coarse.3
  59.0 0.4 collective-permute-start.18
  59.4 2.6 %collective-permute-start.19 = (f32[64,128]{1,0:T(8,128)S(1)}, f32[64,128]{1,0:T(8,128)S(1)}, u32[]{:S(2)}, u32[]{:S(2)}) collective-permute-start(f32[64,128]{1,0:T(8,128)S(1)} %get-tuple-element.131), channel_id=1, source_target_pairs={{0,12},{4,8},{8,4},{12,0},{1,13},{5,9},{9,5},{13,1},{2,14},{6,10},... | collective-permute-start | bytes 98312 | tf_op jit(solution)/shard_map/ppermute | solution.py:332
  62.0 0.6 collective-permute-start.20
  62.5 1.7 %collective-permute-done.18.refs_1_ = f32[64,128]{1,0:T(8,128)S(1)} collective-permute-done((f32[64,128]{1,0:T(8,128)S(1)}, f32[64,128]{1,0:T(8,128)S(1)}, u32[]{:S(2)}, u32[]{:S(2)}) %collective-permute-start.18) | collective-permute-done | bytes 32800 | tf_op jit(solution)/shard_map/ppermute | solution.py:332
  64.2 0.9 %collective-permute-done.19.refs_2_ = f32[64,128]{1,0:T(8,128)S(1)} collective-permute-done((f32[64,128]{1,0:T(8,128)S(1)}, f32[64,128]{1,0:T(8,128)S(1)}, u32[]{:S(2)}, u32[]{:S(2)}) %collective-permute-start.19) | collective-permute-done | bytes 32800 | tf_op jit(solution)/shard_map/ppermute | solution.py:332
  65.1 0.8 collective-permute-done.20.refs_3_
  66.5 1.5 %collective-permute-start.23 = (f32[64,128]{1,0:T(8,128)S(1)}, f32[64,128]{1,0:T(8,128)S(1)}, u32[]{:S(2)}, u32[]{:S(2)}) collective-permute-start(f32[64,128]{1,0:T(8,128)S(1)} %get-tuple-element.136), channel_id=1, source_target_pairs={{0,1},{1,0},{2,3},{3,2},{4,5},{5,4},{6,7},{7,6},{8,9},{9,8},{10,11... | collective-permute-start | bytes 98312 | tf_op jit(solution)/shard_map/ppermute | solution.py:332
  68.1 1.5 %collective-permute-done.21.refs_1_ = f32[64,128]{1,0:T(8,128)S(1)} collective-permute-done((f32[64,128]{1,0:T(8,128)S(1)}, f32[64,128]{1,0:T(8,128)S(1)}, u32[]{:S(2)}, u32[]{:S(2)}) %collective-permute-start.21) | collective-permute-done | bytes 32800 | tf_op jit(solution)/shard_map/ppermute | solution.py:332
  69.6 0.7 collective-permute-done.22.refs_2_
  70.3 0.9 lift.3
  71.1 0.8 collective-permute-start.24
  71.9 1.6 %collective-permute-start.25 = (f32[128,128]{1,0:T(8,128)S(1)}, f32[128,128]{1,0:T(8,128)S(1)}, u32[]{:S(2)}, u32[]{:S(2)}) collective-permute-start(f32[128,128]{1,0:T(8,128)S(1)} %get-tuple-element.140), channel_id=1, source_target_pairs={{0,4},{4,0},{8,12},{12,8},{1,5},{5,1},{9,13},{13,9},{2,6},{6,2},{1... | collective-permute-start | bytes 196616 | tf_op jit(solution)/shard_map/ppermute | solution.py:332
  73.6 2.0 %collective-permute-start.26 = (f32[128,128]{1,0:T(8,128)S(1)}, f32[128,128]{1,0:T(8,128)S(1)}, u32[]{:S(2)}, u32[]{:S(2)}) collective-permute-start(f32[128,128]{1,0:T(8,128)S(1)} %get-tuple-element.141), channel_id=1, source_target_pairs={{0,12},{4,8},{8,4},{12,0},{1,13},{5,9},{9,5},{13,1},{2,14},{6,10},... | collective-permute-start | bytes 196616 | tf_op jit(solution)/shard_map/ppermute | solution.py:332
  75.8 1.5 %rest.5 = (f32[768,128]{1,0:T(8,128)S(1)}, f32[640,128]{1,0:T(8,128)S(1)}) custom-call(s32[1]{0:T(128)S(6)} %copy.15.size, bf16[768,1024]{1,0:T(8,128)(2,1)S(1)} %get-tuple-element.111.high, bf16[768,1024]{1,0:T(8,128)(2,1)S(1)} %get-tuple-element.112.low, f32[256,128]{1,0:T(8,128)S(1)} %get-tuple-element.143.mult_s.refs_5_, ...), custom_call_target="tpu_custom_call" | custom-call | flops 805306368 | bytes 4194304 | tf_op jit(solution)/shard_map/rest/pallas_call | solution.py:49
  77.3 1.0 %collective-permute-done.24.refs_0_ = f32[128,128]{1,0:T(8,128)S(1)} collective-permute-done((f32[128,128]{1,0:T(8,128)S(1)}, f32[128,128]{1,0:T(8,128)S(1)}, u32[]{:S(2)}, u32[]{:S(2)}) %collective-permute-start.24) | collective-permute-done | bytes 65568 | tf_op jit(solution)/shard_map/ppermute | solution.py:332
  78.3 1.4 %collective-permute-done.26.refs_2_ = f32[128,128]{1,0:T(8,128)S(1)} collective-permute-done((f32[128,128]{1,0:T(8,128)S(1)}, f32[128,128]{1,0:T(8,128)S(1)}, u32[]{:S(2)}, u32[]{:S(2)}) %collective-permute-start.26) | collective-permute-done | bytes 65568 | tf_op jit(solution)/shard_map/ppermute | solution.py:332
  79.7 0.5 sweep.5
  80.2 1.4 %collective-permute-start.27 = (f32[128,128]{1,0:T(8,128)S(1)}, f32[128,128]{1,0:T(8,128)S(1)}, u32[]{:S(2)}, u32[]{:S(2)}) collective-permute-start(f32[128,128]{1,0:T(8,128)S(1)} %get-tuple-element.146), channel_id=1, source_target_pairs={{0,8},{4,12},{8,0},{12,4},{1,9},{5,13},{9,1},{13,5},{2,10},{6,14},... | collective-permute-start | bytes 196616 | tf_op jit(solution)/shard_map/ppermute | solution.py:332
  81.6 2.1 %collective-permute-start.28 = (f32[128,128]{1,0:T(8,128)S(1)}, f32[128,128]{1,0:T(8,128)S(1)}, u32[]{:S(2)}, u32[]{:S(2)}) collective-permute-start(f32[128,128]{1,0:T(8,128)S(1)} %get-tuple-element.147), channel_id=1, source_target_pairs={{0,12},{4,8},{8,4},{12,0},{1,13},{5,9},{9,5},{13,1},{2,14},{6,10},... | collective-permute-start | bytes 196616 | tf_op jit(solution)/shard_map/ppermute | solution.py:332
  84.0 1.9 %rest_last.1 = (f32[1024,128]{1,0:T(8,128)}, f32[1024,128]{1,0:T(8,128)}) custom-call(s32[1]{0:T(128)S(6)} %copy.15.size, bf16[768,1024]{1,0:T(8,128)(2,1)S(1)} %get-tuple-element.111.high, bf16[768,1024]{1,0:T(8,128)(2,1)S(1)} %get-tuple-element.112.low, f32[256,128]{1,0:T(8,128)S(1)} %get-tuple-element.150.mult_s.refs_5_, ...), custom_call_target="tpu_custom_call" | custom-call | flops 603979776 | bytes 3145728 | tf_op jit(solution)/shard_map/rest_last/pallas_call | solution.py:49
  85.9 1.0 %collective-permute-done.27.refs_0_ = f32[128,128]{1,0:T(8,128)S(1)} collective-permute-done((f32[128,128]{1,0:T(8,128)S(1)}, f32[128,128]{1,0:T(8,128)S(1)}, u32[]{:S(2)}, u32[]{:S(2)}) %collective-permute-start.27) | collective-permute-done | bytes 65568 | tf_op jit(solution)/shard_map/ppermute | solution.py:332
  86.9 0.8 collective-permute-done.28.refs_1_
  87.7 0.7 collective-permute-done.29.refs_2_
  88.4 0.9 %last.1 = (f32[1024,128]{1,0:T(8,128)}, f32[1024,128]{1,0:T(8,128)}) custom-call(s32[1]{0:T(128)S(6)} %copy.15.size, f32[128,128]{1,0:T(8,128)S(1)} %collective-permute-done.27.refs_0_, f32[128,128]{1,0:T(8,128)S(1)} %collective-permute-done.28.refs_1_, ...), custom_call_target="tpu_custom_call", output_to_operand_aliasing={{0}: (8, {}), {1}: (9, {})} | custom-call | flops 75497472 | bytes 196608 | tf_op jit(solution)/shard_map/last/pallas_call | solution.py:49
  (33 shorter events, 3.0 us)
Async XLA Ops:
  0.6 8.5 %copy-start = (f32[1,1024,128]{2,1,0:T(8,128)S(1)}, f32[1,1024,128]{2,1,0:T(8,128)}, u32[]{:S(2)}) copy-start(f32[1,1024,128]{2,1,0:T(8,128)} %param.12) | copy-start | bytes 1572868
  0.6 8.7 %copy-start.1 = (f32[1,1024,1024]{2,1,0:T(8,128)S(1)}, f32[1,1024,1024]{2,1,0:T(8,128)}, u32[]{:S(2)}) copy-start(f32[1,1024,1024]{2,1,0:T(8,128)} %param.9) | copy-start | bytes 12582916
  0.7 8.7 %copy-start.2 = (f32[1,1024,128]{2,1,0:T(8,128)S(1)}, f32[1,1024,128]{2,1,0:T(8,128)}, u32[]{:S(2)}) copy-start(f32[1,1024,128]{2,1,0:T(8,128)} %param.13) | copy-start | bytes 1572868
  0.7 8.7 %copy-start.3 = (f32[1,64,1024]{2,1,0:T(8,128)S(1)}, f32[1,64,1024]{2,1,0:T(8,128)}, u32[]{:S(2)}) copy-start(f32[1,64,1024]{2,1,0:T(8,128)} %param.11) | copy-start | bytes 786436
  2.7 9.6 %collective-permute-start = (f32[264,128]{1,0:T(8,128)S(1)}, f32[264,128]{1,0:T(8,128)S(1)}, u32[]{:S(2)}, u32[]{:S(2)}) collective-permute-start(f32[264,128]{1,0:T(8,128)S(1)} %get-tuple-element.81), channel_id=1, source_target_pairs={{0,12},{4,8},{8,4},{12,0},{1,13},{5,9},{9,5},{13,1},{2,14},{6,10},... | collective-permute-start | bytes 405512 | tf_op jit(solution)/shard_map/ppermute | solution.py:332
  7.9 7.6 %collective-permute-start.1 = (f32[264,128]{1,0:T(8,128)S(1)}, f32[264,128]{1,0:T(8,128)S(1)}, u32[]{:S(2)}, u32[]{:S(2)}) collective-permute-start(f32[264,128]{1,0:T(8,128)S(1)} %get-tuple-element.82), channel_id=1, source_target_pairs={{0,4},{4,0},{8,12},{12,8},{1,5},{5,1},{9,13},{13,9},{2,6},{6,2},{1... | collective-permute-start | bytes 405512 | tf_op jit(solution)/shard_map/ppermute | solution.py:332
  7.9 11.4 %collective-permute-start.2 = (f32[264,128]{1,0:T(8,128)S(1)}, f32[264,128]{1,0:T(8,128)S(1)}, u32[]{:S(2)}, u32[]{:S(2)}) collective-permute-start(f32[264,128]{1,0:T(8,128)S(1)} %get-tuple-element.83), channel_id=1, source_target_pairs={{0,8},{4,12},{8,0},{12,4},{1,9},{5,13},{9,1},{13,5},{2,10},{6,14},... | collective-permute-start | bytes 405512 | tf_op jit(solution)/shard_map/ppermute | solution.py:332
  11.4 11.9 %copy-start.4 = (f32[256,256]{1,0:T(8,128)S(1)}, f32[256,256]{1,0:T(8,128)}, u32[]{:S(2)}) copy-start(f32[256,256]{1,0:T(8,128)} %tile.3) | copy-start | bytes 786436
  11.4 11.9 %copy-start.5 = (s32[1,1024]{1,0:T(1,128)S(1)}, s32[1,1024]{1,0:T(1,128)}, u32[]{:S(2)}) copy-start(s32[1,1024]{1,0:T(1,128)} %contact.1) | copy-start | bytes 12292
  19.7 5.0 %collective-permute-start.3 = (f32[64,128]{1,0:T(8,128)S(1)}, f32[64,128]{1,0:T(8,128)S(1)}, u32[]{:S(2)}, u32[]{:S(2)}) collective-permute-start(f32[64,128]{1,0:T(8,128)S(1)} %get-tuple-element.89), channel_id=1, source_target_pairs={{0,8},{4,12},{8,0},{12,4},{1,9},{5,13},{9,1},{13,5},{2,10},{6,14},... | collective-permute-start | bytes 98312 | tf_op jit(solution)/shard_map/ppermute | solution.py:332
  20.5 5.9 %collective-permute-start.4 = (f32[64,128]{1,0:T(8,128)S(1)}, f32[64,128]{1,0:T(8,128)S(1)}, u32[]{:S(2)}, u32[]{:S(2)}) collective-permute-start(f32[64,128]{1,0:T(8,128)S(1)} %get-tuple-element.90), channel_id=1, source_target_pairs={{0,12},{4,8},{8,4},{12,0},{1,13},{5,9},{9,5},{13,1},{2,14},{6,10},... | collective-permute-start | bytes 98312 | tf_op jit(solution)/shard_map/ppermute | solution.py:332
  22.4 4.3 %collective-permute-start.5 = (f32[64,128]{1,0:T(8,128)S(1)}, f32[64,128]{1,0:T(8,128)S(1)}, u32[]{:S(2)}, u32[]{:S(2)}) collective-permute-start(f32[64,128]{1,0:T(8,128)S(1)} %get-tuple-element.91), channel_id=1, source_target_pairs={{0,4},{4,0},{8,12},{12,8},{1,5},{5,1},{9,13},{13,9},{2,6},{6,2},{1... | collective-permute-start | bytes 98312 | tf_op jit(solution)/shard_map/ppermute | solution.py:332
  26.9 3.7 %collective-permute-start.6 = (f32[64,128]{1,0:T(8,128)S(1)}, f32[64,128]{1,0:T(8,128)S(1)}, u32[]{:S(2)}, u32[]{:S(2)}) collective-permute-start(f32[64,128]{1,0:T(8,128)S(1)} %get-tuple-element.93), channel_id=1, source_target_pairs={{0,3},{1,2},{2,1},{3,0},{4,7},{5,6},{6,5},{7,4},{8,11},{9,10},{10,... | collective-permute-start | bytes 98312 | tf_op jit(solution)/shard_map/ppermute | solution.py:332
  27.0 4.0 %collective-permute-start.7 = (f32[64,128]{1,0:T(8,128)S(1)}, f32[64,128]{1,0:T(8,128)S(1)}, u32[]{:S(2)}, u32[]{:S(2)}) collective-permute-start(f32[64,128]{1,0:T(8,128)S(1)} %get-tuple-element.94), channel_id=1, source_target_pairs={{0,2},{1,3},{2,0},{3,1},{4,6},{5,7},{6,4},{7,5},{8,10},{9,11},{10,... | collective-permute-start | bytes 98312 | tf_op jit(solution)/shard_map/ppermute | solution.py:332
  28.5 2.5 %collective-permute-start.8 = (f32[64,128]{1,0:T(8,128)S(1)}, f32[64,128]{1,0:T(8,128)S(1)}, u32[]{:S(2)}, u32[]{:S(2)}) collective-permute-start(f32[64,128]{1,0:T(8,128)S(1)} %get-tuple-element.95), channel_id=1, source_target_pairs={{0,1},{1,0},{2,3},{3,2},{4,5},{5,4},{6,7},{7,6},{8,9},{9,8},{10,11... | collective-permute-start | bytes 98312 | tf_op jit(solution)/shard_map/ppermute | solution.py:332
  31.9 7.6 %collective-permute-start.9 = (f32[128,128]{1,0:T(8,128)S(1)}, f32[128,128]{1,0:T(8,128)S(1)}, u32[]{:S(2)}, u32[]{:S(2)}) collective-permute-start(f32[128,128]{1,0:T(8,128)S(1)} %get-tuple-element.103), channel_id=1, source_target_pairs={{0,8},{4,12},{8,0},{12,4},{1,9},{5,13},{9,1},{13,5},{2,10},{6,14},... | collective-permute-start | bytes 196616 | tf_op jit(solution)/shard_map/ppermute | solution.py:332
  33.5 6.6 %collective-permute-start.10 = (f32[128,128]{1,0:T(8,128)S(1)}, f32[128,128]{1,0:T(8,128)S(1)}, u32[]{:S(2)}, u32[]{:S(2)}) collective-permute-start(f32[128,128]{1,0:T(8,128)S(1)} %get-tuple-element.104), channel_id=1, source_target_pairs={{0,4},{4,0},{8,12},{12,8},{1,5},{5,1},{9,13},{13,9},{2,6},{6,2},{1... | collective-permute-start | bytes 196616 | tf_op jit(solution)/shard_map/ppermute | solution.py:332
  34.3 6.1 %collective-permute-start.11 = (f32[128,128]{1,0:T(8,128)S(1)}, f32[128,128]{1,0:T(8,128)S(1)}, u32[]{:S(2)}, u32[]{:S(2)}) collective-permute-start(f32[128,128]{1,0:T(8,128)S(1)} %get-tuple-element.105), channel_id=1, source_target_pairs={{0,12},{4,8},{8,4},{12,0},{1,13},{5,9},{9,5},{13,1},{2,14},{6,10},... | collective-permute-start | bytes 196616 | tf_op jit(solution)/shard_map/ppermute | solution.py:332
  40.9 7.5 %collective-permute-start.12 = (f32[128,128]{1,0:T(8,128)S(1)}, f32[128,128]{1,0:T(8,128)S(1)}, u32[]{:S(2)}, u32[]{:S(2)}) collective-permute-start(f32[128,128]{1,0:T(8,128)S(1)} %get-tuple-element.115), channel_id=1, source_target_pairs={{0,8},{4,12},{8,0},{12,4},{1,9},{5,13},{9,1},{13,5},{2,10},{6,14},... | collective-permute-start | bytes 196616 | tf_op jit(solution)/shard_map/ppermute | solution.py:332
  42.9 6.5 %collective-permute-start.13 = (f32[128,128]{1,0:T(8,128)S(1)}, f32[128,128]{1,0:T(8,128)S(1)}, u32[]{:S(2)}, u32[]{:S(2)}) collective-permute-start(f32[128,128]{1,0:T(8,128)S(1)} %get-tuple-element.116), channel_id=1, source_target_pairs={{0,12},{4,8},{8,4},{12,0},{1,13},{5,9},{9,5},{13,1},{2,14},{6,10},... | collective-permute-start | bytes 196616 | tf_op jit(solution)/shard_map/ppermute | solution.py:332
  44.9 5.1 %collective-permute-start.14 = (f32[128,128]{1,0:T(8,128)S(1)}, f32[128,128]{1,0:T(8,128)S(1)}, u32[]{:S(2)}, u32[]{:S(2)}) collective-permute-start(f32[128,128]{1,0:T(8,128)S(1)} %get-tuple-element.117), channel_id=1, source_target_pairs={{0,4},{4,0},{8,12},{12,8},{1,5},{5,1},{9,13},{13,9},{2,6},{6,2},{1... | collective-permute-start | bytes 196616 | tf_op jit(solution)/shard_map/ppermute | solution.py:332
  50.6 7.4 %collective-permute-start.15 = (f32[128,128]{1,0:T(8,128)S(1)}, f32[128,128]{1,0:T(8,128)S(1)}, u32[]{:S(2)}, u32[]{:S(2)}) collective-permute-start(f32[128,128]{1,0:T(8,128)S(1)} %get-tuple-element.122), channel_id=1, source_target_pairs={{0,8},{4,12},{8,0},{12,4},{1,9},{5,13},{9,1},{13,5},{2,10},{6,14},... | collective-permute-start | bytes 196616 | tf_op jit(solution)/shard_map/ppermute | solution.py:332
  51.3 6.6 %collective-permute-start.16 = (f32[128,128]{1,0:T(8,128)S(1)}, f32[128,128]{1,0:T(8,128)S(1)}, u32[]{:S(2)}, u32[]{:S(2)}) collective-permute-start(f32[128,128]{1,0:T(8,128)S(1)} %get-tuple-element.123), channel_id=1, source_target_pairs={{0,12},{4,8},{8,4},{12,0},{1,13},{5,9},{9,5},{13,1},{2,14},{6,10},... | collective-permute-start | bytes 196616 | tf_op jit(solution)/shard_map/ppermute | solution.py:332
  53.3 5.3 %collective-permute-start.17 = (f32[128,128]{1,0:T(8,128)S(1)}, f32[128,128]{1,0:T(8,128)S(1)}, u32[]{:S(2)}, u32[]{:S(2)}) collective-permute-start(f32[128,128]{1,0:T(8,128)S(1)} %get-tuple-element.124), channel_id=1, source_target_pairs={{0,4},{4,0},{8,12},{12,8},{1,5},{5,1},{9,13},{13,9},{2,6},{6,2},{1... | collective-permute-start | bytes 196616 | tf_op jit(solution)/shard_map/ppermute | solution.py:332
  59.0 5.2 %collective-permute-start.18 = (f32[64,128]{1,0:T(8,128)S(1)}, f32[64,128]{1,0:T(8,128)S(1)}, u32[]{:S(2)}, u32[]{:S(2)}) collective-permute-start(f32[64,128]{1,0:T(8,128)S(1)} %get-tuple-element.130), channel_id=1, source_target_pairs={{0,8},{4,12},{8,0},{12,4},{1,9},{5,13},{9,1},{13,5},{2,10},{6,14},... | collective-permute-start | bytes 98312 | tf_op jit(solution)/shard_map/ppermute | solution.py:332
  59.4 5.7 %collective-permute-start.19 = (f32[64,128]{1,0:T(8,128)S(1)}, f32[64,128]{1,0:T(8,128)S(1)}, u32[]{:S(2)}, u32[]{:S(2)}) collective-permute-start(f32[64,128]{1,0:T(8,128)S(1)} %get-tuple-element.131), channel_id=1, source_target_pairs={{0,12},{4,8},{8,4},{12,0},{1,13},{5,9},{9,5},{13,1},{2,14},{6,10},... | collective-permute-start | bytes 98312 | tf_op jit(solution)/shard_map/ppermute | solution.py:332
  62.0 3.9 %collective-permute-start.20 = (f32[64,128]{1,0:T(8,128)S(1)}, f32[64,128]{1,0:T(8,128)S(1)}, u32[]{:S(2)}, u32[]{:S(2)}) collective-permute-start(f32[64,128]{1,0:T(8,128)S(1)} %get-tuple-element.132), channel_id=1, source_target_pairs={{0,4},{4,0},{8,12},{12,8},{1,5},{5,1},{9,13},{13,9},{2,6},{6,2},{1... | collective-permute-start | bytes 98312 | tf_op jit(solution)/shard_map/ppermute | solution.py:332
  66.2 3.4 %collective-permute-start.21 = (f32[64,128]{1,0:T(8,128)S(1)}, f32[64,128]{1,0:T(8,128)S(1)}, u32[]{:S(2)}, u32[]{:S(2)}) collective-permute-start(f32[64,128]{1,0:T(8,128)S(1)} %get-tuple-element.134), channel_id=1, source_target_pairs={{0,3},{1,2},{2,1},{3,0},{4,7},{5,6},{6,5},{7,4},{8,11},{9,10},{10,... | collective-permute-start | bytes 98312 | tf_op jit(solution)/shard_map/ppermute | solution.py:332
  66.2 4.0 %collective-permute-start.22 = (f32[64,128]{1,0:T(8,128)S(1)}, f32[64,128]{1,0:T(8,128)S(1)}, u32[]{:S(2)}, u32[]{:S(2)}) collective-permute-start(f32[64,128]{1,0:T(8,128)S(1)} %get-tuple-element.135), channel_id=1, source_target_pairs={{0,2},{1,3},{2,0},{3,1},{4,6},{5,7},{6,4},{7,5},{8,10},{9,11},{10,... | collective-permute-start | bytes 98312 | tf_op jit(solution)/shard_map/ppermute | solution.py:332
  66.5 3.7 %collective-permute-start.23 = (f32[64,128]{1,0:T(8,128)S(1)}, f32[64,128]{1,0:T(8,128)S(1)}, u32[]{:S(2)}, u32[]{:S(2)}) collective-permute-start(f32[64,128]{1,0:T(8,128)S(1)} %get-tuple-element.136), channel_id=1, source_target_pairs={{0,1},{1,0},{2,3},{3,2},{4,5},{5,4},{6,7},{7,6},{8,9},{9,8},{10,11... | collective-permute-start | bytes 98312 | tf_op jit(solution)/shard_map/ppermute | solution.py:332
  71.1 7.2 %collective-permute-start.24 = (f32[128,128]{1,0:T(8,128)S(1)}, f32[128,128]{1,0:T(8,128)S(1)}, u32[]{:S(2)}, u32[]{:S(2)}) collective-permute-start(f32[128,128]{1,0:T(8,128)S(1)} %get-tuple-element.139), channel_id=1, source_target_pairs={{0,8},{4,12},{8,0},{12,4},{1,9},{5,13},{9,1},{13,5},{2,10},{6,14},... | collective-permute-start | bytes 196616 | tf_op jit(solution)/shard_map/ppermute | solution.py:332
  71.9 6.3 %collective-permute-start.25 = (f32[128,128]{1,0:T(8,128)S(1)}, f32[128,128]{1,0:T(8,128)S(1)}, u32[]{:S(2)}, u32[]{:S(2)}) collective-permute-start(f32[128,128]{1,0:T(8,128)S(1)} %get-tuple-element.140), channel_id=1, source_target_pairs={{0,4},{4,0},{8,12},{12,8},{1,5},{5,1},{9,13},{13,9},{2,6},{6,2},{1... | collective-permute-start | bytes 196616 | tf_op jit(solution)/shard_map/ppermute | solution.py:332
  73.6 6.1 %collective-permute-start.26 = (f32[128,128]{1,0:T(8,128)S(1)}, f32[128,128]{1,0:T(8,128)S(1)}, u32[]{:S(2)}, u32[]{:S(2)}) collective-permute-start(f32[128,128]{1,0:T(8,128)S(1)} %get-tuple-element.141), channel_id=1, source_target_pairs={{0,12},{4,8},{8,4},{12,0},{1,13},{5,9},{9,5},{13,1},{2,14},{6,10},... | collective-permute-start | bytes 196616 | tf_op jit(solution)/shard_map/ppermute | solution.py:332
  80.2 6.6 %collective-permute-start.27 = (f32[128,128]{1,0:T(8,128)S(1)}, f32[128,128]{1,0:T(8,128)S(1)}, u32[]{:S(2)}, u32[]{:S(2)}) collective-permute-start(f32[128,128]{1,0:T(8,128)S(1)} %get-tuple-element.146), channel_id=1, source_target_pairs={{0,8},{4,12},{8,0},{12,4},{1,9},{5,13},{9,1},{13,5},{2,10},{6,14},... | collective-permute-start | bytes 196616 | tf_op jit(solution)/shard_map/ppermute | solution.py:332
  81.6 6.1 %collective-permute-start.28 = (f32[128,128]{1,0:T(8,128)S(1)}, f32[128,128]{1,0:T(8,128)S(1)}, u32[]{:S(2)}, u32[]{:S(2)}) collective-permute-start(f32[128,128]{1,0:T(8,128)S(1)} %get-tuple-element.147), channel_id=1, source_target_pairs={{0,12},{4,8},{8,4},{12,0},{1,13},{5,9},{9,5},{13,1},{2,14},{6,10},... | collective-permute-start | bytes 196616 | tf_op jit(solution)/shard_map/ppermute | solution.py:332
  83.7 4.7 %collective-permute-start.29 = (f32[128,128]{1,0:T(8,128)S(1)}, f32[128,128]{1,0:T(8,128)S(1)}, u32[]{:S(2)}, u32[]{:S(2)}) collective-permute-start(f32[128,128]{1,0:T(8,128)S(1)} %get-tuple-element.148), channel_id=1, source_target_pairs={{0,4},{4,0},{8,12},{12,8},{1,5},{5,1},{9,13},{13,9},{2,6},{6,2},{1... | collective-permute-start | bytes 196616 | tf_op jit(solution)/shard_map/ppermute | solution.py:332

commit v18 on v17

--- a/solution.py
+++ b/solution.py
@@ -31,10 +31,25 @@
     return both[:, :width] + (both[:, width:] + mm(left_low, right_high))
 
 
-def pick(chosen, value):
+def pick(chosen, value, start=0, stop=None):
     width = value.shape[1]
-    both = mm(chosen, jnp.concatenate(split(value), axis=1))
-    return both[:, :width] + both[:, width:]
+    halves = jnp.concatenate(split(value), axis=1)
+    chunks = []
+    for at in range(start, chosen.shape[0] if stop is None else stop, 128):
+        both = mm(chosen[at:at + 128, :], halves)
+        chunks.append(both[:, :width] + both[:, width:])
+    return chunks[0] if len(chunks) == 1 else jnp.concatenate(chunks, axis=0)
+
+
+def keep(halves, at, value):
+    rows, width = value.shape
+    halves[at:at + rows, :width], halves[at:at + rows, width:] = split(value)
+
+
+def kept_product(high, low, rows, halves):
+    width = halves.shape[1] // 2
+    both = mm(high[rows, :], halves[...])
+    return both[:, :width] + (both[:, width:] + mm(low[rows, :], halves[:, :width]))
 
 
 def live(size, start, rows, width):
@@ -81,7 +96,7 @@
 
 def first_kernel(n, cap, peers_at, rows_at, operator_at, mult_at, *refs):
     unpack_own, unpack_all, unpack, high, low, image = refs[:6]
-    sends, (peers, rows, operator, mult, done) = refs[6:6 + n], refs[6 + n:]
+    sends, (peers, rows, operator, mult, halves, done) = refs[6:6 + n], refs[6 + n:]
     shared, width = image.shape
     pieces = [(peers_at, peers), (rows_at, rows)]
     for source, target, count in ((mult_at, mult, 2), (operator_at, operator, 4)):
@@ -117,11 +132,15 @@
             out[shared + c:shared + c + 1, :] = jnp.sum(
                 jnp.where(hit, wanted.astype(F32), 0.0), axis=0, keepdims=True
             )
-    for copy in copies[2:]:
+    for copy in copies[2:4]:
         copy.wait()
-    parts = split(operator[...])
-    high[...], low[...] = parts
-    value = product(parts, split(mult[...]))
+    for at in range(0, mult.shape[0], shared):
+        keep(halves, at, mult[at:at + shared, :])
+    step = shared // 4
+    for at, copy in zip(range(0, shared, step), copies[4:]):
+        copy.wait()
+        high[at:at + step, :], low[at:at + step, :] = split(operator[at:at + step, :])
+    value = kept_product(high, low, slice(None), halves)
     image[...] = value
     for out in sends:
         out[:shared, :] = value
@@ -169,12 +188,12 @@
     rows = sum(b.shape[0] for b in blocks)
     if rows < unpack.shape[1]:
         blocks.append(jnp.zeros((unpack.shape[1] - rows, blocks[0].shape[1]), F32))
-    return pick(unpack[...], jnp.concatenate(blocks, axis=0))
+    return pick(unpack, jnp.concatenate(blocks, axis=0))
 
 
 def base_kernel(image, unpack_own, gap, base):
     own = image[...]
-    base[...] = gap[:own.shape[0], :] - own + pick(unpack_own[...], own)
+    base[...] = gap[:own.shape[0], :] - own + pick(unpack_own, own)
 
 
 def settle(trial, floor, alive):
@@ -227,7 +246,7 @@
     mult_out[...] = mult
     value = product((top_high[:, shared:], top_low[:, shared:]), split(mult))
     ahead[:shared, :] = value
-    ahead[shared:, :] = pick(pack[...], value)
+    ahead[shared:, :] = pick(pack, value)
 
 
 def rest_last_kernel(size, high, low, mult_s, mult_n, gap, floor, mult_out, residual_out, settled, left, done):
@@ -291,25 +310,25 @@
             mult_s[...] = mult
         else:
             mult_n[at - shared:at, :] = mult
-        halves[rows, :width], halves[rows, width:] = split(mult)
-    both = mm(high[...], halves[...])
-    value = both[:, :width] + (both[:, width:] + mm(low[...], halves[:, :width]))
+        keep(halves, at, mult)
+    value = kept_product(high, low, slice(None), halves)
     image[...] = value
-    send(cap, pack[...], value, sends)
+    send(cap, pack, value, sends)
 
 
 def sweep_kernel(times, cap, size, *refs):
     n = len(times)
     recvs = refs[:n]
     base, unpack, mult, floor, high, low, ahead, mult_out, image_out = refs[n:n + 9]
+    sends, halves = refs[n + 9:-1], refs[-1]
     shared = base.shape[0]
     residual, alive = shared_residual(times, recvs, base, unpack, size)
     value = settle(mult[...] + STEP * residual, floor[:shared, :], alive)
     mult_out[...] = value
-    both = ahead[...] + product((high[...], low[...]), split(value))
-    image_out[...] = both[:shared]
-    for d, out in enumerate(refs[n + 9:]):
-        out[...] = both[shared + d * cap:shared + (d + 1) * cap]
+    keep(halves, 0, value)
+    for out, at in [(out, shared + d * cap) for d, out in enumerate(sends)] + [(image_out, 0)]:
+        rows = slice(at, at + out.shape[0])
+        out[...] = ahead[rows, :] + kept_product(high, low, rows, halves)
 
 
 def last_kernel(times, size, *refs):
@@ -404,6 +423,7 @@
             pltpu.VMEM((1, shared), jnp.int32),
             pltpu.VMEM((shared, order), F32),
             pltpu.VMEM((order, loads), F32),
+            pltpu.VMEM((order, 2 * loads), BF16),
             pltpu.SemaphoreType.DMA((8,)),
         ],
         flops=3 * full * shared,
@@ -553,6 +573,7 @@
                 functools.partial(sweep_kernel, times, cap),
                 (*shadow, stack_high, stack_low, ahead),
                 [shape(shared, loads)] * 2 + sent,
+                scratch=[pltpu.VMEM((shared, 2 * loads), BF16)],
                 name="sweep",
                 **cost,
             )

time: 89.5 us -> 89.8 us (level)
  transfers between devices with their start and end apart: 30 -> 30, of which waited for: 26 -> 26; matrix products, arithmetic and copies ran while one was open for 0% -> 0% of each run, Pallas kernels for 13% -> 12%
where the time goes in v18:
time: 89.8 us; the launch traced here: 89.6 us
  starting transfers between devices  36.7 us (41%)
  waiting for transfers between devices  32.3 us (36%)
  Pallas kernels  19.1 us (21%)
  between operations  1.57 us (2%)
    ppermute x30, starting transfers between devices, swap(): return lax.ppermute(block, axis, [(i, i ^ d) for i in range(count)])  36.7 us
    ppermute x30, waiting for transfers between devices, swap(): return lax.ppermute(block, axis, [(i, i ^ d) for i in range(count)])  32.3 us
    pallas_call x25, Pallas kernels, call(): pl.pallas_call(body, out_shape=outs, grid=grid, in_specs=in_specs, out_sp...  19.1 us
  transfers between devices with their start and end apart: 30, of which 26 were waited for; matrix products, arithmetic and copies ran while one was open for 0% of the time, Pallas kernels for 12%

profile of v18, /device:TPU:0, one launch (start us, length us, event | category | flops | bytes accessed | tf_op | source)
XLA Modules:
  0.0 89.6 jit_solution(2654382063636738388)
XLA Ops:
  0.7 2.1 %first.1 = (bf16[256,256]{1,0:T(8,128)(2,1)S(1)}, bf16[256,768]{1,0:T(8,128)(2,1)S(1)}, bf16[256,384]{1,0:T(8,128)(2,1)S(1)}, bf16[256,1024]{1,0:T(8,128)(2,1)S(...) custom-call(s32[1,256]{1,0:T(1,128)} %bitcast.32, ...), custom_call_target="tpu_custom_call" | custom-call | flops 201326592 | bytes 2097152 | tf_op jit(solution)/shard_map/first/pallas_call | solution.py:64
  2.8 5.1 %collective-permute-start = (f32[264,128]{1,0:T(8,128)S(1)}, f32[264,128]{1,0:T(8,128)S(1)}, u32[]{:S(2)}, u32[]{:S(2)}) collective-permute-start(f32[264,128]{1,0:T(8,128)S(1)} %get-tuple-element.81), channel_id=1, source_target_pairs={{0,12},{4,8},{8,4},{12,0},{1,13},{5,9},{9,5},{13,1},{2,14},{6,10},... | collective-permute-start | bytes 405512 | tf_op jit(solution)/shard_map/ppermute | solution.py:351
  7.9 0.6 collective-permute-start.2
  9.4 2.0 %rest_start.1 = (f32[768,128]{1,0:T(8,128)S(1)}, f32[64,128]{1,0:T(8,128)S(1)}, bf16[768,1024]{1,0:T(8,128)(2,1)S(1)}, bf16[768,1024]{1,0:T(8,128)(2,1)S(1)}) custom-call(s32[1]{0:T(128)S(6)} %copy.15.size, f32[1024,1024]{1,0:T(8,128)S(1)} %bitcast.20, f32[1024,128]{1,0:T(8,128)S(1)} %bitcast.22, f32[1024,128]{1,0:T(8,128)S(1)} %bitcast.23, ...), custom_call_target="tpu_custom_call" | custom-call | flops 603979776 | bytes 6291456 | tf_op jit(solution)/shard_map/rest_start/pallas_call | solution.py:64
  11.5 0.9 collective-permute-done.refs_0_
  12.3 3.1 %collective-permute-done.1.refs_1_ = f32[264,128]{1,0:T(8,128)S(1)} collective-permute-done((f32[264,128]{1,0:T(8,128)S(1)}, f32[264,128]{1,0:T(8,128)S(1)}, u32[]{:S(2)}, u32[]{:S(2)}) %collective-permute-start.1) | collective-permute-done | bytes 135200 | tf_op jit(solution)/shard_map/ppermute | solution.py:351
  15.5 3.9 %collective-permute-done.2.refs_2_ = f32[264,128]{1,0:T(8,128)S(1)} collective-permute-done((f32[264,128]{1,0:T(8,128)S(1)}, f32[264,128]{1,0:T(8,128)S(1)}, u32[]{:S(2)}, u32[]{:S(2)}) %collective-permute-start.2) | collective-permute-done | bytes 135200 | tf_op jit(solution)/shard_map/ppermute | solution.py:351
  19.3 0.4 coarse.2
  19.8 0.8 collective-permute-start.3
  20.6 1.8 %collective-permute-start.4 = (f32[64,128]{1,0:T(8,128)S(1)}, f32[64,128]{1,0:T(8,128)S(1)}, u32[]{:S(2)}, u32[]{:S(2)}) collective-permute-start(f32[64,128]{1,0:T(8,128)S(1)} %get-tuple-element.90), channel_id=1, source_target_pairs={{0,12},{4,8},{8,4},{12,0},{1,13},{5,9},{9,5},{13,1},{2,14},{6,10},... | collective-permute-start | bytes 98312 | tf_op jit(solution)/shard_map/ppermute | solution.py:351
  22.4 0.9 %collective-permute-start.5 = (f32[64,128]{1,0:T(8,128)S(1)}, f32[64,128]{1,0:T(8,128)S(1)}, u32[]{:S(2)}, u32[]{:S(2)}) collective-permute-start(f32[64,128]{1,0:T(8,128)S(1)} %get-tuple-element.91), channel_id=1, source_target_pairs={{0,4},{4,0},{8,12},{12,8},{1,5},{5,1},{9,13},{13,9},{2,6},{6,2},{1... | collective-permute-start | bytes 98312 | tf_op jit(solution)/shard_map/ppermute | solution.py:351
  23.3 0.4 prepare.1
  23.7 1.1 %collective-permute-done.3.refs_1_ = f32[64,128]{1,0:T(8,128)S(1)} collective-permute-done((f32[64,128]{1,0:T(8,128)S(1)}, f32[64,128]{1,0:T(8,128)S(1)}, u32[]{:S(2)}, u32[]{:S(2)}) %collective-permute-start.3) | collective-permute-done | bytes 32800 | tf_op jit(solution)/shard_map/ppermute | solution.py:351
  24.8 1.7 %collective-permute-done.4.refs_2_ = f32[64,128]{1,0:T(8,128)S(1)} collective-permute-done((f32[64,128]{1,0:T(8,128)S(1)}, f32[64,128]{1,0:T(8,128)S(1)}, u32[]{:S(2)}, u32[]{:S(2)}) %collective-permute-start.4) | collective-permute-done | bytes 32800 | tf_op jit(solution)/shard_map/ppermute | solution.py:351
  27.0 1.6 %collective-permute-start.7 = (f32[64,128]{1,0:T(8,128)S(1)}, f32[64,128]{1,0:T(8,128)S(1)}, u32[]{:S(2)}, u32[]{:S(2)}) collective-permute-start(f32[64,128]{1,0:T(8,128)S(1)} %get-tuple-element.94), channel_id=1, source_target_pairs={{0,2},{1,3},{2,0},{3,1},{4,6},{5,7},{6,4},{7,5},{8,10},{9,11},{10,... | collective-permute-start | bytes 98312 | tf_op jit(solution)/shard_map/ppermute | solution.py:351
  29.1 1.5 %collective-permute-done.6.refs_1_ = f32[64,128]{1,0:T(8,128)S(1)} collective-permute-done((f32[64,128]{1,0:T(8,128)S(1)}, f32[64,128]{1,0:T(8,128)S(1)}, u32[]{:S(2)}, u32[]{:S(2)}) %collective-permute-start.6) | collective-permute-done | bytes 32800 | tf_op jit(solution)/shard_map/ppermute | solution.py:351
  30.6 0.4 collective-permute-done.7.refs_2_
  31.0 0.9 %lift.2 = (f32[256,128]{1,0:T(8,128)S(1)}, f32[768,128]{1,0:T(8,128)S(1)}, f32[256,128]{1,0:T(8,128)S(1)}, f32[128,128]{1,0:T(8,128)S(1)}, f32[128,128]{1,0:T(8,128)S(1)}, /*index=5*/f32[128,128]{1,0:T(8,128)S(1)}) custom-call(s32[1]{0:T(128)S(6)} %copy.15.size, f32[64,128]{1,0:T(8,128)S(1)} %get-tuple-element.92.refs_0_, ...), custom_call_target="tpu_custom_call" | custom-call | flops 201326592 | bytes 1048576 | tf_op jit(solution)/shard_map/lift/pallas_call | solution.py:64
  31.9 1.7 %collective-permute-start.9 = (f32[128,128]{1,0:T(8,128)S(1)}, f32[128,128]{1,0:T(8,128)S(1)}, u32[]{:S(2)}, u32[]{:S(2)}) collective-permute-start(f32[128,128]{1,0:T(8,128)S(1)} %get-tuple-element.103), channel_id=1, source_target_pairs={{0,8},{4,12},{8,0},{12,4},{1,9},{5,13},{9,1},{13,5},{2,10},{6,14},... | collective-permute-start | bytes 196616 | tf_op jit(solution)/shard_map/ppermute | solution.py:351
  33.6 0.8 collective-permute-start.10
  34.4 2.0 %collective-permute-start.11 = (f32[128,128]{1,0:T(8,128)S(1)}, f32[128,128]{1,0:T(8,128)S(1)}, u32[]{:S(2)}, u32[]{:S(2)}) collective-permute-start(f32[128,128]{1,0:T(8,128)S(1)} %get-tuple-element.105), channel_id=1, source_target_pairs={{0,12},{4,8},{8,4},{12,0},{1,13},{5,9},{9,5},{13,1},{2,14},{6,10},... | collective-permute-start | bytes 196616 | tf_op jit(solution)/shard_map/ppermute | solution.py:351
  36.6 1.4 %rest.3 = (f32[768,128]{1,0:T(8,128)S(1)}, f32[640,128]{1,0:T(8,128)S(1)}) custom-call(s32[1]{0:T(128)S(6)} %copy.15.size, bf16[768,1024]{1,0:T(8,128)(2,1)S(1)} %get-tuple-element.111.high, bf16[768,1024]{1,0:T(8,128)(2,1)S(1)} %get-tuple-element.112.low, f32[256,128]{1,0:T(8,128)S(1)} %get-tuple-element.108.mult_s.refs_5_, ...), custom_call_target="tpu_custom_call" | custom-call | flops 805306368 | bytes 4194304 | tf_op jit(solution)/shard_map/rest/pallas_call | solution.py:64
  38.0 1.5 %collective-permute-done.9.refs_0_ = f32[128,128]{1,0:T(8,128)S(1)} collective-permute-done((f32[128,128]{1,0:T(8,128)S(1)}, f32[128,128]{1,0:T(8,128)S(1)}, u32[]{:S(2)}, u32[]{:S(2)}) %collective-permute-start.9) | collective-permute-done | bytes 65568 | tf_op jit(solution)/shard_map/ppermute | solution.py:351
  39.5 0.7 collective-permute-done.10.refs_1_
  40.5 0.6 sweep.3
  41.1 1.9 %collective-permute-start.12 = (f32[128,128]{1,0:T(8,128)S(1)}, f32[128,128]{1,0:T(8,128)S(1)}, u32[]{:S(2)}, u32[]{:S(2)}) collective-permute-start(f32[128,128]{1,0:T(8,128)S(1)} %get-tuple-element.115), channel_id=1, source_target_pairs={{0,8},{4,12},{8,0},{12,4},{1,9},{5,13},{9,1},{13,5},{2,10},{6,14},... | collective-permute-start | bytes 196616 | tf_op jit(solution)/shard_map/ppermute | solution.py:351
  43.0 2.0 %collective-permute-start.13 = (f32[128,128]{1,0:T(8,128)S(1)}, f32[128,128]{1,0:T(8,128)S(1)}, u32[]{:S(2)}, u32[]{:S(2)}) collective-permute-start(f32[128,128]{1,0:T(8,128)S(1)} %get-tuple-element.116), channel_id=1, source_target_pairs={{0,12},{4,8},{8,4},{12,0},{1,13},{5,9},{9,5},{13,1},{2,14},{6,10},... | collective-permute-start | bytes 196616 | tf_op jit(solution)/shard_map/ppermute | solution.py:351
  45.2 1.4 %rest.4 = (f32[768,128]{1,0:T(8,128)S(1)}, f32[640,128]{1,0:T(8,128)S(1)}) custom-call(s32[1]{0:T(128)S(6)} %copy.15.size, bf16[768,1024]{1,0:T(8,128)(2,1)S(1)} %get-tuple-element.111.high, bf16[768,1024]{1,0:T(8,128)(2,1)S(1)} %get-tuple-element.112.low, f32[256,128]{1,0:T(8,128)S(1)} %get-tuple-element.119.mult_s.refs_5_, ...), custom_call_target="tpu_custom_call" | custom-call | flops 805306368 | bytes 4194304 | tf_op jit(solution)/shard_map/rest/pallas_call | solution.py:64
  46.6 2.0 %collective-permute-done.12.refs_0_ = f32[128,128]{1,0:T(8,128)S(1)} collective-permute-done((f32[128,128]{1,0:T(8,128)S(1)}, f32[128,128]{1,0:T(8,128)S(1)}, u32[]{:S(2)}, u32[]{:S(2)}) %collective-permute-start.12) | collective-permute-done | bytes 65568 | tf_op jit(solution)/shard_map/ppermute | solution.py:351
  48.6 0.9 %collective-permute-done.13.refs_1_ = f32[128,128]{1,0:T(8,128)S(1)} collective-permute-done((f32[128,128]{1,0:T(8,128)S(1)}, f32[128,128]{1,0:T(8,128)S(1)}, u32[]{:S(2)}, u32[]{:S(2)}) %collective-permute-start.13) | collective-permute-done | bytes 65568 | tf_op jit(solution)/shard_map/ppermute | solution.py:351
  49.5 0.6 collective-permute-done.14.refs_2_
  50.2 0.6 sweep.4
  50.7 0.8 collective-permute-start.15
  51.5 1.9 %collective-permute-start.16 = (f32[128,128]{1,0:T(8,128)S(1)}, f32[128,128]{1,0:T(8,128)S(1)}, u32[]{:S(2)}, u32[]{:S(2)}) collective-permute-start(f32[128,128]{1,0:T(8,128)S(1)} %get-tuple-element.123), channel_id=1, source_target_pairs={{0,12},{4,8},{8,4},{12,0},{1,13},{5,9},{9,5},{13,1},{2,14},{6,10},... | collective-permute-start | bytes 196616 | tf_op jit(solution)/shard_map/ppermute | solution.py:351
  53.5 0.8 collective-permute-start.17
  54.5 1.1 %rest_first.1 = (f32[768,128]{1,0:T(8,128)S(1)}, f32[64,128]{1,0:T(8,128)S(1)}) custom-call(s32[1]{0:T(128)S(6)} %copy.15.size, bf16[768,1024]{1,0:T(8,128)(2,1)S(1)} %get-tuple-element.111.high, bf16[768,1024]{1,0:T(8,128)(2,1)S(1)} %get-tuple-element.112.low, f32[256,128]{1,0:T(8,128)S(1)} %get-tuple-element.126.mult_s.refs_5_, ...), custom_call_target="tpu_custom_call" | custom-call | flops 603979776 | bytes 3145728 | tf_op jit(solution)/shard_map/rest_first/pallas_call | solution.py:64
  55.6 2.4 %collective-permute-done.15.refs_0_ = f32[128,128]{1,0:T(8,128)S(1)} collective-permute-done((f32[128,128]{1,0:T(8,128)S(1)}, f32[128,128]{1,0:T(8,128)S(1)}, u32[]{:S(2)}, u32[]{:S(2)}) %collective-permute-start.15) | collective-permute-done | bytes 65568 | tf_op jit(solution)/shard_map/ppermute | solution.py:351
  58.1 0.6 collective-permute-done.17.refs_2_
  58.7 0.4 coarse.3
  59.1 0.4 collective-permute-start.18
  59.6 2.6 %collective-permute-start.19 = (f32[64,128]{1,0:T(8,128)S(1)}, f32[64,128]{1,0:T(8,128)S(1)}, u32[]{:S(2)}, u32[]{:S(2)}) collective-permute-start(f32[64,128]{1,0:T(8,128)S(1)} %get-tuple-element.131), channel_id=1, source_target_pairs={{0,12},{4,8},{8,4},{12,0},{1,13},{5,9},{9,5},{13,1},{2,14},{6,10},... | collective-permute-start | bytes 98312 | tf_op jit(solution)/shard_map/ppermute | solution.py:351
  62.1 0.6 collective-permute-start.20
  62.7 1.7 %collective-permute-done.18.refs_1_ = f32[64,128]{1,0:T(8,128)S(1)} collective-permute-done((f32[64,128]{1,0:T(8,128)S(1)}, f32[64,128]{1,0:T(8,128)S(1)}, u32[]{:S(2)}, u32[]{:S(2)}) %collective-permute-start.18) | collective-permute-done | bytes 32800 | tf_op jit(solution)/shard_map/ppermute | solution.py:351
  64.4 0.9 %collective-permute-done.19.refs_2_ = f32[64,128]{1,0:T(8,128)S(1)} collective-permute-done((f32[64,128]{1,0:T(8,128)S(1)}, f32[64,128]{1,0:T(8,128)S(1)}, u32[]{:S(2)}, u32[]{:S(2)}) %collective-permute-start.19) | collective-permute-done | bytes 32800 | tf_op jit(solution)/shard_map/ppermute | solution.py:351
  65.3 0.8 collective-permute-done.20.refs_3_
  66.4 0.3 collective-permute-start.22
  66.7 1.5 %collective-permute-start.23 = (f32[64,128]{1,0:T(8,128)S(1)}, f32[64,128]{1,0:T(8,128)S(1)}, u32[]{:S(2)}, u32[]{:S(2)}) collective-permute-start(f32[64,128]{1,0:T(8,128)S(1)} %get-tuple-element.136), channel_id=1, source_target_pairs={{0,1},{1,0},{2,3},{3,2},{4,5},{5,4},{6,7},{7,6},{8,9},{9,8},{10,11... | collective-permute-start | bytes 98312 | tf_op jit(solution)/shard_map/ppermute | solution.py:351
  68.3 1.5 %collective-permute-done.21.refs_1_ = f32[64,128]{1,0:T(8,128)S(1)} collective-permute-done((f32[64,128]{1,0:T(8,128)S(1)}, f32[64,128]{1,0:T(8,128)S(1)}, u32[]{:S(2)}, u32[]{:S(2)}) %collective-permute-start.21) | collective-permute-done | bytes 32800 | tf_op jit(solution)/shard_map/ppermute | solution.py:351
  69.7 0.7 collective-permute-done.22.refs_2_
  70.4 0.9 %lift.3 = (f32[256,128]{1,0:T(8,128)S(1)}, f32[768,128]{1,0:T(8,128)S(1)}, f32[256,128]{1,0:T(8,128)S(1)}, f32[128,128]{1,0:T(8,128)S(1)}, f32[128,128]{1,0:T(8,128)S(1)}, /*index=5*/f32[128,128]{1,0:T(8,128)S(1)}) custom-call(s32[1]{0:T(128)S(6)} %copy.15.size, f32[64,128]{1,0:T(8,128)S(1)} %get-tuple-element.133.refs_0_, ...), custom_call_target="tpu_custom_call" | custom-call | flops 201326592 | bytes 1048576 | tf_op jit(solution)/shard_map/lift/pallas_call | solution.py:64
  71.4 0.8 collective-permute-start.24
  72.2 1.6 %collective-permute-start.25 = (f32[128,128]{1,0:T(8,128)S(1)}, f32[128,128]{1,0:T(8,128)S(1)}, u32[]{:S(2)}, u32[]{:S(2)}) collective-permute-start(f32[128,128]{1,0:T(8,128)S(1)} %get-tuple-element.140), channel_id=1, source_target_pairs={{0,4},{4,0},{8,12},{12,8},{1,5},{5,1},{9,13},{13,9},{2,6},{6,2},{1... | collective-permute-start | bytes 196616 | tf_op jit(solution)/shard_map/ppermute | solution.py:351
  73.8 2.0 %collective-permute-start.26 = (f32[128,128]{1,0:T(8,128)S(1)}, f32[128,128]{1,0:T(8,128)S(1)}, u32[]{:S(2)}, u32[]{:S(2)}) collective-permute-start(f32[128,128]{1,0:T(8,128)S(1)} %get-tuple-element.141), channel_id=1, source_target_pairs={{0,12},{4,8},{8,4},{12,0},{1,13},{5,9},{9,5},{13,1},{2,14},{6,10},... | collective-permute-start | bytes 196616 | tf_op jit(solution)/shard_map/ppermute | solution.py:351
  76.0 1.4 %rest.5 = (f32[768,128]{1,0:T(8,128)S(1)}, f32[640,128]{1,0:T(8,128)S(1)}) custom-call(s32[1]{0:T(128)S(6)} %copy.15.size, bf16[768,1024]{1,0:T(8,128)(2,1)S(1)} %get-tuple-element.111.high, bf16[768,1024]{1,0:T(8,128)(2,1)S(1)} %get-tuple-element.112.low, f32[256,128]{1,0:T(8,128)S(1)} %get-tuple-element.143.mult_s.refs_5_, ...), custom_call_target="tpu_custom_call" | custom-call | flops 805306368 | bytes 4194304 | tf_op jit(solution)/shard_map/rest/pallas_call | solution.py:64
  77.4 1.1 %collective-permute-done.24.refs_0_ = f32[128,128]{1,0:T(8,128)S(1)} collective-permute-done((f32[128,128]{1,0:T(8,128)S(1)}, f32[128,128]{1,0:T(8,128)S(1)}, u32[]{:S(2)}, u32[]{:S(2)}) %collective-permute-start.24) | collective-permute-done | bytes 65568 | tf_op jit(solution)/shard_map/ppermute | solution.py:351
  78.5 1.4 %collective-permute-done.26.refs_2_ = f32[128,128]{1,0:T(8,128)S(1)} collective-permute-done((f32[128,128]{1,0:T(8,128)S(1)}, f32[128,128]{1,0:T(8,128)S(1)}, u32[]{:S(2)}, u32[]{:S(2)}) %collective-permute-start.26) | collective-permute-done | bytes 65568 | tf_op jit(solution)/shard_map/ppermute | solution.py:351
  79.9 0.6 sweep.5
  80.5 1.4 %collective-permute-start.27 = (f32[128,128]{1,0:T(8,128)S(1)}, f32[128,128]{1,0:T(8,128)S(1)}, u32[]{:S(2)}, u32[]{:S(2)}) collective-permute-start(f32[128,128]{1,0:T(8,128)S(1)} %get-tuple-element.146), channel_id=1, source_target_pairs={{0,8},{4,12},{8,0},{12,4},{1,9},{5,13},{9,1},{13,5},{2,10},{6,14},... | collective-permute-start | bytes 196616 | tf_op jit(solution)/shard_map/ppermute | solution.py:351
  81.9 2.1 %collective-permute-start.28 = (f32[128,128]{1,0:T(8,128)S(1)}, f32[128,128]{1,0:T(8,128)S(1)}, u32[]{:S(2)}, u32[]{:S(2)}) collective-permute-start(f32[128,128]{1,0:T(8,128)S(1)} %get-tuple-element.147), channel_id=1, source_target_pairs={{0,12},{4,8},{8,4},{12,0},{1,13},{5,9},{9,5},{13,1},{2,14},{6,10},... | collective-permute-start | bytes 196616 | tf_op jit(solution)/shard_map/ppermute | solution.py:351
  84.2 1.9 %rest_last.1 = (f32[1024,128]{1,0:T(8,128)}, f32[1024,128]{1,0:T(8,128)}) custom-call(s32[1]{0:T(128)S(6)} %copy.15.size, bf16[768,1024]{1,0:T(8,128)(2,1)S(1)} %get-tuple-element.111.high, bf16[768,1024]{1,0:T(8,128)(2,1)S(1)} %get-tuple-element.112.low, f32[256,128]{1,0:T(8,128)S(1)} %get-tuple-element.150.mult_s.refs_5_, ...), custom_call_target="tpu_custom_call" | custom-call | flops 603979776 | bytes 3145728 | tf_op jit(solution)/shard_map/rest_last/pallas_call | solution.py:64
  86.1 1.1 %collective-permute-done.27.refs_0_ = f32[128,128]{1,0:T(8,128)S(1)} collective-permute-done((f32[128,128]{1,0:T(8,128)S(1)}, f32[128,128]{1,0:T(8,128)S(1)}, u32[]{:S(2)}, u32[]{:S(2)}) %collective-permute-start.27) | collective-permute-done | bytes 65568 | tf_op jit(solution)/shard_map/ppermute | solution.py:351
  87.2 0.8 collective-permute-done.28.refs_1_
  88.0 0.7 collective-permute-done.29.refs_2_
  88.7 0.9 %last.1 = (f32[1024,128]{1,0:T(8,128)}, f32[1024,128]{1,0:T(8,128)}) custom-call(s32[1]{0:T(128)S(6)} %copy.15.size, f32[128,128]{1,0:T(8,128)S(1)} %collective-permute-done.27.refs_0_, f32[128,128]{1,0:T(8,128)S(1)} %collective-permute-done.28.refs_1_, ...), custom_call_target="tpu_custom_call", output_to_operand_aliasing={{0}: (8, {}), {1}: (9, {})} | custom-call | flops 75497472 | bytes 196608 | tf_op jit(solution)/shard_map/last/pallas_call | solution.py:64
  (33 shorter events, 3.0 us)
Async XLA Ops:
  0.6 8.5 %copy-start = (f32[1,1024,128]{2,1,0:T(8,128)S(1)}, f32[1,1024,128]{2,1,0:T(8,128)}, u32[]{:S(2)}) copy-start(f32[1,1024,128]{2,1,0:T(8,128)} %param.12) | copy-start | bytes 1572868
  0.6 8.7 %copy-start.1 = (f32[1,1024,1024]{2,1,0:T(8,128)S(1)}, f32[1,1024,1024]{2,1,0:T(8,128)}, u32[]{:S(2)}) copy-start(f32[1,1024,1024]{2,1,0:T(8,128)} %param.9) | copy-start | bytes 12582916
  0.7 8.7 %copy-start.2 = (f32[1,1024,128]{2,1,0:T(8,128)S(1)}, f32[1,1024,128]{2,1,0:T(8,128)}, u32[]{:S(2)}) copy-start(f32[1,1024,128]{2,1,0:T(8,128)} %param.13) | copy-start | bytes 1572868
  0.7 8.7 %copy-start.3 = (f32[1,64,1024]{2,1,0:T(8,128)S(1)}, f32[1,64,1024]{2,1,0:T(8,128)}, u32[]{:S(2)}) copy-start(f32[1,64,1024]{2,1,0:T(8,128)} %param.11) | copy-start | bytes 786436
  2.8 9.6 %collective-permute-start = (f32[264,128]{1,0:T(8,128)S(1)}, f32[264,128]{1,0:T(8,128)S(1)}, u32[]{:S(2)}, u32[]{:S(2)}) collective-permute-start(f32[264,128]{1,0:T(8,128)S(1)} %get-tuple-element.81), channel_id=1, source_target_pairs={{0,12},{4,8},{8,4},{12,0},{1,13},{5,9},{9,5},{13,1},{2,14},{6,10},... | collective-permute-start | bytes 405512 | tf_op jit(solution)/shard_map/ppermute | solution.py:351
  7.9 7.6 %collective-permute-start.1 = (f32[264,128]{1,0:T(8,128)S(1)}, f32[264,128]{1,0:T(8,128)S(1)}, u32[]{:S(2)}, u32[]{:S(2)}) collective-permute-start(f32[264,128]{1,0:T(8,128)S(1)} %get-tuple-element.82), channel_id=1, source_target_pairs={{0,4},{4,0},{8,12},{12,8},{1,5},{5,1},{9,13},{13,9},{2,6},{6,2},{1... | collective-permute-start | bytes 405512 | tf_op jit(solution)/shard_map/ppermute | solution.py:351
  7.9 11.4 %collective-permute-start.2 = (f32[264,128]{1,0:T(8,128)S(1)}, f32[264,128]{1,0:T(8,128)S(1)}, u32[]{:S(2)}, u32[]{:S(2)}) collective-permute-start(f32[264,128]{1,0:T(8,128)S(1)} %get-tuple-element.83), channel_id=1, source_target_pairs={{0,8},{4,12},{8,0},{12,4},{1,9},{5,13},{9,1},{13,5},{2,10},{6,14},... | collective-permute-start | bytes 405512 | tf_op jit(solution)/shard_map/ppermute | solution.py:351
  11.4 11.9 %copy-start.4 = (f32[256,256]{1,0:T(8,128)S(1)}, f32[256,256]{1,0:T(8,128)}, u32[]{:S(2)}) copy-start(f32[256,256]{1,0:T(8,128)} %tile.3) | copy-start | bytes 786436
  11.4 11.9 %copy-start.5 = (s32[1,1024]{1,0:T(1,128)S(1)}, s32[1,1024]{1,0:T(1,128)}, u32[]{:S(2)}) copy-start(s32[1,1024]{1,0:T(1,128)} %contact.1) | copy-start | bytes 12292
  19.8 5.0 %collective-permute-start.3 = (f32[64,128]{1,0:T(8,128)S(1)}, f32[64,128]{1,0:T(8,128)S(1)}, u32[]{:S(2)}, u32[]{:S(2)}) collective-permute-start(f32[64,128]{1,0:T(8,128)S(1)} %get-tuple-element.89), channel_id=1, source_target_pairs={{0,8},{4,12},{8,0},{12,4},{1,9},{5,13},{9,1},{13,5},{2,10},{6,14},... | collective-permute-start | bytes 98312 | tf_op jit(solution)/shard_map/ppermute | solution.py:351
  20.6 5.9 %collective-permute-start.4 = (f32[64,128]{1,0:T(8,128)S(1)}, f32[64,128]{1,0:T(8,128)S(1)}, u32[]{:S(2)}, u32[]{:S(2)}) collective-permute-start(f32[64,128]{1,0:T(8,128)S(1)} %get-tuple-element.90), channel_id=1, source_target_pairs={{0,12},{4,8},{8,4},{12,0},{1,13},{5,9},{9,5},{13,1},{2,14},{6,10},... | collective-permute-start | bytes 98312 | tf_op jit(solution)/shard_map/ppermute | solution.py:351
  22.4 4.3 %collective-permute-start.5 = (f32[64,128]{1,0:T(8,128)S(1)}, f32[64,128]{1,0:T(8,128)S(1)}, u32[]{:S(2)}, u32[]{:S(2)}) collective-permute-start(f32[64,128]{1,0:T(8,128)S(1)} %get-tuple-element.91), channel_id=1, source_target_pairs={{0,4},{4,0},{8,12},{12,8},{1,5},{5,1},{9,13},{13,9},{2,6},{6,2},{1... | collective-permute-start | bytes 98312 | tf_op jit(solution)/shard_map/ppermute | solution.py:351
  26.9 3.7 %collective-permute-start.6 = (f32[64,128]{1,0:T(8,128)S(1)}, f32[64,128]{1,0:T(8,128)S(1)}, u32[]{:S(2)}, u32[]{:S(2)}) collective-permute-start(f32[64,128]{1,0:T(8,128)S(1)} %get-tuple-element.93), channel_id=1, source_target_pairs={{0,3},{1,2},{2,1},{3,0},{4,7},{5,6},{6,5},{7,4},{8,11},{9,10},{10,... | collective-permute-start | bytes 98312 | tf_op jit(solution)/shard_map/ppermute | solution.py:351
  27.0 4.0 %collective-permute-start.7 = (f32[64,128]{1,0:T(8,128)S(1)}, f32[64,128]{1,0:T(8,128)S(1)}, u32[]{:S(2)}, u32[]{:S(2)}) collective-permute-start(f32[64,128]{1,0:T(8,128)S(1)} %get-tuple-element.94), channel_id=1, source_target_pairs={{0,2},{1,3},{2,0},{3,1},{4,6},{5,7},{6,4},{7,5},{8,10},{9,11},{10,... | collective-permute-start | bytes 98312 | tf_op jit(solution)/shard_map/ppermute | solution.py:351
  28.5 2.5 %collective-permute-start.8 = (f32[64,128]{1,0:T(8,128)S(1)}, f32[64,128]{1,0:T(8,128)S(1)}, u32[]{:S(2)}, u32[]{:S(2)}) collective-permute-start(f32[64,128]{1,0:T(8,128)S(1)} %get-tuple-element.95), channel_id=1, source_target_pairs={{0,1},{1,0},{2,3},{3,2},{4,5},{5,4},{6,7},{7,6},{8,9},{9,8},{10,11... | collective-permute-start | bytes 98312 | tf_op jit(solution)/shard_map/ppermute | solution.py:351
  31.9 7.6 %collective-permute-start.9 = (f32[128,128]{1,0:T(8,128)S(1)}, f32[128,128]{1,0:T(8,128)S(1)}, u32[]{:S(2)}, u32[]{:S(2)}) collective-permute-start(f32[128,128]{1,0:T(8,128)S(1)} %get-tuple-element.103), channel_id=1, source_target_pairs={{0,8},{4,12},{8,0},{12,4},{1,9},{5,13},{9,1},{13,5},{2,10},{6,14},... | collective-permute-start | bytes 196616 | tf_op jit(solution)/shard_map/ppermute | solution.py:351
  33.6 6.6 %collective-permute-start.10 = (f32[128,128]{1,0:T(8,128)S(1)}, f32[128,128]{1,0:T(8,128)S(1)}, u32[]{:S(2)}, u32[]{:S(2)}) collective-permute-start(f32[128,128]{1,0:T(8,128)S(1)} %get-tuple-element.104), channel_id=1, source_target_pairs={{0,4},{4,0},{8,12},{12,8},{1,5},{5,1},{9,13},{13,9},{2,6},{6,2},{1... | collective-permute-start | bytes 196616 | tf_op jit(solution)/shard_map/ppermute | solution.py:351
  34.4 6.1 %collective-permute-start.11 = (f32[128,128]{1,0:T(8,128)S(1)}, f32[128,128]{1,0:T(8,128)S(1)}, u32[]{:S(2)}, u32[]{:S(2)}) collective-permute-start(f32[128,128]{1,0:T(8,128)S(1)} %get-tuple-element.105), channel_id=1, source_target_pairs={{0,12},{4,8},{8,4},{12,0},{1,13},{5,9},{9,5},{13,1},{2,14},{6,10},... | collective-permute-start | bytes 196616 | tf_op jit(solution)/shard_map/ppermute | solution.py:351
  41.1 7.5 %collective-permute-start.12 = (f32[128,128]{1,0:T(8,128)S(1)}, f32[128,128]{1,0:T(8,128)S(1)}, u32[]{:S(2)}, u32[]{:S(2)}) collective-permute-start(f32[128,128]{1,0:T(8,128)S(1)} %get-tuple-element.115), channel_id=1, source_target_pairs={{0,8},{4,12},{8,0},{12,4},{1,9},{5,13},{9,1},{13,5},{2,10},{6,14},... | collective-permute-start | bytes 196616 | tf_op jit(solution)/shard_map/ppermute | solution.py:351
  43.0 6.5 %collective-permute-start.13 = (f32[128,128]{1,0:T(8,128)S(1)}, f32[128,128]{1,0:T(8,128)S(1)}, u32[]{:S(2)}, u32[]{:S(2)}) collective-permute-start(f32[128,128]{1,0:T(8,128)S(1)} %get-tuple-element.116), channel_id=1, source_target_pairs={{0,12},{4,8},{8,4},{12,0},{1,13},{5,9},{9,5},{13,1},{2,14},{6,10},... | collective-permute-start | bytes 196616 | tf_op jit(solution)/shard_map/ppermute | solution.py:351
  45.0 5.1 %collective-permute-start.14 = (f32[128,128]{1,0:T(8,128)S(1)}, f32[128,128]{1,0:T(8,128)S(1)}, u32[]{:S(2)}, u32[]{:S(2)}) collective-permute-start(f32[128,128]{1,0:T(8,128)S(1)} %get-tuple-element.117), channel_id=1, source_target_pairs={{0,4},{4,0},{8,12},{12,8},{1,5},{5,1},{9,13},{13,9},{2,6},{6,2},{1... | collective-permute-start | bytes 196616 | tf_op jit(solution)/shard_map/ppermute | solution.py:351
  50.7 7.4 %collective-permute-start.15 = (f32[128,128]{1,0:T(8,128)S(1)}, f32[128,128]{1,0:T(8,128)S(1)}, u32[]{:S(2)}, u32[]{:S(2)}) collective-permute-start(f32[128,128]{1,0:T(8,128)S(1)} %get-tuple-element.122), channel_id=1, source_target_pairs={{0,8},{4,12},{8,0},{12,4},{1,9},{5,13},{9,1},{13,5},{2,10},{6,14},... | collective-permute-start | bytes 196616 | tf_op jit(solution)/shard_map/ppermute | solution.py:351
  51.5 6.6 %collective-permute-start.16 = (f32[128,128]{1,0:T(8,128)S(1)}, f32[128,128]{1,0:T(8,128)S(1)}, u32[]{:S(2)}, u32[]{:S(2)}) collective-permute-start(f32[128,128]{1,0:T(8,128)S(1)} %get-tuple-element.123), channel_id=1, source_target_pairs={{0,12},{4,8},{8,4},{12,0},{1,13},{5,9},{9,5},{13,1},{2,14},{6,10},... | collective-permute-start | bytes 196616 | tf_op jit(solution)/shard_map/ppermute | solution.py:351
  53.5 5.3 %collective-permute-start.17 = (f32[128,128]{1,0:T(8,128)S(1)}, f32[128,128]{1,0:T(8,128)S(1)}, u32[]{:S(2)}, u32[]{:S(2)}) collective-permute-start(f32[128,128]{1,0:T(8,128)S(1)} %get-tuple-element.124), channel_id=1, source_target_pairs={{0,4},{4,0},{8,12},{12,8},{1,5},{5,1},{9,13},{13,9},{2,6},{6,2},{1... | collective-permute-start | bytes 196616 | tf_op jit(solution)/shard_map/ppermute | solution.py:351
  59.1 5.2 %collective-permute-start.18 = (f32[64,128]{1,0:T(8,128)S(1)}, f32[64,128]{1,0:T(8,128)S(1)}, u32[]{:S(2)}, u32[]{:S(2)}) collective-permute-start(f32[64,128]{1,0:T(8,128)S(1)} %get-tuple-element.130), channel_id=1, source_target_pairs={{0,8},{4,12},{8,0},{12,4},{1,9},{5,13},{9,1},{13,5},{2,10},{6,14},... | collective-permute-start | bytes 98312 | tf_op jit(solution)/shard_map/ppermute | solution.py:351
  59.6 5.7 %collective-permute-start.19 = (f32[64,128]{1,0:T(8,128)S(1)}, f32[64,128]{1,0:T(8,128)S(1)}, u32[]{:S(2)}, u32[]{:S(2)}) collective-permute-start(f32[64,128]{1,0:T(8,128)S(1)} %get-tuple-element.131), channel_id=1, source_target_pairs={{0,12},{4,8},{8,4},{12,0},{1,13},{5,9},{9,5},{13,1},{2,14},{6,10},... | collective-permute-start | bytes 98312 | tf_op jit(solution)/shard_map/ppermute | solution.py:351
  62.1 3.9 %collective-permute-start.20 = (f32[64,128]{1,0:T(8,128)S(1)}, f32[64,128]{1,0:T(8,128)S(1)}, u32[]{:S(2)}, u32[]{:S(2)}) collective-permute-start(f32[64,128]{1,0:T(8,128)S(1)} %get-tuple-element.132), channel_id=1, source_target_pairs={{0,4},{4,0},{8,12},{12,8},{1,5},{5,1},{9,13},{13,9},{2,6},{6,2},{1... | collective-permute-start | bytes 98312 | tf_op jit(solution)/shard_map/ppermute | solution.py:351
  66.3 3.4 %collective-permute-start.21 = (f32[64,128]{1,0:T(8,128)S(1)}, f32[64,128]{1,0:T(8,128)S(1)}, u32[]{:S(2)}, u32[]{:S(2)}) collective-permute-start(f32[64,128]{1,0:T(8,128)S(1)} %get-tuple-element.134), channel_id=1, source_target_pairs={{0,3},{1,2},{2,1},{3,0},{4,7},{5,6},{6,5},{7,4},{8,11},{9,10},{10,... | collective-permute-start | bytes 98312 | tf_op jit(solution)/shard_map/ppermute | solution.py:351
  66.4 4.0 %collective-permute-start.22 = (f32[64,128]{1,0:T(8,128)S(1)}, f32[64,128]{1,0:T(8,128)S(1)}, u32[]{:S(2)}, u32[]{:S(2)}) collective-permute-start(f32[64,128]{1,0:T(8,128)S(1)} %get-tuple-element.135), channel_id=1, source_target_pairs={{0,2},{1,3},{2,0},{3,1},{4,6},{5,7},{6,4},{7,5},{8,10},{9,11},{10,... | collective-permute-start | bytes 98312 | tf_op jit(solution)/shard_map/ppermute | solution.py:351
  66.7 3.7 %collective-permute-start.23 = (f32[64,128]{1,0:T(8,128)S(1)}, f32[64,128]{1,0:T(8,128)S(1)}, u32[]{:S(2)}, u32[]{:S(2)}) collective-permute-start(f32[64,128]{1,0:T(8,128)S(1)} %get-tuple-element.136), channel_id=1, source_target_pairs={{0,1},{1,0},{2,3},{3,2},{4,5},{5,4},{6,7},{7,6},{8,9},{9,8},{10,11... | collective-permute-start | bytes 98312 | tf_op jit(solution)/shard_map/ppermute | solution.py:351
  71.4 7.1 %collective-permute-start.24 = (f32[128,128]{1,0:T(8,128)S(1)}, f32[128,128]{1,0:T(8,128)S(1)}, u32[]{:S(2)}, u32[]{:S(2)}) collective-permute-start(f32[128,128]{1,0:T(8,128)S(1)} %get-tuple-element.139), channel_id=1, source_target_pairs={{0,8},{4,12},{8,0},{12,4},{1,9},{5,13},{9,1},{13,5},{2,10},{6,14},... | collective-permute-start | bytes 196616 | tf_op jit(solution)/shard_map/ppermute | solution.py:351
  72.2 6.3 %collective-permute-start.25 = (f32[128,128]{1,0:T(8,128)S(1)}, f32[128,128]{1,0:T(8,128)S(1)}, u32[]{:S(2)}, u32[]{:S(2)}) collective-permute-start(f32[128,128]{1,0:T(8,128)S(1)} %get-tuple-element.140), channel_id=1, source_target_pairs={{0,4},{4,0},{8,12},{12,8},{1,5},{5,1},{9,13},{13,9},{2,6},{6,2},{1... | collective-permute-start | bytes 196616 | tf_op jit(solution)/shard_map/ppermute | solution.py:351
  73.8 6.1 %collective-permute-start.26 = (f32[128,128]{1,0:T(8,128)S(1)}, f32[128,128]{1,0:T(8,128)S(1)}, u32[]{:S(2)}, u32[]{:S(2)}) collective-permute-start(f32[128,128]{1,0:T(8,128)S(1)} %get-tuple-element.141), channel_id=1, source_target_pairs={{0,12},{4,8},{8,4},{12,0},{1,13},{5,9},{9,5},{13,1},{2,14},{6,10},... | collective-permute-start | bytes 196616 | tf_op jit(solution)/shard_map/ppermute | solution.py:351
  80.5 6.7 %collective-permute-start.27 = (f32[128,128]{1,0:T(8,128)S(1)}, f32[128,128]{1,0:T(8,128)S(1)}, u32[]{:S(2)}, u32[]{:S(2)}) collective-permute-start(f32[128,128]{1,0:T(8,128)S(1)} %get-tuple-element.146), channel_id=1, source_target_pairs={{0,8},{4,12},{8,0},{12,4},{1,9},{5,13},{9,1},{13,5},{2,10},{6,14},... | collective-permute-start | bytes 196616 | tf_op jit(solution)/shard_map/ppermute | solution.py:351
  81.9 6.1 %collective-permute-start.28 = (f32[128,128]{1,0:T(8,128)S(1)}, f32[128,128]{1,0:T(8,128)S(1)}, u32[]{:S(2)}, u32[]{:S(2)}) collective-permute-start(f32[128,128]{1,0:T(8,128)S(1)} %get-tuple-element.147), channel_id=1, source_target_pairs={{0,12},{4,8},{8,4},{12,0},{1,13},{5,9},{9,5},{13,1},{2,14},{6,10},... | collective-permute-start | bytes 196616 | tf_op jit(solution)/shard_map/ppermute | solution.py:351
  84.0 4.7 %collective-permute-start.29 = (f32[128,128]{1,0:T(8,128)S(1)}, f32[128,128]{1,0:T(8,128)S(1)}, u32[]{:S(2)}, u32[]{:S(2)}) collective-permute-start(f32[128,128]{1,0:T(8,128)S(1)} %get-tuple-element.148), channel_id=1, source_target_pairs={{0,4},{4,0},{8,12},{12,8},{1,5},{5,1},{9,13},{13,9},{2,6},{6,2},{1... | collective-permute-start | bytes 196616 | tf_op jit(solution)/shard_map/ppermute | solution.py:351

commit v19 on v17

--- a/solution.py
+++ b/solution.py
@@ -169,7 +169,13 @@
     rows = sum(b.shape[0] for b in blocks)
     if rows < unpack.shape[1]:
         blocks.append(jnp.zeros((unpack.shape[1] - rows, blocks[0].shape[1]), F32))
-    return pick(unpack[...], jnp.concatenate(blocks, axis=0))
+    halves = jnp.concatenate(split(jnp.concatenate(blocks, axis=0)), axis=1)
+    width = blocks[0].shape[1]
+    chunks = []
+    for at in range(0, shared, 128):
+        both = mm(unpack[at:at + 128, :], halves)
+        chunks.append(both[:, :width] + both[:, width:])
+    return jnp.concatenate(chunks, axis=0)
 
 
 def base_kernel(image, unpack_own, gap, base):
@@ -436,7 +442,13 @@
             next_loads = block((shared, loads), 1)
             trial_n, started, high, low = call(
                 rest_start_kernel,
-                (size, operator, mult, mult, gap, modes),
+                (
+                    size,
+                    *(
+                        pltpu.with_memory_space_constraint(value, pltpu.HBM)
+                        for value in (operator, mult, mult, gap, modes)
+                    ),
+                ),
                 [shape(rest, loads), shape(count, loads)] + [shape(rest, order, BF16)] * 2,
                 [
                     SMEM,

time: 89.5 us -> 89.5 us (level)
  waiting for transfers between devices: 32.1 us -> 29.4 us
  Pallas kernels: 19 us -> 21.6 us
    ppermute x30, waiting for transfers between devices: 32.1 us -> 29.4 us  [swap(): return lax.ppermute(block, axis, [(i, i ^ d) for i in range(count)])]
    pallas_call x25, Pallas kernels: 19 us -> 21.6 us  [call(): pl.pallas_call(body, out_shape=outs, grid=grid, in_specs=in_specs, out_sp...]
  transfers between devices with their start and end apart: 30 -> 30, of which waited for: 26 -> 25; matrix products, arithmetic and copies ran while one was open for 0% -> 0% of each run, Pallas kernels for 13% -> 16%
where the time goes in v19:
time: 89.5 us; the launch traced here: 89.3 us
  starting transfers between devices  36.7 us (41%)
  waiting for transfers between devices  29.4 us (33%)
  Pallas kernels  21.6 us (24%)
  between operations  1.56 us (2%)
    ppermute x30, starting transfers between devices, swap(): return lax.ppermute(block, axis, [(i, i ^ d) for i in range(count)])  36.7 us
    ppermute x30, waiting for transfers between devices, swap(): return lax.ppermute(block, axis, [(i, i ^ d) for i in range(count)])  29.4 us
    pallas_call x25, Pallas kernels, call(): pl.pallas_call(body, out_shape=outs, grid=grid, in_specs=in_specs, out_sp...  21.6 us
  transfers between devices with their start and end apart: 30, of which 25 were waited for; matrix products, arithmetic and copies ran while one was open for 0% of the time, Pallas kernels for 16%

profile of v19, /device:TPU:0, one launch (start us, length us, event | category | flops | bytes accessed | tf_op | source)
XLA Modules:
  0.0 89.3 jit_solution(14802889578191442689)
XLA Ops:
  0.6 2.0 %first.1 = (bf16[256,256]{1,0:T(8,128)(2,1)S(1)}, bf16[256,768]{1,0:T(8,128)(2,1)S(1)}, bf16[256,384]{1,0:T(8,128)(2,1)S(1)}, bf16[256,1024]{1,0:T(8,128)(2,1)S(...) custom-call(s32[1,256]{1,0:T(1,128)} %bitcast.32, ...), custom_call_target="tpu_custom_call" | custom-call | flops 201326592 | bytes 2097152 | tf_op jit(solution)/shard_map/first/pallas_call | solution.py:49
  2.6 5.1 %collective-permute-start = (f32[264,128]{1,0:T(8,128)S(1)}, f32[264,128]{1,0:T(8,128)S(1)}, u32[]{:S(2)}, u32[]{:S(2)}) collective-permute-start(f32[264,128]{1,0:T(8,128)S(1)} %get-tuple-element.81), channel_id=1, source_target_pairs={{0,12},{4,8},{8,4},{12,0},{1,13},{5,9},{9,5},{13,1},{2,14},{6,10},... | collective-permute-start | bytes 405512 | tf_op jit(solution)/shard_map/ppermute | solution.py:338
  7.7 0.6 collective-permute-start.2
  9.3 4.6 %rest_start.1 = (f32[768,128]{1,0:T(8,128)S(1)}, f32[64,128]{1,0:T(8,128)S(1)}, bf16[768,1024]{1,0:T(8,128)(2,1)S(1)}, bf16[768,1024]{1,0:T(8,128)(2,1)S(1)}) custom-call(s32[1]{0:T(128)S(6)} %copy.15.size, f32[1024,1024]{1,0:T(8,128)} %bitcast.29, f32[1024,128]{1,0:T(8,128)} %bitcast.20, f32[1024,128]{1,0:T(8,128)} %bitcast.21, f32[1024,128]{1,0:T(8,128)} %bitcast.7, ...), custom_call_target="tpu_custom_call" | custom-call | flops 603979776 | bytes 6291456 | tf_op jit(solution)/shard_map/rest_start/pallas_call | solution.py:49
  13.9 1.4 %collective-permute-done.1.refs_1_ = f32[264,128]{1,0:T(8,128)S(1)} collective-permute-done((f32[264,128]{1,0:T(8,128)S(1)}, f32[264,128]{1,0:T(8,128)S(1)}, u32[]{:S(2)}, u32[]{:S(2)}) %collective-permute-start.1) | collective-permute-done | bytes 135200 | tf_op jit(solution)/shard_map/ppermute | solution.py:338
  15.3 3.9 %collective-permute-done.2.refs_2_ = f32[264,128]{1,0:T(8,128)S(1)} collective-permute-done((f32[264,128]{1,0:T(8,128)S(1)}, f32[264,128]{1,0:T(8,128)S(1)}, u32[]{:S(2)}, u32[]{:S(2)}) %collective-permute-start.2) | collective-permute-done | bytes 135200 | tf_op jit(solution)/shard_map/ppermute | solution.py:338
  19.2 0.4 coarse.2
  19.6 0.8 collective-permute-start.3
  20.4 1.8 %collective-permute-start.4 = (f32[64,128]{1,0:T(8,128)S(1)}, f32[64,128]{1,0:T(8,128)S(1)}, u32[]{:S(2)}, u32[]{:S(2)}) collective-permute-start(f32[64,128]{1,0:T(8,128)S(1)} %get-tuple-element.90), channel_id=1, source_target_pairs={{0,12},{4,8},{8,4},{12,0},{1,13},{5,9},{9,5},{13,1},{2,14},{6,10},... | collective-permute-start | bytes 98312 | tf_op jit(solution)/shard_map/ppermute | solution.py:338
  22.2 0.9 %collective-permute-start.5 = (f32[64,128]{1,0:T(8,128)S(1)}, f32[64,128]{1,0:T(8,128)S(1)}, u32[]{:S(2)}, u32[]{:S(2)}) collective-permute-start(f32[64,128]{1,0:T(8,128)S(1)} %get-tuple-element.91), channel_id=1, source_target_pairs={{0,4},{4,0},{8,12},{12,8},{1,5},{5,1},{9,13},{13,9},{2,6},{6,2},{1... | collective-permute-start | bytes 98312 | tf_op jit(solution)/shard_map/ppermute | solution.py:338
  23.2 0.4 prepare.1
  23.6 1.1 %collective-permute-done.3.refs_1_ = f32[64,128]{1,0:T(8,128)S(1)} collective-permute-done((f32[64,128]{1,0:T(8,128)S(1)}, f32[64,128]{1,0:T(8,128)S(1)}, u32[]{:S(2)}, u32[]{:S(2)}) %collective-permute-start.3) | collective-permute-done | bytes 32800 | tf_op jit(solution)/shard_map/ppermute | solution.py:338
  24.6 1.7 %collective-permute-done.4.refs_2_ = f32[64,128]{1,0:T(8,128)S(1)} collective-permute-done((f32[64,128]{1,0:T(8,128)S(1)}, f32[64,128]{1,0:T(8,128)S(1)}, u32[]{:S(2)}, u32[]{:S(2)}) %collective-permute-start.4) | collective-permute-done | bytes 32800 | tf_op jit(solution)/shard_map/ppermute | solution.py:338
  26.8 1.6 %collective-permute-start.7 = (f32[64,128]{1,0:T(8,128)S(1)}, f32[64,128]{1,0:T(8,128)S(1)}, u32[]{:S(2)}, u32[]{:S(2)}) collective-permute-start(f32[64,128]{1,0:T(8,128)S(1)} %get-tuple-element.94), channel_id=1, source_target_pairs={{0,2},{1,3},{2,0},{3,1},{4,6},{5,7},{6,4},{7,5},{8,10},{9,11},{10,... | collective-permute-start | bytes 98312 | tf_op jit(solution)/shard_map/ppermute | solution.py:338
  28.7 0.3 pack.1
  29.0 1.5 %collective-permute-done.6.refs_1_ = f32[64,128]{1,0:T(8,128)S(1)} collective-permute-done((f32[64,128]{1,0:T(8,128)S(1)}, f32[64,128]{1,0:T(8,128)S(1)}, u32[]{:S(2)}, u32[]{:S(2)}) %collective-permute-start.6) | collective-permute-done | bytes 32800 | tf_op jit(solution)/shard_map/ppermute | solution.py:338
  30.5 0.4 collective-permute-done.7.refs_2_
  30.9 0.9 lift.2
  31.7 1.7 %collective-permute-start.9 = (f32[128,128]{1,0:T(8,128)S(1)}, f32[128,128]{1,0:T(8,128)S(1)}, u32[]{:S(2)}, u32[]{:S(2)}) collective-permute-start(f32[128,128]{1,0:T(8,128)S(1)} %get-tuple-element.103), channel_id=1, source_target_pairs={{0,8},{4,12},{8,0},{12,4},{1,9},{5,13},{9,1},{13,5},{2,10},{6,14},... | collective-permute-start | bytes 196616 | tf_op jit(solution)/shard_map/ppermute | solution.py:338
  33.4 0.8 collective-permute-start.10
  34.2 2.0 %collective-permute-start.11 = (f32[128,128]{1,0:T(8,128)S(1)}, f32[128,128]{1,0:T(8,128)S(1)}, u32[]{:S(2)}, u32[]{:S(2)}) collective-permute-start(f32[128,128]{1,0:T(8,128)S(1)} %get-tuple-element.105), channel_id=1, source_target_pairs={{0,12},{4,8},{8,4},{12,0},{1,13},{5,9},{9,5},{13,1},{2,14},{6,10},... | collective-permute-start | bytes 196616 | tf_op jit(solution)/shard_map/ppermute | solution.py:338
  36.4 1.5 %rest.3 = (f32[768,128]{1,0:T(8,128)S(1)}, f32[640,128]{1,0:T(8,128)S(1)}) custom-call(s32[1]{0:T(128)S(6)} %copy.15.size, bf16[768,1024]{1,0:T(8,128)(2,1)S(1)} %get-tuple-element.111.high, bf16[768,1024]{1,0:T(8,128)(2,1)S(1)} %get-tuple-element.112.low, f32[256,128]{1,0:T(8,128)S(1)} %get-tuple-element.108.mult_s.refs_5_, ...), custom_call_target="tpu_custom_call" | custom-call | flops 805306368 | bytes 4194304 | tf_op jit(solution)/shard_map/rest/pallas_call | solution.py:49
  37.9 1.4 %collective-permute-done.9.refs_0_ = f32[128,128]{1,0:T(8,128)S(1)} collective-permute-done((f32[128,128]{1,0:T(8,128)S(1)}, f32[128,128]{1,0:T(8,128)S(1)}, u32[]{:S(2)}, u32[]{:S(2)}) %collective-permute-start.9) | collective-permute-done | bytes 65568 | tf_op jit(solution)/shard_map/ppermute | solution.py:338
  39.3 0.7 collective-permute-done.10.refs_1_
  40.0 0.3 collective-permute-done.11.refs_2_
  40.3 0.6 sweep.3
  40.9 1.9 %collective-permute-start.12 = (f32[128,128]{1,0:T(8,128)S(1)}, f32[128,128]{1,0:T(8,128)S(1)}, u32[]{:S(2)}, u32[]{:S(2)}) collective-permute-start(f32[128,128]{1,0:T(8,128)S(1)} %get-tuple-element.115), channel_id=1, source_target_pairs={{0,8},{4,12},{8,0},{12,4},{1,9},{5,13},{9,1},{13,5},{2,10},{6,14},... | collective-permute-start | bytes 196616 | tf_op jit(solution)/shard_map/ppermute | solution.py:338
  42.8 2.0 %collective-permute-start.13 = (f32[128,128]{1,0:T(8,128)S(1)}, f32[128,128]{1,0:T(8,128)S(1)}, u32[]{:S(2)}, u32[]{:S(2)}) collective-permute-start(f32[128,128]{1,0:T(8,128)S(1)} %get-tuple-element.116), channel_id=1, source_target_pairs={{0,12},{4,8},{8,4},{12,0},{1,13},{5,9},{9,5},{13,1},{2,14},{6,10},... | collective-permute-start | bytes 196616 | tf_op jit(solution)/shard_map/ppermute | solution.py:338
  45.0 1.5 %rest.4 = (f32[768,128]{1,0:T(8,128)S(1)}, f32[640,128]{1,0:T(8,128)S(1)}) custom-call(s32[1]{0:T(128)S(6)} %copy.15.size, bf16[768,1024]{1,0:T(8,128)(2,1)S(1)} %get-tuple-element.111.high, bf16[768,1024]{1,0:T(8,128)(2,1)S(1)} %get-tuple-element.112.low, f32[256,128]{1,0:T(8,128)S(1)} %get-tuple-element.119.mult_s.refs_5_, ...), custom_call_target="tpu_custom_call" | custom-call | flops 805306368 | bytes 4194304 | tf_op jit(solution)/shard_map/rest/pallas_call | solution.py:49
  46.5 1.9 %collective-permute-done.12.refs_0_ = f32[128,128]{1,0:T(8,128)S(1)} collective-permute-done((f32[128,128]{1,0:T(8,128)S(1)}, f32[128,128]{1,0:T(8,128)S(1)}, u32[]{:S(2)}, u32[]{:S(2)}) %collective-permute-start.12) | collective-permute-done | bytes 65568 | tf_op jit(solution)/shard_map/ppermute | solution.py:338
  48.4 0.9 %collective-permute-done.13.refs_1_ = f32[128,128]{1,0:T(8,128)S(1)} collective-permute-done((f32[128,128]{1,0:T(8,128)S(1)}, f32[128,128]{1,0:T(8,128)S(1)}, u32[]{:S(2)}, u32[]{:S(2)}) %collective-permute-start.13) | collective-permute-done | bytes 65568 | tf_op jit(solution)/shard_map/ppermute | solution.py:338
  49.3 0.6 collective-permute-done.14.refs_2_
  49.9 0.6 sweep.4
  50.5 0.8 collective-permute-start.15
  51.3 1.9 %collective-permute-start.16 = (f32[128,128]{1,0:T(8,128)S(1)}, f32[128,128]{1,0:T(8,128)S(1)}, u32[]{:S(2)}, u32[]{:S(2)}) collective-permute-start(f32[128,128]{1,0:T(8,128)S(1)} %get-tuple-element.123), channel_id=1, source_target_pairs={{0,12},{4,8},{8,4},{12,0},{1,13},{5,9},{9,5},{13,1},{2,14},{6,10},... | collective-permute-start | bytes 196616 | tf_op jit(solution)/shard_map/ppermute | solution.py:338
  53.2 0.8 collective-permute-start.17
  54.3 1.1 %rest_first.1 = (f32[768,128]{1,0:T(8,128)S(1)}, f32[64,128]{1,0:T(8,128)S(1)}) custom-call(s32[1]{0:T(128)S(6)} %copy.15.size, bf16[768,1024]{1,0:T(8,128)(2,1)S(1)} %get-tuple-element.111.high, bf16[768,1024]{1,0:T(8,128)(2,1)S(1)} %get-tuple-element.112.low, f32[256,128]{1,0:T(8,128)S(1)} %get-tuple-element.126.mult_s.refs_5_, ...), custom_call_target="tpu_custom_call" | custom-call | flops 603979776 | bytes 3145728 | tf_op jit(solution)/shard_map/rest_first/pallas_call | solution.py:49
  55.4 2.5 %collective-permute-done.15.refs_0_ = f32[128,128]{1,0:T(8,128)S(1)} collective-permute-done((f32[128,128]{1,0:T(8,128)S(1)}, f32[128,128]{1,0:T(8,128)S(1)}, u32[]{:S(2)}, u32[]{:S(2)}) %collective-permute-start.15) | collective-permute-done | bytes 65568 | tf_op jit(solution)/shard_map/ppermute | solution.py:338
  57.9 0.6 collective-permute-done.17.refs_2_
  58.5 0.4 coarse.3
  58.9 0.4 collective-permute-start.18
  59.3 2.6 %collective-permute-start.19 = (f32[64,128]{1,0:T(8,128)S(1)}, f32[64,128]{1,0:T(8,128)S(1)}, u32[]{:S(2)}, u32[]{:S(2)}) collective-permute-start(f32[64,128]{1,0:T(8,128)S(1)} %get-tuple-element.131), channel_id=1, source_target_pairs={{0,12},{4,8},{8,4},{12,0},{1,13},{5,9},{9,5},{13,1},{2,14},{6,10},... | collective-permute-start | bytes 98312 | tf_op jit(solution)/shard_map/ppermute | solution.py:338
  61.9 0.6 collective-permute-start.20
  62.5 1.7 %collective-permute-done.18.refs_1_ = f32[64,128]{1,0:T(8,128)S(1)} collective-permute-done((f32[64,128]{1,0:T(8,128)S(1)}, f32[64,128]{1,0:T(8,128)S(1)}, u32[]{:S(2)}, u32[]{:S(2)}) %collective-permute-start.18) | collective-permute-done | bytes 32800 | tf_op jit(solution)/shard_map/ppermute | solution.py:338
  64.1 0.9 %collective-permute-done.19.refs_2_ = f32[64,128]{1,0:T(8,128)S(1)} collective-permute-done((f32[64,128]{1,0:T(8,128)S(1)}, f32[64,128]{1,0:T(8,128)S(1)}, u32[]{:S(2)}, u32[]{:S(2)}) %collective-permute-start.19) | collective-permute-done | bytes 32800 | tf_op jit(solution)/shard_map/ppermute | solution.py:338
  65.0 0.8 collective-permute-done.20.refs_3_
  66.5 1.5 %collective-permute-start.23 = (f32[64,128]{1,0:T(8,128)S(1)}, f32[64,128]{1,0:T(8,128)S(1)}, u32[]{:S(2)}, u32[]{:S(2)}) collective-permute-start(f32[64,128]{1,0:T(8,128)S(1)} %get-tuple-element.136), channel_id=1, source_target_pairs={{0,1},{1,0},{2,3},{3,2},{4,5},{5,4},{6,7},{7,6},{8,9},{9,8},{10,11... | collective-permute-start | bytes 98312 | tf_op jit(solution)/shard_map/ppermute | solution.py:338
  68.0 1.5 %collective-permute-done.21.refs_1_ = f32[64,128]{1,0:T(8,128)S(1)} collective-permute-done((f32[64,128]{1,0:T(8,128)S(1)}, f32[64,128]{1,0:T(8,128)S(1)}, u32[]{:S(2)}, u32[]{:S(2)}) %collective-permute-start.21) | collective-permute-done | bytes 32800 | tf_op jit(solution)/shard_map/ppermute | solution.py:338
  69.5 0.7 collective-permute-done.22.refs_2_
  70.2 0.9 lift.3
  71.1 0.8 collective-permute-start.24
  71.9 1.6 %collective-permute-start.25 = (f32[128,128]{1,0:T(8,128)S(1)}, f32[128,128]{1,0:T(8,128)S(1)}, u32[]{:S(2)}, u32[]{:S(2)}) collective-permute-start(f32[128,128]{1,0:T(8,128)S(1)} %get-tuple-element.140), channel_id=1, source_target_pairs={{0,4},{4,0},{8,12},{12,8},{1,5},{5,1},{9,13},{13,9},{2,6},{6,2},{1... | collective-permute-start | bytes 196616 | tf_op jit(solution)/shard_map/ppermute | solution.py:338
  73.5 2.0 %collective-permute-start.26 = (f32[128,128]{1,0:T(8,128)S(1)}, f32[128,128]{1,0:T(8,128)S(1)}, u32[]{:S(2)}, u32[]{:S(2)}) collective-permute-start(f32[128,128]{1,0:T(8,128)S(1)} %get-tuple-element.141), channel_id=1, source_target_pairs={{0,12},{4,8},{8,4},{12,0},{1,13},{5,9},{9,5},{13,1},{2,14},{6,10},... | collective-permute-start | bytes 196616 | tf_op jit(solution)/shard_map/ppermute | solution.py:338
  75.7 1.5 %rest.5 = (f32[768,128]{1,0:T(8,128)S(1)}, f32[640,128]{1,0:T(8,128)S(1)}) custom-call(s32[1]{0:T(128)S(6)} %copy.15.size, bf16[768,1024]{1,0:T(8,128)(2,1)S(1)} %get-tuple-element.111.high, bf16[768,1024]{1,0:T(8,128)(2,1)S(1)} %get-tuple-element.112.low, f32[256,128]{1,0:T(8,128)S(1)} %get-tuple-element.143.mult_s.refs_5_, ...), custom_call_target="tpu_custom_call" | custom-call | flops 805306368 | bytes 4194304 | tf_op jit(solution)/shard_map/rest/pallas_call | solution.py:49
  77.2 1.0 %collective-permute-done.24.refs_0_ = f32[128,128]{1,0:T(8,128)S(1)} collective-permute-done((f32[128,128]{1,0:T(8,128)S(1)}, f32[128,128]{1,0:T(8,128)S(1)}, u32[]{:S(2)}, u32[]{:S(2)}) %collective-permute-start.24) | collective-permute-done | bytes 65568 | tf_op jit(solution)/shard_map/ppermute | solution.py:338
  78.2 1.4 %collective-permute-done.26.refs_2_ = f32[128,128]{1,0:T(8,128)S(1)} collective-permute-done((f32[128,128]{1,0:T(8,128)S(1)}, f32[128,128]{1,0:T(8,128)S(1)}, u32[]{:S(2)}, u32[]{:S(2)}) %collective-permute-start.26) | collective-permute-done | bytes 65568 | tf_op jit(solution)/shard_map/ppermute | solution.py:338
  79.6 0.6 sweep.5
  80.2 1.3 %collective-permute-start.27 = (f32[128,128]{1,0:T(8,128)S(1)}, f32[128,128]{1,0:T(8,128)S(1)}, u32[]{:S(2)}, u32[]{:S(2)}) collective-permute-start(f32[128,128]{1,0:T(8,128)S(1)} %get-tuple-element.146), channel_id=1, source_target_pairs={{0,8},{4,12},{8,0},{12,4},{1,9},{5,13},{9,1},{13,5},{2,10},{6,14},... | collective-permute-start | bytes 196616 | tf_op jit(solution)/shard_map/ppermute | solution.py:338
  81.5 2.1 %collective-permute-start.28 = (f32[128,128]{1,0:T(8,128)S(1)}, f32[128,128]{1,0:T(8,128)S(1)}, u32[]{:S(2)}, u32[]{:S(2)}) collective-permute-start(f32[128,128]{1,0:T(8,128)S(1)} %get-tuple-element.147), channel_id=1, source_target_pairs={{0,12},{4,8},{8,4},{12,0},{1,13},{5,9},{9,5},{13,1},{2,14},{6,10},... | collective-permute-start | bytes 196616 | tf_op jit(solution)/shard_map/ppermute | solution.py:338
  83.9 1.9 %rest_last.1 = (f32[1024,128]{1,0:T(8,128)}, f32[1024,128]{1,0:T(8,128)}) custom-call(s32[1]{0:T(128)S(6)} %copy.15.size, bf16[768,1024]{1,0:T(8,128)(2,1)S(1)} %get-tuple-element.111.high, bf16[768,1024]{1,0:T(8,128)(2,1)S(1)} %get-tuple-element.112.low, f32[256,128]{1,0:T(8,128)S(1)} %get-tuple-element.150.mult_s.refs_5_, ...), custom_call_target="tpu_custom_call" | custom-call | flops 603979776 | bytes 3145728 | tf_op jit(solution)/shard_map/rest_last/pallas_call | solution.py:49
  85.8 1.0 %collective-permute-done.27.refs_0_ = f32[128,128]{1,0:T(8,128)S(1)} collective-permute-done((f32[128,128]{1,0:T(8,128)S(1)}, f32[128,128]{1,0:T(8,128)S(1)}, u32[]{:S(2)}, u32[]{:S(2)}) %collective-permute-start.27) | collective-permute-done | bytes 65568 | tf_op jit(solution)/shard_map/ppermute | solution.py:338
  86.8 0.9 collective-permute-done.28.refs_1_
  87.7 0.7 collective-permute-done.29.refs_2_
  88.3 1.0 %last.1 = (f32[1024,128]{1,0:T(8,128)}, f32[1024,128]{1,0:T(8,128)}) custom-call(s32[1]{0:T(128)S(6)} %copy.15.size, f32[128,128]{1,0:T(8,128)S(1)} %collective-permute-done.27.refs_0_, f32[128,128]{1,0:T(8,128)S(1)} %collective-permute-done.28.refs_1_, ...), custom_call_target="tpu_custom_call", output_to_operand_aliasing={{0}: (8, {}), {1}: (9, {})} | custom-call | flops 75497472 | bytes 196608 | tf_op jit(solution)/shard_map/last/pallas_call | solution.py:49
  (33 shorter events, 2.7 us)
Async XLA Ops:
  0.6 8.4 %copy-start = (f32[1,1024,128]{2,1,0:T(8,128)S(1)}, f32[1,1024,128]{2,1,0:T(8,128)}, u32[]{:S(2)}) copy-start(f32[1,1024,128]{2,1,0:T(8,128)} %param.12) | copy-start | bytes 1572868
  2.6 11.3 %collective-permute-start = (f32[264,128]{1,0:T(8,128)S(1)}, f32[264,128]{1,0:T(8,128)S(1)}, u32[]{:S(2)}, u32[]{:S(2)}) collective-permute-start(f32[264,128]{1,0:T(8,128)S(1)} %get-tuple-element.81), channel_id=1, source_target_pairs={{0,12},{4,8},{8,4},{12,0},{1,13},{5,9},{9,5},{13,1},{2,14},{6,10},... | collective-permute-start | bytes 405512 | tf_op jit(solution)/shard_map/ppermute | solution.py:338
  7.7 7.6 %collective-permute-start.1 = (f32[264,128]{1,0:T(8,128)S(1)}, f32[264,128]{1,0:T(8,128)S(1)}, u32[]{:S(2)}, u32[]{:S(2)}) collective-permute-start(f32[264,128]{1,0:T(8,128)S(1)} %get-tuple-element.82), channel_id=1, source_target_pairs={{0,4},{4,0},{8,12},{12,8},{1,5},{5,1},{9,13},{13,9},{2,6},{6,2},{1... | collective-permute-start | bytes 405512 | tf_op jit(solution)/shard_map/ppermute | solution.py:338
  7.7 11.4 %collective-permute-start.2 = (f32[264,128]{1,0:T(8,128)S(1)}, f32[264,128]{1,0:T(8,128)S(1)}, u32[]{:S(2)}, u32[]{:S(2)}) collective-permute-start(f32[264,128]{1,0:T(8,128)S(1)} %get-tuple-element.83), channel_id=1, source_target_pairs={{0,8},{4,12},{8,0},{12,4},{1,9},{5,13},{9,1},{13,5},{2,10},{6,14},... | collective-permute-start | bytes 405512 | tf_op jit(solution)/shard_map/ppermute | solution.py:338
  9.2 9.9 %copy-start.2 = (f32[1,1024,128]{2,1,0:T(8,128)S(1)}, f32[1,1024,128]{2,1,0:T(8,128)}, u32[]{:S(2)}) copy-start(f32[1,1024,128]{2,1,0:T(8,128)} %param.13) | copy-start | bytes 1572868
  9.3 9.9 %copy-start.3 = (f32[1,64,1024]{2,1,0:T(8,128)S(1)}, f32[1,64,1024]{2,1,0:T(8,128)}, u32[]{:S(2)}) copy-start(f32[1,64,1024]{2,1,0:T(8,128)} %param.11) | copy-start | bytes 786436
  13.8 9.3 %copy-start.4 = (f32[256,256]{1,0:T(8,128)S(1)}, f32[256,256]{1,0:T(8,128)}, u32[]{:S(2)}) copy-start(f32[256,256]{1,0:T(8,128)} %tile.3) | copy-start | bytes 786436
  13.9 9.3 %copy-start.5 = (s32[1,1024]{1,0:T(1,128)S(1)}, s32[1,1024]{1,0:T(1,128)}, u32[]{:S(2)}) copy-start(s32[1,1024]{1,0:T(1,128)} %contact.1) | copy-start | bytes 12292
  19.6 5.0 %collective-permute-start.3 = (f32[64,128]{1,0:T(8,128)S(1)}, f32[64,128]{1,0:T(8,128)S(1)}, u32[]{:S(2)}, u32[]{:S(2)}) collective-permute-start(f32[64,128]{1,0:T(8,128)S(1)} %get-tuple-element.89), channel_id=1, source_target_pairs={{0,8},{4,12},{8,0},{12,4},{1,9},{5,13},{9,1},{13,5},{2,10},{6,14},... | collective-permute-start | bytes 98312 | tf_op jit(solution)/shard_map/ppermute | solution.py:338
  20.4 5.9 %collective-permute-start.4 = (f32[64,128]{1,0:T(8,128)S(1)}, f32[64,128]{1,0:T(8,128)S(1)}, u32[]{:S(2)}, u32[]{:S(2)}) collective-permute-start(f32[64,128]{1,0:T(8,128)S(1)} %get-tuple-element.90), channel_id=1, source_target_pairs={{0,12},{4,8},{8,4},{12,0},{1,13},{5,9},{9,5},{13,1},{2,14},{6,10},... | collective-permute-start | bytes 98312 | tf_op jit(solution)/shard_map/ppermute | solution.py:338
  22.2 4.3 %collective-permute-start.5 = (f32[64,128]{1,0:T(8,128)S(1)}, f32[64,128]{1,0:T(8,128)S(1)}, u32[]{:S(2)}, u32[]{:S(2)}) collective-permute-start(f32[64,128]{1,0:T(8,128)S(1)} %get-tuple-element.91), channel_id=1, source_target_pairs={{0,4},{4,0},{8,12},{12,8},{1,5},{5,1},{9,13},{13,9},{2,6},{6,2},{1... | collective-permute-start | bytes 98312 | tf_op jit(solution)/shard_map/ppermute | solution.py:338
  26.8 3.7 %collective-permute-start.6 = (f32[64,128]{1,0:T(8,128)S(1)}, f32[64,128]{1,0:T(8,128)S(1)}, u32[]{:S(2)}, u32[]{:S(2)}) collective-permute-start(f32[64,128]{1,0:T(8,128)S(1)} %get-tuple-element.93), channel_id=1, source_target_pairs={{0,3},{1,2},{2,1},{3,0},{4,7},{5,6},{6,5},{7,4},{8,11},{9,10},{10,... | collective-permute-start | bytes 98312 | tf_op jit(solution)/shard_map/ppermute | solution.py:338
  26.8 4.0 %collective-permute-start.7 = (f32[64,128]{1,0:T(8,128)S(1)}, f32[64,128]{1,0:T(8,128)S(1)}, u32[]{:S(2)}, u32[]{:S(2)}) collective-permute-start(f32[64,128]{1,0:T(8,128)S(1)} %get-tuple-element.94), channel_id=1, source_target_pairs={{0,2},{1,3},{2,0},{3,1},{4,6},{5,7},{6,4},{7,5},{8,10},{9,11},{10,... | collective-permute-start | bytes 98312 | tf_op jit(solution)/shard_map/ppermute | solution.py:338
  28.4 2.5 %collective-permute-start.8 = (f32[64,128]{1,0:T(8,128)S(1)}, f32[64,128]{1,0:T(8,128)S(1)}, u32[]{:S(2)}, u32[]{:S(2)}) collective-permute-start(f32[64,128]{1,0:T(8,128)S(1)} %get-tuple-element.95), channel_id=1, source_target_pairs={{0,1},{1,0},{2,3},{3,2},{4,5},{5,4},{6,7},{7,6},{8,9},{9,8},{10,11... | collective-permute-start | bytes 98312 | tf_op jit(solution)/shard_map/ppermute | solution.py:338
  29.0 7.2 %copy-start.1 = (f32[1,1024,128]{2,1,0:T(8,128)S(1)}, f32[1,1024,128]{2,1,0:T(8,128)}, u32[]{:S(2)}) copy-start(f32[1,1024,128]{2,1,0:T(8,128)} %param.12) | copy-start | bytes 1572868
  31.7 7.6 %collective-permute-start.9 = (f32[128,128]{1,0:T(8,128)S(1)}, f32[128,128]{1,0:T(8,128)S(1)}, u32[]{:S(2)}, u32[]{:S(2)}) collective-permute-start(f32[128,128]{1,0:T(8,128)S(1)} %get-tuple-element.103), channel_id=1, source_target_pairs={{0,8},{4,12},{8,0},{12,4},{1,9},{5,13},{9,1},{13,5},{2,10},{6,14},... | collective-permute-start | bytes 196616 | tf_op jit(solution)/shard_map/ppermute | solution.py:338
  33.4 6.6 %collective-permute-start.10 = (f32[128,128]{1,0:T(8,128)S(1)}, f32[128,128]{1,0:T(8,128)S(1)}, u32[]{:S(2)}, u32[]{:S(2)}) collective-permute-start(f32[128,128]{1,0:T(8,128)S(1)} %get-tuple-element.104), channel_id=1, source_target_pairs={{0,4},{4,0},{8,12},{12,8},{1,5},{5,1},{9,13},{13,9},{2,6},{6,2},{1... | collective-permute-start | bytes 196616 | tf_op jit(solution)/shard_map/ppermute | solution.py:338
  34.2 6.1 %collective-permute-start.11 = (f32[128,128]{1,0:T(8,128)S(1)}, f32[128,128]{1,0:T(8,128)S(1)}, u32[]{:S(2)}, u32[]{:S(2)}) collective-permute-start(f32[128,128]{1,0:T(8,128)S(1)} %get-tuple-element.105), channel_id=1, source_target_pairs={{0,12},{4,8},{8,4},{12,0},{1,13},{5,9},{9,5},{13,1},{2,14},{6,10},... | collective-permute-start | bytes 196616 | tf_op jit(solution)/shard_map/ppermute | solution.py:338
  40.9 7.5 %collective-permute-start.12 = (f32[128,128]{1,0:T(8,128)S(1)}, f32[128,128]{1,0:T(8,128)S(1)}, u32[]{:S(2)}, u32[]{:S(2)}) collective-permute-start(f32[128,128]{1,0:T(8,128)S(1)} %get-tuple-element.115), channel_id=1, source_target_pairs={{0,8},{4,12},{8,0},{12,4},{1,9},{5,13},{9,1},{13,5},{2,10},{6,14},... | collective-permute-start | bytes 196616 | tf_op jit(solution)/shard_map/ppermute | solution.py:338
  42.8 6.5 %collective-permute-start.13 = (f32[128,128]{1,0:T(8,128)S(1)}, f32[128,128]{1,0:T(8,128)S(1)}, u32[]{:S(2)}, u32[]{:S(2)}) collective-permute-start(f32[128,128]{1,0:T(8,128)S(1)} %get-tuple-element.116), channel_id=1, source_target_pairs={{0,12},{4,8},{8,4},{12,0},{1,13},{5,9},{9,5},{13,1},{2,14},{6,10},... | collective-permute-start | bytes 196616 | tf_op jit(solution)/shard_map/ppermute | solution.py:338
  44.8 5.1 %collective-permute-start.14 = (f32[128,128]{1,0:T(8,128)S(1)}, f32[128,128]{1,0:T(8,128)S(1)}, u32[]{:S(2)}, u32[]{:S(2)}) collective-permute-start(f32[128,128]{1,0:T(8,128)S(1)} %get-tuple-element.117), channel_id=1, source_target_pairs={{0,4},{4,0},{8,12},{12,8},{1,5},{5,1},{9,13},{13,9},{2,6},{6,2},{1... | collective-permute-start | bytes 196616 | tf_op jit(solution)/shard_map/ppermute | solution.py:338
  50.5 7.4 %collective-permute-start.15 = (f32[128,128]{1,0:T(8,128)S(1)}, f32[128,128]{1,0:T(8,128)S(1)}, u32[]{:S(2)}, u32[]{:S(2)}) collective-permute-start(f32[128,128]{1,0:T(8,128)S(1)} %get-tuple-element.122), channel_id=1, source_target_pairs={{0,8},{4,12},{8,0},{12,4},{1,9},{5,13},{9,1},{13,5},{2,10},{6,14},... | collective-permute-start | bytes 196616 | tf_op jit(solution)/shard_map/ppermute | solution.py:338
  51.3 6.6 %collective-permute-start.16 = (f32[128,128]{1,0:T(8,128)S(1)}, f32[128,128]{1,0:T(8,128)S(1)}, u32[]{:S(2)}, u32[]{:S(2)}) collective-permute-start(f32[128,128]{1,0:T(8,128)S(1)} %get-tuple-element.123), channel_id=1, source_target_pairs={{0,12},{4,8},{8,4},{12,0},{1,13},{5,9},{9,5},{13,1},{2,14},{6,10},... | collective-permute-start | bytes 196616 | tf_op jit(solution)/shard_map/ppermute | solution.py:338
  53.2 5.3 %collective-permute-start.17 = (f32[128,128]{1,0:T(8,128)S(1)}, f32[128,128]{1,0:T(8,128)S(1)}, u32[]{:S(2)}, u32[]{:S(2)}) collective-permute-start(f32[128,128]{1,0:T(8,128)S(1)} %get-tuple-element.124), channel_id=1, source_target_pairs={{0,4},{4,0},{8,12},{12,8},{1,5},{5,1},{9,13},{13,9},{2,6},{6,2},{1... | collective-permute-start | bytes 196616 | tf_op jit(solution)/shard_map/ppermute | solution.py:338
  58.9 5.2 %collective-permute-start.18 = (f32[64,128]{1,0:T(8,128)S(1)}, f32[64,128]{1,0:T(8,128)S(1)}, u32[]{:S(2)}, u32[]{:S(2)}) collective-permute-start(f32[64,128]{1,0:T(8,128)S(1)} %get-tuple-element.130), channel_id=1, source_target_pairs={{0,8},{4,12},{8,0},{12,4},{1,9},{5,13},{9,1},{13,5},{2,10},{6,14},... | collective-permute-start | bytes 98312 | tf_op jit(solution)/shard_map/ppermute | solution.py:338
  59.3 5.7 %collective-permute-start.19 = (f32[64,128]{1,0:T(8,128)S(1)}, f32[64,128]{1,0:T(8,128)S(1)}, u32[]{:S(2)}, u32[]{:S(2)}) collective-permute-start(f32[64,128]{1,0:T(8,128)S(1)} %get-tuple-element.131), channel_id=1, source_target_pairs={{0,12},{4,8},{8,4},{12,0},{1,13},{5,9},{9,5},{13,1},{2,14},{6,10},... | collective-permute-start | bytes 98312 | tf_op jit(solution)/shard_map/ppermute | solution.py:338
  61.9 3.9 %collective-permute-start.20 = (f32[64,128]{1,0:T(8,128)S(1)}, f32[64,128]{1,0:T(8,128)S(1)}, u32[]{:S(2)}, u32[]{:S(2)}) collective-permute-start(f32[64,128]{1,0:T(8,128)S(1)} %get-tuple-element.132), channel_id=1, source_target_pairs={{0,4},{4,0},{8,12},{12,8},{1,5},{5,1},{9,13},{13,9},{2,6},{6,2},{1... | collective-permute-start | bytes 98312 | tf_op jit(solution)/shard_map/ppermute | solution.py:338
  66.1 3.4 %collective-permute-start.21 = (f32[64,128]{1,0:T(8,128)S(1)}, f32[64,128]{1,0:T(8,128)S(1)}, u32[]{:S(2)}, u32[]{:S(2)}) collective-permute-start(f32[64,128]{1,0:T(8,128)S(1)} %get-tuple-element.134), channel_id=1, source_target_pairs={{0,3},{1,2},{2,1},{3,0},{4,7},{5,6},{6,5},{7,4},{8,11},{9,10},{10,... | collective-permute-start | bytes 98312 | tf_op jit(solution)/shard_map/ppermute | solution.py:338
  66.2 4.0 %collective-permute-start.22 = (f32[64,128]{1,0:T(8,128)S(1)}, f32[64,128]{1,0:T(8,128)S(1)}, u32[]{:S(2)}, u32[]{:S(2)}) collective-permute-start(f32[64,128]{1,0:T(8,128)S(1)} %get-tuple-element.135), channel_id=1, source_target_pairs={{0,2},{1,3},{2,0},{3,1},{4,6},{5,7},{6,4},{7,5},{8,10},{9,11},{10,... | collective-permute-start | bytes 98312 | tf_op jit(solution)/shard_map/ppermute | solution.py:338
  66.5 3.7 %collective-permute-start.23 = (f32[64,128]{1,0:T(8,128)S(1)}, f32[64,128]{1,0:T(8,128)S(1)}, u32[]{:S(2)}, u32[]{:S(2)}) collective-permute-start(f32[64,128]{1,0:T(8,128)S(1)} %get-tuple-element.136), channel_id=1, source_target_pairs={{0,1},{1,0},{2,3},{3,2},{4,5},{5,4},{6,7},{7,6},{8,9},{9,8},{10,11... | collective-permute-start | bytes 98312 | tf_op jit(solution)/shard_map/ppermute | solution.py:338
  71.1 7.2 %collective-permute-start.24 = (f32[128,128]{1,0:T(8,128)S(1)}, f32[128,128]{1,0:T(8,128)S(1)}, u32[]{:S(2)}, u32[]{:S(2)}) collective-permute-start(f32[128,128]{1,0:T(8,128)S(1)} %get-tuple-element.139), channel_id=1, source_target_pairs={{0,8},{4,12},{8,0},{12,4},{1,9},{5,13},{9,1},{13,5},{2,10},{6,14},... | collective-permute-start | bytes 196616 | tf_op jit(solution)/shard_map/ppermute | solution.py:338
  71.9 6.3 %collective-permute-start.25 = (f32[128,128]{1,0:T(8,128)S(1)}, f32[128,128]{1,0:T(8,128)S(1)}, u32[]{:S(2)}, u32[]{:S(2)}) collective-permute-start(f32[128,128]{1,0:T(8,128)S(1)} %get-tuple-element.140), channel_id=1, source_target_pairs={{0,4},{4,0},{8,12},{12,8},{1,5},{5,1},{9,13},{13,9},{2,6},{6,2},{1... | collective-permute-start | bytes 196616 | tf_op jit(solution)/shard_map/ppermute | solution.py:338
  73.5 6.1 %collective-permute-start.26 = (f32[128,128]{1,0:T(8,128)S(1)}, f32[128,128]{1,0:T(8,128)S(1)}, u32[]{:S(2)}, u32[]{:S(2)}) collective-permute-start(f32[128,128]{1,0:T(8,128)S(1)} %get-tuple-element.141), channel_id=1, source_target_pairs={{0,12},{4,8},{8,4},{12,0},{1,13},{5,9},{9,5},{13,1},{2,14},{6,10},... | collective-permute-start | bytes 196616 | tf_op jit(solution)/shard_map/ppermute | solution.py:338
  80.2 6.6 %collective-permute-start.27 = (f32[128,128]{1,0:T(8,128)S(1)}, f32[128,128]{1,0:T(8,128)S(1)}, u32[]{:S(2)}, u32[]{:S(2)}) collective-permute-start(f32[128,128]{1,0:T(8,128)S(1)} %get-tuple-element.146), channel_id=1, source_target_pairs={{0,8},{4,12},{8,0},{12,4},{1,9},{5,13},{9,1},{13,5},{2,10},{6,14},... | collective-permute-start | bytes 196616 | tf_op jit(solution)/shard_map/ppermute | solution.py:338
  81.5 6.1 %collective-permute-start.28 = (f32[128,128]{1,0:T(8,128)S(1)}, f32[128,128]{1,0:T(8,128)S(1)}, u32[]{:S(2)}, u32[]{:S(2)}) collective-permute-start(f32[128,128]{1,0:T(8,128)S(1)} %get-tuple-element.147), channel_id=1, source_target_pairs={{0,12},{4,8},{8,4},{12,0},{1,13},{5,9},{9,5},{13,1},{2,14},{6,10},... | collective-permute-start | bytes 196616 | tf_op jit(solution)/shard_map/ppermute | solution.py:338
  83.6 4.7 %collective-permute-start.29 = (f32[128,128]{1,0:T(8,128)S(1)}, f32[128,128]{1,0:T(8,128)S(1)}, u32[]{:S(2)}, u32[]{:S(2)}) collective-permute-start(f32[128,128]{1,0:T(8,128)S(1)} %get-tuple-element.148), channel_id=1, source_target_pairs={{0,4},{4,0},{8,12},{12,8},{1,5},{5,1},{9,13},{13,9},{2,6},{6,2},{1... | collective-permute-start | bytes 196616 | tf_op jit(solution)/shard_map/ppermute | solution.py:338

commit v20 on v19

--- a/solution.py
+++ b/solution.py
@@ -164,18 +164,16 @@
         out[...] = picked[d * cap:(d + 1) * cap]
 
 
-def arrived(times, recvs, shared, unpack):
+def arrived(times, recvs, shared, unpack, chunk):
     blocks = [recvs[times.index(d)][...][:shared] for d in sorted(times)]
     rows = sum(b.shape[0] for b in blocks)
     if rows < unpack.shape[1]:
         blocks.append(jnp.zeros((unpack.shape[1] - rows, blocks[0].shape[1]), F32))
     halves = jnp.concatenate(split(jnp.concatenate(blocks, axis=0)), axis=1)
     width = blocks[0].shape[1]
-    chunks = []
-    for at in range(0, shared, 128):
-        both = mm(unpack[at:at + 128, :], halves)
-        chunks.append(both[:, :width] + both[:, width:])
-    return jnp.concatenate(chunks, axis=0)
+    for at in range(0, shared, chunk):
+        both = mm(unpack[at:at + chunk, :], halves)
+        yield both[:, :width] + both[:, width:]
 
 
 def base_kernel(image, unpack_own, gap, base):
@@ -187,10 +185,12 @@
     return jnp.where(alive, jnp.maximum(trial, floor), 0.0)
 
 
-def shared_residual(times, recvs, base, unpack, size):
+def shared_residual(times, recvs, base, unpack, size, chunk):
     known = base[...]
+    shared = known.shape[0]
+    across = jnp.concatenate(list(arrived(times, recvs, shared, unpack, chunk)), axis=0)
     alive = live(size[0], 0, *known.shape)
-    return jnp.where(alive, known + arrived(times, recvs, known.shape[0], unpack), 0.0), alive
+    return jnp.where(alive, known + across, 0.0), alive
 
 
 def rest_start_kernel(size, operator, mult, mult_block, gap, modes, trial, coarse, high, low, halves):
@@ -256,7 +256,7 @@
     recvs = refs[:n]
     base, unpack, mult, modes, started, trial = refs[n:n + 6]
     shared = base.shape[0]
-    residual, _ = shared_residual(times, recvs, base, unpack, size)
+    residual, _ = shared_residual(times, recvs, base, unpack, size, 128)
     coarse = started[...] + product(split(modes[:, :shared]), split(residual))
     for out in refs[n + 6:]:
         out[...] = coarse
@@ -309,7 +309,7 @@
     recvs = refs[:n]
     base, unpack, mult, floor, high, low, ahead, mult_out, image_out = refs[n:n + 9]
     shared = base.shape[0]
-    residual, alive = shared_residual(times, recvs, base, unpack, size)
+    residual, alive = shared_residual(times, recvs, base, unpack, size, shared)
     value = settle(mult[...] + STEP * residual, floor[:shared, :], alive)
     mult_out[...] = value
     both = ahead[...] + product((high[...], low[...]), split(value))
@@ -323,15 +323,21 @@
     recvs = refs[:n]
     base, unpack, mult, floor, _, _, mult_out, residual_out, settled, left, done = refs[n:]
     shared = base.shape[0]
-    residual, alive = shared_residual(times, recvs, base, unpack, size)
-    left[...] = residual
-    first = pltpu.make_async_copy(left, residual_out.at[pl.ds(0, shared)], done.at[0])
-    first.start()
-    settled[...] = settle(mult[...] + STEP * residual, floor[:shared, :], alive)
-    second = pltpu.make_async_copy(settled, mult_out.at[pl.ds(0, shared)], done.at[1])
-    second.start()
-    first.wait()
-    second.wait()
+    copies = []
+    for k, across in enumerate(arrived(times, recvs, shared, unpack, 128)):
+        rows, at = slice(k * 128, (k + 1) * 128), pl.ds(k * 128, 128)
+        alive = live(size[0], k * 128, *across.shape)
+        residual = jnp.where(alive, base[rows, :] + across, 0.0)
+        left[rows, :] = residual
+        settled[rows, :] = settle(mult[rows, :] + STEP * residual, floor[rows, :], alive)
+        copies += [
+            pltpu.make_async_copy(left.at[at], residual_out.at[at], done.at[2 * k]),
+            pltpu.make_async_copy(settled.at[at], mult_out.at[at], done.at[2 * k + 1]),
+        ]
+        for copy in copies[-2:]:
+            copy.start()
+    for copy in copies:
+        copy.wait()
 
 
 def swap(block, axis, count, d):
@@ -547,7 +553,7 @@
                     [shape(order, loads)] * 2,
                     in_specs=[SMEM] + [VMEM] * (len(shadow) - 1) + [HBM] * 2,
                     out_specs=[HBM] * 2,
-                    scratch=[pltpu.VMEM((shared, loads), F32)] * 2 + [pltpu.SemaphoreType.DMA((2,))],
+                    scratch=[pltpu.VMEM((shared, loads), F32)] * 2 + [pltpu.SemaphoreType.DMA((2 * (shared // 128),))],
                     alias={len(shadow): 0, len(shadow) + 1: 1},
                     name="last",
                     **cost,

time: 89.5 us -> 89.4 us (level)
  no operation moved by 1% of the time
where the time goes in v20:
time: 89.4 us; the launch traced here: 89.2 us
  starting transfers between devices  36.7 us (41%)
  waiting for transfers between devices  29.5 us (33%)
  Pallas kernels  21.5 us (24%)
  between operations  1.56 us (2%)
    ppermute x30, starting transfers between devices, swap(): return lax.ppermute(block, axis, [(i, i ^ d) for i in range(count)])  36.7 us
    ppermute x30, waiting for transfers between devices, swap(): return lax.ppermute(block, axis, [(i, i ^ d) for i in range(count)])  29.5 us
    pallas_call x25, Pallas kernels, call(): pl.pallas_call(body, out_shape=outs, grid=grid, in_specs=in_specs, out_sp...  21.5 us
  transfers between devices with their start and end apart: 30, of which 25 were waited for; matrix products, arithmetic and copies ran while one was open for 0% of the time, Pallas kernels for 16%

profile of v20, /device:TPU:0, one launch (start us, length us, event | category | flops | bytes accessed | tf_op | source)
XLA Modules:
  0.0 89.2 jit_solution(4545157396100250064)
XLA Ops:
  0.6 2.0 %first.1 = (bf16[256,256]{1,0:T(8,128)(2,1)S(1)}, bf16[256,768]{1,0:T(8,128)(2,1)S(1)}, bf16[256,384]{1,0:T(8,128)(2,1)S(1)}, bf16[256,1024]{1,0:T(8,128)(2,1)S(...) custom-call(s32[1,256]{1,0:T(1,128)} %bitcast.32, ...), custom_call_target="tpu_custom_call" | custom-call | flops 201326592 | bytes 2097152 | tf_op jit(solution)/shard_map/first/pallas_call | solution.py:49
  2.6 5.1 %collective-permute-start = (f32[264,128]{1,0:T(8,128)S(1)}, f32[264,128]{1,0:T(8,128)S(1)}, u32[]{:S(2)}, u32[]{:S(2)}) collective-permute-start(f32[264,128]{1,0:T(8,128)S(1)} %get-tuple-element.81), channel_id=1, source_target_pairs={{0,12},{4,8},{8,4},{12,0},{1,13},{5,9},{9,5},{13,1},{2,14},{6,10},... | collective-permute-start | bytes 405512 | tf_op jit(solution)/shard_map/ppermute | solution.py:344
  7.7 0.6 collective-permute-start.2
  9.3 4.6 %rest_start.1 = (f32[768,128]{1,0:T(8,128)S(1)}, f32[64,128]{1,0:T(8,128)S(1)}, bf16[768,1024]{1,0:T(8,128)(2,1)S(1)}, bf16[768,1024]{1,0:T(8,128)(2,1)S(1)}) custom-call(s32[1]{0:T(128)S(6)} %copy.15.size, f32[1024,1024]{1,0:T(8,128)} %bitcast.29, f32[1024,128]{1,0:T(8,128)} %bitcast.20, f32[1024,128]{1,0:T(8,128)} %bitcast.21, f32[1024,128]{1,0:T(8,128)} %bitcast.7, ...), custom_call_target="tpu_custom_call" | custom-call | flops 603979776 | bytes 6291456 | tf_op jit(solution)/shard_map/rest_start/pallas_call | solution.py:49
  13.9 1.4 %collective-permute-done.1.refs_1_ = f32[264,128]{1,0:T(8,128)S(1)} collective-permute-done((f32[264,128]{1,0:T(8,128)S(1)}, f32[264,128]{1,0:T(8,128)S(1)}, u32[]{:S(2)}, u32[]{:S(2)}) %collective-permute-start.1) | collective-permute-done | bytes 135200 | tf_op jit(solution)/shard_map/ppermute | solution.py:344
  15.3 3.9 %collective-permute-done.2.refs_2_ = f32[264,128]{1,0:T(8,128)S(1)} collective-permute-done((f32[264,128]{1,0:T(8,128)S(1)}, f32[264,128]{1,0:T(8,128)S(1)}, u32[]{:S(2)}, u32[]{:S(2)}) %collective-permute-start.2) | collective-permute-done | bytes 135200 | tf_op jit(solution)/shard_map/ppermute | solution.py:344
  19.2 0.4 coarse.2
  19.6 0.8 collective-permute-start.3
  20.4 1.8 %collective-permute-start.4 = (f32[64,128]{1,0:T(8,128)S(1)}, f32[64,128]{1,0:T(8,128)S(1)}, u32[]{:S(2)}, u32[]{:S(2)}) collective-permute-start(f32[64,128]{1,0:T(8,128)S(1)} %get-tuple-element.90), channel_id=1, source_target_pairs={{0,12},{4,8},{8,4},{12,0},{1,13},{5,9},{9,5},{13,1},{2,14},{6,10},... | collective-permute-start | bytes 98312 | tf_op jit(solution)/shard_map/ppermute | solution.py:344
  22.2 0.9 %collective-permute-start.5 = (f32[64,128]{1,0:T(8,128)S(1)}, f32[64,128]{1,0:T(8,128)S(1)}, u32[]{:S(2)}, u32[]{:S(2)}) collective-permute-start(f32[64,128]{1,0:T(8,128)S(1)} %get-tuple-element.91), channel_id=1, source_target_pairs={{0,4},{4,0},{8,12},{12,8},{1,5},{5,1},{9,13},{13,9},{2,6},{6,2},{1... | collective-permute-start | bytes 98312 | tf_op jit(solution)/shard_map/ppermute | solution.py:344
  23.2 0.4 prepare.1
  23.6 1.1 %collective-permute-done.3.refs_1_ = f32[64,128]{1,0:T(8,128)S(1)} collective-permute-done((f32[64,128]{1,0:T(8,128)S(1)}, f32[64,128]{1,0:T(8,128)S(1)}, u32[]{:S(2)}, u32[]{:S(2)}) %collective-permute-start.3) | collective-permute-done | bytes 32800 | tf_op jit(solution)/shard_map/ppermute | solution.py:344
  24.6 1.7 %collective-permute-done.4.refs_2_ = f32[64,128]{1,0:T(8,128)S(1)} collective-permute-done((f32[64,128]{1,0:T(8,128)S(1)}, f32[64,128]{1,0:T(8,128)S(1)}, u32[]{:S(2)}, u32[]{:S(2)}) %collective-permute-start.4) | collective-permute-done | bytes 32800 | tf_op jit(solution)/shard_map/ppermute | solution.py:344
  26.8 1.6 %collective-permute-start.7 = (f32[64,128]{1,0:T(8,128)S(1)}, f32[64,128]{1,0:T(8,128)S(1)}, u32[]{:S(2)}, u32[]{:S(2)}) collective-permute-start(f32[64,128]{1,0:T(8,128)S(1)} %get-tuple-element.94), channel_id=1, source_target_pairs={{0,2},{1,3},{2,0},{3,1},{4,6},{5,7},{6,4},{7,5},{8,10},{9,11},{10,... | collective-permute-start | bytes 98312 | tf_op jit(solution)/shard_map/ppermute | solution.py:344
  28.7 0.3 pack.1
  29.0 1.5 %collective-permute-done.6.refs_1_ = f32[64,128]{1,0:T(8,128)S(1)} collective-permute-done((f32[64,128]{1,0:T(8,128)S(1)}, f32[64,128]{1,0:T(8,128)S(1)}, u32[]{:S(2)}, u32[]{:S(2)}) %collective-permute-start.6) | collective-permute-done | bytes 32800 | tf_op jit(solution)/shard_map/ppermute | solution.py:344
  30.5 0.4 collective-permute-done.7.refs_2_
  30.9 0.9 lift.2
  31.7 1.7 %collective-permute-start.9 = (f32[128,128]{1,0:T(8,128)S(1)}, f32[128,128]{1,0:T(8,128)S(1)}, u32[]{:S(2)}, u32[]{:S(2)}) collective-permute-start(f32[128,128]{1,0:T(8,128)S(1)} %get-tuple-element.103), channel_id=1, source_target_pairs={{0,8},{4,12},{8,0},{12,4},{1,9},{5,13},{9,1},{13,5},{2,10},{6,14},... | collective-permute-start | bytes 196616 | tf_op jit(solution)/shard_map/ppermute | solution.py:344
  33.4 0.8 collective-permute-start.10
  34.2 2.0 %collective-permute-start.11 = (f32[128,128]{1,0:T(8,128)S(1)}, f32[128,128]{1,0:T(8,128)S(1)}, u32[]{:S(2)}, u32[]{:S(2)}) collective-permute-start(f32[128,128]{1,0:T(8,128)S(1)} %get-tuple-element.105), channel_id=1, source_target_pairs={{0,12},{4,8},{8,4},{12,0},{1,13},{5,9},{9,5},{13,1},{2,14},{6,10},... | collective-permute-start | bytes 196616 | tf_op jit(solution)/shard_map/ppermute | solution.py:344
  36.4 1.5 %rest.3 = (f32[768,128]{1,0:T(8,128)S(1)}, f32[640,128]{1,0:T(8,128)S(1)}) custom-call(s32[1]{0:T(128)S(6)} %copy.15.size, bf16[768,1024]{1,0:T(8,128)(2,1)S(1)} %get-tuple-element.111.high, bf16[768,1024]{1,0:T(8,128)(2,1)S(1)} %get-tuple-element.112.low, f32[256,128]{1,0:T(8,128)S(1)} %get-tuple-element.108.mult_s.refs_5_, ...), custom_call_target="tpu_custom_call" | custom-call | flops 805306368 | bytes 4194304 | tf_op jit(solution)/shard_map/rest/pallas_call | solution.py:49
  37.9 1.4 %collective-permute-done.9.refs_0_ = f32[128,128]{1,0:T(8,128)S(1)} collective-permute-done((f32[128,128]{1,0:T(8,128)S(1)}, f32[128,128]{1,0:T(8,128)S(1)}, u32[]{:S(2)}, u32[]{:S(2)}) %collective-permute-start.9) | collective-permute-done | bytes 65568 | tf_op jit(solution)/shard_map/ppermute | solution.py:344
  39.3 0.7 collective-permute-done.10.refs_1_
  40.0 0.3 collective-permute-done.11.refs_2_
  40.3 0.5 sweep.3
  40.8 1.9 %collective-permute-start.12 = (f32[128,128]{1,0:T(8,128)S(1)}, f32[128,128]{1,0:T(8,128)S(1)}, u32[]{:S(2)}, u32[]{:S(2)}) collective-permute-start(f32[128,128]{1,0:T(8,128)S(1)} %get-tuple-element.115), channel_id=1, source_target_pairs={{0,8},{4,12},{8,0},{12,4},{1,9},{5,13},{9,1},{13,5},{2,10},{6,14},... | collective-permute-start | bytes 196616 | tf_op jit(solution)/shard_map/ppermute | solution.py:344
  42.8 2.0 %collective-permute-start.13 = (f32[128,128]{1,0:T(8,128)S(1)}, f32[128,128]{1,0:T(8,128)S(1)}, u32[]{:S(2)}, u32[]{:S(2)}) collective-permute-start(f32[128,128]{1,0:T(8,128)S(1)} %get-tuple-element.116), channel_id=1, source_target_pairs={{0,12},{4,8},{8,4},{12,0},{1,13},{5,9},{9,5},{13,1},{2,14},{6,10},... | collective-permute-start | bytes 196616 | tf_op jit(solution)/shard_map/ppermute | solution.py:344
  45.0 1.5 %rest.4 = (f32[768,128]{1,0:T(8,128)S(1)}, f32[640,128]{1,0:T(8,128)S(1)}) custom-call(s32[1]{0:T(128)S(6)} %copy.15.size, bf16[768,1024]{1,0:T(8,128)(2,1)S(1)} %get-tuple-element.111.high, bf16[768,1024]{1,0:T(8,128)(2,1)S(1)} %get-tuple-element.112.low, f32[256,128]{1,0:T(8,128)S(1)} %get-tuple-element.119.mult_s.refs_5_, ...), custom_call_target="tpu_custom_call" | custom-call | flops 805306368 | bytes 4194304 | tf_op jit(solution)/shard_map/rest/pallas_call | solution.py:49
  46.5 1.9 %collective-permute-done.12.refs_0_ = f32[128,128]{1,0:T(8,128)S(1)} collective-permute-done((f32[128,128]{1,0:T(8,128)S(1)}, f32[128,128]{1,0:T(8,128)S(1)}, u32[]{:S(2)}, u32[]{:S(2)}) %collective-permute-start.12) | collective-permute-done | bytes 65568 | tf_op jit(solution)/shard_map/ppermute | solution.py:344
  48.3 0.9 %collective-permute-done.13.refs_1_ = f32[128,128]{1,0:T(8,128)S(1)} collective-permute-done((f32[128,128]{1,0:T(8,128)S(1)}, f32[128,128]{1,0:T(8,128)S(1)}, u32[]{:S(2)}, u32[]{:S(2)}) %collective-permute-start.13) | collective-permute-done | bytes 65568 | tf_op jit(solution)/shard_map/ppermute | solution.py:344
  49.3 0.6 collective-permute-done.14.refs_2_
  49.9 0.5 sweep.4
  50.4 0.8 collective-permute-start.15
  51.2 1.9 %collective-permute-start.16 = (f32[128,128]{1,0:T(8,128)S(1)}, f32[128,128]{1,0:T(8,128)S(1)}, u32[]{:S(2)}, u32[]{:S(2)}) collective-permute-start(f32[128,128]{1,0:T(8,128)S(1)} %get-tuple-element.123), channel_id=1, source_target_pairs={{0,12},{4,8},{8,4},{12,0},{1,13},{5,9},{9,5},{13,1},{2,14},{6,10},... | collective-permute-start | bytes 196616 | tf_op jit(solution)/shard_map/ppermute | solution.py:344
  53.1 0.9 collective-permute-start.17
  54.2 1.1 %rest_first.1 = (f32[768,128]{1,0:T(8,128)S(1)}, f32[64,128]{1,0:T(8,128)S(1)}) custom-call(s32[1]{0:T(128)S(6)} %copy.15.size, bf16[768,1024]{1,0:T(8,128)(2,1)S(1)} %get-tuple-element.111.high, bf16[768,1024]{1,0:T(8,128)(2,1)S(1)} %get-tuple-element.112.low, f32[256,128]{1,0:T(8,128)S(1)} %get-tuple-element.126.mult_s.refs_5_, ...), custom_call_target="tpu_custom_call" | custom-call | flops 603979776 | bytes 3145728 | tf_op jit(solution)/shard_map/rest_first/pallas_call | solution.py:49
  55.3 2.5 %collective-permute-done.15.refs_0_ = f32[128,128]{1,0:T(8,128)S(1)} collective-permute-done((f32[128,128]{1,0:T(8,128)S(1)}, f32[128,128]{1,0:T(8,128)S(1)}, u32[]{:S(2)}, u32[]{:S(2)}) %collective-permute-start.15) | collective-permute-done | bytes 65568 | tf_op jit(solution)/shard_map/ppermute | solution.py:344
  57.8 0.6 collective-permute-done.17.refs_2_
  58.4 0.4 coarse.3
  58.8 0.4 collective-permute-start.18
  59.3 2.6 %collective-permute-start.19 = (f32[64,128]{1,0:T(8,128)S(1)}, f32[64,128]{1,0:T(8,128)S(1)}, u32[]{:S(2)}, u32[]{:S(2)}) collective-permute-start(f32[64,128]{1,0:T(8,128)S(1)} %get-tuple-element.131), channel_id=1, source_target_pairs={{0,12},{4,8},{8,4},{12,0},{1,13},{5,9},{9,5},{13,1},{2,14},{6,10},... | collective-permute-start | bytes 98312 | tf_op jit(solution)/shard_map/ppermute | solution.py:344
  61.8 0.6 collective-permute-start.20
  62.4 1.7 %collective-permute-done.18.refs_1_ = f32[64,128]{1,0:T(8,128)S(1)} collective-permute-done((f32[64,128]{1,0:T(8,128)S(1)}, f32[64,128]{1,0:T(8,128)S(1)}, u32[]{:S(2)}, u32[]{:S(2)}) %collective-permute-start.18) | collective-permute-done | bytes 32800 | tf_op jit(solution)/shard_map/ppermute | solution.py:344
  64.1 0.9 %collective-permute-done.19.refs_2_ = f32[64,128]{1,0:T(8,128)S(1)} collective-permute-done((f32[64,128]{1,0:T(8,128)S(1)}, f32[64,128]{1,0:T(8,128)S(1)}, u32[]{:S(2)}, u32[]{:S(2)}) %collective-permute-start.19) | collective-permute-done | bytes 32800 | tf_op jit(solution)/shard_map/ppermute | solution.py:344
  65.0 0.8 collective-permute-done.20.refs_3_
  66.4 1.6 %collective-permute-start.23 = (f32[64,128]{1,0:T(8,128)S(1)}, f32[64,128]{1,0:T(8,128)S(1)}, u32[]{:S(2)}, u32[]{:S(2)}) collective-permute-start(f32[64,128]{1,0:T(8,128)S(1)} %get-tuple-element.136), channel_id=1, source_target_pairs={{0,1},{1,0},{2,3},{3,2},{4,5},{5,4},{6,7},{7,6},{8,9},{9,8},{10,11... | collective-permute-start | bytes 98312 | tf_op jit(solution)/shard_map/ppermute | solution.py:344
  67.9 1.5 %collective-permute-done.21.refs_1_ = f32[64,128]{1,0:T(8,128)S(1)} collective-permute-done((f32[64,128]{1,0:T(8,128)S(1)}, f32[64,128]{1,0:T(8,128)S(1)}, u32[]{:S(2)}, u32[]{:S(2)}) %collective-permute-start.21) | collective-permute-done | bytes 32800 | tf_op jit(solution)/shard_map/ppermute | solution.py:344
  69.4 0.7 collective-permute-done.22.refs_2_
  70.1 0.9 lift.3
  71.0 0.8 collective-permute-start.24
  71.8 1.6 %collective-permute-start.25 = (f32[128,128]{1,0:T(8,128)S(1)}, f32[128,128]{1,0:T(8,128)S(1)}, u32[]{:S(2)}, u32[]{:S(2)}) collective-permute-start(f32[128,128]{1,0:T(8,128)S(1)} %get-tuple-element.140), channel_id=1, source_target_pairs={{0,4},{4,0},{8,12},{12,8},{1,5},{5,1},{9,13},{13,9},{2,6},{6,2},{1... | collective-permute-start | bytes 196616 | tf_op jit(solution)/shard_map/ppermute | solution.py:344
  73.4 2.0 %collective-permute-start.26 = (f32[128,128]{1,0:T(8,128)S(1)}, f32[128,128]{1,0:T(8,128)S(1)}, u32[]{:S(2)}, u32[]{:S(2)}) collective-permute-start(f32[128,128]{1,0:T(8,128)S(1)} %get-tuple-element.141), channel_id=1, source_target_pairs={{0,12},{4,8},{8,4},{12,0},{1,13},{5,9},{9,5},{13,1},{2,14},{6,10},... | collective-permute-start | bytes 196616 | tf_op jit(solution)/shard_map/ppermute | solution.py:344
  75.6 1.5 %rest.5 = (f32[768,128]{1,0:T(8,128)S(1)}, f32[640,128]{1,0:T(8,128)S(1)}) custom-call(s32[1]{0:T(128)S(6)} %copy.15.size, bf16[768,1024]{1,0:T(8,128)(2,1)S(1)} %get-tuple-element.111.high, bf16[768,1024]{1,0:T(8,128)(2,1)S(1)} %get-tuple-element.112.low, f32[256,128]{1,0:T(8,128)S(1)} %get-tuple-element.143.mult_s.refs_5_, ...), custom_call_target="tpu_custom_call" | custom-call | flops 805306368 | bytes 4194304 | tf_op jit(solution)/shard_map/rest/pallas_call | solution.py:49
  77.1 1.0 %collective-permute-done.24.refs_0_ = f32[128,128]{1,0:T(8,128)S(1)} collective-permute-done((f32[128,128]{1,0:T(8,128)S(1)}, f32[128,128]{1,0:T(8,128)S(1)}, u32[]{:S(2)}, u32[]{:S(2)}) %collective-permute-start.24) | collective-permute-done | bytes 65568 | tf_op jit(solution)/shard_map/ppermute | solution.py:344
  78.2 1.4 %collective-permute-done.26.refs_2_ = f32[128,128]{1,0:T(8,128)S(1)} collective-permute-done((f32[128,128]{1,0:T(8,128)S(1)}, f32[128,128]{1,0:T(8,128)S(1)}, u32[]{:S(2)}, u32[]{:S(2)}) %collective-permute-start.26) | collective-permute-done | bytes 65568 | tf_op jit(solution)/shard_map/ppermute | solution.py:344
  79.5 0.5 sweep.5
  80.1 1.4 %collective-permute-start.27 = (f32[128,128]{1,0:T(8,128)S(1)}, f32[128,128]{1,0:T(8,128)S(1)}, u32[]{:S(2)}, u32[]{:S(2)}) collective-permute-start(f32[128,128]{1,0:T(8,128)S(1)} %get-tuple-element.146), channel_id=1, source_target_pairs={{0,8},{4,12},{8,0},{12,4},{1,9},{5,13},{9,1},{13,5},{2,10},{6,14},... | collective-permute-start | bytes 196616 | tf_op jit(solution)/shard_map/ppermute | solution.py:344
  81.4 2.1 %collective-permute-start.28 = (f32[128,128]{1,0:T(8,128)S(1)}, f32[128,128]{1,0:T(8,128)S(1)}, u32[]{:S(2)}, u32[]{:S(2)}) collective-permute-start(f32[128,128]{1,0:T(8,128)S(1)} %get-tuple-element.147), channel_id=1, source_target_pairs={{0,12},{4,8},{8,4},{12,0},{1,13},{5,9},{9,5},{13,1},{2,14},{6,10},... | collective-permute-start | bytes 196616 | tf_op jit(solution)/shard_map/ppermute | solution.py:344
  83.8 1.9 %rest_last.1 = (f32[1024,128]{1,0:T(8,128)}, f32[1024,128]{1,0:T(8,128)}) custom-call(s32[1]{0:T(128)S(6)} %copy.15.size, bf16[768,1024]{1,0:T(8,128)(2,1)S(1)} %get-tuple-element.111.high, bf16[768,1024]{1,0:T(8,128)(2,1)S(1)} %get-tuple-element.112.low, f32[256,128]{1,0:T(8,128)S(1)} %get-tuple-element.150.mult_s.refs_5_, ...), custom_call_target="tpu_custom_call" | custom-call | flops 603979776 | bytes 3145728 | tf_op jit(solution)/shard_map/rest_last/pallas_call | solution.py:49
  85.7 1.1 %collective-permute-done.27.refs_0_ = f32[128,128]{1,0:T(8,128)S(1)} collective-permute-done((f32[128,128]{1,0:T(8,128)S(1)}, f32[128,128]{1,0:T(8,128)S(1)}, u32[]{:S(2)}, u32[]{:S(2)}) %collective-permute-start.27) | collective-permute-done | bytes 65568 | tf_op jit(solution)/shard_map/ppermute | solution.py:344
  86.8 0.8 collective-permute-done.28.refs_1_
  87.6 0.7 collective-permute-done.29.refs_2_
  88.2 1.0 %last.1 = (f32[1024,128]{1,0:T(8,128)}, f32[1024,128]{1,0:T(8,128)}) custom-call(s32[1]{0:T(128)S(6)} %copy.15.size, f32[128,128]{1,0:T(8,128)S(1)} %collective-permute-done.27.refs_0_, f32[128,128]{1,0:T(8,128)S(1)} %collective-permute-done.28.refs_1_, ...), custom_call_target="tpu_custom_call", output_to_operand_aliasing={{0}: (8, {}), {1}: (9, {})} | custom-call | flops 75497472 | bytes 196608 | tf_op jit(solution)/shard_map/last/pallas_call | solution.py:49
  (33 shorter events, 2.7 us)
Async XLA Ops:
  0.6 8.4 %copy-start = (f32[1,1024,128]{2,1,0:T(8,128)S(1)}, f32[1,1024,128]{2,1,0:T(8,128)}, u32[]{:S(2)}) copy-start(f32[1,1024,128]{2,1,0:T(8,128)} %param.12) | copy-start | bytes 1572868
  2.6 11.3 %collective-permute-start = (f32[264,128]{1,0:T(8,128)S(1)}, f32[264,128]{1,0:T(8,128)S(1)}, u32[]{:S(2)}, u32[]{:S(2)}) collective-permute-start(f32[264,128]{1,0:T(8,128)S(1)} %get-tuple-element.81), channel_id=1, source_target_pairs={{0,12},{4,8},{8,4},{12,0},{1,13},{5,9},{9,5},{13,1},{2,14},{6,10},... | collective-permute-start | bytes 405512 | tf_op jit(solution)/shard_map/ppermute | solution.py:344
  7.7 7.6 %collective-permute-start.1 = (f32[264,128]{1,0:T(8,128)S(1)}, f32[264,128]{1,0:T(8,128)S(1)}, u32[]{:S(2)}, u32[]{:S(2)}) collective-permute-start(f32[264,128]{1,0:T(8,128)S(1)} %get-tuple-element.82), channel_id=1, source_target_pairs={{0,4},{4,0},{8,12},{12,8},{1,5},{5,1},{9,13},{13,9},{2,6},{6,2},{1... | collective-permute-start | bytes 405512 | tf_op jit(solution)/shard_map/ppermute | solution.py:344
  7.7 11.4 %collective-permute-start.2 = (f32[264,128]{1,0:T(8,128)S(1)}, f32[264,128]{1,0:T(8,128)S(1)}, u32[]{:S(2)}, u32[]{:S(2)}) collective-permute-start(f32[264,128]{1,0:T(8,128)S(1)} %get-tuple-element.83), channel_id=1, source_target_pairs={{0,8},{4,12},{8,0},{12,4},{1,9},{5,13},{9,1},{13,5},{2,10},{6,14},... | collective-permute-start | bytes 405512 | tf_op jit(solution)/shard_map/ppermute | solution.py:344
  9.2 9.9 %copy-start.2 = (f32[1,1024,128]{2,1,0:T(8,128)S(1)}, f32[1,1024,128]{2,1,0:T(8,128)}, u32[]{:S(2)}) copy-start(f32[1,1024,128]{2,1,0:T(8,128)} %param.13) | copy-start | bytes 1572868
  9.3 9.9 %copy-start.3 = (f32[1,64,1024]{2,1,0:T(8,128)S(1)}, f32[1,64,1024]{2,1,0:T(8,128)}, u32[]{:S(2)}) copy-start(f32[1,64,1024]{2,1,0:T(8,128)} %param.11) | copy-start | bytes 786436
  13.8 9.3 %copy-start.4 = (f32[256,256]{1,0:T(8,128)S(1)}, f32[256,256]{1,0:T(8,128)}, u32[]{:S(2)}) copy-start(f32[256,256]{1,0:T(8,128)} %tile.3) | copy-start | bytes 786436
  13.9 9.3 %copy-start.5 = (s32[1,1024]{1,0:T(1,128)S(1)}, s32[1,1024]{1,0:T(1,128)}, u32[]{:S(2)}) copy-start(s32[1,1024]{1,0:T(1,128)} %contact.1) | copy-start | bytes 12292
  19.6 5.0 %collective-permute-start.3 = (f32[64,128]{1,0:T(8,128)S(1)}, f32[64,128]{1,0:T(8,128)S(1)}, u32[]{:S(2)}, u32[]{:S(2)}) collective-permute-start(f32[64,128]{1,0:T(8,128)S(1)} %get-tuple-element.89), channel_id=1, source_target_pairs={{0,8},{4,12},{8,0},{12,4},{1,9},{5,13},{9,1},{13,5},{2,10},{6,14},... | collective-permute-start | bytes 98312 | tf_op jit(solution)/shard_map/ppermute | solution.py:344
  20.4 5.9 %collective-permute-start.4 = (f32[64,128]{1,0:T(8,128)S(1)}, f32[64,128]{1,0:T(8,128)S(1)}, u32[]{:S(2)}, u32[]{:S(2)}) collective-permute-start(f32[64,128]{1,0:T(8,128)S(1)} %get-tuple-element.90), channel_id=1, source_target_pairs={{0,12},{4,8},{8,4},{12,0},{1,13},{5,9},{9,5},{13,1},{2,14},{6,10},... | collective-permute-start | bytes 98312 | tf_op jit(solution)/shard_map/ppermute | solution.py:344
  22.2 4.3 %collective-permute-start.5 = (f32[64,128]{1,0:T(8,128)S(1)}, f32[64,128]{1,0:T(8,128)S(1)}, u32[]{:S(2)}, u32[]{:S(2)}) collective-permute-start(f32[64,128]{1,0:T(8,128)S(1)} %get-tuple-element.91), channel_id=1, source_target_pairs={{0,4},{4,0},{8,12},{12,8},{1,5},{5,1},{9,13},{13,9},{2,6},{6,2},{1... | collective-permute-start | bytes 98312 | tf_op jit(solution)/shard_map/ppermute | solution.py:344
  26.8 3.7 %collective-permute-start.6 = (f32[64,128]{1,0:T(8,128)S(1)}, f32[64,128]{1,0:T(8,128)S(1)}, u32[]{:S(2)}, u32[]{:S(2)}) collective-permute-start(f32[64,128]{1,0:T(8,128)S(1)} %get-tuple-element.93), channel_id=1, source_target_pairs={{0,3},{1,2},{2,1},{3,0},{4,7},{5,6},{6,5},{7,4},{8,11},{9,10},{10,... | collective-permute-start | bytes 98312 | tf_op jit(solution)/shard_map/ppermute | solution.py:344
  26.8 4.0 %collective-permute-start.7 = (f32[64,128]{1,0:T(8,128)S(1)}, f32[64,128]{1,0:T(8,128)S(1)}, u32[]{:S(2)}, u32[]{:S(2)}) collective-permute-start(f32[64,128]{1,0:T(8,128)S(1)} %get-tuple-element.94), channel_id=1, source_target_pairs={{0,2},{1,3},{2,0},{3,1},{4,6},{5,7},{6,4},{7,5},{8,10},{9,11},{10,... | collective-permute-start | bytes 98312 | tf_op jit(solution)/shard_map/ppermute | solution.py:344
  28.4 2.5 %collective-permute-start.8 = (f32[64,128]{1,0:T(8,128)S(1)}, f32[64,128]{1,0:T(8,128)S(1)}, u32[]{:S(2)}, u32[]{:S(2)}) collective-permute-start(f32[64,128]{1,0:T(8,128)S(1)} %get-tuple-element.95), channel_id=1, source_target_pairs={{0,1},{1,0},{2,3},{3,2},{4,5},{5,4},{6,7},{7,6},{8,9},{9,8},{10,11... | collective-permute-start | bytes 98312 | tf_op jit(solution)/shard_map/ppermute | solution.py:344
  29.0 7.2 %copy-start.1 = (f32[1,1024,128]{2,1,0:T(8,128)S(1)}, f32[1,1024,128]{2,1,0:T(8,128)}, u32[]{:S(2)}) copy-start(f32[1,1024,128]{2,1,0:T(8,128)} %param.12) | copy-start | bytes 1572868
  31.7 7.6 %collective-permute-start.9 = (f32[128,128]{1,0:T(8,128)S(1)}, f32[128,128]{1,0:T(8,128)S(1)}, u32[]{:S(2)}, u32[]{:S(2)}) collective-permute-start(f32[128,128]{1,0:T(8,128)S(1)} %get-tuple-element.103), channel_id=1, source_target_pairs={{0,8},{4,12},{8,0},{12,4},{1,9},{5,13},{9,1},{13,5},{2,10},{6,14},... | collective-permute-start | bytes 196616 | tf_op jit(solution)/shard_map/ppermute | solution.py:344
  33.4 6.6 %collective-permute-start.10 = (f32[128,128]{1,0:T(8,128)S(1)}, f32[128,128]{1,0:T(8,128)S(1)}, u32[]{:S(2)}, u32[]{:S(2)}) collective-permute-start(f32[128,128]{1,0:T(8,128)S(1)} %get-tuple-element.104), channel_id=1, source_target_pairs={{0,4},{4,0},{8,12},{12,8},{1,5},{5,1},{9,13},{13,9},{2,6},{6,2},{1... | collective-permute-start | bytes 196616 | tf_op jit(solution)/shard_map/ppermute | solution.py:344
  34.2 6.1 %collective-permute-start.11 = (f32[128,128]{1,0:T(8,128)S(1)}, f32[128,128]{1,0:T(8,128)S(1)}, u32[]{:S(2)}, u32[]{:S(2)}) collective-permute-start(f32[128,128]{1,0:T(8,128)S(1)} %get-tuple-element.105), channel_id=1, source_target_pairs={{0,12},{4,8},{8,4},{12,0},{1,13},{5,9},{9,5},{13,1},{2,14},{6,10},... | collective-permute-start | bytes 196616 | tf_op jit(solution)/shard_map/ppermute | solution.py:344
  40.8 7.5 %collective-permute-start.12 = (f32[128,128]{1,0:T(8,128)S(1)}, f32[128,128]{1,0:T(8,128)S(1)}, u32[]{:S(2)}, u32[]{:S(2)}) collective-permute-start(f32[128,128]{1,0:T(8,128)S(1)} %get-tuple-element.115), channel_id=1, source_target_pairs={{0,8},{4,12},{8,0},{12,4},{1,9},{5,13},{9,1},{13,5},{2,10},{6,14},... | collective-permute-start | bytes 196616 | tf_op jit(solution)/shard_map/ppermute | solution.py:344
  42.8 6.5 %collective-permute-start.13 = (f32[128,128]{1,0:T(8,128)S(1)}, f32[128,128]{1,0:T(8,128)S(1)}, u32[]{:S(2)}, u32[]{:S(2)}) collective-permute-start(f32[128,128]{1,0:T(8,128)S(1)} %get-tuple-element.116), channel_id=1, source_target_pairs={{0,12},{4,8},{8,4},{12,0},{1,13},{5,9},{9,5},{13,1},{2,14},{6,10},... | collective-permute-start | bytes 196616 | tf_op jit(solution)/shard_map/ppermute | solution.py:344
  44.8 5.1 %collective-permute-start.14 = (f32[128,128]{1,0:T(8,128)S(1)}, f32[128,128]{1,0:T(8,128)S(1)}, u32[]{:S(2)}, u32[]{:S(2)}) collective-permute-start(f32[128,128]{1,0:T(8,128)S(1)} %get-tuple-element.117), channel_id=1, source_target_pairs={{0,4},{4,0},{8,12},{12,8},{1,5},{5,1},{9,13},{13,9},{2,6},{6,2},{1... | collective-permute-start | bytes 196616 | tf_op jit(solution)/shard_map/ppermute | solution.py:344
  50.4 7.4 %collective-permute-start.15 = (f32[128,128]{1,0:T(8,128)S(1)}, f32[128,128]{1,0:T(8,128)S(1)}, u32[]{:S(2)}, u32[]{:S(2)}) collective-permute-start(f32[128,128]{1,0:T(8,128)S(1)} %get-tuple-element.122), channel_id=1, source_target_pairs={{0,8},{4,12},{8,0},{12,4},{1,9},{5,13},{9,1},{13,5},{2,10},{6,14},... | collective-permute-start | bytes 196616 | tf_op jit(solution)/shard_map/ppermute | solution.py:344
  51.2 6.6 %collective-permute-start.16 = (f32[128,128]{1,0:T(8,128)S(1)}, f32[128,128]{1,0:T(8,128)S(1)}, u32[]{:S(2)}, u32[]{:S(2)}) collective-permute-start(f32[128,128]{1,0:T(8,128)S(1)} %get-tuple-element.123), channel_id=1, source_target_pairs={{0,12},{4,8},{8,4},{12,0},{1,13},{5,9},{9,5},{13,1},{2,14},{6,10},... | collective-permute-start | bytes 196616 | tf_op jit(solution)/shard_map/ppermute | solution.py:344
  53.1 5.3 %collective-permute-start.17 = (f32[128,128]{1,0:T(8,128)S(1)}, f32[128,128]{1,0:T(8,128)S(1)}, u32[]{:S(2)}, u32[]{:S(2)}) collective-permute-start(f32[128,128]{1,0:T(8,128)S(1)} %get-tuple-element.124), channel_id=1, source_target_pairs={{0,4},{4,0},{8,12},{12,8},{1,5},{5,1},{9,13},{13,9},{2,6},{6,2},{1... | collective-permute-start | bytes 196616 | tf_op jit(solution)/shard_map/ppermute | solution.py:344
  58.8 5.2 %collective-permute-start.18 = (f32[64,128]{1,0:T(8,128)S(1)}, f32[64,128]{1,0:T(8,128)S(1)}, u32[]{:S(2)}, u32[]{:S(2)}) collective-permute-start(f32[64,128]{1,0:T(8,128)S(1)} %get-tuple-element.130), channel_id=1, source_target_pairs={{0,8},{4,12},{8,0},{12,4},{1,9},{5,13},{9,1},{13,5},{2,10},{6,14},... | collective-permute-start | bytes 98312 | tf_op jit(solution)/shard_map/ppermute | solution.py:344
  59.3 5.7 %collective-permute-start.19 = (f32[64,128]{1,0:T(8,128)S(1)}, f32[64,128]{1,0:T(8,128)S(1)}, u32[]{:S(2)}, u32[]{:S(2)}) collective-permute-start(f32[64,128]{1,0:T(8,128)S(1)} %get-tuple-element.131), channel_id=1, source_target_pairs={{0,12},{4,8},{8,4},{12,0},{1,13},{5,9},{9,5},{13,1},{2,14},{6,10},... | collective-permute-start | bytes 98312 | tf_op jit(solution)/shard_map/ppermute | solution.py:344
  61.8 3.9 %collective-permute-start.20 = (f32[64,128]{1,0:T(8,128)S(1)}, f32[64,128]{1,0:T(8,128)S(1)}, u32[]{:S(2)}, u32[]{:S(2)}) collective-permute-start(f32[64,128]{1,0:T(8,128)S(1)} %get-tuple-element.132), channel_id=1, source_target_pairs={{0,4},{4,0},{8,12},{12,8},{1,5},{5,1},{9,13},{13,9},{2,6},{6,2},{1... | collective-permute-start | bytes 98312 | tf_op jit(solution)/shard_map/ppermute | solution.py:344
  66.0 3.4 %collective-permute-start.21 = (f32[64,128]{1,0:T(8,128)S(1)}, f32[64,128]{1,0:T(8,128)S(1)}, u32[]{:S(2)}, u32[]{:S(2)}) collective-permute-start(f32[64,128]{1,0:T(8,128)S(1)} %get-tuple-element.134), channel_id=1, source_target_pairs={{0,3},{1,2},{2,1},{3,0},{4,7},{5,6},{6,5},{7,4},{8,11},{9,10},{10,... | collective-permute-start | bytes 98312 | tf_op jit(solution)/shard_map/ppermute | solution.py:344
  66.1 4.0 %collective-permute-start.22 = (f32[64,128]{1,0:T(8,128)S(1)}, f32[64,128]{1,0:T(8,128)S(1)}, u32[]{:S(2)}, u32[]{:S(2)}) collective-permute-start(f32[64,128]{1,0:T(8,128)S(1)} %get-tuple-element.135), channel_id=1, source_target_pairs={{0,2},{1,3},{2,0},{3,1},{4,6},{5,7},{6,4},{7,5},{8,10},{9,11},{10,... | collective-permute-start | bytes 98312 | tf_op jit(solution)/shard_map/ppermute | solution.py:344
  66.4 3.7 %collective-permute-start.23 = (f32[64,128]{1,0:T(8,128)S(1)}, f32[64,128]{1,0:T(8,128)S(1)}, u32[]{:S(2)}, u32[]{:S(2)}) collective-permute-start(f32[64,128]{1,0:T(8,128)S(1)} %get-tuple-element.136), channel_id=1, source_target_pairs={{0,1},{1,0},{2,3},{3,2},{4,5},{5,4},{6,7},{7,6},{8,9},{9,8},{10,11... | collective-permute-start | bytes 98312 | tf_op jit(solution)/shard_map/ppermute | solution.py:344
  71.0 7.2 %collective-permute-start.24 = (f32[128,128]{1,0:T(8,128)S(1)}, f32[128,128]{1,0:T(8,128)S(1)}, u32[]{:S(2)}, u32[]{:S(2)}) collective-permute-start(f32[128,128]{1,0:T(8,128)S(1)} %get-tuple-element.139), channel_id=1, source_target_pairs={{0,8},{4,12},{8,0},{12,4},{1,9},{5,13},{9,1},{13,5},{2,10},{6,14},... | collective-permute-start | bytes 196616 | tf_op jit(solution)/shard_map/ppermute | solution.py:344
  71.8 6.4 %collective-permute-start.25 = (f32[128,128]{1,0:T(8,128)S(1)}, f32[128,128]{1,0:T(8,128)S(1)}, u32[]{:S(2)}, u32[]{:S(2)}) collective-permute-start(f32[128,128]{1,0:T(8,128)S(1)} %get-tuple-element.140), channel_id=1, source_target_pairs={{0,4},{4,0},{8,12},{12,8},{1,5},{5,1},{9,13},{13,9},{2,6},{6,2},{1... | collective-permute-start | bytes 196616 | tf_op jit(solution)/shard_map/ppermute | solution.py:344
  73.4 6.1 %collective-permute-start.26 = (f32[128,128]{1,0:T(8,128)S(1)}, f32[128,128]{1,0:T(8,128)S(1)}, u32[]{:S(2)}, u32[]{:S(2)}) collective-permute-start(f32[128,128]{1,0:T(8,128)S(1)} %get-tuple-element.141), channel_id=1, source_target_pairs={{0,12},{4,8},{8,4},{12,0},{1,13},{5,9},{9,5},{13,1},{2,14},{6,10},... | collective-permute-start | bytes 196616 | tf_op jit(solution)/shard_map/ppermute | solution.py:344
  80.1 6.7 %collective-permute-start.27 = (f32[128,128]{1,0:T(8,128)S(1)}, f32[128,128]{1,0:T(8,128)S(1)}, u32[]{:S(2)}, u32[]{:S(2)}) collective-permute-start(f32[128,128]{1,0:T(8,128)S(1)} %get-tuple-element.146), channel_id=1, source_target_pairs={{0,8},{4,12},{8,0},{12,4},{1,9},{5,13},{9,1},{13,5},{2,10},{6,14},... | collective-permute-start | bytes 196616 | tf_op jit(solution)/shard_map/ppermute | solution.py:344
  81.4 6.1 %collective-permute-start.28 = (f32[128,128]{1,0:T(8,128)S(1)}, f32[128,128]{1,0:T(8,128)S(1)}, u32[]{:S(2)}, u32[]{:S(2)}) collective-permute-start(f32[128,128]{1,0:T(8,128)S(1)} %get-tuple-element.147), channel_id=1, source_target_pairs={{0,12},{4,8},{8,4},{12,0},{1,13},{5,9},{9,5},{13,1},{2,14},{6,10},... | collective-permute-start | bytes 196616 | tf_op jit(solution)/shard_map/ppermute | solution.py:344
  83.6 4.7 %collective-permute-start.29 = (f32[128,128]{1,0:T(8,128)S(1)}, f32[128,128]{1,0:T(8,128)S(1)}, u32[]{:S(2)}, u32[]{:S(2)}) collective-permute-start(f32[128,128]{1,0:T(8,128)S(1)} %get-tuple-element.148), channel_id=1, source_target_pairs={{0,4},{4,0},{8,12},{12,8},{1,5},{5,1},{9,13},{13,9},{2,6},{6,2},{1... | collective-permute-start | bytes 196616 | tf_op jit(solution)/shard_map/ppermute | solution.py:344

commit v21 on v20

--- a/solution.py
+++ b/solution.py
@@ -77,6 +77,14 @@
 
 def shape(rows, columns, dtype=F32):
     return jax.ShapeDtypeStruct((rows, columns), dtype)
+
+
+def lines_of(times):
+    return times if isinstance(times[0], tuple) else (times, times)
+
+
+def by_line(even, odd):
+    return even if odd is even else jnp.where(lax.axis_index("narrow") % 2 == 1, odd, even)
 
 
 def first_kernel(n, cap, peers_at, rows_at, operator_at, mult_at, *refs):
@@ -158,14 +166,17 @@
     tile_high[...], tile_low[...] = split(tile[...])
 
 
-def send(cap, chosen, image, sends):
+def send(times, cap, chosen, image, sends):
     picked = pick(chosen, image)
-    for d, out in enumerate(sends):
-        out[...] = picked[d * cap:(d + 1) * cap]
+    rows = [picked[at:at + cap] for at in range(0, len(sends) * cap, cap)]
+    for out, (even, odd) in zip(sends, zip(*lines_of(times))):
+        out[...] = by_line(rows[even - 1], rows[odd - 1])
 
 
 def arrived(times, recvs, shared, unpack, chunk):
-    blocks = [recvs[times.index(d)][...][:shared] for d in sorted(times)]
+    lines = lines_of(times)
+    got = [recv[...][:shared] for recv in recvs]
+    blocks = [by_line(*(got[line.index(d)] for line in lines)) for d in sorted(lines[0])]
     rows = sum(b.shape[0] for b in blocks)
     if rows < unpack.shape[1]:
         blocks.append(jnp.zeros((unpack.shape[1] - rows, blocks[0].shape[1]), F32))
@@ -276,7 +287,7 @@
         out[...] = parts[pl.ds(at, count), :]
 
 
-def lift_kernel(n, m, cap, size, *refs):
+def lift_kernel(times, m, cap, size, *refs):
     parts = refs[:m + 1]
     ins, (mult_s, mult_n, image), sends, halves = refs[m + 1:m + 8], refs[m + 8:m + 11], refs[m + 11:-1], refs[-1]
     basis, trial_s, trial_n, floor, high, low, pack = ins
@@ -301,11 +312,11 @@
     both = mm(high[...], halves[...])
     value = both[:, :width] + (both[:, width:] + mm(low[...], halves[:, :width]))
     image[...] = value
-    send(cap, pack[...], value, sends)
+    send(times, cap, pack[...], value, sends)
 
 
 def sweep_kernel(times, cap, size, *refs):
-    n = len(times)
+    n = len(lines_of(times)[0])
     recvs = refs[:n]
     base, unpack, mult, floor, high, low, ahead, mult_out, image_out = refs[n:n + 9]
     shared = base.shape[0]
@@ -346,6 +357,17 @@
 
 def swap_all(blocks, axis, count, order):
     return [swap(block, axis, count, d) for block, d in zip(blocks, order)]
+
+
+def swap_lines(blocks, wide, narrow, times):
+    return [
+        lax.ppermute(
+            block,
+            ("wide", "narrow"),
+            [(w * narrow + i, (w ^ ds[i % 2]) * narrow + i) for w in range(wide) for i in range(narrow)],
+        )
+        for block, ds in zip(blocks, zip(*times))
+    ]
 
 
 def swap_rows(blocks, axis, count, times):
@@ -394,8 +416,9 @@
     padded = -(-listed // 128) * 128
     size = interface_size
     coarse_order, part_order = half_first(wide, True), far_first(narrow)
-    half, half_back, middle = half_first(wide, False), half_first(wide, True), middle_first(wide)
-    orders = ((middle, half, half_back), (half_back, half, half_back))
+    half_back, middle = half_first(wide, True), middle_first(wide)
+    apart = tuple(range(1, wide)), half_back
+    orders = ((middle, apart, half_back), (half_back, apart, half_back))
     sent = [shape(cap, loads)] * n
     full = 2 * order * loads
 
@@ -513,7 +536,7 @@
         )
         parts = [own] + swap_all(parts, "narrow", narrow, part_order)
         mult_s, mult_n, image, *sends = call(
-            functools.partial(lift_kernel, n, m, cap),
+            functools.partial(lift_kernel, orders[outer][1], m, cap),
             (size, *parts, basis, trial_s, trial_n, floor, top_high, top_low, pack),
             [shape(shared, loads), shape(rest, loads), shape(shared, loads)] + sent,
             flops=3 * full * shared,
@@ -524,7 +547,10 @@
         for inner in range(1, INNER):
             last = outer == OUTER - 1 and inner == INNER - 1
             times = orders[outer][inner]
-            recvs = swap_rows(sends, "wide", wide, times)
+            if inner == 1:
+                recvs = swap_lines(sends, wide, narrow, times)
+            else:
+                recvs = swap_rows(sends, "wide", wide, times)
             base = call(
                 base_kernel,
                 (image, unpack_own, gap),

time: 89.4 us -> 89.1 us (level)
    ppermute x30 -> x24, starting transfers between devices: 36.7 us -> 27.4 us  [swap(): return lax.ppermute(block, axis, [(i, i ^ d) for i in range(count)])]
    ppermute x0 -> x6, starting transfers between devices: none -> 8.9 us  [swap_lines(): lax.ppermute(block, ('wide', 'narrow'), [(w * narrow + i, (w ^ ds[i % 2])...]
    ppermute x0 -> x6, waiting for transfers between devices: none -> 5.36 us  [swap_lines(): lax.ppermute(block, ('wide', 'narrow'), [(w * narrow + i, (w ^ ds[i % 2])...]
    ppermute x30 -> x24, waiting for transfers between devices: 29.5 us -> 24.2 us  [swap(): return lax.ppermute(block, axis, [(i, i ^ d) for i in range(count)])]
where the time goes in v21:
time: 89.1 us; the launch traced here: 89 us
  starting transfers between devices  36.3 us (41%)
  waiting for transfers between devices  29.5 us (33%)
  Pallas kernels  21.5 us (24%)
  between operations  1.57 us (2%)
    ppermute x24, starting transfers between devices, swap(): return lax.ppermute(block, axis, [(i, i ^ d) for i in range(count)])  27.4 us
    ppermute x24, waiting for transfers between devices, swap(): return lax.ppermute(block, axis, [(i, i ^ d) for i in range(count)])  24.2 us
    pallas_call x25, Pallas kernels, call(): pl.pallas_call(body, out_shape=outs, grid=grid, in_specs=in_specs, out_sp...  21.5 us
    ppermute x6, starting transfers between devices, swap_lines(): lax.ppermute(block, ('wide', 'narrow'), [(w * narrow + i, (w ^ ds[i % 2])...  8.9 us
    ppermute x6, waiting for transfers between devices, swap_lines(): lax.ppermute(block, ('wide', 'narrow'), [(w * narrow + i, (w ^ ds[i % 2])...  5.36 us
  transfers between devices with their start and end apart: 30, of which 25 were waited for; matrix products, arithmetic and copies ran while one was open for 0% of the time, Pallas kernels for 16%

profile of v21, /device:TPU:0, one launch (start us, length us, event | category | flops | bytes accessed | tf_op | source)
XLA Modules:
  0.0 89.0 jit_solution(16926688965929048517)
XLA Ops:
  0.6 2.0 %first.1 = (bf16[256,256]{1,0:T(8,128)(2,1)S(1)}, bf16[256,768]{1,0:T(8,128)(2,1)S(1)}, bf16[256,384]{1,0:T(8,128)(2,1)S(1)}, bf16[256,1024]{1,0:T(8,128)(2,1)S(...) custom-call(s32[1,256]{1,0:T(1,128)} %bitcast.32, ...), custom_call_target="tpu_custom_call" | custom-call | flops 201326592 | bytes 2097152 | tf_op jit(solution)/shard_map/first/pallas_call | solution.py:49
  2.6 5.1 %collective-permute-start = (f32[264,128]{1,0:T(8,128)S(1)}, f32[264,128]{1,0:T(8,128)S(1)}, u32[]{:S(2)}, u32[]{:S(2)}) collective-permute-start(f32[264,128]{1,0:T(8,128)S(1)} %get-tuple-element.81), channel_id=1, source_target_pairs={{0,12},{4,8},{8,4},{12,0},{1,13},{5,9},{9,5},{13,1},{2,14},{6,10},... | collective-permute-start | bytes 405512 | tf_op jit(solution)/shard_map/ppermute | solution.py:355
  7.7 0.6 collective-permute-start.2
  9.3 4.6 %rest_start.1 = (f32[768,128]{1,0:T(8,128)S(1)}, f32[64,128]{1,0:T(8,128)S(1)}, bf16[768,1024]{1,0:T(8,128)(2,1)S(1)}, bf16[768,1024]{1,0:T(8,128)(2,1)S(1)}) custom-call(s32[1]{0:T(128)S(6)} %copy.15.size, f32[1024,1024]{1,0:T(8,128)} %bitcast.29, f32[1024,128]{1,0:T(8,128)} %bitcast.20, f32[1024,128]{1,0:T(8,128)} %bitcast.21, f32[1024,128]{1,0:T(8,128)} %bitcast.7, ...), custom_call_target="tpu_custom_call" | custom-call | flops 603979776 | bytes 6291456 | tf_op jit(solution)/shard_map/rest_start/pallas_call | solution.py:49
  13.9 1.4 %collective-permute-done.1.refs_1_ = f32[264,128]{1,0:T(8,128)S(1)} collective-permute-done((f32[264,128]{1,0:T(8,128)S(1)}, f32[264,128]{1,0:T(8,128)S(1)}, u32[]{:S(2)}, u32[]{:S(2)}) %collective-permute-start.1) | collective-permute-done | bytes 135200 | tf_op jit(solution)/shard_map/ppermute | solution.py:355
  15.3 3.9 %collective-permute-done.2.refs_2_ = f32[264,128]{1,0:T(8,128)S(1)} collective-permute-done((f32[264,128]{1,0:T(8,128)S(1)}, f32[264,128]{1,0:T(8,128)S(1)}, u32[]{:S(2)}, u32[]{:S(2)}) %collective-permute-start.2) | collective-permute-done | bytes 135200 | tf_op jit(solution)/shard_map/ppermute | solution.py:355
  19.2 0.4 coarse.2
  19.6 0.8 collective-permute-start.3
  20.4 1.8 %collective-permute-start.4 = (f32[64,128]{1,0:T(8,128)S(1)}, f32[64,128]{1,0:T(8,128)S(1)}, u32[]{:S(2)}, u32[]{:S(2)}) collective-permute-start(f32[64,128]{1,0:T(8,128)S(1)} %get-tuple-element.90), channel_id=1, source_target_pairs={{0,12},{4,8},{8,4},{12,0},{1,13},{5,9},{9,5},{13,1},{2,14},{6,10},... | collective-permute-start | bytes 98312 | tf_op jit(solution)/shard_map/ppermute | solution.py:355
  22.2 0.9 %collective-permute-start.5 = (f32[64,128]{1,0:T(8,128)S(1)}, f32[64,128]{1,0:T(8,128)S(1)}, u32[]{:S(2)}, u32[]{:S(2)}) collective-permute-start(f32[64,128]{1,0:T(8,128)S(1)} %get-tuple-element.91), channel_id=1, source_target_pairs={{0,4},{4,0},{8,12},{12,8},{1,5},{5,1},{9,13},{13,9},{2,6},{6,2},{1... | collective-permute-start | bytes 98312 | tf_op jit(solution)/shard_map/ppermute | solution.py:355
  23.2 0.4 prepare.1
  23.6 1.1 %collective-permute-done.3.refs_1_ = f32[64,128]{1,0:T(8,128)S(1)} collective-permute-done((f32[64,128]{1,0:T(8,128)S(1)}, f32[64,128]{1,0:T(8,128)S(1)}, u32[]{:S(2)}, u32[]{:S(2)}) %collective-permute-start.3) | collective-permute-done | bytes 32800 | tf_op jit(solution)/shard_map/ppermute | solution.py:355
  24.6 1.7 %collective-permute-done.4.refs_2_ = f32[64,128]{1,0:T(8,128)S(1)} collective-permute-done((f32[64,128]{1,0:T(8,128)S(1)}, f32[64,128]{1,0:T(8,128)S(1)}, u32[]{:S(2)}, u32[]{:S(2)}) %collective-permute-start.4) | collective-permute-done | bytes 32800 | tf_op jit(solution)/shard_map/ppermute | solution.py:355
  26.8 1.6 %collective-permute-start.7 = (f32[64,128]{1,0:T(8,128)S(1)}, f32[64,128]{1,0:T(8,128)S(1)}, u32[]{:S(2)}, u32[]{:S(2)}) collective-permute-start(f32[64,128]{1,0:T(8,128)S(1)} %get-tuple-element.94), channel_id=1, source_target_pairs={{0,2},{1,3},{2,0},{3,1},{4,6},{5,7},{6,4},{7,5},{8,10},{9,11},{10,... | collective-permute-start | bytes 98312 | tf_op jit(solution)/shard_map/ppermute | solution.py:355
  28.7 0.3 pack.1
  29.0 1.5 %collective-permute-done.6.refs_1_ = f32[64,128]{1,0:T(8,128)S(1)} collective-permute-done((f32[64,128]{1,0:T(8,128)S(1)}, f32[64,128]{1,0:T(8,128)S(1)}, u32[]{:S(2)}, u32[]{:S(2)}) %collective-permute-start.6) | collective-permute-done | bytes 32800 | tf_op jit(solution)/shard_map/ppermute | solution.py:355
  30.5 0.4 collective-permute-done.7.refs_2_
  30.9 0.9 lift.2
  31.7 0.7 collective-permute-start.9
  32.4 1.8 %collective-permute-start.10 = (f32[128,128]{1,0:T(8,128)S(1)}, f32[128,128]{1,0:T(8,128)S(1)}, u32[]{:S(2)}, u32[]{:S(2)}) collective-permute-start(f32[128,128]{1,0:T(8,128)S(1)} %get-tuple-element.104), channel_id=1, source_target_pairs={{0,8},{1,13},{2,10},{3,15},{4,12},{5,9},{6,14},{7,11},{8,0},{9,5},... | collective-permute-start | bytes 196616 | tf_op jit(solution)/shard_map/ppermute | solution.py:364
  34.2 2.0 %collective-permute-start.11 = (f32[128,128]{1,0:T(8,128)S(1)}, f32[128,128]{1,0:T(8,128)S(1)}, u32[]{:S(2)}, u32[]{:S(2)}) collective-permute-start(f32[128,128]{1,0:T(8,128)S(1)} %get-tuple-element.105), channel_id=1, source_target_pairs={{0,12},{1,5},{2,14},{3,7},{4,8},{5,1},{6,10},{7,3},{8,4},{9,13},{1... | collective-permute-start | bytes 196616 | tf_op jit(solution)/shard_map/ppermute | solution.py:364
  36.4 1.5 %rest.3 = (f32[768,128]{1,0:T(8,128)S(1)}, f32[640,128]{1,0:T(8,128)S(1)}) custom-call(s32[1]{0:T(128)S(6)} %copy.15.size, bf16[768,1024]{1,0:T(8,128)(2,1)S(1)} %get-tuple-element.111.high, bf16[768,1024]{1,0:T(8,128)(2,1)S(1)} %get-tuple-element.112.low, f32[256,128]{1,0:T(8,128)S(1)} %get-tuple-element.108.mult_s.refs_5_, ...), custom_call_target="tpu_custom_call" | custom-call | flops 805306368 | bytes 4194304 | tf_op jit(solution)/shard_map/rest/pallas_call | solution.py:49
  37.9 1.9 %collective-permute-done.10.refs_1_ = f32[128,128]{1,0:T(8,128)S(1)} collective-permute-done((f32[128,128]{1,0:T(8,128)S(1)}, f32[128,128]{1,0:T(8,128)S(1)}, u32[]{:S(2)}, u32[]{:S(2)}) %collective-permute-start.10) | collective-permute-done | bytes 65568 | tf_op jit(solution)/shard_map/ppermute | solution.py:364
  39.8 0.8 collective-permute-done.11.refs_2_
  40.6 0.5 sweep.3
  41.2 1.6 %collective-permute-start.12 = (f32[128,128]{1,0:T(8,128)S(1)}, f32[128,128]{1,0:T(8,128)S(1)}, u32[]{:S(2)}, u32[]{:S(2)}) collective-permute-start(f32[128,128]{1,0:T(8,128)S(1)} %get-tuple-element.115), channel_id=1, source_target_pairs={{0,8},{4,12},{8,0},{12,4},{1,9},{5,13},{9,1},{13,5},{2,10},{6,14},... | collective-permute-start | bytes 196616 | tf_op jit(solution)/shard_map/ppermute | solution.py:355
  42.8 2.0 %collective-permute-start.13 = (f32[128,128]{1,0:T(8,128)S(1)}, f32[128,128]{1,0:T(8,128)S(1)}, u32[]{:S(2)}, u32[]{:S(2)}) collective-permute-start(f32[128,128]{1,0:T(8,128)S(1)} %get-tuple-element.116), channel_id=1, source_target_pairs={{0,12},{4,8},{8,4},{12,0},{1,13},{5,9},{9,5},{13,1},{2,14},{6,10},... | collective-permute-start | bytes 196616 | tf_op jit(solution)/shard_map/ppermute | solution.py:355
  45.0 1.5 %rest.4 = (f32[768,128]{1,0:T(8,128)S(1)}, f32[640,128]{1,0:T(8,128)S(1)}) custom-call(s32[1]{0:T(128)S(6)} %copy.15.size, bf16[768,1024]{1,0:T(8,128)(2,1)S(1)} %get-tuple-element.111.high, bf16[768,1024]{1,0:T(8,128)(2,1)S(1)} %get-tuple-element.112.low, f32[256,128]{1,0:T(8,128)S(1)} %get-tuple-element.119.mult_s.refs_5_, ...), custom_call_target="tpu_custom_call" | custom-call | flops 805306368 | bytes 4194304 | tf_op jit(solution)/shard_map/rest/pallas_call | solution.py:49
  46.5 1.2 %collective-permute-done.12.refs_0_ = f32[128,128]{1,0:T(8,128)S(1)} collective-permute-done((f32[128,128]{1,0:T(8,128)S(1)}, f32[128,128]{1,0:T(8,128)S(1)}, u32[]{:S(2)}, u32[]{:S(2)}) %collective-permute-start.12) | collective-permute-done | bytes 65568 | tf_op jit(solution)/shard_map/ppermute | solution.py:355
  47.7 1.3 %collective-permute-done.13.refs_1_ = f32[128,128]{1,0:T(8,128)S(1)} collective-permute-done((f32[128,128]{1,0:T(8,128)S(1)}, f32[128,128]{1,0:T(8,128)S(1)}, u32[]{:S(2)}, u32[]{:S(2)}) %collective-permute-start.13) | collective-permute-done | bytes 65568 | tf_op jit(solution)/shard_map/ppermute | solution.py:355
  48.9 0.6 collective-permute-done.14.refs_2_
  49.6 0.5 sweep.4
  50.1 0.6 collective-permute-start.15
  50.7 2.1 %collective-permute-start.16 = (f32[128,128]{1,0:T(8,128)S(1)}, f32[128,128]{1,0:T(8,128)S(1)}, u32[]{:S(2)}, u32[]{:S(2)}) collective-permute-start(f32[128,128]{1,0:T(8,128)S(1)} %get-tuple-element.123), channel_id=1, source_target_pairs={{0,12},{4,8},{8,4},{12,0},{1,13},{5,9},{9,5},{13,1},{2,14},{6,10},... | collective-permute-start | bytes 196616 | tf_op jit(solution)/shard_map/ppermute | solution.py:355
  52.8 0.8 collective-permute-start.17
  53.9 1.1 %rest_first.1 = (f32[768,128]{1,0:T(8,128)S(1)}, f32[64,128]{1,0:T(8,128)S(1)}) custom-call(s32[1]{0:T(128)S(6)} %copy.15.size, bf16[768,1024]{1,0:T(8,128)(2,1)S(1)} %get-tuple-element.111.high, bf16[768,1024]{1,0:T(8,128)(2,1)S(1)} %get-tuple-element.112.low, f32[256,128]{1,0:T(8,128)S(1)} %get-tuple-element.126.mult_s.refs_5_, ...), custom_call_target="tpu_custom_call" | custom-call | flops 603979776 | bytes 3145728 | tf_op jit(solution)/shard_map/rest_first/pallas_call | solution.py:49
  55.0 1.1 %collective-permute-done.15.refs_0_ = f32[128,128]{1,0:T(8,128)S(1)} collective-permute-done((f32[128,128]{1,0:T(8,128)S(1)}, f32[128,128]{1,0:T(8,128)S(1)}, u32[]{:S(2)}, u32[]{:S(2)}) %collective-permute-start.15) | collective-permute-done | bytes 65568 | tf_op jit(solution)/shard_map/ppermute | solution.py:355
  56.1 0.8 collective-permute-done.16.refs_1_
  56.9 0.7 collective-permute-done.17.refs_2_
  57.6 0.4 coarse.3
  58.0 0.9 %collective-permute-start.18 = (f32[64,128]{1,0:T(8,128)S(1)}, f32[64,128]{1,0:T(8,128)S(1)}, u32[]{:S(2)}, u32[]{:S(2)}) collective-permute-start(f32[64,128]{1,0:T(8,128)S(1)} %get-tuple-element.130), channel_id=1, source_target_pairs={{0,8},{4,12},{8,0},{12,4},{1,9},{5,13},{9,1},{13,5},{2,10},{6,14},... | collective-permute-start | bytes 98312 | tf_op jit(solution)/shard_map/ppermute | solution.py:355
  58.9 2.0 %collective-permute-start.19 = (f32[64,128]{1,0:T(8,128)S(1)}, f32[64,128]{1,0:T(8,128)S(1)}, u32[]{:S(2)}, u32[]{:S(2)}) collective-permute-start(f32[64,128]{1,0:T(8,128)S(1)} %get-tuple-element.131), channel_id=1, source_target_pairs={{0,12},{4,8},{8,4},{12,0},{1,13},{5,9},{9,5},{13,1},{2,14},{6,10},... | collective-permute-start | bytes 98312 | tf_op jit(solution)/shard_map/ppermute | solution.py:355
  60.9 0.7 collective-permute-start.20
  61.5 1.6 %collective-permute-done.18.refs_1_ = f32[64,128]{1,0:T(8,128)S(1)} collective-permute-done((f32[64,128]{1,0:T(8,128)S(1)}, f32[64,128]{1,0:T(8,128)S(1)}, u32[]{:S(2)}, u32[]{:S(2)}) %collective-permute-start.18) | collective-permute-done | bytes 32800 | tf_op jit(solution)/shard_map/ppermute | solution.py:355
  63.1 1.5 %collective-permute-done.19.refs_2_ = f32[64,128]{1,0:T(8,128)S(1)} collective-permute-done((f32[64,128]{1,0:T(8,128)S(1)}, f32[64,128]{1,0:T(8,128)S(1)}, u32[]{:S(2)}, u32[]{:S(2)}) %collective-permute-start.19) | collective-permute-done | bytes 32800 | tf_op jit(solution)/shard_map/ppermute | solution.py:355
  64.7 0.3 collective-permute-done.20.refs_3_
  65.3 1.1 %collective-permute-start.22 = (f32[64,128]{1,0:T(8,128)S(1)}, f32[64,128]{1,0:T(8,128)S(1)}, u32[]{:S(2)}, u32[]{:S(2)}) collective-permute-start(f32[64,128]{1,0:T(8,128)S(1)} %get-tuple-element.135), channel_id=1, source_target_pairs={{0,2},{1,3},{2,0},{3,1},{4,6},{5,7},{6,4},{7,5},{8,10},{9,11},{10,... | collective-permute-start | bytes 98312 | tf_op jit(solution)/shard_map/ppermute | solution.py:355
  66.5 0.7 collective-permute-start.23
  67.2 1.5 %collective-permute-done.21.refs_1_ = f32[64,128]{1,0:T(8,128)S(1)} collective-permute-done((f32[64,128]{1,0:T(8,128)S(1)}, f32[64,128]{1,0:T(8,128)S(1)}, u32[]{:S(2)}, u32[]{:S(2)}) %collective-permute-start.21) | collective-permute-done | bytes 32800 | tf_op jit(solution)/shard_map/ppermute | solution.py:355
  68.7 0.9 collective-permute-done.22.refs_2_
  69.5 0.9 lift.3
  70.4 0.5 collective-permute-start.24
  70.9 2.1 %collective-permute-start.25 = (f32[128,128]{1,0:T(8,128)S(1)}, f32[128,128]{1,0:T(8,128)S(1)}, u32[]{:S(2)}, u32[]{:S(2)}) collective-permute-start(f32[128,128]{1,0:T(8,128)S(1)} %get-tuple-element.140), channel_id=1, source_target_pairs={{0,8},{1,13},{2,10},{3,15},{4,12},{5,9},{6,14},{7,11},{8,0},{9,5},... | collective-permute-start | bytes 196616 | tf_op jit(solution)/shard_map/ppermute | solution.py:364
  73.0 1.9 %collective-permute-start.26 = (f32[128,128]{1,0:T(8,128)S(1)}, f32[128,128]{1,0:T(8,128)S(1)}, u32[]{:S(2)}, u32[]{:S(2)}) collective-permute-start(f32[128,128]{1,0:T(8,128)S(1)} %get-tuple-element.141), channel_id=1, source_target_pairs={{0,12},{1,5},{2,14},{3,7},{4,8},{5,1},{6,10},{7,3},{8,4},{9,13},{1... | collective-permute-start | bytes 196616 | tf_op jit(solution)/shard_map/ppermute | solution.py:364
  75.1 1.5 %rest.5 = (f32[768,128]{1,0:T(8,128)S(1)}, f32[640,128]{1,0:T(8,128)S(1)}) custom-call(s32[1]{0:T(128)S(6)} %copy.15.size, bf16[768,1024]{1,0:T(8,128)(2,1)S(1)} %get-tuple-element.111.high, bf16[768,1024]{1,0:T(8,128)(2,1)S(1)} %get-tuple-element.112.low, f32[256,128]{1,0:T(8,128)S(1)} %get-tuple-element.143.mult_s.refs_5_, ...), custom_call_target="tpu_custom_call" | custom-call | flops 805306368 | bytes 4194304 | tf_op jit(solution)/shard_map/rest/pallas_call | solution.py:49
  76.6 1.6 %collective-permute-done.25.refs_1_ = f32[128,128]{1,0:T(8,128)S(1)} collective-permute-done((f32[128,128]{1,0:T(8,128)S(1)}, f32[128,128]{1,0:T(8,128)S(1)}, u32[]{:S(2)}, u32[]{:S(2)}) %collective-permute-start.25) | collective-permute-done | bytes 65568 | tf_op jit(solution)/shard_map/ppermute | solution.py:364
  78.2 1.0 %collective-permute-done.26.refs_2_ = f32[128,128]{1,0:T(8,128)S(1)} collective-permute-done((f32[128,128]{1,0:T(8,128)S(1)}, f32[128,128]{1,0:T(8,128)S(1)}, u32[]{:S(2)}, u32[]{:S(2)}) %collective-permute-start.26) | collective-permute-done | bytes 65568 | tf_op jit(solution)/shard_map/ppermute | solution.py:364
  79.2 0.5 sweep.5
  79.7 1.5 %collective-permute-start.27 = (f32[128,128]{1,0:T(8,128)S(1)}, f32[128,128]{1,0:T(8,128)S(1)}, u32[]{:S(2)}, u32[]{:S(2)}) collective-permute-start(f32[128,128]{1,0:T(8,128)S(1)} %get-tuple-element.146), channel_id=1, source_target_pairs={{0,8},{4,12},{8,0},{12,4},{1,9},{5,13},{9,1},{13,5},{2,10},{6,14},... | collective-permute-start | bytes 196616 | tf_op jit(solution)/shard_map/ppermute | solution.py:355
  81.2 1.9 %collective-permute-start.28 = (f32[128,128]{1,0:T(8,128)S(1)}, f32[128,128]{1,0:T(8,128)S(1)}, u32[]{:S(2)}, u32[]{:S(2)}) collective-permute-start(f32[128,128]{1,0:T(8,128)S(1)} %get-tuple-element.147), channel_id=1, source_target_pairs={{0,12},{4,8},{8,4},{12,0},{1,13},{5,9},{9,5},{13,1},{2,14},{6,10},... | collective-permute-start | bytes 196616 | tf_op jit(solution)/shard_map/ppermute | solution.py:355
  83.5 1.9 %rest_last.1 = (f32[1024,128]{1,0:T(8,128)}, f32[1024,128]{1,0:T(8,128)}) custom-call(s32[1]{0:T(128)S(6)} %copy.15.size, bf16[768,1024]{1,0:T(8,128)(2,1)S(1)} %get-tuple-element.111.high, bf16[768,1024]{1,0:T(8,128)(2,1)S(1)} %get-tuple-element.112.low, f32[256,128]{1,0:T(8,128)S(1)} %get-tuple-element.150.mult_s.refs_5_, ...), custom_call_target="tpu_custom_call" | custom-call | flops 603979776 | bytes 3145728 | tf_op jit(solution)/shard_map/rest_last/pallas_call | solution.py:49
  85.6 1.8 %collective-permute-done.28.refs_1_ = f32[128,128]{1,0:T(8,128)S(1)} collective-permute-done((f32[128,128]{1,0:T(8,128)S(1)}, f32[128,128]{1,0:T(8,128)S(1)}, u32[]{:S(2)}, u32[]{:S(2)}) %collective-permute-start.28) | collective-permute-done | bytes 65568 | tf_op jit(solution)/shard_map/ppermute | solution.py:355
  87.4 0.6 collective-permute-done.29.refs_2_
  88.0 1.0 %last.1 = (f32[1024,128]{1,0:T(8,128)}, f32[1024,128]{1,0:T(8,128)}) custom-call(s32[1]{0:T(128)S(6)} %copy.15.size, f32[128,128]{1,0:T(8,128)S(1)} %collective-permute-done.27.refs_0_, f32[128,128]{1,0:T(8,128)S(1)} %collective-permute-done.28.refs_1_, ...), custom_call_target="tpu_custom_call", output_to_operand_aliasing={{0}: (8, {}), {1}: (9, {})} | custom-call | flops 75497472 | bytes 196608 | tf_op jit(solution)/shard_map/last/pallas_call | solution.py:49
  (33 shorter events, 2.7 us)
Async XLA Ops:
  0.6 8.4 %copy-start = (f32[1,1024,128]{2,1,0:T(8,128)S(1)}, f32[1,1024,128]{2,1,0:T(8,128)}, u32[]{:S(2)}) copy-start(f32[1,1024,128]{2,1,0:T(8,128)} %param.12) | copy-start | bytes 1572868
  2.6 11.3 %collective-permute-start = (f32[264,128]{1,0:T(8,128)S(1)}, f32[264,128]{1,0:T(8,128)S(1)}, u32[]{:S(2)}, u32[]{:S(2)}) collective-permute-start(f32[264,128]{1,0:T(8,128)S(1)} %get-tuple-element.81), channel_id=1, source_target_pairs={{0,12},{4,8},{8,4},{12,0},{1,13},{5,9},{9,5},{13,1},{2,14},{6,10},... | collective-permute-start | bytes 405512 | tf_op jit(solution)/shard_map/ppermute | solution.py:355
  7.7 7.6 %collective-permute-start.1 = (f32[264,128]{1,0:T(8,128)S(1)}, f32[264,128]{1,0:T(8,128)S(1)}, u32[]{:S(2)}, u32[]{:S(2)}) collective-permute-start(f32[264,128]{1,0:T(8,128)S(1)} %get-tuple-element.82), channel_id=1, source_target_pairs={{0,4},{4,0},{8,12},{12,8},{1,5},{5,1},{9,13},{13,9},{2,6},{6,2},{1... | collective-permute-start | bytes 405512 | tf_op jit(solution)/shard_map/ppermute | solution.py:355
  7.7 11.4 %collective-permute-start.2 = (f32[264,128]{1,0:T(8,128)S(1)}, f32[264,128]{1,0:T(8,128)S(1)}, u32[]{:S(2)}, u32[]{:S(2)}) collective-permute-start(f32[264,128]{1,0:T(8,128)S(1)} %get-tuple-element.83), channel_id=1, source_target_pairs={{0,8},{4,12},{8,0},{12,4},{1,9},{5,13},{9,1},{13,5},{2,10},{6,14},... | collective-permute-start | bytes 405512 | tf_op jit(solution)/shard_map/ppermute | solution.py:355
  9.2 9.9 %copy-start.2 = (f32[1,1024,128]{2,1,0:T(8,128)S(1)}, f32[1,1024,128]{2,1,0:T(8,128)}, u32[]{:S(2)}) copy-start(f32[1,1024,128]{2,1,0:T(8,128)} %param.13) | copy-start | bytes 1572868
  9.3 9.9 %copy-start.3 = (f32[1,64,1024]{2,1,0:T(8,128)S(1)}, f32[1,64,1024]{2,1,0:T(8,128)}, u32[]{:S(2)}) copy-start(f32[1,64,1024]{2,1,0:T(8,128)} %param.11) | copy-start | bytes 786436
  13.8 9.3 %copy-start.4 = (f32[256,256]{1,0:T(8,128)S(1)}, f32[256,256]{1,0:T(8,128)}, u32[]{:S(2)}) copy-start(f32[256,256]{1,0:T(8,128)} %tile.3) | copy-start | bytes 786436
  13.9 9.3 %copy-start.5 = (s32[1,1024]{1,0:T(1,128)S(1)}, s32[1,1024]{1,0:T(1,128)}, u32[]{:S(2)}) copy-start(s32[1,1024]{1,0:T(1,128)} %contact.1) | copy-start | bytes 12292
  19.6 5.0 %collective-permute-start.3 = (f32[64,128]{1,0:T(8,128)S(1)}, f32[64,128]{1,0:T(8,128)S(1)}, u32[]{:S(2)}, u32[]{:S(2)}) collective-permute-start(f32[64,128]{1,0:T(8,128)S(1)} %get-tuple-element.89), channel_id=1, source_target_pairs={{0,8},{4,12},{8,0},{12,4},{1,9},{5,13},{9,1},{13,5},{2,10},{6,14},... | collective-permute-start | bytes 98312 | tf_op jit(solution)/shard_map/ppermute | solution.py:355
  20.4 5.9 %collective-permute-start.4 = (f32[64,128]{1,0:T(8,128)S(1)}, f32[64,128]{1,0:T(8,128)S(1)}, u32[]{:S(2)}, u32[]{:S(2)}) collective-permute-start(f32[64,128]{1,0:T(8,128)S(1)} %get-tuple-element.90), channel_id=1, source_target_pairs={{0,12},{4,8},{8,4},{12,0},{1,13},{5,9},{9,5},{13,1},{2,14},{6,10},... | collective-permute-start | bytes 98312 | tf_op jit(solution)/shard_map/ppermute | solution.py:355
  22.2 4.3 %collective-permute-start.5 = (f32[64,128]{1,0:T(8,128)S(1)}, f32[64,128]{1,0:T(8,128)S(1)}, u32[]{:S(2)}, u32[]{:S(2)}) collective-permute-start(f32[64,128]{1,0:T(8,128)S(1)} %get-tuple-element.91), channel_id=1, source_target_pairs={{0,4},{4,0},{8,12},{12,8},{1,5},{5,1},{9,13},{13,9},{2,6},{6,2},{1... | collective-permute-start | bytes 98312 | tf_op jit(solution)/shard_map/ppermute | solution.py:355
  26.8 3.7 %collective-permute-start.6 = (f32[64,128]{1,0:T(8,128)S(1)}, f32[64,128]{1,0:T(8,128)S(1)}, u32[]{:S(2)}, u32[]{:S(2)}) collective-permute-start(f32[64,128]{1,0:T(8,128)S(1)} %get-tuple-element.93), channel_id=1, source_target_pairs={{0,3},{1,2},{2,1},{3,0},{4,7},{5,6},{6,5},{7,4},{8,11},{9,10},{10,... | collective-permute-start | bytes 98312 | tf_op jit(solution)/shard_map/ppermute | solution.py:355
  26.8 4.0 %collective-permute-start.7 = (f32[64,128]{1,0:T(8,128)S(1)}, f32[64,128]{1,0:T(8,128)S(1)}, u32[]{:S(2)}, u32[]{:S(2)}) collective-permute-start(f32[64,128]{1,0:T(8,128)S(1)} %get-tuple-element.94), channel_id=1, source_target_pairs={{0,2},{1,3},{2,0},{3,1},{4,6},{5,7},{6,4},{7,5},{8,10},{9,11},{10,... | collective-permute-start | bytes 98312 | tf_op jit(solution)/shard_map/ppermute | solution.py:355
  28.4 2.5 %collective-permute-start.8 = (f32[64,128]{1,0:T(8,128)S(1)}, f32[64,128]{1,0:T(8,128)S(1)}, u32[]{:S(2)}, u32[]{:S(2)}) collective-permute-start(f32[64,128]{1,0:T(8,128)S(1)} %get-tuple-element.95), channel_id=1, source_target_pairs={{0,1},{1,0},{2,3},{3,2},{4,5},{5,4},{6,7},{7,6},{8,9},{9,8},{10,11... | collective-permute-start | bytes 98312 | tf_op jit(solution)/shard_map/ppermute | solution.py:355
  29.0 7.2 %copy-start.1 = (f32[1,1024,128]{2,1,0:T(8,128)S(1)}, f32[1,1024,128]{2,1,0:T(8,128)}, u32[]{:S(2)}) copy-start(f32[1,1024,128]{2,1,0:T(8,128)} %param.12) | copy-start | bytes 1572868
  31.7 6.1 %collective-permute-start.9 = (f32[128,128]{1,0:T(8,128)S(1)}, f32[128,128]{1,0:T(8,128)S(1)}, u32[]{:S(2)}, u32[]{:S(2)}) collective-permute-start(f32[128,128]{1,0:T(8,128)S(1)} %get-tuple-element.103), channel_id=1, source_target_pairs={{0,4},{1,9},{2,6},{3,11},{4,0},{5,13},{6,2},{7,15},{8,12},{9,1},{1... | collective-permute-start | bytes 196616 | tf_op jit(solution)/shard_map/ppermute | solution.py:364
  32.4 7.4 %collective-permute-start.10 = (f32[128,128]{1,0:T(8,128)S(1)}, f32[128,128]{1,0:T(8,128)S(1)}, u32[]{:S(2)}, u32[]{:S(2)}) collective-permute-start(f32[128,128]{1,0:T(8,128)S(1)} %get-tuple-element.104), channel_id=1, source_target_pairs={{0,8},{1,13},{2,10},{3,15},{4,12},{5,9},{6,14},{7,11},{8,0},{9,5},... | collective-permute-start | bytes 196616 | tf_op jit(solution)/shard_map/ppermute | solution.py:364
  34.2 6.4 %collective-permute-start.11 = (f32[128,128]{1,0:T(8,128)S(1)}, f32[128,128]{1,0:T(8,128)S(1)}, u32[]{:S(2)}, u32[]{:S(2)}) collective-permute-start(f32[128,128]{1,0:T(8,128)S(1)} %get-tuple-element.105), channel_id=1, source_target_pairs={{0,12},{1,5},{2,14},{3,7},{4,8},{5,1},{6,10},{7,3},{8,4},{9,13},{1... | collective-permute-start | bytes 196616 | tf_op jit(solution)/shard_map/ppermute | solution.py:364
  41.2 6.5 %collective-permute-start.12 = (f32[128,128]{1,0:T(8,128)S(1)}, f32[128,128]{1,0:T(8,128)S(1)}, u32[]{:S(2)}, u32[]{:S(2)}) collective-permute-start(f32[128,128]{1,0:T(8,128)S(1)} %get-tuple-element.115), channel_id=1, source_target_pairs={{0,8},{4,12},{8,0},{12,4},{1,9},{5,13},{9,1},{13,5},{2,10},{6,14},... | collective-permute-start | bytes 196616 | tf_op jit(solution)/shard_map/ppermute | solution.py:355
  42.8 6.1 %collective-permute-start.13 = (f32[128,128]{1,0:T(8,128)S(1)}, f32[128,128]{1,0:T(8,128)S(1)}, u32[]{:S(2)}, u32[]{:S(2)}) collective-permute-start(f32[128,128]{1,0:T(8,128)S(1)} %get-tuple-element.116), channel_id=1, source_target_pairs={{0,12},{4,8},{8,4},{12,0},{1,13},{5,9},{9,5},{13,1},{2,14},{6,10},... | collective-permute-start | bytes 196616 | tf_op jit(solution)/shard_map/ppermute | solution.py:355
  44.8 4.8 %collective-permute-start.14 = (f32[128,128]{1,0:T(8,128)S(1)}, f32[128,128]{1,0:T(8,128)S(1)}, u32[]{:S(2)}, u32[]{:S(2)}) collective-permute-start(f32[128,128]{1,0:T(8,128)S(1)} %get-tuple-element.117), channel_id=1, source_target_pairs={{0,4},{4,0},{8,12},{12,8},{1,5},{5,1},{9,13},{13,9},{2,6},{6,2},{1... | collective-permute-start | bytes 196616 | tf_op jit(solution)/shard_map/ppermute | solution.py:355
  50.1 6.0 %collective-permute-start.15 = (f32[128,128]{1,0:T(8,128)S(1)}, f32[128,128]{1,0:T(8,128)S(1)}, u32[]{:S(2)}, u32[]{:S(2)}) collective-permute-start(f32[128,128]{1,0:T(8,128)S(1)} %get-tuple-element.122), channel_id=1, source_target_pairs={{0,8},{4,12},{8,0},{12,4},{1,9},{5,13},{9,1},{13,5},{2,10},{6,14},... | collective-permute-start | bytes 196616 | tf_op jit(solution)/shard_map/ppermute | solution.py:355
  50.7 6.2 %collective-permute-start.16 = (f32[128,128]{1,0:T(8,128)S(1)}, f32[128,128]{1,0:T(8,128)S(1)}, u32[]{:S(2)}, u32[]{:S(2)}) collective-permute-start(f32[128,128]{1,0:T(8,128)S(1)} %get-tuple-element.123), channel_id=1, source_target_pairs={{0,12},{4,8},{8,4},{12,0},{1,13},{5,9},{9,5},{13,1},{2,14},{6,10},... | collective-permute-start | bytes 196616 | tf_op jit(solution)/shard_map/ppermute | solution.py:355
  52.8 4.8 %collective-permute-start.17 = (f32[128,128]{1,0:T(8,128)S(1)}, f32[128,128]{1,0:T(8,128)S(1)}, u32[]{:S(2)}, u32[]{:S(2)}) collective-permute-start(f32[128,128]{1,0:T(8,128)S(1)} %get-tuple-element.124), channel_id=1, source_target_pairs={{0,4},{4,0},{8,12},{12,8},{1,5},{5,1},{9,13},{13,9},{2,6},{6,2},{1... | collective-permute-start | bytes 196616 | tf_op jit(solution)/shard_map/ppermute | solution.py:355
  58.0 5.1 %collective-permute-start.18 = (f32[64,128]{1,0:T(8,128)S(1)}, f32[64,128]{1,0:T(8,128)S(1)}, u32[]{:S(2)}, u32[]{:S(2)}) collective-permute-start(f32[64,128]{1,0:T(8,128)S(1)} %get-tuple-element.130), channel_id=1, source_target_pairs={{0,8},{4,12},{8,0},{12,4},{1,9},{5,13},{9,1},{13,5},{2,10},{6,14},... | collective-permute-start | bytes 98312 | tf_op jit(solution)/shard_map/ppermute | solution.py:355
  58.9 5.7 %collective-permute-start.19 = (f32[64,128]{1,0:T(8,128)S(1)}, f32[64,128]{1,0:T(8,128)S(1)}, u32[]{:S(2)}, u32[]{:S(2)}) collective-permute-start(f32[64,128]{1,0:T(8,128)S(1)} %get-tuple-element.131), channel_id=1, source_target_pairs={{0,12},{4,8},{8,4},{12,0},{1,13},{5,9},{9,5},{13,1},{2,14},{6,10},... | collective-permute-start | bytes 98312 | tf_op jit(solution)/shard_map/ppermute | solution.py:355
  60.9 4.1 %collective-permute-start.20 = (f32[64,128]{1,0:T(8,128)S(1)}, f32[64,128]{1,0:T(8,128)S(1)}, u32[]{:S(2)}, u32[]{:S(2)}) collective-permute-start(f32[64,128]{1,0:T(8,128)S(1)} %get-tuple-element.132), channel_id=1, source_target_pairs={{0,4},{4,0},{8,12},{12,8},{1,5},{5,1},{9,13},{13,9},{2,6},{6,2},{1... | collective-permute-start | bytes 98312 | tf_op jit(solution)/shard_map/ppermute | solution.py:355
  65.3 3.4 %collective-permute-start.21 = (f32[64,128]{1,0:T(8,128)S(1)}, f32[64,128]{1,0:T(8,128)S(1)}, u32[]{:S(2)}, u32[]{:S(2)}) collective-permute-start(f32[64,128]{1,0:T(8,128)S(1)} %get-tuple-element.134), channel_id=1, source_target_pairs={{0,3},{1,2},{2,1},{3,0},{4,7},{5,6},{6,5},{7,4},{8,11},{9,10},{10,... | collective-permute-start | bytes 98312 | tf_op jit(solution)/shard_map/ppermute | solution.py:355
  65.3 4.2 %collective-permute-start.22 = (f32[64,128]{1,0:T(8,128)S(1)}, f32[64,128]{1,0:T(8,128)S(1)}, u32[]{:S(2)}, u32[]{:S(2)}) collective-permute-start(f32[64,128]{1,0:T(8,128)S(1)} %get-tuple-element.135), channel_id=1, source_target_pairs={{0,2},{1,3},{2,0},{3,1},{4,6},{5,7},{6,4},{7,5},{8,10},{9,11},{10,... | collective-permute-start | bytes 98312 | tf_op jit(solution)/shard_map/ppermute | solution.py:355
  66.5 3.0 %collective-permute-start.23 = (f32[64,128]{1,0:T(8,128)S(1)}, f32[64,128]{1,0:T(8,128)S(1)}, u32[]{:S(2)}, u32[]{:S(2)}) collective-permute-start(f32[64,128]{1,0:T(8,128)S(1)} %get-tuple-element.136), channel_id=1, source_target_pairs={{0,1},{1,0},{2,3},{3,2},{4,5},{5,4},{6,7},{7,6},{8,9},{9,8},{10,11... | collective-permute-start | bytes 98312 | tf_op jit(solution)/shard_map/ppermute | solution.py:355
  70.4 6.1 %collective-permute-start.24 = (f32[128,128]{1,0:T(8,128)S(1)}, f32[128,128]{1,0:T(8,128)S(1)}, u32[]{:S(2)}, u32[]{:S(2)}) collective-permute-start(f32[128,128]{1,0:T(8,128)S(1)} %get-tuple-element.139), channel_id=1, source_target_pairs={{0,4},{1,9},{2,6},{3,11},{4,0},{5,13},{6,2},{7,15},{8,12},{9,1},{1... | collective-permute-start | bytes 196616 | tf_op jit(solution)/shard_map/ppermute | solution.py:364
  70.9 7.2 %collective-permute-start.25 = (f32[128,128]{1,0:T(8,128)S(1)}, f32[128,128]{1,0:T(8,128)S(1)}, u32[]{:S(2)}, u32[]{:S(2)}) collective-permute-start(f32[128,128]{1,0:T(8,128)S(1)} %get-tuple-element.140), channel_id=1, source_target_pairs={{0,8},{1,13},{2,10},{3,15},{4,12},{5,9},{6,14},{7,11},{8,0},{9,5},... | collective-permute-start | bytes 196616 | tf_op jit(solution)/shard_map/ppermute | solution.py:364
  73.0 6.2 %collective-permute-start.26 = (f32[128,128]{1,0:T(8,128)S(1)}, f32[128,128]{1,0:T(8,128)S(1)}, u32[]{:S(2)}, u32[]{:S(2)}) collective-permute-start(f32[128,128]{1,0:T(8,128)S(1)} %get-tuple-element.141), channel_id=1, source_target_pairs={{0,12},{1,5},{2,14},{3,7},{4,8},{5,1},{6,10},{7,3},{8,4},{9,13},{1... | collective-permute-start | bytes 196616 | tf_op jit(solution)/shard_map/ppermute | solution.py:364
  79.7 5.9 %collective-permute-start.27 = (f32[128,128]{1,0:T(8,128)S(1)}, f32[128,128]{1,0:T(8,128)S(1)}, u32[]{:S(2)}, u32[]{:S(2)}) collective-permute-start(f32[128,128]{1,0:T(8,128)S(1)} %get-tuple-element.146), channel_id=1, source_target_pairs={{0,8},{4,12},{8,0},{12,4},{1,9},{5,13},{9,1},{13,5},{2,10},{6,14},... | collective-permute-start | bytes 196616 | tf_op jit(solution)/shard_map/ppermute | solution.py:355
  81.2 6.1 %collective-permute-start.28 = (f32[128,128]{1,0:T(8,128)S(1)}, f32[128,128]{1,0:T(8,128)S(1)}, u32[]{:S(2)}, u32[]{:S(2)}) collective-permute-start(f32[128,128]{1,0:T(8,128)S(1)} %get-tuple-element.147), channel_id=1, source_target_pairs={{0,12},{4,8},{8,4},{12,0},{1,13},{5,9},{9,5},{13,1},{2,14},{6,10},... | collective-permute-start | bytes 196616 | tf_op jit(solution)/shard_map/ppermute | solution.py:355
  83.1 4.9 %collective-permute-start.29 = (f32[128,128]{1,0:T(8,128)S(1)}, f32[128,128]{1,0:T(8,128)S(1)}, u32[]{:S(2)}, u32[]{:S(2)}) collective-permute-start(f32[128,128]{1,0:T(8,128)S(1)} %get-tuple-element.148), channel_id=1, source_target_pairs={{0,4},{4,0},{8,12},{12,8},{1,5},{5,1},{9,13},{13,9},{2,6},{6,2},{1... | collective-permute-start | bytes 196616 | tf_op jit(solution)/shard_map/ppermute | solution.py:355

commit v22 on v20

--- a/solution.py
+++ b/solution.py
@@ -79,9 +79,34 @@
     return jax.ShapeDtypeStruct((rows, columns), dtype)
 
 
+def places(peers, rows):
+    shared = peers.shape[1]
+    across = jnp.broadcast_to(peers[...], (shared, shared))
+    down = across.T
+    first = lax.broadcasted_iota(jnp.int32, (shared, shared), 0)
+    second = lax.broadcasted_iota(jnp.int32, (shared, shared), 1)
+    slot = jnp.sum(
+        jnp.where((across == down) & (second < first), 1.0, 0.0), axis=1, keepdims=True
+    ).astype(jnp.int32)
+    wanted = jnp.broadcast_to(rows[...], (shared, shared)).T[:, :1]
+    return down[:, :1] ^ lax.axis_index("wide"), slot, wanted
+
+
+def marks_kernel(cap, peers, rows, unpack_own, unpack_all, unpack):
+    far, slot, wanted = places(peers, rows)
+    shared = peers.shape[1]
+    for key, out in (
+        (jnp.where(far == 0, wanted, -1), unpack_own),
+        (jnp.where(far == 0, -1, (far - 1) * shared + wanted), unpack_all),
+        (jnp.where(far == 0, -1, (far - 1) * cap + slot), unpack),
+    ):
+        hit = key == lax.broadcasted_iota(jnp.int32, out.shape, 1)
+        out[...] = jnp.where(hit, 1.0, 0.0).astype(BF16)
+
+
 def first_kernel(n, cap, peers_at, rows_at, operator_at, mult_at, *refs):
-    unpack_own, unpack_all, unpack, high, low, image = refs[:6]
-    sends, (peers, rows, operator, mult, done) = refs[6:6 + n], refs[6 + n:]
+    high, low, image = refs[:3]
+    sends, (peers, rows, operator, mult, done) = refs[3:3 + n], refs[3 + n:]
     shared, width = image.shape
     pieces = [(peers_at, peers), (rows_at, rows)]
     for source, target, count in ((mult_at, mult, 2), (operator_at, operator, 4)):
@@ -92,23 +117,7 @@
         copy.start()
     copies[0].wait()
     copies[1].wait()
-    across = jnp.broadcast_to(peers[...], (shared, shared))
-    down = across.T
-    first = lax.broadcasted_iota(jnp.int32, (shared, shared), 0)
-    second = lax.broadcasted_iota(jnp.int32, (shared, shared), 1)
-    slot = jnp.sum(
-        jnp.where((across == down) & (second < first), 1.0, 0.0), axis=1, keepdims=True
-    ).astype(jnp.int32)
-    wanted = jnp.broadcast_to(rows[...], (shared, shared)).T[:, :1]
-    far = down[:, :1] ^ lax.axis_index("wide")
-
-    def marks(key, columns):
-        hit = key == lax.broadcasted_iota(jnp.int32, (shared, columns), 1)
-        return jnp.where(hit, 1.0, 0.0).astype(BF16)
-
-    unpack_own[...] = marks(jnp.where(far == 0, wanted, -1), shared)
-    unpack_all[...] = marks(jnp.where(far == 0, -1, (far - 1) * shared + wanted), unpack_all.shape[1])
-    unpack[...] = marks(jnp.where(far == 0, -1, (far - 1) * cap + slot), unpack.shape[1])
+    far, slot, wanted = places(peers, rows)
     lane = lax.broadcasted_iota(jnp.int32, (shared, width), 1)
     for d, out in enumerate(sends, 1):
         out[shared:, :] = jnp.zeros((out.shape[0] - shared, width), F32)
@@ -400,14 +409,14 @@
     full = 2 * order * loads
 
     list_rows = -(-(-(-cap // loads)) // 8) * 8
-    unpack_own, unpack_all, unpack, top_high, top_low, image, *sends = call(
+    pairs = peer_list[0].reshape(1, shared), partner_row
+    top_high, top_low, image, *sends = call(
         functools.partial(first_kernel, n, cap),
         tuple(
             pltpu.with_memory_space_constraint(value, pltpu.HBM)
-            for value in (peer_list[0].reshape(1, shared), partner_row, operator, mult)
+            for value in (*pairs, operator, mult)
         ),
-        [shape(shared, shared, BF16), shape(shared, n * shared, BF16), shape(shared, padded, BF16)]
-        + [shape(shared, order, BF16)] * 2
+        [shape(shared, order, BF16)] * 2
         + [shape(shared, loads)]
         + [shape(shared + list_rows, loads)] * n,
         in_specs=[HBM] * 4,
@@ -421,6 +430,14 @@
         flops=3 * full * shared,
         moved=8 * shared * order,
         name="first",
+    )
+    unpack_own, unpack_all, unpack = call(
+        functools.partial(marks_kernel, cap),
+        pairs,
+        [shape(shared, shared, BF16), shape(shared, n * shared, BF16), shape(shared, padded, BF16)],
+        flops=8 * shared * shared * wide,
+        moved=2 * shared * shared * wide,
+        name="marks",
     )
     floor, basis, tile_high, tile_low = call(
         prepare_kernel,

time: 89.4 us -> 89.4 us (level)
    pallas_call x25 -> x26, Pallas kernels: 21.5 us -> 21.8 us  [call(): pl.pallas_call(body, out_shape=outs, grid=grid, in_specs=in_specs, out_sp...]
where the time goes in v22:
time: 89.4 us; the launch traced here: 89.2 us
  starting transfers between devices  36.7 us (41%)
  waiting for transfers between devices  29.1 us (33%)
  Pallas kernels  21.8 us (24%)
  between operations  1.6 us (2%)
    ppermute x30, starting transfers between devices, swap(): return lax.ppermute(block, axis, [(i, i ^ d) for i in range(count)])  36.7 us
    ppermute x30, waiting for transfers between devices, swap(): return lax.ppermute(block, axis, [(i, i ^ d) for i in range(count)])  29.1 us
    pallas_call x26, Pallas kernels, call(): pl.pallas_call(body, out_shape=outs, grid=grid, in_specs=in_specs, out_sp...  21.8 us
  transfers between devices with their start and end apart: 30, of which 25 were waited for; matrix products, arithmetic and copies ran while one was open for 0% of the time, Pallas kernels for 16%

profile of v22, /device:TPU:0, one launch (start us, length us, event | category | flops | bytes accessed | tf_op | source)
XLA Modules:
  0.0 89.2 jit_solution(7837989318886625210)
XLA Ops:
  0.7 2.0 %first.1 = (bf16[256,1024]{1,0:T(8,128)(2,1)S(1)}, bf16[256,1024]{1,0:T(8,128)(2,1)S(1)}, f32[256,128]{1,0:T(8,128)S(1)}, f32[264,128]{1,0:T(8,128)S(1)}, f32[26...) custom-call(s32[1,256]{1,0:T(1,128)} %bitcast.28, s32[1,256]{1,0:T(1,128)} %rows.1, f32[1024,1024]{1,0:T(8,128)} %bitcast.30, ...), custom_call_target="tpu_custom_call" | custom-call | flops 201326592 | bytes 2097152 | tf_op jit(solution)/shard_map/first/pallas_call | solution.py:49
  2.6 5.1 %collective-permute-start = (f32[264,128]{1,0:T(8,128)S(1)}, f32[264,128]{1,0:T(8,128)S(1)}, u32[]{:S(2)}, u32[]{:S(2)}) collective-permute-start(f32[264,128]{1,0:T(8,128)S(1)} %get-tuple-element.81), channel_id=1, source_target_pairs={{0,12},{4,8},{8,4},{12,0},{1,13},{5,9},{9,5},{13,1},{2,14},{6,10},... | collective-permute-start | bytes 405512 | tf_op jit(solution)/shard_map/ppermute | solution.py:353
  7.8 0.6 collective-permute-start.2
  9.1 0.4 marks.1
  9.7 4.6 %rest_start.1 = (f32[768,128]{1,0:T(8,128)S(1)}, f32[64,128]{1,0:T(8,128)S(1)}, bf16[768,1024]{1,0:T(8,128)(2,1)S(1)}, bf16[768,1024]{1,0:T(8,128)(2,1)S(1)}) custom-call(s32[1]{0:T(128)S(6)} %copy.15.size, f32[1024,1024]{1,0:T(8,128)} %bitcast.31, f32[1024,128]{1,0:T(8,128)} %bitcast.20, f32[1024,128]{1,0:T(8,128)} %bitcast.21, f32[1024,128]{1,0:T(8,128)} %bitcast.7, ...), custom_call_target="tpu_custom_call" | custom-call | flops 603979776 | bytes 6291456 | tf_op jit(solution)/shard_map/rest_start/pallas_call | solution.py:49
  14.3 1.0 %collective-permute-done.1.refs_1_ = f32[264,128]{1,0:T(8,128)S(1)} collective-permute-done((f32[264,128]{1,0:T(8,128)S(1)}, f32[264,128]{1,0:T(8,128)S(1)}, u32[]{:S(2)}, u32[]{:S(2)}) %collective-permute-start.1) | collective-permute-done | bytes 135200 | tf_op jit(solution)/shard_map/ppermute | solution.py:353
  15.3 3.9 %collective-permute-done.2.refs_2_ = f32[264,128]{1,0:T(8,128)S(1)} collective-permute-done((f32[264,128]{1,0:T(8,128)S(1)}, f32[264,128]{1,0:T(8,128)S(1)}, u32[]{:S(2)}, u32[]{:S(2)}) %collective-permute-start.2) | collective-permute-done | bytes 135200 | tf_op jit(solution)/shard_map/ppermute | solution.py:353
  19.2 0.4 coarse.2
  19.6 0.8 collective-permute-start.3
  20.4 1.8 %collective-permute-start.4 = (f32[64,128]{1,0:T(8,128)S(1)}, f32[64,128]{1,0:T(8,128)S(1)}, u32[]{:S(2)}, u32[]{:S(2)}) collective-permute-start(f32[64,128]{1,0:T(8,128)S(1)} %get-tuple-element.90), channel_id=1, source_target_pairs={{0,12},{4,8},{8,4},{12,0},{1,13},{5,9},{9,5},{13,1},{2,14},{6,10},... | collective-permute-start | bytes 98312 | tf_op jit(solution)/shard_map/ppermute | solution.py:353
  22.3 0.9 %collective-permute-start.5 = (f32[64,128]{1,0:T(8,128)S(1)}, f32[64,128]{1,0:T(8,128)S(1)}, u32[]{:S(2)}, u32[]{:S(2)}) collective-permute-start(f32[64,128]{1,0:T(8,128)S(1)} %get-tuple-element.91), channel_id=1, source_target_pairs={{0,4},{4,0},{8,12},{12,8},{1,5},{5,1},{9,13},{13,9},{2,6},{6,2},{1... | collective-permute-start | bytes 98312 | tf_op jit(solution)/shard_map/ppermute | solution.py:353
  23.2 0.4 prepare.1
  23.6 1.1 %collective-permute-done.3.refs_1_ = f32[64,128]{1,0:T(8,128)S(1)} collective-permute-done((f32[64,128]{1,0:T(8,128)S(1)}, f32[64,128]{1,0:T(8,128)S(1)}, u32[]{:S(2)}, u32[]{:S(2)}) %collective-permute-start.3) | collective-permute-done | bytes 32800 | tf_op jit(solution)/shard_map/ppermute | solution.py:353
  24.6 1.7 %collective-permute-done.4.refs_2_ = f32[64,128]{1,0:T(8,128)S(1)} collective-permute-done((f32[64,128]{1,0:T(8,128)S(1)}, f32[64,128]{1,0:T(8,128)S(1)}, u32[]{:S(2)}, u32[]{:S(2)}) %collective-permute-start.4) | collective-permute-done | bytes 32800 | tf_op jit(solution)/shard_map/ppermute | solution.py:353
  26.9 1.6 %collective-permute-start.7 = (f32[64,128]{1,0:T(8,128)S(1)}, f32[64,128]{1,0:T(8,128)S(1)}, u32[]{:S(2)}, u32[]{:S(2)}) collective-permute-start(f32[64,128]{1,0:T(8,128)S(1)} %get-tuple-element.94), channel_id=1, source_target_pairs={{0,2},{1,3},{2,0},{3,1},{4,6},{5,7},{6,4},{7,5},{8,10},{9,11},{10,... | collective-permute-start | bytes 98312 | tf_op jit(solution)/shard_map/ppermute | solution.py:353
  29.0 1.5 %collective-permute-done.6.refs_1_ = f32[64,128]{1,0:T(8,128)S(1)} collective-permute-done((f32[64,128]{1,0:T(8,128)S(1)}, f32[64,128]{1,0:T(8,128)S(1)}, u32[]{:S(2)}, u32[]{:S(2)}) %collective-permute-start.6) | collective-permute-done | bytes 32800 | tf_op jit(solution)/shard_map/ppermute | solution.py:353
  30.5 0.4 collective-permute-done.7.refs_2_
  30.9 0.9 lift.2
  31.8 1.7 %collective-permute-start.9 = (f32[128,128]{1,0:T(8,128)S(1)}, f32[128,128]{1,0:T(8,128)S(1)}, u32[]{:S(2)}, u32[]{:S(2)}) collective-permute-start(f32[128,128]{1,0:T(8,128)S(1)} %get-tuple-element.103), channel_id=1, source_target_pairs={{0,8},{4,12},{8,0},{12,4},{1,9},{5,13},{9,1},{13,5},{2,10},{6,14},... | collective-permute-start | bytes 196616 | tf_op jit(solution)/shard_map/ppermute | solution.py:353
  33.4 0.8 collective-permute-start.10
  34.2 2.0 %collective-permute-start.11 = (f32[128,128]{1,0:T(8,128)S(1)}, f32[128,128]{1,0:T(8,128)S(1)}, u32[]{:S(2)}, u32[]{:S(2)}) collective-permute-start(f32[128,128]{1,0:T(8,128)S(1)} %get-tuple-element.105), channel_id=1, source_target_pairs={{0,12},{4,8},{8,4},{12,0},{1,13},{5,9},{9,5},{13,1},{2,14},{6,10},... | collective-permute-start | bytes 196616 | tf_op jit(solution)/shard_map/ppermute | solution.py:353
  36.4 1.5 %rest.3 = (f32[768,128]{1,0:T(8,128)S(1)}, f32[640,128]{1,0:T(8,128)S(1)}) custom-call(s32[1]{0:T(128)S(6)} %copy.15.size, bf16[768,1024]{1,0:T(8,128)(2,1)S(1)} %get-tuple-element.111.high, bf16[768,1024]{1,0:T(8,128)(2,1)S(1)} %get-tuple-element.112.low, f32[256,128]{1,0:T(8,128)S(1)} %get-tuple-element.108.mult_s.refs_5_, ...), custom_call_target="tpu_custom_call" | custom-call | flops 805306368 | bytes 4194304 | tf_op jit(solution)/shard_map/rest/pallas_call | solution.py:49
  37.9 1.4 %collective-permute-done.9.refs_0_ = f32[128,128]{1,0:T(8,128)S(1)} collective-permute-done((f32[128,128]{1,0:T(8,128)S(1)}, f32[128,128]{1,0:T(8,128)S(1)}, u32[]{:S(2)}, u32[]{:S(2)}) %collective-permute-start.9) | collective-permute-done | bytes 65568 | tf_op jit(solution)/shard_map/ppermute | solution.py:353
  39.3 0.7 collective-permute-done.10.refs_1_
  40.0 0.3 collective-permute-done.11.refs_2_
  40.3 0.5 sweep.3
  40.8 1.9 %collective-permute-start.12 = (f32[128,128]{1,0:T(8,128)S(1)}, f32[128,128]{1,0:T(8,128)S(1)}, u32[]{:S(2)}, u32[]{:S(2)}) collective-permute-start(f32[128,128]{1,0:T(8,128)S(1)} %get-tuple-element.115), channel_id=1, source_target_pairs={{0,8},{4,12},{8,0},{12,4},{1,9},{5,13},{9,1},{13,5},{2,10},{6,14},... | collective-permute-start | bytes 196616 | tf_op jit(solution)/shard_map/ppermute | solution.py:353
  42.8 2.0 %collective-permute-start.13 = (f32[128,128]{1,0:T(8,128)S(1)}, f32[128,128]{1,0:T(8,128)S(1)}, u32[]{:S(2)}, u32[]{:S(2)}) collective-permute-start(f32[128,128]{1,0:T(8,128)S(1)} %get-tuple-element.116), channel_id=1, source_target_pairs={{0,12},{4,8},{8,4},{12,0},{1,13},{5,9},{9,5},{13,1},{2,14},{6,10},... | collective-permute-start | bytes 196616 | tf_op jit(solution)/shard_map/ppermute | solution.py:353
  45.0 1.5 %rest.4 = (f32[768,128]{1,0:T(8,128)S(1)}, f32[640,128]{1,0:T(8,128)S(1)}) custom-call(s32[1]{0:T(128)S(6)} %copy.15.size, bf16[768,1024]{1,0:T(8,128)(2,1)S(1)} %get-tuple-element.111.high, bf16[768,1024]{1,0:T(8,128)(2,1)S(1)} %get-tuple-element.112.low, f32[256,128]{1,0:T(8,128)S(1)} %get-tuple-element.119.mult_s.refs_5_, ...), custom_call_target="tpu_custom_call" | custom-call | flops 805306368 | bytes 4194304 | tf_op jit(solution)/shard_map/rest/pallas_call | solution.py:49
  46.5 1.9 %collective-permute-done.12.refs_0_ = f32[128,128]{1,0:T(8,128)S(1)} collective-permute-done((f32[128,128]{1,0:T(8,128)S(1)}, f32[128,128]{1,0:T(8,128)S(1)}, u32[]{:S(2)}, u32[]{:S(2)}) %collective-permute-start.12) | collective-permute-done | bytes 65568 | tf_op jit(solution)/shard_map/ppermute | solution.py:353
  48.4 0.9 %collective-permute-done.13.refs_1_ = f32[128,128]{1,0:T(8,128)S(1)} collective-permute-done((f32[128,128]{1,0:T(8,128)S(1)}, f32[128,128]{1,0:T(8,128)S(1)}, u32[]{:S(2)}, u32[]{:S(2)}) %collective-permute-start.13) | collective-permute-done | bytes 65568 | tf_op jit(solution)/shard_map/ppermute | solution.py:353
  49.3 0.6 collective-permute-done.14.refs_2_
  49.9 0.5 sweep.4
  50.5 0.8 collective-permute-start.15
  51.2 1.9 %collective-permute-start.16 = (f32[128,128]{1,0:T(8,128)S(1)}, f32[128,128]{1,0:T(8,128)S(1)}, u32[]{:S(2)}, u32[]{:S(2)}) collective-permute-start(f32[128,128]{1,0:T(8,128)S(1)} %get-tuple-element.123), channel_id=1, source_target_pairs={{0,12},{4,8},{8,4},{12,0},{1,13},{5,9},{9,5},{13,1},{2,14},{6,10},... | collective-permute-start | bytes 196616 | tf_op jit(solution)/shard_map/ppermute | solution.py:353
  53.1 0.9 collective-permute-start.17
  54.2 1.1 %rest_first.1 = (f32[768,128]{1,0:T(8,128)S(1)}, f32[64,128]{1,0:T(8,128)S(1)}) custom-call(s32[1]{0:T(128)S(6)} %copy.15.size, bf16[768,1024]{1,0:T(8,128)(2,1)S(1)} %get-tuple-element.111.high, bf16[768,1024]{1,0:T(8,128)(2,1)S(1)} %get-tuple-element.112.low, f32[256,128]{1,0:T(8,128)S(1)} %get-tuple-element.126.mult_s.refs_5_, ...), custom_call_target="tpu_custom_call" | custom-call | flops 603979776 | bytes 3145728 | tf_op jit(solution)/shard_map/rest_first/pallas_call | solution.py:49
  55.4 2.5 %collective-permute-done.15.refs_0_ = f32[128,128]{1,0:T(8,128)S(1)} collective-permute-done((f32[128,128]{1,0:T(8,128)S(1)}, f32[128,128]{1,0:T(8,128)S(1)}, u32[]{:S(2)}, u32[]{:S(2)}) %collective-permute-start.15) | collective-permute-done | bytes 65568 | tf_op jit(solution)/shard_map/ppermute | solution.py:353
  57.8 0.6 collective-permute-done.17.refs_2_
  58.5 0.4 coarse.3
  58.9 0.4 collective-permute-start.18
  59.3 2.6 %collective-permute-start.19 = (f32[64,128]{1,0:T(8,128)S(1)}, f32[64,128]{1,0:T(8,128)S(1)}, u32[]{:S(2)}, u32[]{:S(2)}) collective-permute-start(f32[64,128]{1,0:T(8,128)S(1)} %get-tuple-element.131), channel_id=1, source_target_pairs={{0,12},{4,8},{8,4},{12,0},{1,13},{5,9},{9,5},{13,1},{2,14},{6,10},... | collective-permute-start | bytes 98312 | tf_op jit(solution)/shard_map/ppermute | solution.py:353
  61.9 0.6 collective-permute-start.20
  62.4 1.7 %collective-permute-done.18.refs_1_ = f32[64,128]{1,0:T(8,128)S(1)} collective-permute-done((f32[64,128]{1,0:T(8,128)S(1)}, f32[64,128]{1,0:T(8,128)S(1)}, u32[]{:S(2)}, u32[]{:S(2)}) %collective-permute-start.18) | collective-permute-done | bytes 32800 | tf_op jit(solution)/shard_map/ppermute | solution.py:353
  64.1 0.9 %collective-permute-done.19.refs_2_ = f32[64,128]{1,0:T(8,128)S(1)} collective-permute-done((f32[64,128]{1,0:T(8,128)S(1)}, f32[64,128]{1,0:T(8,128)S(1)}, u32[]{:S(2)}, u32[]{:S(2)}) %collective-permute-start.19) | collective-permute-done | bytes 32800 | tf_op jit(solution)/shard_map/ppermute | solution.py:353
  65.0 0.8 collective-permute-done.20.refs_3_
  66.4 1.6 %collective-permute-start.23 = (f32[64,128]{1,0:T(8,128)S(1)}, f32[64,128]{1,0:T(8,128)S(1)}, u32[]{:S(2)}, u32[]{:S(2)}) collective-permute-start(f32[64,128]{1,0:T(8,128)S(1)} %get-tuple-element.136), channel_id=1, source_target_pairs={{0,1},{1,0},{2,3},{3,2},{4,5},{5,4},{6,7},{7,6},{8,9},{9,8},{10,11... | collective-permute-start | bytes 98312 | tf_op jit(solution)/shard_map/ppermute | solution.py:353
  68.0 1.5 %collective-permute-done.21.refs_1_ = f32[64,128]{1,0:T(8,128)S(1)} collective-permute-done((f32[64,128]{1,0:T(8,128)S(1)}, f32[64,128]{1,0:T(8,128)S(1)}, u32[]{:S(2)}, u32[]{:S(2)}) %collective-permute-start.21) | collective-permute-done | bytes 32800 | tf_op jit(solution)/shard_map/ppermute | solution.py:353
  69.4 0.7 collective-permute-done.22.refs_2_
  70.1 0.9 lift.3
  71.0 0.8 collective-permute-start.24
  71.8 1.6 %collective-permute-start.25 = (f32[128,128]{1,0:T(8,128)S(1)}, f32[128,128]{1,0:T(8,128)S(1)}, u32[]{:S(2)}, u32[]{:S(2)}) collective-permute-start(f32[128,128]{1,0:T(8,128)S(1)} %get-tuple-element.140), channel_id=1, source_target_pairs={{0,4},{4,0},{8,12},{12,8},{1,5},{5,1},{9,13},{13,9},{2,6},{6,2},{1... | collective-permute-start | bytes 196616 | tf_op jit(solution)/shard_map/ppermute | solution.py:353
  73.4 2.0 %collective-permute-start.26 = (f32[128,128]{1,0:T(8,128)S(1)}, f32[128,128]{1,0:T(8,128)S(1)}, u32[]{:S(2)}, u32[]{:S(2)}) collective-permute-start(f32[128,128]{1,0:T(8,128)S(1)} %get-tuple-element.141), channel_id=1, source_target_pairs={{0,12},{4,8},{8,4},{12,0},{1,13},{5,9},{9,5},{13,1},{2,14},{6,10},... | collective-permute-start | bytes 196616 | tf_op jit(solution)/shard_map/ppermute | solution.py:353
  75.7 1.5 %rest.5 = (f32[768,128]{1,0:T(8,128)S(1)}, f32[640,128]{1,0:T(8,128)S(1)}) custom-call(s32[1]{0:T(128)S(6)} %copy.15.size, bf16[768,1024]{1,0:T(8,128)(2,1)S(1)} %get-tuple-element.111.high, bf16[768,1024]{1,0:T(8,128)(2,1)S(1)} %get-tuple-element.112.low, f32[256,128]{1,0:T(8,128)S(1)} %get-tuple-element.143.mult_s.refs_5_, ...), custom_call_target="tpu_custom_call" | custom-call | flops 805306368 | bytes 4194304 | tf_op jit(solution)/shard_map/rest/pallas_call | solution.py:49
  77.1 1.0 %collective-permute-done.24.refs_0_ = f32[128,128]{1,0:T(8,128)S(1)} collective-permute-done((f32[128,128]{1,0:T(8,128)S(1)}, f32[128,128]{1,0:T(8,128)S(1)}, u32[]{:S(2)}, u32[]{:S(2)}) %collective-permute-start.24) | collective-permute-done | bytes 65568 | tf_op jit(solution)/shard_map/ppermute | solution.py:353
  78.2 1.4 %collective-permute-done.26.refs_2_ = f32[128,128]{1,0:T(8,128)S(1)} collective-permute-done((f32[128,128]{1,0:T(8,128)S(1)}, f32[128,128]{1,0:T(8,128)S(1)}, u32[]{:S(2)}, u32[]{:S(2)}) %collective-permute-start.26) | collective-permute-done | bytes 65568 | tf_op jit(solution)/shard_map/ppermute | solution.py:353
  79.6 0.5 sweep.5
  80.1 1.4 %collective-permute-start.27 = (f32[128,128]{1,0:T(8,128)S(1)}, f32[128,128]{1,0:T(8,128)S(1)}, u32[]{:S(2)}, u32[]{:S(2)}) collective-permute-start(f32[128,128]{1,0:T(8,128)S(1)} %get-tuple-element.146), channel_id=1, source_target_pairs={{0,8},{4,12},{8,0},{12,4},{1,9},{5,13},{9,1},{13,5},{2,10},{6,14},... | collective-permute-start | bytes 196616 | tf_op jit(solution)/shard_map/ppermute | solution.py:353
  81.4 2.1 %collective-permute-start.28 = (f32[128,128]{1,0:T(8,128)S(1)}, f32[128,128]{1,0:T(8,128)S(1)}, u32[]{:S(2)}, u32[]{:S(2)}) collective-permute-start(f32[128,128]{1,0:T(8,128)S(1)} %get-tuple-element.147), channel_id=1, source_target_pairs={{0,12},{4,8},{8,4},{12,0},{1,13},{5,9},{9,5},{13,1},{2,14},{6,10},... | collective-permute-start | bytes 196616 | tf_op jit(solution)/shard_map/ppermute | solution.py:353
  83.8 1.9 %rest_last.1 = (f32[1024,128]{1,0:T(8,128)}, f32[1024,128]{1,0:T(8,128)}) custom-call(s32[1]{0:T(128)S(6)} %copy.15.size, bf16[768,1024]{1,0:T(8,128)(2,1)S(1)} %get-tuple-element.111.high, bf16[768,1024]{1,0:T(8,128)(2,1)S(1)} %get-tuple-element.112.low, f32[256,128]{1,0:T(8,128)S(1)} %get-tuple-element.150.mult_s.refs_5_, ...), custom_call_target="tpu_custom_call" | custom-call | flops 603979776 | bytes 3145728 | tf_op jit(solution)/shard_map/rest_last/pallas_call | solution.py:49
  85.7 1.0 %collective-permute-done.27.refs_0_ = f32[128,128]{1,0:T(8,128)S(1)} collective-permute-done((f32[128,128]{1,0:T(8,128)S(1)}, f32[128,128]{1,0:T(8,128)S(1)}, u32[]{:S(2)}, u32[]{:S(2)}) %collective-permute-start.27) | collective-permute-done | bytes 65568 | tf_op jit(solution)/shard_map/ppermute | solution.py:353
  86.7 0.8 collective-permute-done.28.refs_1_
  87.6 0.7 collective-permute-done.29.refs_2_
  88.2 1.0 %last.1 = (f32[1024,128]{1,0:T(8,128)}, f32[1024,128]{1,0:T(8,128)}) custom-call(s32[1]{0:T(128)S(6)} %copy.15.size, f32[128,128]{1,0:T(8,128)S(1)} %collective-permute-done.27.refs_0_, f32[128,128]{1,0:T(8,128)S(1)} %collective-permute-done.28.refs_1_, ...), custom_call_target="tpu_custom_call", output_to_operand_aliasing={{0}: (8, {}), {1}: (9, {})} | custom-call | flops 75497472 | bytes 196608 | tf_op jit(solution)/shard_map/last/pallas_call | solution.py:49
  (38 shorter events, 3.0 us)
Async XLA Ops:
  0.6 8.4 %copy-start.6 = (s32[1,256,1]{1,2,0:T(1,128)S(1)}, s32[1,256,1]{1,2,0:T(1,128)}, u32[]{:S(2)}) copy-start(s32[1,256,1]{1,2,0:T(1,128)} %param.14) | copy-start | bytes 3076
  0.6 8.4 %copy-start.7 = (s32[1,256]{1,0:T(1,128)S(1)}, s32[1,256]{1,0:T(1,128)}, u32[]{:S(2)}) copy-start(s32[1,256]{1,0:T(1,128)} %rows.1) | copy-start | bytes 3076
  0.6 8.8 %copy-start = (f32[1,1024,128]{2,1,0:T(8,128)S(1)}, f32[1,1024,128]{2,1,0:T(8,128)}, u32[]{:S(2)}) copy-start(f32[1,1024,128]{2,1,0:T(8,128)} %param.12) | copy-start | bytes 1572868
  2.6 11.7 %collective-permute-start = (f32[264,128]{1,0:T(8,128)S(1)}, f32[264,128]{1,0:T(8,128)S(1)}, u32[]{:S(2)}, u32[]{:S(2)}) collective-permute-start(f32[264,128]{1,0:T(8,128)S(1)} %get-tuple-element.81), channel_id=1, source_target_pairs={{0,12},{4,8},{8,4},{12,0},{1,13},{5,9},{9,5},{13,1},{2,14},{6,10},... | collective-permute-start | bytes 405512 | tf_op jit(solution)/shard_map/ppermute | solution.py:353
  7.8 7.6 %collective-permute-start.1 = (f32[264,128]{1,0:T(8,128)S(1)}, f32[264,128]{1,0:T(8,128)S(1)}, u32[]{:S(2)}, u32[]{:S(2)}) collective-permute-start(f32[264,128]{1,0:T(8,128)S(1)} %get-tuple-element.82), channel_id=1, source_target_pairs={{0,4},{4,0},{8,12},{12,8},{1,5},{5,1},{9,13},{13,9},{2,6},{6,2},{1... | collective-permute-start | bytes 405512 | tf_op jit(solution)/shard_map/ppermute | solution.py:353
  7.8 11.4 %collective-permute-start.2 = (f32[264,128]{1,0:T(8,128)S(1)}, f32[264,128]{1,0:T(8,128)S(1)}, u32[]{:S(2)}, u32[]{:S(2)}) collective-permute-start(f32[264,128]{1,0:T(8,128)S(1)} %get-tuple-element.83), channel_id=1, source_target_pairs={{0,8},{4,12},{8,0},{12,4},{1,9},{5,13},{9,1},{13,5},{2,10},{6,14},... | collective-permute-start | bytes 405512 | tf_op jit(solution)/shard_map/ppermute | solution.py:353
  9.7 9.5 %copy-start.2 = (f32[1,1024,128]{2,1,0:T(8,128)S(1)}, f32[1,1024,128]{2,1,0:T(8,128)}, u32[]{:S(2)}) copy-start(f32[1,1024,128]{2,1,0:T(8,128)} %param.13) | copy-start | bytes 1572868
  9.7 9.5 %copy-start.3 = (f32[1,64,1024]{2,1,0:T(8,128)S(1)}, f32[1,64,1024]{2,1,0:T(8,128)}, u32[]{:S(2)}) copy-start(f32[1,64,1024]{2,1,0:T(8,128)} %param.11) | copy-start | bytes 786436
  14.3 8.9 %copy-start.4 = (f32[256,256]{1,0:T(8,128)S(1)}, f32[256,256]{1,0:T(8,128)}, u32[]{:S(2)}) copy-start(f32[256,256]{1,0:T(8,128)} %tile.3) | copy-start | bytes 786436
  14.3 8.9 %copy-start.5 = (s32[1,1024]{1,0:T(1,128)S(1)}, s32[1,1024]{1,0:T(1,128)}, u32[]{:S(2)}) copy-start(s32[1,1024]{1,0:T(1,128)} %contact.1) | copy-start | bytes 12292
  19.6 5.0 %collective-permute-start.3 = (f32[64,128]{1,0:T(8,128)S(1)}, f32[64,128]{1,0:T(8,128)S(1)}, u32[]{:S(2)}, u32[]{:S(2)}) collective-permute-start(f32[64,128]{1,0:T(8,128)S(1)} %get-tuple-element.89), channel_id=1, source_target_pairs={{0,8},{4,12},{8,0},{12,4},{1,9},{5,13},{9,1},{13,5},{2,10},{6,14},... | collective-permute-start | bytes 98312 | tf_op jit(solution)/shard_map/ppermute | solution.py:353
  20.4 5.9 %collective-permute-start.4 = (f32[64,128]{1,0:T(8,128)S(1)}, f32[64,128]{1,0:T(8,128)S(1)}, u32[]{:S(2)}, u32[]{:S(2)}) collective-permute-start(f32[64,128]{1,0:T(8,128)S(1)} %get-tuple-element.90), channel_id=1, source_target_pairs={{0,12},{4,8},{8,4},{12,0},{1,13},{5,9},{9,5},{13,1},{2,14},{6,10},... | collective-permute-start | bytes 98312 | tf_op jit(solution)/shard_map/ppermute | solution.py:353
  22.3 4.3 %collective-permute-start.5 = (f32[64,128]{1,0:T(8,128)S(1)}, f32[64,128]{1,0:T(8,128)S(1)}, u32[]{:S(2)}, u32[]{:S(2)}) collective-permute-start(f32[64,128]{1,0:T(8,128)S(1)} %get-tuple-element.91), channel_id=1, source_target_pairs={{0,4},{4,0},{8,12},{12,8},{1,5},{5,1},{9,13},{13,9},{2,6},{6,2},{1... | collective-permute-start | bytes 98312 | tf_op jit(solution)/shard_map/ppermute | solution.py:353
  26.8 3.7 %collective-permute-start.6 = (f32[64,128]{1,0:T(8,128)S(1)}, f32[64,128]{1,0:T(8,128)S(1)}, u32[]{:S(2)}, u32[]{:S(2)}) collective-permute-start(f32[64,128]{1,0:T(8,128)S(1)} %get-tuple-element.93), channel_id=1, source_target_pairs={{0,3},{1,2},{2,1},{3,0},{4,7},{5,6},{6,5},{7,4},{8,11},{9,10},{10,... | collective-permute-start | bytes 98312 | tf_op jit(solution)/shard_map/ppermute | solution.py:353
  26.9 4.0 %collective-permute-start.7 = (f32[64,128]{1,0:T(8,128)S(1)}, f32[64,128]{1,0:T(8,128)S(1)}, u32[]{:S(2)}, u32[]{:S(2)}) collective-permute-start(f32[64,128]{1,0:T(8,128)S(1)} %get-tuple-element.94), channel_id=1, source_target_pairs={{0,2},{1,3},{2,0},{3,1},{4,6},{5,7},{6,4},{7,5},{8,10},{9,11},{10,... | collective-permute-start | bytes 98312 | tf_op jit(solution)/shard_map/ppermute | solution.py:353
  28.4 2.5 %collective-permute-start.8 = (f32[64,128]{1,0:T(8,128)S(1)}, f32[64,128]{1,0:T(8,128)S(1)}, u32[]{:S(2)}, u32[]{:S(2)}) collective-permute-start(f32[64,128]{1,0:T(8,128)S(1)} %get-tuple-element.95), channel_id=1, source_target_pairs={{0,1},{1,0},{2,3},{3,2},{4,5},{5,4},{6,7},{7,6},{8,9},{9,8},{10,11... | collective-permute-start | bytes 98312 | tf_op jit(solution)/shard_map/ppermute | solution.py:353
  29.0 7.2 %copy-start.1 = (f32[1,1024,128]{2,1,0:T(8,128)S(1)}, f32[1,1024,128]{2,1,0:T(8,128)}, u32[]{:S(2)}) copy-start(f32[1,1024,128]{2,1,0:T(8,128)} %param.12) | copy-start | bytes 1572868
  31.8 7.6 %collective-permute-start.9 = (f32[128,128]{1,0:T(8,128)S(1)}, f32[128,128]{1,0:T(8,128)S(1)}, u32[]{:S(2)}, u32[]{:S(2)}) collective-permute-start(f32[128,128]{1,0:T(8,128)S(1)} %get-tuple-element.103), channel_id=1, source_target_pairs={{0,8},{4,12},{8,0},{12,4},{1,9},{5,13},{9,1},{13,5},{2,10},{6,14},... | collective-permute-start | bytes 196616 | tf_op jit(solution)/shard_map/ppermute | solution.py:353
  33.4 6.6 %collective-permute-start.10 = (f32[128,128]{1,0:T(8,128)S(1)}, f32[128,128]{1,0:T(8,128)S(1)}, u32[]{:S(2)}, u32[]{:S(2)}) collective-permute-start(f32[128,128]{1,0:T(8,128)S(1)} %get-tuple-element.104), channel_id=1, source_target_pairs={{0,4},{4,0},{8,12},{12,8},{1,5},{5,1},{9,13},{13,9},{2,6},{6,2},{1... | collective-permute-start | bytes 196616 | tf_op jit(solution)/shard_map/ppermute | solution.py:353
  34.2 6.1 %collective-permute-start.11 = (f32[128,128]{1,0:T(8,128)S(1)}, f32[128,128]{1,0:T(8,128)S(1)}, u32[]{:S(2)}, u32[]{:S(2)}) collective-permute-start(f32[128,128]{1,0:T(8,128)S(1)} %get-tuple-element.105), channel_id=1, source_target_pairs={{0,12},{4,8},{8,4},{12,0},{1,13},{5,9},{9,5},{13,1},{2,14},{6,10},... | collective-permute-start | bytes 196616 | tf_op jit(solution)/shard_map/ppermute | solution.py:353
  40.8 7.5 %collective-permute-start.12 = (f32[128,128]{1,0:T(8,128)S(1)}, f32[128,128]{1,0:T(8,128)S(1)}, u32[]{:S(2)}, u32[]{:S(2)}) collective-permute-start(f32[128,128]{1,0:T(8,128)S(1)} %get-tuple-element.115), channel_id=1, source_target_pairs={{0,8},{4,12},{8,0},{12,4},{1,9},{5,13},{9,1},{13,5},{2,10},{6,14},... | collective-permute-start | bytes 196616 | tf_op jit(solution)/shard_map/ppermute | solution.py:353
  42.8 6.5 %collective-permute-start.13 = (f32[128,128]{1,0:T(8,128)S(1)}, f32[128,128]{1,0:T(8,128)S(1)}, u32[]{:S(2)}, u32[]{:S(2)}) collective-permute-start(f32[128,128]{1,0:T(8,128)S(1)} %get-tuple-element.116), channel_id=1, source_target_pairs={{0,12},{4,8},{8,4},{12,0},{1,13},{5,9},{9,5},{13,1},{2,14},{6,10},... | collective-permute-start | bytes 196616 | tf_op jit(solution)/shard_map/ppermute | solution.py:353
  44.8 5.1 %collective-permute-start.14 = (f32[128,128]{1,0:T(8,128)S(1)}, f32[128,128]{1,0:T(8,128)S(1)}, u32[]{:S(2)}, u32[]{:S(2)}) collective-permute-start(f32[128,128]{1,0:T(8,128)S(1)} %get-tuple-element.117), channel_id=1, source_target_pairs={{0,4},{4,0},{8,12},{12,8},{1,5},{5,1},{9,13},{13,9},{2,6},{6,2},{1... | collective-permute-start | bytes 196616 | tf_op jit(solution)/shard_map/ppermute | solution.py:353
  50.5 7.4 %collective-permute-start.15 = (f32[128,128]{1,0:T(8,128)S(1)}, f32[128,128]{1,0:T(8,128)S(1)}, u32[]{:S(2)}, u32[]{:S(2)}) collective-permute-start(f32[128,128]{1,0:T(8,128)S(1)} %get-tuple-element.122), channel_id=1, source_target_pairs={{0,8},{4,12},{8,0},{12,4},{1,9},{5,13},{9,1},{13,5},{2,10},{6,14},... | collective-permute-start | bytes 196616 | tf_op jit(solution)/shard_map/ppermute | solution.py:353
  51.2 6.6 %collective-permute-start.16 = (f32[128,128]{1,0:T(8,128)S(1)}, f32[128,128]{1,0:T(8,128)S(1)}, u32[]{:S(2)}, u32[]{:S(2)}) collective-permute-start(f32[128,128]{1,0:T(8,128)S(1)} %get-tuple-element.123), channel_id=1, source_target_pairs={{0,12},{4,8},{8,4},{12,0},{1,13},{5,9},{9,5},{13,1},{2,14},{6,10},... | collective-permute-start | bytes 196616 | tf_op jit(solution)/shard_map/ppermute | solution.py:353
  53.1 5.3 %collective-permute-start.17 = (f32[128,128]{1,0:T(8,128)S(1)}, f32[128,128]{1,0:T(8,128)S(1)}, u32[]{:S(2)}, u32[]{:S(2)}) collective-permute-start(f32[128,128]{1,0:T(8,128)S(1)} %get-tuple-element.124), channel_id=1, source_target_pairs={{0,4},{4,0},{8,12},{12,8},{1,5},{5,1},{9,13},{13,9},{2,6},{6,2},{1... | collective-permute-start | bytes 196616 | tf_op jit(solution)/shard_map/ppermute | solution.py:353
  58.9 5.2 %collective-permute-start.18 = (f32[64,128]{1,0:T(8,128)S(1)}, f32[64,128]{1,0:T(8,128)S(1)}, u32[]{:S(2)}, u32[]{:S(2)}) collective-permute-start(f32[64,128]{1,0:T(8,128)S(1)} %get-tuple-element.130), channel_id=1, source_target_pairs={{0,8},{4,12},{8,0},{12,4},{1,9},{5,13},{9,1},{13,5},{2,10},{6,14},... | collective-permute-start | bytes 98312 | tf_op jit(solution)/shard_map/ppermute | solution.py:353
  59.3 5.7 %collective-permute-start.19 = (f32[64,128]{1,0:T(8,128)S(1)}, f32[64,128]{1,0:T(8,128)S(1)}, u32[]{:S(2)}, u32[]{:S(2)}) collective-permute-start(f32[64,128]{1,0:T(8,128)S(1)} %get-tuple-element.131), channel_id=1, source_target_pairs={{0,12},{4,8},{8,4},{12,0},{1,13},{5,9},{9,5},{13,1},{2,14},{6,10},... | collective-permute-start | bytes 98312 | tf_op jit(solution)/shard_map/ppermute | solution.py:353
  61.9 3.9 %collective-permute-start.20 = (f32[64,128]{1,0:T(8,128)S(1)}, f32[64,128]{1,0:T(8,128)S(1)}, u32[]{:S(2)}, u32[]{:S(2)}) collective-permute-start(f32[64,128]{1,0:T(8,128)S(1)} %get-tuple-element.132), channel_id=1, source_target_pairs={{0,4},{4,0},{8,12},{12,8},{1,5},{5,1},{9,13},{13,9},{2,6},{6,2},{1... | collective-permute-start | bytes 98312 | tf_op jit(solution)/shard_map/ppermute | solution.py:353
  66.0 3.4 %collective-permute-start.21 = (f32[64,128]{1,0:T(8,128)S(1)}, f32[64,128]{1,0:T(8,128)S(1)}, u32[]{:S(2)}, u32[]{:S(2)}) collective-permute-start(f32[64,128]{1,0:T(8,128)S(1)} %get-tuple-element.134), channel_id=1, source_target_pairs={{0,3},{1,2},{2,1},{3,0},{4,7},{5,6},{6,5},{7,4},{8,11},{9,10},{10,... | collective-permute-start | bytes 98312 | tf_op jit(solution)/shard_map/ppermute | solution.py:353
  66.1 4.0 %collective-permute-start.22 = (f32[64,128]{1,0:T(8,128)S(1)}, f32[64,128]{1,0:T(8,128)S(1)}, u32[]{:S(2)}, u32[]{:S(2)}) collective-permute-start(f32[64,128]{1,0:T(8,128)S(1)} %get-tuple-element.135), channel_id=1, source_target_pairs={{0,2},{1,3},{2,0},{3,1},{4,6},{5,7},{6,4},{7,5},{8,10},{9,11},{10,... | collective-permute-start | bytes 98312 | tf_op jit(solution)/shard_map/ppermute | solution.py:353
  66.4 3.7 %collective-permute-start.23 = (f32[64,128]{1,0:T(8,128)S(1)}, f32[64,128]{1,0:T(8,128)S(1)}, u32[]{:S(2)}, u32[]{:S(2)}) collective-permute-start(f32[64,128]{1,0:T(8,128)S(1)} %get-tuple-element.136), channel_id=1, source_target_pairs={{0,1},{1,0},{2,3},{3,2},{4,5},{5,4},{6,7},{7,6},{8,9},{9,8},{10,11... | collective-permute-start | bytes 98312 | tf_op jit(solution)/shard_map/ppermute | solution.py:353
  71.0 7.2 %collective-permute-start.24 = (f32[128,128]{1,0:T(8,128)S(1)}, f32[128,128]{1,0:T(8,128)S(1)}, u32[]{:S(2)}, u32[]{:S(2)}) collective-permute-start(f32[128,128]{1,0:T(8,128)S(1)} %get-tuple-element.139), channel_id=1, source_target_pairs={{0,8},{4,12},{8,0},{12,4},{1,9},{5,13},{9,1},{13,5},{2,10},{6,14},... | collective-permute-start | bytes 196616 | tf_op jit(solution)/shard_map/ppermute | solution.py:353
  71.8 6.4 %collective-permute-start.25 = (f32[128,128]{1,0:T(8,128)S(1)}, f32[128,128]{1,0:T(8,128)S(1)}, u32[]{:S(2)}, u32[]{:S(2)}) collective-permute-start(f32[128,128]{1,0:T(8,128)S(1)} %get-tuple-element.140), channel_id=1, source_target_pairs={{0,4},{4,0},{8,12},{12,8},{1,5},{5,1},{9,13},{13,9},{2,6},{6,2},{1... | collective-permute-start | bytes 196616 | tf_op jit(solution)/shard_map/ppermute | solution.py:353
  73.4 6.1 %collective-permute-start.26 = (f32[128,128]{1,0:T(8,128)S(1)}, f32[128,128]{1,0:T(8,128)S(1)}, u32[]{:S(2)}, u32[]{:S(2)}) collective-permute-start(f32[128,128]{1,0:T(8,128)S(1)} %get-tuple-element.141), channel_id=1, source_target_pairs={{0,12},{4,8},{8,4},{12,0},{1,13},{5,9},{9,5},{13,1},{2,14},{6,10},... | collective-permute-start | bytes 196616 | tf_op jit(solution)/shard_map/ppermute | solution.py:353
  80.1 6.6 %collective-permute-start.27 = (f32[128,128]{1,0:T(8,128)S(1)}, f32[128,128]{1,0:T(8,128)S(1)}, u32[]{:S(2)}, u32[]{:S(2)}) collective-permute-start(f32[128,128]{1,0:T(8,128)S(1)} %get-tuple-element.146), channel_id=1, source_target_pairs={{0,8},{4,12},{8,0},{12,4},{1,9},{5,13},{9,1},{13,5},{2,10},{6,14},... | collective-permute-start | bytes 196616 | tf_op jit(solution)/shard_map/ppermute | solution.py:353
  81.4 6.1 %collective-permute-start.28 = (f32[128,128]{1,0:T(8,128)S(1)}, f32[128,128]{1,0:T(8,128)S(1)}, u32[]{:S(2)}, u32[]{:S(2)}) collective-permute-start(f32[128,128]{1,0:T(8,128)S(1)} %get-tuple-element.147), channel_id=1, source_target_pairs={{0,12},{4,8},{8,4},{12,0},{1,13},{5,9},{9,5},{13,1},{2,14},{6,10},... | collective-permute-start | bytes 196616 | tf_op jit(solution)/shard_map/ppermute | solution.py:353
  83.6 4.7 %collective-permute-start.29 = (f32[128,128]{1,0:T(8,128)S(1)}, f32[128,128]{1,0:T(8,128)S(1)}, u32[]{:S(2)}, u32[]{:S(2)}) collective-permute-start(f32[128,128]{1,0:T(8,128)S(1)} %get-tuple-element.148), channel_id=1, source_target_pairs={{0,4},{4,0},{8,12},{12,8},{1,5},{5,1},{9,13},{13,9},{2,6},{6,2},{1... | collective-permute-start | bytes 196616 | tf_op jit(solution)/shard_map/ppermute | solution.py:353
